TPU v7x, 32 devices: a whole 2x2x4 slice. The times are simulated.
32 devices in a mesh: groups: 2 (over y), seq: 4 (over z), head: 2 (over x), sub: 2 (over core).
Axes of the slice: x: 2, y: 2, z: 4, core: 2. Of those that a mesh axis runs over, the one named last changes fastest.
Arguments:
- hidden: bfloat16 [4096, 2048], P(('groups', 'seq', 'sub')), parts along dimension 0, may hold values from -6 to 6
- w_query: bfloat16 [2048, 2048], P('sub', 'head')
- w_key: bfloat16 [2048, 2048], P('sub', 'head')
- w_value: bfloat16 [2048, 2048], P('sub', 'head'), may hold values from -0.125 to 0.125
- cluster_rank: int32 [512], P('groups'), parts along dimension 0, may hold values from 0 to 255, as said below
- assign: int32 [16, 4096], P('head', ('groups', 'seq', 'sub')), parts along dimension 1, may hold values from 0 to 255, as said below
- d_attended: bfloat16 [4096, 2048], P(('groups', 'seq', 'sub'), 'head'), parts along dimension 0, may hold values from -6 to 6
Outputs:
- attended: bfloat16 [4096, 2048], P(('groups', 'seq', 'sub'), 'head'), parts along dimension 0
- d_hidden: bfloat16 [4096, 2048], P(('groups', 'seq', 'sub'), 'head'), parts along dimension 0
- centroid_sums: float32 [16, 512, 128], P('head', ('groups', 'seq', 'sub')), parts along dimension 1
There are 2 independent parts, one for each index of `groups`. A program takes and returns all parts, laid end to end along the dimension named above; an argument that names none is the same for every part. Nothing has to cross between parts.
Inputs may be any that keep to these rules, and one draw needn't show every extreme that they name: `cluster_rank` is `cluster_rank` is a permutation; cluster c belongs to owner cluster_rank[c] // 32, owners numbered like the shards of seq+sub. `assign`: in each head and each aligned block of 256 tokens at most 64 tokens have clusters of one owner, exactly 64 for some owners of every block; in every head one owner has exactly 64 from every block.
All inputs are finite; a program needn't handle non-finite values.
Results may differ from a plain program's by a relative error of at most 0.011.
Values may be sent and summed in bfloat16 or wider, within the bound.
No kernel may reach another device: no remote copies, remote signals or barrier semaphores. Data moves between devices by JAX's collectives and lax.ppermute only.
A program may use at most 128 MiB of HBM per device.

v0:
```python
from functools import partial

import jax
import jax.numpy as jnp
from jax import lax
from jax.sharding import PartitionSpec as P

epsilon = 1e-06


def keep_mask(filled, cluster_ids, positions):
    count = filled.shape[0]
    same = filled[:, None] & filled[None, :] & (cluster_ids[:, None] == cluster_ids[None, :])
    causal = positions[None, :] <= positions[:, None]
    diagonal = jnp.arange(count)[:, None] == jnp.arange(count)[None, :]
    return same & causal | diagonal


def head_forward(packed, scale):
    queries, keys_in, values, filled, cluster_ids, positions = packed
    scores = (
        lax.dot_general(
            queries, keys_in, (((1,), (1,)), ((), ())), preferred_element_type=jnp.float32
        )
        * scale
    )
    allowed = keep_mask(filled, cluster_ids, positions)
    row_top = jnp.max(jnp.where(allowed, scores, -jnp.inf), axis=1)
    expd = jnp.where(allowed, jnp.exp(scores - row_top[:, None]), 0.0)
    row_total = jnp.sum(expd, axis=1)
    probs_low = (expd / row_total[:, None]).astype(jnp.bfloat16)
    outputs = jnp.dot(probs_low, values, preferred_element_type=jnp.float32).astype(jnp.bfloat16)
    return (outputs, row_top, row_total)


def head_backward(packed, scale):
    queries, keys_in, values, grads_in, filled, cluster_ids, positions, row_top, row_total = packed
    contract_last = (((1,), (1,)), ((), ()))
    contract_first = (((0,), (0,)), ((), ()))
    scores = (
        lax.dot_general(queries, keys_in, contract_last, preferred_element_type=jnp.float32) * scale
    )
    allowed = keep_mask(filled, cluster_ids, positions)
    probs = jnp.where(allowed, jnp.exp(scores - row_top[:, None]), 0.0) / row_total[:, None]
    probs_low = probs.astype(jnp.bfloat16)
    grad_probs = lax.dot_general(
        grads_in, values, contract_last, preferred_element_type=jnp.float32
    )
    delta_rows = jnp.sum(probs * grad_probs, axis=1)
    grad_low = (probs * (grad_probs - delta_rows[:, None]) * scale).astype(jnp.bfloat16)
    grad_query = jnp.dot(grad_low, keys_in, preferred_element_type=jnp.float32).astype(jnp.bfloat16)
    grad_key = lax.dot_general(
        grad_low, queries, contract_first, preferred_element_type=jnp.float32
    ).astype(jnp.bfloat16)
    grad_value = lax.dot_general(
        probs_low, grads_in, contract_first, preferred_element_type=jnp.float32
    ).astype(jnp.bfloat16)
    return (grad_query, grad_key, grad_value)


def per_device(hidden, w_query, w_key, w_value, cluster_rank, assign, d_attended):
    tok_rows = hidden.shape[0]
    heads_here = assign.shape[0]
    head_dim = w_query.shape[1] // heads_here
    clusters = cluster_rank.shape[0]
    seq_count = lax.axis_size("seq")
    sub_count = lax.axis_size("sub")
    owners = seq_count * sub_count
    capacity = 2 * tok_rows // owners
    slot_count = owners * capacity
    per_owner = clusters // owners
    scale = head_dim ** (-0.5)
    pieces = (
        lax.all_gather(w_query, "sub", axis=0, tiled=True),
        lax.all_gather(w_key, "sub", axis=0, tiled=True),
        lax.all_gather(w_value, "sub", axis=0, tiled=True),
    )
    projected = tuple(
        (
            jnp.dot(hidden, weight_piece, preferred_element_type=jnp.float32)
            for weight_piece in pieces
        )
    )

    def split_heads(matrix):
        return (
            matrix.astype(jnp.bfloat16).reshape(tok_rows, heads_here, head_dim).transpose(1, 0, 2)
        )

    queries, keys_all, values = tuple((split_heads(matrix) for matrix in projected))
    cluster_range = jnp.arange(clusters, dtype=jnp.int32)
    rank_tok = jnp.sum(jnp.where(assign[:, :, None] == cluster_range, cluster_rank, 0), axis=2)
    owner_ids = rank_tok // per_owner
    owner_hot = (owner_ids[:, :, None] == jnp.arange(owners, dtype=jnp.int32)).astype(jnp.int32)
    within = jnp.sum(owner_hot * (jnp.cumsum(owner_hot, axis=1) - 1), axis=2)
    slot_tok = owner_ids * capacity + within
    token_ids = jnp.arange(tok_rows, dtype=jnp.int32)
    slot_range = jnp.arange(slot_count, dtype=jnp.int32)
    slot_match = slot_tok[:, None, :] == slot_range[None, :, None]
    slot_hot = slot_match.astype(jnp.bfloat16)

    def to_slots(rows_in):
        kept = jnp.einsum(
            "hst,htd->hsd", slot_hot, rows_in, preferred_element_type=jnp.float32
        ).astype(jnp.bfloat16)
        return kept.reshape(heads_here, owners, capacity, head_dim)

    def from_slots(slotted):
        flat_slots = slotted.reshape(heads_here, slot_count, head_dim)
        return jnp.einsum(
            "hst,hsd->htd", slot_hot, flat_slots, preferred_element_type=jnp.float32
        ).astype(jnp.bfloat16)

    def exchange_three(first, second, third):
        return (
            lax.all_to_all(first, ("seq", "sub"), split_axis=1, concat_axis=1, tiled=True),
            lax.all_to_all(second, ("seq", "sub"), split_axis=1, concat_axis=1, tiled=True),
            lax.all_to_all(third, ("seq", "sub"), split_axis=1, concat_axis=1, tiled=True),
        )

    sent = exchange_three(to_slots(queries), to_slots(keys_all), to_slots(values))
    tag_tok = assign * tok_rows + token_ids
    slot_tag = jnp.sum(jnp.where(slot_match, tag_tok[:, None, :] + 1, 0), axis=2) - 1
    tags = lax.all_to_all(
        slot_tag.reshape(heads_here, owners, capacity),
        ("seq", "sub"),
        split_axis=1,
        concat_axis=1,
        tiled=True,
    )
    tags = tags.reshape(heads_here, slot_count)
    owner_q, owner_k, owner_v = tuple(
        (member.reshape(heads_here, slot_count, head_dim) for member in sent)
    )
    filled = tags >= 0
    cluster_ids = jnp.where(filled, tags // tok_rows, -1)
    positions = slot_range // capacity * tok_rows + tags % tok_rows
    outputs, row_top, row_total = lax.map(
        partial(head_forward, scale=scale),
        (owner_q, owner_k, owner_v, filled, cluster_ids, positions),
    )
    returned = lax.all_to_all(
        outputs.reshape(heads_here, owners, capacity, head_dim),
        ("seq", "sub"),
        split_axis=1,
        concat_axis=1,
        tiled=True,
    )

    def merge_heads(slotted):
        return from_slots(slotted).transpose(1, 0, 2).reshape(tok_rows, heads_here * head_dim)

    attended = merge_heads(returned)
    grads_tok = d_attended.reshape(tok_rows, heads_here, head_dim).transpose(1, 0, 2)
    owner_g = lax.all_to_all(
        to_slots(grads_tok), ("seq", "sub"), split_axis=1, concat_axis=1, tiled=True
    ).reshape(heads_here, slot_count, head_dim)
    grad_q, grad_k, grad_v = lax.map(
        partial(head_backward, scale=scale),
        (owner_q, owner_k, owner_v, owner_g, filled, cluster_ids, positions, row_top, row_total),
    )
    shape_four = (heads_here, owners, capacity, head_dim)
    back = exchange_three(
        grad_q.reshape(shape_four), grad_k.reshape(shape_four), grad_v.reshape(shape_four)
    )
    token_grads = tuple((merge_heads(member) for member in back))
    pieces = lax.all_gather((w_query, w_key, w_value), "sub", axis=0, tiled=True)
    terms = [
        jnp.einsum("tc,rc->tr", grad_rows_in, weight_piece, preferred_element_type=jnp.float32)
        for grad_rows_in, weight_piece in zip(token_grads, pieces)
    ]
    partial_grad = terms[0] + terms[1] + terms[2]
    d_hidden = lax.psum_scatter(
        partial_grad.astype(jnp.bfloat16), "head", scatter_dimension=1, tiled=True
    )
    keys_float = keys_all.astype(jnp.float32)
    unit_keys = keys_float * lax.rsqrt(
        jnp.sum(keys_float * keys_float, axis=2, keepdims=True) + epsilon
    )
    member_hot = (rank_tok[:, :, None] == cluster_range).astype(jnp.float32)
    local_sums = jnp.einsum("htr,htd->hrd", member_hot, unit_keys, precision=lax.Precision.HIGHEST)
    centroid_sums = lax.psum_scatter(
        local_sums.astype(jnp.bfloat16), ("seq", "sub"), scatter_dimension=1, tiled=True
    ).astype(jnp.float32)
    return (attended, d_hidden, centroid_sums)


def solution(mesh):
    placed = (
        P(("groups", "seq", "sub"), None),
        P("sub", "head"),
        P("sub", "head"),
        P("sub", "head"),
        P("groups"),
        P("head", ("groups", "seq", "sub")),
        P(("groups", "seq", "sub"), "head"),
    )
    return jax.shard_map(
        per_device,
        mesh=mesh,
        in_specs=placed,
        out_specs=(
            P(("groups", "seq", "sub"), "head"),
            P(("groups", "seq", "sub"), "head"),
            P("head", ("groups", "seq", "sub"), None),
        ),
        check_vma=False,
    )
```

profile of v0, /device:TPU:1, one launch (start us, length us, event | category | flops | bytes accessed | tf_op | source)
XLA Modules:
  0.0 369.2 jit_solution(16538210735246105769)
XLA Ops:
  9.5 4.5 %reduce-window.6 = s32[8,8,2,128]{3,1,2,0:T(8,128)S(1)} reduce-window(s32[8,8,2,128]{3,1,2,0:T(8,128)S(1)} %fusion.88, s32[]{:T(128)} %copy.176), window={size=1x1x1x128 pad=0_0x0_0x0_0x127_0}, to_apply=%region_1.2 | reduce-window | flops 2080768 | bytes 131076 | tf_op jit(solution)/shard_map/reduce-window
  16.0 6.4 %all-to-all-start = ((s32[8,1,512]{2,1,0:T(1,128)}), s32[8,1,512]{2,1,0:T(1,128)S(1)}, u32[]{:S(2)}, u32[]{:S(2)}) async-start(s32[8,1,512]{2,1,0:T(1,128)} %reshape.214), calls=%async_computation | async-start | bytes 32768 | tf_op jit(solution)/shard_map/all_to_all | solution.py:124
  24.3 2.9 all-to-all-done
  27.3 4.2 %all-to-all-start.5 = ((bf16[8,8,64,128]{3,2,0,1:T(8,128)(2,1)}), bf16[8,8,64,128]{3,2,0,1:T(8,128)(2,1)S(1)}, u32[]{:S(2)}, u32[]{:S(2)}) async-start(bf16[8,8,64,128]{3,2,0,1:T(8,128)(2,1)} %copy.102), calls=%async_computation.5 | async-start | bytes 2097152 | tf_op jit(solution)/shard_map/all_to_all | solution.py:155
  32.2 3.5 fusion.77
  37.6 19.6 %all-to-all-done.5 = bf16[8,8,64,128]{3,2,0,1:T(8,128)(2,1)S(1)} async-done(((bf16[8,8,64,128]{3,2,0,1:T(8,128)(2,1)}), bf16[8,8,64,128]{3,2,0,1:T(8,128)(2,1)S(1)}, u32[]{:S(2)}, u32[]{:S(2)}) %all-to-all-start.5) | async-done | bytes 1048608 | tf_op jit(solution)/shard_map/all_to_all | solution.py:155
  57.2 4.3 %all-to-all-start.2 = ((bf16[8,8,64,128]{3,2,0,1:T(8,128)(2,1)}), bf16[8,8,64,128]{3,2,0,1:T(8,128)(2,1)S(1)}, u32[]{:S(2)}, u32[]{:S(2)}) async-start(bf16[8,8,64,128]{3,2,0,1:T(8,128)(2,1)} %copy.93), calls=%async_computation.2 | async-start | bytes 2097152 | tf_op jit(solution)/shard_map/all_to_all | solution.py:117
  61.5 3.4 fusion.78
  67.0 20.3 %all-to-all-done.2 = bf16[8,8,64,128]{3,2,0,1:T(8,128)(2,1)S(1)} async-done(((bf16[8,8,64,128]{3,2,0,1:T(8,128)(2,1)}), bf16[8,8,64,128]{3,2,0,1:T(8,128)(2,1)S(1)}, u32[]{:S(2)}, u32[]{:S(2)}) %all-to-all-start.2) | async-done | bytes 1048608 | tf_op jit(solution)/shard_map/all_to_all | solution.py:117
  87.3 5.0 %all-to-all-start.3 = ((bf16[8,8,64,128]{3,2,0,1:T(8,128)(2,1)}), bf16[8,8,64,128]{3,2,0,1:T(8,128)(2,1)}, u32[]{:S(2)}, u32[]{:S(2)}) async-start(bf16[8,8,64,128]{3,2,0,1:T(8,128)(2,1)} %copy.96), calls=%async_computation.3 | async-start | bytes 2097152 | tf_op jit(solution)/shard_map/all_to_all | solution.py:118
  92.3 3.4 fusion.76
  97.6 20.5 %all-to-all-done.3 = bf16[8,8,64,128]{3,2,0,1:T(8,128)(2,1)} async-done(((bf16[8,8,64,128]{3,2,0,1:T(8,128)(2,1)}), bf16[8,8,64,128]{3,2,0,1:T(8,128)(2,1)}, u32[]{:S(2)}, u32[]{:S(2)}) %all-to-all-start.3) | async-done | bytes 1048608 | tf_op jit(solution)/shard_map/all_to_all | solution.py:118
  118.1 5.0 %all-to-all-start.1 = ((bf16[8,8,64,128]{3,2,0,1:T(8,128)(2,1)}), bf16[8,8,64,128]{3,2,0,1:T(8,128)(2,1)}, u32[]{:S(2)}, u32[]{:S(2)}) async-start(bf16[8,8,64,128]{3,2,0,1:T(8,128)(2,1)} %copy.90), calls=%async_computation.1 | async-start | bytes 2097152 | tf_op jit(solution)/shard_map/all_to_all | solution.py:116
  125.8 1.3 copy.97
  127.2 21.8 %all-to-all-done.1 = bf16[8,8,64,128]{3,2,0,1:T(8,128)(2,1)} async-done(((bf16[8,8,64,128]{3,2,0,1:T(8,128)(2,1)}), bf16[8,8,64,128]{3,2,0,1:T(8,128)(2,1)}, u32[]{:S(2)}, u32[]{:S(2)}) %all-to-all-start.1) | async-done | bytes 1048608 | tf_op jit(solution)/shard_map/all_to_all | solution.py:116
  149.0 2.3 copy.91
  151.4 25.1 %while.28 = (s32[]{:T(128)}, bf16[8,512,128]{2,1,0:T(8,128)(2,1)S(1)}, f32[8,512]{1,0:T(8,128)S(1)}, f32[8,512]{1,0:T(8,128)S(1)}, pred[8,512]{1,0:T(8,128)(4,1)...) while((s32[]{:T(128)}, ...), condition=%wide.region_8.9_spmd, body=%wide.region_5.8_spmd.sunk | while | flops 142408704 | bytes 3722893 | solution.py:138
  151.5 1.5 select_reduce_fusion.4
  154.6 1.5 select_reduce_fusion.4
  157.8 1.5 select_reduce_fusion.4
  160.9 1.5 select_reduce_fusion.4
  164.0 1.5 select_reduce_fusion.4
  167.2 1.5 select_reduce_fusion.4
  170.3 1.5 select_reduce_fusion.4
  173.5 1.5 select_reduce_fusion.4
  179.3 54.3 %while.29 = (s32[]{:T(128)}, bf16[8,512,128]{2,1,0:T(8,128)(2,1)}, bf16[8,512,128]{2,1,0:T(8,128)(2,1)S(1)}, bf16[8,512,128]{2,1,0:T(8,128)(2,1)S(1)}, pred[8,51...) while((s32[]{:T(128)}, bf16[8,512,128]{2,1,0:T(8,128)(2,1)}, ...), condition=%wide.region_11.12_spmd, body=%wide.region_9.11_spmd.sunk | while | flops 340459008 | bytes 9215129 | solution.py:158
  180.5 1.7 multiply_reduce_fusion.2
  182.9 1.3 fusion.152
  184.1 1.9 fusion.151
  187.3 1.7 multiply_reduce_fusion.2
  190.9 1.9 fusion.151
  194.1 1.7 multiply_reduce_fusion.2
  196.4 1.3 fusion.152
  197.7 1.9 fusion.151
  200.9 1.7 multiply_reduce_fusion.2
  204.5 1.9 fusion.151
  207.7 1.7 multiply_reduce_fusion.2
  211.3 1.9 fusion.151
  214.5 1.7 multiply_reduce_fusion.2
  216.8 1.3 fusion.152
  218.1 1.9 fusion.151
  221.2 1.7 multiply_reduce_fusion.2
  224.8 1.9 fusion.151
  228.0 1.7 multiply_reduce_fusion.2
  230.4 1.3 fusion.152
  231.6 1.9 fusion.151
  233.5 2.7 copy.104
  236.2 4.3 %all-to-all-start.6 = ((bf16[8,8,64,128]{3,2,0,1:T(8,128)(2,1)}), bf16[8,8,64,128]{3,2,0,1:T(8,128)(2,1)S(1)}, u32[]{:S(2)}, u32[]{:S(2)}) async-start(bf16[8,8,64,128]{3,2,0,1:T(8,128)(2,1)} %copy.104), calls=%async_computation.6 | async-start | bytes 2097152 | tf_op jit(solution)/shard_map/all_to_all | solution.py:116
  241.6 24.7 %all-to-all-done.6 = bf16[8,8,64,128]{3,2,0,1:T(8,128)(2,1)S(1)} async-done(((bf16[8,8,64,128]{3,2,0,1:T(8,128)(2,1)}), bf16[8,8,64,128]{3,2,0,1:T(8,128)(2,1)S(1)}, u32[]{:S(2)}, u32[]{:S(2)}) %all-to-all-start.6) | async-done | bytes 1048608 | tf_op jit(solution)/shard_map/all_to_all | solution.py:116
  266.3 4.3 %all-to-all-start.8 = ((bf16[8,8,64,128]{3,2,0,1:T(8,128)(2,1)}), bf16[8,8,64,128]{3,2,0,1:T(8,128)(2,1)S(1)}, u32[]{:S(2)}, u32[]{:S(2)}) async-start(bf16[8,8,64,128]{3,2,0,1:T(8,128)(2,1)} %copy.110), calls=%async_computation.8 | async-start | bytes 2097152 | tf_op jit(solution)/shard_map/all_to_all | solution.py:118
  270.6 2.3 copy.107
  272.9 23.4 %all-to-all-done.8 = bf16[8,8,64,128]{3,2,0,1:T(8,128)(2,1)S(1)} async-done(((bf16[8,8,64,128]{3,2,0,1:T(8,128)(2,1)}), bf16[8,8,64,128]{3,2,0,1:T(8,128)(2,1)S(1)}, u32[]{:S(2)}, u32[]{:S(2)}) %all-to-all-start.8) | async-done | bytes 1048608 | tf_op jit(solution)/shard_map/all_to_all | solution.py:118
  296.4 4.3 %all-to-all-start.7 = ((bf16[8,8,64,128]{3,2,0,1:T(8,128)(2,1)}), bf16[8,8,64,128]{3,2,0,1:T(8,128)(2,1)S(1)}, u32[]{:S(2)}, u32[]{:S(2)}) async-start(bf16[8,8,64,128]{3,2,0,1:T(8,128)(2,1)} %copy.107), calls=%async_computation.7 | async-start | bytes 2097152 | tf_op jit(solution)/shard_map/all_to_all | solution.py:117
  300.7 1.4 fusion.79
  302.1 3.2 fusion.71
  305.3 2.3 copy.98
  308.9 1.8 fusion.75
  310.7 2.7 fusion.104
  313.4 15.5 %all-to-all-done.7 = bf16[8,8,64,128]{3,2,0,1:T(8,128)(2,1)S(1)} async-done(((bf16[8,8,64,128]{3,2,0,1:T(8,128)(2,1)}), bf16[8,8,64,128]{3,2,0,1:T(8,128)(2,1)S(1)}, u32[]{:S(2)}, u32[]{:S(2)}) %all-to-all-start.7) | async-done | bytes 1048608 | tf_op jit(solution)/shard_map/all_to_all | solution.py:117
  328.9 4.4 %all-to-all-start.4 = ((bf16[8,8,64,128]{3,2,0,1:T(8,128)(2,1)}), bf16[8,8,64,128]{3,2,0,1:T(8,128)(2,1)S(1)}, u32[]{:S(2)}, u32[]{:S(2)}) async-start(bf16[8,8,64,128]{3,2,0,1:T(8,128)(2,1)} %copy.98), calls=%async_computation.4 | async-start | bytes 2097152 | tf_op jit(solution)/shard_map/all_to_all | solution.py:142
  335.5 3.0 convolution_add_fusion.1
  338.6 2.3 fusion.57
  340.9 1.5 convert_element_type.108
  342.4 17.1 %all-to-all-done.4 = bf16[8,8,64,128]{3,2,0,1:T(8,128)(2,1)S(1)} async-done(((bf16[8,8,64,128]{3,2,0,1:T(8,128)(2,1)}), bf16[8,8,64,128]{3,2,0,1:T(8,128)(2,1)S(1)}, u32[]{:S(2)}, u32[]{:S(2)}) %all-to-all-start.4) | async-done | bytes 1048608 | tf_op jit(solution)/shard_map/all_to_all | solution.py:142
  (193 shorter events, 58.3 us)
Async XLA Ops:
  7.2 25.0 %copy-start = (bf16[256,2048]{1,0:T(8,128)(2,1)S(1)}, bf16[256,2048]{1,0:T(8,128)(2,1)}, u32[]{:S(2)}) copy-start(bf16[256,2048]{1,0:T(8,128)(2,1)} %param.11) | copy-start | bytes 3145732
  7.2 1.5 copy-start.7
  7.2 1.5 copy-start.8
  7.2 15.1 %copy-start.11 = (bf16[256,1024]{1,0:T(8,128)(2,1)S(1)}, bf16[256,1024]{1,0:T(8,128)(2,1)}, u32[]{:S(2)}) copy-start(bf16[256,1024]{1,0:T(8,128)(2,1)} %param.17) | copy-start | bytes 1572868
  7.2 25.0 %all-gather.6.cloned.1.call-start = ((), (), s32[]{:S(2)}) async-start(), calls=%async_computation.12 | async-start | bytes 6291456 | tf_op jit(solution)/shard_map/all_gather | solution.py:75
  7.9 53.6 %all-gather.8.cloned.1.call-start = ((), (), s32[]{:S(2)}) async-start(), calls=%async_computation.13 | async-start | bytes 6291456 | tf_op jit(solution)/shard_map/all_gather | solution.py:76
  16.0 11.3 %all-to-all-start = ((s32[8,1,512]{2,1,0:T(1,128)}), s32[8,1,512]{2,1,0:T(1,128)S(1)}, u32[]{:S(2)}, u32[]{:S(2)}) async-start(s32[8,1,512]{2,1,0:T(1,128)} %reshape.214), calls=%async_computation | async-start | bytes 32768 | tf_op jit(solution)/shard_map/all_to_all | solution.py:124
  27.3 29.9 %all-to-all-start.5 = ((bf16[8,8,64,128]{3,2,0,1:T(8,128)(2,1)}), bf16[8,8,64,128]{3,2,0,1:T(8,128)(2,1)S(1)}, u32[]{:S(2)}, u32[]{:S(2)}) async-start(bf16[8,8,64,128]{3,2,0,1:T(8,128)(2,1)} %copy.102), calls=%async_computation.5 | async-start | bytes 2097152 | tf_op jit(solution)/shard_map/all_to_all | solution.py:155
  31.5 60.8 %all-gather.4.cloned.1.call-start = ((), (), s32[]{:S(2)}) async-start(), calls=%async_computation.11 | async-start | bytes 6291456 | tf_op jit(solution)/shard_map/all_gather | solution.py:74
  35.7 0.9 copy-start.6
  57.2 30.1 %all-to-all-start.2 = ((bf16[8,8,64,128]{3,2,0,1:T(8,128)(2,1)}), bf16[8,8,64,128]{3,2,0,1:T(8,128)(2,1)S(1)}, u32[]{:S(2)}, u32[]{:S(2)}) async-start(bf16[8,8,64,128]{3,2,0,1:T(8,128)(2,1)} %copy.93), calls=%async_computation.2 | async-start | bytes 2097152 | tf_op jit(solution)/shard_map/all_to_all | solution.py:117
  87.3 30.9 %all-to-all-start.3 = ((bf16[8,8,64,128]{3,2,0,1:T(8,128)(2,1)}), bf16[8,8,64,128]{3,2,0,1:T(8,128)(2,1)}, u32[]{:S(2)}, u32[]{:S(2)}) async-start(bf16[8,8,64,128]{3,2,0,1:T(8,128)(2,1)} %copy.96), calls=%async_computation.3 | async-start | bytes 2097152 | tf_op jit(solution)/shard_map/all_to_all | solution.py:118
  118.1 30.9 %all-to-all-start.1 = ((bf16[8,8,64,128]{3,2,0,1:T(8,128)(2,1)}), bf16[8,8,64,128]{3,2,0,1:T(8,128)(2,1)}, u32[]{:S(2)}, u32[]{:S(2)}) async-start(bf16[8,8,64,128]{3,2,0,1:T(8,128)(2,1)} %copy.90), calls=%async_computation.1 | async-start | bytes 2097152 | tf_op jit(solution)/shard_map/all_to_all | solution.py:116
  176.5 1.1 copy-start.4
  176.6 1.3 copy-start.5
  233.5 32.8 %copy-start.3 = (bf16[8,512,128]{2,1,0:T(8,128)(2,1)}, bf16[8,512,128]{2,1,0:T(8,128)(2,1)S(1)}, u32[]{:S(2)}) copy-start(bf16[8,512,128]{2,1,0:T(8,128)(2,1)S(1)} %get-tuple-element.130) | copy-start | bytes 3145732
  236.2 30.1 %all-to-all-start.6 = ((bf16[8,8,64,128]{3,2,0,1:T(8,128)(2,1)}), bf16[8,8,64,128]{3,2,0,1:T(8,128)(2,1)S(1)}, u32[]{:S(2)}, u32[]{:S(2)}) async-start(bf16[8,8,64,128]{3,2,0,1:T(8,128)(2,1)} %copy.104), calls=%async_computation.6 | async-start | bytes 2097152 | tf_op jit(solution)/shard_map/all_to_all | solution.py:116
  266.3 30.1 %all-to-all-start.8 = ((bf16[8,8,64,128]{3,2,0,1:T(8,128)(2,1)}), bf16[8,8,64,128]{3,2,0,1:T(8,128)(2,1)S(1)}, u32[]{:S(2)}, u32[]{:S(2)}) async-start(bf16[8,8,64,128]{3,2,0,1:T(8,128)(2,1)} %copy.110), calls=%async_computation.8 | async-start | bytes 2097152 | tf_op jit(solution)/shard_map/all_to_all | solution.py:118
  296.4 32.5 %all-to-all-start.7 = ((bf16[8,8,64,128]{3,2,0,1:T(8,128)(2,1)}), bf16[8,8,64,128]{3,2,0,1:T(8,128)(2,1)S(1)}, u32[]{:S(2)}, u32[]{:S(2)}) async-start(bf16[8,8,64,128]{3,2,0,1:T(8,128)(2,1)} %copy.107), calls=%async_computation.7 | async-start | bytes 2097152 | tf_op jit(solution)/shard_map/all_to_all | solution.py:117
  300.7 40.2 %reduce-scatter.5.cloned.1.call-start = ((), (), s32[]{:S(2)}) async-start(), calls=%async_computation.15 | async-start | bytes 589824 | tf_op jit(solution)/shard_map/reduce_scatter | solution.py:182
  307.7 3.0 copy-start.10
  328.9 30.6 %all-to-all-start.4 = ((bf16[8,8,64,128]{3,2,0,1:T(8,128)(2,1)}), bf16[8,8,64,128]{3,2,0,1:T(8,128)(2,1)S(1)}, u32[]{:S(2)}, u32[]{:S(2)}) async-start(bf16[8,8,64,128]{3,2,0,1:T(8,128)(2,1)} %copy.98), calls=%async_computation.4 | async-start | bytes 2097152 | tf_op jit(solution)/shard_map/all_to_all | solution.py:142
  333.3 29.4 %reduce-scatter.3.cloned.1.call-start = ((), (), s32[]{:S(2)}) async-start(), calls=%async_computation.14 | async-start | bytes 1572864 | tf_op jit(solution)/shard_map/reduce_scatter | solution.py:173
  333.3 2.2 copy-start.2
  335.5 3.1 copy-start.9
  335.5 3.1 copy-start.12
  338.6 24.1 %copy-start.1 = (bf16[256,2048]{1,0:T(8,128)(2,1)S(1)}, bf16[256,2048]{1,0:T(8,128)(2,1)}, u32[]{:S(2)}) copy-start(bf16[256,2048]{1,0:T(8,128)(2,1)} %param.11) | copy-start | bytes 3145732
Sparse Core Ops, SparseCore 0:
  9.6 16.1 all-gather.5
  27.3 14.8 all-gather.7
  43.7 14.8 all-gather.3
  305.5 31.8 reduce-scatter.4
  341.0 21.5 reduce-scatter.2
where the time goes:
time: 372 us; the launch traced here: 369 us
  waiting for transfers between devices  169 us (45%)
  matrix products  100 us (27%)
  starting transfers between devices  42.4 us (11%)
  local copies, waits for them, and re-layouts  26.2 us (7%)
  other arithmetic  16.2 us (4%)
  between operations  14.2 us (4%)
    all_to_all x2, waiting for transfers between devices, exchange_three(): lax.all_to_all(first, ('seq', 'sub'), split_axis=1, concat_axis=1, tiled=...  46.5 us
    all_to_all x2, waiting for transfers between devices, exchange_three(): lax.all_to_all(third, ('seq', 'sub'), split_axis=1, concat_axis=1, tiled=...  43.9 us
    all_to_all x2, waiting for transfers between devices, exchange_three(): lax.all_to_all(second, ('seq', 'sub'), split_axis=1, concat_axis=1, tiled...  35.9 us
    all_to_all x1, waiting for transfers between devices, per_device(): lax.all_to_all(to_slots(grads_tok), ('seq', 'sub'), split_axis=1, concat_...  19.6 us
    all_to_all x1, waiting for transfers between devices, per_device(): lax.all_to_all(outputs.reshape(heads_here, owners, capacity, head_dim), (...  17.1 us
    dot_general x8, matrix products, head_backward(): jnp.dot(grad_low, keys_in, preferred_element_type=jnp.float32)  15.3 us
    dot_general x8, matrix products, head_backward(): lax.dot_general(queries, keys_in, contract_last, preferred_element_type=j...  13.7 us
    dot_general x8, matrix products, head_forward(): lax.dot_general(queries, keys_in, (((1,), (1,)), ((), ())), preferred_ele...  12.1 us
  transfers between devices with their start and end apart: 14, of which 10 were waited for; matrix products, arithmetic and copies ran while one was open for 15% of the time, Pallas kernels for 0%

commit v1 on v0

--- a/solution.py
+++ b/solution.py
@@ -3,6 +3,8 @@
 import jax
 import jax.numpy as jnp
 from jax import lax
+from jax.experimental import pallas as pl
+from jax.experimental.pallas import tpu as pltpu
 from jax.sharding import PartitionSpec as P
 
 epsilon = 1e-06
@@ -58,7 +60,7 @@
     return (grad_query, grad_key, grad_value)
 
 
-def per_device(hidden, w_query, w_key, w_value, cluster_rank, assign, d_attended):
+def by_owner(hidden, w_query, w_key, w_value, cluster_rank, assign, d_attended):
     tok_rows = hidden.shape[0]
     heads_here = assign.shape[0]
     head_dim = w_query.shape[1] // heads_here
@@ -185,6 +187,226 @@
     return (attended, d_hidden, centroid_sums)
 
 
+contract_last = (((1,), (1,)), ((), ()))
+log2_e = 1.4426950408889634
+
+
+def masked_scores(keys_in, query_rows, col_ids, row_ids, block, factor):
+    seen = keys_in.shape[0]
+    count = query_rows.shape[0]
+    scores = (
+        lax.dot_general(keys_in, query_rows, contract_last, preferred_element_type=jnp.float32)
+        * factor
+    )
+    same = col_ids == row_ids
+    key_at = lax.broadcasted_iota(jnp.int32, (count, count), 0)
+    query_at = lax.broadcasted_iota(jnp.int32, (count, count), 1)
+    last = same[seen - count :] & (key_at <= query_at)
+    if block == 0:
+        allowed = last
+    else:
+        allowed = jnp.concatenate([same[: seen - count], last], axis=0)
+    return jnp.where(allowed, scores, -jnp.inf)
+
+
+def forward_kernel(factor, packed_ref, col_ref, row_ref, out_ref, lse_ref):
+    blocks, triple, head_dim = packed_ref.shape
+    rows = triple // 3
+    for block in range(blocks):
+        seen = (block + 1) * rows
+        keys_in = packed_ref[: block + 1, rows : 2 * rows, :].reshape(seen, head_dim)
+        values = packed_ref[: block + 1, 2 * rows :, :].reshape(seen, head_dim)
+        scores = masked_scores(
+            keys_in,
+            packed_ref[block, :rows, :],
+            col_ref[:seen, :],
+            row_ref[block : block + 1, :],
+            block,
+            factor,
+        )
+        top = jnp.max(scores, axis=0, keepdims=True)
+        expd = jnp.exp2(scores - top)
+        total = jnp.sum(expd, axis=0, keepdims=True)
+        probs_low = (expd * (1.0 / total)).astype(jnp.bfloat16)
+        flipped = lax.dot_general(
+            values, probs_low, (((0,), (0,)), ((), ())), preferred_element_type=jnp.float32
+        )
+        out_ref[block] = flipped.T.astype(jnp.bfloat16)
+        lse_ref[block : block + 1, :] = top + jnp.log2(total)
+
+
+def backward_kernel(
+    factor, scale, packed_ref, grads_ref, col_ref, row_ref, rank_ref, lse_ref, out_ref, dk_ref, dv_ref
+):
+    blocks, triple, head_dim = packed_ref.shape
+    rows = triple // 3
+    tokens = blocks * rows
+    clusters = rank_ref.shape[1]
+    owned = clusters // blocks
+    dk_ref[...] = jnp.zeros_like(dk_ref)
+    dv_ref[...] = jnp.zeros_like(dv_ref)
+    for block in range(blocks):
+        seen = (block + 1) * rows
+        keys_in = packed_ref[: block + 1, rows : 2 * rows, :].reshape(seen, head_dim)
+        values = packed_ref[: block + 1, 2 * rows :, :].reshape(seen, head_dim)
+        query_rows = packed_ref[block, :rows, :]
+        grad_rows = grads_ref[block, :rows, :]
+        scores = masked_scores(
+            keys_in, query_rows, col_ref[:seen, :], row_ref[block : block + 1, :], block, factor
+        )
+        probs = jnp.exp2(scores - lse_ref[block : block + 1, :])
+        grad_probs = lax.dot_general(
+            values, grad_rows, contract_last, preferred_element_type=jnp.float32
+        )
+        weighted = probs * grad_probs
+        delta = jnp.sum(weighted, axis=0, keepdims=True)
+        grad_low = (weighted - probs * delta).astype(jnp.bfloat16)
+        dv_ref[:seen, :] += jnp.dot(
+            probs.astype(jnp.bfloat16), grad_rows, preferred_element_type=jnp.float32
+        )
+        dk_ref[:seen, :] += jnp.dot(grad_low, query_rows, preferred_element_type=jnp.float32)
+        flipped = lax.dot_general(
+            keys_in, grad_low, (((0,), (0,)), ((), ())), preferred_element_type=jnp.float32
+        )
+        out_ref[block, :rows, :] = (flipped.T * scale).astype(jnp.bfloat16)
+    out_ref[:, rows : 2 * rows, :] = (
+        (dk_ref[...] * scale).astype(jnp.bfloat16).reshape(blocks, rows, head_dim)
+    )
+    out_ref[:, 2 * rows : triple, :] = (
+        dv_ref[...].astype(jnp.bfloat16).reshape(blocks, rows, head_dim)
+    )
+    sums = jnp.zeros((clusters, head_dim), jnp.float32)
+    cluster_at = lax.broadcasted_iota(jnp.int32, (clusters, rows), 0)
+    for block in range(blocks):
+        keys_float = packed_ref[block, rows : 2 * rows, :].astype(jnp.float32)
+        unit = keys_float * lax.rsqrt(
+            jnp.sum(keys_float * keys_float, axis=1, keepdims=True) + epsilon
+        )
+        unit_high = unit.astype(jnp.bfloat16)
+        unit_low = (unit - unit_high.astype(jnp.float32)).astype(jnp.bfloat16)
+        member = jnp.where(cluster_at == row_ref[block : block + 1, :], 1.0, 0.0).astype(
+            jnp.bfloat16
+        )
+        sums += jnp.dot(member, unit_high, preferred_element_type=jnp.float32)
+        sums += jnp.dot(member, unit_low, preferred_element_type=jnp.float32)
+    rank_at = lax.broadcasted_iota(jnp.int32, (clusters, clusters), 0)
+    ordered = jnp.where(rank_at == rank_ref[...], 1.0, 0.0).astype(jnp.bfloat16)
+    ranked = jnp.dot(ordered, sums.astype(jnp.bfloat16), preferred_element_type=jnp.float32)
+    out_ref[:, triple:, :] = ranked.astype(jnp.bfloat16).reshape(blocks, owned, head_dim)
+
+
+def by_head(hidden, w_query, w_key, w_value, cluster_rank, assign, d_attended):
+    rows = hidden.shape[0]
+    blocks = assign.shape[0]
+    head_dim = w_query.shape[1] // blocks
+    width = w_query.shape[1]
+    half = w_query.shape[0]
+    tokens = blocks * rows
+    clusters = cluster_rank.shape[0]
+    owned = clusters // blocks
+    scale = head_dim ** (-0.5)
+    factor = scale * log2_e
+    line = ("seq", "sub")
+    vmem = pl.BlockSpec(memory_space=pltpu.VMEM)
+    params = pltpu.CompilerParams(vmem_limit_bytes=48 * 1024 * 1024)
+    pairs_seen = tokens * (tokens + rows) // 2
+
+    def exchange(packed):
+        return lax.all_to_all(packed, line, split_axis=0, concat_axis=0, tiled=True)
+
+    def split_heads(matrix):
+        return matrix.reshape(rows, blocks, head_dim).transpose(1, 0, 2)
+
+    tag_rows = -(-rows // head_dim // 16) * 16
+    tags = assign.astype(jnp.bfloat16).reshape(blocks, rows // head_dim, head_dim)
+    tags = jnp.pad(tags, ((0, 0), (0, tag_rows - rows // head_dim), (0, 0)))
+    grads = exchange(jnp.concatenate([split_heads(d_attended), tags], axis=1))
+    row_ids = (
+        grads[:, rows : rows + rows // head_dim, :].reshape(blocks, rows).astype(jnp.int32)
+    )
+    col_ids = row_ids.reshape(tokens, 1)
+
+    swap = [(0, 1), (1, 0)]
+    side = lax.axis_index("sub")
+    near = lax.dynamic_slice_in_dim(hidden, side * half, half, axis=1)
+    far = lax.dynamic_slice_in_dim(hidden, (1 - side) * half, half, axis=1)
+    own = (w_query, w_key, w_value)
+    other = tuple(lax.ppermute(piece, "sub", swap) for piece in own)
+    projected = [
+        split_heads(
+            (
+                jnp.dot(near, mine, preferred_element_type=jnp.float32)
+                + jnp.dot(far, theirs, preferred_element_type=jnp.float32)
+            ).astype(jnp.bfloat16)
+        )
+        for mine, theirs in zip(own, other)
+    ]
+    packed = exchange(jnp.concatenate(projected, axis=1))
+
+    outputs, lse = pl.pallas_call(
+        partial(forward_kernel, factor),
+        out_shape=(
+            jax.ShapeDtypeStruct((blocks, rows, head_dim), jnp.bfloat16),
+            jax.ShapeDtypeStruct((blocks, rows), jnp.float32),
+        ),
+        in_specs=[vmem] * 3,
+        out_specs=(vmem, vmem),
+        compiler_params=params,
+        cost_estimate=pl.CostEstimate(
+            flops=4 * pairs_seen * head_dim,
+            bytes_accessed=8 * tokens * head_dim,
+            transcendentals=pairs_seen,
+        ),
+    )(packed, col_ids, row_ids)
+    returned = exchange(outputs)
+    attended = returned.transpose(1, 0, 2).reshape(rows, width)
+
+    grads_out = pl.pallas_call(
+        partial(backward_kernel, factor, scale),
+        out_shape=jax.ShapeDtypeStruct((blocks, 3 * rows + owned, head_dim), jnp.bfloat16),
+        in_specs=[vmem] * 6,
+        out_specs=vmem,
+        scratch_shapes=[
+            pltpu.VMEM((tokens, head_dim), jnp.float32),
+            pltpu.VMEM((tokens, head_dim), jnp.float32),
+        ],
+        compiler_params=params,
+        cost_estimate=pl.CostEstimate(
+            flops=10 * pairs_seen * head_dim,
+            bytes_accessed=14 * tokens * head_dim,
+            transcendentals=pairs_seen,
+        ),
+    )(packed, grads, col_ids, row_ids, cluster_rank.reshape(1, clusters), lse)
+    back = exchange(grads_out)
+    centroid_sums = back[:, 3 * rows :, :].astype(jnp.float32)
+    token_grads = [
+        back[:, index * rows : (index + 1) * rows, :].transpose(1, 0, 2).reshape(rows, width)
+        for index in range(3)
+    ]
+
+    def input_part(pieces):
+        terms = [
+            jnp.einsum("tc,rc->tr", grad_rows, piece, preferred_element_type=jnp.float32)
+            for grad_rows, piece in zip(token_grads, pieces)
+        ]
+        return terms[0] + terms[1] + terms[2]
+
+    straight = side == lax.axis_index("head")
+    part_own, part_other = input_part(own), input_part(other)
+    sent = jnp.where(straight, part_other, part_own).astype(jnp.bfloat16)
+    kept = jnp.where(straight, part_own, part_other)
+    arrived = lax.ppermute(sent, "head", swap)
+    d_hidden = (kept + arrived.astype(jnp.float32)).astype(jnp.bfloat16)
+    return (attended, d_hidden, centroid_sums)
+
+
+def per_device(hidden, w_query, w_key, w_value, cluster_rank, assign, d_attended):
+    owners = lax.axis_size("seq") * lax.axis_size("sub")
+    halves = lax.axis_size("sub") == 2 and lax.axis_size("head") == 2
+    plan = by_head if assign.shape[0] == owners and halves else by_owner
+    return plan(hidden, w_query, w_key, w_value, cluster_rank, assign, d_attended)
+
+
 def solution(mesh):
     placed = (
         P(("groups", "seq", "sub"), None),

time: 372 us -> 179 us (0.48)
  waiting for transfers between devices: 169 us -> 80.8 us
  matrix products: 100 us -> 23.5 us
  starting transfers between devices: 42.4 us -> 22.6 us
  Pallas kernels: 0 us -> 17.3 us
  between operations: 14.2 us -> 0.85 us
  other arithmetic: 16.2 us -> 7.52 us
    all_to_all x9 -> x4, waiting for transfers between devices: 166 us -> 73.9 us  [exchange(): return lax.all_to_all(packed, line, split_axis=0, concat_axis=0, tiled=True)]
    dot_general x71 -> x12, matrix products: 100 us -> 23.5 us  [the longest x6 11.5 us: input_part(): jnp.einsum('tc,rc->tr', grad_rows, piece, preferred_element_type=jnp.floa...]
    all_to_all x9 -> x4, starting transfers between devices: 42.3 us -> 20.8 us  [exchange(): return lax.all_to_all(packed, line, split_axis=0, concat_axis=0, tiled=True)]
    pallas_call x0 -> x2, Pallas kernels: none -> 17.3 us  [the longest x1 9.38 us: by_head(): pl.pallas_call(partial(backward_kernel, factor, scale), out_shape=jax.Sha...]
    transpose x0 -> x5, local copies, waits for them, and re-layouts: none -> 9.59 us  [the longest x4 7.54 us: by_head(): back[:, index * rows:(index + 1) * rows, :].transpose(1, 0, 2)]
    reshape x9 -> x5, local copies, waits for them, and re-layouts: 12.9 us -> 4.66 us  [the longest x4 4.65 us: split_heads(): return matrix.reshape(rows, blocks, head_dim).transpose(1, 0, 2)]
    reduce_sum x12 -> x0, other arithmetic: 7.2 us -> none  [the longest x8 4.34 us: head_forward(): row_total = jnp.sum(expd, axis=1)]
    ppermute x0 -> x4, waiting for transfers between devices: none -> 6.9 us  [the longest x1 6.89 us: by_head(): arrived = lax.ppermute(sent, 'head', swap)]
  transfers between devices with their start and end apart: 14 -> 8, of which waited for: 10 -> 3; matrix products, arithmetic and copies ran while one was open for 15% -> 28% of each run, Pallas kernels for 0% -> 0%
where the time goes in v1:
time: 179 us; the launch traced here: 177 us
  waiting for transfers between devices  80.8 us (45%)
  local copies, waits for them, and re-layouts  23.9 us (13%)
  matrix products  23.5 us (13%)
  starting transfers between devices  22.6 us (13%)
  Pallas kernels  17.3 us (10%)
  other arithmetic  7.52 us (4%)
    all_to_all x4, waiting for transfers between devices, exchange(): return lax.all_to_all(packed, line, split_axis=0, concat_axis=0, tiled=True)  73.9 us
    all_to_all x4, starting transfers between devices, exchange(): return lax.all_to_all(packed, line, split_axis=0, concat_axis=0, tiled=True)  20.8 us
    dot_general x6, matrix products, input_part(): jnp.einsum('tc,rc->tr', grad_rows, piece, preferred_element_type=jnp.floa...  11.5 us
    pallas_call x1, Pallas kernels, by_head(): pl.pallas_call(partial(backward_kernel, factor, scale), out_shape=jax.Sha...  9.38 us
    pallas_call x1, Pallas kernels, by_head(): pl.pallas_call(partial(forward_kernel, factor), out_shape=(jax.ShapeDtype...  7.95 us
    transpose x4, local copies, waits for them, and re-layouts, by_head(): back[:, index * rows:(index + 1) * rows, :].transpose(1, 0, 2)  7.54 us
    dot_general x3, matrix products, by_head(): jnp.dot(far, theirs, preferred_element_type=jnp.float32)  7.17 us
    ppermute x1, waiting for transfers between devices, by_head(): arrived = lax.ppermute(sent, 'head', swap)  6.89 us
  transfers between devices with their start and end apart: 8, of which 3 were waited for; matrix products, arithmetic and copies ran while one was open for 28% of the time, Pallas kernels for 0%

profile of v1, /device:TPU:1, one launch (start us, length us, event | category | flops | bytes accessed | tf_op | source)
XLA Modules:
  0.0 176.5 jit_solution(17336076267253452585)
XLA Ops:
  0.6 0.0 copy-start
  0.6 0.1 collective-permute-start
  0.8 0.5 collective-permute-start.1
  1.2 0.1 collective-permute-start.2
  1.3 0.7 convert_element_type.38
  2.0 1.2 copy.16
  3.3 0.3 copy.17
  3.5 0.9 fusion.5
  4.4 6.4 %all-to-all-start.1 = ((bf16[8,272,128]{2,1,0:T(8,128)(2,1)}), bf16[8,272,128]{2,1,0:T(8,128)(2,1)S(1)}, u32[]{:S(2)}, u32[]{:S(2)}) async-start(bf16[8,272,128]{2,1,0:T(8,128)(2,1)} %fusion.5), calls=%async_computation.1 | async-start | bytes 1114112 | tf_op jit(solution)/shard_map/all_to_all | solution.py:315
  10.9 0.0 copy-done
  10.9 2.4 %fusion.13 = f32[256,1024]{1,0:T(8,128)S(1)} fusion(bf16[1024,1024]{1,0:T(8,128)(2,1)} %param.8, bf16[256,2048]{1,0:T(8,128)(2,1)S(1)} %copy-done, s32[]{:T(128)S(6)} %select_n.18), kind=kOutput, calls=%fused_computation.26 | convolution fusion | flops 536870912 | bytes 3670020 | tf_op jit(solution)/shard_map/dot_general | solution.py:338
  13.3 0.0 copy-done.4
  13.3 0.0 copy-start.6
  13.3 1.7 fusion.11
  15.0 0.0 copy-done.6
  15.0 0.7 fusion.9
  15.7 0.0 collective-permute-done
  15.8 2.3 %fusion.1 = bf16[256,1024]{1,0:T(8,128)(2,1)S(1)} fusion(f32[256,1024]{1,0:T(8,128)S(1)} %fusion.13, bf16[1024,1024]{1,0:T(8,128)(2,1)} %collective-permute-done, bf16[256,2048]{1,0:T(8,128)(2,1)S(1)} %copy-done, s32[]{:T(128)S(6)} %select_n.19), kind=kOutput, calls=%fused_computation.8 | convolution fusion | flops 537395200 | bytes 4194308 | tf_op jit(solution)/shard_map/dot_general | solution.py:339
  18.1 1.0 copy.10
  19.1 2.1 %copy.11 = bf16[256,8,128]{2,0,1:T(8,128)(2,1)} copy(bf16[256,8,128]{0,2,1:T(8,128)(2,1)} %bitcast.54) | data formatting | bytes 1048576 | tf_op jit(solution)/shard_map/reshape | solution.py:318
  21.1 0.0 collective-permute-done.1
  21.1 2.6 %fusion.2 = bf16[256,1024]{1,0:T(8,128)(2,1)S(1)} fusion(f32[256,1024]{1,0:T(8,128)} %fusion.11, bf16[1024,1024]{1,0:T(8,128)(2,1)} %collective-permute-done.1, bf16[256,2048]{1,0:T(8,128)(2,1)S(1)} %copy-done, s32[]{:T(128)S(6)} %select_n.19), kind=kOutput, calls=%fused_computation.9 | convolution fusion | flops 537395200 | bytes 4194308 | tf_op jit(solution)/shard_map/dot_general | solution.py:339
  23.7 1.0 copy.12
  24.7 2.0 %copy.13 = bf16[256,8,128]{2,0,1:T(8,128)(2,1)} copy(bf16[256,8,128]{0,2,1:T(8,128)(2,1)} %bitcast.55) | data formatting | bytes 1048576 | tf_op jit(solution)/shard_map/reshape | solution.py:318
  26.8 0.0 collective-permute-done.2
  26.8 2.3 %fusion.3 = bf16[256,1024]{1,0:T(8,128)(2,1)S(1)} fusion(f32[256,1024]{1,0:T(8,128)S(1)} %fusion.9, bf16[1024,1024]{1,0:T(8,128)(2,1)} %collective-permute-done.2, bf16[256,2048]{1,0:T(8,128)(2,1)S(1)} %copy-done, s32[]{:T(128)S(6)} %select_n.19), kind=kOutput, calls=%fused_computation.10 | convolution fusion | flops 537395200 | bytes 4194308 | tf_op jit(solution)/shard_map/dot_general | solution.py:339
  29.1 0.0 copy-start.12
  29.1 0.2 copy.14
  29.3 0.3 copy.15
  29.6 0.5 copy-done.12
  30.1 2.3 %pad_maximum_fusion = bf16[8,768,128]{2,1,0:T(8,128)(2,1)} fusion(bf16[8,256,128]{2,1,0:T(8,128)(2,1)S(1)} %bitcast.61, bf16[8,256,128]{2,1,0:T(8,128)(2,1)} %bitcast.60, bf16[8,256,128]{2,1,0:T(8,128)(2,1)S(1)} %bitcast.59), kind=kLoop, calls=%fused_computation | loop fusion | flops 4718592 | bytes 3145728 | tf_op jit(solution)/shard_map/concatenate | solution.py:344
  32.4 0.0 all-to-all-done.1.grads_ref
  32.4 5.1 %all-to-all-start = ((bf16[8,768,128]{2,1,0:T(8,128)(2,1)}), bf16[8,768,128]{2,1,0:T(8,128)(2,1)S(1)}, u32[]{:S(2)}, u32[]{:S(2)}) async-start(bf16[8,768,128]{2,1,0:T(8,128)(2,1)} %pad_maximum_fusion), calls=%async_computation | async-start | bytes 3145728 | tf_op jit(solution)/shard_map/all_to_all | solution.py:315
  37.5 1.4 copy.18.col_ref
  39.0 35.5 %all-to-all-done.packed_ref = bf16[8,768,128]{2,1,0:T(8,128)(2,1)S(1)} async-done(((bf16[8,768,128]{2,1,0:T(8,128)(2,1)}), bf16[8,768,128]{2,1,0:T(8,128)(2,1)S(1)}, u32[]{:S(2)}, u32[]{:S(2)}) %all-to-all-start) | async-done | bytes 1572896 | tf_op jit(solution)/shard_map/all_to_all | solution.py:315
  74.5 1.2 copy-done.1
  75.7 8.0 %shard_map.94 = (bf16[8,256,128]{2,1,0:T(8,128)(2,1)}, f32[8,256]{1,0:T(8,128)S(1)}) custom-call(bf16[8,768,128]{2,1,0:T(8,128)(2,1)S(1)} %all-to-all-done.packed_ref, s32[2048,1]{1,0:T(8,128)S(1)} %copy-done.1, s32[8,256]{1,0:T(8,128)S(1)} %bitcast.44), custom_call_target="tpu_custom_call" | custom-call | flops 1207959552 | bytes 2097152 | tf_op jit(solution)/shard_map/pallas_call | solution.py:346
  83.7 0.0 copy-done.2
  83.7 9.4 %shard_map.95 = bf16[8,800,128]{2,1,0:T(8,128)(2,1)} custom-call(bf16[8,768,128]{2,1,0:T(8,128)(2,1)S(1)} %all-to-all-done.packed_ref, bf16[8,272,128]{2,1,0:T(8,128)(2,1)S(1)} %all-to-all-done.1.grads_ref, s32[2048,1]{1,0:T(8,128)S(1)} %copy-done.1, s32[8,256]{1,0:T(8,128)S(1)} %bitcast.45, s32[1,256]{1,0:T(1,128)S(1)} %bitcast.46, ...), custom_call_target="tpu_custom_call" | custom-call | flops 3019898880 | bytes 3670016 | tf_op jit(solution)/shard_map/pallas_call | solution.py:364
  93.0 4.4 %all-to-all-start.3 = ((bf16[8,800,128]{2,1,0:T(8,128)(2,1)}), bf16[8,800,128]{2,1,0:T(8,128)(2,1)S(1)}, u32[]{:S(2)}, u32[]{:S(2)}) async-start(bf16[8,800,128]{2,1,0:T(8,128)(2,1)} %shard_map.95), calls=%async_computation.3 | async-start | bytes 3276800 | tf_op jit(solution)/shard_map/all_to_all | solution.py:315
  97.4 38.4 %all-to-all-done.3 = bf16[8,800,128]{2,1,0:T(8,128)(2,1)S(1)} async-done(((bf16[8,800,128]{2,1,0:T(8,128)(2,1)}), bf16[8,800,128]{2,1,0:T(8,128)(2,1)S(1)}, u32[]{:S(2)}, u32[]{:S(2)}) %all-to-all-start.3) | async-done | bytes 1638432 | tf_op jit(solution)/shard_map/all_to_all | solution.py:315
  135.8 4.9 %all-to-all-start.2 = ((bf16[8,256,128]{2,1,0:T(8,128)(2,1)}), bf16[8,256,128]{2,1,0:T(8,128)(2,1)}, u32[]{:S(2)}, u32[]{:S(2)}) async-start(bf16[8,256,128]{2,1,0:T(8,128)(2,1)} %get-tuple-element.5), calls=%async_computation.2 | async-start | bytes 1048576 | tf_op jit(solution)/shard_map/all_to_all | solution.py:315
  140.7 0.0 copy-done.8
  140.7 1.2 slice_bitcast_fusion.2
  141.9 2.3 %copy.21 = bf16[256,8,128]{0,2,1:T(8,128)(2,1)} copy(bf16[256,8,128]{2,0,1:T(8,128)(2,1)} %get-tuple-element.10) | data formatting | bytes 1048576 | tf_op jit(solution)/shard_map/transpose | solution.py:383
  144.1 2.1 %copy.23 = bf16[256,8,128]{0,2,1:T(8,128)(2,1)} copy(bf16[256,8,128]{2,0,1:T(8,128)(2,1)} %get-tuple-element.11) | data formatting | bytes 1048576 | tf_op jit(solution)/shard_map/transpose | solution.py:383
  146.2 2.0 %copy.22 = bf16[256,8,128]{0,2,1:T(8,128)(2,1)} copy(bf16[256,8,128]{2,0,1:T(8,128)(2,1)} %get-tuple-element.12) | data formatting | bytes 1048576 | tf_op jit(solution)/shard_map/transpose | solution.py:383
  148.3 1.9 %fusion.22 = f32[256,1024]{1,0:T(8,128)S(1)} fusion(bf16[256,1024]{0,1:T(8,128)(2,1)} %bitcast.51, bf16[1024,1024]{1,0:T(8,128)(2,1)S(1)} %copy-done.3), kind=kOutput, calls=%fused_computation.38 | convolution fusion | flops 536870912 | bytes 3670016 | tf_op jit(solution)/shard_map/tc,rc->tr/dot_general | solution.py:389
  150.2 0.0 copy-start.7
  150.2 0.0 copy-start.9
  150.2 0.8 convolution_add_fusion.2
  151.0 0.8 copy-done.7
  151.8 0.1 copy-done.9
  151.9 0.8 convolution_add_fusion.1
  152.7 2.4 %fusion.24 = f32[256,1024]{1,0:T(8,128)S(1)} fusion(bf16[256,1024]{0,1:T(8,128)(2,1)S(1)} %bitcast.48, bf16[1024,1024]{1,0:T(8,128)(2,1)} %collective-permute-done.2), kind=kOutput, calls=%fused_computation.40 | convolution fusion | flops 536870912 | bytes 3670016 | tf_op jit(solution)/shard_map/tc,rc->tr/dot_general | solution.py:389
  155.0 2.4 %fusion.23 = f32[256,1024]{1,0:T(8,128)S(1)} fusion(bf16[256,1024]{0,1:T(8,128)(2,1)S(1)} %bitcast.50, bf16[1024,1024]{1,0:T(8,128)(2,1)} %collective-permute-done.1), kind=kOutput, calls=%fused_computation.39 | convolution fusion | flops 536870912 | bytes 3670016 | tf_op jit(solution)/shard_map/tc,rc->tr/dot_general | solution.py:389
  157.5 3.3 %select_convert_fusion = (bf16[256,1024]{1,0:T(8,128)(2,1)}, f32[256,1024]{1,0:T(8,128)S(1)}) fusion(f32[256,1024]{1,0:T(8,128)S(1)} %convolution_add_fusion.1, pred[]{:T(512)S(6)} %eq.3, f32[256,1024]{1,0:T(8,128)S(1)} %fusion.24, f32[256,1024]{1,0:T(8,128)S(1)} %fusion.23, bf16[256,1024]{0,1:T(8,128)(2,1)S(1)} %bitcast.52, ...), kind=kOutput, calls=%fused_computation.14 | convolution fusion | flops 537657344 | bytes 7340033 | tf_op jit(solution)/shard_map/tc,rc->tr/dot_general | solution.py:389
  160.8 1.2 collective-permute-start.3
  162.0 0.0 all-to-all-done.2
  162.0 2.0 %copy.19 = bf16[256,8,128]{0,2,1:T(8,128)(2,1)} copy(bf16[256,8,128]{2,0,1:T(8,128)(2,1)} %bitcast.9) | data formatting | bytes 1048576 | tf_op jit(solution)/shard_map/transpose | solution.py:362
  164.0 2.0 %copy.24 = bf16[256,1024]{1,0:T(8,128)(2,1)} copy(bf16[256,1024]{0,1:T(8,128)(2,1)} %bitcast.57) | data formatting | bytes 1048576
  166.1 1.5 slice_convert_fusion
  167.6 6.9 %collective-permute-done.3 = bf16[256,1024]{1,0:T(8,128)(2,1)} collective-permute-done((bf16[256,1024]{1,0:T(8,128)(2,1)}, bf16[256,1024]{1,0:T(8,128)(2,1)}, u32[]{:S(2)}, u32[]{:S(2)}) %collective-permute-start.3) | collective-permute-done | bytes 524320 | tf_op jit(solution)/shard_map/ppermute | solution.py:398
  174.4 2.1 %add_convert_fusion = bf16[256,1024]{1,0:T(8,128)(2,1)} fusion(bf16[256,1024]{1,0:T(8,128)(2,1)} %collective-permute-done.3, f32[256,1024]{1,0:T(8,128)S(1)} %convolution_add_fusion.1, f32[256,1024]{1,0:T(8,128)S(1)} %get-tuple-element.16, pred[]{:T(512)S(6)} %eq.3), kind=kLoop, calls=%fused_computation.13 | loop fusion | flops 1048576 | bytes 3145729 | tf_op jit(solution)/shard_map/convert_element_type | solution.py:399
  (15 shorter events, 0.0 us)
Async XLA Ops:
  0.6 10.2 %copy-start = (bf16[256,2048]{1,0:T(8,128)(2,1)S(1)}, bf16[256,2048]{1,0:T(8,128)(2,1)}, u32[]{:S(2)}) copy-start(bf16[256,2048]{1,0:T(8,128)(2,1)} %param.7) | copy-start | bytes 3145732
  0.6 15.1 %collective-permute-start = (bf16[1024,1024]{1,0:T(8,128)(2,1)}, bf16[1024,1024]{1,0:T(8,128)(2,1)}, u32[]{:S(2)}, u32[]{:S(2)}) collective-permute-start(bf16[1024,1024]{1,0:T(8,128)(2,1)} %param.8), channel_id=1, source_target_pairs={{0,1},{1,0},{2,3},{3,2},{4,5},{5,4},{6,7},{7,6},{8,9},{9,8},{10,11... | collective-permute-start | bytes 6291464 | tf_op jit(solution)/shard_map/ppermute | solution.py:334
  0.8 20.4 %collective-permute-start.1 = (bf16[1024,1024]{1,0:T(8,128)(2,1)}, bf16[1024,1024]{1,0:T(8,128)(2,1)}, u32[]{:S(2)}, u32[]{:S(2)}) collective-permute-start(bf16[1024,1024]{1,0:T(8,128)(2,1)} %param.9), channel_id=1, source_target_pairs={{0,1},{1,0},{2,3},{3,2},{4,5},{5,4},{6,7},{7,6},{8,9},{9,8},{10,11... | collective-permute-start | bytes 6291464 | tf_op jit(solution)/shard_map/ppermute | solution.py:334
  1.2 25.5 %collective-permute-start.2 = (bf16[1024,1024]{1,0:T(8,128)(2,1)}, bf16[1024,1024]{1,0:T(8,128)(2,1)}, u32[]{:S(2)}, u32[]{:S(2)}) collective-permute-start(bf16[1024,1024]{1,0:T(8,128)(2,1)} %param.10), channel_id=1, source_target_pairs={{0,1},{1,0},{2,3},{3,2},{4,5},{5,4},{6,7},{7,6},{8,9},{9,8},{10,11... | collective-permute-start | bytes 6291464 | tf_op jit(solution)/shard_map/ppermute | solution.py:334
  4.4 28.0 %all-to-all-start.1 = ((bf16[8,272,128]{2,1,0:T(8,128)(2,1)}), bf16[8,272,128]{2,1,0:T(8,128)(2,1)S(1)}, u32[]{:S(2)}, u32[]{:S(2)}) async-start(bf16[8,272,128]{2,1,0:T(8,128)(2,1)} %fusion.5), calls=%async_computation.1 | async-start | bytes 1114112 | tf_op jit(solution)/shard_map/all_to_all | solution.py:315
  10.9 2.5 %copy-start.4 = (bf16[1024,1024]{1,0:T(8,128)(2,1)S(1)}, bf16[1024,1024]{1,0:T(8,128)(2,1)}, u32[]{:S(2)}) copy-start(bf16[1024,1024]{1,0:T(8,128)(2,1)} %param.9) | copy-start | bytes 6291460
  13.3 1.7 copy-start.6
  29.1 1.0 copy-start.12
  32.4 42.1 %all-to-all-start = ((bf16[8,768,128]{2,1,0:T(8,128)(2,1)}), bf16[8,768,128]{2,1,0:T(8,128)(2,1)S(1)}, u32[]{:S(2)}, u32[]{:S(2)}) async-start(bf16[8,768,128]{2,1,0:T(8,128)(2,1)} %pad_maximum_fusion), calls=%async_computation | async-start | bytes 3145728 | tf_op jit(solution)/shard_map/all_to_all | solution.py:315
  74.5 1.2 copy-start.1
  75.7 8.0 %copy-start.2 = (s32[256]{0:T(256)S(1)}, s32[256]{0:T(256)}, u32[]{:S(2)}) copy-start(s32[256]{0:T(256)} %param.11) | copy-start | bytes 3076
  93.0 42.7 %all-to-all-start.3 = ((bf16[8,800,128]{2,1,0:T(8,128)(2,1)}), bf16[8,800,128]{2,1,0:T(8,128)(2,1)S(1)}, u32[]{:S(2)}, u32[]{:S(2)}) async-start(bf16[8,800,128]{2,1,0:T(8,128)(2,1)} %shard_map.95), calls=%async_computation.3 | async-start | bytes 3276800 | tf_op jit(solution)/shard_map/all_to_all | solution.py:315
  135.8 4.9 %copy-start.8 = (bf16[8,800,128]{2,1,0:T(8,128)(2,1)}, bf16[8,800,128]{2,1,0:T(8,128)(2,1)S(1)}, u32[]{:S(2)}) copy-start(bf16[8,800,128]{2,1,0:T(8,128)(2,1)S(1)} %all-to-all-done.3) | copy-start | bytes 4915204
  135.8 26.2 %all-to-all-start.2 = ((bf16[8,256,128]{2,1,0:T(8,128)(2,1)}), bf16[8,256,128]{2,1,0:T(8,128)(2,1)}, u32[]{:S(2)}, u32[]{:S(2)}) async-start(bf16[8,256,128]{2,1,0:T(8,128)(2,1)} %get-tuple-element.5), calls=%async_computation.2 | async-start | bytes 1048576 | tf_op jit(solution)/shard_map/all_to_all | solution.py:315
  141.9 6.4 %copy-start.3 = (bf16[1024,1024]{1,0:T(8,128)(2,1)S(1)}, bf16[1024,1024]{1,0:T(8,128)(2,1)}, u32[]{:S(2)}) copy-start(bf16[1024,1024]{1,0:T(8,128)(2,1)} %param.8) | copy-start | bytes 6291460
  148.2 2.0 %copy-start.5 = (bf16[1024,1024]{1,0:T(8,128)(2,1)S(1)}, bf16[1024,1024]{1,0:T(8,128)(2,1)}, u32[]{:S(2)}) copy-start(bf16[1024,1024]{1,0:T(8,128)(2,1)} %param.9) | copy-start | bytes 6291460
  148.2 2.0 %copy-start.10 = (bf16[256,8,128]{0,2,1:T(8,128)(2,1)S(1)}, bf16[256,8,128]{0,2,1:T(8,128)(2,1)}, u32[]{:S(2)}) copy-start(bf16[256,8,128]{0,2,1:T(8,128)(2,1)} %copy.22) | copy-start | bytes 1572868
  150.2 1.6 copy-start.7
  150.2 1.7 copy-start.9
  155.0 2.4 %copy-start.11 = (bf16[256,8,128]{0,2,1:T(8,128)(2,1)S(1)}, bf16[256,8,128]{0,2,1:T(8,128)(2,1)}, u32[]{:S(2)}) copy-start(bf16[256,8,128]{0,2,1:T(8,128)(2,1)} %copy.21) | copy-start | bytes 1572868
  160.8 13.7 %collective-permute-start.3 = (bf16[256,1024]{1,0:T(8,128)(2,1)}, bf16[256,1024]{1,0:T(8,128)(2,1)}, u32[]{:S(2)}, u32[]{:S(2)}) collective-permute-start(bf16[256,1024]{1,0:T(8,128)(2,1)} %get-tuple-element.15), channel_id=1, source_target_pairs={{0,2},{2,0},{1,3},{3,1},{4,6},{6,4},{5,7},{7,5},{8,10},{10,8},{9,1... | collective-permute-start | bytes 1572872 | tf_op jit(solution)/shard_map/ppermute | solution.py:398

commit v2 on v0

--- a/solution.py
+++ b/solution.py
@@ -3,6 +3,8 @@
 import jax
 import jax.numpy as jnp
 from jax import lax
+from jax.experimental import pallas as pl
+from jax.experimental.pallas import tpu as pltpu
 from jax.sharding import PartitionSpec as P
 
 epsilon = 1e-06
@@ -58,7 +60,7 @@
     return (grad_query, grad_key, grad_value)
 
 
-def per_device(hidden, w_query, w_key, w_value, cluster_rank, assign, d_attended):
+def by_owner(hidden, w_query, w_key, w_value, cluster_rank, assign, d_attended):
     tok_rows = hidden.shape[0]
     heads_here = assign.shape[0]
     head_dim = w_query.shape[1] // heads_here
@@ -185,6 +187,262 @@
     return (attended, d_hidden, centroid_sums)
 
 
+contract_last = (((1,), (1,)), ((), ()))
+contract_first = (((0,), (0,)), ((), ()))
+log2_e = 1.4426950408889634
+vmem_bytes = 48 * 1024 * 1024
+
+
+def pack_kernel(grads_ref, assign_ref, out_ref):
+    blocks, padded, head_dim = out_ref.shape
+    rows = grads_ref.shape[0]
+    spare = padded - rows - rows // head_dim
+    for head in range(blocks):
+        out_ref[head, :rows, :] = grads_ref[:, head * head_dim : (head + 1) * head_dim]
+        ids = assign_ref[head : head + 1, :].astype(jnp.float32)
+        lines = [
+            ids[:, start : start + head_dim] for start in range(0, rows, head_dim)
+        ] + [jnp.zeros((spare, head_dim), jnp.float32)]
+        out_ref[head, rows:, :] = jnp.concatenate(lines, axis=0).astype(jnp.bfloat16)
+
+
+def project_kernel(side_ref, hidden_ref, *refs):
+    out_ref = refs[-1]
+    heads, triple, head_dim = out_ref.shape
+    rows = triple // 3
+    half = refs[0].shape[0]
+    side = side_ref[0]
+    near = hidden_ref[:, pl.ds(pl.multiple_of(side * half, half), half)]
+    far = hidden_ref[:, pl.ds(pl.multiple_of((1 - side) * half, half), half)]
+    for index in range(3):
+        total = jnp.dot(near, refs[index][...], preferred_element_type=jnp.float32)
+        total += jnp.dot(far, refs[3 + index][...], preferred_element_type=jnp.float32)
+        low = total.astype(jnp.bfloat16)
+        for head in range(heads):
+            out_ref[head, index * rows : (index + 1) * rows, :] = low[
+                :, head * head_dim : (head + 1) * head_dim
+            ]
+
+
+def attend_kernel(factor, scale, packed_ref, grads_ref, rank_ref, out_ref, grad_ref, ids_ref, dk_ref, dv_ref):
+    blocks, triple, head_dim = packed_ref.shape
+    rows = triple // 3
+    clusters = rank_ref.shape[1]
+    owned = clusters // blocks
+    id_rows = []
+    for block in range(blocks):
+        lines = grads_ref[block, rows : rows + 16, :].astype(jnp.float32)
+        ids = jnp.concatenate([lines[at : at + 1, :] for at in range(rows // head_dim)], axis=1)
+        id_rows.append(ids)
+        ids_ref[block * rows : (block + 1) * rows, :] = jnp.broadcast_to(ids, (head_dim, rows)).T
+    key_at = lax.broadcasted_iota(jnp.int32, (rows, rows), 0)
+    query_at = lax.broadcasted_iota(jnp.int32, (rows, rows), 1)
+    dk_ref[...] = jnp.zeros_like(dk_ref)
+    dv_ref[...] = jnp.zeros_like(dv_ref)
+    for block in range(blocks):
+        seen = (block + 1) * rows
+        keys_in = packed_ref[: block + 1, rows : 2 * rows, :].reshape(seen, head_dim)
+        values = packed_ref[: block + 1, 2 * rows :, :].reshape(seen, head_dim)
+        query_rows = packed_ref[block, :rows, :]
+        grad_rows = grads_ref[block, :rows, :]
+        scores = lax.dot_general(
+            keys_in, query_rows, contract_last, preferred_element_type=jnp.float32
+        )
+        grad_probs = lax.dot_general(
+            values, grad_rows, contract_last, preferred_element_type=jnp.float32
+        )
+        ids = ids_ref[:seen, :]
+        same = jnp.concatenate(
+            [
+                ids == id_rows[block][:, start : start + head_dim]
+                for start in range(0, rows, head_dim)
+            ],
+            axis=1,
+        )
+        last = same[seen - rows :] & (key_at <= query_at)
+        allowed = last if block == 0 else jnp.concatenate([same[: seen - rows], last], axis=0)
+        scores = jnp.where(allowed, scores * factor, -jnp.inf)
+        top = jnp.max(scores, axis=0, keepdims=True)
+        expd = jnp.exp2(scores - top)
+        total = jnp.sum(expd, axis=0, keepdims=True)
+        probs = expd * (1.0 / total)
+        weighted = probs * grad_probs
+        delta = jnp.sum(weighted, axis=0, keepdims=True)
+        grad_low = (weighted - probs * delta).astype(jnp.bfloat16)
+        probs_low = probs.astype(jnp.bfloat16)
+        flipped = lax.dot_general(
+            values, probs_low, contract_first, preferred_element_type=jnp.float32
+        )
+        out_ref[block] = flipped.T.astype(jnp.bfloat16)
+        dv_ref[:seen, :] += jnp.dot(probs_low, grad_rows, preferred_element_type=jnp.float32)
+        dk_ref[:seen, :] += jnp.dot(grad_low, query_rows, preferred_element_type=jnp.float32)
+        flipped = lax.dot_general(
+            keys_in, grad_low, contract_first, preferred_element_type=jnp.float32
+        )
+        grad_ref[block, :rows, :] = (flipped.T * scale).astype(jnp.bfloat16)
+    grad_ref[:, rows : 2 * rows, :] = (
+        (dk_ref[...] * scale).astype(jnp.bfloat16).reshape(blocks, rows, head_dim)
+    )
+    grad_ref[:, 2 * rows : triple, :] = (
+        dv_ref[...].astype(jnp.bfloat16).reshape(blocks, rows, head_dim)
+    )
+    sums = jnp.zeros((clusters, head_dim), jnp.float32)
+    cluster_at = lax.broadcasted_iota(jnp.int32, (clusters, rows), 0).astype(jnp.float32)
+    for block in range(blocks):
+        keys_float = packed_ref[block, rows : 2 * rows, :].astype(jnp.float32)
+        unit = keys_float * lax.rsqrt(
+            jnp.sum(keys_float * keys_float, axis=1, keepdims=True) + epsilon
+        )
+        unit_high = unit.astype(jnp.bfloat16)
+        unit_low = (unit - unit_high.astype(jnp.float32)).astype(jnp.bfloat16)
+        member = jnp.where(cluster_at == id_rows[block], 1.0, 0.0).astype(jnp.bfloat16)
+        sums += jnp.dot(member, unit_high, preferred_element_type=jnp.float32)
+        sums += jnp.dot(member, unit_low, preferred_element_type=jnp.float32)
+    rank_at = lax.broadcasted_iota(jnp.int32, (clusters, clusters), 0)
+    ordered = jnp.where(rank_at == rank_ref[...], 1.0, 0.0).astype(jnp.bfloat16)
+    ranked = jnp.dot(ordered, sums.astype(jnp.bfloat16), preferred_element_type=jnp.float32)
+    grad_ref[:, triple:, :] = ranked.astype(jnp.bfloat16).reshape(blocks, owned, head_dim)
+
+
+def input_kernel(pick_ref, back_ref, *refs):
+    out_ref, gathered_ref = refs[-2:]
+    blocks, padded, head_dim = back_ref.shape
+    rows = out_ref.shape[0]
+    width = blocks * head_dim
+
+    @pl.when(pl.program_id(0) == 0)
+    def gather():
+        for index in range(3):
+            for head in range(blocks):
+                at = index * width + head * head_dim
+                gathered_ref[:, at : at + head_dim] = back_ref[
+                    head, index * rows : (index + 1) * rows, :
+                ]
+
+    def multiply(first):
+        total = None
+        for index in range(3):
+            term = lax.dot_general(
+                gathered_ref[:, index * width : (index + 1) * width],
+                refs[first + index][...],
+                contract_last,
+                preferred_element_type=jnp.float32,
+            )
+            total = term if total is None else total + term
+        out_ref[...] = total.astype(out_ref.dtype)
+
+    pl.when(pick_ref[0] == 0)(lambda: multiply(0))
+    pl.when(pick_ref[0] != 0)(lambda: multiply(3))
+
+
+def by_head(hidden, w_query, w_key, w_value, cluster_rank, assign, d_attended):
+    rows = hidden.shape[0]
+    blocks = assign.shape[0]
+    half, width = w_query.shape
+    head_dim = width // blocks
+    tokens = blocks * rows
+    clusters = cluster_rank.shape[0]
+    owned = clusters // blocks
+    scale = head_dim ** (-0.5)
+    factor = scale * log2_e
+    line = ("seq", "sub")
+    vmem = pl.BlockSpec(memory_space=pltpu.VMEM)
+    params = pltpu.CompilerParams(vmem_limit_bytes=vmem_bytes)
+    pairs_seen = tokens * (tokens + rows) // 2
+    wide = 2 * head_dim
+
+    def exchange(packed):
+        return lax.all_to_all(packed, line, split_axis=0, concat_axis=0, tiled=True)
+
+    id_rows = -(-(rows // head_dim) // 16) * 16
+    grads = exchange(
+        pl.pallas_call(
+            pack_kernel,
+            out_shape=jax.ShapeDtypeStruct((blocks, rows + id_rows, head_dim), jnp.bfloat16),
+            in_specs=[vmem] * 2,
+            out_specs=vmem,
+            compiler_params=params,
+        )(d_attended, assign)
+    )
+
+    swap = [(0, 1), (1, 0)]
+    side = lax.axis_index("sub")
+    own = (w_query, w_key, w_value)
+    other = tuple(lax.ppermute(piece, "sub", swap) for piece in own)
+    projected = pl.pallas_call(
+        project_kernel,
+        out_shape=jax.ShapeDtypeStruct((blocks, 3 * rows, head_dim), jnp.bfloat16),
+        grid_spec=pltpu.PrefetchScalarGridSpec(
+            num_scalar_prefetch=1,
+            grid=(width // wide,),
+            in_specs=[pl.BlockSpec((rows, 2 * half), lambda step, side_at: (0, 0))]
+            + [pl.BlockSpec((half, wide), lambda step, side_at: (0, step))] * 6,
+            out_specs=pl.BlockSpec((2, 3 * rows, head_dim), lambda step, side_at: (step, 0, 0)),
+        ),
+        compiler_params=params,
+        cost_estimate=pl.CostEstimate(
+            flops=12 * rows * half * width, bytes_accessed=14 * half * width, transcendentals=0
+        ),
+    )(side.reshape(1), hidden, *own, *other)
+    packed = exchange(projected)
+
+    outputs, grads_out = pl.pallas_call(
+        partial(attend_kernel, factor, scale),
+        out_shape=(
+            jax.ShapeDtypeStruct((blocks, rows, head_dim), jnp.bfloat16),
+            jax.ShapeDtypeStruct((blocks, 3 * rows + owned, head_dim), jnp.bfloat16),
+        ),
+        in_specs=[vmem] * 3,
+        out_specs=(vmem, vmem),
+        scratch_shapes=[pltpu.VMEM((tokens, head_dim), jnp.float32)] * 3,
+        compiler_params=params,
+        cost_estimate=pl.CostEstimate(
+            flops=12 * pairs_seen * head_dim,
+            bytes_accessed=16 * tokens * head_dim,
+            transcendentals=pairs_seen,
+        ),
+    )(packed, grads, cluster_rank.reshape(1, clusters))
+    back = exchange(grads_out)
+    returned = exchange(outputs)
+    attended = returned.transpose(1, 0, 2).reshape(rows, width)
+    centroid_sums = back[:, 3 * rows :, :].astype(jnp.float32)
+
+    def input_part(pick, kept_type):
+        def rows_of(first):
+            return lambda step, pick_at: (jnp.where(pick_at[0] == first, step, 0), 0)
+
+        return pl.pallas_call(
+            input_kernel,
+            out_shape=jax.ShapeDtypeStruct((rows, half), kept_type),
+            grid_spec=pltpu.PrefetchScalarGridSpec(
+                num_scalar_prefetch=1,
+                grid=(half // wide,),
+                in_specs=[pl.BlockSpec(back.shape, lambda step, pick_at: (0, 0, 0))]
+                + [pl.BlockSpec((wide, width), rows_of(0))] * 3
+                + [pl.BlockSpec((wide, width), rows_of(1))] * 3,
+                out_specs=pl.BlockSpec((rows, wide), lambda step, pick_at: (0, step)),
+                scratch_shapes=[pltpu.VMEM((rows, 3 * width), jnp.bfloat16)],
+            ),
+            compiler_params=params,
+            cost_estimate=pl.CostEstimate(
+                flops=6 * rows * half * width, bytes_accessed=10 * half * width, transcendentals=0
+            ),
+        )(pick.reshape(1), back, *own, *other)
+
+    crossed = (side != lax.axis_index("head")).astype(jnp.int32)
+    arrived = lax.ppermute(input_part(1 - crossed, jnp.bfloat16), "head", swap)
+    kept = input_part(crossed, jnp.float32)
+    d_hidden = (kept + arrived.astype(jnp.float32)).astype(jnp.bfloat16)
+    return (attended, d_hidden, centroid_sums)
+
+
+def per_device(hidden, w_query, w_key, w_value, cluster_rank, assign, d_attended):
+    owners = lax.axis_size("seq") * lax.axis_size("sub")
+    halves = lax.axis_size("sub") == 2 and lax.axis_size("head") == 2
+    plan = by_head if assign.shape[0] == owners and halves else by_owner
+    return plan(hidden, w_query, w_key, w_value, cluster_rank, assign, d_attended)
+
+
 def solution(mesh):
     placed = (
         P(("groups", "seq", "sub"), None),

time: 372 us -> 154 us (0.41)
  waiting for transfers between devices: 169 us -> 12.2 us
  matrix products: 100 us -> 0 us
  blocking collectives: 0 us -> 83.8 us
  Pallas kernels: 0 us -> 30.6 us
  starting transfers between devices: 42.4 us -> 12.7 us
  local copies, waits for them, and re-layouts: 26.2 us -> 10 us
  other arithmetic: 16.2 us -> 2.65 us
  between operations: 14.2 us -> 0.69 us
    all_to_all x9 -> x2, waiting for transfers between devices: 166 us -> 11.4 us  [exchange(): return lax.all_to_all(packed, line, split_axis=0, concat_axis=0, tiled=True)]
    dot_general x71 -> x0, matrix products: 100 us -> none  [the longest x8 15.3 us: head_backward(): jnp.dot(grad_low, keys_in, preferred_element_type=jnp.float32)]
    all_to_all x0 -> x2, blocking collectives: none -> 83.8 us  [exchange(): return lax.all_to_all(packed, line, split_axis=0, concat_axis=0, tiled=True)]
    all_to_all x9 -> x2, starting transfers between devices: 42.3 us -> 10.6 us  [exchange(): return lax.all_to_all(packed, line, split_axis=0, concat_axis=0, tiled=True)]
    pallas_call x0 -> x5, Pallas kernels: none -> 30.6 us  [the longest x1 11.8 us: by_head(): pl.pallas_call(partial(attend_kernel, factor, scale), out_shape=(jax.Shap...]
    reshape x9 -> x0, local copies, waits for them, and re-layouts: 12.9 us -> none  [the longest x4 4.43 us: to_slots(): return kept.reshape(heads_here, owners, capacity, head_dim)]
    reduce_sum x12 -> x0, other arithmetic: 7.2 us -> none  [the longest x8 4.34 us: head_forward(): row_total = jnp.sum(expd, axis=1)]
    all_to_all x10 -> x0, local copies, waits for them, and re-layouts: 5.7 us -> none  [the longest x2 2.39 us: exchange_three(): lax.all_to_all(first, ('seq', 'sub'), split_axis=1, concat_axis=1, tiled=...]
  transfers between devices with their start and end apart: 14 -> 6, of which waited for: 10 -> 3; matrix products, arithmetic and copies ran while one was open for 15% -> 2% of each run, Pallas kernels for 0% -> 12%
where the time goes in v2:
time: 154 us; the launch traced here: 153 us
  blocking collectives  83.8 us (54%)
  Pallas kernels  30.6 us (20%)
  starting transfers between devices  12.7 us (8%)
  waiting for transfers between devices  12.2 us (8%)
  local copies, waits for them, and re-layouts  10 us (6%)
  other arithmetic  2.65 us (2%)
    all_to_all x2, blocking collectives, exchange(): return lax.all_to_all(packed, line, split_axis=0, concat_axis=0, tiled=True)  83.8 us
    pallas_call x1, Pallas kernels, by_head(): pl.pallas_call(partial(attend_kernel, factor, scale), out_shape=(jax.Shap...  11.8 us
    all_to_all x2, waiting for transfers between devices, exchange(): return lax.all_to_all(packed, line, split_axis=0, concat_axis=0, tiled=True)  11.4 us
    pallas_call x2, Pallas kernels, input_part(): pl.pallas_call(input_kernel, out_shape=jax.ShapeDtypeStruct((rows, half),...  11 us
    all_to_all x2, starting transfers between devices, exchange(): return lax.all_to_all(packed, line, split_axis=0, concat_axis=0, tiled=True)  10.6 us
    unnamed x17, local copies, waits for them, and re-layouts  9.01 us
    pallas_call x1, Pallas kernels, by_head(): pl.pallas_call(project_kernel, out_shape=jax.ShapeDtypeStruct((blocks, 3...  6.8 us
  transfers between devices with their start and end apart: 6, of which 3 were waited for; matrix products, arithmetic and copies ran while one was open for 2% of the time, Pallas kernels for 12%

profile of v2, /device:TPU:1, one launch (start us, length us, event | category | flops | bytes accessed | tf_op | source)
XLA Modules:
  0.0 152.7 jit_solution(6871571940867980350)
XLA Ops:
  0.6 0.0 copy-start
  0.6 0.1 collective-permute-start
  0.8 0.5 collective-permute-start.1
  1.2 0.1 collective-permute-start.2
  1.3 0.0 copy-start.5
  1.3 1.0 copy-done.5
  2.3 0.0 copy-start.6
  2.3 0.7 copy-done.6
  3.0 1.0 shard_map.95
  4.0 6.4 %all-to-all-start.1 = ((bf16[8,272,128]{2,1,0:T(8,128)(2,1)}), bf16[8,272,128]{2,1,0:T(8,128)(2,1)S(1)}, u32[]{:S(2)}, u32[]{:S(2)}) async-start(bf16[8,272,128]{2,1,0:T(8,128)(2,1)} %shard_map.95), calls=%async_computation.1 | async-start | bytes 1114112 | tf_op jit(solution)/shard_map/all_to_all | solution.py:355
  10.4 0.0 collective-permute-done.refs_3_
  10.4 0.0 collective-permute-done.1.refs_4_
  10.4 0.8 collective-permute-done.2.refs_5_
  11.2 0.0 copy-done
  11.2 0.0 copy-start.4
  11.2 1.2 copy-done.4
  12.4 6.8 %shard_map.94 = bf16[8,768,128]{2,1,0:T(8,128)(2,1)S(1)} custom-call(s32[1]{0:T(128)} %bitcast.side_ref, bf16[256,2048]{1,0:T(8,128)(2,1)S(1)} %copy-done.4, bf16[1024,1024]{1,0:T(8,128)(2,1)S(1)} %copy-done, bf16[1024,1024]{1,0:T(8,128)(2,1)} %refs_1_.5, bf16[1024,1024]{1,0:T(8,128)(2,1)} %refs_2_.5, bf16[1024,1024]{1,0:T(8,128)(2,1)} %collective-permute-done.refs_3_, ...), custom_call_target="tpu_custom_call" | custom-call | flops 3221225472 | bytes 14680064 | tf_op jit(solution)/shard_map/pallas_call | solution.py:372
  19.2 0.0 copy-start.3
  19.2 1.1 copy-done.3
  20.4 0.0 copy-start.7
  20.4 5.2 %all-to-all-done.1.grads_ref = bf16[8,272,128]{2,1,0:T(8,128)(2,1)S(1)} async-done(((bf16[8,272,128]{2,1,0:T(8,128)(2,1)}), bf16[8,272,128]{2,1,0:T(8,128)(2,1)S(1)}, u32[]{:S(2)}, u32[]{:S(2)}) %all-to-all-start.1) | async-done | bytes 557088 | tf_op jit(solution)/shard_map/all_to_all | solution.py:355
  25.6 41.1 %all_to_all.20.packed_ref = bf16[8,768,128]{2,1,0:T(8,128)(2,1)S(1)} all-to-all(bf16[8,768,128]{2,1,0:T(8,128)(2,1)} %copy-done.3), channel_id=1, replica_groups=mesh['groups'=2,'seq'=4,'head'=2,'sub'=2] {'seq','sub'}, dimensions={0} | all-to-all | bytes 3145728 | tf_op jit(solution)/shard_map/all_to_all | solution.py:355
  66.8 0.0 copy-done.7
  66.8 11.8 %shard_map.96 = (bf16[8,256,128]{2,1,0:T(8,128)(2,1)}, bf16[8,800,128]{2,1,0:T(8,128)(2,1)S(1)}) custom-call(bf16[8,768,128]{2,1,0:T(8,128)(2,1)S(1)} %all_to_all.20.packed_ref, bf16[8,272,128]{2,1,0:T(8,128)(2,1)S(1)} %all-to-all-done.1.grads_ref, s32[1,256]{1,0:T(1,128)S(1)} %bitcast.6), custom_call_target="tpu_custom_call" | custom-call | flops 3623878656 | bytes 4194304 | tf_op jit(solution)/shard_map/pallas_call | solution.py:389
  78.6 42.6 %all_to_all.21.back_ref = bf16[8,800,128]{2,1,0:T(8,128)(2,1)} all-to-all(bf16[8,800,128]{2,1,0:T(8,128)(2,1)S(1)} %get-tuple-element.6), channel_id=1, replica_groups=mesh['groups'=2,'seq'=4,'head'=2,'sub'=2] {'seq','sub'}, dimensions={0} | all-to-all | bytes 3276800 | tf_op jit(solution)/shard_map/all_to_all | solution.py:355
  121.2 4.1 %all-to-all-start.2 = ((bf16[8,256,128]{2,1,0:T(8,128)(2,1)}), bf16[8,256,128]{2,1,0:T(8,128)(2,1)S(1)}, u32[]{:S(2)}, u32[]{:S(2)}) async-start(bf16[8,256,128]{2,1,0:T(8,128)(2,1)} %get-tuple-element.5), calls=%async_computation.2 | async-start | bytes 1048576 | tf_op jit(solution)/shard_map/all_to_all | solution.py:355
  125.4 0.0 copy-start.1
  125.4 1.4 copy-done.1
  126.8 5.4 %shard_map.98 = bf16[256,1024]{1,0:T(8,128)(2,1)S(1)} custom-call(s32[1]{0:T(128)} %bitcast.5.pick_ref, bf16[8,800,128]{2,1,0:T(8,128)(2,1)S(1)} %copy-done.1, bf16[1024,1024]{1,0:T(8,128)(2,1)S(1)} %copy-done, bf16[1024,1024]{1,0:T(8,128)(2,1)} %refs_1_.5, bf16[1024,1024]{1,0:T(8,128)(2,1)} %refs_2_.5, bf16[1024,1024]{1,0:T(8,128)(2,1)} %collective-permute-done.refs_3_, ...), custom_call_target="tpu_custom_call" | custom-call | flops 1610612736 | bytes 10485760 | tf_op jit(solution)/shard_map/pallas_call | solution.py:414
  132.2 1.5 collective-permute-start.3
  133.7 6.2 %all-to-all-done.2 = bf16[8,256,128]{2,1,0:T(8,128)(2,1)S(1)} async-done(((bf16[8,256,128]{2,1,0:T(8,128)(2,1)}), bf16[8,256,128]{2,1,0:T(8,128)(2,1)S(1)}, u32[]{:S(2)}, u32[]{:S(2)}) %all-to-all-start.2) | async-done | bytes 524320 | tf_op jit(solution)/shard_map/all_to_all | solution.py:355
  139.9 1.0 copy.10
  140.9 2.0 %copy.11 = bf16[256,1024]{1,0:T(8,128)(2,1)} copy(bf16[256,1024]{0,1:T(8,128)(2,1)} %bitcast.8) | data formatting | bytes 1048576
  142.9 0.0 copy-start.2
  142.9 1.4 copy-done.2
  144.4 5.6 %shard_map.97 = f32[256,1024]{1,0:T(8,128)S(1)} custom-call(s32[1]{0:T(128)} %bitcast.4.pick_ref, bf16[8,800,128]{2,1,0:T(8,128)(2,1)S(1)} %copy-done.2, bf16[1024,1024]{1,0:T(8,128)(2,1)S(1)} %copy-done, bf16[1024,1024]{1,0:T(8,128)(2,1)} %refs_1_.5, bf16[1024,1024]{1,0:T(8,128)(2,1)} %refs_2_.5, bf16[1024,1024]{1,0:T(8,128)(2,1)} %collective-permute-done.refs_3_, ...), custom_call_target="tpu_custom_call" | custom-call | flops 1610612736 | bytes 10485760 | tf_op jit(solution)/shard_map/pallas_call | solution.py:414
  150.0 0.7 slice_convert_fusion
  150.7 0.0 collective-permute-done.3
  150.7 2.0 %add_convert_fusion = bf16[256,1024]{1,0:T(8,128)(2,1)} fusion(f32[256,1024]{1,0:T(8,128)S(1)} %shard_map.97, bf16[256,1024]{1,0:T(8,128)(2,1)} %collective-permute-done.3), kind=kLoop, calls=%fused_computation | loop fusion | flops 786432 | bytes 2097152 | tf_op jit(solution)/shard_map/convert_element_type | solution.py:435
Async XLA Ops:
  0.6 10.6 %copy-start = (bf16[1024,1024]{1,0:T(8,128)(2,1)S(1)}, bf16[1024,1024]{1,0:T(8,128)(2,1)}, u32[]{:S(2)}) copy-start(bf16[1024,1024]{1,0:T(8,128)(2,1)} %refs_0_.5) | copy-start | bytes 6291460
  0.6 9.8 %collective-permute-start = (bf16[1024,1024]{1,0:T(8,128)(2,1)}, bf16[1024,1024]{1,0:T(8,128)(2,1)}, u32[]{:S(2)}, u32[]{:S(2)}) collective-permute-start(bf16[1024,1024]{1,0:T(8,128)(2,1)} %refs_0_.5), channel_id=1, source_target_pairs={{0,1},{1,0},{2,3},{3,2},{4,5},{5,4},{6,7},{7,6},{8,9},{9,8},{10,11... | collective-permute-start | bytes 6291464 | tf_op jit(solution)/shard_map/ppermute | solution.py:371
  0.8 9.7 %collective-permute-start.1 = (bf16[1024,1024]{1,0:T(8,128)(2,1)}, bf16[1024,1024]{1,0:T(8,128)(2,1)}, u32[]{:S(2)}, u32[]{:S(2)}) collective-permute-start(bf16[1024,1024]{1,0:T(8,128)(2,1)} %refs_1_.5), channel_id=1, source_target_pairs={{0,1},{1,0},{2,3},{3,2},{4,5},{5,4},{6,7},{7,6},{8,9},{9,8},{10,11... | collective-permute-start | bytes 6291464 | tf_op jit(solution)/shard_map/ppermute | solution.py:371
  1.2 10.0 %collective-permute-start.2 = (bf16[1024,1024]{1,0:T(8,128)(2,1)}, bf16[1024,1024]{1,0:T(8,128)(2,1)}, u32[]{:S(2)}, u32[]{:S(2)}) collective-permute-start(bf16[1024,1024]{1,0:T(8,128)(2,1)} %refs_2_.5), channel_id=1, source_target_pairs={{0,1},{1,0},{2,3},{3,2},{4,5},{5,4},{6,7},{7,6},{8,9},{9,8},{10,11... | collective-permute-start | bytes 6291464 | tf_op jit(solution)/shard_map/ppermute | solution.py:371
  1.3 1.0 copy-start.5
  2.3 0.7 copy-start.6
  4.0 21.6 %all-to-all-start.1 = ((bf16[8,272,128]{2,1,0:T(8,128)(2,1)}), bf16[8,272,128]{2,1,0:T(8,128)(2,1)S(1)}, u32[]{:S(2)}, u32[]{:S(2)}) async-start(bf16[8,272,128]{2,1,0:T(8,128)(2,1)} %shard_map.95), calls=%async_computation.1 | async-start | bytes 1114112 | tf_op jit(solution)/shard_map/all_to_all | solution.py:355
  11.2 1.2 copy-start.4
  19.2 1.1 copy-start.3
  20.4 46.4 %copy-start.7 = (s32[256]{0:T(256)S(1)}, s32[256]{0:T(256)}, u32[]{:S(2)}) copy-start(s32[256]{0:T(256)} %param.11) | copy-start | bytes 3076
  121.2 18.7 %all-to-all-start.2 = ((bf16[8,256,128]{2,1,0:T(8,128)(2,1)}), bf16[8,256,128]{2,1,0:T(8,128)(2,1)S(1)}, u32[]{:S(2)}, u32[]{:S(2)}) async-start(bf16[8,256,128]{2,1,0:T(8,128)(2,1)} %get-tuple-element.5), calls=%async_computation.2 | async-start | bytes 1048576 | tf_op jit(solution)/shard_map/all_to_all | solution.py:355
  125.4 1.4 copy-start.1
  132.2 18.5 %collective-permute-start.3 = (bf16[256,1024]{1,0:T(8,128)(2,1)S(1)}, bf16[256,1024]{1,0:T(8,128)(2,1)}, u32[]{:S(2)}, u32[]{:S(2)}) collective-permute-start(bf16[256,1024]{1,0:T(8,128)(2,1)S(1)} %shard_map.98), channel_id=1, source_target_pairs={{0,2},{2,0},{1,3},{3,1},{4,6},{6,4},{5,7},{7,5},{8,10},{10,8},{9,1... | collective-permute-start | bytes 1572872 | tf_op jit(solution)/shard_map/ppermute | solution.py:433
  142.9 1.4 copy-start.2

commit v3 on v0

--- a/solution.py
+++ b/solution.py
@@ -3,6 +3,8 @@
 import jax
 import jax.numpy as jnp
 from jax import lax
+from jax.experimental import pallas as pl
+from jax.experimental.pallas import tpu as pltpu
 from jax.sharding import PartitionSpec as P
 
 epsilon = 1e-06
@@ -58,7 +60,7 @@
     return (grad_query, grad_key, grad_value)
 
 
-def per_device(hidden, w_query, w_key, w_value, cluster_rank, assign, d_attended):
+def by_owner(hidden, w_query, w_key, w_value, cluster_rank, assign, d_attended):
     tok_rows = hidden.shape[0]
     heads_here = assign.shape[0]
     head_dim = w_query.shape[1] // heads_here
@@ -185,6 +187,392 @@
     return (attended, d_hidden, centroid_sums)
 
 
+contract_last = (((1,), (1,)), ((), ()))
+contract_first = (((0,), (0,)), ((), ()))
+log2_e = 1.4426950408889634
+vmem_bytes = 48 * 1024 * 1024
+
+
+def pack_kernel(place_ref, grads_ref, assign_ref, *out_refs):
+    padded, head_dim = out_refs[0].shape
+    rows = grads_ref.shape[0]
+    spare = padded - rows - rows // head_dim
+    for offset, out_ref in enumerate(out_refs):
+        head = place_ref[0] ^ offset
+        at = pl.multiple_of(head * head_dim, head_dim)
+        out_ref[:rows, :] = grads_ref[:, pl.ds(at, head_dim)]
+        ids = assign_ref[pl.ds(head, 1), :].astype(jnp.float32)
+        lines = [
+            ids[:, start : start + head_dim] for start in range(0, rows, head_dim)
+        ] + [jnp.zeros((spare, head_dim), jnp.float32)]
+        out_ref[rows:, :] = jnp.concatenate(lines, axis=0).astype(jnp.bfloat16)
+
+
+def project_kernel(count, place_ref, hidden_ref, *refs):
+    weights, out_refs = refs[: 2 * count], refs[2 * count :]
+    triple, head_dim = out_refs[0].shape
+    rows = triple // count
+    half = weights[0].shape[0]
+    odd = place_ref[0] % 2
+    near = hidden_ref[:, pl.ds(pl.multiple_of(odd * half, half), half)]
+    far = hidden_ref[:, pl.ds(pl.multiple_of((1 - odd) * half, half), half)]
+    for index in range(count):
+        total = jnp.dot(near, weights[index][...], preferred_element_type=jnp.float32)
+        total += jnp.dot(far, weights[count + index][...], preferred_element_type=jnp.float32)
+        low = total.astype(jnp.bfloat16)
+        first = jnp.where(odd == 0, low[:, :head_dim], low[:, head_dim:])
+        second = jnp.where(odd == 0, low[:, head_dim:], low[:, :head_dim])
+        for pair in range(len(out_refs) // 2):
+
+            @pl.when(pl.program_id(0) == pair)
+            def store(pair=pair, index=index, first=first, second=second):
+                out_refs[2 * pair][index * rows : (index + 1) * rows, :] = first
+                out_refs[2 * pair + 1][index * rows : (index + 1) * rows, :] = second
+
+
+def take_ids(grads_ref, rows):
+    head_dim = grads_ref.shape[1]
+    lines = grads_ref[rows : rows + 16, :].astype(jnp.float32)
+    return jnp.concatenate([lines[at : at + 1, :] for at in range(rows // head_dim)], axis=1)
+
+
+def in_order(place, parts, rows, ordered):
+    for offset, part in enumerate(parts):
+        for index, held in enumerate(ordered):
+            held[place ^ offset] = part[index * rows : (index + 1) * rows, :]
+
+
+def order_ids(place, grads, rows, id_rows, id_cols):
+    for offset, part in enumerate(grads):
+        ids = take_ids(part, rows)
+        id_rows[place ^ offset] = jnp.broadcast_to(ids, id_rows.shape[1:])
+        id_cols[place ^ offset] = jnp.broadcast_to(ids, (id_cols.shape[2], rows)).T
+
+
+def block_scores(factor, block, queries, keys_in, id_rows, id_cols):
+    rows, head_dim = queries.shape[1:]
+    seen = (block + 1) * rows
+    scores = lax.dot_general(
+        keys_in[: block + 1].reshape(seen, head_dim),
+        queries[block],
+        contract_last,
+        preferred_element_type=jnp.float32,
+    )
+    ids = id_cols[: block + 1].reshape(seen, head_dim)
+    mine = id_rows[block][:1, :]
+    same = jnp.concatenate(
+        [ids == mine[:, start : start + head_dim] for start in range(0, rows, head_dim)], axis=1
+    )
+    key_at = lax.broadcasted_iota(jnp.int32, (rows, rows), 0)
+    query_at = lax.broadcasted_iota(jnp.int32, (rows, rows), 1)
+    last = same[seen - rows :] & (key_at <= query_at)
+    allowed = last if block == 0 else jnp.concatenate([same[: seen - rows], last], axis=0)
+    return jnp.where(allowed, scores * factor, -jnp.inf)
+
+
+def value_grad_kernel(factor, count, place_ref, *refs):
+    packed, grads = refs[:count], refs[count : 2 * count]
+    out_refs, lse_ref = refs[2 * count : 3 * count], refs[3 * count]
+    queries, keys_in, grad_rows, id_rows, id_cols, total_ref = refs[3 * count + 1 :]
+    rows, head_dim = queries.shape[1:]
+    place = place_ref[0]
+    in_order(place, packed, rows, (queries, keys_in))
+    in_order(place, grads, rows, (grad_rows,))
+    order_ids(place, grads, rows, id_rows, id_cols)
+    total_ref[...] = jnp.zeros_like(total_ref)
+    for block in range(count):
+        seen = (block + 1) * rows
+        scores = block_scores(factor, block, queries, keys_in, id_rows, id_cols)
+        top = jnp.max(scores, axis=0, keepdims=True)
+        expd = jnp.exp2(scores - top)
+        total = jnp.sum(expd, axis=0, keepdims=True)
+        lse_ref[block : block + 1, :] = top + jnp.log2(total)
+        probs_low = (expd * (1.0 / total)).astype(jnp.bfloat16)
+        total_ref[:seen, :] += jnp.dot(
+            probs_low, grad_rows[block], preferred_element_type=jnp.float32
+        )
+    for offset in range(count):
+        at = pl.multiple_of((place ^ offset) * rows, rows)
+        out_refs[offset][...] = total_ref[pl.ds(at, rows), :].astype(jnp.bfloat16)
+
+
+def query_grad_kernel(factor, scale, count, place_ref, *refs):
+    packed, valued, grads = refs[:count], refs[count : 2 * count], refs[2 * count : 3 * count]
+    lse_ref, rank_ref = refs[3 * count : 3 * count + 2]
+    grad_refs, out_refs = refs[3 * count + 2 : 4 * count + 2], refs[4 * count + 2 : 5 * count + 2]
+    queries, keys_in, values, grad_rows, id_rows, id_cols, total_ref, dq_ref, attended_ref = refs[
+        5 * count + 2 :
+    ]
+    rows, head_dim = queries.shape[1:]
+    clusters = rank_ref.shape[1]
+    owned = clusters // count
+    place = place_ref[0]
+    in_order(place, packed, rows, (queries, keys_in))
+    in_order(place, valued, rows, (values,))
+    in_order(place, grads, rows, (grad_rows,))
+    order_ids(place, grads, rows, id_rows, id_cols)
+    total_ref[...] = jnp.zeros_like(total_ref)
+    for block in range(count):
+        seen = (block + 1) * rows
+        scores = block_scores(factor, block, queries, keys_in, id_rows, id_cols)
+        probs = jnp.exp2(scores - lse_ref[block : block + 1, :])
+        seen_values = values[: block + 1].reshape(seen, head_dim)
+        grad_probs = lax.dot_general(
+            seen_values, grad_rows[block], contract_last, preferred_element_type=jnp.float32
+        )
+        flipped = lax.dot_general(
+            seen_values,
+            probs.astype(jnp.bfloat16),
+            contract_first,
+            preferred_element_type=jnp.float32,
+        )
+        attended_ref[block] = flipped.T.astype(jnp.bfloat16)
+        weighted = probs * grad_probs
+        delta = jnp.sum(weighted, axis=0, keepdims=True)
+        grad_low = (weighted - probs * delta).astype(jnp.bfloat16)
+        total_ref[:seen, :] += jnp.dot(
+            grad_low, queries[block], preferred_element_type=jnp.float32
+        )
+        flipped = lax.dot_general(
+            keys_in[: block + 1].reshape(seen, head_dim),
+            grad_low,
+            contract_first,
+            preferred_element_type=jnp.float32,
+        )
+        dq_ref[block] = (flipped.T * scale).astype(jnp.bfloat16)
+    sums = jnp.zeros((clusters, head_dim), jnp.float32)
+    cluster_at = lax.broadcasted_iota(jnp.int32, (clusters, rows), 0).astype(jnp.float32)
+    for block in range(count):
+        keys_float = keys_in[block].astype(jnp.float32)
+        unit = keys_float * lax.rsqrt(
+            jnp.sum(keys_float * keys_float, axis=1, keepdims=True) + epsilon
+        )
+        unit_high = unit.astype(jnp.bfloat16)
+        unit_low = (unit - unit_high.astype(jnp.float32)).astype(jnp.bfloat16)
+        member = jnp.where(cluster_at == id_rows[block][:1, :], 1.0, 0.0).astype(jnp.bfloat16)
+        sums += jnp.dot(member, unit_high, preferred_element_type=jnp.float32)
+        sums += jnp.dot(member, unit_low, preferred_element_type=jnp.float32)
+    rank_at = lax.broadcasted_iota(jnp.int32, (clusters, clusters), 0)
+    ordered = jnp.where(rank_at == rank_ref[...], 1.0, 0.0).astype(jnp.bfloat16)
+    ranked = jnp.dot(ordered, sums.astype(jnp.bfloat16), preferred_element_type=jnp.float32)
+    ranked_low = ranked.astype(jnp.bfloat16).reshape(count, owned, head_dim)
+    dq_end = rows
+    for part in range(count):
+        attended_ref[count + part, :owned, :] = ranked_low[part]
+    for offset in range(count):
+        owner = place ^ offset
+        at = pl.multiple_of(owner * rows, rows)
+        grad_refs[offset][:dq_end, :] = dq_ref[owner]
+        grad_refs[offset][dq_end:, :] = (total_ref[pl.ds(at, rows), :] * scale).astype(jnp.bfloat16)
+        out_refs[offset][:rows, :] = attended_ref[owner]
+        out_refs[offset][rows:, :] = attended_ref[count + owner, :owned, :]
+
+
+def finish_kernel(count, place_ref, *refs):
+    parts, attended_ref, sums_ref = refs[:count], refs[count], refs[count + 1]
+    rows = attended_ref.shape[0]
+    head_dim = sums_ref.shape[2]
+    for offset, part in enumerate(parts):
+        head = place_ref[0] ^ offset
+        at = pl.multiple_of(head * head_dim, head_dim)
+        attended_ref[:, pl.ds(at, head_dim)] = part[:rows, :]
+        sums_ref[head] = part[rows:, :].astype(jnp.float32)
+
+
+def input_kernel(count, place_ref, *refs):
+    parts, valued, weights = refs[:count], refs[count : 2 * count], refs[2 * count : 2 * count + 6]
+    out_ref, gathered_ref = refs[2 * count + 6 :]
+    rows = out_ref.shape[0]
+    head_dim = parts[0].shape[1]
+    width = count * head_dim
+
+    @pl.when(pl.program_id(0) == 0)
+    def gather():
+        for offset in range(count):
+            at = (place_ref[0] ^ offset) * head_dim
+            for index, piece in enumerate(
+                (parts[offset][:rows, :], parts[offset][rows:, :], valued[offset][...])
+            ):
+                start = pl.multiple_of(index * width + at, head_dim)
+                gathered_ref[:, pl.ds(start, head_dim)] = piece
+
+    def multiply(first):
+        total = None
+        for index in range(3):
+            term = lax.dot_general(
+                gathered_ref[:, index * width : (index + 1) * width],
+                weights[first + index][...],
+                contract_last,
+                preferred_element_type=jnp.float32,
+            )
+            total = term if total is None else total + term
+        out_ref[...] = total.astype(out_ref.dtype)
+
+    pl.when(place_ref[1] == 0)(lambda: multiply(0))
+    pl.when(place_ref[1] != 0)(lambda: multiply(3))
+
+
+def by_head(hidden, w_query, w_key, w_value, cluster_rank, assign, d_attended):
+    rows = hidden.shape[0]
+    count = assign.shape[0]
+    half, width = w_query.shape
+    head_dim = width // count
+    tokens = count * rows
+    clusters = cluster_rank.shape[0]
+    owned = clusters // count
+    scale = head_dim ** (-0.5)
+    factor = scale * log2_e
+    line = ("seq", "sub")
+    smem = pl.BlockSpec(memory_space=pltpu.SMEM)
+    vmem = pl.BlockSpec(memory_space=pltpu.VMEM)
+    params = pltpu.CompilerParams(vmem_limit_bytes=vmem_bytes)
+    pairs_seen = tokens * (tokens + rows) // 2
+    wide = 2 * head_dim
+    side = lax.axis_index("sub")
+    place = lax.axis_index("seq") * 2 + side
+    here = place.reshape(1)
+
+    def buffers(height):
+        return (jax.ShapeDtypeStruct((height, head_dim), jnp.bfloat16),) * count
+
+    def exchange(parts):
+        moved = [
+            lax.ppermute(parts[offset], line, [(at, at ^ offset) for at in range(count)])
+            for offset in range(count - 1, 0, -1)
+        ]
+        return (parts[0], *moved[::-1])
+
+    def scratch(kind):
+        return pltpu.VMEM((count, rows, head_dim), kind)
+
+    id_scratch = [
+        pltpu.VMEM((count, 8, rows), jnp.float32),
+        pltpu.VMEM((count, rows, head_dim), jnp.float32),
+    ]
+    total_scratch = [pltpu.VMEM((tokens, head_dim), jnp.float32)]
+
+    id_height = -(-(rows // head_dim) // 16) * 16
+    grads = exchange(
+        pl.pallas_call(
+            pack_kernel,
+            out_shape=buffers(rows + id_height),
+            in_specs=[smem] + [vmem] * 2,
+            out_specs=(vmem,) * count,
+            compiler_params=params,
+        )(here, d_attended, assign)
+    )
+
+    swap = [(0, 1), (1, 0)]
+    own = (w_query, w_key, w_value)
+    other = tuple(lax.ppermute(piece, "sub", swap) for piece in own)
+
+    def project(mine, theirs):
+        number = len(mine)
+        return pl.pallas_call(
+            partial(project_kernel, number),
+            out_shape=buffers(number * rows),
+            grid_spec=pltpu.PrefetchScalarGridSpec(
+                num_scalar_prefetch=1,
+                grid=(count // 2,),
+                in_specs=[pl.BlockSpec((rows, 2 * half), lambda step, at: (0, 0))]
+                + [pl.BlockSpec((half, wide), lambda step, at: (0, (at[0] // 2) ^ step))]
+                * (2 * number),
+                out_specs=[pl.BlockSpec((number * rows, head_dim), lambda step, at: (0, 0))]
+                * count,
+            ),
+            compiler_params=params,
+            cost_estimate=pl.CostEstimate(
+                flops=4 * number * rows * half * width,
+                bytes_accessed=5 * number * half * width,
+                transcendentals=0,
+            ),
+        )(here, hidden, *mine, *theirs)
+
+    packed = exchange(project(own[:2], other[:2]))
+    valued = exchange(project(own[2:], other[2:]))
+
+    *value_grads, lse = pl.pallas_call(
+        partial(value_grad_kernel, factor, count),
+        out_shape=(*buffers(rows), jax.ShapeDtypeStruct((count, rows), jnp.float32)),
+        in_specs=[smem] + [vmem] * (2 * count),
+        out_specs=(vmem,) * (count + 1),
+        scratch_shapes=[scratch(jnp.bfloat16)] * 3 + id_scratch + total_scratch,
+        compiler_params=params,
+        cost_estimate=pl.CostEstimate(
+            flops=4 * pairs_seen * head_dim,
+            bytes_accessed=8 * tokens * head_dim,
+            transcendentals=pairs_seen,
+        ),
+    )(here, *packed, *grads)
+    value_back = exchange(value_grads)
+
+    results = pl.pallas_call(
+        partial(query_grad_kernel, factor, scale, count),
+        out_shape=(*buffers(2 * rows), *buffers(rows + owned)),
+        in_specs=[smem] + [vmem] * (3 * count + 2),
+        out_specs=(vmem,) * (2 * count),
+        scratch_shapes=[scratch(jnp.bfloat16)] * 4
+        + id_scratch
+        + total_scratch
+        + [scratch(jnp.bfloat16), pltpu.VMEM((2 * count, rows, head_dim), jnp.bfloat16)],
+        compiler_params=params,
+        cost_estimate=pl.CostEstimate(
+            flops=10 * pairs_seen * head_dim,
+            bytes_accessed=14 * tokens * head_dim,
+            transcendentals=pairs_seen,
+        ),
+    )(here, *packed, *valued, *grads, lse, cluster_rank.reshape(1, clusters))
+    back = exchange(results[:count])
+    returned = exchange(results[count:])
+
+    def input_part(pick, kept_type):
+        def rows_of(first):
+            return lambda step, at: (jnp.where(at[1] == first, step, 0), 0)
+
+        return pl.pallas_call(
+            partial(input_kernel, count),
+            out_shape=jax.ShapeDtypeStruct((rows, half), kept_type),
+            grid_spec=pltpu.PrefetchScalarGridSpec(
+                num_scalar_prefetch=1,
+                grid=(half // wide,),
+                in_specs=[pl.BlockSpec((2 * rows, head_dim), lambda step, at: (0, 0))] * count
+                + [pl.BlockSpec((rows, head_dim), lambda step, at: (0, 0))] * count
+                + [pl.BlockSpec((wide, width), rows_of(0))] * 3
+                + [pl.BlockSpec((wide, width), rows_of(1))] * 3,
+                out_specs=pl.BlockSpec((rows, wide), lambda step, at: (0, step)),
+                scratch_shapes=[pltpu.VMEM((rows, 3 * width), jnp.bfloat16)],
+            ),
+            compiler_params=params,
+            cost_estimate=pl.CostEstimate(
+                flops=6 * rows * half * width, bytes_accessed=10 * half * width, transcendentals=0
+            ),
+        )(jnp.stack([place, pick]), *back, *value_back, *own, *other)
+
+    crossed = (side != lax.axis_index("head")).astype(jnp.int32)
+    arrived = lax.ppermute(input_part(1 - crossed, jnp.bfloat16), "head", swap)
+    kept = input_part(crossed, jnp.float32)
+    attended, centroid_sums = pl.pallas_call(
+        partial(finish_kernel, count),
+        out_shape=(
+            jax.ShapeDtypeStruct((rows, width), jnp.bfloat16),
+            jax.ShapeDtypeStruct((count, owned, head_dim), jnp.float32),
+        ),
+        in_specs=[smem] + [vmem] * count,
+        out_specs=(vmem, vmem),
+        compiler_params=params,
+    )(here, *returned)
+    d_hidden = (kept + arrived.astype(jnp.float32)).astype(jnp.bfloat16)
+    return (attended, d_hidden, centroid_sums)
+
+
+def per_device(hidden, w_query, w_key, w_value, cluster_rank, assign, d_attended):
+    owners = lax.axis_size("seq") * lax.axis_size("sub")
+    halves = lax.axis_size("sub") == 2 and lax.axis_size("head") == 2
+    paired = owners & (owners - 1) == 0
+    plan = by_head if assign.shape[0] == owners and halves and paired else by_owner
+    return plan(hidden, w_query, w_key, w_value, cluster_rank, assign, d_attended)
+
+
 def solution(mesh):
     placed = (
         P(("groups", "seq", "sub"), None),

time: 372 us -> 163 us (0.44)
  waiting for transfers between devices: 169 us -> 46.9 us
  matrix products: 100 us -> 0 us
  Pallas kernels: 0 us -> 37.8 us
  starting transfers between devices: 42.4 us -> 62.4 us
  other arithmetic: 16.2 us -> 1.11 us
  local copies, waits for them, and re-layouts: 26.2 us -> 12.5 us
  between operations: 14.2 us -> 0.86 us
    all_to_all x9 -> x0, waiting for transfers between devices: 166 us -> none  [the longest x2 46.5 us: exchange_three(): lax.all_to_all(first, ('seq', 'sub'), split_axis=1, concat_axis=1, tiled=...]
    dot_general x71 -> x0, matrix products: 100 us -> none  [the longest x8 15.3 us: head_backward(): jnp.dot(grad_low, keys_in, preferred_element_type=jnp.float32)]
    ppermute x0 -> x46, starting transfers between devices: none -> 62.4 us  [the longest x42 60.3 us: exchange(): lax.ppermute(parts[offset], line, [(at, at ^ offset) for at in range(coun...]
    ppermute x0 -> x46, waiting for transfers between devices: none -> 46.9 us  [the longest x42 43.5 us: exchange(): lax.ppermute(parts[offset], line, [(at, at ^ offset) for at in range(coun...]
    all_to_all x9 -> x0, starting transfers between devices: 42.3 us -> none  [the longest x2 9.34 us: exchange_three(): lax.all_to_all(third, ('seq', 'sub'), split_axis=1, concat_axis=1, tiled=...]
    pallas_call x0 -> x8, Pallas kernels: none -> 37.8 us  [the longest x2 12.3 us: input_part(): pl.pallas_call(partial(input_kernel, count), out_shape=jax.ShapeDtypeStru...]
    reshape x9 -> x0, local copies, waits for them, and re-layouts: 12.9 us -> none  [the longest x4 4.43 us: to_slots(): return kept.reshape(heads_here, owners, capacity, head_dim)]
    unnamed x29 -> x56, local copies, waits for them, and re-layouts: 4.22 us -> 12.5 us
  transfers between devices with their start and end apart: 14 -> 46, of which waited for: 10 -> 10; matrix products, arithmetic and copies ran while one was open for 15% -> 0% of each run, Pallas kernels for 0% -> 20%
where the time goes in v3:
time: 163 us; the launch traced here: 162 us
  starting transfers between devices  62.4 us (38%)
  waiting for transfers between devices  46.9 us (29%)
  Pallas kernels  37.8 us (23%)
  local copies, waits for them, and re-layouts  12.5 us (8%)
    ppermute x42, starting transfers between devices, exchange(): lax.ppermute(parts[offset], line, [(at, at ^ offset) for at in range(coun...  60.3 us
    ppermute x42, waiting for transfers between devices, exchange(): lax.ppermute(parts[offset], line, [(at, at ^ offset) for at in range(coun...  43.5 us
    unnamed x56, local copies, waits for them, and re-layouts  12.5 us
    pallas_call x2, Pallas kernels, input_part(): pl.pallas_call(partial(input_kernel, count), out_shape=jax.ShapeDtypeStru...  12.3 us
    pallas_call x2, Pallas kernels, project(): pl.pallas_call(partial(project_kernel, number), out_shape=buffers(number...  10.5 us
    pallas_call x1, Pallas kernels, by_head(): pl.pallas_call(partial(query_grad_kernel, factor, scale, count), out_shap...  8.96 us
    pallas_call x1, Pallas kernels, by_head(): pl.pallas_call(partial(value_grad_kernel, factor, count), out_shape=(*buf...  4.94 us
    ppermute x3, waiting for transfers between devices, by_head(): other = tuple((lax.ppermute(piece, 'sub', swap) for piece in own))  3.42 us
  transfers between devices with their start and end apart: 46, of which 10 were waited for; matrix products, arithmetic and copies ran while one was open for 0% of the time, Pallas kernels for 20%

profile of v3, /device:TPU:1, one launch (start us, length us, event | category | flops | bytes accessed | tf_op | source)
XLA Modules:
  0.0 161.6 jit_solution(13829565424848346102)
XLA Ops:
  0.8 0.5 collective-permute-start.1
  1.3 1.0 copy-done.5
  2.3 0.7 copy-done.12
  3.2 0.5 collective-permute-start.17
  3.7 2.4 %collective-permute-start.18 = (bf16[272,128]{1,0:T(8,128)(2,1)S(1)}, bf16[272,128]{1,0:T(8,128)(2,1)S(1)}, u32[]{:S(2)}, u32[]{:S(2)}) collective-permute-start(bf16[272,128]{1,0:T(8,128)(2,1)S(1)} %get-tuple-element.72), channel_id=1, source_target_pairs={{0,4},{1,5},{4,0},{5,1},{8,12},{9,13},{12,8},{13,9},{2,6},{3,7},{6... | collective-permute-start | bytes 208904 | tf_op jit(solution)/shard_map/ppermute | solution.py:440
  6.0 1.8 %collective-permute-start.19 = (bf16[272,128]{1,0:T(8,128)(2,1)S(1)}, bf16[272,128]{1,0:T(8,128)(2,1)S(1)}, u32[]{:S(2)}, u32[]{:S(2)}) collective-permute-start(bf16[272,128]{1,0:T(8,128)(2,1)S(1)} %get-tuple-element.73), channel_id=1, source_target_pairs={{0,5},{1,4},{4,1},{5,0},{8,13},{9,12},{12,9},{13,8},{2,7},{3,6},{6... | collective-permute-start | bytes 208904 | tf_op jit(solution)/shard_map/ppermute | solution.py:440
  7.9 3.4 %collective-permute-done.1.refs_3_.refs_20_ = bf16[1024,1024]{1,0:T(8,128)(2,1)} collective-permute-done((bf16[1024,1024]{1,0:T(8,128)(2,1)}, bf16[1024,1024]{1,0:T(8,128)(2,1)}, u32[]{:S(2)}, u32[]{:S(2)}) %collective-permute-start.1) | collective-permute-done | bytes 2097184 | tf_op jit(solution)/shard_map/ppermute | solution.py:467
  11.3 3.4 %collective-permute-start.20 = (bf16[272,128]{1,0:T(8,128)(2,1)S(1)}, bf16[272,128]{1,0:T(8,128)(2,1)S(1)}, u32[]{:S(2)}, u32[]{:S(2)}) collective-permute-start(bf16[272,128]{1,0:T(8,128)(2,1)S(1)} %get-tuple-element.74), channel_id=1, source_target_pairs={{0,8},{1,9},{4,12},{5,13},{8,0},{9,1},{12,4},{13,5},{2,10},{3,11},... | collective-permute-start | bytes 208904 | tf_op jit(solution)/shard_map/ppermute | solution.py:440
  14.7 1.6 copy-done
  16.3 1.2 copy-done.4
  17.6 7.6 %shard_map.94 = (bf16[512,128]{1,0:T(8,128)(2,1)S(1)}, bf16[512,128]{1,0:T(8,128)(2,1)S(1)}, bf16[512,128]{1,0:T(8,128)(2,1)S(1)}, bf16[512,128]{1,0:T(8,128)(2,...) custom-call(s32[1]{0:T(128)} %bitcast.place_ref, ...), custom_call_target="tpu_custom_call" | custom-call | flops 2147483648 | bytes 10485760 | tf_op jit(solution)/shard_map/pallas_call | solution.py:471
  25.2 0.3 collective-permute-start.21
  25.5 3.7 %collective-permute-start.22 = (bf16[272,128]{1,0:T(8,128)(2,1)S(1)}, bf16[272,128]{1,0:T(8,128)(2,1)S(1)}, u32[]{:S(2)}, u32[]{:S(2)}) collective-permute-start(bf16[272,128]{1,0:T(8,128)(2,1)S(1)} %get-tuple-element.76), channel_id=1, source_target_pairs={{0,12},{1,13},{4,8},{5,9},{8,4},{9,5},{12,0},{13,1},{2,14},{3,15},... | collective-permute-start | bytes 208904 | tf_op jit(solution)/shard_map/ppermute | solution.py:440
  29.7 2.9 %shard_map.95 = (bf16[256,128]{1,0:T(8,128)(2,1)S(1)}, bf16[256,128]{1,0:T(8,128)(2,1)S(1)}, bf16[256,128]{1,0:T(8,128)(2,1)S(1)}, bf16[256,128]{1,0:T(8,128)(2,...) custom-call(s32[1]{0:T(128)} %bitcast.place_ref, ...), custom_call_target="tpu_custom_call" | custom-call | flops 1073741824 | bytes 5242880 | tf_op jit(solution)/shard_map/pallas_call | solution.py:471
  32.6 2.5 %collective-permute-done.21.refs_13_.refs_21_ = bf16[272,128]{1,0:T(8,128)(2,1)S(1)} collective-permute-done((bf16[272,128]{1,0:T(8,128)(2,1)S(1)}, bf16[272,128]{1,0:T(8,128)(2,1)S(1)}, u32[]{:S(2)}, u32[]{:S(2)}) %collective-permute-start.21) | collective-permute-done | bytes 69664 | tf_op jit(solution)/shard_map/ppermute | solution.py:440
  35.1 0.5 collective-permute-start.10
  35.5 1.6 %collective-permute-start.11 = (bf16[256,128]{1,0:T(8,128)(2,1)S(1)}, bf16[256,128]{1,0:T(8,128)(2,1)S(1)}, u32[]{:S(2)}, u32[]{:S(2)}) collective-permute-start(bf16[256,128]{1,0:T(8,128)(2,1)S(1)} %get-tuple-element.64), channel_id=1, source_target_pairs={{0,4},{1,5},{4,0},{5,1},{8,12},{9,13},{12,8},{13,9},{2,6},{3,7},{6... | collective-permute-start | bytes 196616 | tf_op jit(solution)/shard_map/ppermute | solution.py:440
  37.2 1.8 %collective-permute-start.4 = (bf16[512,128]{1,0:T(8,128)(2,1)S(1)}, bf16[512,128]{1,0:T(8,128)(2,1)S(1)}, u32[]{:S(2)}, u32[]{:S(2)}) collective-permute-start(bf16[512,128]{1,0:T(8,128)(2,1)S(1)} %get-tuple-element.57), channel_id=1, source_target_pairs={{0,5},{1,4},{4,1},{5,0},{8,13},{9,12},{12,9},{13,8},{2,7},{3,6},{6... | collective-permute-start | bytes 393224 | tf_op jit(solution)/shard_map/ppermute | solution.py:440
  39.2 2.4 %collective-permute-start.6 = (bf16[512,128]{1,0:T(8,128)(2,1)S(1)}, bf16[512,128]{1,0:T(8,128)(2,1)S(1)}, u32[]{:S(2)}, u32[]{:S(2)}) collective-permute-start(bf16[512,128]{1,0:T(8,128)(2,1)S(1)} %get-tuple-element.59), channel_id=1, source_target_pairs={{0,9},{1,8},{4,13},{5,12},{8,1},{9,0},{12,5},{13,4},{2,11},{3,10},... | collective-permute-start | bytes 393224 | tf_op jit(solution)/shard_map/ppermute | solution.py:440
  41.6 2.3 %collective-permute-start.7 = (bf16[512,128]{1,0:T(8,128)(2,1)S(1)}, bf16[512,128]{1,0:T(8,128)(2,1)S(1)}, u32[]{:S(2)}, u32[]{:S(2)}) collective-permute-start(bf16[512,128]{1,0:T(8,128)(2,1)S(1)} %get-tuple-element.60), channel_id=1, source_target_pairs={{0,12},{1,13},{4,8},{5,9},{8,4},{9,5},{12,0},{13,1},{2,14},{3,15},... | collective-permute-start | bytes 393224 | tf_op jit(solution)/shard_map/ppermute | solution.py:440
  43.9 1.3 collective-permute-start.8
  45.2 11.1 %collective-permute-done.5.refs_4_ = bf16[512,128]{1,0:T(8,128)(2,1)S(1)} collective-permute-done((bf16[512,128]{1,0:T(8,128)(2,1)S(1)}, bf16[512,128]{1,0:T(8,128)(2,1)S(1)}, u32[]{:S(2)}, u32[]{:S(2)}) %collective-permute-start.5) | collective-permute-done | bytes 131104 | tf_op jit(solution)/shard_map/ppermute | solution.py:440
  56.3 4.7 %collective-permute-done.6.refs_5_ = bf16[512,128]{1,0:T(8,128)(2,1)S(1)} collective-permute-done((bf16[512,128]{1,0:T(8,128)(2,1)S(1)}, bf16[512,128]{1,0:T(8,128)(2,1)S(1)}, u32[]{:S(2)}, u32[]{:S(2)}) %collective-permute-start.6) | collective-permute-done | bytes 131104 | tf_op jit(solution)/shard_map/ppermute | solution.py:440
  61.1 2.5 %collective-permute-start.16 = (bf16[256,128]{1,0:T(8,128)(2,1)S(1)}, bf16[256,128]{1,0:T(8,128)(2,1)S(1)}, u32[]{:S(2)}, u32[]{:S(2)}) collective-permute-start(bf16[256,128]{1,0:T(8,128)(2,1)S(1)} %get-tuple-element.69), channel_id=1, source_target_pairs={{0,13},{1,12},{4,9},{5,8},{8,5},{9,4},{12,1},{13,0},{2,15},{3,14},... | collective-permute-start | bytes 196616 | tf_op jit(solution)/shard_map/ppermute | solution.py:440
  63.5 4.9 %shard_map.97 = (bf16[256,128]{1,0:T(8,128)(2,1)S(1)}, bf16[256,128]{1,0:T(8,128)(2,1)S(1)}, bf16[256,128]{1,0:T(8,128)(2,1)S(1)}, bf16[256,128]{1,0:T(8,128)(2,...) custom-call(s32[1]{0:T(128)} %bitcast.place_ref, ...), custom_call_target="tpu_custom_call" | custom-call | flops 1207959552 | bytes 2097152 | tf_op jit(solution)/shard_map/pallas_call | solution.py:494
  68.5 1.3 collective-permute-start.38
  69.7 1.9 %collective-permute-done.13.refs_12_ = bf16[256,128]{1,0:T(8,128)(2,1)S(1)} collective-permute-done((bf16[256,128]{1,0:T(8,128)(2,1)S(1)}, bf16[256,128]{1,0:T(8,128)(2,1)S(1)}, u32[]{:S(2)}, u32[]{:S(2)}) %collective-permute-start.13) | collective-permute-done | bytes 65568 | tf_op jit(solution)/shard_map/ppermute | solution.py:440
  71.6 4.7 %collective-permute-start.39 = (bf16[256,128]{1,0:T(8,128)(2,1)S(1)}, bf16[256,128]{1,0:T(8,128)(2,1)S(1)}, u32[]{:S(2)}, u32[]{:S(2)}) collective-permute-start(bf16[256,128]{1,0:T(8,128)(2,1)S(1)} %get-tuple-element.98), channel_id=1, source_target_pairs={{0,4},{1,5},{4,0},{5,1},{8,12},{9,13},{12,8},{13,9},{2,6},{3,7},{6... | collective-permute-start | bytes 196616 | tf_op jit(solution)/shard_map/ppermute | solution.py:440
  76.3 0.3 collective-permute-start.40
  76.6 2.8 %collective-permute-start.41 = (bf16[256,128]{1,0:T(8,128)(2,1)S(1)}, bf16[256,128]{1,0:T(8,128)(2,1)S(1)}, u32[]{:S(2)}, u32[]{:S(2)}) collective-permute-start(bf16[256,128]{1,0:T(8,128)(2,1)S(1)} %get-tuple-element.100), channel_id=1, source_target_pairs={{0,8},{1,9},{4,12},{5,13},{8,0},{9,1},{12,4},{13,5},{2,10},{3,11},... | collective-permute-start | bytes 196616 | tf_op jit(solution)/shard_map/ppermute | solution.py:440
  79.5 9.0 %shard_map.98 = (bf16[512,128]{1,0:T(8,128)(2,1)S(1)}, bf16[512,128]{1,0:T(8,128)(2,1)S(1)}, bf16[512,128]{1,0:T(8,128)(2,1)S(1)}, bf16[512,128]{1,0:T(8,128)(2,...) custom-call(s32[1]{0:T(128)} %bitcast.place_ref, ...), custom_call_target="tpu_custom_call" | custom-call | flops 3019898880 | bytes 3670016 | tf_op jit(solution)/shard_map/pallas_call | solution.py:509
  88.4 0.6 copy-done.10
  89.1 0.6 copy-done.13
  89.7 0.6 copy-done.15
  90.3 0.6 copy-done.17
  90.9 0.6 copy-done.19
  91.6 0.7 copy-done.21
  92.2 0.6 copy-done.23
  92.9 0.6 copy-done.25
  93.5 0.4 collective-permute-start.31
  94.0 1.4 collective-permute-start.42
  95.4 2.3 %collective-permute-start.43 = (bf16[256,128]{1,0:T(8,128)(2,1)S(1)}, bf16[256,128]{1,0:T(8,128)(2,1)S(1)}, u32[]{:S(2)}, u32[]{:S(2)}) collective-permute-start(bf16[256,128]{1,0:T(8,128)(2,1)S(1)} %get-tuple-element.102), channel_id=1, source_target_pairs={{0,12},{1,13},{4,8},{5,9},{8,4},{9,5},{12,0},{13,1},{2,14},{3,15},... | collective-permute-start | bytes 196616 | tf_op jit(solution)/shard_map/ppermute | solution.py:440
  97.7 1.0 collective-permute-start.44
  98.7 3.4 %collective-permute-done.42.refs_13_ = bf16[256,128]{1,0:T(8,128)(2,1)S(1)} collective-permute-done((bf16[256,128]{1,0:T(8,128)(2,1)S(1)}, bf16[256,128]{1,0:T(8,128)(2,1)S(1)}, u32[]{:S(2)}, u32[]{:S(2)}) %collective-permute-start.42) | collective-permute-done | bytes 65568 | tf_op jit(solution)/shard_map/ppermute | solution.py:440
  102.1 0.6 copy-done.6
  102.7 1.6 collective-permute-start.34
  104.3 0.6 copy-done.8
  104.9 2.2 %collective-permute-start.35 = (bf16[512,128]{1,0:T(8,128)(2,1)}, bf16[512,128]{1,0:T(8,128)(2,1)S(1)}, u32[]{:S(2)}, u32[]{:S(2)}) collective-permute-start(bf16[512,128]{1,0:T(8,128)(2,1)} %get-tuple-element.93), channel_id=1, source_target_pairs={{0,9},{1,8},{4,13},{5,12},{8,1},{9,0},{12,5},{13,4},{2,11},{3,10},... | collective-permute-start | bytes 393224 | tf_op jit(solution)/shard_map/ppermute | solution.py:440
  107.2 2.1 %collective-permute-start.36 = (bf16[512,128]{1,0:T(8,128)(2,1)}, bf16[512,128]{1,0:T(8,128)(2,1)S(1)}, u32[]{:S(2)}, u32[]{:S(2)}) collective-permute-start(bf16[512,128]{1,0:T(8,128)(2,1)} %get-tuple-element.94), channel_id=1, source_target_pairs={{0,12},{1,13},{4,8},{5,9},{8,4},{9,5},{12,0},{13,1},{2,14},{3,15},... | collective-permute-start | bytes 393224 | tf_op jit(solution)/shard_map/ppermute | solution.py:440
  109.2 1.8 %collective-permute-start.37 = (bf16[512,128]{1,0:T(8,128)(2,1)}, bf16[512,128]{1,0:T(8,128)(2,1)S(1)}, u32[]{:S(2)}, u32[]{:S(2)}) collective-permute-start(bf16[512,128]{1,0:T(8,128)(2,1)} %get-tuple-element.95), channel_id=1, source_target_pairs={{0,13},{1,12},{4,9},{5,8},{8,5},{9,4},{12,1},{13,0},{2,15},{3,14},... | collective-permute-start | bytes 393224 | tf_op jit(solution)/shard_map/ppermute | solution.py:440
  111.1 12.8 %collective-permute-done.35.refs_5_ = bf16[512,128]{1,0:T(8,128)(2,1)S(1)} collective-permute-done((bf16[512,128]{1,0:T(8,128)(2,1)}, bf16[512,128]{1,0:T(8,128)(2,1)S(1)}, u32[]{:S(2)}, u32[]{:S(2)}) %collective-permute-start.35) | collective-permute-done | bytes 131104 | tf_op jit(solution)/shard_map/ppermute | solution.py:440
  124.0 0.8 copy-done.7
  124.8 0.8 copy-done.9
  125.7 6.0 %shard_map.101 = bf16[256,1024]{1,0:T(8,128)(2,1)S(1)} custom-call(s32[2]{0:T(128)S(1)} %pad_add_fusion.1.place_ref, bf16[512,128]{1,0:T(8,128)(2,1)S(1)} %get-tuple-element.88.refs_0_, bf16[512,128]{1,0:T(8,128)(2,1)S(1)} %collective-permute-done.31.refs_1_, bf16[512,128]{1,0:T(8,128)(2,1)S(1)} %collective-permute-done.32.refs_2_, ...), custom_call_target="tpu_custom_call" | custom-call | flops 1610612736 | bytes 10485760 | tf_op jit(solution)/shard_map/pallas_call | solution.py:532
  131.7 1.5 collective-permute-start.45
  133.2 5.7 %collective-permute-start.25 = (bf16[288,128]{1,0:T(8,128)(2,1)S(1)}, bf16[288,128]{1,0:T(8,128)(2,1)S(1)}, u32[]{:S(2)}, u32[]{:S(2)}) collective-permute-start(bf16[288,128]{1,0:T(8,128)(2,1)S(1)} %copy-done.24), channel_id=1, source_target_pairs={{0,4},{1,5},{4,0},{5,1},{8,12},{9,13},{12,8},{13,9},{2,6},{3,7},{6... | collective-permute-start | bytes 221192 | tf_op jit(solution)/shard_map/ppermute | solution.py:440
  139.1 2.9 %collective-permute-start.27 = (bf16[288,128]{1,0:T(8,128)(2,1)S(1)}, bf16[288,128]{1,0:T(8,128)(2,1)S(1)}, u32[]{:S(2)}, u32[]{:S(2)}) collective-permute-start(bf16[288,128]{1,0:T(8,128)(2,1)S(1)} %copy-done.20), channel_id=1, source_target_pairs={{0,8},{1,9},{4,12},{5,13},{8,0},{9,1},{12,4},{13,5},{2,10},{3,11},... | collective-permute-start | bytes 221192 | tf_op jit(solution)/shard_map/ppermute | solution.py:440
  142.1 2.4 %collective-permute-start.29 = (bf16[288,128]{1,0:T(8,128)(2,1)S(1)}, bf16[288,128]{1,0:T(8,128)(2,1)S(1)}, u32[]{:S(2)}, u32[]{:S(2)}) collective-permute-start(bf16[288,128]{1,0:T(8,128)(2,1)S(1)} %copy-done.16), channel_id=1, source_target_pairs={{0,12},{1,13},{4,8},{5,9},{8,4},{9,5},{12,0},{13,1},{2,14},{3,15},... | collective-permute-start | bytes 221192 | tf_op jit(solution)/shard_map/ppermute | solution.py:440
  144.5 0.7 collective-permute-done.26.refs_3_
  145.2 2.2 %collective-permute-start.30 = (bf16[288,128]{1,0:T(8,128)(2,1)S(1)}, bf16[288,128]{1,0:T(8,128)(2,1)S(1)}, u32[]{:S(2)}, u32[]{:S(2)}) collective-permute-start(bf16[288,128]{1,0:T(8,128)(2,1)S(1)} %copy-done.14), channel_id=1, source_target_pairs={{0,13},{1,12},{4,9},{5,8},{8,5},{9,4},{12,1},{13,0},{2,15},{3,14},... | collective-permute-start | bytes 221192 | tf_op jit(solution)/shard_map/ppermute | solution.py:440
  147.5 5.9 %collective-permute-done.28.refs_5_ = bf16[288,128]{1,0:T(8,128)(2,1)S(1)} collective-permute-done((bf16[288,128]{1,0:T(8,128)(2,1)S(1)}, bf16[288,128]{1,0:T(8,128)(2,1)S(1)}, u32[]{:S(2)}, u32[]{:S(2)}) %collective-permute-start.28) | collective-permute-done | bytes 73760 | tf_op jit(solution)/shard_map/ppermute | solution.py:440
  153.4 1.0 shard_map.99
  154.4 6.2 %shard_map.100 = f32[256,1024]{1,0:T(8,128)S(1)} custom-call(s32[2]{0:T(128)S(1)} %pad_add_fusion.place_ref, bf16[512,128]{1,0:T(8,128)(2,1)S(1)} %get-tuple-element.88.refs_0_, bf16[512,128]{1,0:T(8,128)(2,1)S(1)} %collective-permute-done.31.refs_1_, bf16[512,128]{1,0:T(8,128)(2,1)S(1)} %collective-permute-done.32.refs_2_, ...), custom_call_target="tpu_custom_call" | custom-call | flops 1610612736 | bytes 10485760 | tf_op jit(solution)/shard_map/pallas_call | solution.py:532
  160.7 1.0 add_convert_fusion
  (95 shorter events, 1.8 us)
Async XLA Ops:
  0.6 5.4 %collective-permute-start = (bf16[1024,1024]{1,0:T(8,128)(2,1)}, bf16[1024,1024]{1,0:T(8,128)(2,1)}, u32[]{:S(2)}, u32[]{:S(2)}) collective-permute-start(bf16[1024,1024]{1,0:T(8,128)(2,1)} %refs_16_.3), channel_id=1, source_target_pairs={{0,1},{1,0},{2,3},{3,2},{4,5},{5,4},{6,7},{7,6},{8,9},{9,8},{10,11... | collective-permute-start | bytes 6291464 | tf_op jit(solution)/shard_map/ppermute | solution.py:467
  0.8 10.5 %collective-permute-start.1 = (bf16[1024,1024]{1,0:T(8,128)(2,1)}, bf16[1024,1024]{1,0:T(8,128)(2,1)}, u32[]{:S(2)}, u32[]{:S(2)}) collective-permute-start(bf16[1024,1024]{1,0:T(8,128)(2,1)} %refs_17_.3), channel_id=1, source_target_pairs={{0,1},{1,0},{2,3},{3,2},{4,5},{5,4},{6,7},{7,6},{8,9},{9,8},{10,11... | collective-permute-start | bytes 6291464 | tf_op jit(solution)/shard_map/ppermute | solution.py:467
  1.2 28.5 %collective-permute-start.9 = (bf16[1024,1024]{1,0:T(8,128)(2,1)}, bf16[1024,1024]{1,0:T(8,128)(2,1)S(1)}, u32[]{:S(2)}, u32[]{:S(2)}) collective-permute-start(bf16[1024,1024]{1,0:T(8,128)(2,1)} %refs_18_.3), channel_id=1, source_target_pairs={{0,1},{1,0},{2,3},{3,2},{4,5},{5,4},{6,7},{7,6},{8,9},{9,8},{10,11... | collective-permute-start | bytes 6291464 | tf_op jit(solution)/shard_map/ppermute | solution.py:467
  1.3 1.0 copy-start.5
  2.3 0.7 copy-start.12
  3.2 22.0 %collective-permute-start.17 = (bf16[272,128]{1,0:T(8,128)(2,1)S(1)}, bf16[272,128]{1,0:T(8,128)(2,1)S(1)}, u32[]{:S(2)}, u32[]{:S(2)}) collective-permute-start(bf16[272,128]{1,0:T(8,128)(2,1)S(1)} %get-tuple-element.71), channel_id=1, source_target_pairs={{0,1},{1,0},{4,5},{5,4},{8,9},{9,8},{12,13},{13,12},{2,3},{3,2},{6... | collective-permute-start | bytes 208904 | tf_op jit(solution)/shard_map/ppermute | solution.py:440
  3.7 21.9 %collective-permute-start.18 = (bf16[272,128]{1,0:T(8,128)(2,1)S(1)}, bf16[272,128]{1,0:T(8,128)(2,1)S(1)}, u32[]{:S(2)}, u32[]{:S(2)}) collective-permute-start(bf16[272,128]{1,0:T(8,128)(2,1)S(1)} %get-tuple-element.72), channel_id=1, source_target_pairs={{0,4},{1,5},{4,0},{5,1},{8,12},{9,13},{12,8},{13,9},{2,6},{3,7},{6... | collective-permute-start | bytes 208904 | tf_op jit(solution)/shard_map/ppermute | solution.py:440
  6.0 23.1 %collective-permute-start.19 = (bf16[272,128]{1,0:T(8,128)(2,1)S(1)}, bf16[272,128]{1,0:T(8,128)(2,1)S(1)}, u32[]{:S(2)}, u32[]{:S(2)}) collective-permute-start(bf16[272,128]{1,0:T(8,128)(2,1)S(1)} %get-tuple-element.73), channel_id=1, source_target_pairs={{0,5},{1,4},{4,1},{5,0},{8,13},{9,12},{12,9},{13,8},{2,7},{3,6},{6... | collective-permute-start | bytes 208904 | tf_op jit(solution)/shard_map/ppermute | solution.py:440
  11.3 18.1 %collective-permute-start.20 = (bf16[272,128]{1,0:T(8,128)(2,1)S(1)}, bf16[272,128]{1,0:T(8,128)(2,1)S(1)}, u32[]{:S(2)}, u32[]{:S(2)}) collective-permute-start(bf16[272,128]{1,0:T(8,128)(2,1)S(1)} %get-tuple-element.74), channel_id=1, source_target_pairs={{0,8},{1,9},{4,12},{5,13},{8,0},{9,1},{12,4},{13,5},{2,10},{3,11},... | collective-permute-start | bytes 208904 | tf_op jit(solution)/shard_map/ppermute | solution.py:440
  14.7 1.6 copy-start
  16.3 1.2 copy-start.4
  17.6 12.1 %copy-start.2 = (bf16[1024,1024]{1,0:T(8,128)(2,1)S(1)}, bf16[1024,1024]{1,0:T(8,128)(2,1)}, u32[]{:S(2)}) copy-start(bf16[1024,1024]{1,0:T(8,128)(2,1)} %refs_18_.3) | copy-start | bytes 6291460
  25.2 9.9 %collective-permute-start.21 = (bf16[272,128]{1,0:T(8,128)(2,1)S(1)}, bf16[272,128]{1,0:T(8,128)(2,1)S(1)}, u32[]{:S(2)}, u32[]{:S(2)}) collective-permute-start(bf16[272,128]{1,0:T(8,128)(2,1)S(1)} %get-tuple-element.75), channel_id=1, source_target_pairs={{0,9},{1,8},{4,13},{5,12},{8,1},{9,0},{12,5},{13,4},{2,11},{3,10},... | collective-permute-start | bytes 208904 | tf_op jit(solution)/shard_map/ppermute | solution.py:440
  25.5 10.0 %collective-permute-start.22 = (bf16[272,128]{1,0:T(8,128)(2,1)S(1)}, bf16[272,128]{1,0:T(8,128)(2,1)S(1)}, u32[]{:S(2)}, u32[]{:S(2)}) collective-permute-start(bf16[272,128]{1,0:T(8,128)(2,1)S(1)} %get-tuple-element.76), channel_id=1, source_target_pairs={{0,12},{1,13},{4,8},{5,9},{8,4},{9,5},{12,0},{13,1},{2,14},{3,15},... | collective-permute-start | bytes 208904 | tf_op jit(solution)/shard_map/ppermute | solution.py:440
  29.2 8.0 %collective-permute-start.23 = (bf16[272,128]{1,0:T(8,128)(2,1)S(1)}, bf16[272,128]{1,0:T(8,128)(2,1)S(1)}, u32[]{:S(2)}, u32[]{:S(2)}) collective-permute-start(bf16[272,128]{1,0:T(8,128)(2,1)S(1)} %get-tuple-element.77), channel_id=1, source_target_pairs={{0,13},{1,12},{4,9},{5,8},{8,5},{9,4},{12,1},{13,0},{2,15},{3,14},... | collective-permute-start | bytes 208904 | tf_op jit(solution)/shard_map/ppermute | solution.py:440
  29.4 12.1 %collective-permute-start.2 = (bf16[512,128]{1,0:T(8,128)(2,1)S(1)}, bf16[512,128]{1,0:T(8,128)(2,1)S(1)}, u32[]{:S(2)}, u32[]{:S(2)}) collective-permute-start(bf16[512,128]{1,0:T(8,128)(2,1)S(1)} %get-tuple-element.55), channel_id=1, source_target_pairs={{0,1},{1,0},{4,5},{5,4},{8,9},{9,8},{12,13},{13,12},{2,3},{3,2},{6... | collective-permute-start | bytes 393224 | tf_op jit(solution)/shard_map/ppermute | solution.py:440
  29.7 2.9 %copy-start.3 = (bf16[1024,1024]{1,0:T(8,128)(2,1)}, bf16[1024,1024]{1,0:T(8,128)(2,1)S(1)}, u32[]{:S(2)}) copy-start(bf16[1024,1024]{1,0:T(8,128)(2,1)S(1)} %collective-permute-done.9.refs_1_.refs_21_) | copy-start | bytes 6291460
  29.7 14.2 %collective-permute-start.3 = (bf16[512,128]{1,0:T(8,128)(2,1)S(1)}, bf16[512,128]{1,0:T(8,128)(2,1)S(1)}, u32[]{:S(2)}, u32[]{:S(2)}) collective-permute-start(bf16[512,128]{1,0:T(8,128)(2,1)S(1)} %get-tuple-element.56), channel_id=1, source_target_pairs={{0,4},{1,5},{4,0},{5,1},{8,12},{9,13},{12,8},{13,9},{2,6},{3,7},{6... | collective-permute-start | bytes 393224 | tf_op jit(solution)/shard_map/ppermute | solution.py:440
  35.1 3.9 %collective-permute-start.10 = (bf16[256,128]{1,0:T(8,128)(2,1)S(1)}, bf16[256,128]{1,0:T(8,128)(2,1)S(1)}, u32[]{:S(2)}, u32[]{:S(2)}) collective-permute-start(bf16[256,128]{1,0:T(8,128)(2,1)S(1)} %get-tuple-element.63), channel_id=1, source_target_pairs={{0,1},{1,0},{4,5},{5,4},{8,9},{9,8},{12,13},{13,12},{2,3},{3,2},{6... | collective-permute-start | bytes 196616 | tf_op jit(solution)/shard_map/ppermute | solution.py:440
  35.5 3.7 %collective-permute-start.11 = (bf16[256,128]{1,0:T(8,128)(2,1)S(1)}, bf16[256,128]{1,0:T(8,128)(2,1)S(1)}, u32[]{:S(2)}, u32[]{:S(2)}) collective-permute-start(bf16[256,128]{1,0:T(8,128)(2,1)S(1)} %get-tuple-element.64), channel_id=1, source_target_pairs={{0,4},{1,5},{4,0},{5,1},{8,12},{9,13},{12,8},{13,9},{2,6},{3,7},{6... | collective-permute-start | bytes 196616 | tf_op jit(solution)/shard_map/ppermute | solution.py:440
  37.2 8.0 %collective-permute-start.4 = (bf16[512,128]{1,0:T(8,128)(2,1)S(1)}, bf16[512,128]{1,0:T(8,128)(2,1)S(1)}, u32[]{:S(2)}, u32[]{:S(2)}) collective-permute-start(bf16[512,128]{1,0:T(8,128)(2,1)S(1)} %get-tuple-element.57), channel_id=1, source_target_pairs={{0,5},{1,4},{4,1},{5,0},{8,13},{9,12},{12,9},{13,8},{2,7},{3,6},{6... | collective-permute-start | bytes 393224 | tf_op jit(solution)/shard_map/ppermute | solution.py:440
  38.9 17.4 %collective-permute-start.5 = (bf16[512,128]{1,0:T(8,128)(2,1)S(1)}, bf16[512,128]{1,0:T(8,128)(2,1)S(1)}, u32[]{:S(2)}, u32[]{:S(2)}) collective-permute-start(bf16[512,128]{1,0:T(8,128)(2,1)S(1)} %get-tuple-element.58), channel_id=1, source_target_pairs={{0,8},{1,9},{4,12},{5,13},{8,0},{9,1},{12,4},{13,5},{2,10},{3,11},... | collective-permute-start | bytes 393224 | tf_op jit(solution)/shard_map/ppermute | solution.py:440
  39.2 21.8 %collective-permute-start.6 = (bf16[512,128]{1,0:T(8,128)(2,1)S(1)}, bf16[512,128]{1,0:T(8,128)(2,1)S(1)}, u32[]{:S(2)}, u32[]{:S(2)}) collective-permute-start(bf16[512,128]{1,0:T(8,128)(2,1)S(1)} %get-tuple-element.59), channel_id=1, source_target_pairs={{0,9},{1,8},{4,13},{5,12},{8,1},{9,0},{12,5},{13,4},{2,11},{3,10},... | collective-permute-start | bytes 393224 | tf_op jit(solution)/shard_map/ppermute | solution.py:440
  41.6 19.4 %collective-permute-start.7 = (bf16[512,128]{1,0:T(8,128)(2,1)S(1)}, bf16[512,128]{1,0:T(8,128)(2,1)S(1)}, u32[]{:S(2)}, u32[]{:S(2)}) collective-permute-start(bf16[512,128]{1,0:T(8,128)(2,1)S(1)} %get-tuple-element.60), channel_id=1, source_target_pairs={{0,12},{1,13},{4,8},{5,9},{8,4},{9,5},{12,0},{13,1},{2,14},{3,15},... | collective-permute-start | bytes 393224 | tf_op jit(solution)/shard_map/ppermute | solution.py:440
  43.9 17.2 %collective-permute-start.8 = (bf16[512,128]{1,0:T(8,128)(2,1)S(1)}, bf16[512,128]{1,0:T(8,128)(2,1)S(1)}, u32[]{:S(2)}, u32[]{:S(2)}) collective-permute-start(bf16[512,128]{1,0:T(8,128)(2,1)S(1)} %get-tuple-element.61), channel_id=1, source_target_pairs={{0,13},{1,12},{4,9},{5,8},{8,5},{9,4},{12,1},{13,0},{2,15},{3,14},... | collective-permute-start | bytes 393224 | tf_op jit(solution)/shard_map/ppermute | solution.py:440
  45.2 23.3 %collective-permute-start.12 = (bf16[256,128]{1,0:T(8,128)(2,1)S(1)}, bf16[256,128]{1,0:T(8,128)(2,1)S(1)}, u32[]{:S(2)}, u32[]{:S(2)}) collective-permute-start(bf16[256,128]{1,0:T(8,128)(2,1)S(1)} %get-tuple-element.65), channel_id=1, source_target_pairs={{0,5},{1,4},{4,1},{5,0},{8,13},{9,12},{12,9},{13,8},{2,7},{3,6},{6... | collective-permute-start | bytes 196616 | tf_op jit(solution)/shard_map/ppermute | solution.py:440
  56.3 15.3 %collective-permute-start.13 = (bf16[256,128]{1,0:T(8,128)(2,1)S(1)}, bf16[256,128]{1,0:T(8,128)(2,1)S(1)}, u32[]{:S(2)}, u32[]{:S(2)}) collective-permute-start(bf16[256,128]{1,0:T(8,128)(2,1)S(1)} %get-tuple-element.66), channel_id=1, source_target_pairs={{0,8},{1,9},{4,12},{5,13},{8,0},{9,1},{12,4},{13,5},{2,10},{3,11},... | collective-permute-start | bytes 196616 | tf_op jit(solution)/shard_map/ppermute | solution.py:440
  61.0 15.3 %collective-permute-start.14 = (bf16[256,128]{1,0:T(8,128)(2,1)S(1)}, bf16[256,128]{1,0:T(8,128)(2,1)S(1)}, u32[]{:S(2)}, u32[]{:S(2)}) collective-permute-start(bf16[256,128]{1,0:T(8,128)(2,1)S(1)} %get-tuple-element.67), channel_id=1, source_target_pairs={{0,9},{1,8},{4,13},{5,12},{8,1},{9,0},{12,5},{13,4},{2,11},{3,10},... | collective-permute-start | bytes 196616 | tf_op jit(solution)/shard_map/ppermute | solution.py:440
  61.0 15.6 %collective-permute-start.15 = (bf16[256,128]{1,0:T(8,128)(2,1)S(1)}, bf16[256,128]{1,0:T(8,128)(2,1)S(1)}, u32[]{:S(2)}, u32[]{:S(2)}) collective-permute-start(bf16[256,128]{1,0:T(8,128)(2,1)S(1)} %get-tuple-element.68), channel_id=1, source_target_pairs={{0,12},{1,13},{4,8},{5,9},{8,4},{9,5},{12,0},{13,1},{2,14},{3,15},... | collective-permute-start | bytes 196616 | tf_op jit(solution)/shard_map/ppermute | solution.py:440
  61.1 18.4 %collective-permute-start.16 = (bf16[256,128]{1,0:T(8,128)(2,1)S(1)}, bf16[256,128]{1,0:T(8,128)(2,1)S(1)}, u32[]{:S(2)}, u32[]{:S(2)}) collective-permute-start(bf16[256,128]{1,0:T(8,128)(2,1)S(1)} %get-tuple-element.69), channel_id=1, source_target_pairs={{0,13},{1,12},{4,9},{5,8},{8,5},{9,4},{12,1},{13,0},{2,15},{3,14},... | collective-permute-start | bytes 196616 | tf_op jit(solution)/shard_map/ppermute | solution.py:440
  63.5 16.0 %copy-start.27 = (s32[256]{0:T(256)S(1)}, s32[256]{0:T(256)}, u32[]{:S(2)}) copy-start(s32[256]{0:T(256)} %param.11) | copy-start | bytes 3076
  68.5 25.5 %collective-permute-start.38 = (bf16[256,128]{1,0:T(8,128)(2,1)S(1)}, bf16[256,128]{1,0:T(8,128)(2,1)S(1)}, u32[]{:S(2)}, u32[]{:S(2)}) collective-permute-start(bf16[256,128]{1,0:T(8,128)(2,1)S(1)} %get-tuple-element.97), channel_id=1, source_target_pairs={{0,1},{1,0},{4,5},{5,4},{8,9},{9,8},{12,13},{13,12},{2,3},{3,2},{6... | collective-permute-start | bytes 196616 | tf_op jit(solution)/shard_map/ppermute | solution.py:440
  71.6 22.4 %collective-permute-start.39 = (bf16[256,128]{1,0:T(8,128)(2,1)S(1)}, bf16[256,128]{1,0:T(8,128)(2,1)S(1)}, u32[]{:S(2)}, u32[]{:S(2)}) collective-permute-start(bf16[256,128]{1,0:T(8,128)(2,1)S(1)} %get-tuple-element.98), channel_id=1, source_target_pairs={{0,4},{1,5},{4,0},{5,1},{8,12},{9,13},{12,8},{13,9},{2,6},{3,7},{6... | collective-permute-start | bytes 196616 | tf_op jit(solution)/shard_map/ppermute | solution.py:440
  76.3 19.1 %collective-permute-start.40 = (bf16[256,128]{1,0:T(8,128)(2,1)S(1)}, bf16[256,128]{1,0:T(8,128)(2,1)S(1)}, u32[]{:S(2)}, u32[]{:S(2)}) collective-permute-start(bf16[256,128]{1,0:T(8,128)(2,1)S(1)} %get-tuple-element.99), channel_id=1, source_target_pairs={{0,5},{1,4},{4,1},{5,0},{8,13},{9,12},{12,9},{13,8},{2,7},{3,6},{6... | collective-permute-start | bytes 196616 | tf_op jit(solution)/shard_map/ppermute | solution.py:440
  76.6 21.1 %collective-permute-start.41 = (bf16[256,128]{1,0:T(8,128)(2,1)S(1)}, bf16[256,128]{1,0:T(8,128)(2,1)S(1)}, u32[]{:S(2)}, u32[]{:S(2)}) collective-permute-start(bf16[256,128]{1,0:T(8,128)(2,1)S(1)} %get-tuple-element.100), channel_id=1, source_target_pairs={{0,8},{1,9},{4,12},{5,13},{8,0},{9,1},{12,4},{13,5},{2,10},{3,11},... | collective-permute-start | bytes 196616 | tf_op jit(solution)/shard_map/ppermute | solution.py:440
  79.5 44.5 %copy-start.1 = (bf16[1024,1024]{1,0:T(8,128)(2,1)S(1)}, bf16[1024,1024]{1,0:T(8,128)(2,1)}, u32[]{:S(2)}) copy-start(bf16[1024,1024]{1,0:T(8,128)(2,1)} %refs_16_.3) | copy-start | bytes 6291460
  93.5 13.7 %collective-permute-start.31 = (bf16[512,128]{1,0:T(8,128)(2,1)S(1)}, bf16[512,128]{1,0:T(8,128)(2,1)S(1)}, u32[]{:S(2)}, u32[]{:S(2)}) collective-permute-start(bf16[512,128]{1,0:T(8,128)(2,1)S(1)} %get-tuple-element.89), channel_id=1, source_target_pairs={{0,1},{1,0},{4,5},{5,4},{8,9},{9,8},{12,13},{13,12},{2,3},{3,2},{6... | collective-permute-start | bytes 393224 | tf_op jit(solution)/shard_map/ppermute | solution.py:440
  93.9 15.3 %collective-permute-start.32 = (bf16[512,128]{1,0:T(8,128)(2,1)S(1)}, bf16[512,128]{1,0:T(8,128)(2,1)S(1)}, u32[]{:S(2)}, u32[]{:S(2)}) collective-permute-start(bf16[512,128]{1,0:T(8,128)(2,1)S(1)} %get-tuple-element.90), channel_id=1, source_target_pairs={{0,4},{1,5},{4,0},{5,1},{8,12},{9,13},{12,8},{13,9},{2,6},{3,7},{6... | collective-permute-start | bytes 393224 | tf_op jit(solution)/shard_map/ppermute | solution.py:440
  94.0 8.1 %collective-permute-start.42 = (bf16[256,128]{1,0:T(8,128)(2,1)S(1)}, bf16[256,128]{1,0:T(8,128)(2,1)S(1)}, u32[]{:S(2)}, u32[]{:S(2)}) collective-permute-start(bf16[256,128]{1,0:T(8,128)(2,1)S(1)} %get-tuple-element.101), channel_id=1, source_target_pairs={{0,9},{1,8},{4,13},{5,12},{8,1},{9,0},{12,5},{13,4},{2,11},{3,10},... | collective-permute-start | bytes 196616 | tf_op jit(solution)/shard_map/ppermute | solution.py:440
  95.4 6.7 %collective-permute-start.43 = (bf16[256,128]{1,0:T(8,128)(2,1)S(1)}, bf16[256,128]{1,0:T(8,128)(2,1)S(1)}, u32[]{:S(2)}, u32[]{:S(2)}) collective-permute-start(bf16[256,128]{1,0:T(8,128)(2,1)S(1)} %get-tuple-element.102), channel_id=1, source_target_pairs={{0,12},{1,13},{4,8},{5,9},{8,4},{9,5},{12,0},{13,1},{2,14},{3,15},... | collective-permute-start | bytes 196616 | tf_op jit(solution)/shard_map/ppermute | solution.py:440
  97.7 6.6 %collective-permute-start.44 = (bf16[256,128]{1,0:T(8,128)(2,1)S(1)}, bf16[256,128]{1,0:T(8,128)(2,1)S(1)}, u32[]{:S(2)}, u32[]{:S(2)}) collective-permute-start(bf16[256,128]{1,0:T(8,128)(2,1)S(1)} %get-tuple-element.103), channel_id=1, source_target_pairs={{0,13},{1,12},{4,9},{5,8},{8,5},{9,4},{12,1},{13,0},{2,15},{3,14},... | collective-permute-start | bytes 196616 | tf_op jit(solution)/shard_map/ppermute | solution.py:440
  102.1 9.0 %collective-permute-start.33 = (bf16[512,128]{1,0:T(8,128)(2,1)}, bf16[512,128]{1,0:T(8,128)(2,1)S(1)}, u32[]{:S(2)}, u32[]{:S(2)}) collective-permute-start(bf16[512,128]{1,0:T(8,128)(2,1)} %get-tuple-element.91), channel_id=1, source_target_pairs={{0,5},{1,4},{4,1},{5,0},{8,13},{9,12},{12,9},{13,8},{2,7},{3,6},{6... | collective-permute-start | bytes 393224 | tf_op jit(solution)/shard_map/ppermute | solution.py:440
  102.7 8.4 %collective-permute-start.34 = (bf16[512,128]{1,0:T(8,128)(2,1)}, bf16[512,128]{1,0:T(8,128)(2,1)S(1)}, u32[]{:S(2)}, u32[]{:S(2)}) collective-permute-start(bf16[512,128]{1,0:T(8,128)(2,1)} %get-tuple-element.92), channel_id=1, source_target_pairs={{0,8},{1,9},{4,12},{5,13},{8,0},{9,1},{12,4},{13,5},{2,10},{3,11},... | collective-permute-start | bytes 393224 | tf_op jit(solution)/shard_map/ppermute | solution.py:440
  104.9 19.0 %collective-permute-start.35 = (bf16[512,128]{1,0:T(8,128)(2,1)}, bf16[512,128]{1,0:T(8,128)(2,1)S(1)}, u32[]{:S(2)}, u32[]{:S(2)}) collective-permute-start(bf16[512,128]{1,0:T(8,128)(2,1)} %get-tuple-element.93), channel_id=1, source_target_pairs={{0,9},{1,8},{4,13},{5,12},{8,1},{9,0},{12,5},{13,4},{2,11},{3,10},... | collective-permute-start | bytes 393224 | tf_op jit(solution)/shard_map/ppermute | solution.py:440
  107.2 16.8 %collective-permute-start.36 = (bf16[512,128]{1,0:T(8,128)(2,1)}, bf16[512,128]{1,0:T(8,128)(2,1)S(1)}, u32[]{:S(2)}, u32[]{:S(2)}) collective-permute-start(bf16[512,128]{1,0:T(8,128)(2,1)} %get-tuple-element.94), channel_id=1, source_target_pairs={{0,12},{1,13},{4,8},{5,9},{8,4},{9,5},{12,0},{13,1},{2,14},{3,15},... | collective-permute-start | bytes 393224 | tf_op jit(solution)/shard_map/ppermute | solution.py:440
  109.2 14.7 %collective-permute-start.37 = (bf16[512,128]{1,0:T(8,128)(2,1)}, bf16[512,128]{1,0:T(8,128)(2,1)S(1)}, u32[]{:S(2)}, u32[]{:S(2)}) collective-permute-start(bf16[512,128]{1,0:T(8,128)(2,1)} %get-tuple-element.95), channel_id=1, source_target_pairs={{0,13},{1,12},{4,9},{5,8},{8,5},{9,4},{12,1},{13,0},{2,15},{3,14},... | collective-permute-start | bytes 393224 | tf_op jit(solution)/shard_map/ppermute | solution.py:440
  123.9 0.8 copy-start.7
  124.8 0.8 copy-start.9
  125.6 7.6 %copy-start.26 = (bf16[288,128]{1,0:T(8,128)(2,1)S(1)}, bf16[288,128]{1,0:T(8,128)(2,1)}, u32[]{:S(2)}) copy-start(bf16[288,128]{1,0:T(8,128)(2,1)} %copy-done.25) | copy-start | bytes 221188
  125.6 7.6 %copy-start.24 = (bf16[288,128]{1,0:T(8,128)(2,1)S(1)}, bf16[288,128]{1,0:T(8,128)(2,1)}, u32[]{:S(2)}) copy-start(bf16[288,128]{1,0:T(8,128)(2,1)} %copy-done.23) | copy-start | bytes 221188
  125.6 13.3 %copy-start.22 = (bf16[288,128]{1,0:T(8,128)(2,1)S(1)}, bf16[288,128]{1,0:T(8,128)(2,1)}, u32[]{:S(2)}) copy-start(bf16[288,128]{1,0:T(8,128)(2,1)} %copy-done.21) | copy-start | bytes 221188
  125.6 13.5 %copy-start.20 = (bf16[288,128]{1,0:T(8,128)(2,1)S(1)}, bf16[288,128]{1,0:T(8,128)(2,1)}, u32[]{:S(2)}) copy-start(bf16[288,128]{1,0:T(8,128)(2,1)} %copy-done.19) | copy-start | bytes 221188
  125.6 16.3 %copy-start.18 = (bf16[288,128]{1,0:T(8,128)(2,1)S(1)}, bf16[288,128]{1,0:T(8,128)(2,1)}, u32[]{:S(2)}) copy-start(bf16[288,128]{1,0:T(8,128)(2,1)} %copy-done.17) | copy-start | bytes 221188
  125.6 16.4 %copy-start.16 = (bf16[288,128]{1,0:T(8,128)(2,1)S(1)}, bf16[288,128]{1,0:T(8,128)(2,1)}, u32[]{:S(2)}) copy-start(bf16[288,128]{1,0:T(8,128)(2,1)} %copy-done.15) | copy-start | bytes 221188
  125.7 19.5 %copy-start.14 = (bf16[288,128]{1,0:T(8,128)(2,1)S(1)}, bf16[288,128]{1,0:T(8,128)(2,1)}, u32[]{:S(2)}) copy-start(bf16[288,128]{1,0:T(8,128)(2,1)} %copy-done.13) | copy-start | bytes 221188
  125.7 27.7 %copy-start.11 = (bf16[288,128]{1,0:T(8,128)(2,1)S(1)}, bf16[288,128]{1,0:T(8,128)(2,1)}, u32[]{:S(2)}) copy-start(bf16[288,128]{1,0:T(8,128)(2,1)} %copy-done.10) | copy-start | bytes 221188
  131.7 28.9 %collective-permute-start.45 = (bf16[256,1024]{1,0:T(8,128)(2,1)S(1)}, bf16[256,1024]{1,0:T(8,128)(2,1)S(1)}, u32[]{:S(2)}, u32[]{:S(2)}) collective-permute-start(bf16[256,1024]{1,0:T(8,128)(2,1)S(1)} %shard_map.101), channel_id=1, source_target_pairs={{0,2},{2,0},{1,3},{3,1},{4,6},{6,4},{5,7},{7,5},{8,10},{10,8},{9,1... | collective-permute-start | bytes 1572872 | tf_op jit(solution)/shard_map/ppermute | solution.py:552
  133.2 8.7 %collective-permute-start.24 = (bf16[288,128]{1,0:T(8,128)(2,1)S(1)}, bf16[288,128]{1,0:T(8,128)(2,1)S(1)}, u32[]{:S(2)}, u32[]{:S(2)}) collective-permute-start(bf16[288,128]{1,0:T(8,128)(2,1)S(1)} %copy-done.26), channel_id=1, source_target_pairs={{0,1},{1,0},{4,5},{5,4},{8,9},{9,8},{12,13},{13,12},{2,3},{3,2},{6... | collective-permute-start | bytes 221192 | tf_op jit(solution)/shard_map/ppermute | solution.py:440
  133.2 8.9 %collective-permute-start.25 = (bf16[288,128]{1,0:T(8,128)(2,1)S(1)}, bf16[288,128]{1,0:T(8,128)(2,1)S(1)}, u32[]{:S(2)}, u32[]{:S(2)}) collective-permute-start(bf16[288,128]{1,0:T(8,128)(2,1)S(1)} %copy-done.24), channel_id=1, source_target_pairs={{0,4},{1,5},{4,0},{5,1},{8,12},{9,13},{12,8},{13,9},{2,6},{3,7},{6... | collective-permute-start | bytes 221192 | tf_op jit(solution)/shard_map/ppermute | solution.py:440
  138.9 6.3 %collective-permute-start.26 = (bf16[288,128]{1,0:T(8,128)(2,1)S(1)}, bf16[288,128]{1,0:T(8,128)(2,1)S(1)}, u32[]{:S(2)}, u32[]{:S(2)}) collective-permute-start(bf16[288,128]{1,0:T(8,128)(2,1)S(1)} %copy-done.22), channel_id=1, source_target_pairs={{0,5},{1,4},{4,1},{5,0},{8,13},{9,12},{12,9},{13,8},{2,7},{3,6},{6... | collective-permute-start | bytes 221192 | tf_op jit(solution)/shard_map/ppermute | solution.py:440
  139.1 8.4 %collective-permute-start.27 = (bf16[288,128]{1,0:T(8,128)(2,1)S(1)}, bf16[288,128]{1,0:T(8,128)(2,1)S(1)}, u32[]{:S(2)}, u32[]{:S(2)}) collective-permute-start(bf16[288,128]{1,0:T(8,128)(2,1)S(1)} %copy-done.20), channel_id=1, source_target_pairs={{0,8},{1,9},{4,12},{5,13},{8,0},{9,1},{12,4},{13,5},{2,10},{3,11},... | collective-permute-start | bytes 221192 | tf_op jit(solution)/shard_map/ppermute | solution.py:440
  142.0 11.4 %collective-permute-start.28 = (bf16[288,128]{1,0:T(8,128)(2,1)S(1)}, bf16[288,128]{1,0:T(8,128)(2,1)S(1)}, u32[]{:S(2)}, u32[]{:S(2)}) collective-permute-start(bf16[288,128]{1,0:T(8,128)(2,1)S(1)} %copy-done.18), channel_id=1, source_target_pairs={{0,9},{1,8},{4,13},{5,12},{8,1},{9,0},{12,5},{13,4},{2,11},{3,10},... | collective-permute-start | bytes 221192 | tf_op jit(solution)/shard_map/ppermute | solution.py:440
  142.1 11.3 %collective-permute-start.29 = (bf16[288,128]{1,0:T(8,128)(2,1)S(1)}, bf16[288,128]{1,0:T(8,128)(2,1)S(1)}, u32[]{:S(2)}, u32[]{:S(2)}) collective-permute-start(bf16[288,128]{1,0:T(8,128)(2,1)S(1)} %copy-done.16), channel_id=1, source_target_pairs={{0,12},{1,13},{4,8},{5,9},{8,4},{9,5},{12,0},{13,1},{2,14},{3,15},... | collective-permute-start | bytes 221192 | tf_op jit(solution)/shard_map/ppermute | solution.py:440
  145.2 8.2 %collective-permute-start.30 = (bf16[288,128]{1,0:T(8,128)(2,1)S(1)}, bf16[288,128]{1,0:T(8,128)(2,1)S(1)}, u32[]{:S(2)}, u32[]{:S(2)}) collective-permute-start(bf16[288,128]{1,0:T(8,128)(2,1)S(1)} %copy-done.14), channel_id=1, source_target_pairs={{0,13},{1,12},{4,9},{5,8},{8,5},{9,4},{12,1},{13,0},{2,15},{3,14},... | collective-permute-start | bytes 221192 | tf_op jit(solution)/shard_map/ppermute | solution.py:440
  (10 other events, 6.3 us)

commit v4 on v2

--- a/solution.py
+++ b/solution.py
@@ -190,45 +190,68 @@
 contract_last = (((1,), (1,)), ((), ()))
 contract_first = (((0,), (0,)), ((), ()))
 log2_e = 1.4426950408889634
-vmem_bytes = 48 * 1024 * 1024
+vmem_bytes = 40 * 1024 * 1024
 
 
 def pack_kernel(grads_ref, assign_ref, out_ref):
-    blocks, padded, head_dim = out_ref.shape
+    count, padded, head_dim = out_ref.shape
     rows = grads_ref.shape[0]
     spare = padded - rows - rows // head_dim
-    for head in range(blocks):
-        out_ref[head, :rows, :] = grads_ref[:, head * head_dim : (head + 1) * head_dim]
+    for device in range(count):
+        head = device % 2 * (count // 2) + device // 2
+        out_ref[device, :rows, :] = grads_ref[:, head * head_dim : (head + 1) * head_dim]
         ids = assign_ref[head : head + 1, :].astype(jnp.float32)
         lines = [
             ids[:, start : start + head_dim] for start in range(0, rows, head_dim)
         ] + [jnp.zeros((spare, head_dim), jnp.float32)]
-        out_ref[head, rows:, :] = jnp.concatenate(lines, axis=0).astype(jnp.bfloat16)
-
-
-def project_kernel(side_ref, hidden_ref, *refs):
-    out_ref = refs[-1]
-    heads, triple, head_dim = out_ref.shape
-    rows = triple // 3
-    half = refs[0].shape[0]
-    side = side_ref[0]
+        out_ref[device, rows:, :] = jnp.concatenate(lines, axis=0).astype(jnp.bfloat16)
+
+
+def project_kernel(chips, place_ref, mine_ref, theirs_ref, *refs):
+    weights, out_refs, hidden_ref = refs[:6], refs[6 : 6 + chips], refs[6 + chips]
+    rows = mine_ref.shape[0]
+    tall = 2 * rows
+    half = weights[0].shape[0]
+    head_dim = out_refs[0].shape[1]
+    odd = place_ref[0] % 2
+    side = place_ref[1]
+
+    @pl.when(pl.program_id(0) == 0)
+    def join():
+        hidden_ref[pl.ds(pl.multiple_of(side * rows, rows), rows), :] = mine_ref[...]
+        hidden_ref[pl.ds(pl.multiple_of((1 - side) * rows, rows), rows), :] = theirs_ref[...]
+
     near = hidden_ref[:, pl.ds(pl.multiple_of(side * half, half), half)]
     far = hidden_ref[:, pl.ds(pl.multiple_of((1 - side) * half, half), half)]
     for index in range(3):
-        total = jnp.dot(near, refs[index][...], preferred_element_type=jnp.float32)
-        total += jnp.dot(far, refs[3 + index][...], preferred_element_type=jnp.float32)
+        total = jnp.dot(near, weights[index][...], preferred_element_type=jnp.float32)
+        total += jnp.dot(far, weights[3 + index][...], preferred_element_type=jnp.float32)
         low = total.astype(jnp.bfloat16)
-        for head in range(heads):
-            out_ref[head, index * rows : (index + 1) * rows, :] = low[
-                :, head * head_dim : (head + 1) * head_dim
-            ]
-
-
-def attend_kernel(factor, scale, packed_ref, grads_ref, rank_ref, out_ref, grad_ref, ids_ref, dk_ref, dv_ref):
-    blocks, triple, head_dim = packed_ref.shape
-    rows = triple // 3
+        first = jnp.where(odd == 0, low[:, :head_dim], low[:, head_dim:])
+        second = jnp.where(odd == 0, low[:, head_dim:], low[:, :head_dim])
+        for pair in range(chips // 2):
+
+            @pl.when(pl.program_id(0) == pair)
+            def store(pair=pair, index=index, first=first, second=second):
+                out_refs[2 * pair][index * tall : (index + 1) * tall, :] = first
+                out_refs[2 * pair + 1][index * tall : (index + 1) * tall, :] = second
+
+
+def attend_kernel(factor, scale, chips, place_ref, *refs):
+    packed, grads_ref, rank_ref = refs[:chips], refs[chips], refs[chips + 1]
+    back_refs, out_ref = refs[chips + 2 : 2 * chips + 2], refs[2 * chips + 2]
+    queries, keys_in, values, ids_ref, dq_ref, dk_ref, dv_ref = refs[2 * chips + 3 :]
+    place = place_ref[0]
+    blocks = grads_ref.shape[0]
+    tokens, head_dim = queries.shape
+    rows = tokens // blocks
+    tall = 2 * rows
     clusters = rank_ref.shape[1]
     owned = clusters // blocks
+    for offset in range(chips):
+        at = pl.ds(pl.multiple_of((place ^ offset) * tall, tall), tall)
+        for index, held in enumerate((queries, keys_in, values)):
+            held[at, :] = packed[offset][index * tall : (index + 1) * tall, :]
     id_rows = []
     for block in range(blocks):
         lines = grads_ref[block, rows : rows + 16, :].astype(jnp.float32)
@@ -241,15 +264,15 @@
     dv_ref[...] = jnp.zeros_like(dv_ref)
     for block in range(blocks):
         seen = (block + 1) * rows
-        keys_in = packed_ref[: block + 1, rows : 2 * rows, :].reshape(seen, head_dim)
-        values = packed_ref[: block + 1, 2 * rows :, :].reshape(seen, head_dim)
-        query_rows = packed_ref[block, :rows, :]
+        seen_keys = keys_in[:seen, :]
+        seen_values = values[:seen, :]
+        query_rows = queries[block * rows : seen, :]
         grad_rows = grads_ref[block, :rows, :]
         scores = lax.dot_general(
-            keys_in, query_rows, contract_last, preferred_element_type=jnp.float32
+            seen_keys, query_rows, contract_last, preferred_element_type=jnp.float32
         )
         grad_probs = lax.dot_general(
-            values, grad_rows, contract_last, preferred_element_type=jnp.float32
+            seen_values, grad_rows, contract_last, preferred_element_type=jnp.float32
         )
         ids = ids_ref[:seen, :]
         same = jnp.concatenate(
@@ -271,25 +294,24 @@
         grad_low = (weighted - probs * delta).astype(jnp.bfloat16)
         probs_low = probs.astype(jnp.bfloat16)
         flipped = lax.dot_general(
-            values, probs_low, contract_first, preferred_element_type=jnp.float32
-        )
-        out_ref[block] = flipped.T.astype(jnp.bfloat16)
+            seen_values, probs_low, contract_first, preferred_element_type=jnp.float32
+        )
+        out_ref[block, :rows, :] = flipped.T.astype(jnp.bfloat16)
         dv_ref[:seen, :] += jnp.dot(probs_low, grad_rows, preferred_element_type=jnp.float32)
         dk_ref[:seen, :] += jnp.dot(grad_low, query_rows, preferred_element_type=jnp.float32)
         flipped = lax.dot_general(
-            keys_in, grad_low, contract_first, preferred_element_type=jnp.float32
-        )
-        grad_ref[block, :rows, :] = (flipped.T * scale).astype(jnp.bfloat16)
-    grad_ref[:, rows : 2 * rows, :] = (
-        (dk_ref[...] * scale).astype(jnp.bfloat16).reshape(blocks, rows, head_dim)
-    )
-    grad_ref[:, 2 * rows : triple, :] = (
-        dv_ref[...].astype(jnp.bfloat16).reshape(blocks, rows, head_dim)
-    )
+            seen_keys, grad_low, contract_first, preferred_element_type=jnp.float32
+        )
+        dq_ref[block * rows : seen, :] = (flipped.T * scale).astype(jnp.bfloat16)
+    for offset in range(chips):
+        at = pl.ds(pl.multiple_of((place ^ offset) * tall, tall), tall)
+        back_refs[offset][:tall, :] = dq_ref[at, :]
+        back_refs[offset][tall : 2 * tall, :] = (dk_ref[at, :] * scale).astype(jnp.bfloat16)
+        back_refs[offset][2 * tall :, :] = dv_ref[at, :].astype(jnp.bfloat16)
     sums = jnp.zeros((clusters, head_dim), jnp.float32)
     cluster_at = lax.broadcasted_iota(jnp.int32, (clusters, rows), 0).astype(jnp.float32)
     for block in range(blocks):
-        keys_float = packed_ref[block, rows : 2 * rows, :].astype(jnp.float32)
+        keys_float = keys_in[block * rows : (block + 1) * rows, :].astype(jnp.float32)
         unit = keys_float * lax.rsqrt(
             jnp.sum(keys_float * keys_float, axis=1, keepdims=True) + epsilon
         )
@@ -301,145 +323,228 @@
     rank_at = lax.broadcasted_iota(jnp.int32, (clusters, clusters), 0)
     ordered = jnp.where(rank_at == rank_ref[...], 1.0, 0.0).astype(jnp.bfloat16)
     ranked = jnp.dot(ordered, sums.astype(jnp.bfloat16), preferred_element_type=jnp.float32)
-    grad_ref[:, triple:, :] = ranked.astype(jnp.bfloat16).reshape(blocks, owned, head_dim)
-
-
-def input_kernel(pick_ref, back_ref, *refs):
-    out_ref, gathered_ref = refs[-2:]
-    blocks, padded, head_dim = back_ref.shape
+    out_ref[:, rows:, :] = ranked.astype(jnp.bfloat16).reshape(blocks, owned, head_dim)
+
+
+def input_kernel(chips, place_ref, *refs):
+    parts, weights = refs[:chips], refs[chips : chips + 6]
+    out_ref, gathered_ref = refs[chips + 6 :]
     rows = out_ref.shape[0]
-    width = blocks * head_dim
+    head_dim = parts[0].shape[1]
+    width = chips * head_dim
+    steps = pl.num_programs(0) // 2
 
     @pl.when(pl.program_id(0) == 0)
     def gather():
-        for index in range(3):
-            for head in range(blocks):
-                at = index * width + head * head_dim
-                gathered_ref[:, at : at + head_dim] = back_ref[
-                    head, index * rows : (index + 1) * rows, :
-                ]
+        for offset in range(chips):
+            at = (place_ref[0] ^ offset) * head_dim
+            for index in range(3):
+                start = pl.multiple_of(index * width + at, head_dim)
+                first = pl.multiple_of((2 * index + place_ref[2]) * rows, rows)
+                gathered_ref[:, pl.ds(start, head_dim)] = parts[offset][pl.ds(first, rows), :]
 
     def multiply(first):
         total = None
         for index in range(3):
             term = lax.dot_general(
                 gathered_ref[:, index * width : (index + 1) * width],
-                refs[first + index][...],
+                weights[first + index][...],
                 contract_last,
                 preferred_element_type=jnp.float32,
             )
             total = term if total is None else total + term
         out_ref[...] = total.astype(out_ref.dtype)
 
-    pl.when(pick_ref[0] == 0)(lambda: multiply(0))
-    pl.when(pick_ref[0] != 0)(lambda: multiply(3))
+    mine = pl.program_id(0) // steps == place_ref[1]
+    pl.when(mine)(lambda: multiply(0))
+    pl.when(jnp.logical_not(mine))(lambda: multiply(3))
+
+
+def cross_kernel(place_ref, mine_ref, theirs_ref, out_ref):
+    out_ref[...] = (mine_ref[...] + theirs_ref[...].astype(jnp.float32)).astype(jnp.bfloat16)
+
+
+def finish_kernel(place_ref, mine_ref, theirs_ref, crossed_ref, returned_ref, hidden_ref, attended_ref, sums_ref):
+    total = mine_ref[...] + theirs_ref[...].astype(jnp.float32)
+    hidden_ref[...] = (total + crossed_ref[...].astype(jnp.float32)).astype(jnp.bfloat16)
+    rows = attended_ref.shape[0]
+    count, owned, head_dim = sums_ref.shape
+    for device in range(count):
+        head = device % 2 * (count // 2) + device // 2
+        attended_ref[:, head * head_dim : (head + 1) * head_dim] = returned_ref[device, :rows, :]
+        sums_ref[head] = returned_ref[device, rows:, :].astype(jnp.float32)
 
 
 def by_head(hidden, w_query, w_key, w_value, cluster_rank, assign, d_attended):
     rows = hidden.shape[0]
-    blocks = assign.shape[0]
+    count = assign.shape[0]
+    chips = count // 2
     half, width = w_query.shape
-    head_dim = width // blocks
-    tokens = blocks * rows
+    head_dim = width // count
+    tokens = count * rows
     clusters = cluster_rank.shape[0]
-    owned = clusters // blocks
+    owned = clusters // count
     scale = head_dim ** (-0.5)
     factor = scale * log2_e
     line = ("seq", "sub")
+    smem = pl.BlockSpec(memory_space=pltpu.SMEM)
     vmem = pl.BlockSpec(memory_space=pltpu.VMEM)
     params = pltpu.CompilerParams(vmem_limit_bytes=vmem_bytes)
     pairs_seen = tokens * (tokens + rows) // 2
     wide = 2 * head_dim
+    swap = [(0, 1), (1, 0)]
+    chip, side, column = (lax.axis_index(name) for name in ("seq", "sub", "head"))
+    place = jnp.stack([chip, side, side, column])
+    place_sibling = jnp.stack([chip, side, 1 - side, column])
+
+    def whole(array):
+        return pl.BlockSpec(array.shape, lambda step, at: (0,) * len(array.shape))
 
     def exchange(packed):
         return lax.all_to_all(packed, line, split_axis=0, concat_axis=0, tiled=True)
 
-    id_rows = -(-(rows // head_dim) // 16) * 16
+    def exchange_chips(parts):
+        moved = {
+            offset: lax.ppermute(parts[offset], "seq", [(at, at ^ offset) for at in range(chips)])
+            for offset in (2, 3, 1)
+        }
+        return (parts[0], moved[1], moved[2], moved[3])
+
+    def buffers(height):
+        return (jax.ShapeDtypeStruct((height, head_dim), jnp.bfloat16),) * chips
+
+    hidden_other = lax.ppermute(hidden, "sub", swap)
+    own = (w_query, w_key, w_value)
+    other = tuple(lax.ppermute(piece, "sub", swap) for piece in own)
+
+    id_height = -(-(rows // head_dim) // 16) * 16
     grads = exchange(
         pl.pallas_call(
             pack_kernel,
-            out_shape=jax.ShapeDtypeStruct((blocks, rows + id_rows, head_dim), jnp.bfloat16),
+            out_shape=jax.ShapeDtypeStruct((count, rows + id_height, head_dim), jnp.bfloat16),
             in_specs=[vmem] * 2,
             out_specs=vmem,
             compiler_params=params,
         )(d_attended, assign)
     )
 
-    swap = [(0, 1), (1, 0)]
-    side = lax.axis_index("sub")
-    own = (w_query, w_key, w_value)
-    other = tuple(lax.ppermute(piece, "sub", swap) for piece in own)
     projected = pl.pallas_call(
-        project_kernel,
-        out_shape=jax.ShapeDtypeStruct((blocks, 3 * rows, head_dim), jnp.bfloat16),
+        partial(project_kernel, chips),
+        out_shape=buffers(6 * rows),
         grid_spec=pltpu.PrefetchScalarGridSpec(
             num_scalar_prefetch=1,
-            grid=(width // wide,),
-            in_specs=[pl.BlockSpec((rows, 2 * half), lambda step, side_at: (0, 0))]
-            + [pl.BlockSpec((half, wide), lambda step, side_at: (0, step))] * 6,
-            out_specs=pl.BlockSpec((2, 3 * rows, head_dim), lambda step, side_at: (step, 0, 0)),
+            grid=(chips // 2,),
+            in_specs=[whole(hidden)] * 2
+            + [
+                pl.BlockSpec(
+                    (half, wide), lambda step, at: (0, at[1] * (chips // 2) + ((at[0] // 2) ^ step))
+                )
+            ]
+            * 6,
+            out_specs=[pl.BlockSpec((6 * rows, head_dim), lambda step, at: (0, 0))] * chips,
+            scratch_shapes=[pltpu.VMEM((2 * rows, 2 * half), jnp.bfloat16)],
         ),
         compiler_params=params,
         cost_estimate=pl.CostEstimate(
-            flops=12 * rows * half * width, bytes_accessed=14 * half * width, transcendentals=0
-        ),
-    )(side.reshape(1), hidden, *own, *other)
-    packed = exchange(projected)
-
-    outputs, grads_out = pl.pallas_call(
-        partial(attend_kernel, factor, scale),
+            flops=12 * rows * half * width, bytes_accessed=8 * half * width, transcendentals=0
+        ),
+    )(place, hidden, hidden_other, *own, *other)
+    packed = exchange_chips(projected)
+
+    *grads_out, outputs = pl.pallas_call(
+        partial(attend_kernel, factor, scale, chips),
         out_shape=(
-            jax.ShapeDtypeStruct((blocks, rows, head_dim), jnp.bfloat16),
-            jax.ShapeDtypeStruct((blocks, 3 * rows + owned, head_dim), jnp.bfloat16),
-        ),
-        in_specs=[vmem] * 3,
-        out_specs=(vmem, vmem),
-        scratch_shapes=[pltpu.VMEM((tokens, head_dim), jnp.float32)] * 3,
+            *buffers(6 * rows),
+            jax.ShapeDtypeStruct((count, rows + owned, head_dim), jnp.bfloat16),
+        ),
+        in_specs=[smem] + [vmem] * (chips + 2),
+        out_specs=(vmem,) * (chips + 1),
+        scratch_shapes=[pltpu.VMEM((tokens, head_dim), jnp.bfloat16)] * 3
+        + [pltpu.VMEM((tokens, head_dim), jnp.float32)]
+        + [pltpu.VMEM((tokens, head_dim), jnp.bfloat16)]
+        + [pltpu.VMEM((tokens, head_dim), jnp.float32)] * 2,
         compiler_params=params,
         cost_estimate=pl.CostEstimate(
             flops=12 * pairs_seen * head_dim,
             bytes_accessed=16 * tokens * head_dim,
             transcendentals=pairs_seen,
         ),
-    )(packed, grads, cluster_rank.reshape(1, clusters))
-    back = exchange(grads_out)
-    returned = exchange(outputs)
-    attended = returned.transpose(1, 0, 2).reshape(rows, width)
-    centroid_sums = back[:, 3 * rows :, :].astype(jnp.float32)
-
-    def input_part(pick, kept_type):
+    )(place, *packed, grads, cluster_rank.reshape(1, clusters))
+    back = exchange_chips(grads_out)
+
+    steps = half // wide
+
+    def input_part(at, kind):
         def rows_of(first):
-            return lambda step, pick_at: (jnp.where(pick_at[0] == first, step, 0), 0)
+            return lambda step, at: (
+                jnp.where((step // steps == at[1]) == first, step % steps, 0),
+                at[1],
+            )
 
         return pl.pallas_call(
-            input_kernel,
-            out_shape=jax.ShapeDtypeStruct((rows, half), kept_type),
+            partial(input_kernel, chips),
+            out_shape=jax.ShapeDtypeStruct((rows, 2 * half), kind),
             grid_spec=pltpu.PrefetchScalarGridSpec(
                 num_scalar_prefetch=1,
-                grid=(half // wide,),
-                in_specs=[pl.BlockSpec(back.shape, lambda step, pick_at: (0, 0, 0))]
-                + [pl.BlockSpec((wide, width), rows_of(0))] * 3
-                + [pl.BlockSpec((wide, width), rows_of(1))] * 3,
-                out_specs=pl.BlockSpec((rows, wide), lambda step, pick_at: (0, step)),
-                scratch_shapes=[pltpu.VMEM((rows, 3 * width), jnp.bfloat16)],
+                grid=(2 * steps,),
+                in_specs=[whole(back[0])] * chips
+                + [pl.BlockSpec((wide, width // 2), rows_of(True))] * 3
+                + [pl.BlockSpec((wide, width // 2), rows_of(False))] * 3,
+                out_specs=pl.BlockSpec((rows, wide), lambda step, at: (0, step)),
+                scratch_shapes=[pltpu.VMEM((rows, 3 * width // 2), jnp.bfloat16)],
             ),
             compiler_params=params,
             cost_estimate=pl.CostEstimate(
                 flops=6 * rows * half * width, bytes_accessed=10 * half * width, transcendentals=0
             ),
-        )(pick.reshape(1), back, *own, *other)
-
-    crossed = (side != lax.axis_index("head")).astype(jnp.int32)
-    arrived = lax.ppermute(input_part(1 - crossed, jnp.bfloat16), "head", swap)
-    kept = input_part(crossed, jnp.float32)
-    d_hidden = (kept + arrived.astype(jnp.float32)).astype(jnp.bfloat16)
+        )(at, *back, *own, *other)
+
+    theirs = lax.ppermute(input_part(place_sibling, jnp.bfloat16), "sub", swap)
+    mine = input_part(place, jnp.float32)
+
+    def half_of(pick):
+        return pl.BlockSpec((rows, half), lambda step, at: (0, pick(at)))
+
+    crossing = pl.pallas_call(
+        cross_kernel,
+        out_shape=jax.ShapeDtypeStruct((rows, half), jnp.bfloat16),
+        grid_spec=pltpu.PrefetchScalarGridSpec(
+            num_scalar_prefetch=1,
+            grid=(1,),
+            in_specs=[half_of(lambda at: 1 - at[3])] * 2,
+            out_specs=pl.BlockSpec((rows, half), lambda step, at: (0, 0)),
+        ),
+        compiler_params=params,
+    )(place, mine, theirs)
+    crossed = lax.ppermute(crossing, "head", swap)
+    outputs, _ = lax.optimization_barrier((outputs, back[1]))
+    returned = exchange(outputs)
+    d_hidden, attended, centroid_sums = pl.pallas_call(
+        finish_kernel,
+        out_shape=(
+            jax.ShapeDtypeStruct((rows, half), jnp.bfloat16),
+            jax.ShapeDtypeStruct((rows, width), jnp.bfloat16),
+            jax.ShapeDtypeStruct((count, owned, head_dim), jnp.float32),
+        ),
+        grid_spec=pltpu.PrefetchScalarGridSpec(
+            num_scalar_prefetch=1,
+            grid=(1,),
+            in_specs=[half_of(lambda at: at[3])] * 2 + [whole(crossed), whole(returned)],
+            out_specs=(
+                pl.BlockSpec((rows, half), lambda step, at: (0, 0)),
+                pl.BlockSpec((rows, width), lambda step, at: (0, 0)),
+                pl.BlockSpec((count, owned, head_dim), lambda step, at: (0, 0, 0)),
+            ),
+        ),
+        compiler_params=params,
+    )(place, mine, theirs, crossed, returned)
     return (attended, d_hidden, centroid_sums)
 
 
 def per_device(hidden, w_query, w_key, w_value, cluster_rank, assign, d_attended):
-    owners = lax.axis_size("seq") * lax.axis_size("sub")
-    halves = lax.axis_size("sub") == 2 and lax.axis_size("head") == 2
-    plan = by_head if assign.shape[0] == owners and halves else by_owner
+    chips = lax.axis_size("seq")
+    fits = chips == 4 and lax.axis_size("sub") == 2 and lax.axis_size("head") == 2
+    plan = by_head if fits and assign.shape[0] == 2 * chips else by_owner
     return plan(hidden, w_query, w_key, w_value, cluster_rank, assign, d_attended)
 
 

time: 154 us -> 173 us (1.12)
  blocking collectives: 83.8 us -> 0 us
  waiting for transfers between devices: 12.2 us -> 64.4 us
  starting transfers between devices: 12.7 us -> 38.3 us
  local copies, waits for them, and re-layouts: 10 us -> 23.7 us
  Pallas kernels: 30.6 us -> 43.7 us
  other arithmetic: 2.65 us -> 0.15 us
    all_to_all x2 -> x0, blocking collectives: 83.8 us -> none  [exchange(): return lax.all_to_all(packed, line, split_axis=0, concat_axis=0, tiled=True)]
    ppermute x1 -> x9, waiting for transfers between devices: 0.01 us -> 62.5 us  [the longest x6 49.9 us: exchange_chips(): lax.ppermute(parts[offset], 'seq', [(at, at ^ offset) for at in range(chi...]
    ppermute x1 -> x9, starting transfers between devices: 1.48 us -> 22 us  [the longest x6 15.5 us: exchange_chips(): lax.ppermute(parts[offset], 'seq', [(at, at ^ offset) for at in range(chi...]
    unnamed x17 -> x46, local copies, waits for them, and re-layouts: 9.01 us -> 23.7 us
    pallas_call x5 -> x7, Pallas kernels: 30.6 us -> 43.7 us  [the longest x2 15.5 us: input_part(): pl.pallas_call(partial(input_kernel, chips), out_shape=jax.ShapeDtypeStru...]
    all_to_all x2, waiting for transfers between devices: 11.4 us -> 0.01 us  [exchange(): return lax.all_to_all(packed, line, split_axis=0, concat_axis=0, tiled=True)]
    all_to_all x2, starting transfers between devices: 10.6 us -> 15.7 us  [exchange(): return lax.all_to_all(packed, line, split_axis=0, concat_axis=0, tiled=True)]
    convert_element_type x2 -> x0, other arithmetic: 2.65 us -> none  [the longest x1 1.98 us: by_head(): d_hidden = (kept + arrived.astype(jnp.float32)).astype(jnp.bfloat16)]
  transfers between devices with their start and end apart: 6 -> 14, of which waited for: 3 -> 7; matrix products, arithmetic and copies ran while one was open for 2% -> 0% of each run, Pallas kernels for 12% -> 12%
where the time goes in v4:
time: 173 us; the launch traced here: 171 us
  waiting for transfers between devices  64.4 us (37%)
  Pallas kernels  43.7 us (25%)
  starting transfers between devices  38.3 us (22%)
  local copies, waits for them, and re-layouts  23.7 us (14%)
    ppermute x6, waiting for transfers between devices, exchange_chips(): lax.ppermute(parts[offset], 'seq', [(at, at ^ offset) for at in range(chi...  49.9 us
    unnamed x46, local copies, waits for them, and re-layouts  23.7 us
    all_to_all x2, starting transfers between devices, exchange(): return lax.all_to_all(packed, line, split_axis=0, concat_axis=0, tiled=True)  15.7 us
    ppermute x6, starting transfers between devices, exchange_chips(): lax.ppermute(parts[offset], 'seq', [(at, at ^ offset) for at in range(chi...  15.5 us
    pallas_call x2, Pallas kernels, input_part(): pl.pallas_call(partial(input_kernel, chips), out_shape=jax.ShapeDtypeStru...  15.5 us
    pallas_call x1, Pallas kernels, by_head(): pl.pallas_call(partial(attend_kernel, factor, scale, chips), out_shape=(*...  13 us
    ppermute x1, waiting for transfers between devices, by_head(): crossed = lax.ppermute(crossing, 'head', swap)  12.6 us
    pallas_call x1, Pallas kernels, by_head(): pl.pallas_call(partial(project_kernel, chips), out_shape=buffers(6 * rows...  9.98 us
  transfers between devices with their start and end apart: 14, of which 7 were waited for; matrix products, arithmetic and copies ran while one was open for 0% of the time, Pallas kernels for 12%

profile of v4, /device:TPU:1, one launch (start us, length us, event | category | flops | bytes accessed | tf_op | source)
XLA Modules:
  0.0 170.9 jit_solution(5079665207987459836)
XLA Ops:
  0.6 0.0 copy-start
  0.6 0.1 collective-permute-start.1
  0.8 0.5 collective-permute-start.2
  1.2 0.1 collective-permute-start.3
  1.3 0.4 collective-permute-start
  1.7 0.0 copy-start.14
  1.7 1.0 copy-done.14
  2.8 0.0 copy-start.15
  2.8 0.7 copy-done.15
  3.5 0.9 shard_map.95
  4.4 6.4 %all-to-all-start = ((bf16[8,272,128]{2,1,0:T(8,128)(2,1)}), bf16[8,272,128]{2,1,0:T(8,128)(2,1)}, u32[]{:S(2)}, u32[]{:S(2)}) async-start(bf16[8,272,128]{2,1,0:T(8,128)(2,1)} %shard_map.95), calls=%async_computation | async-start | bytes 1114112 | tf_op jit(solution)/shard_map/all_to_all | solution.py:404
  10.7 0.0 copy-start.22
  10.8 0.1 add_add_fusion.place_ref
  10.8 0.0 collective-permute-done.theirs_ref
  10.8 0.0 collective-permute-done.1.refs_3_.refs_7_
  10.8 0.0 collective-permute-done.2.refs_4_.refs_8_
  10.8 1.9 %collective-permute-done.3.refs_5_.refs_9_ = bf16[1024,1024]{1,0:T(8,128)(2,1)} collective-permute-done((bf16[1024,1024]{1,0:T(8,128)(2,1)}, bf16[1024,1024]{1,0:T(8,128)(2,1)}, u32[]{:S(2)}, u32[]{:S(2)}) %collective-permute-start.3) | collective-permute-done | bytes 2097184 | tf_op jit(solution)/shard_map/ppermute | solution.py:418
  12.7 0.0 copy-done
  12.7 1.6 copy-done.2
  14.3 1.6 copy-done.5
  15.9 1.2 copy-done.12
  17.1 10.0 %shard_map.94 = (bf16[1536,128]{1,0:T(8,128)(2,1)S(1)}, bf16[1536,128]{1,0:T(8,128)(2,1)}, bf16[1536,128]{1,0:T(8,128)(2,1)}, bf16[1536,128]{1,0:T(8,128)(2,1)}) custom-call(s32[4]{0:T(128)S(1)} %add_add_fusion.place_ref, bf16[256,2048]{1,0:T(8,128)(2,1)S(1)} %copy-done.12, bf16[256,2048]{1,0:T(8,128)(2,1)S(1)} %collective-permute-done.theirs_ref, ...), custom_call_target="tpu_custom_call" | custom-call | flops 3221225472 | bytes 8388608 | tf_op jit(solution)/shard_map/pallas_call | solution.py:431
  27.1 0.8 copy-done.16
  27.9 2.4 %collective-permute-start.4 = (bf16[1536,128]{1,0:T(8,128)(2,1)}, bf16[1536,128]{1,0:T(8,128)(2,1)S(1)}, u32[]{:S(2)}, u32[]{:S(2)}) collective-permute-start(bf16[1536,128]{1,0:T(8,128)(2,1)} %get-tuple-element.17), channel_id=1, source_target_pairs={{0,4},{4,0},{8,12},{12,8},{1,5},{5,1},{9,13},{13,9},{2,6},{6,2},{1... | collective-permute-start | bytes 1179656 | tf_op jit(solution)/shard_map/ppermute | solution.py:408
  30.3 2.3 %collective-permute-start.5 = (bf16[1536,128]{1,0:T(8,128)(2,1)}, bf16[1536,128]{1,0:T(8,128)(2,1)S(1)}, u32[]{:S(2)}, u32[]{:S(2)}) collective-permute-start(bf16[1536,128]{1,0:T(8,128)(2,1)} %get-tuple-element.18), channel_id=1, source_target_pairs={{0,8},{4,12},{8,0},{12,4},{1,9},{5,13},{9,1},{13,5},{2,10},{6,14},... | collective-permute-start | bytes 1179656 | tf_op jit(solution)/shard_map/ppermute | solution.py:408
  32.6 0.0 collective-permute-start.6
  32.6 0.0 all-to-all-done.refs_4_
  32.6 14.9 %collective-permute-done.4.refs_1_ = bf16[1536,128]{1,0:T(8,128)(2,1)S(1)} collective-permute-done((bf16[1536,128]{1,0:T(8,128)(2,1)}, bf16[1536,128]{1,0:T(8,128)(2,1)S(1)}, u32[]{:S(2)}, u32[]{:S(2)}) %collective-permute-start.4) | collective-permute-done | bytes 393248 | tf_op jit(solution)/shard_map/ppermute | solution.py:408
  47.5 0.0 collective-permute-done.5.refs_2_
  47.6 0.7 copy-done.18
  48.3 10.2 %collective-permute-done.6.refs_3_ = bf16[1536,128]{1,0:T(8,128)(2,1)S(1)} collective-permute-done((bf16[1536,128]{1,0:T(8,128)(2,1)}, bf16[1536,128]{1,0:T(8,128)(2,1)S(1)}, u32[]{:S(2)}, u32[]{:S(2)}) %collective-permute-start.6) | collective-permute-done | bytes 393248 | tf_op jit(solution)/shard_map/ppermute | solution.py:408
  58.5 0.7 copy-done.20
  59.2 0.0 copy-done.22
  59.2 1.0 copy-done.17
  60.2 1.0 copy-done.19
  61.2 1.0 copy-done.21
  62.2 13.0 %shard_map.96 = (bf16[1536,128]{1,0:T(8,128)(2,1)S(1)}, bf16[1536,128]{1,0:T(8,128)(2,1)}, bf16[1536,128]{1,0:T(8,128)(2,1)}, bf16[1536,128]{1,0:T(8,128)(2,1)}, bf16[8,288,128]{2,1,0:T(8,128)(2,1)S(1)}) custom-call(s32[4]{0:T(128)S(1)} %add_add_fusion.place_ref, bf16[1536,128]{1,0:T(8,128)(2,1)S(1)} %copy-done.17, ...), custom_call_target="tpu_custom_call" | custom-call | flops 3623878656 | bytes 4194304 | tf_op jit(solution)/shard_map/pallas_call | solution.py:454
  75.2 0.9 copy-done.13
  76.0 8.6 %collective-permute-start.7 = (bf16[1536,128]{1,0:T(8,128)(2,1)}, bf16[1536,128]{1,0:T(8,128)(2,1)S(1)}, u32[]{:S(2)}, u32[]{:S(2)}) collective-permute-start(bf16[1536,128]{1,0:T(8,128)(2,1)} %get-tuple-element.21), channel_id=1, source_target_pairs={{0,4},{4,0},{8,12},{12,8},{1,5},{5,1},{9,13},{13,9},{2,6},{6,2},{1... | collective-permute-start | bytes 1179656 | tf_op jit(solution)/shard_map/ppermute | solution.py:408
  84.7 1.0 collective-permute-start.8
  85.7 1.2 collective-permute-start.9
  86.9 0.1 add_add_fusion.1.place_ref
  86.9 13.1 %collective-permute-done.7.refs_1_ = bf16[1536,128]{1,0:T(8,128)(2,1)S(1)} collective-permute-done((bf16[1536,128]{1,0:T(8,128)(2,1)}, bf16[1536,128]{1,0:T(8,128)(2,1)S(1)}, u32[]{:S(2)}, u32[]{:S(2)}) %collective-permute-start.7) | collective-permute-done | bytes 393248 | tf_op jit(solution)/shard_map/ppermute | solution.py:408
  100.1 0.3 collective-permute-done.8.refs_2_
  100.4 11.4 %collective-permute-done.9.refs_3_ = bf16[1536,128]{1,0:T(8,128)(2,1)} collective-permute-done((bf16[1536,128]{1,0:T(8,128)(2,1)}, bf16[1536,128]{1,0:T(8,128)(2,1)}, u32[]{:S(2)}, u32[]{:S(2)}) %collective-permute-start.9) | collective-permute-done | bytes 393248 | tf_op jit(solution)/shard_map/ppermute | solution.py:408
  111.7 1.6 copy-done.3
  113.3 1.6 copy-done.6
  114.9 8.0 %shard_map.98 = bf16[256,2048]{1,0:T(8,128)(2,1)} custom-call(s32[4]{0:T(128)S(1)} %add_add_fusion.1.place_ref, bf16[1536,128]{1,0:T(8,128)(2,1)S(1)} %get-tuple-element.20.refs_0_, bf16[1536,128]{1,0:T(8,128)(2,1)S(1)} %collective-permute-done.7.refs_1_, bf16[1536,128]{1,0:T(8,128)(2,1)S(1)} %collective-permute-done.8.refs_2_, ...), custom_call_target="tpu_custom_call" | custom-call | flops 1610612736 | bytes 10485760 | tf_op jit(solution)/shard_map/pallas_call | solution.py:484
  123.0 0.7 copy-done.8
  123.7 0.7 copy-done.10
  124.4 4.8 %collective-permute-start.10 = (bf16[256,2048]{1,0:T(8,128)(2,1)}, bf16[256,2048]{1,0:T(8,128)(2,1)S(1)}, u32[]{:S(2)}, u32[]{:S(2)}) collective-permute-start(bf16[256,2048]{1,0:T(8,128)(2,1)} %shard_map.98), channel_id=1, source_target_pairs={{0,1},{1,0},{2,3},{3,2},{4,5},{5,4},{6,7},{7,6},{8,9},{9,8},{10,11... | collective-permute-start | bytes 3145736 | tf_op jit(solution)/shard_map/ppermute | solution.py:502
  129.3 9.3 %all-to-all-start.1 = ((bf16[8,288,128]{2,1,0:T(8,128)(2,1)}), bf16[8,288,128]{2,1,0:T(8,128)(2,1)}, u32[]{:S(2)}, u32[]{:S(2)}) async-start(bf16[8,288,128]{2,1,0:T(8,128)(2,1)} %copy-done.13), calls=%async_computation.1 | async-start | bytes 1179648 | tf_op jit(solution)/shard_map/all_to_all | solution.py:404
  138.5 1.6 copy-done.1
  140.1 1.6 copy-done.4
  141.7 1.6 copy-done.7
  143.3 1.0 copy-done.9
  144.3 1.0 copy-done.11
  145.3 7.4 %shard_map.97.mine_ref = f32[256,2048]{1,0:T(8,128)S(1)} custom-call(s32[4]{0:T(128)S(1)} %add_add_fusion.place_ref, bf16[1536,128]{1,0:T(8,128)(2,1)S(1)} %get-tuple-element.20.refs_0_, bf16[1536,128]{1,0:T(8,128)(2,1)S(1)} %copy-done.9, bf16[1536,128]{1,0:T(8,128)(2,1)S(1)} %copy-done.11, bf16[1536,128]{1,0:T(8,128)(2,1)} %collective-permute-done.9.refs_3_, ...), custom_call_target="tpu_custom_call" | custom-call | flops 1610612736 | bytes 10485760 | tf_op jit(solution)/shard_map/pallas_call | solution.py:484
  152.7 0.0 collective-permute-done.10.theirs_ref
  152.8 1.4 shard_map.99
  154.2 1.2 collective-permute-start.11
  155.4 0.0 all-to-all-done.1.returned_ref
  155.4 12.6 %collective-permute-done.11.crossed_ref = bf16[256,1024]{1,0:T(8,128)(2,1)} collective-permute-done((bf16[256,1024]{1,0:T(8,128)(2,1)}, bf16[256,1024]{1,0:T(8,128)(2,1)}, u32[]{:S(2)}, u32[]{:S(2)}) %collective-permute-start.11) | collective-permute-done | bytes 524320 | tf_op jit(solution)/shard_map/ppermute | solution.py:519
  168.0 3.0 %shard_map.100 = (bf16[256,1024]{1,0:T(8,128)(2,1)}, bf16[256,1024]{1,0:T(8,128)(2,1)}, f32[8,32,128]{2,1,0:T(8,128)}) custom-call(s32[4]{0:T(128)S(1)} %add_add_fusion.place_ref, f32[256,2048]{1,0:T(8,128)S(1)} %shard_map.97.mine_ref, bf16[256,2048]{1,0:T(8,128)(2,1)S(1)} %collective-permute-done.10.theirs_ref, ...), custom_call_target="tpu_custom_call" | custom-call | tf_op jit(solution)/shard_map/pallas_call | solution.py:522
  (19 shorter events, 0.0 us)
Async XLA Ops:
  0.6 12.1 %copy-start = (bf16[1024,1024]{1,0:T(8,128)(2,1)S(1)}, bf16[1024,1024]{1,0:T(8,128)(2,1)}, u32[]{:S(2)}) copy-start(bf16[1024,1024]{1,0:T(8,128)(2,1)} %refs_4_.3) | copy-start | bytes 6291460
  0.6 10.2 %collective-permute-start.1 = (bf16[1024,1024]{1,0:T(8,128)(2,1)}, bf16[1024,1024]{1,0:T(8,128)(2,1)}, u32[]{:S(2)}, u32[]{:S(2)}) collective-permute-start(bf16[1024,1024]{1,0:T(8,128)(2,1)} %refs_4_.3), channel_id=1, source_target_pairs={{0,1},{1,0},{2,3},{3,2},{4,5},{5,4},{6,7},{7,6},{8,9},{9,8},{10,11... | collective-permute-start | bytes 6291464 | tf_op jit(solution)/shard_map/ppermute | solution.py:418
  0.8 10.1 %collective-permute-start.2 = (bf16[1024,1024]{1,0:T(8,128)(2,1)}, bf16[1024,1024]{1,0:T(8,128)(2,1)}, u32[]{:S(2)}, u32[]{:S(2)}) collective-permute-start(bf16[1024,1024]{1,0:T(8,128)(2,1)} %refs_5_.3), channel_id=1, source_target_pairs={{0,1},{1,0},{2,3},{3,2},{4,5},{5,4},{6,7},{7,6},{8,9},{9,8},{10,11... | collective-permute-start | bytes 6291464 | tf_op jit(solution)/shard_map/ppermute | solution.py:418
  1.2 11.5 %collective-permute-start.3 = (bf16[1024,1024]{1,0:T(8,128)(2,1)}, bf16[1024,1024]{1,0:T(8,128)(2,1)}, u32[]{:S(2)}, u32[]{:S(2)}) collective-permute-start(bf16[1024,1024]{1,0:T(8,128)(2,1)} %refs_6_.3), channel_id=1, source_target_pairs={{0,1},{1,0},{2,3},{3,2},{4,5},{5,4},{6,7},{7,6},{8,9},{9,8},{10,11... | collective-permute-start | bytes 6291464 | tf_op jit(solution)/shard_map/ppermute | solution.py:418
  1.3 9.5 %collective-permute-start = (bf16[256,2048]{1,0:T(8,128)(2,1)}, bf16[256,2048]{1,0:T(8,128)(2,1)S(1)}, u32[]{:S(2)}, u32[]{:S(2)}) collective-permute-start(bf16[256,2048]{1,0:T(8,128)(2,1)} %mine_ref.1), channel_id=1, source_target_pairs={{0,1},{1,0},{2,3},{3,2},{4,5},{5,4},{6,7},{7,6},{8,9},{9,8},{10,11... | collective-permute-start | bytes 3145736 | tf_op jit(solution)/shard_map/ppermute | solution.py:416
  1.7 1.0 copy-start.14
  2.8 0.7 copy-start.15
  4.4 28.3 %all-to-all-start = ((bf16[8,272,128]{2,1,0:T(8,128)(2,1)}), bf16[8,272,128]{2,1,0:T(8,128)(2,1)}, u32[]{:S(2)}, u32[]{:S(2)}) async-start(bf16[8,272,128]{2,1,0:T(8,128)(2,1)} %shard_map.95), calls=%async_computation | async-start | bytes 1114112 | tf_op jit(solution)/shard_map/all_to_all | solution.py:404
  10.7 48.5 %copy-start.22 = (s32[256]{0:T(256)S(1)}, s32[256]{0:T(256)}, u32[]{:S(2)}) copy-start(s32[256]{0:T(256)} %param.11) | copy-start | bytes 3076
  12.7 1.6 copy-start.2
  14.3 1.6 copy-start.5
  15.9 1.2 copy-start.12
  27.1 0.8 copy-start.16
  27.9 19.7 %collective-permute-start.4 = (bf16[1536,128]{1,0:T(8,128)(2,1)}, bf16[1536,128]{1,0:T(8,128)(2,1)S(1)}, u32[]{:S(2)}, u32[]{:S(2)}) collective-permute-start(bf16[1536,128]{1,0:T(8,128)(2,1)} %get-tuple-element.17), channel_id=1, source_target_pairs={{0,4},{4,0},{8,12},{12,8},{1,5},{5,1},{9,13},{13,9},{2,6},{6,2},{1... | collective-permute-start | bytes 1179656 | tf_op jit(solution)/shard_map/ppermute | solution.py:408
  30.3 17.2 %collective-permute-start.5 = (bf16[1536,128]{1,0:T(8,128)(2,1)}, bf16[1536,128]{1,0:T(8,128)(2,1)S(1)}, u32[]{:S(2)}, u32[]{:S(2)}) collective-permute-start(bf16[1536,128]{1,0:T(8,128)(2,1)} %get-tuple-element.18), channel_id=1, source_target_pairs={{0,8},{4,12},{8,0},{12,4},{1,9},{5,13},{9,1},{13,5},{2,10},{6,14},... | collective-permute-start | bytes 1179656 | tf_op jit(solution)/shard_map/ppermute | solution.py:408
  32.6 25.9 %collective-permute-start.6 = (bf16[1536,128]{1,0:T(8,128)(2,1)}, bf16[1536,128]{1,0:T(8,128)(2,1)S(1)}, u32[]{:S(2)}, u32[]{:S(2)}) collective-permute-start(bf16[1536,128]{1,0:T(8,128)(2,1)} %get-tuple-element.19), channel_id=1, source_target_pairs={{0,12},{4,8},{8,4},{12,0},{1,13},{5,9},{9,5},{13,1},{2,14},{6,10},... | collective-permute-start | bytes 1179656 | tf_op jit(solution)/shard_map/ppermute | solution.py:408
  47.6 0.7 copy-start.18
  58.5 0.7 copy-start.20
  59.2 1.0 copy-start.17
  60.2 1.0 copy-start.19
  61.2 1.0 copy-start.21
  75.2 0.9 copy-start.13
  76.0 24.0 %collective-permute-start.7 = (bf16[1536,128]{1,0:T(8,128)(2,1)}, bf16[1536,128]{1,0:T(8,128)(2,1)S(1)}, u32[]{:S(2)}, u32[]{:S(2)}) collective-permute-start(bf16[1536,128]{1,0:T(8,128)(2,1)} %get-tuple-element.21), channel_id=1, source_target_pairs={{0,4},{4,0},{8,12},{12,8},{1,5},{5,1},{9,13},{13,9},{2,6},{6,2},{1... | collective-permute-start | bytes 1179656 | tf_op jit(solution)/shard_map/ppermute | solution.py:408
  84.7 15.7 %collective-permute-start.8 = (bf16[1536,128]{1,0:T(8,128)(2,1)}, bf16[1536,128]{1,0:T(8,128)(2,1)S(1)}, u32[]{:S(2)}, u32[]{:S(2)}) collective-permute-start(bf16[1536,128]{1,0:T(8,128)(2,1)} %get-tuple-element.22), channel_id=1, source_target_pairs={{0,8},{4,12},{8,0},{12,4},{1,9},{5,13},{9,1},{13,5},{2,10},{6,14},... | collective-permute-start | bytes 1179656 | tf_op jit(solution)/shard_map/ppermute | solution.py:408
  85.7 26.1 %collective-permute-start.9 = (bf16[1536,128]{1,0:T(8,128)(2,1)}, bf16[1536,128]{1,0:T(8,128)(2,1)}, u32[]{:S(2)}, u32[]{:S(2)}) collective-permute-start(bf16[1536,128]{1,0:T(8,128)(2,1)} %get-tuple-element.23), channel_id=1, source_target_pairs={{0,12},{4,8},{8,4},{12,0},{1,13},{5,9},{9,5},{13,1},{2,14},{6,10},... | collective-permute-start | bytes 1179656 | tf_op jit(solution)/shard_map/ppermute | solution.py:408
  111.7 1.6 copy-start.3
  113.3 1.6 copy-start.6
  123.0 0.7 copy-start.8
  123.7 0.7 copy-start.10
  124.4 28.3 %collective-permute-start.10 = (bf16[256,2048]{1,0:T(8,128)(2,1)}, bf16[256,2048]{1,0:T(8,128)(2,1)S(1)}, u32[]{:S(2)}, u32[]{:S(2)}) collective-permute-start(bf16[256,2048]{1,0:T(8,128)(2,1)} %shard_map.98), channel_id=1, source_target_pairs={{0,1},{1,0},{2,3},{3,2},{4,5},{5,4},{6,7},{7,6},{8,9},{9,8},{10,11... | collective-permute-start | bytes 3145736 | tf_op jit(solution)/shard_map/ppermute | solution.py:502
  129.3 26.2 %all-to-all-start.1 = ((bf16[8,288,128]{2,1,0:T(8,128)(2,1)}), bf16[8,288,128]{2,1,0:T(8,128)(2,1)}, u32[]{:S(2)}, u32[]{:S(2)}) async-start(bf16[8,288,128]{2,1,0:T(8,128)(2,1)} %copy-done.13), calls=%async_computation.1 | async-start | bytes 1179648 | tf_op jit(solution)/shard_map/all_to_all | solution.py:404
  138.5 1.6 copy-start.1
  140.1 1.6 copy-start.4
  141.7 1.6 copy-start.7
  143.3 1.0 copy-start.9
  144.3 1.0 copy-start.11
  154.2 13.8 %collective-permute-start.11 = (bf16[256,1024]{1,0:T(8,128)(2,1)}, bf16[256,1024]{1,0:T(8,128)(2,1)}, u32[]{:S(2)}, u32[]{:S(2)}) collective-permute-start(bf16[256,1024]{1,0:T(8,128)(2,1)} %shard_map.99), channel_id=1, source_target_pairs={{0,2},{2,0},{1,3},{3,1},{4,6},{6,4},{5,7},{7,5},{8,10},{10,8},{9,1... | collective-permute-start | bytes 1572872 | tf_op jit(solution)/shard_map/ppermute | solution.py:519

commit v5 on v4

--- a/solution.py
+++ b/solution.py
@@ -190,7 +190,7 @@
 contract_last = (((1,), (1,)), ((), ()))
 contract_first = (((0,), (0,)), ((), ()))
 log2_e = 1.4426950408889634
-vmem_bytes = 40 * 1024 * 1024
+mebi = 1024 * 1024
 
 
 def pack_kernel(grads_ref, assign_ref, out_ref):
@@ -207,41 +207,61 @@
         out_ref[device, rows:, :] = jnp.concatenate(lines, axis=0).astype(jnp.bfloat16)
 
 
-def project_kernel(chips, place_ref, mine_ref, theirs_ref, *refs):
-    weights, out_refs, hidden_ref = refs[:6], refs[6 : 6 + chips], refs[6 + chips]
-    rows = mine_ref.shape[0]
-    tall = 2 * rows
-    half = weights[0].shape[0]
-    head_dim = out_refs[0].shape[1]
-    odd = place_ref[0] % 2
+def join_rows(side, mine_ref, theirs_ref, start, joined_ref):
+    rows, columns = mine_ref.shape[0], joined_ref.shape[1]
+    at = pl.ds(pl.multiple_of(start, columns), columns)
+    joined_ref[pl.ds(pl.multiple_of(side * rows, rows), rows), :] = mine_ref[:, at]
+    joined_ref[pl.ds(pl.multiple_of((1 - side) * rows, rows), rows), :] = theirs_ref[:, at]
+
+
+def fetch_columns(side, weights, held_ref, sems):
+    columns = held_ref.shape[2]
+    at = pl.ds(pl.multiple_of(side * columns, columns), columns)
+    copies = [
+        pltpu.make_async_copy(weight.at[:, at], held_ref.at[index], sems.at[index])
+        for index, weight in enumerate(weights)
+    ]
+    for copy in copies:
+        copy.start()
+    return copies
+
+
+def near_kernel(place_ref, mine_ref, theirs_ref, *refs):
+    weights, out_ref, joined_ref, held_ref, sems = refs[:3], *refs[3:]
     side = place_ref[1]
-
-    @pl.when(pl.program_id(0) == 0)
-    def join():
-        hidden_ref[pl.ds(pl.multiple_of(side * rows, rows), rows), :] = mine_ref[...]
-        hidden_ref[pl.ds(pl.multiple_of((1 - side) * rows, rows), rows), :] = theirs_ref[...]
-
-    near = hidden_ref[:, pl.ds(pl.multiple_of(side * half, half), half)]
-    far = hidden_ref[:, pl.ds(pl.multiple_of((1 - side) * half, half), half)]
-    for index in range(3):
-        total = jnp.dot(near, weights[index][...], preferred_element_type=jnp.float32)
-        total += jnp.dot(far, weights[3 + index][...], preferred_element_type=jnp.float32)
-        low = total.astype(jnp.bfloat16)
-        first = jnp.where(odd == 0, low[:, :head_dim], low[:, head_dim:])
-        second = jnp.where(odd == 0, low[:, head_dim:], low[:, :head_dim])
-        for pair in range(chips // 2):
-
-            @pl.when(pl.program_id(0) == pair)
-            def store(pair=pair, index=index, first=first, second=second):
-                out_refs[2 * pair][index * tall : (index + 1) * tall, :] = first
-                out_refs[2 * pair + 1][index * tall : (index + 1) * tall, :] = second
+    copies = fetch_columns(side, weights, held_ref, sems)
+    join_rows(side, mine_ref, theirs_ref, side * joined_ref.shape[1], joined_ref)
+    for index, copy in enumerate(copies):
+        copy.wait()
+        out_ref[index] = jnp.dot(
+            joined_ref[...], held_ref[index], preferred_element_type=jnp.float32
+        )
+
+
+def far_kernel(place_ref, mine_ref, theirs_ref, near_ref, *refs):
+    weights, refs = refs[:3], refs[3:]
+    out_refs, (joined_ref, held_ref, low_ref, sems) = refs[:-4], refs[-4:]
+    chips = len(out_refs)
+    tall, head_dim = joined_ref.shape[0], out_refs[0].shape[1]
+    side = place_ref[1]
+    copies = fetch_columns(side, weights, held_ref, sems)
+    join_rows(side, mine_ref, theirs_ref, (1 - side) * joined_ref.shape[1], joined_ref)
+    for index, copy in enumerate(copies):
+        copy.wait()
+        total = near_ref[index] + jnp.dot(
+            joined_ref[...], held_ref[index], preferred_element_type=jnp.float32
+        )
+        low_ref[...] = total.astype(jnp.bfloat16)
+        for offset in range(chips):
+            at = pl.multiple_of((place_ref[0] ^ offset) * head_dim, head_dim)
+            out_refs[offset][index * tall : (index + 1) * tall, :] = low_ref[:, pl.ds(at, head_dim)]
 
 
 def attend_kernel(factor, scale, chips, place_ref, *refs):
     packed, grads_ref, rank_ref = refs[:chips], refs[chips], refs[chips + 1]
-    back_refs, out_ref = refs[chips + 2 : 2 * chips + 2], refs[2 * chips + 2]
-    queries, keys_in, values, ids_ref, dq_ref, dk_ref, dv_ref = refs[2 * chips + 3 :]
-    place = place_ref[0]
+    back_refs, out_ref = refs[chips + 2 : 3 * chips + 2], refs[3 * chips + 2]
+    queries, keys_in, values, ids_ref, dq_ref, dk_ref, dv_ref = refs[3 * chips + 3 :]
+    place, side = place_ref[0], place_ref[1]
     blocks = grads_ref.shape[0]
     tokens, head_dim = queries.shape
     rows = tokens // blocks
@@ -303,11 +323,14 @@
             seen_keys, grad_low, contract_first, preferred_element_type=jnp.float32
         )
         dq_ref[block * rows : seen, :] = (flipped.T * scale).astype(jnp.bfloat16)
-    for offset in range(chips):
-        at = pl.ds(pl.multiple_of((place ^ offset) * tall, tall), tall)
-        back_refs[offset][:tall, :] = dq_ref[at, :]
-        back_refs[offset][tall : 2 * tall, :] = (dk_ref[at, :] * scale).astype(jnp.bfloat16)
-        back_refs[offset][2 * tall :, :] = dv_ref[at, :].astype(jnp.bfloat16)
+    for turn in range(2):
+        for offset in range(chips):
+            back_ref = back_refs[turn * chips + offset]
+            shard = (place ^ offset) * 2 + (side ^ turn)
+            at = pl.ds(pl.multiple_of(shard * rows, rows), rows)
+            back_ref[:rows, :] = dq_ref[at, :]
+            back_ref[rows : 2 * rows, :] = (dk_ref[at, :] * scale).astype(jnp.bfloat16)
+            back_ref[2 * rows :, :] = dv_ref[at, :].astype(jnp.bfloat16)
     sums = jnp.zeros((clusters, head_dim), jnp.float32)
     cluster_at = lax.broadcasted_iota(jnp.int32, (clusters, rows), 0).astype(jnp.float32)
     for block in range(blocks):
@@ -326,47 +349,43 @@
     out_ref[:, rows:, :] = ranked.astype(jnp.bfloat16).reshape(blocks, owned, head_dim)
 
 
-def input_kernel(chips, place_ref, *refs):
-    parts, weights = refs[:chips], refs[chips : chips + 6]
-    out_ref, gathered_ref = refs[chips + 6 :]
-    rows = out_ref.shape[0]
+def input_kernel(place_ref, *refs):
+    parts, weights, (out_ref, gathered_ref, held_ref, sems) = refs[:-10], refs[-10:-4], refs[-4:]
+    chips = len(parts) // 2
+    rows, width = out_ref.shape[0], held_ref.shape[2]
     head_dim = parts[0].shape[1]
-    width = chips * head_dim
-    steps = pl.num_programs(0) // 2
-
-    @pl.when(pl.program_id(0) == 0)
-    def gather():
+
+    def fetch(first):
+        for index in range(3):
+            pltpu.make_async_copy(
+                weights[first + index], held_ref.at[index], sems.at[index]
+            ).start()
+
+    pl.when(place_ref[2] == 0)(lambda: fetch(0))
+    pl.when(place_ref[2] != 0)(lambda: fetch(3))
+    for turn in range(2):
         for offset in range(chips):
-            at = (place_ref[0] ^ offset) * head_dim
+            head = (place_ref[1] ^ turn) * chips + (place_ref[0] ^ offset)
             for index in range(3):
-                start = pl.multiple_of(index * width + at, head_dim)
-                first = pl.multiple_of((2 * index + place_ref[2]) * rows, rows)
-                gathered_ref[:, pl.ds(start, head_dim)] = parts[offset][pl.ds(first, rows), :]
-
-    def multiply(first):
-        total = None
-        for index in range(3):
-            term = lax.dot_general(
-                gathered_ref[:, index * width : (index + 1) * width],
-                weights[first + index][...],
-                contract_last,
-                preferred_element_type=jnp.float32,
-            )
-            total = term if total is None else total + term
-        out_ref[...] = total.astype(out_ref.dtype)
-
-    mine = pl.program_id(0) // steps == place_ref[1]
-    pl.when(mine)(lambda: multiply(0))
-    pl.when(jnp.logical_not(mine))(lambda: multiply(3))
-
-
-def cross_kernel(place_ref, mine_ref, theirs_ref, out_ref):
-    out_ref[...] = (mine_ref[...] + theirs_ref[...].astype(jnp.float32)).astype(jnp.bfloat16)
-
-
-def finish_kernel(place_ref, mine_ref, theirs_ref, crossed_ref, returned_ref, hidden_ref, attended_ref, sums_ref):
-    total = mine_ref[...] + theirs_ref[...].astype(jnp.float32)
-    hidden_ref[...] = (total + crossed_ref[...].astype(jnp.float32)).astype(jnp.bfloat16)
+                start = pl.multiple_of(index * width + head * head_dim, head_dim)
+                gathered_ref[:, pl.ds(start, head_dim)] = parts[turn * chips + offset][
+                    index * rows : (index + 1) * rows, :
+                ]
+    flipped = None
+    for index in range(3):
+        pltpu.make_async_copy(weights[index], held_ref.at[index], sems.at[index]).wait()
+        term = lax.dot_general(
+            held_ref[index],
+            gathered_ref[:, index * width : (index + 1) * width],
+            contract_last,
+            preferred_element_type=jnp.float32,
+        )
+        flipped = term if flipped is None else flipped + term
+    out_ref[...] = flipped.T.astype(out_ref.dtype)
+
+
+def finish_kernel(kept_ref, crossed_ref, returned_ref, hidden_ref, attended_ref, sums_ref):
+    hidden_ref[...] = (kept_ref[...] + crossed_ref[...].astype(jnp.float32)).astype(jnp.bfloat16)
     rows = attended_ref.shape[0]
     count, owned, head_dim = sums_ref.shape
     for device in range(count):
@@ -389,16 +408,14 @@
     line = ("seq", "sub")
     smem = pl.BlockSpec(memory_space=pltpu.SMEM)
     vmem = pl.BlockSpec(memory_space=pltpu.VMEM)
-    params = pltpu.CompilerParams(vmem_limit_bytes=vmem_bytes)
+    anywhere = pl.BlockSpec(memory_space=pl.ANY)
+    params = pltpu.CompilerParams(vmem_limit_bytes=32 * mebi)
+    project_params = pltpu.CompilerParams(vmem_limit_bytes=56 * mebi)
+    input_params = pltpu.CompilerParams(vmem_limit_bytes=58 * mebi)
     pairs_seen = tokens * (tokens + rows) // 2
-    wide = 2 * head_dim
     swap = [(0, 1), (1, 0)]
     chip, side, column = (lax.axis_index(name) for name in ("seq", "sub", "head"))
-    place = jnp.stack([chip, side, side, column])
-    place_sibling = jnp.stack([chip, side, 1 - side, column])
-
-    def whole(array):
-        return pl.BlockSpec(array.shape, lambda step, at: (0,) * len(array.shape))
+    crossed_over = (side != column).astype(jnp.int32)
 
     def exchange(packed):
         return lax.all_to_all(packed, line, split_axis=0, concat_axis=0, tiled=True)
@@ -410,8 +427,8 @@
         }
         return (parts[0], moved[1], moved[2], moved[3])
 
-    def buffers(height):
-        return (jax.ShapeDtypeStruct((height, head_dim), jnp.bfloat16),) * chips
+    def buffers(height, number=chips):
+        return (jax.ShapeDtypeStruct((height, head_dim), jnp.bfloat16),) * number
 
     hidden_other = lax.ppermute(hidden, "sub", swap)
     own = (w_query, w_key, w_value)
@@ -428,37 +445,46 @@
         )(d_attended, assign)
     )
 
+    place = jnp.stack([chip, side])
+    project_scratch = [
+        pltpu.VMEM((2 * rows, half), jnp.bfloat16),
+        pltpu.VMEM((3, half, width // 2), jnp.bfloat16),
+    ]
+    project_cost = pl.CostEstimate(
+        flops=6 * rows * half * width, bytes_accessed=8 * half * width, transcendentals=0
+    )
+    near = pl.pallas_call(
+        near_kernel,
+        out_shape=jax.ShapeDtypeStruct((3, 2 * rows, width // 2), jnp.float32),
+        in_specs=[smem] + [vmem] * 2 + [anywhere] * 3,
+        out_specs=vmem,
+        scratch_shapes=project_scratch + [pltpu.SemaphoreType.DMA((3,))],
+        compiler_params=project_params,
+        cost_estimate=project_cost,
+    )(place, hidden, hidden_other, *own)
     projected = pl.pallas_call(
-        partial(project_kernel, chips),
+        far_kernel,
         out_shape=buffers(6 * rows),
-        grid_spec=pltpu.PrefetchScalarGridSpec(
-            num_scalar_prefetch=1,
-            grid=(chips // 2,),
-            in_specs=[whole(hidden)] * 2
-            + [
-                pl.BlockSpec(
-                    (half, wide), lambda step, at: (0, at[1] * (chips // 2) + ((at[0] // 2) ^ step))
-                )
-            ]
-            * 6,
-            out_specs=[pl.BlockSpec((6 * rows, head_dim), lambda step, at: (0, 0))] * chips,
-            scratch_shapes=[pltpu.VMEM((2 * rows, 2 * half), jnp.bfloat16)],
-        ),
-        compiler_params=params,
-        cost_estimate=pl.CostEstimate(
-            flops=12 * rows * half * width, bytes_accessed=8 * half * width, transcendentals=0
-        ),
-    )(place, hidden, hidden_other, *own, *other)
+        in_specs=[smem] + [vmem] * 3 + [anywhere] * 3,
+        out_specs=(vmem,) * chips,
+        scratch_shapes=project_scratch
+        + [
+            pltpu.VMEM((2 * rows, width // 2), jnp.bfloat16),
+            pltpu.SemaphoreType.DMA((3,)),
+        ],
+        compiler_params=project_params,
+        cost_estimate=project_cost,
+    )(place, hidden, hidden_other, near, *other)
     packed = exchange_chips(projected)
 
     *grads_out, outputs = pl.pallas_call(
         partial(attend_kernel, factor, scale, chips),
         out_shape=(
-            *buffers(6 * rows),
+            *buffers(3 * rows, count),
             jax.ShapeDtypeStruct((count, rows + owned, head_dim), jnp.bfloat16),
         ),
         in_specs=[smem] + [vmem] * (chips + 2),
-        out_specs=(vmem,) * (chips + 1),
+        out_specs=(vmem,) * (count + 1),
         scratch_shapes=[pltpu.VMEM((tokens, head_dim), jnp.bfloat16)] * 3
         + [pltpu.VMEM((tokens, head_dim), jnp.float32)]
         + [pltpu.VMEM((tokens, head_dim), jnp.bfloat16)]
@@ -470,55 +496,32 @@
             transcendentals=pairs_seen,
         ),
     )(place, *packed, grads, cluster_rank.reshape(1, clusters))
-    back = exchange_chips(grads_out)
-
-    steps = half // wide
-
-    def input_part(at, kind):
-        def rows_of(first):
-            return lambda step, at: (
-                jnp.where((step // steps == at[1]) == first, step % steps, 0),
-                at[1],
-            )
-
+    passing = exchange_chips(grads_out[chips:])
+    back = exchange_chips(grads_out[:chips])
+    back = (*back, *(lax.ppermute(part, "sub", swap) for part in passing))
+
+    def input_part(pick, kind):
         return pl.pallas_call(
-            partial(input_kernel, chips),
-            out_shape=jax.ShapeDtypeStruct((rows, 2 * half), kind),
-            grid_spec=pltpu.PrefetchScalarGridSpec(
-                num_scalar_prefetch=1,
-                grid=(2 * steps,),
-                in_specs=[whole(back[0])] * chips
-                + [pl.BlockSpec((wide, width // 2), rows_of(True))] * 3
-                + [pl.BlockSpec((wide, width // 2), rows_of(False))] * 3,
-                out_specs=pl.BlockSpec((rows, wide), lambda step, at: (0, step)),
-                scratch_shapes=[pltpu.VMEM((rows, 3 * width // 2), jnp.bfloat16)],
-            ),
-            compiler_params=params,
+            input_kernel,
+            out_shape=jax.ShapeDtypeStruct((rows, half), kind),
+            in_specs=[smem] + [vmem] * count + [anywhere] * 6,
+            out_specs=vmem,
+            scratch_shapes=[
+                pltpu.VMEM((rows, 3 * width), jnp.bfloat16),
+                pltpu.VMEM((3, half, width), jnp.bfloat16),
+                pltpu.SemaphoreType.DMA((3,)),
+            ],
+            compiler_params=input_params,
             cost_estimate=pl.CostEstimate(
                 flops=6 * rows * half * width, bytes_accessed=10 * half * width, transcendentals=0
             ),
-        )(at, *back, *own, *other)
-
-    theirs = lax.ppermute(input_part(place_sibling, jnp.bfloat16), "sub", swap)
-    mine = input_part(place, jnp.float32)
-
-    def half_of(pick):
-        return pl.BlockSpec((rows, half), lambda step, at: (0, pick(at)))
-
-    crossing = pl.pallas_call(
-        cross_kernel,
-        out_shape=jax.ShapeDtypeStruct((rows, half), jnp.bfloat16),
-        grid_spec=pltpu.PrefetchScalarGridSpec(
-            num_scalar_prefetch=1,
-            grid=(1,),
-            in_specs=[half_of(lambda at: 1 - at[3])] * 2,
-            out_specs=pl.BlockSpec((rows, half), lambda step, at: (0, 0)),
-        ),
-        compiler_params=params,
-    )(place, mine, theirs)
+        )(jnp.stack([chip, side, pick]), *back, *own, *other)
+
+    crossing = input_part(1 - crossed_over, jnp.bfloat16)
     crossed = lax.ppermute(crossing, "head", swap)
-    outputs, _ = lax.optimization_barrier((outputs, back[1]))
+    outputs, _ = lax.optimization_barrier((outputs, crossing))
     returned = exchange(outputs)
+    kept = input_part(crossed_over, jnp.float32)
     d_hidden, attended, centroid_sums = pl.pallas_call(
         finish_kernel,
         out_shape=(
@@ -526,18 +529,10 @@
             jax.ShapeDtypeStruct((rows, width), jnp.bfloat16),
             jax.ShapeDtypeStruct((count, owned, head_dim), jnp.float32),
         ),
-        grid_spec=pltpu.PrefetchScalarGridSpec(
-            num_scalar_prefetch=1,
-            grid=(1,),
-            in_specs=[half_of(lambda at: at[3])] * 2 + [whole(crossed), whole(returned)],
-            out_specs=(
-                pl.BlockSpec((rows, half), lambda step, at: (0, 0)),
-                pl.BlockSpec((rows, width), lambda step, at: (0, 0)),
-                pl.BlockSpec((count, owned, head_dim), lambda step, at: (0, 0, 0)),
-            ),
-        ),
+        in_specs=[vmem] * 3,
+        out_specs=(vmem,) * 3,
         compiler_params=params,
-    )(place, mine, theirs, crossed, returned)
+    )(kept, crossed, returned)
     return (attended, d_hidden, centroid_sums)
 
 

time: 173 us -> 148 us (0.86)
  waiting for transfers between devices: 64.4 us -> 45.8 us
  local copies, waits for them, and re-layouts: 23.7 us -> 6.54 us
  starting transfers between devices: 38.3 us -> 46.8 us
    unnamed x46 -> x30, local copies, waits for them, and re-layouts: 23.7 us -> 6.54 us
    ppermute x6 -> x9, waiting for transfers between devices: 49.9 us -> 39.9 us  [exchange_chips(): lax.ppermute(parts[offset], 'seq', [(at, at ^ offset) for at in range(chi...]
    ppermute x1, waiting for transfers between devices: 12.6 us -> 3.78 us  [by_head(): crossed = lax.ppermute(crossing, 'head', swap)]
    ppermute x1 -> x4, starting transfers between devices: 4.81 us -> 9.82 us  [by_head(): back = (*back, *(lax.ppermute(part, 'sub', swap) for part in passing))]
    ppermute x6 -> x9, starting transfers between devices: 15.5 us -> 19 us  [exchange_chips(): lax.ppermute(parts[offset], 'seq', [(at, at ^ offset) for at in range(chi...]
    pallas_call x4, Pallas kernels: 26.9 us -> 30.1 us  [the longest x2 16.2 us: input_part(): pl.pallas_call(input_kernel, out_shape=jax.ShapeDtypeStruct((rows, half),...]
    all_to_all x2, waiting for transfers between devices: 0.01 us -> 2.13 us  [exchange(): return lax.all_to_all(packed, line, split_axis=0, concat_axis=0, tiled=True)]
    ppermute x3, waiting for transfers between devices: 1.87 us -> 0.01 us  [by_head(): other = tuple((lax.ppermute(piece, 'sub', swap) for piece in own))]
  transfers between devices with their start and end apart: 14 -> 20, of which waited for: 7 -> 8; matrix products, arithmetic and copies ran while one was open for 0% -> 1% of each run, Pallas kernels for 12% -> 16%
where the time goes in v5:
time: 148 us; the launch traced here: 147 us
  starting transfers between devices  46.8 us (32%)
  waiting for transfers between devices  45.8 us (31%)
  Pallas kernels  44.9 us (30%)
  local copies, waits for them, and re-layouts  6.54 us (4%)
  other arithmetic  1.72 us (1%)
    ppermute x9, waiting for transfers between devices, exchange_chips(): lax.ppermute(parts[offset], 'seq', [(at, at ^ offset) for at in range(chi...  39.9 us
    ppermute x9, starting transfers between devices, exchange_chips(): lax.ppermute(parts[offset], 'seq', [(at, at ^ offset) for at in range(chi...  19 us
    pallas_call x2, Pallas kernels, input_part(): pl.pallas_call(input_kernel, out_shape=jax.ShapeDtypeStruct((rows, half),...  16.2 us
    all_to_all x2, starting transfers between devices, exchange(): return lax.all_to_all(packed, line, split_axis=0, concat_axis=0, tiled=True)  15.8 us
    pallas_call x1, Pallas kernels, by_head(): pl.pallas_call(partial(attend_kernel, factor, scale, chips), out_shape=(*...  12.7 us
    ppermute x4, starting transfers between devices, by_head(): back = (*back, *(lax.ppermute(part, 'sub', swap) for part in passing))  9.82 us
    pallas_call x1, Pallas kernels, by_head(): pl.pallas_call(far_kernel, out_shape=buffers(6 * rows), in_specs=[smem] +...  7.25 us
    pallas_call x1, Pallas kernels, by_head(): pl.pallas_call(near_kernel, out_shape=jax.ShapeDtypeStruct((3, 2 * rows,...  6.55 us
  transfers between devices with their start and end apart: 20, of which 8 were waited for; matrix products, arithmetic and copies ran while one was open for 1% of the time, Pallas kernels for 16%

profile of v5, /device:TPU:1, one launch (start us, length us, event | category | flops | bytes accessed | tf_op | source)
XLA Modules:
  0.0 146.6 jit_solution(12510180422801028646)
XLA Ops:
  0.6 0.1 collective-permute-start.1
  0.8 0.5 collective-permute-start.2
  1.2 0.1 collective-permute-start.3
  1.3 0.4 collective-permute-start
  1.7 1.0 copy-done.2
  2.8 0.7 copy-done.3
  3.5 0.9 shard_map.96
  4.4 6.4 %all-to-all-start = ((bf16[8,272,128]{2,1,0:T(8,128)(2,1)}), bf16[8,272,128]{2,1,0:T(8,128)(2,1)S(1)}, u32[]{:S(2)}, u32[]{:S(2)}) async-start(bf16[8,272,128]{2,1,0:T(8,128)(2,1)} %shard_map.96), calls=%async_computation | async-start | bytes 1114112 | tf_op jit(solution)/shard_map/all_to_all | solution.py:421
  10.7 0.6 pad_add_fusion.2.place_ref
  11.3 0.0 collective-permute-done.theirs_ref
  11.3 1.0 copy-done.7
  12.3 6.6 %shard_map.94.near_ref = f32[3,512,512]{2,1,0:T(8,128)} custom-call(s32[2]{0:T(128)} %pad_add_fusion.2.place_ref, bf16[256,2048]{1,0:T(8,128)(2,1)} %mine_ref.3, bf16[256,2048]{1,0:T(8,128)(2,1)} %copy-done.7, bf16[1024,1024]{1,0:T(8,128)(2,1)} %refs_8_.3, bf16[1024,1024]{1,0:T(8,128)(2,1)} %refs_9_.3, bf16[1024,1024]{1,0:T(8,128)(2,1)} %refs_10_.3), custom_call_target="tpu_custom_call" | custom-call | flops 1610612736 | bytes 8388608 | tf_op jit(solution)/shard_map/pallas_call | solution.py:456
  18.9 0.0 copy-start.4
  18.9 0.0 copy-start.6
  18.9 0.0 collective-permute-done.1.refs_0_.refs_11_
  18.9 0.0 collective-permute-done.2.refs_1_.refs_12_
  18.9 0.0 collective-permute-done.3.refs_2_.refs_13_
  18.9 7.3 %shard_map.95 = (bf16[1536,128]{1,0:T(8,128)(2,1)}, bf16[1536,128]{1,0:T(8,128)(2,1)}, bf16[1536,128]{1,0:T(8,128)(2,1)}, bf16[1536,128]{1,0:T(8,128)(2,1)}) custom-call(s32[2]{0:T(128)} %pad_add_fusion.2.place_ref, bf16[256,2048]{1,0:T(8,128)(2,1)} %mine_ref.3, bf16[256,2048]{1,0:T(8,128)(2,1)} %copy-done.7, f32[3,512,512]{2,1,0:T(8,128)} %shard_map.94.near_ref, ...), custom_call_target="tpu_custom_call" | custom-call | flops 1610612736 | bytes 8388608 | tf_op jit(solution)/shard_map/pallas_call | solution.py:465
  26.2 1.5 collective-permute-start.4
  27.6 2.1 %collective-permute-start.5 = (bf16[1536,128]{1,0:T(8,128)(2,1)}, bf16[1536,128]{1,0:T(8,128)(2,1)S(1)}, u32[]{:S(2)}, u32[]{:S(2)}) collective-permute-start(bf16[1536,128]{1,0:T(8,128)(2,1)} %get-tuple-element.22), channel_id=1, source_target_pairs={{0,8},{4,12},{8,0},{12,4},{1,9},{5,13},{9,1},{13,5},{2,10},{6,14},... | collective-permute-start | bytes 1179656 | tf_op jit(solution)/shard_map/ppermute | solution.py:425
  29.7 0.1 collective-permute-start.6
  29.8 0.0 all-to-all-done.refs_4_
  29.8 15.2 %collective-permute-done.4.refs_1_ = bf16[1536,128]{1,0:T(8,128)(2,1)S(1)} collective-permute-done((bf16[1536,128]{1,0:T(8,128)(2,1)}, bf16[1536,128]{1,0:T(8,128)(2,1)S(1)}, u32[]{:S(2)}, u32[]{:S(2)}) %collective-permute-start.4) | collective-permute-done | bytes 393248 | tf_op jit(solution)/shard_map/ppermute | solution.py:425
  45.0 0.0 collective-permute-done.5.refs_2_
  45.0 10.7 %collective-permute-done.6.refs_3_ = bf16[1536,128]{1,0:T(8,128)(2,1)S(1)} collective-permute-done((bf16[1536,128]{1,0:T(8,128)(2,1)}, bf16[1536,128]{1,0:T(8,128)(2,1)S(1)}, u32[]{:S(2)}, u32[]{:S(2)}) %collective-permute-start.6) | collective-permute-done | bytes 393248 | tf_op jit(solution)/shard_map/ppermute | solution.py:425
  55.7 0.0 copy-done.4
  55.7 1.0 copy-done.5
  56.7 12.7 %shard_map.97 = (bf16[768,128]{1,0:T(8,128)(2,1)S(1)}, bf16[768,128]{1,0:T(8,128)(2,1)S(1)}, bf16[768,128]{1,0:T(8,128)(2,1)S(1)}, bf16[768,128]{1,0:T(8,128)(2,...) custom-call(s32[2]{0:T(128)S(1)} %copy-done.4, ...), custom_call_target="tpu_custom_call" | custom-call | flops 3623878656 | bytes 4194304 | tf_op jit(solution)/shard_map/pallas_call | solution.py:480
  69.4 0.7 copy-done.1
  70.1 8.7 %collective-permute-start.11 = (bf16[768,128]{1,0:T(8,128)(2,1)S(1)}, bf16[768,128]{1,0:T(8,128)(2,1)S(1)}, u32[]{:S(2)}, u32[]{:S(2)}) collective-permute-start(bf16[768,128]{1,0:T(8,128)(2,1)S(1)} %get-tuple-element.29), channel_id=1, source_target_pairs={{0,4},{4,0},{8,12},{12,8},{1,5},{5,1},{9,13},{13,9},{2,6},{6,2},{1... | collective-permute-start | bytes 589832 | tf_op jit(solution)/shard_map/ppermute | solution.py:425
  78.8 0.9 collective-permute-start.13
  79.7 1.2 collective-permute-start.15
  80.9 2.0 %collective-permute-start.10 = (bf16[768,128]{1,0:T(8,128)(2,1)S(1)}, bf16[768,128]{1,0:T(8,128)(2,1)S(1)}, u32[]{:S(2)}, u32[]{:S(2)}) collective-permute-start(bf16[768,128]{1,0:T(8,128)(2,1)S(1)} %get-tuple-element.28), channel_id=1, source_target_pairs={{0,1},{1,0},{2,3},{3,2},{4,5},{5,4},{6,7},{7,6},{8,9},{9,8},{10,11... | collective-permute-start | bytes 589832 | tf_op jit(solution)/shard_map/ppermute | solution.py:501
  82.9 0.8 collective-permute-start.7
  83.8 0.8 collective-permute-done.11
  84.6 0.8 collective-permute-start.8
  85.3 0.5 collective-permute-done.13
  85.8 2.9 %collective-permute-start.9 = (bf16[768,128]{1,0:T(8,128)(2,1)S(1)}, bf16[768,128]{1,0:T(8,128)(2,1)S(1)}, u32[]{:S(2)}, u32[]{:S(2)}) collective-permute-start(bf16[768,128]{1,0:T(8,128)(2,1)S(1)} %get-tuple-element.27), channel_id=1, source_target_pairs={{0,12},{4,8},{8,4},{12,0},{1,13},{5,9},{9,5},{13,1},{2,14},{6,10},... | collective-permute-start | bytes 589832 | tf_op jit(solution)/shard_map/ppermute | solution.py:425
  88.7 4.1 %collective-permute-done.15 = bf16[768,128]{1,0:T(8,128)(2,1)S(1)} collective-permute-done((bf16[768,128]{1,0:T(8,128)(2,1)S(1)}, bf16[768,128]{1,0:T(8,128)(2,1)S(1)}, u32[]{:S(2)}, u32[]{:S(2)}) %collective-permute-start.15) | collective-permute-done | bytes 196640 | tf_op jit(solution)/shard_map/ppermute | solution.py:425
  92.8 7.3 %collective-permute-start.12 = (bf16[768,128]{1,0:T(8,128)(2,1)S(1)}, bf16[768,128]{1,0:T(8,128)(2,1)S(1)}, u32[]{:S(2)}, u32[]{:S(2)}) collective-permute-start(bf16[768,128]{1,0:T(8,128)(2,1)S(1)} %collective-permute-done.11), channel_id=1, source_target_pairs={{0,1},{1,0},{2,3},{3,2},{4,5},{5,4},{6,7},{7,6},{8,9},{9,8},{10,11... | collective-permute-start | bytes 589832 | tf_op jit(solution)/shard_map/ppermute | solution.py:501
  100.1 0.0 collective-permute-done.10.refs_4_
  100.1 0.1 collective-permute-start.14
  100.2 0.0 collective-permute-done.7.refs_1_
  100.2 0.4 collective-permute-start.16
  100.6 0.6 pad_add_fusion.3.place_ref
  101.2 8.6 %collective-permute-done.8.refs_2_ = bf16[768,128]{1,0:T(8,128)(2,1)S(1)} collective-permute-done((bf16[768,128]{1,0:T(8,128)(2,1)S(1)}, bf16[768,128]{1,0:T(8,128)(2,1)S(1)}, u32[]{:S(2)}, u32[]{:S(2)}) %collective-permute-start.8) | collective-permute-done | bytes 196640 | tf_op jit(solution)/shard_map/ppermute | solution.py:425
  109.9 0.0 collective-permute-done.9.refs_3_
  109.9 0.0 collective-permute-done.12.refs_5_
  109.9 0.0 collective-permute-done.14.refs_6_
  109.9 0.0 collective-permute-done.16.refs_7_
  110.0 0.6 copy-done.10
  110.5 0.1 copy-done.11
  110.6 0.1 copy-done.12
  110.7 0.1 copy-done.13
  110.8 0.1 copy-done.14
  110.8 8.0 %shard_map.99 = bf16[256,1024]{1,0:T(8,128)(2,1)} custom-call(s32[3]{0:T(128)} %pad_add_fusion.3.place_ref, bf16[768,128]{1,0:T(8,128)(2,1)} %copy-done.1, bf16[768,128]{1,0:T(8,128)(2,1)} %copy-done.9, bf16[768,128]{1,0:T(8,128)(2,1)} %copy-done.10, bf16[768,128]{1,0:T(8,128)(2,1)} %copy-done.11, bf16[768,128]{1,0:T(8,128)(2,1)} %copy-done.8, ...), custom_call_target="tpu_custom_call" | custom-call | flops 1610612736 | bytes 10485760 | tf_op jit(solution)/shard_map/pallas_call | solution.py:504
  118.8 9.4 %all-to-all-start.1 = ((bf16[8,288,128]{2,1,0:T(8,128)(2,1)}), bf16[8,288,128]{2,1,0:T(8,128)(2,1)S(1)}, u32[]{:S(2)}, u32[]{:S(2)}) async-start(bf16[8,288,128]{2,1,0:T(8,128)(2,1)} %get-tuple-element.33), calls=%async_computation.1 | async-start | bytes 1179648 | tf_op jit(solution)/shard_map/all_to_all | solution.py:421
  128.3 1.1 collective-permute-start.17
  129.4 0.6 pad_add_fusion.place_ref
  130.0 8.2 %shard_map.98.kept_ref = f32[256,1024]{1,0:T(8,128)} custom-call(s32[3]{0:T(128)} %pad_add_fusion.place_ref, bf16[768,128]{1,0:T(8,128)(2,1)} %copy-done.1, bf16[768,128]{1,0:T(8,128)(2,1)} %copy-done.9, bf16[768,128]{1,0:T(8,128)(2,1)} %copy-done.10, bf16[768,128]{1,0:T(8,128)(2,1)} %copy-done.11, bf16[768,128]{1,0:T(8,128)(2,1)} %copy-done.8, ...), custom_call_target="tpu_custom_call" | custom-call | flops 1610612736 | bytes 10485760 | tf_op jit(solution)/shard_map/pallas_call | solution.py:504
  138.3 3.8 %collective-permute-done.17.crossed_ref = bf16[256,1024]{1,0:T(8,128)(2,1)S(1)} collective-permute-done((bf16[256,1024]{1,0:T(8,128)(2,1)}, bf16[256,1024]{1,0:T(8,128)(2,1)S(1)}, u32[]{:S(2)}, u32[]{:S(2)}) %collective-permute-start.17) | collective-permute-done | bytes 524320 | tf_op jit(solution)/shard_map/ppermute | solution.py:521
  142.0 2.1 %all-to-all-done.1.returned_ref = bf16[8,288,128]{2,1,0:T(8,128)(2,1)S(1)} async-done(((bf16[8,288,128]{2,1,0:T(8,128)(2,1)}), bf16[8,288,128]{2,1,0:T(8,128)(2,1)S(1)}, u32[]{:S(2)}, u32[]{:S(2)}) %all-to-all-start.1) | async-done | bytes 589856 | tf_op jit(solution)/shard_map/all_to_all | solution.py:421
  144.2 1.2 copy-done
  145.4 1.2 shard_map.100
  (16 shorter events, 0.0 us)
Async XLA Ops:
  0.6 18.2 %collective-permute-start.1 = (bf16[1024,1024]{1,0:T(8,128)(2,1)}, bf16[1024,1024]{1,0:T(8,128)(2,1)}, u32[]{:S(2)}, u32[]{:S(2)}) collective-permute-start(bf16[1024,1024]{1,0:T(8,128)(2,1)} %refs_8_.3), channel_id=1, source_target_pairs={{0,1},{1,0},{2,3},{3,2},{4,5},{5,4},{6,7},{7,6},{8,9},{9,8},{10,11... | collective-permute-start | bytes 6291464 | tf_op jit(solution)/shard_map/ppermute | solution.py:435
  0.8 18.1 %collective-permute-start.2 = (bf16[1024,1024]{1,0:T(8,128)(2,1)}, bf16[1024,1024]{1,0:T(8,128)(2,1)}, u32[]{:S(2)}, u32[]{:S(2)}) collective-permute-start(bf16[1024,1024]{1,0:T(8,128)(2,1)} %refs_9_.3), channel_id=1, source_target_pairs={{0,1},{1,0},{2,3},{3,2},{4,5},{5,4},{6,7},{7,6},{8,9},{9,8},{10,11... | collective-permute-start | bytes 6291464 | tf_op jit(solution)/shard_map/ppermute | solution.py:435
  1.2 17.7 %collective-permute-start.3 = (bf16[1024,1024]{1,0:T(8,128)(2,1)}, bf16[1024,1024]{1,0:T(8,128)(2,1)}, u32[]{:S(2)}, u32[]{:S(2)}) collective-permute-start(bf16[1024,1024]{1,0:T(8,128)(2,1)} %refs_10_.3), channel_id=1, source_target_pairs={{0,1},{1,0},{2,3},{3,2},{4,5},{5,4},{6,7},{7,6},{8,9},{9,8},{10,11... | collective-permute-start | bytes 6291464 | tf_op jit(solution)/shard_map/ppermute | solution.py:435
  1.3 10.0 %collective-permute-start = (bf16[256,2048]{1,0:T(8,128)(2,1)}, bf16[256,2048]{1,0:T(8,128)(2,1)S(1)}, u32[]{:S(2)}, u32[]{:S(2)}) collective-permute-start(bf16[256,2048]{1,0:T(8,128)(2,1)} %mine_ref.3), channel_id=1, source_target_pairs={{0,1},{1,0},{2,3},{3,2},{4,5},{5,4},{6,7},{7,6},{8,9},{9,8},{10,11... | collective-permute-start | bytes 3145736 | tf_op jit(solution)/shard_map/ppermute | solution.py:433
  1.7 1.0 copy-start.2
  2.8 0.7 copy-start.3
  4.4 25.4 %all-to-all-start = ((bf16[8,272,128]{2,1,0:T(8,128)(2,1)}), bf16[8,272,128]{2,1,0:T(8,128)(2,1)S(1)}, u32[]{:S(2)}, u32[]{:S(2)}) async-start(bf16[8,272,128]{2,1,0:T(8,128)(2,1)} %shard_map.96), calls=%async_computation | async-start | bytes 1114112 | tf_op jit(solution)/shard_map/all_to_all | solution.py:421
  11.3 1.0 copy-start.7
  18.9 36.8 %copy-start.4 = (s32[2]{0:T(128)S(1)}, s32[2]{0:T(128)}, u32[]{:S(2)}) copy-start(s32[2]{0:T(128)} %pad_add_fusion.2.place_ref) | copy-start | bytes 28
  18.9 36.8 %copy-start.6 = (s32[256]{0:T(256)S(1)}, s32[256]{0:T(256)}, u32[]{:S(2)}) copy-start(s32[256]{0:T(256)} %param.11) | copy-start | bytes 3076
  26.2 18.8 %collective-permute-start.4 = (bf16[1536,128]{1,0:T(8,128)(2,1)}, bf16[1536,128]{1,0:T(8,128)(2,1)S(1)}, u32[]{:S(2)}, u32[]{:S(2)}) collective-permute-start(bf16[1536,128]{1,0:T(8,128)(2,1)} %get-tuple-element.21), channel_id=1, source_target_pairs={{0,4},{4,0},{8,12},{12,8},{1,5},{5,1},{9,13},{13,9},{2,6},{6,2},{1... | collective-permute-start | bytes 1179656 | tf_op jit(solution)/shard_map/ppermute | solution.py:425
  27.6 17.3 %collective-permute-start.5 = (bf16[1536,128]{1,0:T(8,128)(2,1)}, bf16[1536,128]{1,0:T(8,128)(2,1)S(1)}, u32[]{:S(2)}, u32[]{:S(2)}) collective-permute-start(bf16[1536,128]{1,0:T(8,128)(2,1)} %get-tuple-element.22), channel_id=1, source_target_pairs={{0,8},{4,12},{8,0},{12,4},{1,9},{5,13},{9,1},{13,5},{2,10},{6,14},... | collective-permute-start | bytes 1179656 | tf_op jit(solution)/shard_map/ppermute | solution.py:425
  29.7 26.0 %collective-permute-start.6 = (bf16[1536,128]{1,0:T(8,128)(2,1)}, bf16[1536,128]{1,0:T(8,128)(2,1)S(1)}, u32[]{:S(2)}, u32[]{:S(2)}) collective-permute-start(bf16[1536,128]{1,0:T(8,128)(2,1)} %get-tuple-element.23), channel_id=1, source_target_pairs={{0,12},{4,8},{8,4},{12,0},{1,13},{5,9},{9,5},{13,1},{2,14},{6,10},... | collective-permute-start | bytes 1179656 | tf_op jit(solution)/shard_map/ppermute | solution.py:425
  55.7 1.0 copy-start.5
  69.4 0.7 copy-start.1
  70.1 14.5 %collective-permute-start.11 = (bf16[768,128]{1,0:T(8,128)(2,1)S(1)}, bf16[768,128]{1,0:T(8,128)(2,1)S(1)}, u32[]{:S(2)}, u32[]{:S(2)}) collective-permute-start(bf16[768,128]{1,0:T(8,128)(2,1)S(1)} %get-tuple-element.29), channel_id=1, source_target_pairs={{0,4},{4,0},{8,12},{12,8},{1,5},{5,1},{9,13},{13,9},{2,6},{6,2},{1... | collective-permute-start | bytes 589832 | tf_op jit(solution)/shard_map/ppermute | solution.py:425
  78.8 6.9 %collective-permute-start.13 = (bf16[768,128]{1,0:T(8,128)(2,1)S(1)}, bf16[768,128]{1,0:T(8,128)(2,1)S(1)}, u32[]{:S(2)}, u32[]{:S(2)}) collective-permute-start(bf16[768,128]{1,0:T(8,128)(2,1)S(1)} %get-tuple-element.30), channel_id=1, source_target_pairs={{0,8},{4,12},{8,0},{12,4},{1,9},{5,13},{9,1},{13,5},{2,10},{6,14},... | collective-permute-start | bytes 589832 | tf_op jit(solution)/shard_map/ppermute | solution.py:425
  79.7 13.1 %collective-permute-start.15 = (bf16[768,128]{1,0:T(8,128)(2,1)S(1)}, bf16[768,128]{1,0:T(8,128)(2,1)S(1)}, u32[]{:S(2)}, u32[]{:S(2)}) collective-permute-start(bf16[768,128]{1,0:T(8,128)(2,1)S(1)} %get-tuple-element.31), channel_id=1, source_target_pairs={{0,12},{4,8},{8,4},{12,0},{1,13},{5,9},{9,5},{13,1},{2,14},{6,10},... | collective-permute-start | bytes 589832 | tf_op jit(solution)/shard_map/ppermute | solution.py:425
  80.9 19.2 %collective-permute-start.10 = (bf16[768,128]{1,0:T(8,128)(2,1)S(1)}, bf16[768,128]{1,0:T(8,128)(2,1)S(1)}, u32[]{:S(2)}, u32[]{:S(2)}) collective-permute-start(bf16[768,128]{1,0:T(8,128)(2,1)S(1)} %get-tuple-element.28), channel_id=1, source_target_pairs={{0,1},{1,0},{2,3},{3,2},{4,5},{5,4},{6,7},{7,6},{8,9},{9,8},{10,11... | collective-permute-start | bytes 589832 | tf_op jit(solution)/shard_map/ppermute | solution.py:501
  82.9 17.3 %collective-permute-start.7 = (bf16[768,128]{1,0:T(8,128)(2,1)S(1)}, bf16[768,128]{1,0:T(8,128)(2,1)S(1)}, u32[]{:S(2)}, u32[]{:S(2)}) collective-permute-start(bf16[768,128]{1,0:T(8,128)(2,1)S(1)} %get-tuple-element.25), channel_id=1, source_target_pairs={{0,4},{4,0},{8,12},{12,8},{1,5},{5,1},{9,13},{13,9},{2,6},{6,2},{1... | collective-permute-start | bytes 589832 | tf_op jit(solution)/shard_map/ppermute | solution.py:425
  84.6 25.3 %collective-permute-start.8 = (bf16[768,128]{1,0:T(8,128)(2,1)S(1)}, bf16[768,128]{1,0:T(8,128)(2,1)S(1)}, u32[]{:S(2)}, u32[]{:S(2)}) collective-permute-start(bf16[768,128]{1,0:T(8,128)(2,1)S(1)} %get-tuple-element.26), channel_id=1, source_target_pairs={{0,8},{4,12},{8,0},{12,4},{1,9},{5,13},{9,1},{13,5},{2,10},{6,14},... | collective-permute-start | bytes 589832 | tf_op jit(solution)/shard_map/ppermute | solution.py:425
  85.8 24.1 %collective-permute-start.9 = (bf16[768,128]{1,0:T(8,128)(2,1)S(1)}, bf16[768,128]{1,0:T(8,128)(2,1)S(1)}, u32[]{:S(2)}, u32[]{:S(2)}) collective-permute-start(bf16[768,128]{1,0:T(8,128)(2,1)S(1)} %get-tuple-element.27), channel_id=1, source_target_pairs={{0,12},{4,8},{8,4},{12,0},{1,13},{5,9},{9,5},{13,1},{2,14},{6,10},... | collective-permute-start | bytes 589832 | tf_op jit(solution)/shard_map/ppermute | solution.py:425
  92.8 17.0 %collective-permute-start.12 = (bf16[768,128]{1,0:T(8,128)(2,1)S(1)}, bf16[768,128]{1,0:T(8,128)(2,1)S(1)}, u32[]{:S(2)}, u32[]{:S(2)}) collective-permute-start(bf16[768,128]{1,0:T(8,128)(2,1)S(1)} %collective-permute-done.11), channel_id=1, source_target_pairs={{0,1},{1,0},{2,3},{3,2},{4,5},{5,4},{6,7},{7,6},{8,9},{9,8},{10,11... | collective-permute-start | bytes 589832 | tf_op jit(solution)/shard_map/ppermute | solution.py:501
  100.1 9.8 %copy-start.8 = (bf16[768,128]{1,0:T(8,128)(2,1)}, bf16[768,128]{1,0:T(8,128)(2,1)S(1)}, u32[]{:S(2)}) copy-start(bf16[768,128]{1,0:T(8,128)(2,1)S(1)} %collective-permute-done.10.refs_4_) | copy-start | bytes 589828
  100.1 9.8 %collective-permute-start.14 = (bf16[768,128]{1,0:T(8,128)(2,1)S(1)}, bf16[768,128]{1,0:T(8,128)(2,1)S(1)}, u32[]{:S(2)}, u32[]{:S(2)}) collective-permute-start(bf16[768,128]{1,0:T(8,128)(2,1)S(1)} %collective-permute-done.13), channel_id=1, source_target_pairs={{0,1},{1,0},{2,3},{3,2},{4,5},{5,4},{6,7},{7,6},{8,9},{9,8},{10,11... | collective-permute-start | bytes 589832 | tf_op jit(solution)/shard_map/ppermute | solution.py:501
  100.2 9.7 %copy-start.9 = (bf16[768,128]{1,0:T(8,128)(2,1)}, bf16[768,128]{1,0:T(8,128)(2,1)S(1)}, u32[]{:S(2)}) copy-start(bf16[768,128]{1,0:T(8,128)(2,1)S(1)} %collective-permute-done.7.refs_1_) | copy-start | bytes 589828
  100.2 9.7 %collective-permute-start.16 = (bf16[768,128]{1,0:T(8,128)(2,1)S(1)}, bf16[768,128]{1,0:T(8,128)(2,1)S(1)}, u32[]{:S(2)}, u32[]{:S(2)}) collective-permute-start(bf16[768,128]{1,0:T(8,128)(2,1)S(1)} %collective-permute-done.15), channel_id=1, source_target_pairs={{0,1},{1,0},{2,3},{3,2},{4,5},{5,4},{6,7},{7,6},{8,9},{9,8},{10,11... | collective-permute-start | bytes 589832 | tf_op jit(solution)/shard_map/ppermute | solution.py:501
  109.9 0.7 copy-start.10
  109.9 0.8 copy-start.11
  109.9 0.8 copy-start.12
  109.9 0.8 copy-start.13
  109.9 0.9 copy-start.14
  118.8 25.3 %all-to-all-start.1 = ((bf16[8,288,128]{2,1,0:T(8,128)(2,1)}), bf16[8,288,128]{2,1,0:T(8,128)(2,1)S(1)}, u32[]{:S(2)}, u32[]{:S(2)}) async-start(bf16[8,288,128]{2,1,0:T(8,128)(2,1)} %get-tuple-element.33), calls=%async_computation.1 | async-start | bytes 1179648 | tf_op jit(solution)/shard_map/all_to_all | solution.py:421
  128.3 13.8 %collective-permute-start.17 = (bf16[256,1024]{1,0:T(8,128)(2,1)}, bf16[256,1024]{1,0:T(8,128)(2,1)S(1)}, u32[]{:S(2)}, u32[]{:S(2)}) collective-permute-start(bf16[256,1024]{1,0:T(8,128)(2,1)} %shard_map.99), channel_id=1, source_target_pairs={{0,2},{2,0},{1,3},{3,1},{4,6},{6,4},{5,7},{7,5},{8,10},{10,8},{9,1... | collective-permute-start | bytes 1572872 | tf_op jit(solution)/shard_map/ppermute | solution.py:521
  144.2 1.2 copy-start

commit v6 on v0

--- a/solution.py
+++ b/solution.py
@@ -3,6 +3,8 @@
 import jax
 import jax.numpy as jnp
 from jax import lax
+from jax.experimental import pallas as pl
+from jax.experimental.pallas import tpu as pltpu
 from jax.sharding import PartitionSpec as P
 
 epsilon = 1e-06
@@ -58,7 +60,7 @@
     return (grad_query, grad_key, grad_value)
 
 
-def per_device(hidden, w_query, w_key, w_value, cluster_rank, assign, d_attended):
+def by_owner(hidden, w_query, w_key, w_value, cluster_rank, assign, d_attended):
     tok_rows = hidden.shape[0]
     heads_here = assign.shape[0]
     head_dim = w_query.shape[1] // heads_here
@@ -185,6 +187,476 @@
     return (attended, d_hidden, centroid_sums)
 
 
+contract_last = (((1,), (1,)), ((), ()))
+contract_first = (((0,), (0,)), ((), ()))
+log2_e = 1.4426950408889634
+mebi = 1024 * 1024
+
+
+def id_lines(rows, head_dim):
+    return -(-(rows // head_dim) // 16) * 16
+
+
+def pack_kernel(place_ref, grads_ref, assign_ref, mine_ref, theirs_ref):
+    chips, padded, head_dim = mine_ref.shape
+    rows = grads_ref.shape[0]
+    spare = padded - rows - rows // head_dim
+    for turn, out_ref in enumerate((mine_ref, theirs_ref)):
+        for chip in range(chips):
+            head = (place_ref[1] ^ turn) * chips + chip
+            at = pl.multiple_of(head * head_dim, head_dim)
+            out_ref[chip, :rows, :] = grads_ref[:, pl.ds(at, head_dim)]
+            ids = assign_ref[pl.ds(head, 1), :].astype(jnp.float32)
+            lines = [
+                ids[:, start : start + head_dim] for start in range(0, rows, head_dim)
+            ] + [jnp.zeros((spare, head_dim), jnp.float32)]
+            out_ref[chip, rows:, :] = jnp.concatenate(lines, axis=0).astype(jnp.bfloat16)
+
+
+def merge_kernel(place_ref, mine_ref, theirs_ref, *out_refs):
+    height = mine_ref.shape[1]
+    for turn, held_ref in enumerate((mine_ref, theirs_ref)):
+        at = pl.ds(pl.multiple_of((place_ref[1] ^ turn) * height, height), height)
+        for offset, out_ref in enumerate(out_refs):
+            out_ref[at, :] = held_ref[place_ref[0] ^ offset]
+
+
+def fetch_columns(half, weights, held_ref, sems):
+    chunks = sems.shape[1]
+    columns = held_ref.shape[2]
+    rows = held_ref.shape[1] // chunks
+    at = pl.ds(pl.multiple_of(half * columns, columns), columns)
+    copies = []
+    for index, weight in enumerate(weights):
+        for chunk in range(chunks):
+            lines = pl.ds(chunk * rows, rows)
+            copy = pltpu.make_async_copy(
+                weight.at[lines, at], held_ref.at[index, lines], sems.at[index, chunk]
+            )
+            copy.start()
+            copies.append(copy)
+    return copies
+
+
+def project_kernel(count, turn, place_ref, mine_ref, theirs_ref, *refs):
+    weights, refs = refs[:count], refs[count:]
+    if turn == 0:
+        arrived_ref, refs = refs[0], refs[1:]
+    out_refs, (joined_ref, held_ref, low_ref, sems) = refs[:-4], refs[-4:]
+    side = place_ref[1]
+    rows, depth = mine_ref.shape[0], joined_ref.shape[1]
+    tall = 2 * rows
+    copies = fetch_columns(side ^ turn, weights, held_ref, sems)
+    near = pl.ds(pl.multiple_of(side * depth, depth), depth)
+    joined_ref[pl.ds(pl.multiple_of(side * rows, rows), rows), :] = mine_ref[:, near]
+    joined_ref[pl.ds(pl.multiple_of((1 - side) * rows, rows), rows), :] = theirs_ref[:, near]
+    chunks = sems.shape[1]
+    for index in range(count):
+        for chunk in range(chunks):
+            copies[index * chunks + chunk].wait()
+        total = jnp.dot(joined_ref[...], held_ref[index], preferred_element_type=jnp.float32)
+        if turn == 1:
+            out_refs[0][index] = total.astype(jnp.bfloat16)
+            continue
+        low_ref[...] = (total + arrived_ref[index].astype(jnp.float32)).astype(jnp.bfloat16)
+        for offset, out_ref in enumerate(out_refs):
+            head_dim = out_ref.shape[1]
+            at = pl.multiple_of((place_ref[0] ^ offset) * head_dim, head_dim)
+            out_ref[index * tall : (index + 1) * tall, :] = low_ref[:, pl.ds(at, head_dim)]
+
+
+def in_order(place, parts, start, ordered):
+    for offset, part in enumerate(parts):
+        tall = ordered.shape[0] // len(parts)
+        at = pl.ds(pl.multiple_of((place ^ offset) * tall, tall), tall)
+        ordered[at, :] = part[start : start + tall, :]
+
+
+def order_grads(place, parts, rows, grad_rows, id_rows, id_cols):
+    head_dim = grad_rows.shape[1]
+    height = parts[0].shape[0] // 2
+    for offset, part in enumerate(parts):
+        for core in range(2):
+            block = (place ^ offset) * 2 + core
+            at = pl.ds(pl.multiple_of(block * rows, rows), rows)
+            start = core * height
+            grad_rows[at, :] = part[start : start + rows, :]
+            lines = part[start + rows : start + rows + 16, :].astype(jnp.float32)
+            ids = jnp.concatenate(
+                [lines[line : line + 1, :] for line in range(rows // head_dim)], axis=1
+            )
+            id_rows[block] = jnp.broadcast_to(ids, id_rows.shape[1:])
+            id_cols[at, :] = jnp.broadcast_to(ids, (head_dim, rows)).T
+
+
+def block_scores(factor, block, rows, queries, keys_in, id_rows, id_cols):
+    head_dim = queries.shape[1]
+    seen = (block + 1) * rows
+    scores = lax.dot_general(
+        keys_in[:seen, :],
+        queries[block * rows : seen, :],
+        contract_last,
+        preferred_element_type=jnp.float32,
+    )
+    ids = id_cols[:seen, :]
+    mine = id_rows[block][:1, :]
+    same = jnp.concatenate(
+        [ids == mine[:, start : start + head_dim] for start in range(0, rows, head_dim)], axis=1
+    )
+    key_at = lax.broadcasted_iota(jnp.int32, (rows, rows), 0)
+    query_at = lax.broadcasted_iota(jnp.int32, (rows, rows), 1)
+    last = same[seen - rows :] & (key_at <= query_at)
+    allowed = last if block == 0 else jnp.concatenate([same[: seen - rows], last], axis=0)
+    return jnp.where(allowed, scores * factor, -jnp.inf)
+
+
+def value_grad_kernel(factor, chips, rows, place_ref, *refs):
+    packed, grads = refs[:chips], refs[chips : 2 * chips]
+    out_refs, lse_ref = refs[2 * chips : 3 * chips], refs[3 * chips]
+    queries, keys_in, grad_rows, id_rows, id_cols, total_ref = refs[3 * chips + 1 :]
+    tall = 2 * rows
+    place = place_ref[0]
+    in_order(place, packed, 0, queries)
+    in_order(place, packed, tall, keys_in)
+    order_grads(place, grads, rows, grad_rows, id_rows, id_cols)
+    total_ref[...] = jnp.zeros_like(total_ref)
+    for block in range(2 * chips):
+        seen = (block + 1) * rows
+        scores = block_scores(factor, block, rows, queries, keys_in, id_rows, id_cols)
+        top = jnp.max(scores, axis=0, keepdims=True)
+        expd = jnp.exp2(scores - top)
+        total = jnp.sum(expd, axis=0, keepdims=True)
+        lse_ref[block : block + 1, :] = top + jnp.log2(total)
+        total_ref[:seen, :] += jnp.dot(
+            (expd * (1.0 / total)).astype(jnp.bfloat16),
+            grad_rows[block * rows : seen, :],
+            preferred_element_type=jnp.float32,
+        )
+    for offset, out_ref in enumerate(out_refs):
+        at = pl.multiple_of((place ^ offset) * tall, tall)
+        out_ref[...] = total_ref[pl.ds(at, tall), :].astype(jnp.bfloat16)
+
+
+def query_grad_kernel(factor, scale, chips, rows, place_ref, *refs):
+    packed, valued, grads = refs[:chips], refs[chips : 2 * chips], refs[2 * chips : 3 * chips]
+    lse_ref, rank_ref = refs[3 * chips : 3 * chips + 2]
+    refs = refs[3 * chips + 2 :]
+    grad_refs, out_refs, refs = refs[:chips], refs[chips : 2 * chips], refs[2 * chips :]
+    queries, keys_in, values, grad_rows, id_rows, id_cols, total_ref, dq_ref, attended_ref = refs
+    head_dim = queries.shape[1]
+    clusters = rank_ref.shape[1]
+    tall = 2 * rows
+    place = place_ref[0]
+    in_order(place, packed, 0, queries)
+    in_order(place, packed, tall, keys_in)
+    in_order(place, valued, 0, values)
+    order_grads(place, grads, rows, grad_rows, id_rows, id_cols)
+    total_ref[...] = jnp.zeros_like(total_ref)
+    for block in range(2 * chips):
+        seen = (block + 1) * rows
+        mine = slice(block * rows, seen)
+        scores = block_scores(factor, block, rows, queries, keys_in, id_rows, id_cols)
+        probs = jnp.exp2(scores - lse_ref[block : block + 1, :])
+        seen_values = values[:seen, :]
+        grad_probs = lax.dot_general(
+            seen_values, grad_rows[mine, :], contract_last, preferred_element_type=jnp.float32
+        )
+        flipped = lax.dot_general(
+            seen_values,
+            probs.astype(jnp.bfloat16),
+            contract_first,
+            preferred_element_type=jnp.float32,
+        )
+        attended_ref[mine, :] = flipped.T.astype(jnp.bfloat16)
+        weighted = probs * grad_probs
+        delta = jnp.sum(weighted, axis=0, keepdims=True)
+        grad_low = (weighted - probs * delta).astype(jnp.bfloat16)
+        total_ref[:seen, :] += jnp.dot(
+            grad_low, queries[mine, :], preferred_element_type=jnp.float32
+        )
+        flipped = lax.dot_general(
+            keys_in[:seen, :], grad_low, contract_first, preferred_element_type=jnp.float32
+        )
+        dq_ref[mine, :] = (flipped.T * scale).astype(jnp.bfloat16)
+    sums = jnp.zeros((clusters, head_dim), jnp.float32)
+    cluster_at = lax.broadcasted_iota(jnp.int32, (clusters, rows), 0).astype(jnp.float32)
+    for block in range(2 * chips):
+        keys_float = keys_in[block * rows : (block + 1) * rows, :].astype(jnp.float32)
+        unit = keys_float * lax.rsqrt(
+            jnp.sum(keys_float * keys_float, axis=1, keepdims=True) + epsilon
+        )
+        unit_high = unit.astype(jnp.bfloat16)
+        unit_low = (unit - unit_high.astype(jnp.float32)).astype(jnp.bfloat16)
+        member = jnp.where(cluster_at == id_rows[block][:1, :], 1.0, 0.0).astype(jnp.bfloat16)
+        sums += jnp.dot(member, unit_high, preferred_element_type=jnp.float32)
+        sums += jnp.dot(member, unit_low, preferred_element_type=jnp.float32)
+    rank_at = lax.broadcasted_iota(jnp.int32, (clusters, clusters), 0)
+    ordered = jnp.where(rank_at == rank_ref[...], 1.0, 0.0).astype(jnp.bfloat16)
+    ranked = jnp.dot(ordered, sums.astype(jnp.bfloat16), preferred_element_type=jnp.float32)
+    attended_ref[2 * chips * rows :, :] = ranked.astype(jnp.bfloat16)
+    owned = clusters // (2 * chips)
+    for offset in range(chips):
+        at = pl.ds(pl.multiple_of((place ^ offset) * tall, tall), tall)
+        grad_refs[offset][:tall, :] = dq_ref[at, :]
+        grad_refs[offset][tall:, :] = (total_ref[at, :] * scale).astype(jnp.bfloat16)
+        for core in range(2):
+            shard = (place ^ offset) * 2 + core
+            start = core * (rows + owned)
+            at = pl.ds(pl.multiple_of(shard * rows, rows), rows)
+            out_refs[offset][start : start + rows, :] = attended_ref[at, :]
+            at = pl.ds(pl.multiple_of(2 * chips * rows + shard * owned, owned), owned)
+            out_refs[offset][start + rows : start + rows + owned, :] = attended_ref[at, :]
+
+
+def stage_kernel(*refs):
+    weights, (held_ref, sems) = refs[:-2], refs[-2:]
+    copies = [
+        pltpu.make_async_copy(weight, held_ref.at[index], sems.at[index])
+        for index, weight in enumerate(weights)
+    ]
+    for copy in copies:
+        copy.start()
+    for copy in copies:
+        copy.wait()
+
+
+def input_kernel(chips, place_ref, *refs):
+    held_ref, out_ref, gathered_ref = refs[4 * chips :]
+    rows, width = out_ref.shape[0], held_ref.shape[2]
+    head_dim = width // (2 * chips)
+    for turn in range(2):
+        parts = refs[turn * chips : (turn + 1) * chips]
+        valued = refs[(2 + turn) * chips : (3 + turn) * chips]
+        for offset in range(chips):
+            head = (place_ref[1] ^ turn) * chips + (place_ref[0] ^ offset)
+            for index in range(3):
+                source = parts[offset] if index < 2 else valued[offset]
+                at = pl.multiple_of((2 * (index % 2) + place_ref[2]) * rows, rows)
+                start = pl.multiple_of(index * width + head * head_dim, head_dim)
+                gathered_ref[:, pl.ds(start, head_dim)] = source[pl.ds(at, rows), :]
+    flipped = None
+    for index in range(3):
+        term = lax.dot_general(
+            held_ref[index],
+            gathered_ref[:, index * width : (index + 1) * width],
+            contract_last,
+            preferred_element_type=jnp.float32,
+        )
+        flipped = term if flipped is None else flipped + term
+    out_ref[...] = flipped.T.astype(out_ref.dtype)
+
+
+def finish_kernel(chips, place_ref, first_ref, second_ref, kept_ref, *refs):
+    parts, (hidden_ref, attended_ref, sums_ref) = refs[: 2 * chips], refs[2 * chips :]
+    side = place_ref[1]
+    second = jnp.where(place_ref[2] == side, kept_ref[...], second_ref[...])
+    total = first_ref[...].astype(jnp.float32) + second.astype(jnp.float32)
+    hidden_ref[...] = total.astype(jnp.bfloat16)
+    rows = attended_ref.shape[0]
+    head_dim = sums_ref.shape[2]
+    height = parts[0].shape[0] // 2
+    start = pl.multiple_of(side * height, height)
+    for turn in range(2):
+        for offset in range(chips):
+            part = parts[turn * chips + offset]
+            head = (side ^ turn) * chips + (place_ref[0] ^ offset)
+            at = pl.multiple_of(head * head_dim, head_dim)
+            attended_ref[:, pl.ds(at, head_dim)] = part[pl.ds(start, rows), :]
+            sums_ref[head] = part[pl.ds(start + rows, height - rows), :].astype(jnp.float32)
+
+
+def by_head(hidden, w_query, w_key, w_value, cluster_rank, assign, d_attended):
+    rows = hidden.shape[0]
+    count = assign.shape[0]
+    chips = count // 2
+    half, width = w_query.shape
+    head_dim = width // count
+    tokens = count * rows
+    clusters = cluster_rank.shape[0]
+    owned = clusters // count
+    scale = head_dim ** (-0.5)
+    factor = scale * log2_e
+    smem = pl.BlockSpec(memory_space=pltpu.SMEM)
+    vmem = pl.BlockSpec(memory_space=pltpu.VMEM)
+    anywhere = pl.BlockSpec(memory_space=pl.ANY)
+    params = pltpu.CompilerParams(vmem_limit_bytes=32 * mebi)
+    project_params = pltpu.CompilerParams(vmem_limit_bytes=48 * mebi)
+    swap = [(0, 1), (1, 0)]
+    chip, side, column = (lax.axis_index(name) for name in ("seq", "sub", "head"))
+    place = jnp.stack([chip, side])
+
+    def call(kernel, outs, *operands, scratch=(), hbm=0, limits=params, takes=1):
+        return pl.pallas_call(
+            kernel,
+            out_shape=outs,
+            in_specs=[smem] + [vmem] * (len(operands) - 1 - hbm) + [anywhere] * hbm,
+            out_specs=jax.tree.map(lambda _: vmem, outs),
+            scratch_shapes=list(scratch),
+            compiler_params=limits,
+            cost_estimate=pl.CostEstimate(
+                flops=int(takes * 1.15e9), bytes_accessed=mebi, transcendentals=0
+            ),
+        )(*operands)
+
+    def low(*shape):
+        return jax.ShapeDtypeStruct(shape, jnp.bfloat16)
+
+    def buffers(height):
+        return (low(height, head_dim),) * chips
+
+    def exchange(parts):
+        moved = {
+            offset: lax.ppermute(parts[offset], "seq", [(at, at ^ offset) for at in range(chips)])
+            for offset in (2, 3, 1)
+        }
+        return (parts[0], moved[1], moved[2], moved[3])
+
+    def to_sibling(piece):
+        return lax.ppermute(piece, "sub", swap)
+
+    hidden_other = to_sibling(hidden)
+    block = low(chips, rows + id_lines(rows, head_dim), head_dim)
+    grads_mine, grads_theirs = call(pack_kernel, (block, block), place, d_attended, assign)
+    grads_other = to_sibling(grads_theirs)
+
+    def project(turn, weights, *arrived):
+        number = len(weights)
+        outs = buffers(2 * number * rows) if turn == 0 else low(number, 2 * rows, width // 2)
+
+        def kernel(place_ref, mine_ref, theirs_ref, *refs):
+            early, refs = refs[: 1 - turn], refs[1 - turn :]
+            project_kernel(
+                number, turn, place_ref, mine_ref, theirs_ref, *refs[:number], *early, *refs[number:]
+            )
+
+        return call(
+            kernel,
+            outs,
+            place,
+            hidden,
+            hidden_other,
+            *arrived,
+            *weights,
+            scratch=[
+                pltpu.VMEM((2 * rows, half), jnp.bfloat16),
+                pltpu.VMEM((number, half, width // 2), jnp.bfloat16),
+                pltpu.VMEM((2 * rows, width // 2), jnp.bfloat16),
+                pltpu.SemaphoreType.DMA((number, 4)),
+            ],
+            hbm=number,
+            limits=project_params,
+            takes=1 + 1.5 * number,
+        )
+
+    early, late = (w_query, w_key), (w_value,)
+    early_arrived = to_sibling(project(1, early))
+    late_arrived = to_sibling(project(1, late))
+    grads = exchange(call(merge_kernel, buffers(2 * block.shape[1]), place, grads_mine, grads_other))
+    early_arrived, _ = lax.optimization_barrier((early_arrived, grads[0]))
+    early_projected = project(0, early, early_arrived)
+    packed = exchange(early_projected)
+    late_arrived, _, _ = lax.optimization_barrier((late_arrived, early_projected[0], grads))
+    late_projected = project(0, late, late_arrived)
+    valued = exchange(late_projected)
+    packed = lax.optimization_barrier((*packed, late_projected[0]))[:chips]
+
+    def held(kind):
+        return pltpu.VMEM((tokens, head_dim), kind)
+
+    id_scratch = [pltpu.VMEM((count, 8, rows), jnp.float32), held(jnp.float32)]
+    *value_grads, lse = call(
+        partial(value_grad_kernel, factor, chips, rows),
+        (*buffers(2 * rows), jax.ShapeDtypeStruct((count, rows), jnp.float32)),
+        place,
+        *packed,
+        *grads,
+        scratch=[held(jnp.bfloat16)] * 3 + id_scratch + [held(jnp.float32)],
+        takes=7,
+    )
+    value_back = exchange(value_grads)
+    results = call(
+        partial(query_grad_kernel, factor, scale, chips, rows),
+        (*buffers(4 * rows), *buffers(2 * (rows + owned))),
+        place,
+        *packed,
+        *valued,
+        *grads,
+        lse,
+        cluster_rank.reshape(1, clusters),
+        scratch=[held(jnp.bfloat16)] * 4
+        + id_scratch
+        + [
+            held(jnp.float32),
+            held(jnp.bfloat16),
+            pltpu.VMEM((tokens + clusters, head_dim), jnp.bfloat16),
+        ],
+        takes=10,
+    )
+    *ready, _, _ = lax.optimization_barrier((*results[:chips], value_back[2], value_back[3]))
+    back = exchange(ready)
+
+    *own, _ = lax.optimization_barrier((w_query, w_key, w_value, results[0]))
+    staged = pl.pallas_call(
+        stage_kernel,
+        out_shape=pltpu.VMEM((3, half, width), jnp.bfloat16),
+        in_specs=[anywhere] * 3,
+        out_specs=vmem,
+        scratch_shapes=[pltpu.SemaphoreType.DMA((3,))],
+        compiler_params=pltpu.CompilerParams(vmem_limit_bytes=16 * mebi),
+        cost_estimate=pl.CostEstimate(
+            flops=0, bytes_accessed=18 * half * width, transcendentals=0
+        ),
+    )(*own)
+    back = (*lax.optimization_barrier((back[0], staged))[:1], *back[1:])
+
+    back_other = tuple(to_sibling(part) for part in back)
+    value_other = tuple(to_sibling(part) for part in value_back)
+
+    def input_part(shard):
+        return call(
+            partial(input_kernel, chips),
+            low(rows, half),
+            jnp.stack([chip, side, shard]),
+            *back,
+            *back_other,
+            *value_back,
+            *value_other,
+            staged,
+            scratch=[pltpu.VMEM((rows, 3 * width), jnp.bfloat16)],
+            takes=3,
+        )
+
+    square = ("head", "sub")
+    first = lax.ppermute(input_part(1 - column), square, [(0, 1), (1, 3), (3, 2), (2, 0)])
+    kept = input_part(column)
+    second = lax.ppermute(kept, square, [(1, 2), (2, 1)])
+    *outputs, _ = lax.optimization_barrier((*results[chips:], back[2]))
+    returned = exchange(outputs)
+    returned_other = tuple(to_sibling(part) for part in returned)
+    d_hidden, attended, centroid_sums = call(
+        partial(finish_kernel, chips),
+        (
+            low(rows, half),
+            low(rows, width),
+            jax.ShapeDtypeStruct((count, owned, head_dim), jnp.float32),
+        ),
+        jnp.stack([chip, side, column]),
+        first,
+        second,
+        kept,
+        *returned,
+        *returned_other,
+    )
+    return (attended, d_hidden, centroid_sums)
+
+
+def per_device(hidden, w_query, w_key, w_value, cluster_rank, assign, d_attended):
+    chips = lax.axis_size("seq")
+    fits = chips == 4 and lax.axis_size("sub") == 2 and lax.axis_size("head") == 2
+    plan = by_head if fits and assign.shape[0] == 2 * chips else by_owner
+    return plan(hidden, w_query, w_key, w_value, cluster_rank, assign, d_attended)
+
+
 def solution(mesh):
     placed = (
         P(("groups", "seq", "sub"), None),

time: 372 us -> 135 us (0.36)
  waiting for transfers between devices: 169 us -> 27.6 us
  matrix products: 100 us -> 0 us
  Pallas kernels: 0 us -> 33.8 us
  starting transfers between devices: 42.4 us -> 63.5 us
  local copies, waits for them, and re-layouts: 26.2 us -> 8.53 us
  other arithmetic: 16.2 us -> 0.23 us
  between operations: 14.2 us -> 0.85 us
    all_to_all x9 -> x0, waiting for transfers between devices: 166 us -> none  [the longest x2 46.5 us: exchange_three(): lax.all_to_all(first, ('seq', 'sub'), split_axis=1, concat_axis=1, tiled=...]
    dot_general x71 -> x0, matrix products: 100 us -> none  [the longest x8 15.3 us: head_backward(): jnp.dot(grad_low, keys_in, preferred_element_type=jnp.float32)]
    ppermute x0 -> x36, starting transfers between devices: none -> 63.5 us  [the longest x18 40.1 us: exchange(): lax.ppermute(parts[offset], 'seq', [(at, at ^ offset) for at in range(chi...]
    all_to_all x9 -> x0, starting transfers between devices: 42.3 us -> none  [the longest x2 9.34 us: exchange_three(): lax.all_to_all(third, ('seq', 'sub'), split_axis=1, concat_axis=1, tiled=...]
    pallas_call x0 -> x12, Pallas kernels: none -> 33.8 us  [the longest x11 33.4 us: call(): pl.pallas_call(kernel, out_shape=outs, in_specs=[smem] + [vmem] * (len(op...]
    ppermute x0 -> x36, waiting for transfers between devices: none -> 27.6 us  [the longest x18 21.3 us: exchange(): lax.ppermute(parts[offset], 'seq', [(at, at ^ offset) for at in range(chi...]
    reshape x9 -> x0, local copies, waits for them, and re-layouts: 12.9 us -> none  [the longest x4 4.43 us: to_slots(): return kept.reshape(heads_here, owners, capacity, head_dim)]
    reduce_sum x12 -> x0, other arithmetic: 7.2 us -> none  [the longest x8 4.34 us: head_forward(): row_total = jnp.sum(expd, axis=1)]
  transfers between devices with their start and end apart: 14 -> 36, of which waited for: 10 -> 10; matrix products, arithmetic and copies ran while one was open for 15% -> 0% of each run, Pallas kernels for 0% -> 19%
where the time goes in v6:
time: 135 us
  starting transfers between devices  63.5 us (47%)
  Pallas kernels  33.8 us (25%)
  waiting for transfers between devices  27.6 us (20%)
  local copies, waits for them, and re-layouts  8.53 us (6%)
    ppermute x18, starting transfers between devices, exchange(): lax.ppermute(parts[offset], 'seq', [(at, at ^ offset) for at in range(chi...  40.1 us
    pallas_call x11, Pallas kernels, call(): pl.pallas_call(kernel, out_shape=outs, in_specs=[smem] + [vmem] * (len(op...  33.4 us
    ppermute x18, waiting for transfers between devices, exchange(): lax.ppermute(parts[offset], 'seq', [(at, at ^ offset) for at in range(chi...  21.3 us
    ppermute x16, starting transfers between devices, to_sibling(): return lax.ppermute(piece, 'sub', swap)  19.5 us
    unnamed x20, local copies, waits for them, and re-layouts  8.53 us
    ppermute x16, waiting for transfers between devices, to_sibling(): return lax.ppermute(piece, 'sub', swap)  6.23 us
    ppermute x1, starting transfers between devices, by_head(): second = lax.ppermute(kept, square, [(1, 2), (2, 1)])  2.7 us
  transfers between devices with their start and end apart: 36, of which 10 were waited for; matrix products, arithmetic and copies ran while one was open for 0% of the time, Pallas kernels for 19%

profile of v6, /device:TPU:1, one launch (start us, length us, event | category | flops | bytes accessed | tf_op | source)
XLA Modules:
  0.0 134.5 jit_solution(17364638084501043139)
XLA Ops:
  0.6 0.1 collective-permute-start
  0.8 0.1 pad_add_fusion.3.place_ref
  0.8 2.7 %collective-permute-done.theirs_ref = bf16[256,2048]{1,0:T(8,128)(2,1)S(1)} collective-permute-done((bf16[256,2048]{1,0:T(8,128)(2,1)}, bf16[256,2048]{1,0:T(8,128)(2,1)S(1)}, u32[]{:S(2)}, u32[]{:S(2)}) %collective-permute-start) | collective-permute-done | bytes 1048608 | tf_op jit(solution)/shard_map/ppermute | solution.py:515
  3.6 1.6 %copy-done.2 = bf16[1024,1024]{1,0:T(8,128)(2,1)S(1)} copy-done((bf16[1024,1024]{1,0:T(8,128)(2,1)S(1)}, bf16[1024,1024]{1,0:T(8,128)(2,1)}, u32[]{:S(2)}) %copy-start.2) | copy-done | bytes 2097176
  5.2 1.2 copy-done.6
  6.4 2.6 %shard_map.94 = bf16[2,512,512]{2,1,0:T(8,128)(2,1)S(1)} custom-call(s32[2]{0:T(128)S(1)} %pad_add_fusion.3.place_ref, bf16[256,2048]{1,0:T(8,128)(2,1)S(1)} %copy-done.6, bf16[256,2048]{1,0:T(8,128)(2,1)S(1)} %collective-permute-done.theirs_ref, bf16[1024,1024]{1,0:T(8,128)(2,1)S(1)} %copy-done.2, bf16[1024,1024]{1,0:T(8,128)(2,1)} %refs_1_.6), custom_call_target="tpu_custom_call" | custom-call | flops 4600000000 | bytes 1048576 | tf_op jit(solution)/shard_map/pallas_call | solution.py:489
  9.0 0.0 copy-start.5
  9.0 0.2 collective-permute-start.1
  9.2 0.7 shard_map.95
  9.9 0.4 collective-permute-start.2
  10.3 0.2 copy-done.5
  10.6 1.4 %shard_map.98 = bf16[1,512,512]{2,1,0:T(8,128)(2,1)S(1)} custom-call(s32[2]{0:T(128)S(1)} %pad_add_fusion.3.place_ref, bf16[256,2048]{1,0:T(8,128)(2,1)S(1)} %copy-done.6, bf16[256,2048]{1,0:T(8,128)(2,1)S(1)} %collective-permute-done.theirs_ref, bf16[1024,1024]{1,0:T(8,128)(2,1)S(1)} %copy-done.5), custom_call_target="tpu_custom_call" | custom-call | flops 2875000064 | bytes 1048576 | tf_op jit(solution)/shard_map/pallas_call | solution.py:489
  12.0 0.2 collective-permute-start.6
  12.2 0.6 shard_map.96
  12.8 2.7 %collective-permute-start.7 = (bf16[544,128]{1,0:T(8,128)(2,1)S(1)}, bf16[544,128]{1,0:T(8,128)(2,1)S(1)}, u32[]{:S(2)}, u32[]{:S(2)}) collective-permute-start(bf16[544,128]{1,0:T(8,128)(2,1)S(1)} %get-tuple-element.59), channel_id=1, source_target_pairs={{0,4},{4,0},{8,12},{12,8},{1,5},{5,1},{9,13},{13,9},{2,6},{6,2},{1... | collective-permute-start | bytes 417800 | tf_op jit(solution)/shard_map/ppermute | solution.py:509
  15.6 2.3 %collective-permute-start.8 = (bf16[544,128]{1,0:T(8,128)(2,1)S(1)}, bf16[544,128]{1,0:T(8,128)(2,1)S(1)}, u32[]{:S(2)}, u32[]{:S(2)}) collective-permute-start(bf16[544,128]{1,0:T(8,128)(2,1)S(1)} %get-tuple-element.60), channel_id=1, source_target_pairs={{0,8},{4,12},{8,0},{12,4},{1,9},{5,13},{9,1},{13,5},{2,10},{6,14},... | collective-permute-start | bytes 417800 | tf_op jit(solution)/shard_map/ppermute | solution.py:509
  17.9 3.4 %shard_map.97 = (bf16[1024,128]{1,0:T(8,128)(2,1)S(1)}, bf16[1024,128]{1,0:T(8,128)(2,1)S(1)}, bf16[1024,128]{1,0:T(8,128)(2,1)S(1)}, bf16[1024,128]{1,0:T(8,128)(2,1)S(1)}) custom-call(s32[2]{0:T(128)S(1)} %pad_add_fusion.3.place_ref, bf16[256,2048]{1,0:T(8,128)(2,1)S(1)} %copy-done.6, bf16[256,2048]{1,0:T(8,128)(2,1)S(1)} %collective-permute-done.theirs_ref, ...), custom_call_target="tpu_custom_call" | custom-call | flops 4600000000 | bytes 1048576 | tf_op jit(solution)/shard_map/pallas_call | solution.py:489
  21.3 0.4 collective-permute-start.3
  21.7 0.0 collective-permute-done.7.refs_5_.refs_9_
  21.7 3.2 %collective-permute-start.4 = (bf16[1024,128]{1,0:T(8,128)(2,1)S(1)}, bf16[1024,128]{1,0:T(8,128)(2,1)S(1)}, u32[]{:S(2)}, u32[]{:S(2)}) collective-permute-start(bf16[1024,128]{1,0:T(8,128)(2,1)S(1)} %get-tuple-element.57), channel_id=1, source_target_pairs={{0,8},{4,12},{8,0},{12,4},{1,9},{5,13},{9,1},{13,5},{2,10},{6,14},... | collective-permute-start | bytes 786440 | tf_op jit(solution)/shard_map/ppermute | solution.py:509
  24.9 4.5 %collective-permute-start.5 = (bf16[1024,128]{1,0:T(8,128)(2,1)S(1)}, bf16[1024,128]{1,0:T(8,128)(2,1)S(1)}, u32[]{:S(2)}, u32[]{:S(2)}) collective-permute-start(bf16[1024,128]{1,0:T(8,128)(2,1)S(1)} %get-tuple-element.58), channel_id=1, source_target_pairs={{0,12},{4,8},{8,4},{12,0},{1,13},{5,9},{9,5},{13,1},{2,14},{6,10},... | collective-permute-start | bytes 786440 | tf_op jit(solution)/shard_map/ppermute | solution.py:509
  29.4 1.7 %shard_map.99 = (bf16[512,128]{1,0:T(8,128)(2,1)S(1)}, bf16[512,128]{1,0:T(8,128)(2,1)S(1)}, bf16[512,128]{1,0:T(8,128)(2,1)S(1)}, bf16[512,128]{1,0:T(8,128)(2,1)S(1)}) custom-call(s32[2]{0:T(128)S(1)} %pad_add_fusion.3.place_ref, bf16[256,2048]{1,0:T(8,128)(2,1)S(1)} %copy-done.6, bf16[256,2048]{1,0:T(8,128)(2,1)S(1)} %collective-permute-done.theirs_ref, ...), custom_call_target="tpu_custom_call" | custom-call | flops 2875000064 | bytes 1048576 | tf_op jit(solution)/shard_map/pallas_call | solution.py:489
  31.2 1.2 collective-permute-start.10
  32.4 1.1 collective-permute-start.11
  33.5 1.2 collective-permute-done.3.refs_1_
  34.7 2.6 %collective-permute-start.12 = (bf16[512,128]{1,0:T(8,128)(2,1)S(1)}, bf16[512,128]{1,0:T(8,128)(2,1)S(1)}, u32[]{:S(2)}, u32[]{:S(2)}) collective-permute-start(bf16[512,128]{1,0:T(8,128)(2,1)S(1)} %get-tuple-element.70), channel_id=1, source_target_pairs={{0,12},{4,8},{8,4},{12,0},{1,13},{5,9},{9,5},{13,1},{2,14},{6,10},... | collective-permute-start | bytes 393224 | tf_op jit(solution)/shard_map/ppermute | solution.py:509
  37.3 10.0 %collective-permute-done.4.refs_2_ = bf16[1024,128]{1,0:T(8,128)(2,1)S(1)} collective-permute-done((bf16[1024,128]{1,0:T(8,128)(2,1)S(1)}, bf16[1024,128]{1,0:T(8,128)(2,1)S(1)}, u32[]{:S(2)}, u32[]{:S(2)}) %collective-permute-start.4) | collective-permute-done | bytes 262176 | tf_op jit(solution)/shard_map/ppermute | solution.py:509
  47.3 5.5 %shard_map.100 = (bf16[512,128]{1,0:T(8,128)(2,1)S(1)}, bf16[512,128]{1,0:T(8,128)(2,1)S(1)}, bf16[512,128]{1,0:T(8,128)(2,1)S(1)}, bf16[512,128]{1,0:T(8,128)(2,1)S(1)}, f32[8,256]{1,0:T(8,128)S(1)}) custom-call(s32[2]{0:T(128)S(1)} %pad_add_fusion.3.place_ref, bf16[1024,128]{1,0:T(8,128)(2,1)S(1)} %get-tuple-element.64.refs_0_, ...), custom_call_target="tpu_custom_call" | custom-call | flops 8049999872 | bytes 1048576 | tf_op jit(solution)/shard_map/pallas_call | solution.py:489
  52.8 12.5 %collective-permute-start.13 = (bf16[512,128]{1,0:T(8,128)(2,1)S(1)}, bf16[512,128]{1,0:T(8,128)(2,1)S(1)}, u32[]{:S(2)}, u32[]{:S(2)}) collective-permute-start(bf16[512,128]{1,0:T(8,128)(2,1)S(1)} %get-tuple-element.76), channel_id=1, source_target_pairs={{0,8},{4,12},{8,0},{12,4},{1,9},{5,13},{9,1},{13,5},{2,10},{6,14},... | collective-permute-start | bytes 393224 | tf_op jit(solution)/shard_map/ppermute | solution.py:509
  65.2 1.1 collective-permute-start.14
  66.4 0.0 copy-start.3
  66.4 0.0 copy-start.4
  66.4 9.0 %shard_map.101 = (bf16[1024,128]{1,0:T(8,128)(2,1)S(1)}, bf16[1024,128]{1,0:T(8,128)(2,1)S(1)}, bf16[1024,128]{1,0:T(8,128)(2,1)S(1)}, bf16[1024,128]{1,0:T(8,12...) custom-call(s32[2]{0:T(128)S(1)} %pad_add_fusion.3.place_ref, ...), custom_call_target="tpu_custom_call" | custom-call | flops 11500000256 | bytes 1048576 | tf_op jit(solution)/shard_map/pallas_call | solution.py:489
  75.4 1.5 %collective-permute-start.15 = (bf16[1024,128]{1,0:T(8,128)(2,1)S(1)}, bf16[1024,128]{1,0:T(8,128)(2,1)S(1)}, u32[]{:S(2)}, u32[]{:S(2)}) collective-permute-start(bf16[1024,128]{1,0:T(8,128)(2,1)S(1)} %get-tuple-element.83), channel_id=1, source_target_pairs={{0,4},{4,0},{8,12},{12,8},{1,5},{5,1},{9,13},{13,9},{2,6},{6,2},{1... | collective-permute-start | bytes 786440 | tf_op jit(solution)/shard_map/ppermute | solution.py:509
  77.0 1.1 collective-permute-start.16
  78.0 1.1 collective-permute-start.17
  79.1 3.5 %collective-permute-start.23 = (bf16[512,128]{1,0:T(8,128)(2,1)S(1)}, bf16[512,128]{1,0:T(8,128)(2,1)S(1)}, u32[]{:S(2)}, u32[]{:S(2)}) collective-permute-start(bf16[512,128]{1,0:T(8,128)(2,1)S(1)} %get-tuple-element.86.refs_8_), channel_id=1, source_target_pairs={{0,1},{1,0},{2,3},{3,2},{4,5},{5,4},{6,7},{7,6},{8,9},{9,8},{10,11... | collective-permute-start | bytes 393224 | tf_op jit(solution)/shard_map/ppermute | solution.py:515
  82.7 1.0 collective-permute-done.23.refs_12_
  83.7 0.4 collective-permute-start.25
  84.0 0.5 shard_map.102.refs_16_
  84.5 2.7 %copy-done = bf16[3,1024,1024]{2,1,0:T(8,128)(2,1)} copy-done((bf16[3,1024,1024]{2,1,0:T(8,128)(2,1)}, bf16[3,1024,1024]{2,1,0:T(8,128)(2,1)S(1)}, u32[]{:S(2)}) %copy-start) | copy-done | bytes 6291480
  87.2 0.1 collective-permute-start.18
  87.3 0.5 collective-permute-start.19
  87.8 12.9 %collective-permute-start.20 = (bf16[1024,128]{1,0:T(8,128)(2,1)S(1)}, bf16[1024,128]{1,0:T(8,128)(2,1)S(1)}, u32[]{:S(2)}, u32[]{:S(2)}) collective-permute-start(bf16[1024,128]{1,0:T(8,128)(2,1)S(1)} %collective-permute-done.16.refs_2_), channel_id=1, source_target_pairs={{0,1},{1,0},{2,3},{3,2},{4,5},{5,4},{6,7},{7,6},{8,9},{9,8},{10,11... | collective-permute-start | bytes 786440 | tf_op jit(solution)/shard_map/ppermute | solution.py:515
  100.7 0.5 collective-permute-start.26
  101.2 0.1 pad_add_fusion.place_ref
  101.3 0.1 pad_add_fusion.2.place_ref
  101.3 1.2 collective-permute-done.26.refs_15_
  102.6 2.8 %copy-done.1 = bf16[3,1024,1024]{2,1,0:T(8,128)(2,1)S(1)} copy-done((bf16[3,1024,1024]{2,1,0:T(8,128)(2,1)S(1)}, bf16[3,1024,1024]{2,1,0:T(8,128)(2,1)}, u32[]{:S(2)}) %copy-start.1) | copy-done | bytes 6291480
  105.3 3.3 %shard_map.103 = bf16[256,1024]{1,0:T(8,128)(2,1)S(1)} custom-call(s32[3]{0:T(128)S(1)} %pad_add_fusion.2.place_ref, bf16[1024,128]{1,0:T(8,128)(2,1)S(1)} %get-tuple-element.82.refs_0_, bf16[1024,128]{1,0:T(8,128)(2,1)S(1)} %collective-permute-done.15.refs_1_, bf16[1024,128]{1,0:T(8,128)(2,1)S(1)} %collective-permute-done.16.refs_2_, ...), custom_call_target="tpu_custom_call" | custom-call | flops 3449999872 | bytes 1048576 | tf_op jit(solution)/shard_map/pallas_call | solution.py:489
  108.7 1.2 collective-permute-start.27
  109.9 3.3 %shard_map.104.kept_ref = bf16[256,1024]{1,0:T(8,128)(2,1)S(1)} custom-call(s32[3]{0:T(128)S(1)} %pad_add_fusion.place_ref, bf16[1024,128]{1,0:T(8,128)(2,1)S(1)} %get-tuple-element.82.refs_0_, bf16[1024,128]{1,0:T(8,128)(2,1)S(1)} %collective-permute-done.15.refs_1_, bf16[1024,128]{1,0:T(8,128)(2,1)S(1)} %collective-permute-done.16.refs_2_, ...), custom_call_target="tpu_custom_call" | custom-call | flops 3449999872 | bytes 1048576 | tf_op jit(solution)/shard_map/pallas_call | solution.py:489
  113.2 2.7 %collective-permute-start.28 = (bf16[256,1024]{1,0:T(8,128)(2,1)S(1)}, bf16[256,1024]{1,0:T(8,128)(2,1)S(1)}, u32[]{:S(2)}, u32[]{:S(2)}) collective-permute-start(bf16[256,1024]{1,0:T(8,128)(2,1)S(1)} %shard_map.104.kept_ref), channel_id=1, source_target_pairs={{1,2},{2,1},{5,6},{6,5},{9,10},{10,9},{13,14},{14,13},{17,18},{18,... | collective-permute-start | bytes 1572872 | tf_op jit(solution)/shard_map/ppermute | solution.py:632
  116.0 2.7 %collective-permute-start.29 = (bf16[576,128]{1,0:T(8,128)(2,1)S(1)}, bf16[576,128]{1,0:T(8,128)(2,1)S(1)}, u32[]{:S(2)}, u32[]{:S(2)}) collective-permute-start(bf16[576,128]{1,0:T(8,128)(2,1)S(1)} %get-tuple-element.93), channel_id=1, source_target_pairs={{0,4},{4,0},{8,12},{12,8},{1,5},{5,1},{9,13},{13,9},{2,6},{6,2},{1... | collective-permute-start | bytes 442376 | tf_op jit(solution)/shard_map/ppermute | solution.py:509
  118.6 1.1 collective-permute-start.30
  119.7 1.1 collective-permute-start.31
  120.8 2.1 %collective-permute-done.29.refs_1_ = bf16[576,128]{1,0:T(8,128)(2,1)S(1)} collective-permute-done((bf16[576,128]{1,0:T(8,128)(2,1)S(1)}, bf16[576,128]{1,0:T(8,128)(2,1)S(1)}, u32[]{:S(2)}, u32[]{:S(2)}) %collective-permute-start.29) | collective-permute-done | bytes 147488 | tf_op jit(solution)/shard_map/ppermute | solution.py:509
  122.9 7.9 %collective-permute-done.30.refs_2_ = bf16[576,128]{1,0:T(8,128)(2,1)S(1)} collective-permute-done((bf16[576,128]{1,0:T(8,128)(2,1)S(1)}, bf16[576,128]{1,0:T(8,128)(2,1)S(1)}, u32[]{:S(2)}, u32[]{:S(2)}) %collective-permute-start.30) | collective-permute-done | bytes 147488 | tf_op jit(solution)/shard_map/ppermute | solution.py:509
  130.8 0.5 collective-permute-start.34
  131.3 0.1 collective-permute-start.35
  131.4 0.8 collective-permute-done.33.refs_5_
  132.2 0.2 collective-permute-done.34.refs_6_
  132.4 0.3 collective-permute-done.35.refs_7_
  132.7 1.8 %shard_map.105 = (bf16[256,1024]{1,0:T(8,128)(2,1)}, bf16[256,1024]{1,0:T(8,128)(2,1)}, f32[8,32,128]{2,1,0:T(8,128)}) custom-call(s32[3]{0:T(128)S(1)} %pad_add_fusion.place_ref, bf16[256,1024]{1,0:T(8,128)(2,1)S(1)} %collective-permute-done.27.first_ref, bf16[256,1024]{1,0:T(8,128)(2,1)S(1)} %collective-permute-done.28.second_ref, ...), custom_call_target="tpu_custom_call" | custom-call | flops 1150000000 | bytes 1048576 | tf_op jit(solution)/shard_map/pallas_call | solution.py:489
  (43 shorter events, 0.1 us)
Async XLA Ops:
  0.6 2.9 %collective-permute-start = (bf16[256,2048]{1,0:T(8,128)(2,1)}, bf16[256,2048]{1,0:T(8,128)(2,1)S(1)}, u32[]{:S(2)}, u32[]{:S(2)}) collective-permute-start(bf16[256,2048]{1,0:T(8,128)(2,1)} %mine_ref.7), channel_id=1, source_target_pairs={{0,1},{1,0},{2,3},{3,2},{4,5},{5,4},{6,7},{7,6},{8,9},{9,8},{10,11... | collective-permute-start | bytes 3145736 | tf_op jit(solution)/shard_map/ppermute | solution.py:515
  3.6 1.6 %copy-start.2 = (bf16[1024,1024]{1,0:T(8,128)(2,1)S(1)}, bf16[1024,1024]{1,0:T(8,128)(2,1)}, u32[]{:S(2)}) copy-start(bf16[1024,1024]{1,0:T(8,128)(2,1)} %refs_0_.4) | copy-start | bytes 6291460
  5.2 1.2 copy-start.6
  6.4 2.8 %copy-start.7 = (bf16[256,1024]{1,0:T(8,128)(2,1)S(1)}, bf16[256,1024]{1,0:T(8,128)(2,1)}, u32[]{:S(2)}) copy-start(bf16[256,1024]{1,0:T(8,128)(2,1)} %grads_ref.1) | copy-start | bytes 1572868
  6.4 2.8 %copy-start.8 = (s32[8,256]{1,0:T(8,128)S(1)}, s32[8,256]{1,0:T(8,128)}, u32[]{:S(2)}) copy-start(s32[8,256]{1,0:T(8,128)} %assign_ref.1) | copy-start | bytes 24580
  9.0 1.6 %copy-start.5 = (bf16[1024,1024]{1,0:T(8,128)(2,1)S(1)}, bf16[1024,1024]{1,0:T(8,128)(2,1)}, u32[]{:S(2)}) copy-start(bf16[1024,1024]{1,0:T(8,128)(2,1)} %refs_2_.2) | copy-start | bytes 6291460
  9.0 8.9 %collective-permute-start.1 = (bf16[2,512,512]{2,1,0:T(8,128)(2,1)S(1)}, bf16[2,512,512]{2,1,0:T(8,128)(2,1)S(1)}, u32[]{:S(2)}, u32[]{:S(2)}) collective-permute-start(bf16[2,512,512]{2,1,0:T(8,128)(2,1)S(1)} %shard_map.94), channel_id=1, source_target_pairs={{0,1},{1,0},{2,3},{3,2},{4,5},{5,4},{6,7},{7,6},{8,9},{9,8},{10,11... | collective-permute-start | bytes 3145736 | tf_op jit(solution)/shard_map/ppermute | solution.py:515
  9.9 2.3 %collective-permute-start.2 = (bf16[4,272,128]{2,1,0:T(8,128)(2,1)S(1)}, bf16[4,272,128]{2,1,0:T(8,128)(2,1)S(1)}, u32[]{:S(2)}, u32[]{:S(2)}) collective-permute-start(bf16[4,272,128]{2,1,0:T(8,128)(2,1)S(1)} %get-tuple-element.52), channel_id=1, source_target_pairs={{0,1},{1,0},{2,3},{3,2},{4,5},{5,4},{6,7},{7,6},{8,9},{9,8},{10,11... | collective-permute-start | bytes 835592 | tf_op jit(solution)/shard_map/ppermute | solution.py:515
  12.0 17.4 %collective-permute-start.6 = (bf16[1,512,512]{2,1,0:T(8,128)(2,1)S(1)}, bf16[1,512,512]{2,1,0:T(8,128)(2,1)S(1)}, u32[]{:S(2)}, u32[]{:S(2)}) collective-permute-start(bf16[1,512,512]{2,1,0:T(8,128)(2,1)S(1)} %shard_map.98), channel_id=1, source_target_pairs={{0,1},{1,0},{2,3},{3,2},{4,5},{5,4},{6,7},{7,6},{8,9},{9,8},{10,11... | collective-permute-start | bytes 1572872 | tf_op jit(solution)/shard_map/ppermute | solution.py:515
  12.8 8.9 %collective-permute-start.7 = (bf16[544,128]{1,0:T(8,128)(2,1)S(1)}, bf16[544,128]{1,0:T(8,128)(2,1)S(1)}, u32[]{:S(2)}, u32[]{:S(2)}) collective-permute-start(bf16[544,128]{1,0:T(8,128)(2,1)S(1)} %get-tuple-element.59), channel_id=1, source_target_pairs={{0,4},{4,0},{8,12},{12,8},{1,5},{5,1},{9,13},{13,9},{2,6},{6,2},{1... | collective-permute-start | bytes 417800 | tf_op jit(solution)/shard_map/ppermute | solution.py:509
  15.6 9.3 %collective-permute-start.8 = (bf16[544,128]{1,0:T(8,128)(2,1)S(1)}, bf16[544,128]{1,0:T(8,128)(2,1)S(1)}, u32[]{:S(2)}, u32[]{:S(2)}) collective-permute-start(bf16[544,128]{1,0:T(8,128)(2,1)S(1)} %get-tuple-element.60), channel_id=1, source_target_pairs={{0,8},{4,12},{8,0},{12,4},{1,9},{5,13},{9,1},{13,5},{2,10},{6,14},... | collective-permute-start | bytes 417800 | tf_op jit(solution)/shard_map/ppermute | solution.py:509
  17.9 11.6 %collective-permute-start.9 = (bf16[544,128]{1,0:T(8,128)(2,1)S(1)}, bf16[544,128]{1,0:T(8,128)(2,1)S(1)}, u32[]{:S(2)}, u32[]{:S(2)}) collective-permute-start(bf16[544,128]{1,0:T(8,128)(2,1)S(1)} %get-tuple-element.61), channel_id=1, source_target_pairs={{0,12},{4,8},{8,4},{12,0},{1,13},{5,9},{9,5},{13,1},{2,14},{6,10},... | collective-permute-start | bytes 417800 | tf_op jit(solution)/shard_map/ppermute | solution.py:509
  21.3 13.4 %collective-permute-start.3 = (bf16[1024,128]{1,0:T(8,128)(2,1)S(1)}, bf16[1024,128]{1,0:T(8,128)(2,1)S(1)}, u32[]{:S(2)}, u32[]{:S(2)}) collective-permute-start(bf16[1024,128]{1,0:T(8,128)(2,1)S(1)} %get-tuple-element.56), channel_id=1, source_target_pairs={{0,4},{4,0},{8,12},{12,8},{1,5},{5,1},{9,13},{13,9},{2,6},{6,2},{1... | collective-permute-start | bytes 786440 | tf_op jit(solution)/shard_map/ppermute | solution.py:509
  21.7 25.6 %collective-permute-start.4 = (bf16[1024,128]{1,0:T(8,128)(2,1)S(1)}, bf16[1024,128]{1,0:T(8,128)(2,1)S(1)}, u32[]{:S(2)}, u32[]{:S(2)}) collective-permute-start(bf16[1024,128]{1,0:T(8,128)(2,1)S(1)} %get-tuple-element.57), channel_id=1, source_target_pairs={{0,8},{4,12},{8,0},{12,4},{1,9},{5,13},{9,1},{13,5},{2,10},{6,14},... | collective-permute-start | bytes 786440 | tf_op jit(solution)/shard_map/ppermute | solution.py:509
  24.9 22.4 %collective-permute-start.5 = (bf16[1024,128]{1,0:T(8,128)(2,1)S(1)}, bf16[1024,128]{1,0:T(8,128)(2,1)S(1)}, u32[]{:S(2)}, u32[]{:S(2)}) collective-permute-start(bf16[1024,128]{1,0:T(8,128)(2,1)S(1)} %get-tuple-element.58), channel_id=1, source_target_pairs={{0,12},{4,8},{8,4},{12,0},{1,13},{5,9},{9,5},{13,1},{2,14},{6,10},... | collective-permute-start | bytes 786440 | tf_op jit(solution)/shard_map/ppermute | solution.py:509
  31.2 35.2 %collective-permute-start.10 = (bf16[512,128]{1,0:T(8,128)(2,1)S(1)}, bf16[512,128]{1,0:T(8,128)(2,1)S(1)}, u32[]{:S(2)}, u32[]{:S(2)}) collective-permute-start(bf16[512,128]{1,0:T(8,128)(2,1)S(1)} %get-tuple-element.68), channel_id=1, source_target_pairs={{0,4},{4,0},{8,12},{12,8},{1,5},{5,1},{9,13},{13,9},{2,6},{6,2},{1... | collective-permute-start | bytes 393224 | tf_op jit(solution)/shard_map/ppermute | solution.py:509
  32.4 34.0 %collective-permute-start.11 = (bf16[512,128]{1,0:T(8,128)(2,1)S(1)}, bf16[512,128]{1,0:T(8,128)(2,1)S(1)}, u32[]{:S(2)}, u32[]{:S(2)}) collective-permute-start(bf16[512,128]{1,0:T(8,128)(2,1)S(1)} %get-tuple-element.69), channel_id=1, source_target_pairs={{0,8},{4,12},{8,0},{12,4},{1,9},{5,13},{9,1},{13,5},{2,10},{6,14},... | collective-permute-start | bytes 393224 | tf_op jit(solution)/shard_map/ppermute | solution.py:509
  34.7 31.6 %collective-permute-start.12 = (bf16[512,128]{1,0:T(8,128)(2,1)S(1)}, bf16[512,128]{1,0:T(8,128)(2,1)S(1)}, u32[]{:S(2)}, u32[]{:S(2)}) collective-permute-start(bf16[512,128]{1,0:T(8,128)(2,1)S(1)} %get-tuple-element.70), channel_id=1, source_target_pairs={{0,12},{4,8},{8,4},{12,0},{1,13},{5,9},{9,5},{13,1},{2,14},{6,10},... | collective-permute-start | bytes 393224 | tf_op jit(solution)/shard_map/ppermute | solution.py:509
  47.3 19.1 %copy-start.9 = (s32[256]{0:T(256)S(1)}, s32[256]{0:T(256)}, u32[]{:S(2)}) copy-start(s32[256]{0:T(256)} %param.11) | copy-start | bytes 3076
  52.8 22.6 %collective-permute-start.13 = (bf16[512,128]{1,0:T(8,128)(2,1)S(1)}, bf16[512,128]{1,0:T(8,128)(2,1)S(1)}, u32[]{:S(2)}, u32[]{:S(2)}) collective-permute-start(bf16[512,128]{1,0:T(8,128)(2,1)S(1)} %get-tuple-element.76), channel_id=1, source_target_pairs={{0,8},{4,12},{8,0},{12,4},{1,9},{5,13},{9,1},{13,5},{2,10},{6,14},... | collective-permute-start | bytes 393224 | tf_op jit(solution)/shard_map/ppermute | solution.py:509
  65.2 10.2 %collective-permute-start.14 = (bf16[512,128]{1,0:T(8,128)(2,1)S(1)}, bf16[512,128]{1,0:T(8,128)(2,1)S(1)}, u32[]{:S(2)}, u32[]{:S(2)}) collective-permute-start(bf16[512,128]{1,0:T(8,128)(2,1)S(1)} %get-tuple-element.77), channel_id=1, source_target_pairs={{0,12},{4,8},{8,4},{12,0},{1,13},{5,9},{9,5},{13,1},{2,14},{6,10},... | collective-permute-start | bytes 393224 | tf_op jit(solution)/shard_map/ppermute | solution.py:509
  66.3 16.3 %collective-permute-start.22 = (bf16[512,128]{1,0:T(8,128)(2,1)S(1)}, bf16[512,128]{1,0:T(8,128)(2,1)S(1)}, u32[]{:S(2)}, u32[]{:S(2)}) collective-permute-start(bf16[512,128]{1,0:T(8,128)(2,1)S(1)} %get-tuple-element.87), channel_id=1, source_target_pairs={{0,4},{4,0},{8,12},{12,8},{1,5},{5,1},{9,13},{13,9},{2,6},{6,2},{1... | collective-permute-start | bytes 393224 | tf_op jit(solution)/shard_map/ppermute | solution.py:509
  66.4 17.6 %copy-start.3 = (bf16[1024,1024]{1,0:T(8,128)(2,1)S(1)}, bf16[1024,1024]{1,0:T(8,128)(2,1)}, u32[]{:S(2)}) copy-start(bf16[1024,1024]{1,0:T(8,128)(2,1)} %refs_0_.4) | copy-start | bytes 6291460
  66.4 17.6 %copy-start.4 = (bf16[1024,1024]{1,0:T(8,128)(2,1)S(1)}, bf16[1024,1024]{1,0:T(8,128)(2,1)}, u32[]{:S(2)}) copy-start(bf16[1024,1024]{1,0:T(8,128)(2,1)} %refs_1_.6) | copy-start | bytes 6291460
  75.4 11.9 %collective-permute-start.15 = (bf16[1024,128]{1,0:T(8,128)(2,1)S(1)}, bf16[1024,128]{1,0:T(8,128)(2,1)S(1)}, u32[]{:S(2)}, u32[]{:S(2)}) collective-permute-start(bf16[1024,128]{1,0:T(8,128)(2,1)S(1)} %get-tuple-element.83), channel_id=1, source_target_pairs={{0,4},{4,0},{8,12},{12,8},{1,5},{5,1},{9,13},{13,9},{2,6},{6,2},{1... | collective-permute-start | bytes 786440 | tf_op jit(solution)/shard_map/ppermute | solution.py:509
  77.0 10.8 %collective-permute-start.16 = (bf16[1024,128]{1,0:T(8,128)(2,1)S(1)}, bf16[1024,128]{1,0:T(8,128)(2,1)S(1)}, u32[]{:S(2)}, u32[]{:S(2)}) collective-permute-start(bf16[1024,128]{1,0:T(8,128)(2,1)S(1)} %get-tuple-element.84), channel_id=1, source_target_pairs={{0,8},{4,12},{8,0},{12,4},{1,9},{5,13},{9,1},{13,5},{2,10},{6,14},... | collective-permute-start | bytes 786440 | tf_op jit(solution)/shard_map/ppermute | solution.py:509
  78.0 22.7 %collective-permute-start.17 = (bf16[1024,128]{1,0:T(8,128)(2,1)S(1)}, bf16[1024,128]{1,0:T(8,128)(2,1)S(1)}, u32[]{:S(2)}, u32[]{:S(2)}) collective-permute-start(bf16[1024,128]{1,0:T(8,128)(2,1)S(1)} %get-tuple-element.85), channel_id=1, source_target_pairs={{0,12},{4,8},{8,4},{12,0},{1,13},{5,9},{9,5},{13,1},{2,14},{6,10},... | collective-permute-start | bytes 786440 | tf_op jit(solution)/shard_map/ppermute | solution.py:509
  79.1 4.5 %collective-permute-start.23 = (bf16[512,128]{1,0:T(8,128)(2,1)S(1)}, bf16[512,128]{1,0:T(8,128)(2,1)S(1)}, u32[]{:S(2)}, u32[]{:S(2)}) collective-permute-start(bf16[512,128]{1,0:T(8,128)(2,1)S(1)} %get-tuple-element.86.refs_8_), channel_id=1, source_target_pairs={{0,1},{1,0},{2,3},{3,2},{4,5},{5,4},{6,7},{7,6},{8,9},{9,8},{10,11... | collective-permute-start | bytes 393224 | tf_op jit(solution)/shard_map/ppermute | solution.py:515
  82.7 4.5 %collective-permute-start.24 = (bf16[512,128]{1,0:T(8,128)(2,1)S(1)}, bf16[512,128]{1,0:T(8,128)(2,1)S(1)}, u32[]{:S(2)}, u32[]{:S(2)}) collective-permute-start(bf16[512,128]{1,0:T(8,128)(2,1)S(1)} %collective-permute-done.22.refs_9_), channel_id=1, source_target_pairs={{0,1},{1,0},{2,3},{3,2},{4,5},{5,4},{6,7},{7,6},{8,9},{9,8},{10,11... | collective-permute-start | bytes 393224 | tf_op jit(solution)/shard_map/ppermute | solution.py:515
  83.7 17.0 %collective-permute-start.25 = (bf16[512,128]{1,0:T(8,128)(2,1)S(1)}, bf16[512,128]{1,0:T(8,128)(2,1)}, u32[]{:S(2)}, u32[]{:S(2)}) collective-permute-start(bf16[512,128]{1,0:T(8,128)(2,1)S(1)} %collective-permute-done.13.refs_10_), channel_id=1, source_target_pairs={{0,1},{1,0},{2,3},{3,2},{4,5},{5,4},{6,7},{7,6},{8,9},{9,8},{10,11... | collective-permute-start | bytes 393224 | tf_op jit(solution)/shard_map/ppermute | solution.py:515
  84.5 2.7 %copy-start = (bf16[3,1024,1024]{2,1,0:T(8,128)(2,1)}, bf16[3,1024,1024]{2,1,0:T(8,128)(2,1)S(1)}, u32[]{:S(2)}) copy-start(bf16[3,1024,1024]{2,1,0:T(8,128)(2,1)S(1)} %shard_map.102.refs_16_) | copy-start | bytes 18874372
  87.2 15.4 %collective-permute-start.18 = (bf16[1024,128]{1,0:T(8,128)(2,1)S(1)}, bf16[1024,128]{1,0:T(8,128)(2,1)S(1)}, u32[]{:S(2)}, u32[]{:S(2)}) collective-permute-start(bf16[1024,128]{1,0:T(8,128)(2,1)S(1)} %get-tuple-element.82.refs_0_), channel_id=1, source_target_pairs={{0,1},{1,0},{2,3},{3,2},{4,5},{5,4},{6,7},{7,6},{8,9},{9,8},{10,11... | collective-permute-start | bytes 786440 | tf_op jit(solution)/shard_map/ppermute | solution.py:515
  87.3 15.2 %collective-permute-start.19 = (bf16[1024,128]{1,0:T(8,128)(2,1)S(1)}, bf16[1024,128]{1,0:T(8,128)(2,1)S(1)}, u32[]{:S(2)}, u32[]{:S(2)}) collective-permute-start(bf16[1024,128]{1,0:T(8,128)(2,1)S(1)} %collective-permute-done.15.refs_1_), channel_id=1, source_target_pairs={{0,1},{1,0},{2,3},{3,2},{4,5},{5,4},{6,7},{7,6},{8,9},{9,8},{10,11... | collective-permute-start | bytes 786440 | tf_op jit(solution)/shard_map/ppermute | solution.py:515
  87.8 14.8 %collective-permute-start.20 = (bf16[1024,128]{1,0:T(8,128)(2,1)S(1)}, bf16[1024,128]{1,0:T(8,128)(2,1)S(1)}, u32[]{:S(2)}, u32[]{:S(2)}) collective-permute-start(bf16[1024,128]{1,0:T(8,128)(2,1)S(1)} %collective-permute-done.16.refs_2_), channel_id=1, source_target_pairs={{0,1},{1,0},{2,3},{3,2},{4,5},{5,4},{6,7},{7,6},{8,9},{9,8},{10,11... | collective-permute-start | bytes 786440 | tf_op jit(solution)/shard_map/ppermute | solution.py:515
  100.7 1.9 %collective-permute-start.21 = (bf16[1024,128]{1,0:T(8,128)(2,1)S(1)}, bf16[1024,128]{1,0:T(8,128)(2,1)S(1)}, u32[]{:S(2)}, u32[]{:S(2)}) collective-permute-start(bf16[1024,128]{1,0:T(8,128)(2,1)S(1)} %collective-permute-done.17.refs_3_), channel_id=1, source_target_pairs={{0,1},{1,0},{2,3},{3,2},{4,5},{5,4},{6,7},{7,6},{8,9},{9,8},{10,11... | collective-permute-start | bytes 786440 | tf_op jit(solution)/shard_map/ppermute | solution.py:515
  100.7 1.8 %collective-permute-start.26 = (bf16[512,128]{1,0:T(8,128)(2,1)S(1)}, bf16[512,128]{1,0:T(8,128)(2,1)}, u32[]{:S(2)}, u32[]{:S(2)}) collective-permute-start(bf16[512,128]{1,0:T(8,128)(2,1)S(1)} %collective-permute-done.14.refs_11_), channel_id=1, source_target_pairs={{0,1},{1,0},{2,3},{3,2},{4,5},{5,4},{6,7},{7,6},{8,9},{9,8},{10,11... | collective-permute-start | bytes 393224 | tf_op jit(solution)/shard_map/ppermute | solution.py:515
  102.6 2.8 %copy-start.1 = (bf16[3,1024,1024]{2,1,0:T(8,128)(2,1)S(1)}, bf16[3,1024,1024]{2,1,0:T(8,128)(2,1)}, u32[]{:S(2)}) copy-start(bf16[3,1024,1024]{2,1,0:T(8,128)(2,1)} %copy-done) | copy-start | bytes 18874372
  108.7 24.0 %collective-permute-start.27 = (bf16[256,1024]{1,0:T(8,128)(2,1)S(1)}, bf16[256,1024]{1,0:T(8,128)(2,1)S(1)}, u32[]{:S(2)}, u32[]{:S(2)}) collective-permute-start(bf16[256,1024]{1,0:T(8,128)(2,1)S(1)} %shard_map.103), channel_id=1, source_target_pairs={{0,1},{1,3},{3,2},{2,0},{4,5},{5,7},{7,6},{6,4},{8,9},{9,11},{11,1... | collective-permute-start | bytes 1572872 | tf_op jit(solution)/shard_map/ppermute | solution.py:630
  113.2 19.5 %collective-permute-start.28 = (bf16[256,1024]{1,0:T(8,128)(2,1)S(1)}, bf16[256,1024]{1,0:T(8,128)(2,1)S(1)}, u32[]{:S(2)}, u32[]{:S(2)}) collective-permute-start(bf16[256,1024]{1,0:T(8,128)(2,1)S(1)} %shard_map.104.kept_ref), channel_id=1, source_target_pairs={{1,2},{2,1},{5,6},{6,5},{9,10},{10,9},{13,14},{14,13},{17,18},{18,... | collective-permute-start | bytes 1572872 | tf_op jit(solution)/shard_map/ppermute | solution.py:632
  116.0 6.9 %collective-permute-start.29 = (bf16[576,128]{1,0:T(8,128)(2,1)S(1)}, bf16[576,128]{1,0:T(8,128)(2,1)S(1)}, u32[]{:S(2)}, u32[]{:S(2)}) collective-permute-start(bf16[576,128]{1,0:T(8,128)(2,1)S(1)} %get-tuple-element.93), channel_id=1, source_target_pairs={{0,4},{4,0},{8,12},{12,8},{1,5},{5,1},{9,13},{13,9},{2,6},{6,2},{1... | collective-permute-start | bytes 442376 | tf_op jit(solution)/shard_map/ppermute | solution.py:509
  118.6 12.2 %collective-permute-start.30 = (bf16[576,128]{1,0:T(8,128)(2,1)S(1)}, bf16[576,128]{1,0:T(8,128)(2,1)S(1)}, u32[]{:S(2)}, u32[]{:S(2)}) collective-permute-start(bf16[576,128]{1,0:T(8,128)(2,1)S(1)} %get-tuple-element.94), channel_id=1, source_target_pairs={{0,8},{4,12},{8,0},{12,4},{1,9},{5,13},{9,1},{13,5},{2,10},{6,14},... | collective-permute-start | bytes 442376 | tf_op jit(solution)/shard_map/ppermute | solution.py:509
  119.7 11.1 %collective-permute-start.31 = (bf16[576,128]{1,0:T(8,128)(2,1)S(1)}, bf16[576,128]{1,0:T(8,128)(2,1)S(1)}, u32[]{:S(2)}, u32[]{:S(2)}) collective-permute-start(bf16[576,128]{1,0:T(8,128)(2,1)S(1)} %get-tuple-element.95), channel_id=1, source_target_pairs={{0,12},{4,8},{8,4},{12,0},{1,13},{5,9},{9,5},{13,1},{2,14},{6,10},... | collective-permute-start | bytes 442376 | tf_op jit(solution)/shard_map/ppermute | solution.py:509
  122.9 8.4 %collective-permute-start.32 = (bf16[576,128]{1,0:T(8,128)(2,1)S(1)}, bf16[576,128]{1,0:T(8,128)(2,1)S(1)}, u32[]{:S(2)}, u32[]{:S(2)}) collective-permute-start(bf16[576,128]{1,0:T(8,128)(2,1)S(1)} %get-tuple-element.92.refs_0_), channel_id=1, source_target_pairs={{0,1},{1,0},{2,3},{3,2},{4,5},{5,4},{6,7},{7,6},{8,9},{9,8},{10,11... | collective-permute-start | bytes 442376 | tf_op jit(solution)/shard_map/ppermute | solution.py:515
  130.8 1.4 %collective-permute-start.33 = (bf16[576,128]{1,0:T(8,128)(2,1)S(1)}, bf16[576,128]{1,0:T(8,128)(2,1)S(1)}, u32[]{:S(2)}, u32[]{:S(2)}) collective-permute-start(bf16[576,128]{1,0:T(8,128)(2,1)S(1)} %collective-permute-done.29.refs_1_), channel_id=1, source_target_pairs={{0,1},{1,0},{2,3},{3,2},{4,5},{5,4},{6,7},{7,6},{8,9},{9,8},{10,11... | collective-permute-start | bytes 442376 | tf_op jit(solution)/shard_map/ppermute | solution.py:515
  130.8 1.6 %collective-permute-start.34 = (bf16[576,128]{1,0:T(8,128)(2,1)S(1)}, bf16[576,128]{1,0:T(8,128)(2,1)S(1)}, u32[]{:S(2)}, u32[]{:S(2)}) collective-permute-start(bf16[576,128]{1,0:T(8,128)(2,1)S(1)} %collective-permute-done.30.refs_2_), channel_id=1, source_target_pairs={{0,1},{1,0},{2,3},{3,2},{4,5},{5,4},{6,7},{7,6},{8,9},{9,8},{10,11... | collective-permute-start | bytes 442376 | tf_op jit(solution)/shard_map/ppermute | solution.py:515
  131.3 1.4 %collective-permute-start.35 = (bf16[576,128]{1,0:T(8,128)(2,1)S(1)}, bf16[576,128]{1,0:T(8,128)(2,1)S(1)}, u32[]{:S(2)}, u32[]{:S(2)}) collective-permute-start(bf16[576,128]{1,0:T(8,128)(2,1)S(1)} %collective-permute-done.31.refs_3_), channel_id=1, source_target_pairs={{0,1},{1,0},{2,3},{3,2},{4,5},{5,4},{6,7},{7,6},{8,9},{9,8},{10,11... | collective-permute-start | bytes 442376 | tf_op jit(solution)/shard_map/ppermute | solution.py:515

commit v7 on v6

--- a/solution.py
+++ b/solution.py
@@ -238,18 +238,25 @@
     return copies
 
 
-def project_kernel(count, turn, place_ref, mine_ref, theirs_ref, *refs):
-    weights, refs = refs[:count], refs[count:]
+def project_kernel(count, turn, place_ref, *refs):
     if turn == 0:
         arrived_ref, refs = refs[0], refs[1:]
-    out_refs, (joined_ref, held_ref, low_ref, sems) = refs[:-4], refs[-4:]
+    tokens, weights, refs = refs[:2], refs[2 : 2 + count], refs[2 + count :]
+    out_refs, (joined_ref, held_ref, low_ref, sems, token_sems) = refs[:-5], refs[-5:]
     side = place_ref[1]
-    rows, depth = mine_ref.shape[0], joined_ref.shape[1]
-    tall = 2 * rows
+    tall, depth = joined_ref.shape
+    rows = tall // 2
+    near = pl.ds(pl.multiple_of(side * depth, depth), depth)
+    joins = []
+    for core, source in enumerate(tokens):
+        at = pl.ds(pl.multiple_of((side ^ core) * rows, rows), rows)
+        joins.append(
+            pltpu.make_async_copy(source.at[:, near], joined_ref.at[at], token_sems.at[core])
+        )
+        joins[core].start()
     copies = fetch_columns(side ^ turn, weights, held_ref, sems)
-    near = pl.ds(pl.multiple_of(side * depth, depth), depth)
-    joined_ref[pl.ds(pl.multiple_of(side * rows, rows), rows), :] = mine_ref[:, near]
-    joined_ref[pl.ds(pl.multiple_of((1 - side) * rows, rows), rows), :] = theirs_ref[:, near]
+    for copy in joins:
+        copy.wait()
     chunks = sems.shape[1]
     for index in range(count):
         for chunk in range(chunks):
@@ -341,7 +348,7 @@
     packed, valued, grads = refs[:chips], refs[chips : 2 * chips], refs[2 * chips : 3 * chips]
     lse_ref, rank_ref = refs[3 * chips : 3 * chips + 2]
     refs = refs[3 * chips + 2 :]
-    grad_refs, out_refs, refs = refs[:chips], refs[chips : 2 * chips], refs[2 * chips :]
+    grad_refs, out_refs, refs = refs[:chips], refs[chips : chips + 2], refs[chips + 2 :]
     queries, keys_in, values, grad_rows, id_rows, id_cols, total_ref, dq_ref, attended_ref = refs
     head_dim = queries.shape[1]
     clusters = rank_ref.shape[1]
@@ -399,30 +406,18 @@
         at = pl.ds(pl.multiple_of((place ^ offset) * tall, tall), tall)
         grad_refs[offset][:tall, :] = dq_ref[at, :]
         grad_refs[offset][tall:, :] = (total_ref[at, :] * scale).astype(jnp.bfloat16)
-        for core in range(2):
-            shard = (place ^ offset) * 2 + core
-            start = core * (rows + owned)
+    for turn, out_ref in enumerate(out_refs):
+        for chip in range(chips):
+            shard = chip * 2 + (place_ref[1] ^ turn)
             at = pl.ds(pl.multiple_of(shard * rows, rows), rows)
-            out_refs[offset][start : start + rows, :] = attended_ref[at, :]
+            out_ref[chip, :rows, :] = attended_ref[at, :]
             at = pl.ds(pl.multiple_of(2 * chips * rows + shard * owned, owned), owned)
-            out_refs[offset][start + rows : start + rows + owned, :] = attended_ref[at, :]
-
-
-def stage_kernel(*refs):
-    weights, (held_ref, sems) = refs[:-2], refs[-2:]
-    copies = [
-        pltpu.make_async_copy(weight, held_ref.at[index], sems.at[index])
-        for index, weight in enumerate(weights)
-    ]
-    for copy in copies:
-        copy.start()
-    for copy in copies:
-        copy.wait()
+            out_ref[chip, rows:, :] = attended_ref[at, :]
 
 
 def input_kernel(chips, place_ref, *refs):
-    held_ref, out_ref, gathered_ref = refs[4 * chips :]
-    rows, width = out_ref.shape[0], held_ref.shape[2]
+    weights, (out_ref, gathered_ref) = refs[4 * chips : -2], refs[-2:]
+    rows, width = out_ref.shape[0], weights[0].shape[1]
     head_dim = width // (2 * chips)
     for turn in range(2):
         parts = refs[turn * chips : (turn + 1) * chips]
@@ -437,7 +432,7 @@
     flipped = None
     for index in range(3):
         term = lax.dot_general(
-            held_ref[index],
+            weights[index][...],
             gathered_ref[:, index * width : (index + 1) * width],
             contract_last,
             preferred_element_type=jnp.float32,
@@ -446,23 +441,24 @@
     out_ref[...] = flipped.T.astype(out_ref.dtype)
 
 
-def finish_kernel(chips, place_ref, first_ref, second_ref, kept_ref, *refs):
-    parts, (hidden_ref, attended_ref, sums_ref) = refs[: 2 * chips], refs[2 * chips :]
-    side = place_ref[1]
-    second = jnp.where(place_ref[2] == side, kept_ref[...], second_ref[...])
-    total = first_ref[...].astype(jnp.float32) + second.astype(jnp.float32)
-    hidden_ref[...] = total.astype(jnp.bfloat16)
+def attended_kernel(chips, place_ref, *refs):
+    parts, (attended_ref, sums_ref) = refs[:chips], refs[chips:]
     rows = attended_ref.shape[0]
     head_dim = sums_ref.shape[2]
     height = parts[0].shape[0] // 2
-    start = pl.multiple_of(side * height, height)
-    for turn in range(2):
-        for offset in range(chips):
-            part = parts[turn * chips + offset]
-            head = (side ^ turn) * chips + (place_ref[0] ^ offset)
+    for core in range(2):
+        start = core * height
+        for offset, part in enumerate(parts):
+            head = core * chips + (place_ref[0] ^ offset)
             at = pl.multiple_of(head * head_dim, head_dim)
-            attended_ref[:, pl.ds(at, head_dim)] = part[pl.ds(start, rows), :]
-            sums_ref[head] = part[pl.ds(start + rows, height - rows), :].astype(jnp.float32)
+            attended_ref[:, pl.ds(at, head_dim)] = part[start : start + rows, :]
+            sums_ref[head] = part[start + rows : start + height, :].astype(jnp.float32)
+
+
+def sum_kernel(place_ref, first_ref, second_ref, kept_ref, hidden_ref):
+    keeps = place_ref[2] == place_ref[1]
+    second = jnp.where(keeps, kept_ref[...], second_ref[...]).astype(jnp.float32)
+    hidden_ref[...] = (first_ref[...].astype(jnp.float32) + second).astype(jnp.bfloat16)
 
 
 def by_head(hidden, w_query, w_key, w_value, cluster_rank, assign, d_attended):
@@ -480,7 +476,7 @@
     vmem = pl.BlockSpec(memory_space=pltpu.VMEM)
     anywhere = pl.BlockSpec(memory_space=pl.ANY)
     params = pltpu.CompilerParams(vmem_limit_bytes=32 * mebi)
-    project_params = pltpu.CompilerParams(vmem_limit_bytes=48 * mebi)
+    project_params = pltpu.CompilerParams(vmem_limit_bytes=32 * mebi)
     swap = [(0, 1), (1, 0)]
     chip, side, column = (lax.axis_index(name) for name in ("seq", "sub", "head"))
     place = jnp.stack([chip, side])
@@ -519,35 +515,36 @@
     grads_mine, grads_theirs = call(pack_kernel, (block, block), place, d_attended, assign)
     grads_other = to_sibling(grads_theirs)
 
+    def stay(array):
+        return pltpu.with_memory_space_constraint(array, pltpu.HBM)
+
     def project(turn, weights, *arrived):
         number = len(weights)
         outs = buffers(2 * number * rows) if turn == 0 else low(number, 2 * rows, width // 2)
 
-        def kernel(place_ref, mine_ref, theirs_ref, *refs):
-            early, refs = refs[: 1 - turn], refs[1 - turn :]
-            project_kernel(
-                number, turn, place_ref, mine_ref, theirs_ref, *refs[:number], *early, *refs[number:]
-            )
-
         return call(
-            kernel,
+            partial(project_kernel, number, turn),
             outs,
             place,
-            hidden,
+            *arrived,
+            stay(hidden),
             hidden_other,
-            *arrived,
-            *weights,
+            *(stay(weight) for weight in weights),
             scratch=[
                 pltpu.VMEM((2 * rows, half), jnp.bfloat16),
                 pltpu.VMEM((number, half, width // 2), jnp.bfloat16),
                 pltpu.VMEM((2 * rows, width // 2), jnp.bfloat16),
                 pltpu.SemaphoreType.DMA((number, 4)),
+                pltpu.SemaphoreType.DMA((2,)),
             ],
-            hbm=number,
+            hbm=2 + number,
             limits=project_params,
-            takes=1 + 1.5 * number,
-        )
-
+            takes=(8 if number == 2 else 0.1) if turn == 0 else 0.1,
+        )
+
+    merged = call(merge_kernel, buffers(2 * block.shape[1]), place, grads_mine, grads_other)
+    grads = exchange(merged)
+    hidden_other, _ = lax.optimization_barrier((hidden_other, merged[0]))
     early, late = (w_query, w_key), (w_value,)
     early_arrived = to_sibling(project(1, early))
     late_arrived = to_sibling(project(1, late))
@@ -555,7 +552,7 @@
     early_arrived, _ = lax.optimization_barrier((early_arrived, grads[0]))
     early_projected = project(0, early, early_arrived)
     packed = exchange(early_projected)
-    late_arrived, _, _ = lax.optimization_barrier((late_arrived, early_projected[0], grads))
+    late_arrived, _, _ = lax.optimization_barrier((late_arrived, early_projected[0], (grads[2], grads[3])))
     late_projected = project(0, late, late_arrived)
     valued = exchange(late_projected)
     packed = lax.optimization_barrier((*packed, late_projected[0]))[:chips]
@@ -576,7 +573,7 @@
     value_back = exchange(value_grads)
     results = call(
         partial(query_grad_kernel, factor, scale, chips, rows),
-        (*buffers(4 * rows), *buffers(2 * (rows + owned))),
+        (*buffers(4 * rows), *(low(chips, rows + owned, head_dim),) * 2),
         place,
         *packed,
         *valued,
@@ -595,20 +592,10 @@
     *ready, _, _ = lax.optimization_barrier((*results[:chips], value_back[2], value_back[3]))
     back = exchange(ready)
 
-    *own, _ = lax.optimization_barrier((w_query, w_key, w_value, results[0]))
-    staged = pl.pallas_call(
-        stage_kernel,
-        out_shape=pltpu.VMEM((3, half, width), jnp.bfloat16),
-        in_specs=[anywhere] * 3,
-        out_specs=vmem,
-        scratch_shapes=[pltpu.SemaphoreType.DMA((3,))],
-        compiler_params=pltpu.CompilerParams(vmem_limit_bytes=16 * mebi),
-        cost_estimate=pl.CostEstimate(
-            flops=0, bytes_accessed=18 * half * width, transcendentals=0
-        ),
-    )(*own)
-    back = (*lax.optimization_barrier((back[0], staged))[:1], *back[1:])
-
+    attended_mine, attended_theirs = results[chips:]
+    outputs = call(
+        merge_kernel, buffers(2 * (rows + owned)), place, attended_mine, to_sibling(attended_theirs)
+    )
     back_other = tuple(to_sibling(part) for part in back)
     value_other = tuple(to_sibling(part) for part in value_back)
 
@@ -621,32 +608,30 @@
             *back_other,
             *value_back,
             *value_other,
-            staged,
+            w_query,
+            w_key,
+            w_value,
             scratch=[pltpu.VMEM((rows, 3 * width), jnp.bfloat16)],
             takes=3,
         )
 
     square = ("head", "sub")
-    first = lax.ppermute(input_part(1 - column), square, [(0, 1), (1, 3), (3, 2), (2, 0)])
-    kept = input_part(column)
+    crossing = input_part(1 - column)
+    first = lax.ppermute(crossing, square, [(0, 1), (1, 3), (3, 2), (2, 0)])
+    kept = input_part(lax.optimization_barrier((column, crossing))[0])
     second = lax.ppermute(kept, square, [(1, 2), (2, 1)])
-    *outputs, _ = lax.optimization_barrier((*results[chips:], back[2]))
+    *outputs, _, _ = lax.optimization_barrier((*outputs, back[2], back[3]))
     returned = exchange(outputs)
-    returned_other = tuple(to_sibling(part) for part in returned)
-    d_hidden, attended, centroid_sums = call(
-        partial(finish_kernel, chips),
-        (
-            low(rows, half),
-            low(rows, width),
-            jax.ShapeDtypeStruct((count, owned, head_dim), jnp.float32),
-        ),
-        jnp.stack([chip, side, column]),
-        first,
-        second,
-        kept,
+    corner = jnp.stack([chip, side, column])
+    *returned, _ = lax.optimization_barrier((*returned, first))
+    attended, centroid_sums = call(
+        partial(attended_kernel, chips),
+        (low(rows, width), jax.ShapeDtypeStruct((count, owned, head_dim), jnp.float32)),
+        corner,
         *returned,
-        *returned_other,
-    )
+    )
+    first, _ = lax.optimization_barrier((first, attended))
+    d_hidden = call(sum_kernel, low(rows, half), corner, first, second, kept)
     return (attended, d_hidden, centroid_sums)
 
 

time: 135 us -> 139 us (1.030)
  starting transfers between devices: 63.5 us -> 48.1 us
  waiting for transfers between devices: 27.6 us -> 35.6 us
  local copies, waits for them, and re-layouts: 8.53 us -> 14.3 us
  Pallas kernels: 33.8 us -> 39.2 us
    ppermute x16 -> x13, starting transfers between devices: 19.5 us -> 7.93 us  [to_sibling(): return lax.ppermute(piece, 'sub', swap)]
    ppermute x18, waiting for transfers between devices: 21.3 us -> 32.6 us  [exchange(): lax.ppermute(parts[offset], 'seq', [(at, at ^ offset) for at in range(chi...]
    pallas_call x11 -> x13, Pallas kernels: 33.4 us -> 39.2 us  [call(): pl.pallas_call(kernel, out_shape=outs, in_specs=[smem] + [vmem] * (len(op...]
    unnamed x20 -> x48, local copies, waits for them, and re-layouts: 8.53 us -> 14.3 us
    ppermute x18, starting transfers between devices: 40.1 us -> 36.3 us  [exchange(): lax.ppermute(parts[offset], 'seq', [(at, at ^ offset) for at in range(chi...]
    ppermute x16 -> x13, waiting for transfers between devices: 6.23 us -> 3.01 us  [to_sibling(): return lax.ppermute(piece, 'sub', swap)]
  transfers between devices with their start and end apart: 36 -> 33, of which waited for: 10 -> 8; matrix products, arithmetic and copies ran while one was open for 0% -> 0% of each run, Pallas kernels for 19% -> 25%
where the time goes in v7:
time: 139 us; the launch traced here: 138 us
  starting transfers between devices  48.1 us (35%)
  Pallas kernels  39.2 us (28%)
  waiting for transfers between devices  35.6 us (26%)
  local copies, waits for them, and re-layouts  14.3 us (10%)
    pallas_call x13, Pallas kernels, call(): pl.pallas_call(kernel, out_shape=outs, in_specs=[smem] + [vmem] * (len(op...  39.2 us
    ppermute x18, starting transfers between devices, exchange(): lax.ppermute(parts[offset], 'seq', [(at, at ^ offset) for at in range(chi...  36.3 us
    ppermute x18, waiting for transfers between devices, exchange(): lax.ppermute(parts[offset], 'seq', [(at, at ^ offset) for at in range(chi...  32.6 us
    unnamed x48, local copies, waits for them, and re-layouts  14.3 us
    ppermute x13, starting transfers between devices, to_sibling(): return lax.ppermute(piece, 'sub', swap)  7.93 us
    ppermute x13, waiting for transfers between devices, to_sibling(): return lax.ppermute(piece, 'sub', swap)  3.01 us
  transfers between devices with their start and end apart: 33, of which 8 were waited for; matrix products, arithmetic and copies ran while one was open for 0% of the time, Pallas kernels for 25%

profile of v7, /device:TPU:1, one launch (start us, length us, event | category | flops | bytes accessed | tf_op | source)
XLA Modules:
  0.0 138.5 jit_solution(7584103683235258904)
XLA Ops:
  0.6 0.1 collective-permute-start
  0.8 1.0 copy-done.3
  1.9 0.7 copy-done.20
  2.6 0.7 shard_map.94
  3.3 0.5 collective-permute-start.1
  3.8 1.2 collective-permute-done.1.theirs_ref
  5.0 0.6 shard_map.95
  5.6 3.4 %shard_map.96 = bf16[2,512,512]{2,1,0:T(8,128)(2,1)S(1)} custom-call(s32[2]{0:T(128)S(1)} %pad_add_fusion.2.place_ref, bf16[256,2048]{1,0:T(8,128)(2,1)} %refs_1_.3, bf16[256,2048]{1,0:T(8,128)(2,1)S(1)} %collective-permute-done.refs_1_.refs_2_, bf16[1024,1024]{1,0:T(8,128)(2,1)} %refs_16_.3, bf16[1024,1024]{1,0:T(8,128)(2,1)} %refs_17_.3), custom_call_target="tpu_custom_call" | custom-call | flops 115000000 | bytes 1048576 | tf_op jit(solution)/shard_map/pallas_call | solution.py:485
  9.0 0.4 collective-permute-start.2
  9.4 3.4 %collective-permute-start.7 = (bf16[544,128]{1,0:T(8,128)(2,1)S(1)}, bf16[544,128]{1,0:T(8,128)(2,1)S(1)}, u32[]{:S(2)}, u32[]{:S(2)}) collective-permute-start(bf16[544,128]{1,0:T(8,128)(2,1)S(1)} %get-tuple-element.64), channel_id=1, source_target_pairs={{0,8},{4,12},{8,0},{12,4},{1,9},{5,13},{9,1},{13,5},{2,10},{6,14},... | collective-permute-start | bytes 417800 | tf_op jit(solution)/shard_map/ppermute | solution.py:505
  12.9 1.1 collective-permute-start.8
  13.9 2.7 %shard_map.98 = bf16[1,512,512]{2,1,0:T(8,128)(2,1)S(1)} custom-call(s32[2]{0:T(128)S(1)} %pad_add_fusion.2.place_ref, bf16[256,2048]{1,0:T(8,128)(2,1)} %refs_1_.3, bf16[256,2048]{1,0:T(8,128)(2,1)S(1)} %collective-permute-done.refs_1_.refs_2_, bf16[1024,1024]{1,0:T(8,128)(2,1)} %refs_18_.3), custom_call_target="tpu_custom_call" | custom-call | flops 115000000 | bytes 1048576 | tf_op jit(solution)/shard_map/pallas_call | solution.py:485
  16.6 1.0 collective-permute-start.6
  17.6 3.6 %shard_map.97 = (bf16[1024,128]{1,0:T(8,128)(2,1)S(1)}, bf16[1024,128]{1,0:T(8,128)(2,1)S(1)}, bf16[1024,128]{1,0:T(8,128)(2,1)S(1)}, bf16[1024,128]{1,0:T(8,128)(2,1)S(1)}) custom-call(s32[2]{0:T(128)S(1)} %pad_add_fusion.2.place_ref, bf16[2,512,512]{2,1,0:T(8,128)(2,1)S(1)} %collective-permute-done.2.refs_0_, bf16[256,2048]{1,0:T(8,128)(2,1)} %refs_1_.3, ...), custom_call_target="tpu_custom_call" | custom-call | flops 9200000000 | bytes 1048576 | tf_op jit(solution)/shard_map/pallas_call | solution.py:485
  21.3 2.5 %collective-permute-start.4 = (bf16[1024,128]{1,0:T(8,128)(2,1)S(1)}, bf16[1024,128]{1,0:T(8,128)(2,1)S(1)}, u32[]{:S(2)}, u32[]{:S(2)}) collective-permute-start(bf16[1024,128]{1,0:T(8,128)(2,1)S(1)} %get-tuple-element.62), channel_id=1, source_target_pairs={{0,8},{4,12},{8,0},{12,4},{1,9},{5,13},{9,1},{13,5},{2,10},{6,14},... | collective-permute-start | bytes 786440 | tf_op jit(solution)/shard_map/ppermute | solution.py:505
  23.7 2.5 %collective-permute-start.5 = (bf16[1024,128]{1,0:T(8,128)(2,1)S(1)}, bf16[1024,128]{1,0:T(8,128)(2,1)S(1)}, u32[]{:S(2)}, u32[]{:S(2)}) collective-permute-start(bf16[1024,128]{1,0:T(8,128)(2,1)S(1)} %get-tuple-element.63), channel_id=1, source_target_pairs={{0,12},{4,8},{8,4},{12,0},{1,13},{5,9},{9,5},{13,1},{2,14},{6,10},... | collective-permute-start | bytes 786440 | tf_op jit(solution)/shard_map/ppermute | solution.py:505
  26.2 0.2 collective-permute-start.12
  26.4 2.8 %shard_map.99 = (bf16[512,128]{1,0:T(8,128)(2,1)S(1)}, bf16[512,128]{1,0:T(8,128)(2,1)S(1)}, bf16[512,128]{1,0:T(8,128)(2,1)S(1)}, bf16[512,128]{1,0:T(8,128)(2,1)S(1)}) custom-call(s32[2]{0:T(128)S(1)} %pad_add_fusion.2.place_ref, bf16[1,512,512]{2,1,0:T(8,128)(2,1)S(1)} %collective-permute-done.6.refs_0_, bf16[256,2048]{1,0:T(8,128)(2,1)} %refs_1_.3, ...), custom_call_target="tpu_custom_call" | custom-call | flops 115000000 | bytes 1048576 | tf_op jit(solution)/shard_map/pallas_call | solution.py:485
  29.3 1.4 collective-permute-start.9
  30.6 3.3 %collective-permute-done.3.refs_1_ = bf16[1024,128]{1,0:T(8,128)(2,1)S(1)} collective-permute-done((bf16[1024,128]{1,0:T(8,128)(2,1)S(1)}, bf16[1024,128]{1,0:T(8,128)(2,1)S(1)}, u32[]{:S(2)}, u32[]{:S(2)}) %collective-permute-start.3) | collective-permute-done | bytes 262176 | tf_op jit(solution)/shard_map/ppermute | solution.py:505
  33.9 8.6 %collective-permute-done.4.refs_2_ = bf16[1024,128]{1,0:T(8,128)(2,1)S(1)} collective-permute-done((bf16[1024,128]{1,0:T(8,128)(2,1)S(1)}, bf16[1024,128]{1,0:T(8,128)(2,1)S(1)}, u32[]{:S(2)}, u32[]{:S(2)}) %collective-permute-start.4) | collective-permute-done | bytes 262176 | tf_op jit(solution)/shard_map/ppermute | solution.py:505
  42.5 3.7 %collective-permute-start.11 = (bf16[512,128]{1,0:T(8,128)(2,1)S(1)}, bf16[512,128]{1,0:T(8,128)(2,1)S(1)}, u32[]{:S(2)}, u32[]{:S(2)}) collective-permute-start(bf16[512,128]{1,0:T(8,128)(2,1)S(1)} %get-tuple-element.74), channel_id=1, source_target_pairs={{0,12},{4,8},{8,4},{12,0},{1,13},{5,9},{9,5},{13,1},{2,14},{6,10},... | collective-permute-start | bytes 393224 | tf_op jit(solution)/shard_map/ppermute | solution.py:505
  46.2 5.5 %shard_map.100 = (bf16[512,128]{1,0:T(8,128)(2,1)S(1)}, bf16[512,128]{1,0:T(8,128)(2,1)S(1)}, bf16[512,128]{1,0:T(8,128)(2,1)S(1)}, bf16[512,128]{1,0:T(8,128)(2,1)S(1)}, f32[8,256]{1,0:T(8,128)S(1)}) custom-call(s32[2]{0:T(128)S(1)} %pad_add_fusion.2.place_ref, bf16[1024,128]{1,0:T(8,128)(2,1)S(1)} %get-tuple-element.68.refs_0_, ...), custom_call_target="tpu_custom_call" | custom-call | flops 8049999872 | bytes 1048576 | tf_op jit(solution)/shard_map/pallas_call | solution.py:485
  51.7 10.4 %collective-permute-start.14 = (bf16[512,128]{1,0:T(8,128)(2,1)S(1)}, bf16[512,128]{1,0:T(8,128)(2,1)S(1)}, u32[]{:S(2)}, u32[]{:S(2)}) collective-permute-start(bf16[512,128]{1,0:T(8,128)(2,1)S(1)} %get-tuple-element.87), channel_id=1, source_target_pairs={{0,8},{4,12},{8,0},{12,4},{1,9},{5,13},{9,1},{13,5},{2,10},{6,14},... | collective-permute-start | bytes 393224 | tf_op jit(solution)/shard_map/ppermute | solution.py:505
  62.1 0.2 collective-permute-start.15
  62.2 0.2 collective-permute-start.26
  62.5 9.0 %shard_map.101 = (bf16[1024,128]{1,0:T(8,128)(2,1)S(1)}, bf16[1024,128]{1,0:T(8,128)(2,1)S(1)}, bf16[1024,128]{1,0:T(8,128)(2,1)S(1)}, bf16[1024,128]{1,0:T(8,12...) custom-call(s32[2]{0:T(128)S(1)} %pad_add_fusion.2.place_ref, ...), custom_call_target="tpu_custom_call" | custom-call | flops 11500000256 | bytes 1048576 | tf_op jit(solution)/shard_map/pallas_call | solution.py:485
  71.5 0.7 copy-done.22
  72.2 3.2 %collective-permute-start.16 = (bf16[1024,128]{1,0:T(8,128)(2,1)S(1)}, bf16[1024,128]{1,0:T(8,128)(2,1)S(1)}, u32[]{:S(2)}, u32[]{:S(2)}) collective-permute-start(bf16[1024,128]{1,0:T(8,128)(2,1)S(1)} %get-tuple-element.89), channel_id=1, source_target_pairs={{0,8},{4,12},{8,0},{12,4},{1,9},{5,13},{9,1},{13,5},{2,10},{6,14},... | collective-permute-start | bytes 786440 | tf_op jit(solution)/shard_map/ppermute | solution.py:505
  75.4 1.3 collective-permute-start.17
  76.7 1.2 collective-permute-start.27
  78.0 0.7 copy-done.6
  78.7 0.2 collective-permute-done.27.refs_12_
  78.9 0.6 copy-done.12
  79.6 0.4 collective-permute-start.30
  79.9 0.6 copy-done.9
  80.6 0.7 copy-done.15
  81.2 0.1 collective-permute-start.22
  81.4 10.7 %collective-permute-done.16.refs_2_ = bf16[1024,128]{1,0:T(8,128)(2,1)S(1)} collective-permute-done((bf16[1024,128]{1,0:T(8,128)(2,1)S(1)}, bf16[1024,128]{1,0:T(8,128)(2,1)S(1)}, u32[]{:S(2)}, u32[]{:S(2)}) %collective-permute-start.16) | collective-permute-done | bytes 262176 | tf_op jit(solution)/shard_map/ppermute | solution.py:505
  92.1 3.3 %collective-permute-start.24 = (bf16[1024,128]{1,0:T(8,128)(2,1)S(1)}, bf16[1024,128]{1,0:T(8,128)(2,1)}, u32[]{:S(2)}, u32[]{:S(2)}) collective-permute-start(bf16[1024,128]{1,0:T(8,128)(2,1)S(1)} %collective-permute-done.16.refs_2_), channel_id=1, source_target_pairs={{0,1},{1,0},{2,3},{3,2},{4,5},{5,4},{6,7},{7,6},{8,9},{9,8},{10,11... | collective-permute-start | bytes 786440 | tf_op jit(solution)/shard_map/ppermute | solution.py:511
  95.4 0.5 collective-permute-start.23
  95.9 0.6 copy-done.18
  96.7 1.5 %collective-permute-done.28.refs_13_ = bf16[512,128]{1,0:T(8,128)(2,1)} collective-permute-done((bf16[512,128]{1,0:T(8,128)(2,1)}, bf16[512,128]{1,0:T(8,128)(2,1)}, u32[]{:S(2)}, u32[]{:S(2)}) %collective-permute-start.28) | collective-permute-done | bytes 131104 | tf_op jit(solution)/shard_map/ppermute | solution.py:511
  98.3 0.1 collective-permute-start.13
  98.5 1.6 %copy-done.1 = bf16[1024,1024]{1,0:T(8,128)(2,1)S(1)} copy-done((bf16[1024,1024]{1,0:T(8,128)(2,1)S(1)}, bf16[1024,1024]{1,0:T(8,128)(2,1)}, u32[]{:S(2)}) %copy-start.1) | copy-done | bytes 2097176
  100.0 1.6 %copy-done.2 = bf16[1024,1024]{1,0:T(8,128)(2,1)S(1)} copy-done((bf16[1024,1024]{1,0:T(8,128)(2,1)S(1)}, bf16[1024,1024]{1,0:T(8,128)(2,1)}, u32[]{:S(2)}) %copy-start.2) | copy-done | bytes 2097176
  101.6 0.9 copy-done.5
  102.5 0.9 copy-done.7
  103.4 0.9 copy-done.10
  104.3 0.9 copy-done.13
  105.3 0.9 copy-done.16
  106.2 0.9 copy-done.19
  107.1 3.7 %shard_map.103 = bf16[256,1024]{1,0:T(8,128)(2,1)S(1)} custom-call(s32[3]{0:T(128)S(1)} %pad_add_fusion.3.place_ref, bf16[1024,128]{1,0:T(8,128)(2,1)S(1)} %get-tuple-element.95.refs_0_, bf16[1024,128]{1,0:T(8,128)(2,1)S(1)} %collective-permute-done.21.refs_1_, bf16[1024,128]{1,0:T(8,128)(2,1)S(1)} %collective-permute-done.16.refs_2_, ...), custom_call_target="tpu_custom_call" | custom-call | flops 3449999872 | bytes 1048576 | tf_op jit(solution)/shard_map/pallas_call | solution.py:485
  110.8 1.2 collective-permute-start.31
  112.1 3.7 %shard_map.105.kept_ref = bf16[256,1024]{1,0:T(8,128)(2,1)S(1)} custom-call(s32[3]{0:T(128)S(1)} %pad_add_fusion.4.place_ref, bf16[1024,128]{1,0:T(8,128)(2,1)S(1)} %get-tuple-element.95.refs_0_, bf16[1024,128]{1,0:T(8,128)(2,1)S(1)} %collective-permute-done.21.refs_1_, bf16[1024,128]{1,0:T(8,128)(2,1)S(1)} %collective-permute-done.16.refs_2_, ...), custom_call_target="tpu_custom_call" | custom-call | flops 3449999872 | bytes 1048576 | tf_op jit(solution)/shard_map/pallas_call | solution.py:485
  115.8 2.7 %collective-permute-start.32 = (bf16[256,1024]{1,0:T(8,128)(2,1)S(1)}, bf16[256,1024]{1,0:T(8,128)(2,1)S(1)}, u32[]{:S(2)}, u32[]{:S(2)}) collective-permute-start(bf16[256,1024]{1,0:T(8,128)(2,1)S(1)} %shard_map.105.kept_ref), channel_id=1, source_target_pairs={{1,2},{2,1},{5,6},{6,5},{9,10},{10,9},{13,14},{14,13},{17,18},{18,... | collective-permute-start | bytes 1572872 | tf_op jit(solution)/shard_map/ppermute | solution.py:622
  118.5 0.6 shard_map.102
  119.1 4.1 %collective-permute-start.18 = (bf16[576,128]{1,0:T(8,128)(2,1)S(1)}, bf16[576,128]{1,0:T(8,128)(2,1)S(1)}, u32[]{:S(2)}, u32[]{:S(2)}) collective-permute-start(bf16[576,128]{1,0:T(8,128)(2,1)S(1)} %get-tuple-element.92), channel_id=1, source_target_pairs={{0,4},{4,0},{8,12},{12,8},{1,5},{5,1},{9,13},{13,9},{2,6},{6,2},{1... | collective-permute-start | bytes 442376 | tf_op jit(solution)/shard_map/ppermute | solution.py:505
  123.2 1.0 collective-permute-start.19
  124.2 1.2 collective-permute-start.20
  125.5 2.0 %collective-permute-done.18.refs_1_ = bf16[576,128]{1,0:T(8,128)(2,1)S(1)} collective-permute-done((bf16[576,128]{1,0:T(8,128)(2,1)S(1)}, bf16[576,128]{1,0:T(8,128)(2,1)S(1)}, u32[]{:S(2)}, u32[]{:S(2)}) %collective-permute-start.18) | collective-permute-done | bytes 147488 | tf_op jit(solution)/shard_map/ppermute | solution.py:505
  127.4 8.0 %collective-permute-done.19.refs_2_ = bf16[576,128]{1,0:T(8,128)(2,1)S(1)} collective-permute-done((bf16[576,128]{1,0:T(8,128)(2,1)S(1)}, bf16[576,128]{1,0:T(8,128)(2,1)S(1)}, u32[]{:S(2)}, u32[]{:S(2)}) %collective-permute-start.19) | collective-permute-done | bytes 147488 | tf_op jit(solution)/shard_map/ppermute | solution.py:505
  135.5 1.5 %shard_map.104 = (bf16[256,1024]{1,0:T(8,128)(2,1)}, f32[8,32,128]{2,1,0:T(8,128)}) custom-call(s32[3]{0:T(128)S(1)} %pad_add_fusion.place_ref, bf16[576,128]{1,0:T(8,128)(2,1)S(1)} %get-tuple-element.99.refs_0_, bf16[576,128]{1,0:T(8,128)(2,1)S(1)} %collective-permute-done.18.refs_1_, bf16[576,128]{1,0:T(8,128)(2,1)S(1)} %collective-permute-done.19.refs_2_, ...), custom_call_target="tpu_custom_call" | custom-call | flops 1150000000 | bytes 1048576 | tf_op jit(solution)/shard_map/pallas_call | solution.py:485
  137.0 1.5 %shard_map.106 = bf16[256,1024]{1,0:T(8,128)(2,1)} custom-call(s32[3]{0:T(128)S(1)} %pad_add_fusion.place_ref, bf16[256,1024]{1,0:T(8,128)(2,1)S(1)} %collective-permute-done.31.first_ref, bf16[256,1024]{1,0:T(8,128)(2,1)S(1)} %collective-permute-done.32.second_ref, bf16[256,1024]{1,0:T(8,128)(2,1)S(1)} %shard_map.105.kept_ref), custom_call_target="tpu_custom_call" | custom-call | flops 1150000000 | bytes 1048576 | tf_op jit(solution)/shard_map/pallas_call | solution.py:485
  (67 shorter events, 0.7 us)
Async XLA Ops:
  0.6 4.9 %collective-permute-start = (bf16[256,2048]{1,0:T(8,128)(2,1)}, bf16[256,2048]{1,0:T(8,128)(2,1)S(1)}, u32[]{:S(2)}, u32[]{:S(2)}) collective-permute-start(bf16[256,2048]{1,0:T(8,128)(2,1)} %refs_1_.3), channel_id=1, source_target_pairs={{0,1},{1,0},{2,3},{3,2},{4,5},{5,4},{6,7},{7,6},{8,9},{9,8},{10,11... | collective-permute-start | bytes 3145736 | tf_op jit(solution)/shard_map/ppermute | solution.py:511
  0.8 1.0 copy-start.3
  1.9 0.7 copy-start.20
  3.3 1.7 %collective-permute-start.1 = (bf16[4,272,128]{2,1,0:T(8,128)(2,1)S(1)}, bf16[4,272,128]{2,1,0:T(8,128)(2,1)S(1)}, u32[]{:S(2)}, u32[]{:S(2)}) collective-permute-start(bf16[4,272,128]{2,1,0:T(8,128)(2,1)S(1)} %get-tuple-element.56), channel_id=1, source_target_pairs={{0,1},{1,0},{2,3},{3,2},{4,5},{5,4},{6,7},{7,6},{8,9},{9,8},{10,11... | collective-permute-start | bytes 835592 | tf_op jit(solution)/shard_map/ppermute | solution.py:511
  9.0 8.6 %collective-permute-start.2 = (bf16[2,512,512]{2,1,0:T(8,128)(2,1)S(1)}, bf16[2,512,512]{2,1,0:T(8,128)(2,1)S(1)}, u32[]{:S(2)}, u32[]{:S(2)}) collective-permute-start(bf16[2,512,512]{2,1,0:T(8,128)(2,1)S(1)} %shard_map.96), channel_id=1, source_target_pairs={{0,1},{1,0},{2,3},{3,2},{4,5},{5,4},{6,7},{7,6},{8,9},{9,8},{10,11... | collective-permute-start | bytes 3145736 | tf_op jit(solution)/shard_map/ppermute | solution.py:511
  9.4 14.3 %collective-permute-start.7 = (bf16[544,128]{1,0:T(8,128)(2,1)S(1)}, bf16[544,128]{1,0:T(8,128)(2,1)S(1)}, u32[]{:S(2)}, u32[]{:S(2)}) collective-permute-start(bf16[544,128]{1,0:T(8,128)(2,1)S(1)} %get-tuple-element.64), channel_id=1, source_target_pairs={{0,8},{4,12},{8,0},{12,4},{1,9},{5,13},{9,1},{13,5},{2,10},{6,14},... | collective-permute-start | bytes 417800 | tf_op jit(solution)/shard_map/ppermute | solution.py:505
  12.9 13.4 %collective-permute-start.8 = (bf16[544,128]{1,0:T(8,128)(2,1)S(1)}, bf16[544,128]{1,0:T(8,128)(2,1)S(1)}, u32[]{:S(2)}, u32[]{:S(2)}) collective-permute-start(bf16[544,128]{1,0:T(8,128)(2,1)S(1)} %get-tuple-element.65), channel_id=1, source_target_pairs={{0,12},{4,8},{8,4},{12,0},{1,13},{5,9},{9,5},{13,1},{2,14},{6,10},... | collective-permute-start | bytes 417800 | tf_op jit(solution)/shard_map/ppermute | solution.py:505
  16.6 9.8 %collective-permute-start.6 = (bf16[1,512,512]{2,1,0:T(8,128)(2,1)S(1)}, bf16[1,512,512]{2,1,0:T(8,128)(2,1)S(1)}, u32[]{:S(2)}, u32[]{:S(2)}) collective-permute-start(bf16[1,512,512]{2,1,0:T(8,128)(2,1)S(1)} %shard_map.98), channel_id=1, source_target_pairs={{0,1},{1,0},{2,3},{3,2},{4,5},{5,4},{6,7},{7,6},{8,9},{9,8},{10,11... | collective-permute-start | bytes 1572872 | tf_op jit(solution)/shard_map/ppermute | solution.py:511
  21.2 12.7 %collective-permute-start.3 = (bf16[1024,128]{1,0:T(8,128)(2,1)S(1)}, bf16[1024,128]{1,0:T(8,128)(2,1)S(1)}, u32[]{:S(2)}, u32[]{:S(2)}) collective-permute-start(bf16[1024,128]{1,0:T(8,128)(2,1)S(1)} %get-tuple-element.61), channel_id=1, source_target_pairs={{0,4},{4,0},{8,12},{12,8},{1,5},{5,1},{9,13},{13,9},{2,6},{6,2},{1... | collective-permute-start | bytes 786440 | tf_op jit(solution)/shard_map/ppermute | solution.py:505
  21.3 21.2 %collective-permute-start.4 = (bf16[1024,128]{1,0:T(8,128)(2,1)S(1)}, bf16[1024,128]{1,0:T(8,128)(2,1)S(1)}, u32[]{:S(2)}, u32[]{:S(2)}) collective-permute-start(bf16[1024,128]{1,0:T(8,128)(2,1)S(1)} %get-tuple-element.62), channel_id=1, source_target_pairs={{0,8},{4,12},{8,0},{12,4},{1,9},{5,13},{9,1},{13,5},{2,10},{6,14},... | collective-permute-start | bytes 786440 | tf_op jit(solution)/shard_map/ppermute | solution.py:505
  23.7 22.4 %collective-permute-start.5 = (bf16[1024,128]{1,0:T(8,128)(2,1)S(1)}, bf16[1024,128]{1,0:T(8,128)(2,1)S(1)}, u32[]{:S(2)}, u32[]{:S(2)}) collective-permute-start(bf16[1024,128]{1,0:T(8,128)(2,1)S(1)} %get-tuple-element.63), channel_id=1, source_target_pairs={{0,12},{4,8},{8,4},{12,0},{1,13},{5,9},{9,5},{13,1},{2,14},{6,10},... | collective-permute-start | bytes 786440 | tf_op jit(solution)/shard_map/ppermute | solution.py:505
  26.2 19.9 %collective-permute-start.12 = (bf16[544,128]{1,0:T(8,128)(2,1)S(1)}, bf16[544,128]{1,0:T(8,128)(2,1)S(1)}, u32[]{:S(2)}, u32[]{:S(2)}) collective-permute-start(bf16[544,128]{1,0:T(8,128)(2,1)S(1)} %get-tuple-element.75), channel_id=1, source_target_pairs={{0,4},{4,0},{8,12},{12,8},{1,5},{5,1},{9,13},{13,9},{2,6},{6,2},{1... | collective-permute-start | bytes 417800 | tf_op jit(solution)/shard_map/ppermute | solution.py:505
  29.3 33.0 %collective-permute-start.9 = (bf16[512,128]{1,0:T(8,128)(2,1)S(1)}, bf16[512,128]{1,0:T(8,128)(2,1)S(1)}, u32[]{:S(2)}, u32[]{:S(2)}) collective-permute-start(bf16[512,128]{1,0:T(8,128)(2,1)S(1)} %get-tuple-element.72), channel_id=1, source_target_pairs={{0,4},{4,0},{8,12},{12,8},{1,5},{5,1},{9,13},{13,9},{2,6},{6,2},{1... | collective-permute-start | bytes 393224 | tf_op jit(solution)/shard_map/ppermute | solution.py:505
  33.9 28.5 %collective-permute-start.10 = (bf16[512,128]{1,0:T(8,128)(2,1)S(1)}, bf16[512,128]{1,0:T(8,128)(2,1)S(1)}, u32[]{:S(2)}, u32[]{:S(2)}) collective-permute-start(bf16[512,128]{1,0:T(8,128)(2,1)S(1)} %get-tuple-element.73), channel_id=1, source_target_pairs={{0,8},{4,12},{8,0},{12,4},{1,9},{5,13},{9,1},{13,5},{2,10},{6,14},... | collective-permute-start | bytes 393224 | tf_op jit(solution)/shard_map/ppermute | solution.py:505
  42.5 19.9 %collective-permute-start.11 = (bf16[512,128]{1,0:T(8,128)(2,1)S(1)}, bf16[512,128]{1,0:T(8,128)(2,1)S(1)}, u32[]{:S(2)}, u32[]{:S(2)}) collective-permute-start(bf16[512,128]{1,0:T(8,128)(2,1)S(1)} %get-tuple-element.74), channel_id=1, source_target_pairs={{0,12},{4,8},{8,4},{12,0},{1,13},{5,9},{9,5},{13,1},{2,14},{6,10},... | collective-permute-start | bytes 393224 | tf_op jit(solution)/shard_map/ppermute | solution.py:505
  46.2 16.3 %copy-start.21 = (s32[256]{0:T(256)S(1)}, s32[256]{0:T(256)}, u32[]{:S(2)}) copy-start(s32[256]{0:T(256)} %param.11) | copy-start | bytes 3076
  51.7 25.0 %copy-start.4 = (bf16[512,128]{1,0:T(8,128)(2,1)}, bf16[512,128]{1,0:T(8,128)(2,1)S(1)}, u32[]{:S(2)}) copy-start(bf16[512,128]{1,0:T(8,128)(2,1)S(1)} %get-tuple-element.97.refs_8_) | copy-start | bytes 393220
  51.7 20.5 %collective-permute-start.14 = (bf16[512,128]{1,0:T(8,128)(2,1)S(1)}, bf16[512,128]{1,0:T(8,128)(2,1)S(1)}, u32[]{:S(2)}, u32[]{:S(2)}) collective-permute-start(bf16[512,128]{1,0:T(8,128)(2,1)S(1)} %get-tuple-element.87), channel_id=1, source_target_pairs={{0,8},{4,12},{8,0},{12,4},{1,9},{5,13},{9,1},{13,5},{2,10},{6,14},... | collective-permute-start | bytes 393224 | tf_op jit(solution)/shard_map/ppermute | solution.py:505
  62.1 10.1 %collective-permute-start.15 = (bf16[512,128]{1,0:T(8,128)(2,1)S(1)}, bf16[512,128]{1,0:T(8,128)(2,1)S(1)}, u32[]{:S(2)}, u32[]{:S(2)}) collective-permute-start(bf16[512,128]{1,0:T(8,128)(2,1)S(1)} %get-tuple-element.88), channel_id=1, source_target_pairs={{0,12},{4,8},{8,4},{12,0},{1,13},{5,9},{9,5},{13,1},{2,14},{6,10},... | collective-permute-start | bytes 393224 | tf_op jit(solution)/shard_map/ppermute | solution.py:505
  62.2 15.7 %collective-permute-start.26 = (bf16[512,128]{1,0:T(8,128)(2,1)S(1)}, bf16[512,128]{1,0:T(8,128)(2,1)}, u32[]{:S(2)}, u32[]{:S(2)}) collective-permute-start(bf16[512,128]{1,0:T(8,128)(2,1)S(1)} %get-tuple-element.98), channel_id=1, source_target_pairs={{0,4},{4,0},{8,12},{12,8},{1,5},{5,1},{9,13},{13,9},{2,6},{6,2},{1... | collective-permute-start | bytes 393224 | tf_op jit(solution)/shard_map/ppermute | solution.py:505
  62.5 36.0 %copy-start = (bf16[1024,1024]{1,0:T(8,128)(2,1)S(1)}, bf16[1024,1024]{1,0:T(8,128)(2,1)}, u32[]{:S(2)}) copy-start(bf16[1024,1024]{1,0:T(8,128)(2,1)} %refs_18_.3) | copy-start | bytes 6291460
  71.5 0.7 copy-start.22
  72.2 19.9 %collective-permute-start.16 = (bf16[1024,128]{1,0:T(8,128)(2,1)S(1)}, bf16[1024,128]{1,0:T(8,128)(2,1)S(1)}, u32[]{:S(2)}, u32[]{:S(2)}) collective-permute-start(bf16[1024,128]{1,0:T(8,128)(2,1)S(1)} %get-tuple-element.89), channel_id=1, source_target_pairs={{0,8},{4,12},{8,0},{12,4},{1,9},{5,13},{9,1},{13,5},{2,10},{6,14},... | collective-permute-start | bytes 786440 | tf_op jit(solution)/shard_map/ppermute | solution.py:505
  75.4 20.0 %collective-permute-start.17 = (bf16[1024,128]{1,0:T(8,128)(2,1)S(1)}, bf16[1024,128]{1,0:T(8,128)(2,1)S(1)}, u32[]{:S(2)}, u32[]{:S(2)}) collective-permute-start(bf16[1024,128]{1,0:T(8,128)(2,1)S(1)} %get-tuple-element.90), channel_id=1, source_target_pairs={{0,12},{4,8},{8,4},{12,0},{1,13},{5,9},{9,5},{13,1},{2,14},{6,10},... | collective-permute-start | bytes 786440 | tf_op jit(solution)/shard_map/ppermute | solution.py:505
  76.7 18.7 %collective-permute-start.21 = (bf16[1024,128]{1,0:T(8,128)(2,1)S(1)}, bf16[1024,128]{1,0:T(8,128)(2,1)S(1)}, u32[]{:S(2)}, u32[]{:S(2)}) collective-permute-start(bf16[1024,128]{1,0:T(8,128)(2,1)S(1)} %get-tuple-element.96), channel_id=1, source_target_pairs={{0,4},{4,0},{8,12},{12,8},{1,5},{5,1},{9,13},{13,9},{2,6},{6,2},{1... | collective-permute-start | bytes 786440 | tf_op jit(solution)/shard_map/ppermute | solution.py:505
  76.7 2.2 %collective-permute-start.27 = (bf16[512,128]{1,0:T(8,128)(2,1)S(1)}, bf16[512,128]{1,0:T(8,128)(2,1)S(1)}, u32[]{:S(2)}, u32[]{:S(2)}) collective-permute-start(bf16[512,128]{1,0:T(8,128)(2,1)S(1)} %get-tuple-element.97.refs_8_), channel_id=1, source_target_pairs={{0,1},{1,0},{2,3},{3,2},{4,5},{5,4},{6,7},{7,6},{8,9},{9,8},{10,11... | collective-permute-start | bytes 393224 | tf_op jit(solution)/shard_map/ppermute | solution.py:511
  77.9 2.6 %collective-permute-start.29 = (bf16[512,128]{1,0:T(8,128)(2,1)S(1)}, bf16[512,128]{1,0:T(8,128)(2,1)S(1)}, u32[]{:S(2)}, u32[]{:S(2)}) collective-permute-start(bf16[512,128]{1,0:T(8,128)(2,1)S(1)} %collective-permute-done.14.refs_10_), channel_id=1, source_target_pairs={{0,1},{1,0},{2,3},{3,2},{4,5},{5,4},{6,7},{7,6},{8,9},{9,8},{10,11... | collective-permute-start | bytes 393224 | tf_op jit(solution)/shard_map/ppermute | solution.py:511
  78.0 0.7 copy-start.6
  78.9 0.7 copy-start.12
  79.6 16.4 %collective-permute-start.30 = (bf16[512,128]{1,0:T(8,128)(2,1)S(1)}, bf16[512,128]{1,0:T(8,128)(2,1)S(1)}, u32[]{:S(2)}, u32[]{:S(2)}) collective-permute-start(bf16[512,128]{1,0:T(8,128)(2,1)S(1)} %collective-permute-done.15.refs_11_), channel_id=1, source_target_pairs={{0,1},{1,0},{2,3},{3,2},{4,5},{5,4},{6,7},{7,6},{8,9},{9,8},{10,11... | collective-permute-start | bytes 393224 | tf_op jit(solution)/shard_map/ppermute | solution.py:511
  79.9 0.6 copy-start.9
  80.6 0.7 copy-start.15
  81.2 17.2 %collective-permute-start.22 = (bf16[1024,128]{1,0:T(8,128)(2,1)S(1)}, bf16[1024,128]{1,0:T(8,128)(2,1)}, u32[]{:S(2)}, u32[]{:S(2)}) collective-permute-start(bf16[1024,128]{1,0:T(8,128)(2,1)S(1)} %get-tuple-element.95.refs_0_), channel_id=1, source_target_pairs={{0,1},{1,0},{2,3},{3,2},{4,5},{5,4},{6,7},{7,6},{8,9},{9,8},{10,11... | collective-permute-start | bytes 786440 | tf_op jit(solution)/shard_map/ppermute | solution.py:511
  92.1 6.3 %collective-permute-start.24 = (bf16[1024,128]{1,0:T(8,128)(2,1)S(1)}, bf16[1024,128]{1,0:T(8,128)(2,1)}, u32[]{:S(2)}, u32[]{:S(2)}) collective-permute-start(bf16[1024,128]{1,0:T(8,128)(2,1)S(1)} %collective-permute-done.16.refs_2_), channel_id=1, source_target_pairs={{0,1},{1,0},{2,3},{3,2},{4,5},{5,4},{6,7},{7,6},{8,9},{9,8},{10,11... | collective-permute-start | bytes 786440 | tf_op jit(solution)/shard_map/ppermute | solution.py:511
  95.4 3.0 %collective-permute-start.25 = (bf16[1024,128]{1,0:T(8,128)(2,1)S(1)}, bf16[1024,128]{1,0:T(8,128)(2,1)}, u32[]{:S(2)}, u32[]{:S(2)}) collective-permute-start(bf16[1024,128]{1,0:T(8,128)(2,1)S(1)} %collective-permute-done.17.refs_3_), channel_id=1, source_target_pairs={{0,1},{1,0},{2,3},{3,2},{4,5},{5,4},{6,7},{7,6},{8,9},{9,8},{10,11... | collective-permute-start | bytes 786440 | tf_op jit(solution)/shard_map/ppermute | solution.py:511
  95.4 3.0 %collective-permute-start.23 = (bf16[1024,128]{1,0:T(8,128)(2,1)S(1)}, bf16[1024,128]{1,0:T(8,128)(2,1)}, u32[]{:S(2)}, u32[]{:S(2)}) collective-permute-start(bf16[1024,128]{1,0:T(8,128)(2,1)S(1)} %collective-permute-done.21.refs_1_), channel_id=1, source_target_pairs={{0,1},{1,0},{2,3},{3,2},{4,5},{5,4},{6,7},{7,6},{8,9},{9,8},{10,11... | collective-permute-start | bytes 786440 | tf_op jit(solution)/shard_map/ppermute | solution.py:511
  95.9 0.6 copy-start.18
  96.6 1.7 %collective-permute-start.28 = (bf16[512,128]{1,0:T(8,128)(2,1)}, bf16[512,128]{1,0:T(8,128)(2,1)}, u32[]{:S(2)}, u32[]{:S(2)}) collective-permute-start(bf16[512,128]{1,0:T(8,128)(2,1)} %collective-permute-done.26.refs_9_), channel_id=1, source_target_pairs={{0,1},{1,0},{2,3},{3,2},{4,5},{5,4},{6,7},{7,6},{8,9},{9,8},{10,11... | collective-permute-start | bytes 393224 | tf_op jit(solution)/shard_map/ppermute | solution.py:511
  98.3 20.2 %collective-permute-start.13 = (bf16[4,288,128]{2,1,0:T(8,128)(2,1)S(1)}, bf16[4,288,128]{2,1,0:T(8,128)(2,1)S(1)}, u32[]{:S(2)}, u32[]{:S(2)}) collective-permute-start(bf16[4,288,128]{2,1,0:T(8,128)(2,1)S(1)} %get-tuple-element.78), channel_id=1, source_target_pairs={{0,1},{1,0},{2,3},{3,2},{4,5},{5,4},{6,7},{7,6},{8,9},{9,8},{10,11... | collective-permute-start | bytes 884744 | tf_op jit(solution)/shard_map/ppermute | solution.py:511
  98.4 1.6 %copy-start.1 = (bf16[1024,1024]{1,0:T(8,128)(2,1)S(1)}, bf16[1024,1024]{1,0:T(8,128)(2,1)}, u32[]{:S(2)}) copy-start(bf16[1024,1024]{1,0:T(8,128)(2,1)} %refs_16_.3) | copy-start | bytes 6291460
  100.0 1.6 %copy-start.2 = (bf16[1024,1024]{1,0:T(8,128)(2,1)S(1)}, bf16[1024,1024]{1,0:T(8,128)(2,1)}, u32[]{:S(2)}) copy-start(bf16[1024,1024]{1,0:T(8,128)(2,1)} %refs_17_.3) | copy-start | bytes 6291460
  101.6 0.9 copy-start.5
  102.5 0.9 copy-start.7
  103.4 0.9 copy-start.10
  104.3 0.9 copy-start.13
  105.2 0.9 copy-start.16
  106.2 0.9 copy-start.19
  107.1 5.0 %copy-start.8 = (bf16[512,128]{1,0:T(8,128)(2,1)S(1)}, bf16[512,128]{1,0:T(8,128)(2,1)}, u32[]{:S(2)}) copy-start(bf16[512,128]{1,0:T(8,128)(2,1)} %copy-done.6) | copy-start | bytes 393220
  107.1 5.0 %copy-start.11 = (bf16[512,128]{1,0:T(8,128)(2,1)S(1)}, bf16[512,128]{1,0:T(8,128)(2,1)}, u32[]{:S(2)}) copy-start(bf16[512,128]{1,0:T(8,128)(2,1)} %copy-done.9) | copy-start | bytes 393220
  107.1 5.0 %copy-start.14 = (bf16[512,128]{1,0:T(8,128)(2,1)S(1)}, bf16[512,128]{1,0:T(8,128)(2,1)}, u32[]{:S(2)}) copy-start(bf16[512,128]{1,0:T(8,128)(2,1)} %copy-done.12) | copy-start | bytes 393220
  107.1 5.0 %copy-start.17 = (bf16[512,128]{1,0:T(8,128)(2,1)S(1)}, bf16[512,128]{1,0:T(8,128)(2,1)}, u32[]{:S(2)}) copy-start(bf16[512,128]{1,0:T(8,128)(2,1)} %copy-done.15) | copy-start | bytes 393220
  110.8 24.7 %collective-permute-start.31 = (bf16[256,1024]{1,0:T(8,128)(2,1)S(1)}, bf16[256,1024]{1,0:T(8,128)(2,1)S(1)}, u32[]{:S(2)}, u32[]{:S(2)}) collective-permute-start(bf16[256,1024]{1,0:T(8,128)(2,1)S(1)} %shard_map.103), channel_id=1, source_target_pairs={{0,1},{1,3},{3,2},{2,0},{4,5},{5,7},{7,6},{6,4},{8,9},{9,11},{11,1... | collective-permute-start | bytes 1572872 | tf_op jit(solution)/shard_map/ppermute | solution.py:620
  112.1 6.4 %copy-start.23 = (bf16[4,288,128]{2,1,0:T(8,128)(2,1)S(1)}, bf16[4,288,128]{2,1,0:T(8,128)(2,1)}, u32[]{:S(2)}) copy-start(bf16[4,288,128]{2,1,0:T(8,128)(2,1)} %copy-done.22) | copy-start | bytes 884740
  115.8 21.2 %collective-permute-start.32 = (bf16[256,1024]{1,0:T(8,128)(2,1)S(1)}, bf16[256,1024]{1,0:T(8,128)(2,1)S(1)}, u32[]{:S(2)}, u32[]{:S(2)}) collective-permute-start(bf16[256,1024]{1,0:T(8,128)(2,1)S(1)} %shard_map.105.kept_ref), channel_id=1, source_target_pairs={{1,2},{2,1},{5,6},{6,5},{9,10},{10,9},{13,14},{14,13},{17,18},{18,... | collective-permute-start | bytes 1572872 | tf_op jit(solution)/shard_map/ppermute | solution.py:622
  119.1 8.3 %collective-permute-start.18 = (bf16[576,128]{1,0:T(8,128)(2,1)S(1)}, bf16[576,128]{1,0:T(8,128)(2,1)S(1)}, u32[]{:S(2)}, u32[]{:S(2)}) collective-permute-start(bf16[576,128]{1,0:T(8,128)(2,1)S(1)} %get-tuple-element.92), channel_id=1, source_target_pairs={{0,4},{4,0},{8,12},{12,8},{1,5},{5,1},{9,13},{13,9},{2,6},{6,2},{1... | collective-permute-start | bytes 442376 | tf_op jit(solution)/shard_map/ppermute | solution.py:505
  123.2 12.2 %collective-permute-start.19 = (bf16[576,128]{1,0:T(8,128)(2,1)S(1)}, bf16[576,128]{1,0:T(8,128)(2,1)S(1)}, u32[]{:S(2)}, u32[]{:S(2)}) collective-permute-start(bf16[576,128]{1,0:T(8,128)(2,1)S(1)} %get-tuple-element.93), channel_id=1, source_target_pairs={{0,8},{4,12},{8,0},{12,4},{1,9},{5,13},{9,1},{13,5},{2,10},{6,14},... | collective-permute-start | bytes 442376 | tf_op jit(solution)/shard_map/ppermute | solution.py:505
  124.2 11.3 %collective-permute-start.20 = (bf16[576,128]{1,0:T(8,128)(2,1)S(1)}, bf16[576,128]{1,0:T(8,128)(2,1)S(1)}, u32[]{:S(2)}, u32[]{:S(2)}) collective-permute-start(bf16[576,128]{1,0:T(8,128)(2,1)S(1)} %get-tuple-element.94), channel_id=1, source_target_pairs={{0,12},{4,8},{8,4},{12,0},{1,13},{5,9},{9,5},{13,1},{2,14},{6,10},... | collective-permute-start | bytes 442376 | tf_op jit(solution)/shard_map/ppermute | solution.py:505

commit v8 on v7

--- a/solution.py
+++ b/solution.py
@@ -415,7 +415,7 @@
             out_ref[chip, rows:, :] = attended_ref[at, :]
 
 
-def input_kernel(chips, place_ref, *refs):
+def input_kernel(chips, which, place_ref, *refs):
     weights, (out_ref, gathered_ref) = refs[4 * chips : -2], refs[-2:]
     rows, width = out_ref.shape[0], weights[0].shape[1]
     head_dim = width // (2 * chips)
@@ -426,7 +426,7 @@
             head = (place_ref[1] ^ turn) * chips + (place_ref[0] ^ offset)
             for index in range(3):
                 source = parts[offset] if index < 2 else valued[offset]
-                at = pl.multiple_of((2 * (index % 2) + place_ref[2]) * rows, rows)
+                at = pl.multiple_of((2 * (index % 2) + place_ref[which]) * rows, rows)
                 start = pl.multiple_of(index * width + head * head_dim, head_dim)
                 gathered_ref[:, pl.ds(start, head_dim)] = source[pl.ds(at, rows), :]
     flipped = None
@@ -479,7 +479,7 @@
     project_params = pltpu.CompilerParams(vmem_limit_bytes=32 * mebi)
     swap = [(0, 1), (1, 0)]
     chip, side, column = (lax.axis_index(name) for name in ("seq", "sub", "head"))
-    place = jnp.stack([chip, side])
+    place = jnp.stack([chip, side, column, 1 - column])
 
     def call(kernel, outs, *operands, scratch=(), hbm=0, limits=params, takes=1):
         return pl.pallas_call(
@@ -599,11 +599,11 @@
     back_other = tuple(to_sibling(part) for part in back)
     value_other = tuple(to_sibling(part) for part in value_back)
 
-    def input_part(shard):
+    def input_part(which, place):
         return call(
-            partial(input_kernel, chips),
+            partial(input_kernel, chips, which),
             low(rows, half),
-            jnp.stack([chip, side, shard]),
+            place,
             *back,
             *back_other,
             *value_back,
@@ -616,22 +616,21 @@
         )
 
     square = ("head", "sub")
-    crossing = input_part(1 - column)
+    crossing = input_part(3, place)
     first = lax.ppermute(crossing, square, [(0, 1), (1, 3), (3, 2), (2, 0)])
-    kept = input_part(lax.optimization_barrier((column, crossing))[0])
+    kept = input_part(2, lax.optimization_barrier((place, crossing))[0])
     second = lax.ppermute(kept, square, [(1, 2), (2, 1)])
     *outputs, _, _ = lax.optimization_barrier((*outputs, back[2], back[3]))
     returned = exchange(outputs)
-    corner = jnp.stack([chip, side, column])
     *returned, _ = lax.optimization_barrier((*returned, first))
     attended, centroid_sums = call(
         partial(attended_kernel, chips),
         (low(rows, width), jax.ShapeDtypeStruct((count, owned, head_dim), jnp.float32)),
-        corner,
+        place,
         *returned,
     )
     first, _ = lax.optimization_barrier((first, attended))
-    d_hidden = call(sum_kernel, low(rows, half), corner, first, second, kept)
+    d_hidden = call(sum_kernel, low(rows, half), place, first, second, kept)
     return (attended, d_hidden, centroid_sums)
 
 

time: 139 us -> 127 us (0.914)
  local copies, waits for them, and re-layouts: 14.3 us -> 1.76 us
  waiting for transfers between devices: 35.6 us -> 37.5 us
  Pallas kernels: 39.2 us -> 37.7 us
    unnamed x48 -> x12, local copies, waits for them, and re-layouts: 14.3 us -> 1.76 us
    pallas_call x13, Pallas kernels: 39.2 us -> 37.7 us  [call(): pl.pallas_call(kernel, out_shape=outs, in_specs=[smem] + [vmem] * (len(op...]
  transfers between devices with their start and end apart: 33 -> 33, of which waited for: 8 -> 8; matrix products, arithmetic and copies ran while one was open for 0% -> 0% of each run, Pallas kernels for 25% -> 26%
where the time goes in v8:
time: 127 us
  starting transfers between devices  49 us (39%)
  Pallas kernels  37.7 us (30%)
  waiting for transfers between devices  37.5 us (30%)
  local copies, waits for them, and re-layouts  1.76 us (1%)
    pallas_call x13, Pallas kernels, call(): pl.pallas_call(kernel, out_shape=outs, in_specs=[smem] + [vmem] * (len(op...  37.7 us
    ppermute x18, starting transfers between devices, exchange(): lax.ppermute(parts[offset], 'seq', [(at, at ^ offset) for at in range(chi...  36.8 us
    ppermute x18, waiting for transfers between devices, exchange(): lax.ppermute(parts[offset], 'seq', [(at, at ^ offset) for at in range(chi...  33.8 us
    ppermute x13, starting transfers between devices, to_sibling(): return lax.ppermute(piece, 'sub', swap)  8.52 us
    ppermute x13, waiting for transfers between devices, to_sibling(): return lax.ppermute(piece, 'sub', swap)  3.63 us
  transfers between devices with their start and end apart: 33, of which 8 were waited for; matrix products, arithmetic and copies ran while one was open for 0% of the time, Pallas kernels for 26%

profile of v8, /device:TPU:1, one launch (start us, length us, event | category | flops | bytes accessed | tf_op | source)
XLA Modules:
  0.0 126.8 jit_solution(4319952739554234953)
XLA Ops:
  0.6 0.1 collective-permute-start
  0.8 0.1 pad_add_fusion.place_ref
  0.8 1.0 copy-done.3
  1.9 0.7 copy-done.4
  2.6 0.7 shard_map.94
  3.3 0.5 collective-permute-start.1
  3.8 1.2 collective-permute-done.1.theirs_ref
  5.0 0.6 shard_map.95
  5.6 3.4 %shard_map.96 = bf16[2,512,512]{2,1,0:T(8,128)(2,1)S(1)} custom-call(s32[4]{0:T(128)S(1)} %pad_add_fusion.place_ref, bf16[256,2048]{1,0:T(8,128)(2,1)} %refs_1_.3, bf16[256,2048]{1,0:T(8,128)(2,1)S(1)} %collective-permute-done.refs_1_.refs_2_, bf16[1024,1024]{1,0:T(8,128)(2,1)} %refs_16_.3, bf16[1024,1024]{1,0:T(8,128)(2,1)} %refs_17_.3), custom_call_target="tpu_custom_call" | custom-call | flops 115000000 | bytes 1048576 | tf_op jit(solution)/shard_map/pallas_call | solution.py:485
  9.0 0.4 collective-permute-start.2
  9.4 3.4 %collective-permute-start.7 = (bf16[544,128]{1,0:T(8,128)(2,1)S(1)}, bf16[544,128]{1,0:T(8,128)(2,1)S(1)}, u32[]{:S(2)}, u32[]{:S(2)}) collective-permute-start(bf16[544,128]{1,0:T(8,128)(2,1)S(1)} %get-tuple-element.64), channel_id=1, source_target_pairs={{0,8},{4,12},{8,0},{12,4},{1,9},{5,13},{9,1},{13,5},{2,10},{6,14},... | collective-permute-start | bytes 417800 | tf_op jit(solution)/shard_map/ppermute | solution.py:505
  12.9 1.1 collective-permute-start.8
  13.9 2.7 %shard_map.98 = bf16[1,512,512]{2,1,0:T(8,128)(2,1)S(1)} custom-call(s32[4]{0:T(128)S(1)} %pad_add_fusion.place_ref, bf16[256,2048]{1,0:T(8,128)(2,1)} %refs_1_.3, bf16[256,2048]{1,0:T(8,128)(2,1)S(1)} %collective-permute-done.refs_1_.refs_2_, bf16[1024,1024]{1,0:T(8,128)(2,1)} %refs_18_.3), custom_call_target="tpu_custom_call" | custom-call | flops 115000000 | bytes 1048576 | tf_op jit(solution)/shard_map/pallas_call | solution.py:485
  16.6 1.0 collective-permute-start.6
  17.6 0.0 collective-permute-done.2.refs_0_
  17.6 3.6 %shard_map.97 = (bf16[1024,128]{1,0:T(8,128)(2,1)S(1)}, bf16[1024,128]{1,0:T(8,128)(2,1)S(1)}, bf16[1024,128]{1,0:T(8,128)(2,1)S(1)}, bf16[1024,128]{1,0:T(8,128)(2,1)S(1)}) custom-call(s32[4]{0:T(128)S(1)} %pad_add_fusion.place_ref, bf16[2,512,512]{2,1,0:T(8,128)(2,1)S(1)} %collective-permute-done.2.refs_0_, bf16[256,2048]{1,0:T(8,128)(2,1)} %refs_1_.3, ...), custom_call_target="tpu_custom_call" | custom-call | flops 9200000000 | bytes 1048576 | tf_op jit(solution)/shard_map/pallas_call | solution.py:485
  21.2 0.1 collective-permute-start.3
  21.3 2.5 %collective-permute-start.4 = (bf16[1024,128]{1,0:T(8,128)(2,1)S(1)}, bf16[1024,128]{1,0:T(8,128)(2,1)S(1)}, u32[]{:S(2)}, u32[]{:S(2)}) collective-permute-start(bf16[1024,128]{1,0:T(8,128)(2,1)S(1)} %get-tuple-element.62), channel_id=1, source_target_pairs={{0,8},{4,12},{8,0},{12,4},{1,9},{5,13},{9,1},{13,5},{2,10},{6,14},... | collective-permute-start | bytes 786440 | tf_op jit(solution)/shard_map/ppermute | solution.py:505
  23.8 2.5 %collective-permute-start.5 = (bf16[1024,128]{1,0:T(8,128)(2,1)S(1)}, bf16[1024,128]{1,0:T(8,128)(2,1)S(1)}, u32[]{:S(2)}, u32[]{:S(2)}) collective-permute-start(bf16[1024,128]{1,0:T(8,128)(2,1)S(1)} %get-tuple-element.63), channel_id=1, source_target_pairs={{0,12},{4,8},{8,4},{12,0},{1,13},{5,9},{9,5},{13,1},{2,14},{6,10},... | collective-permute-start | bytes 786440 | tf_op jit(solution)/shard_map/ppermute | solution.py:505
  26.2 0.2 collective-permute-start.12
  26.4 2.8 %shard_map.99 = (bf16[512,128]{1,0:T(8,128)(2,1)S(1)}, bf16[512,128]{1,0:T(8,128)(2,1)S(1)}, bf16[512,128]{1,0:T(8,128)(2,1)S(1)}, bf16[512,128]{1,0:T(8,128)(2,1)S(1)}) custom-call(s32[4]{0:T(128)S(1)} %pad_add_fusion.place_ref, bf16[1,512,512]{2,1,0:T(8,128)(2,1)S(1)} %collective-permute-done.6.refs_0_, bf16[256,2048]{1,0:T(8,128)(2,1)} %refs_1_.3, ...), custom_call_target="tpu_custom_call" | custom-call | flops 115000000 | bytes 1048576 | tf_op jit(solution)/shard_map/pallas_call | solution.py:485
  29.3 1.4 %collective-permute-start.9 = (bf16[512,128]{1,0:T(8,128)(2,1)S(1)}, bf16[512,128]{1,0:T(8,128)(2,1)S(1)}, u32[]{:S(2)}, u32[]{:S(2)}) collective-permute-start(bf16[512,128]{1,0:T(8,128)(2,1)S(1)} %get-tuple-element.72), channel_id=1, source_target_pairs={{0,4},{4,0},{8,12},{12,8},{1,5},{5,1},{9,13},{13,9},{2,6},{6,2},{1... | collective-permute-start | bytes 393224 | tf_op jit(solution)/shard_map/ppermute | solution.py:505
  30.6 3.3 %collective-permute-done.3.refs_1_ = bf16[1024,128]{1,0:T(8,128)(2,1)S(1)} collective-permute-done((bf16[1024,128]{1,0:T(8,128)(2,1)S(1)}, bf16[1024,128]{1,0:T(8,128)(2,1)S(1)}, u32[]{:S(2)}, u32[]{:S(2)}) %collective-permute-start.3) | collective-permute-done | bytes 262176 | tf_op jit(solution)/shard_map/ppermute | solution.py:505
  33.9 8.6 %collective-permute-done.4.refs_2_ = bf16[1024,128]{1,0:T(8,128)(2,1)S(1)} collective-permute-done((bf16[1024,128]{1,0:T(8,128)(2,1)S(1)}, bf16[1024,128]{1,0:T(8,128)(2,1)S(1)}, u32[]{:S(2)}, u32[]{:S(2)}) %collective-permute-start.4) | collective-permute-done | bytes 262176 | tf_op jit(solution)/shard_map/ppermute | solution.py:505
  42.5 3.7 %collective-permute-start.11 = (bf16[512,128]{1,0:T(8,128)(2,1)S(1)}, bf16[512,128]{1,0:T(8,128)(2,1)S(1)}, u32[]{:S(2)}, u32[]{:S(2)}) collective-permute-start(bf16[512,128]{1,0:T(8,128)(2,1)S(1)} %get-tuple-element.74), channel_id=1, source_target_pairs={{0,12},{4,8},{8,4},{12,0},{1,13},{5,9},{9,5},{13,1},{2,14},{6,10},... | collective-permute-start | bytes 393224 | tf_op jit(solution)/shard_map/ppermute | solution.py:505
  46.2 5.5 %shard_map.100 = (bf16[512,128]{1,0:T(8,128)(2,1)S(1)}, bf16[512,128]{1,0:T(8,128)(2,1)S(1)}, bf16[512,128]{1,0:T(8,128)(2,1)S(1)}, bf16[512,128]{1,0:T(8,128)(2,1)S(1)}, f32[8,256]{1,0:T(8,128)S(1)}) custom-call(s32[4]{0:T(128)S(1)} %pad_add_fusion.place_ref, bf16[1024,128]{1,0:T(8,128)(2,1)S(1)} %get-tuple-element.68.refs_0_, ...), custom_call_target="tpu_custom_call" | custom-call | flops 8049999872 | bytes 1048576 | tf_op jit(solution)/shard_map/pallas_call | solution.py:485
  51.7 10.4 %collective-permute-start.14 = (bf16[512,128]{1,0:T(8,128)(2,1)S(1)}, bf16[512,128]{1,0:T(8,128)(2,1)S(1)}, u32[]{:S(2)}, u32[]{:S(2)}) collective-permute-start(bf16[512,128]{1,0:T(8,128)(2,1)S(1)} %get-tuple-element.87), channel_id=1, source_target_pairs={{0,8},{4,12},{8,0},{12,4},{1,9},{5,13},{9,1},{13,5},{2,10},{6,14},... | collective-permute-start | bytes 393224 | tf_op jit(solution)/shard_map/ppermute | solution.py:505
  62.1 0.2 collective-permute-start.15
  62.2 0.2 collective-permute-start.26
  62.4 0.0 collective-permute-done.11.refs_7_
  62.4 0.0 copy-start
  62.5 0.0 copy-start.1
  62.5 0.0 copy-start.2
  62.5 9.0 %shard_map.101 = (bf16[1024,128]{1,0:T(8,128)(2,1)S(1)}, bf16[1024,128]{1,0:T(8,128)(2,1)S(1)}, bf16[1024,128]{1,0:T(8,128)(2,1)S(1)}, bf16[1024,128]{1,0:T(8,12...) custom-call(s32[4]{0:T(128)S(1)} %pad_add_fusion.place_ref, ...), custom_call_target="tpu_custom_call" | custom-call | flops 11500000256 | bytes 1048576 | tf_op jit(solution)/shard_map/pallas_call | solution.py:485
  71.5 0.0 collective-permute-done.14.refs_10_
  71.5 3.2 %collective-permute-start.16 = (bf16[1024,128]{1,0:T(8,128)(2,1)S(1)}, bf16[1024,128]{1,0:T(8,128)(2,1)S(1)}, u32[]{:S(2)}, u32[]{:S(2)}) collective-permute-start(bf16[1024,128]{1,0:T(8,128)(2,1)S(1)} %get-tuple-element.89), channel_id=1, source_target_pairs={{0,8},{4,12},{8,0},{12,4},{1,9},{5,13},{9,1},{13,5},{2,10},{6,14},... | collective-permute-start | bytes 786440 | tf_op jit(solution)/shard_map/ppermute | solution.py:505
  74.8 1.9 %collective-permute-start.17 = (bf16[1024,128]{1,0:T(8,128)(2,1)S(1)}, bf16[1024,128]{1,0:T(8,128)(2,1)S(1)}, u32[]{:S(2)}, u32[]{:S(2)}) collective-permute-start(bf16[1024,128]{1,0:T(8,128)(2,1)S(1)} %get-tuple-element.90), channel_id=1, source_target_pairs={{0,12},{4,8},{8,4},{12,0},{1,13},{5,9},{9,5},{13,1},{2,14},{6,10},... | collective-permute-start | bytes 786440 | tf_op jit(solution)/shard_map/ppermute | solution.py:505
  76.7 1.2 collective-permute-start.27
  77.9 0.0 collective-permute-done.26.refs_9_
  77.9 0.1 collective-permute-start.29
  78.0 0.9 collective-permute-done.27.refs_12_
  78.9 0.4 collective-permute-start.30
  79.3 0.0 collective-permute-done.29.refs_14_
  79.3 0.2 collective-permute-start.22
  79.5 11.8 %collective-permute-done.16.refs_2_ = bf16[1024,128]{1,0:T(8,128)(2,1)S(1)} collective-permute-done((bf16[1024,128]{1,0:T(8,128)(2,1)S(1)}, bf16[1024,128]{1,0:T(8,128)(2,1)S(1)}, u32[]{:S(2)}, u32[]{:S(2)}) %collective-permute-start.16) | collective-permute-done | bytes 262176 | tf_op jit(solution)/shard_map/ppermute | solution.py:505
  91.3 3.7 %collective-permute-start.24 = (bf16[1024,128]{1,0:T(8,128)(2,1)S(1)}, bf16[1024,128]{1,0:T(8,128)(2,1)S(1)}, u32[]{:S(2)}, u32[]{:S(2)}) collective-permute-start(bf16[1024,128]{1,0:T(8,128)(2,1)S(1)} %collective-permute-done.16.refs_2_), channel_id=1, source_target_pairs={{0,1},{1,0},{2,3},{3,2},{4,5},{5,4},{6,7},{7,6},{8,9},{9,8},{10,11... | collective-permute-start | bytes 786440 | tf_op jit(solution)/shard_map/ppermute | solution.py:511
  95.0 0.0 collective-permute-start.25
  95.0 0.5 collective-permute-start.23
  95.5 0.0 collective-permute-done.30.refs_15_
  95.5 0.1 collective-permute-start.28
  95.5 1.5 %collective-permute-done.28.refs_13_ = bf16[512,128]{1,0:T(8,128)(2,1)S(1)} collective-permute-done((bf16[512,128]{1,0:T(8,128)(2,1)S(1)}, bf16[512,128]{1,0:T(8,128)(2,1)S(1)}, u32[]{:S(2)}, u32[]{:S(2)}) %collective-permute-start.28) | collective-permute-done | bytes 131104 | tf_op jit(solution)/shard_map/ppermute | solution.py:511
  97.1 0.4 collective-permute-start.13
  97.5 2.9 %shard_map.103 = bf16[256,1024]{1,0:T(8,128)(2,1)S(1)} custom-call(s32[4]{0:T(128)S(1)} %pad_add_fusion.place_ref, bf16[1024,128]{1,0:T(8,128)(2,1)S(1)} %get-tuple-element.95.refs_0_, bf16[1024,128]{1,0:T(8,128)(2,1)S(1)} %collective-permute-done.21.refs_1_, bf16[1024,128]{1,0:T(8,128)(2,1)S(1)} %collective-permute-done.16.refs_2_, ...), custom_call_target="tpu_custom_call" | custom-call | flops 3449999872 | bytes 1048576 | tf_op jit(solution)/shard_map/pallas_call | solution.py:485
  100.4 1.2 collective-permute-start.31
  101.6 2.9 %shard_map.105.kept_ref = bf16[256,1024]{1,0:T(8,128)(2,1)S(1)} custom-call(s32[4]{0:T(128)S(1)} %pad_add_fusion.place_ref, bf16[1024,128]{1,0:T(8,128)(2,1)S(1)} %get-tuple-element.95.refs_0_, bf16[1024,128]{1,0:T(8,128)(2,1)S(1)} %collective-permute-done.21.refs_1_, bf16[1024,128]{1,0:T(8,128)(2,1)S(1)} %collective-permute-done.16.refs_2_, ...), custom_call_target="tpu_custom_call" | custom-call | flops 3449999872 | bytes 1048576 | tf_op jit(solution)/shard_map/pallas_call | solution.py:485
  104.5 2.5 %collective-permute-start.32 = (bf16[256,1024]{1,0:T(8,128)(2,1)S(1)}, bf16[256,1024]{1,0:T(8,128)(2,1)S(1)}, u32[]{:S(2)}, u32[]{:S(2)}) collective-permute-start(bf16[256,1024]{1,0:T(8,128)(2,1)S(1)} %shard_map.105.kept_ref), channel_id=1, source_target_pairs={{1,2},{2,1},{5,6},{6,5},{9,10},{10,9},{13,14},{14,13},{17,18},{18,... | collective-permute-start | bytes 1572872 | tf_op jit(solution)/shard_map/ppermute | solution.py:622
  107.0 0.6 shard_map.102
  107.6 4.0 %collective-permute-start.18 = (bf16[576,128]{1,0:T(8,128)(2,1)S(1)}, bf16[576,128]{1,0:T(8,128)(2,1)S(1)}, u32[]{:S(2)}, u32[]{:S(2)}) collective-permute-start(bf16[576,128]{1,0:T(8,128)(2,1)S(1)} %get-tuple-element.92), channel_id=1, source_target_pairs={{0,4},{4,0},{8,12},{12,8},{1,5},{5,1},{9,13},{13,9},{2,6},{6,2},{1... | collective-permute-start | bytes 442376 | tf_op jit(solution)/shard_map/ppermute | solution.py:505
  111.6 1.0 collective-permute-start.19
  112.6 1.2 collective-permute-start.20
  113.7 2.1 %collective-permute-done.18.refs_1_ = bf16[576,128]{1,0:T(8,128)(2,1)S(1)} collective-permute-done((bf16[576,128]{1,0:T(8,128)(2,1)S(1)}, bf16[576,128]{1,0:T(8,128)(2,1)S(1)}, u32[]{:S(2)}, u32[]{:S(2)}) %collective-permute-start.18) | collective-permute-done | bytes 147488 | tf_op jit(solution)/shard_map/ppermute | solution.py:505
  115.8 8.0 %collective-permute-done.19.refs_2_ = bf16[576,128]{1,0:T(8,128)(2,1)S(1)} collective-permute-done((bf16[576,128]{1,0:T(8,128)(2,1)S(1)}, bf16[576,128]{1,0:T(8,128)(2,1)S(1)}, u32[]{:S(2)}, u32[]{:S(2)}) %collective-permute-start.19) | collective-permute-done | bytes 147488 | tf_op jit(solution)/shard_map/ppermute | solution.py:505
  123.8 1.5 %shard_map.104 = (bf16[256,1024]{1,0:T(8,128)(2,1)}, f32[8,32,128]{2,1,0:T(8,128)}) custom-call(s32[4]{0:T(128)S(1)} %pad_add_fusion.place_ref, bf16[576,128]{1,0:T(8,128)(2,1)S(1)} %get-tuple-element.99.refs_0_, bf16[576,128]{1,0:T(8,128)(2,1)S(1)} %collective-permute-done.18.refs_1_, bf16[576,128]{1,0:T(8,128)(2,1)S(1)} %collective-permute-done.19.refs_2_, ...), custom_call_target="tpu_custom_call" | custom-call | flops 1150000000 | bytes 1048576 | tf_op jit(solution)/shard_map/pallas_call | solution.py:485
  125.4 1.5 %shard_map.106 = bf16[256,1024]{1,0:T(8,128)(2,1)} custom-call(s32[4]{0:T(128)S(1)} %pad_add_fusion.place_ref, bf16[256,1024]{1,0:T(8,128)(2,1)S(1)} %collective-permute-done.31.first_ref, bf16[256,1024]{1,0:T(8,128)(2,1)S(1)} %collective-permute-done.32.second_ref, bf16[256,1024]{1,0:T(8,128)(2,1)S(1)} %shard_map.105.kept_ref), custom_call_target="tpu_custom_call" | custom-call | flops 1150000000 | bytes 1048576 | tf_op jit(solution)/shard_map/pallas_call | solution.py:485
  (28 shorter events, 0.1 us)
Async XLA Ops:
  0.6 4.9 %collective-permute-start = (bf16[256,2048]{1,0:T(8,128)(2,1)}, bf16[256,2048]{1,0:T(8,128)(2,1)S(1)}, u32[]{:S(2)}, u32[]{:S(2)}) collective-permute-start(bf16[256,2048]{1,0:T(8,128)(2,1)} %refs_1_.3), channel_id=1, source_target_pairs={{0,1},{1,0},{2,3},{3,2},{4,5},{5,4},{6,7},{7,6},{8,9},{9,8},{10,11... | collective-permute-start | bytes 3145736 | tf_op jit(solution)/shard_map/ppermute | solution.py:511
  0.8 1.0 copy-start.3
  1.9 0.7 copy-start.4
  3.3 1.7 %collective-permute-start.1 = (bf16[4,272,128]{2,1,0:T(8,128)(2,1)S(1)}, bf16[4,272,128]{2,1,0:T(8,128)(2,1)S(1)}, u32[]{:S(2)}, u32[]{:S(2)}) collective-permute-start(bf16[4,272,128]{2,1,0:T(8,128)(2,1)S(1)} %get-tuple-element.56), channel_id=1, source_target_pairs={{0,1},{1,0},{2,3},{3,2},{4,5},{5,4},{6,7},{7,6},{8,9},{9,8},{10,11... | collective-permute-start | bytes 835592 | tf_op jit(solution)/shard_map/ppermute | solution.py:511
  9.0 8.6 %collective-permute-start.2 = (bf16[2,512,512]{2,1,0:T(8,128)(2,1)S(1)}, bf16[2,512,512]{2,1,0:T(8,128)(2,1)S(1)}, u32[]{:S(2)}, u32[]{:S(2)}) collective-permute-start(bf16[2,512,512]{2,1,0:T(8,128)(2,1)S(1)} %shard_map.96), channel_id=1, source_target_pairs={{0,1},{1,0},{2,3},{3,2},{4,5},{5,4},{6,7},{7,6},{8,9},{9,8},{10,11... | collective-permute-start | bytes 3145736 | tf_op jit(solution)/shard_map/ppermute | solution.py:511
  9.4 14.3 %collective-permute-start.7 = (bf16[544,128]{1,0:T(8,128)(2,1)S(1)}, bf16[544,128]{1,0:T(8,128)(2,1)S(1)}, u32[]{:S(2)}, u32[]{:S(2)}) collective-permute-start(bf16[544,128]{1,0:T(8,128)(2,1)S(1)} %get-tuple-element.64), channel_id=1, source_target_pairs={{0,8},{4,12},{8,0},{12,4},{1,9},{5,13},{9,1},{13,5},{2,10},{6,14},... | collective-permute-start | bytes 417800 | tf_op jit(solution)/shard_map/ppermute | solution.py:505
  12.9 13.4 %collective-permute-start.8 = (bf16[544,128]{1,0:T(8,128)(2,1)S(1)}, bf16[544,128]{1,0:T(8,128)(2,1)S(1)}, u32[]{:S(2)}, u32[]{:S(2)}) collective-permute-start(bf16[544,128]{1,0:T(8,128)(2,1)S(1)} %get-tuple-element.65), channel_id=1, source_target_pairs={{0,12},{4,8},{8,4},{12,0},{1,13},{5,9},{9,5},{13,1},{2,14},{6,10},... | collective-permute-start | bytes 417800 | tf_op jit(solution)/shard_map/ppermute | solution.py:505
  16.6 9.8 %collective-permute-start.6 = (bf16[1,512,512]{2,1,0:T(8,128)(2,1)S(1)}, bf16[1,512,512]{2,1,0:T(8,128)(2,1)S(1)}, u32[]{:S(2)}, u32[]{:S(2)}) collective-permute-start(bf16[1,512,512]{2,1,0:T(8,128)(2,1)S(1)} %shard_map.98), channel_id=1, source_target_pairs={{0,1},{1,0},{2,3},{3,2},{4,5},{5,4},{6,7},{7,6},{8,9},{9,8},{10,11... | collective-permute-start | bytes 1572872 | tf_op jit(solution)/shard_map/ppermute | solution.py:511
  21.2 12.7 %collective-permute-start.3 = (bf16[1024,128]{1,0:T(8,128)(2,1)S(1)}, bf16[1024,128]{1,0:T(8,128)(2,1)S(1)}, u32[]{:S(2)}, u32[]{:S(2)}) collective-permute-start(bf16[1024,128]{1,0:T(8,128)(2,1)S(1)} %get-tuple-element.61), channel_id=1, source_target_pairs={{0,4},{4,0},{8,12},{12,8},{1,5},{5,1},{9,13},{13,9},{2,6},{6,2},{1... | collective-permute-start | bytes 786440 | tf_op jit(solution)/shard_map/ppermute | solution.py:505
  21.3 21.2 %collective-permute-start.4 = (bf16[1024,128]{1,0:T(8,128)(2,1)S(1)}, bf16[1024,128]{1,0:T(8,128)(2,1)S(1)}, u32[]{:S(2)}, u32[]{:S(2)}) collective-permute-start(bf16[1024,128]{1,0:T(8,128)(2,1)S(1)} %get-tuple-element.62), channel_id=1, source_target_pairs={{0,8},{4,12},{8,0},{12,4},{1,9},{5,13},{9,1},{13,5},{2,10},{6,14},... | collective-permute-start | bytes 786440 | tf_op jit(solution)/shard_map/ppermute | solution.py:505
  23.8 22.4 %collective-permute-start.5 = (bf16[1024,128]{1,0:T(8,128)(2,1)S(1)}, bf16[1024,128]{1,0:T(8,128)(2,1)S(1)}, u32[]{:S(2)}, u32[]{:S(2)}) collective-permute-start(bf16[1024,128]{1,0:T(8,128)(2,1)S(1)} %get-tuple-element.63), channel_id=1, source_target_pairs={{0,12},{4,8},{8,4},{12,0},{1,13},{5,9},{9,5},{13,1},{2,14},{6,10},... | collective-permute-start | bytes 786440 | tf_op jit(solution)/shard_map/ppermute | solution.py:505
  26.2 19.9 %collective-permute-start.12 = (bf16[544,128]{1,0:T(8,128)(2,1)S(1)}, bf16[544,128]{1,0:T(8,128)(2,1)S(1)}, u32[]{:S(2)}, u32[]{:S(2)}) collective-permute-start(bf16[544,128]{1,0:T(8,128)(2,1)S(1)} %get-tuple-element.75), channel_id=1, source_target_pairs={{0,4},{4,0},{8,12},{12,8},{1,5},{5,1},{9,13},{13,9},{2,6},{6,2},{1... | collective-permute-start | bytes 417800 | tf_op jit(solution)/shard_map/ppermute | solution.py:505
  29.3 33.0 %collective-permute-start.9 = (bf16[512,128]{1,0:T(8,128)(2,1)S(1)}, bf16[512,128]{1,0:T(8,128)(2,1)S(1)}, u32[]{:S(2)}, u32[]{:S(2)}) collective-permute-start(bf16[512,128]{1,0:T(8,128)(2,1)S(1)} %get-tuple-element.72), channel_id=1, source_target_pairs={{0,4},{4,0},{8,12},{12,8},{1,5},{5,1},{9,13},{13,9},{2,6},{6,2},{1... | collective-permute-start | bytes 393224 | tf_op jit(solution)/shard_map/ppermute | solution.py:505
  33.9 28.5 %collective-permute-start.10 = (bf16[512,128]{1,0:T(8,128)(2,1)S(1)}, bf16[512,128]{1,0:T(8,128)(2,1)S(1)}, u32[]{:S(2)}, u32[]{:S(2)}) collective-permute-start(bf16[512,128]{1,0:T(8,128)(2,1)S(1)} %get-tuple-element.73), channel_id=1, source_target_pairs={{0,8},{4,12},{8,0},{12,4},{1,9},{5,13},{9,1},{13,5},{2,10},{6,14},... | collective-permute-start | bytes 393224 | tf_op jit(solution)/shard_map/ppermute | solution.py:505
  42.5 19.9 %collective-permute-start.11 = (bf16[512,128]{1,0:T(8,128)(2,1)S(1)}, bf16[512,128]{1,0:T(8,128)(2,1)S(1)}, u32[]{:S(2)}, u32[]{:S(2)}) collective-permute-start(bf16[512,128]{1,0:T(8,128)(2,1)S(1)} %get-tuple-element.74), channel_id=1, source_target_pairs={{0,12},{4,8},{8,4},{12,0},{1,13},{5,9},{9,5},{13,1},{2,14},{6,10},... | collective-permute-start | bytes 393224 | tf_op jit(solution)/shard_map/ppermute | solution.py:505
  46.2 16.3 %copy-start.5 = (s32[256]{0:T(256)S(1)}, s32[256]{0:T(256)}, u32[]{:S(2)}) copy-start(s32[256]{0:T(256)} %param.11) | copy-start | bytes 3076
  51.7 19.9 %collective-permute-start.14 = (bf16[512,128]{1,0:T(8,128)(2,1)S(1)}, bf16[512,128]{1,0:T(8,128)(2,1)S(1)}, u32[]{:S(2)}, u32[]{:S(2)}) collective-permute-start(bf16[512,128]{1,0:T(8,128)(2,1)S(1)} %get-tuple-element.87), channel_id=1, source_target_pairs={{0,8},{4,12},{8,0},{12,4},{1,9},{5,13},{9,1},{13,5},{2,10},{6,14},... | collective-permute-start | bytes 393224 | tf_op jit(solution)/shard_map/ppermute | solution.py:505
  62.1 9.5 %collective-permute-start.15 = (bf16[512,128]{1,0:T(8,128)(2,1)S(1)}, bf16[512,128]{1,0:T(8,128)(2,1)S(1)}, u32[]{:S(2)}, u32[]{:S(2)}) collective-permute-start(bf16[512,128]{1,0:T(8,128)(2,1)S(1)} %get-tuple-element.88), channel_id=1, source_target_pairs={{0,12},{4,8},{8,4},{12,0},{1,13},{5,9},{9,5},{13,1},{2,14},{6,10},... | collective-permute-start | bytes 393224 | tf_op jit(solution)/shard_map/ppermute | solution.py:505
  62.2 15.7 %collective-permute-start.26 = (bf16[512,128]{1,0:T(8,128)(2,1)S(1)}, bf16[512,128]{1,0:T(8,128)(2,1)S(1)}, u32[]{:S(2)}, u32[]{:S(2)}) collective-permute-start(bf16[512,128]{1,0:T(8,128)(2,1)S(1)} %get-tuple-element.98), channel_id=1, source_target_pairs={{0,4},{4,0},{8,12},{12,8},{1,5},{5,1},{9,13},{13,9},{2,6},{6,2},{1... | collective-permute-start | bytes 393224 | tf_op jit(solution)/shard_map/ppermute | solution.py:505
  62.4 35.0 %copy-start = (bf16[1024,1024]{1,0:T(8,128)(2,1)S(1)}, bf16[1024,1024]{1,0:T(8,128)(2,1)}, u32[]{:S(2)}) copy-start(bf16[1024,1024]{1,0:T(8,128)(2,1)} %refs_18_.3) | copy-start | bytes 6291460
  62.5 35.0 %copy-start.1 = (bf16[1024,1024]{1,0:T(8,128)(2,1)S(1)}, bf16[1024,1024]{1,0:T(8,128)(2,1)}, u32[]{:S(2)}) copy-start(bf16[1024,1024]{1,0:T(8,128)(2,1)} %refs_16_.3) | copy-start | bytes 6291460
  62.5 35.0 %copy-start.2 = (bf16[1024,1024]{1,0:T(8,128)(2,1)S(1)}, bf16[1024,1024]{1,0:T(8,128)(2,1)}, u32[]{:S(2)}) copy-start(bf16[1024,1024]{1,0:T(8,128)(2,1)} %refs_17_.3) | copy-start | bytes 6291460
  71.5 19.7 %collective-permute-start.16 = (bf16[1024,128]{1,0:T(8,128)(2,1)S(1)}, bf16[1024,128]{1,0:T(8,128)(2,1)S(1)}, u32[]{:S(2)}, u32[]{:S(2)}) collective-permute-start(bf16[1024,128]{1,0:T(8,128)(2,1)S(1)} %get-tuple-element.89), channel_id=1, source_target_pairs={{0,8},{4,12},{8,0},{12,4},{1,9},{5,13},{9,1},{13,5},{2,10},{6,14},... | collective-permute-start | bytes 786440 | tf_op jit(solution)/shard_map/ppermute | solution.py:505
  74.8 20.2 %collective-permute-start.17 = (bf16[1024,128]{1,0:T(8,128)(2,1)S(1)}, bf16[1024,128]{1,0:T(8,128)(2,1)S(1)}, u32[]{:S(2)}, u32[]{:S(2)}) collective-permute-start(bf16[1024,128]{1,0:T(8,128)(2,1)S(1)} %get-tuple-element.90), channel_id=1, source_target_pairs={{0,12},{4,8},{8,4},{12,0},{1,13},{5,9},{9,5},{13,1},{2,14},{6,10},... | collective-permute-start | bytes 786440 | tf_op jit(solution)/shard_map/ppermute | solution.py:505
  76.7 18.3 %collective-permute-start.21 = (bf16[1024,128]{1,0:T(8,128)(2,1)S(1)}, bf16[1024,128]{1,0:T(8,128)(2,1)S(1)}, u32[]{:S(2)}, u32[]{:S(2)}) collective-permute-start(bf16[1024,128]{1,0:T(8,128)(2,1)S(1)} %get-tuple-element.96), channel_id=1, source_target_pairs={{0,4},{4,0},{8,12},{12,8},{1,5},{5,1},{9,13},{13,9},{2,6},{6,2},{1... | collective-permute-start | bytes 786440 | tf_op jit(solution)/shard_map/ppermute | solution.py:505
  76.7 2.2 %collective-permute-start.27 = (bf16[512,128]{1,0:T(8,128)(2,1)S(1)}, bf16[512,128]{1,0:T(8,128)(2,1)S(1)}, u32[]{:S(2)}, u32[]{:S(2)}) collective-permute-start(bf16[512,128]{1,0:T(8,128)(2,1)S(1)} %get-tuple-element.97.refs_8_), channel_id=1, source_target_pairs={{0,1},{1,0},{2,3},{3,2},{4,5},{5,4},{6,7},{7,6},{8,9},{9,8},{10,11... | collective-permute-start | bytes 393224 | tf_op jit(solution)/shard_map/ppermute | solution.py:511
  77.9 1.3 %collective-permute-start.29 = (bf16[512,128]{1,0:T(8,128)(2,1)S(1)}, bf16[512,128]{1,0:T(8,128)(2,1)S(1)}, u32[]{:S(2)}, u32[]{:S(2)}) collective-permute-start(bf16[512,128]{1,0:T(8,128)(2,1)S(1)} %collective-permute-done.14.refs_10_), channel_id=1, source_target_pairs={{0,1},{1,0},{2,3},{3,2},{4,5},{5,4},{6,7},{7,6},{8,9},{9,8},{10,11... | collective-permute-start | bytes 393224 | tf_op jit(solution)/shard_map/ppermute | solution.py:511
  78.9 16.6 %collective-permute-start.30 = (bf16[512,128]{1,0:T(8,128)(2,1)S(1)}, bf16[512,128]{1,0:T(8,128)(2,1)S(1)}, u32[]{:S(2)}, u32[]{:S(2)}) collective-permute-start(bf16[512,128]{1,0:T(8,128)(2,1)S(1)} %collective-permute-done.15.refs_11_), channel_id=1, source_target_pairs={{0,1},{1,0},{2,3},{3,2},{4,5},{5,4},{6,7},{7,6},{8,9},{9,8},{10,11... | collective-permute-start | bytes 393224 | tf_op jit(solution)/shard_map/ppermute | solution.py:511
  79.3 18.2 %collective-permute-start.22 = (bf16[1024,128]{1,0:T(8,128)(2,1)S(1)}, bf16[1024,128]{1,0:T(8,128)(2,1)S(1)}, u32[]{:S(2)}, u32[]{:S(2)}) collective-permute-start(bf16[1024,128]{1,0:T(8,128)(2,1)S(1)} %get-tuple-element.95.refs_0_), channel_id=1, source_target_pairs={{0,1},{1,0},{2,3},{3,2},{4,5},{5,4},{6,7},{7,6},{8,9},{9,8},{10,11... | collective-permute-start | bytes 786440 | tf_op jit(solution)/shard_map/ppermute | solution.py:511
  91.3 6.2 %collective-permute-start.24 = (bf16[1024,128]{1,0:T(8,128)(2,1)S(1)}, bf16[1024,128]{1,0:T(8,128)(2,1)S(1)}, u32[]{:S(2)}, u32[]{:S(2)}) collective-permute-start(bf16[1024,128]{1,0:T(8,128)(2,1)S(1)} %collective-permute-done.16.refs_2_), channel_id=1, source_target_pairs={{0,1},{1,0},{2,3},{3,2},{4,5},{5,4},{6,7},{7,6},{8,9},{9,8},{10,11... | collective-permute-start | bytes 786440 | tf_op jit(solution)/shard_map/ppermute | solution.py:511
  95.0 2.5 %collective-permute-start.25 = (bf16[1024,128]{1,0:T(8,128)(2,1)S(1)}, bf16[1024,128]{1,0:T(8,128)(2,1)S(1)}, u32[]{:S(2)}, u32[]{:S(2)}) collective-permute-start(bf16[1024,128]{1,0:T(8,128)(2,1)S(1)} %collective-permute-done.17.refs_3_), channel_id=1, source_target_pairs={{0,1},{1,0},{2,3},{3,2},{4,5},{5,4},{6,7},{7,6},{8,9},{9,8},{10,11... | collective-permute-start | bytes 786440 | tf_op jit(solution)/shard_map/ppermute | solution.py:511
  95.0 2.5 %collective-permute-start.23 = (bf16[1024,128]{1,0:T(8,128)(2,1)S(1)}, bf16[1024,128]{1,0:T(8,128)(2,1)S(1)}, u32[]{:S(2)}, u32[]{:S(2)}) collective-permute-start(bf16[1024,128]{1,0:T(8,128)(2,1)S(1)} %collective-permute-done.21.refs_1_), channel_id=1, source_target_pairs={{0,1},{1,0},{2,3},{3,2},{4,5},{5,4},{6,7},{7,6},{8,9},{9,8},{10,11... | collective-permute-start | bytes 786440 | tf_op jit(solution)/shard_map/ppermute | solution.py:511
  95.5 1.6 %collective-permute-start.28 = (bf16[512,128]{1,0:T(8,128)(2,1)S(1)}, bf16[512,128]{1,0:T(8,128)(2,1)S(1)}, u32[]{:S(2)}, u32[]{:S(2)}) collective-permute-start(bf16[512,128]{1,0:T(8,128)(2,1)S(1)} %collective-permute-done.26.refs_9_), channel_id=1, source_target_pairs={{0,1},{1,0},{2,3},{3,2},{4,5},{5,4},{6,7},{7,6},{8,9},{9,8},{10,11... | collective-permute-start | bytes 393224 | tf_op jit(solution)/shard_map/ppermute | solution.py:511
  97.1 9.9 %collective-permute-start.13 = (bf16[4,288,128]{2,1,0:T(8,128)(2,1)S(1)}, bf16[4,288,128]{2,1,0:T(8,128)(2,1)S(1)}, u32[]{:S(2)}, u32[]{:S(2)}) collective-permute-start(bf16[4,288,128]{2,1,0:T(8,128)(2,1)S(1)} %get-tuple-element.78), channel_id=1, source_target_pairs={{0,1},{1,0},{2,3},{3,2},{4,5},{5,4},{6,7},{7,6},{8,9},{9,8},{10,11... | collective-permute-start | bytes 884744 | tf_op jit(solution)/shard_map/ppermute | solution.py:511
  100.4 23.4 %collective-permute-start.31 = (bf16[256,1024]{1,0:T(8,128)(2,1)S(1)}, bf16[256,1024]{1,0:T(8,128)(2,1)S(1)}, u32[]{:S(2)}, u32[]{:S(2)}) collective-permute-start(bf16[256,1024]{1,0:T(8,128)(2,1)S(1)} %shard_map.103), channel_id=1, source_target_pairs={{0,1},{1,3},{3,2},{2,0},{4,5},{5,7},{7,6},{6,4},{8,9},{9,11},{11,1... | collective-permute-start | bytes 1572872 | tf_op jit(solution)/shard_map/ppermute | solution.py:620
  104.5 20.8 %collective-permute-start.32 = (bf16[256,1024]{1,0:T(8,128)(2,1)S(1)}, bf16[256,1024]{1,0:T(8,128)(2,1)S(1)}, u32[]{:S(2)}, u32[]{:S(2)}) collective-permute-start(bf16[256,1024]{1,0:T(8,128)(2,1)S(1)} %shard_map.105.kept_ref), channel_id=1, source_target_pairs={{1,2},{2,1},{5,6},{6,5},{9,10},{10,9},{13,14},{14,13},{17,18},{18,... | collective-permute-start | bytes 1572872 | tf_op jit(solution)/shard_map/ppermute | solution.py:622
  107.6 8.2 %collective-permute-start.18 = (bf16[576,128]{1,0:T(8,128)(2,1)S(1)}, bf16[576,128]{1,0:T(8,128)(2,1)S(1)}, u32[]{:S(2)}, u32[]{:S(2)}) collective-permute-start(bf16[576,128]{1,0:T(8,128)(2,1)S(1)} %get-tuple-element.92), channel_id=1, source_target_pairs={{0,4},{4,0},{8,12},{12,8},{1,5},{5,1},{9,13},{13,9},{2,6},{6,2},{1... | collective-permute-start | bytes 442376 | tf_op jit(solution)/shard_map/ppermute | solution.py:505
  111.6 12.2 %collective-permute-start.19 = (bf16[576,128]{1,0:T(8,128)(2,1)S(1)}, bf16[576,128]{1,0:T(8,128)(2,1)S(1)}, u32[]{:S(2)}, u32[]{:S(2)}) collective-permute-start(bf16[576,128]{1,0:T(8,128)(2,1)S(1)} %get-tuple-element.93), channel_id=1, source_target_pairs={{0,8},{4,12},{8,0},{12,4},{1,9},{5,13},{9,1},{13,5},{2,10},{6,14},... | collective-permute-start | bytes 442376 | tf_op jit(solution)/shard_map/ppermute | solution.py:505
  112.6 11.3 %collective-permute-start.20 = (bf16[576,128]{1,0:T(8,128)(2,1)S(1)}, bf16[576,128]{1,0:T(8,128)(2,1)S(1)}, u32[]{:S(2)}, u32[]{:S(2)}) collective-permute-start(bf16[576,128]{1,0:T(8,128)(2,1)S(1)} %get-tuple-element.94), channel_id=1, source_target_pairs={{0,12},{4,8},{8,4},{12,0},{1,13},{5,9},{9,5},{13,1},{2,14},{6,10},... | collective-permute-start | bytes 442376 | tf_op jit(solution)/shard_map/ppermute | solution.py:505

commit v9 on v8

--- a/solution.py
+++ b/solution.py
@@ -197,20 +197,41 @@
     return -(-(rows // head_dim) // 16) * 16
 
 
-def pack_kernel(place_ref, grads_ref, assign_ref, mine_ref, theirs_ref):
+def open_kernel(place_ref, grads_ref, assign_ref, *refs):
+    weights, (held_ref, mine_ref, theirs_ref, ids_ref, sems, id_sem) = refs[:3], refs[3:]
     chips, padded, head_dim = mine_ref.shape
     rows = grads_ref.shape[0]
     spare = padded - rows - rows // head_dim
+    ids_copy = pltpu.make_async_copy(assign_ref, ids_ref, id_sem.at[0])
+    ids_copy.start()
+    copies = []
     for turn, out_ref in enumerate((mine_ref, theirs_ref)):
         for chip in range(chips):
             head = (place_ref[1] ^ turn) * chips + chip
             at = pl.multiple_of(head * head_dim, head_dim)
-            out_ref[chip, :rows, :] = grads_ref[:, pl.ds(at, head_dim)]
-            ids = assign_ref[pl.ds(head, 1), :].astype(jnp.float32)
+            copies.append((grads_ref.at[:, pl.ds(at, head_dim)], out_ref.at[chip, pl.ds(0, rows)]))
+    chunk = held_ref.shape[1] // 4
+    for index, weight in enumerate(weights):
+        for part in range(4):
+            at = pl.ds(part * chunk, chunk)
+            copies.append((weight.at[at], held_ref.at[index, at]))
+    copies = [
+        pltpu.make_async_copy(source, target, sems.at[index])
+        for index, (source, target) in enumerate(copies)
+    ]
+    for copy in copies:
+        copy.start()
+    ids_copy.wait()
+    for turn, out_ref in enumerate((mine_ref, theirs_ref)):
+        for chip in range(chips):
+            head = (place_ref[1] ^ turn) * chips + chip
+            ids = ids_ref[pl.ds(head, 1), :].astype(jnp.float32)
             lines = [
                 ids[:, start : start + head_dim] for start in range(0, rows, head_dim)
             ] + [jnp.zeros((spare, head_dim), jnp.float32)]
             out_ref[chip, rows:, :] = jnp.concatenate(lines, axis=0).astype(jnp.bfloat16)
+    for copy in copies:
+        copy.wait()
 
 
 def merge_kernel(place_ref, mine_ref, theirs_ref, *out_refs):
@@ -221,55 +242,52 @@
             out_ref[at, :] = held_ref[place_ref[0] ^ offset]
 
 
-def fetch_columns(half, weights, held_ref, sems):
-    chunks = sems.shape[1]
-    columns = held_ref.shape[2]
-    rows = held_ref.shape[1] // chunks
-    at = pl.ds(pl.multiple_of(half * columns, columns), columns)
-    copies = []
-    for index, weight in enumerate(weights):
-        for chunk in range(chunks):
-            lines = pl.ds(chunk * rows, rows)
-            copy = pltpu.make_async_copy(
-                weight.at[lines, at], held_ref.at[index, lines], sems.at[index, chunk]
-            )
-            copy.start()
-            copies.append(copy)
-    return copies
-
-
-def project_kernel(count, turn, place_ref, *refs):
-    if turn == 0:
-        arrived_ref, refs = refs[0], refs[1:]
-    tokens, weights, refs = refs[:2], refs[2 : 2 + count], refs[2 + count :]
-    out_refs, (joined_ref, held_ref, low_ref, sems, token_sems) = refs[:-5], refs[-5:]
+def project(indices, turn, place_ref, joined_ref, held_ref, finish):
+    columns = held_ref.shape[2] // 2
+    at = pl.ds(pl.multiple_of((place_ref[1] ^ turn) * columns, columns), columns)
+    for slot, index in enumerate(indices):
+        finish(
+            slot,
+            jnp.dot(joined_ref[...], held_ref[index, :, at], preferred_element_type=jnp.float32),
+        )
+
+
+def sibling_kernel(indices, place_ref, joined_ref, held_ref, out_ref):
+    def finish(slot, total):
+        out_ref[slot] = total.astype(jnp.bfloat16)
+
+    project(indices, 1, place_ref, joined_ref, held_ref, finish)
+
+
+def first_kernel(indices, place_ref, held_ref, mine_ref, theirs_ref, out_ref, joined_ref, sems):
     side = place_ref[1]
     tall, depth = joined_ref.shape
     rows = tall // 2
     near = pl.ds(pl.multiple_of(side * depth, depth), depth)
-    joins = []
-    for core, source in enumerate(tokens):
+    copies = []
+    for core, source in enumerate((mine_ref, theirs_ref)):
         at = pl.ds(pl.multiple_of((side ^ core) * rows, rows), rows)
-        joins.append(
-            pltpu.make_async_copy(source.at[:, near], joined_ref.at[at], token_sems.at[core])
-        )
-        joins[core].start()
-    copies = fetch_columns(side ^ turn, weights, held_ref, sems)
-    for copy in joins:
+        copies.append(
+            pltpu.make_async_copy(source.at[:, near], joined_ref.at[at], sems.at[core])
+        )
+        copies[core].start()
+    for copy in copies:
         copy.wait()
-    chunks = sems.shape[1]
-    for index in range(count):
-        for chunk in range(chunks):
-            copies[index * chunks + chunk].wait()
-        total = jnp.dot(joined_ref[...], held_ref[index], preferred_element_type=jnp.float32)
-        if turn == 1:
-            out_refs[0][index] = total.astype(jnp.bfloat16)
-            continue
-        low_ref[...] = (total + arrived_ref[index].astype(jnp.float32)).astype(jnp.bfloat16)
+    sibling_kernel(indices, place_ref, joined_ref, held_ref, out_ref)
+
+
+def own_kernel(indices, place_ref, joined_ref, held_ref, arrived_ref, *refs):
+    out_refs, low_ref = refs[:-1], refs[-1]
+    tall = joined_ref.shape[0]
+
+    def finish(slot, total):
+        low_ref[...] = (total + arrived_ref[slot].astype(jnp.float32)).astype(jnp.bfloat16)
         for offset, out_ref in enumerate(out_refs):
             head_dim = out_ref.shape[1]
             at = pl.multiple_of((place_ref[0] ^ offset) * head_dim, head_dim)
-            out_ref[index * tall : (index + 1) * tall, :] = low_ref[:, pl.ds(at, head_dim)]
+            out_ref[slot * tall : (slot + 1) * tall, :] = low_ref[:, pl.ds(at, head_dim)]
+
+    project(indices, 0, place_ref, joined_ref, held_ref, finish)
 
 
 def in_order(place, parts, start, ordered):
@@ -416,8 +434,8 @@
 
 
 def input_kernel(chips, which, place_ref, *refs):
-    weights, (out_ref, gathered_ref) = refs[4 * chips : -2], refs[-2:]
-    rows, width = out_ref.shape[0], weights[0].shape[1]
+    held_ref, out_ref, gathered_ref = refs[4 * chips :]
+    rows, width = out_ref.shape[0], held_ref.shape[2]
     head_dim = width // (2 * chips)
     for turn in range(2):
         parts = refs[turn * chips : (turn + 1) * chips]
@@ -432,7 +450,7 @@
     flipped = None
     for index in range(3):
         term = lax.dot_general(
-            weights[index][...],
+            held_ref[index],
             gathered_ref[:, index * width : (index + 1) * width],
             contract_last,
             preferred_element_type=jnp.float32,
@@ -476,7 +494,6 @@
     vmem = pl.BlockSpec(memory_space=pltpu.VMEM)
     anywhere = pl.BlockSpec(memory_space=pl.ANY)
     params = pltpu.CompilerParams(vmem_limit_bytes=32 * mebi)
-    project_params = pltpu.CompilerParams(vmem_limit_bytes=32 * mebi)
     swap = [(0, 1), (1, 0)]
     chip, side, column = (lax.axis_index(name) for name in ("seq", "sub", "head"))
     place = jnp.stack([chip, side, column, 1 - column])
@@ -510,50 +527,63 @@
     def to_sibling(piece):
         return lax.ppermute(piece, "sub", swap)
 
+    def stay(array):
+        return pltpu.with_memory_space_constraint(array, pltpu.HBM)
+
     hidden_other = to_sibling(hidden)
     block = low(chips, rows + id_lines(rows, head_dim), head_dim)
-    grads_mine, grads_theirs = call(pack_kernel, (block, block), place, d_attended, assign)
+    weights, grads_mine, grads_theirs = call(
+        open_kernel,
+        (pltpu.VMEM((3, half, width), jnp.bfloat16), block, block),
+        place,
+        stay(d_attended),
+        stay(assign),
+        *(stay(weight) for weight in (w_query, w_key, w_value)),
+        scratch=[
+            pltpu.VMEM(assign.shape, jnp.int32),
+            pltpu.SemaphoreType.DMA((count + 12,)),
+            pltpu.SemaphoreType.DMA((1,)),
+        ],
+        hbm=5,
+    )
     grads_other = to_sibling(grads_theirs)
-
-    def stay(array):
-        return pltpu.with_memory_space_constraint(array, pltpu.HBM)
-
-    def project(turn, weights, *arrived):
-        number = len(weights)
-        outs = buffers(2 * number * rows) if turn == 0 else low(number, 2 * rows, width // 2)
-
-        return call(
-            partial(project_kernel, number, turn),
-            outs,
-            place,
-            *arrived,
-            stay(hidden),
-            hidden_other,
-            *(stay(weight) for weight in weights),
-            scratch=[
-                pltpu.VMEM((2 * rows, half), jnp.bfloat16),
-                pltpu.VMEM((number, half, width // 2), jnp.bfloat16),
-                pltpu.VMEM((2 * rows, width // 2), jnp.bfloat16),
-                pltpu.SemaphoreType.DMA((number, 4)),
-                pltpu.SemaphoreType.DMA((2,)),
-            ],
-            hbm=2 + number,
-            limits=project_params,
-            takes=(8 if number == 2 else 0.1) if turn == 0 else 0.1,
-        )
-
     merged = call(merge_kernel, buffers(2 * block.shape[1]), place, grads_mine, grads_other)
     grads = exchange(merged)
-    hidden_other, _ = lax.optimization_barrier((hidden_other, merged[0]))
-    early, late = (w_query, w_key), (w_value,)
-    early_arrived = to_sibling(project(1, early))
-    late_arrived = to_sibling(project(1, late))
-    grads = exchange(call(merge_kernel, buffers(2 * block.shape[1]), place, grads_mine, grads_other))
-    early_arrived, _ = lax.optimization_barrier((early_arrived, grads[0]))
-    early_projected = project(0, early, early_arrived)
+    early_part, joined = call(
+        partial(first_kernel, (0, 1)),
+        (low(2, 2 * rows, width // 2), low(2 * rows, half)),
+        place,
+        weights,
+        stay(hidden),
+        hidden_other,
+        scratch=[pltpu.SemaphoreType.DMA((2,))],
+        hbm=2,
+        takes=0.1,
+    )
+    late_part = call(
+        partial(sibling_kernel, (2,)), low(1, 2 * rows, width // 2), place, joined, weights, takes=0.1
+    )
+    early_arrived, late_arrived = to_sibling(early_part), to_sibling(late_part)
+
+    def own_heads(indices, arrived, takes):
+        return call(
+            partial(own_kernel, indices),
+            buffers(2 * len(indices) * rows),
+            place,
+            joined,
+            weights,
+            arrived,
+            scratch=[pltpu.VMEM((2 * rows, width // 2), jnp.bfloat16)],
+            takes=takes,
+        )
+
+    early_arrived, _ = lax.optimization_barrier((early_arrived, merged[0]))
+    early_projected = own_heads((0, 1), early_arrived, 8)
     packed = exchange(early_projected)
-    late_arrived, _, _ = lax.optimization_barrier((late_arrived, early_projected[0], (grads[2], grads[3])))
-    late_projected = project(0, late, late_arrived)
+    late_arrived, *_ = lax.optimization_barrier(
+        (late_arrived, early_projected[0], grads[2], grads[3])
+    )
+    late_projected = own_heads((2,), late_arrived, 0.1)
     valued = exchange(late_projected)
     packed = lax.optimization_barrier((*packed, late_projected[0]))[:chips]
 
@@ -608,28 +638,25 @@
             *back_other,
             *value_back,
             *value_other,
-            w_query,
-            w_key,
-            w_value,
+            weights,
             scratch=[pltpu.VMEM((rows, 3 * width), jnp.bfloat16)],
-            takes=3,
-        )
-
+        )
+
+    *outputs, _, _ = lax.optimization_barrier((*outputs, back[2], back[3]))
+    returned = exchange(outputs)
     square = ("head", "sub")
     crossing = input_part(3, place)
     first = lax.ppermute(crossing, square, [(0, 1), (1, 3), (3, 2), (2, 0)])
     kept = input_part(2, lax.optimization_barrier((place, crossing))[0])
     second = lax.ppermute(kept, square, [(1, 2), (2, 1)])
-    *outputs, _, _ = lax.optimization_barrier((*outputs, back[2], back[3]))
-    returned = exchange(outputs)
-    *returned, _ = lax.optimization_barrier((*returned, first))
     attended, centroid_sums = call(
         partial(attended_kernel, chips),
         (low(rows, width), jax.ShapeDtypeStruct((count, owned, head_dim), jnp.float32)),
         place,
         *returned,
-    )
-    first, _ = lax.optimization_barrier((first, attended))
+        takes=8,
+    )
+    first, second, _ = lax.optimization_barrier((first, second, attended))
     d_hidden = call(sum_kernel, low(rows, half), place, first, second, kept)
     return (attended, d_hidden, centroid_sums)
 

time: 127 us -> 127 us (level)
  starting transfers between devices: 49 us -> 70.6 us
  waiting for transfers between devices: 37.5 us -> 20.1 us
  Pallas kernels: 37.7 us -> 35.6 us
  local copies, waits for them, and re-layouts: 1.76 us -> 0.01 us
    ppermute x18, waiting for transfers between devices: 33.8 us -> 9.45 us  [exchange(): lax.ppermute(parts[offset], 'seq', [(at, at ^ offset) for at in range(chi...]
    ppermute x18, starting transfers between devices: 36.8 us -> 50.2 us  [exchange(): lax.ppermute(parts[offset], 'seq', [(at, at ^ offset) for at in range(chi...]
    ppermute x13, starting transfers between devices: 8.52 us -> 15.9 us  [to_sibling(): return lax.ppermute(piece, 'sub', swap)]
    ppermute x1, waiting for transfers between devices: 0.01 us -> 6.1 us  [by_head(): second = lax.ppermute(kept, square, [(1, 2), (2, 1)])]
    pallas_call x13, Pallas kernels: 37.7 us -> 35.6 us  [call(): pl.pallas_call(kernel, out_shape=outs, in_specs=[smem] + [vmem] * (len(op...]
    unnamed x12 -> x2, local copies, waits for them, and re-layouts: 1.76 us -> 0.01 us
  transfers between devices with their start and end apart: 33 -> 33, of which waited for: 8 -> 7; matrix products, arithmetic and copies ran while one was open for 0% -> 0% of each run, Pallas kernels for 26% -> 25%
where the time goes in v9:
time: 127 us
  starting transfers between devices  70.6 us (56%)
  Pallas kernels  35.6 us (28%)
  waiting for transfers between devices  20.1 us (16%)
    ppermute x18, starting transfers between devices, exchange(): lax.ppermute(parts[offset], 'seq', [(at, at ^ offset) for at in range(chi...  50.2 us
    pallas_call x13, Pallas kernels, call(): pl.pallas_call(kernel, out_shape=outs, in_specs=[smem] + [vmem] * (len(op...  35.6 us
    ppermute x13, starting transfers between devices, to_sibling(): return lax.ppermute(piece, 'sub', swap)  15.9 us
    ppermute x18, waiting for transfers between devices, exchange(): lax.ppermute(parts[offset], 'seq', [(at, at ^ offset) for at in range(chi...  9.45 us
    ppermute x1, waiting for transfers between devices, by_head(): second = lax.ppermute(kept, square, [(1, 2), (2, 1)])  6.1 us
    ppermute x13, waiting for transfers between devices, to_sibling(): return lax.ppermute(piece, 'sub', swap)  4.57 us
    ppermute x1, starting transfers between devices, by_head(): second = lax.ppermute(kept, square, [(1, 2), (2, 1)])  3.26 us
  transfers between devices with their start and end apart: 33, of which 7 were waited for; matrix products, arithmetic and copies ran while one was open for 0% of the time, Pallas kernels for 25%

profile of v9, /device:TPU:1, one launch (start us, length us, event | category | flops | bytes accessed | tf_op | source)
XLA Modules:
  0.0 127.2 jit_solution(3593141731780828381)
XLA Ops:
  0.6 0.1 collective-permute-start
  0.8 0.1 pad_add_fusion.place_ref
  0.8 3.8 %shard_map.94 = (bf16[3,1024,1024]{2,1,0:T(8,128)(2,1)S(1)}, bf16[4,272,128]{2,1,0:T(8,128)(2,1)S(1)}, bf16[4,272,128]{2,1,0:T(8,128)(2,1)S(1)}) custom-call(s32[4]{0:T(128)S(1)} %pad_add_fusion.place_ref, bf16[256,1024]{1,0:T(8,128)(2,1)} %grads_ref.1, s32[8,256]{1,0:T(8,128)} %assign_ref.1, bf16[1024,1024]{1,0:T(8,128)(2,1)} %refs_0_.1, ...), custom_call_target="tpu_custom_call" | custom-call | flops 1150000000 | bytes 1048576 | tf_op jit(solution)/shard_map/pallas_call | solution.py:502
  4.6 2.9 %shard_map.95 = (bf16[2,512,512]{2,1,0:T(8,128)(2,1)S(1)}, bf16[512,1024]{1,0:T(8,128)(2,1)S(1)}) custom-call(s32[4]{0:T(128)S(1)} %pad_add_fusion.place_ref, bf16[3,1024,1024]{2,1,0:T(8,128)(2,1)S(1)} %get-tuple-element.54.held_ref.refs_16_, bf16[256,2048]{1,0:T(8,128)(2,1)} %mine_ref.1, bf16[256,2048]{1,0:T(8,128)(2,1)S(1)} %collective-permute-done.theirs_ref), custom_call_target="tpu_custom_call" | custom-call | flops 115000000 | bytes 1048576 | tf_op jit(solution)/shard_map/pallas_call | solution.py:502
  7.5 0.5 collective-permute-start.1
  8.0 0.1 collective-permute-start.2
  8.1 2.6 %collective-permute-done.2.theirs_ref = bf16[4,272,128]{2,1,0:T(8,128)(2,1)S(1)} collective-permute-done((bf16[4,272,128]{2,1,0:T(8,128)(2,1)S(1)}, bf16[4,272,128]{2,1,0:T(8,128)(2,1)S(1)}, u32[]{:S(2)}, u32[]{:S(2)}) %collective-permute-start.2) | collective-permute-done | bytes 278560 | tf_op jit(solution)/shard_map/ppermute | solution.py:528
  10.7 0.6 shard_map.96
  11.3 3.7 %collective-permute-start.7 = (bf16[544,128]{1,0:T(8,128)(2,1)S(1)}, bf16[544,128]{1,0:T(8,128)(2,1)S(1)}, u32[]{:S(2)}, u32[]{:S(2)}) collective-permute-start(bf16[544,128]{1,0:T(8,128)(2,1)S(1)} %get-tuple-element.65), channel_id=1, source_target_pairs={{0,8},{4,12},{8,0},{12,4},{1,9},{5,13},{9,1},{13,5},{2,10},{6,14},... | collective-permute-start | bytes 417800 | tf_op jit(solution)/shard_map/ppermute | solution.py:522
  15.0 1.1 collective-permute-start.8
  16.1 1.3 shard_map.98
  17.4 0.8 collective-permute-start.6
  18.1 0.0 collective-permute-done.1.arrived_ref
  18.2 2.0 %shard_map.97 = (bf16[1024,128]{1,0:T(8,128)(2,1)S(1)}, bf16[1024,128]{1,0:T(8,128)(2,1)S(1)}, bf16[1024,128]{1,0:T(8,128)(2,1)S(1)}, bf16[1024,128]{1,0:T(8,128)(2,1)S(1)}) custom-call(s32[4]{0:T(128)S(1)} %pad_add_fusion.place_ref, bf16[512,1024]{1,0:T(8,128)(2,1)S(1)} %get-tuple-element.55.joined_ref, ...), custom_call_target="tpu_custom_call" | custom-call | flops 9200000000 | bytes 1048576 | tf_op jit(solution)/shard_map/pallas_call | solution.py:502
  20.1 0.1 collective-permute-start.3
  20.2 2.5 %collective-permute-start.4 = (bf16[1024,128]{1,0:T(8,128)(2,1)S(1)}, bf16[1024,128]{1,0:T(8,128)(2,1)S(1)}, u32[]{:S(2)}, u32[]{:S(2)}) collective-permute-start(bf16[1024,128]{1,0:T(8,128)(2,1)S(1)} %get-tuple-element.63), channel_id=1, source_target_pairs={{0,8},{4,12},{8,0},{12,4},{1,9},{5,13},{9,1},{13,5},{2,10},{6,14},... | collective-permute-start | bytes 786440 | tf_op jit(solution)/shard_map/ppermute | solution.py:522
  22.7 2.3 %collective-permute-done.7.refs_6_.refs_10_ = bf16[544,128]{1,0:T(8,128)(2,1)S(1)} collective-permute-done((bf16[544,128]{1,0:T(8,128)(2,1)S(1)}, bf16[544,128]{1,0:T(8,128)(2,1)S(1)}, u32[]{:S(2)}, u32[]{:S(2)}) %collective-permute-start.7) | collective-permute-done | bytes 139296 | tf_op jit(solution)/shard_map/ppermute | solution.py:522
  25.0 3.5 %collective-permute-start.5 = (bf16[1024,128]{1,0:T(8,128)(2,1)S(1)}, bf16[1024,128]{1,0:T(8,128)(2,1)S(1)}, u32[]{:S(2)}, u32[]{:S(2)}) collective-permute-start(bf16[1024,128]{1,0:T(8,128)(2,1)S(1)} %get-tuple-element.64), channel_id=1, source_target_pairs={{0,12},{4,8},{8,4},{12,0},{1,13},{5,9},{9,5},{13,1},{2,14},{6,10},... | collective-permute-start | bytes 786440 | tf_op jit(solution)/shard_map/ppermute | solution.py:522
  28.5 0.0 collective-permute-done.8.refs_7_.refs_11_
  28.5 0.5 collective-permute-start.12
  29.0 0.0 collective-permute-done.6.arrived_ref
  29.0 1.3 %shard_map.99 = (bf16[512,128]{1,0:T(8,128)(2,1)S(1)}, bf16[512,128]{1,0:T(8,128)(2,1)S(1)}, bf16[512,128]{1,0:T(8,128)(2,1)S(1)}, bf16[512,128]{1,0:T(8,128)(2,1)S(1)}) custom-call(s32[4]{0:T(128)S(1)} %pad_add_fusion.place_ref, bf16[512,1024]{1,0:T(8,128)(2,1)S(1)} %get-tuple-element.55.joined_ref, ...), custom_call_target="tpu_custom_call" | custom-call | flops 115000000 | bytes 1048576 | tf_op jit(solution)/shard_map/pallas_call | solution.py:502
  30.4 12.6 %collective-permute-start.10 = (bf16[512,128]{1,0:T(8,128)(2,1)S(1)}, bf16[512,128]{1,0:T(8,128)(2,1)S(1)}, u32[]{:S(2)}, u32[]{:S(2)}) collective-permute-start(bf16[512,128]{1,0:T(8,128)(2,1)S(1)} %get-tuple-element.74), channel_id=1, source_target_pairs={{0,8},{4,12},{8,0},{12,4},{1,9},{5,13},{9,1},{13,5},{2,10},{6,14},... | collective-permute-start | bytes 393224 | tf_op jit(solution)/shard_map/ppermute | solution.py:522
  42.9 0.0 collective-permute-done.3.refs_1_
  42.9 1.3 collective-permute-start.11
  44.2 0.7 collective-permute-done.4.refs_2_
  44.9 6.4 %collective-permute-start.9 = (bf16[512,128]{1,0:T(8,128)(2,1)S(1)}, bf16[512,128]{1,0:T(8,128)(2,1)S(1)}, u32[]{:S(2)}, u32[]{:S(2)}) collective-permute-start(bf16[512,128]{1,0:T(8,128)(2,1)S(1)} %get-tuple-element.73), channel_id=1, source_target_pairs={{0,4},{4,0},{8,12},{12,8},{1,5},{5,1},{9,13},{13,9},{2,6},{6,2},{1... | collective-permute-start | bytes 393224 | tf_op jit(solution)/shard_map/ppermute | solution.py:522
  51.2 0.0 collective-permute-done.5.refs_3_
  51.2 0.0 collective-permute-done.12.refs_5_.refs_9_
  51.2 5.5 %shard_map.100 = (bf16[512,128]{1,0:T(8,128)(2,1)S(1)}, bf16[512,128]{1,0:T(8,128)(2,1)S(1)}, bf16[512,128]{1,0:T(8,128)(2,1)S(1)}, bf16[512,128]{1,0:T(8,128)(2,1)S(1)}, f32[8,256]{1,0:T(8,128)S(1)}) custom-call(s32[4]{0:T(128)S(1)} %pad_add_fusion.place_ref, bf16[1024,128]{1,0:T(8,128)(2,1)S(1)} %get-tuple-element.69.refs_0_, ...), custom_call_target="tpu_custom_call" | custom-call | flops 8049999872 | bytes 1048576 | tf_op jit(solution)/shard_map/pallas_call | solution.py:502
  56.7 7.6 %collective-permute-start.14 = (bf16[512,128]{1,0:T(8,128)(2,1)S(1)}, bf16[512,128]{1,0:T(8,128)(2,1)S(1)}, u32[]{:S(2)}, u32[]{:S(2)}) collective-permute-start(bf16[512,128]{1,0:T(8,128)(2,1)S(1)} %get-tuple-element.88), channel_id=1, source_target_pairs={{0,8},{4,12},{8,0},{12,4},{1,9},{5,13},{9,1},{13,5},{2,10},{6,14},... | collective-permute-start | bytes 393224 | tf_op jit(solution)/shard_map/ppermute | solution.py:522
  64.3 0.2 collective-permute-start.15
  64.5 0.2 collective-permute-start.26
  64.7 0.0 collective-permute-done.11.refs_7_
  64.7 1.1 collective-permute-start.27
  65.7 0.0 collective-permute-done.9.refs_5_
  65.8 9.0 %shard_map.101 = (bf16[1024,128]{1,0:T(8,128)(2,1)S(1)}, bf16[1024,128]{1,0:T(8,128)(2,1)S(1)}, bf16[1024,128]{1,0:T(8,128)(2,1)S(1)}, bf16[1024,128]{1,0:T(8,12...) custom-call(s32[4]{0:T(128)S(1)} %pad_add_fusion.place_ref, ...), custom_call_target="tpu_custom_call" | custom-call | flops 11500000256 | bytes 1048576 | tf_op jit(solution)/shard_map/pallas_call | solution.py:502
  74.7 0.0 collective-permute-done.26.refs_9_
  74.7 1.0 collective-permute-start.28
  75.8 0.0 collective-permute-done.14.refs_10_
  75.8 1.1 collective-permute-start.21
  76.9 1.6 %collective-permute-start.16 = (bf16[1024,128]{1,0:T(8,128)(2,1)S(1)}, bf16[1024,128]{1,0:T(8,128)(2,1)S(1)}, u32[]{:S(2)}, u32[]{:S(2)}) collective-permute-start(bf16[1024,128]{1,0:T(8,128)(2,1)S(1)} %get-tuple-element.90), channel_id=1, source_target_pairs={{0,8},{4,12},{8,0},{12,4},{1,9},{5,13},{9,1},{13,5},{2,10},{6,14},... | collective-permute-start | bytes 786440 | tf_op jit(solution)/shard_map/ppermute | solution.py:522
  78.5 1.1 collective-permute-start.17
  79.6 1.0 collective-permute-start.13
  80.5 0.1 collective-permute-start.29
  80.6 1.3 %collective-permute-done.29.refs_14_ = bf16[512,128]{1,0:T(8,128)(2,1)S(1)} collective-permute-done((bf16[512,128]{1,0:T(8,128)(2,1)S(1)}, bf16[512,128]{1,0:T(8,128)(2,1)S(1)}, u32[]{:S(2)}, u32[]{:S(2)}) %collective-permute-start.29) | collective-permute-done | bytes 131104 | tf_op jit(solution)/shard_map/ppermute | solution.py:528
  81.9 0.4 collective-permute-start.22
  82.3 6.4 %collective-permute-done.21.refs_1_ = bf16[1024,128]{1,0:T(8,128)(2,1)S(1)} collective-permute-done((bf16[1024,128]{1,0:T(8,128)(2,1)S(1)}, bf16[1024,128]{1,0:T(8,128)(2,1)S(1)}, u32[]{:S(2)}, u32[]{:S(2)}) %collective-permute-start.21) | collective-permute-done | bytes 262176 | tf_op jit(solution)/shard_map/ppermute | solution.py:522
  88.8 0.9 collective-permute-start.23
  89.6 9.5 %collective-permute-start.24 = (bf16[1024,128]{1,0:T(8,128)(2,1)S(1)}, bf16[1024,128]{1,0:T(8,128)(2,1)S(1)}, u32[]{:S(2)}, u32[]{:S(2)}) collective-permute-start(bf16[1024,128]{1,0:T(8,128)(2,1)S(1)} %collective-permute-done.16.refs_2_), channel_id=1, source_target_pairs={{0,1},{1,0},{2,3},{3,2},{4,5},{5,4},{6,7},{7,6},{8,9},{9,8},{10,11... | collective-permute-start | bytes 786440 | tf_op jit(solution)/shard_map/ppermute | solution.py:528
  99.2 0.0 collective-permute-start.25
  99.2 0.5 collective-permute-start.30
  99.7 0.6 shard_map.102
  100.3 0.6 collective-permute-done.30.refs_15_
  100.9 4.1 %collective-permute-start.18 = (bf16[576,128]{1,0:T(8,128)(2,1)S(1)}, bf16[576,128]{1,0:T(8,128)(2,1)S(1)}, u32[]{:S(2)}, u32[]{:S(2)}) collective-permute-start(bf16[576,128]{1,0:T(8,128)(2,1)S(1)} %get-tuple-element.93), channel_id=1, source_target_pairs={{0,4},{4,0},{8,12},{12,8},{1,5},{5,1},{9,13},{13,9},{2,6},{6,2},{1... | collective-permute-start | bytes 442376 | tf_op jit(solution)/shard_map/ppermute | solution.py:522
  105.0 1.5 %collective-permute-start.19 = (bf16[576,128]{1,0:T(8,128)(2,1)S(1)}, bf16[576,128]{1,0:T(8,128)(2,1)S(1)}, u32[]{:S(2)}, u32[]{:S(2)}) collective-permute-start(bf16[576,128]{1,0:T(8,128)(2,1)S(1)} %get-tuple-element.94), channel_id=1, source_target_pairs={{0,8},{4,12},{8,0},{12,4},{1,9},{5,13},{9,1},{13,5},{2,10},{6,14},... | collective-permute-start | bytes 442376 | tf_op jit(solution)/shard_map/ppermute | solution.py:522
  106.5 1.2 collective-permute-start.20
  107.8 2.9 %shard_map.104 = bf16[256,1024]{1,0:T(8,128)(2,1)S(1)} custom-call(s32[4]{0:T(128)S(1)} %pad_add_fusion.place_ref, bf16[1024,128]{1,0:T(8,128)(2,1)S(1)} %get-tuple-element.97.refs_0_, bf16[1024,128]{1,0:T(8,128)(2,1)S(1)} %collective-permute-done.21.refs_1_, bf16[1024,128]{1,0:T(8,128)(2,1)S(1)} %collective-permute-done.16.refs_2_, ...), custom_call_target="tpu_custom_call" | custom-call | flops 1150000000 | bytes 1048576 | tf_op jit(solution)/shard_map/pallas_call | solution.py:502
  110.7 1.2 collective-permute-start.31
  111.9 2.9 %shard_map.105.kept_ref = bf16[256,1024]{1,0:T(8,128)(2,1)S(1)} custom-call(s32[4]{0:T(128)S(1)} %pad_add_fusion.place_ref, bf16[1024,128]{1,0:T(8,128)(2,1)S(1)} %get-tuple-element.97.refs_0_, bf16[1024,128]{1,0:T(8,128)(2,1)S(1)} %collective-permute-done.21.refs_1_, bf16[1024,128]{1,0:T(8,128)(2,1)S(1)} %collective-permute-done.16.refs_2_, ...), custom_call_target="tpu_custom_call" | custom-call | flops 1150000000 | bytes 1048576 | tf_op jit(solution)/shard_map/pallas_call | solution.py:502
  114.8 3.3 %collective-permute-start.32 = (bf16[256,1024]{1,0:T(8,128)(2,1)S(1)}, bf16[256,1024]{1,0:T(8,128)(2,1)S(1)}, u32[]{:S(2)}, u32[]{:S(2)}) collective-permute-start(bf16[256,1024]{1,0:T(8,128)(2,1)S(1)} %shard_map.105.kept_ref), channel_id=1, source_target_pairs={{1,2},{2,1},{5,6},{6,5},{9,10},{10,9},{13,14},{14,13},{17,18},{18,... | collective-permute-start | bytes 1572872 | tf_op jit(solution)/shard_map/ppermute | solution.py:651
  118.1 1.5 %shard_map.103 = (bf16[256,1024]{1,0:T(8,128)(2,1)}, f32[8,32,128]{2,1,0:T(8,128)}) custom-call(s32[4]{0:T(128)S(1)} %pad_add_fusion.place_ref, bf16[576,128]{1,0:T(8,128)(2,1)S(1)} %get-tuple-element.92.refs_0_, bf16[576,128]{1,0:T(8,128)(2,1)S(1)} %collective-permute-done.18.refs_1_, bf16[576,128]{1,0:T(8,128)(2,1)S(1)} %collective-permute-done.19.refs_2_, ...), custom_call_target="tpu_custom_call" | custom-call | flops 9200000000 | bytes 1048576 | tf_op jit(solution)/shard_map/pallas_call | solution.py:502
  119.7 6.1 %collective-permute-done.32.second_ref = bf16[256,1024]{1,0:T(8,128)(2,1)S(1)} collective-permute-done((bf16[256,1024]{1,0:T(8,128)(2,1)S(1)}, bf16[256,1024]{1,0:T(8,128)(2,1)S(1)}, u32[]{:S(2)}, u32[]{:S(2)}) %collective-permute-start.32) | collective-permute-done | bytes 524320 | tf_op jit(solution)/shard_map/ppermute | solution.py:651
  125.8 1.5 %shard_map.106 = bf16[256,1024]{1,0:T(8,128)(2,1)} custom-call(s32[4]{0:T(128)S(1)} %pad_add_fusion.place_ref, bf16[256,1024]{1,0:T(8,128)(2,1)S(1)} %collective-permute-done.31.first_ref, bf16[256,1024]{1,0:T(8,128)(2,1)S(1)} %collective-permute-done.32.second_ref, bf16[256,1024]{1,0:T(8,128)(2,1)S(1)} %shard_map.105.kept_ref), custom_call_target="tpu_custom_call" | custom-call | flops 1150000000 | bytes 1048576 | tf_op jit(solution)/shard_map/pallas_call | solution.py:502
  (18 shorter events, 0.0 us)
Async XLA Ops:
  0.6 4.0 %collective-permute-start = (bf16[256,2048]{1,0:T(8,128)(2,1)}, bf16[256,2048]{1,0:T(8,128)(2,1)S(1)}, u32[]{:S(2)}, u32[]{:S(2)}) collective-permute-start(bf16[256,2048]{1,0:T(8,128)(2,1)} %mine_ref.1), channel_id=1, source_target_pairs={{0,1},{1,0},{2,3},{3,2},{4,5},{5,4},{6,7},{7,6},{8,9},{9,8},{10,11... | collective-permute-start | bytes 3145736 | tf_op jit(solution)/shard_map/ppermute | solution.py:528
  7.5 10.6 %collective-permute-start.1 = (bf16[2,512,512]{2,1,0:T(8,128)(2,1)S(1)}, bf16[2,512,512]{2,1,0:T(8,128)(2,1)S(1)}, u32[]{:S(2)}, u32[]{:S(2)}) collective-permute-start(bf16[2,512,512]{2,1,0:T(8,128)(2,1)S(1)} %get-tuple-element.56), channel_id=1, source_target_pairs={{0,1},{1,0},{2,3},{3,2},{4,5},{5,4},{6,7},{7,6},{8,9},{9,8},{10,11... | collective-permute-start | bytes 3145736 | tf_op jit(solution)/shard_map/ppermute | solution.py:528
  8.0 2.7 %collective-permute-start.2 = (bf16[4,272,128]{2,1,0:T(8,128)(2,1)S(1)}, bf16[4,272,128]{2,1,0:T(8,128)(2,1)S(1)}, u32[]{:S(2)}, u32[]{:S(2)}) collective-permute-start(bf16[4,272,128]{2,1,0:T(8,128)(2,1)S(1)} %get-tuple-element.58), channel_id=1, source_target_pairs={{0,1},{1,0},{2,3},{3,2},{4,5},{5,4},{6,7},{7,6},{8,9},{9,8},{10,11... | collective-permute-start | bytes 835592 | tf_op jit(solution)/shard_map/ppermute | solution.py:528
  11.3 13.7 %collective-permute-start.7 = (bf16[544,128]{1,0:T(8,128)(2,1)S(1)}, bf16[544,128]{1,0:T(8,128)(2,1)S(1)}, u32[]{:S(2)}, u32[]{:S(2)}) collective-permute-start(bf16[544,128]{1,0:T(8,128)(2,1)S(1)} %get-tuple-element.65), channel_id=1, source_target_pairs={{0,8},{4,12},{8,0},{12,4},{1,9},{5,13},{9,1},{13,5},{2,10},{6,14},... | collective-permute-start | bytes 417800 | tf_op jit(solution)/shard_map/ppermute | solution.py:522
  15.0 13.4 %collective-permute-start.8 = (bf16[544,128]{1,0:T(8,128)(2,1)S(1)}, bf16[544,128]{1,0:T(8,128)(2,1)S(1)}, u32[]{:S(2)}, u32[]{:S(2)}) collective-permute-start(bf16[544,128]{1,0:T(8,128)(2,1)S(1)} %get-tuple-element.66), channel_id=1, source_target_pairs={{0,12},{4,8},{8,4},{12,0},{1,13},{5,9},{9,5},{13,1},{2,14},{6,10},... | collective-permute-start | bytes 417800 | tf_op jit(solution)/shard_map/ppermute | solution.py:522
  17.4 11.6 %collective-permute-start.6 = (bf16[1,512,512]{2,1,0:T(8,128)(2,1)S(1)}, bf16[1,512,512]{2,1,0:T(8,128)(2,1)S(1)}, u32[]{:S(2)}, u32[]{:S(2)}) collective-permute-start(bf16[1,512,512]{2,1,0:T(8,128)(2,1)S(1)} %shard_map.98), channel_id=1, source_target_pairs={{0,1},{1,0},{2,3},{3,2},{4,5},{5,4},{6,7},{7,6},{8,9},{9,8},{10,11... | collective-permute-start | bytes 1572872 | tf_op jit(solution)/shard_map/ppermute | solution.py:528
  20.1 22.8 %collective-permute-start.3 = (bf16[1024,128]{1,0:T(8,128)(2,1)S(1)}, bf16[1024,128]{1,0:T(8,128)(2,1)S(1)}, u32[]{:S(2)}, u32[]{:S(2)}) collective-permute-start(bf16[1024,128]{1,0:T(8,128)(2,1)S(1)} %get-tuple-element.62), channel_id=1, source_target_pairs={{0,4},{4,0},{8,12},{12,8},{1,5},{5,1},{9,13},{13,9},{2,6},{6,2},{1... | collective-permute-start | bytes 786440 | tf_op jit(solution)/shard_map/ppermute | solution.py:522
  20.2 24.7 %collective-permute-start.4 = (bf16[1024,128]{1,0:T(8,128)(2,1)S(1)}, bf16[1024,128]{1,0:T(8,128)(2,1)S(1)}, u32[]{:S(2)}, u32[]{:S(2)}) collective-permute-start(bf16[1024,128]{1,0:T(8,128)(2,1)S(1)} %get-tuple-element.63), channel_id=1, source_target_pairs={{0,8},{4,12},{8,0},{12,4},{1,9},{5,13},{9,1},{13,5},{2,10},{6,14},... | collective-permute-start | bytes 786440 | tf_op jit(solution)/shard_map/ppermute | solution.py:522
  25.0 26.2 %collective-permute-start.5 = (bf16[1024,128]{1,0:T(8,128)(2,1)S(1)}, bf16[1024,128]{1,0:T(8,128)(2,1)S(1)}, u32[]{:S(2)}, u32[]{:S(2)}) collective-permute-start(bf16[1024,128]{1,0:T(8,128)(2,1)S(1)} %get-tuple-element.64), channel_id=1, source_target_pairs={{0,12},{4,8},{8,4},{12,0},{1,13},{5,9},{9,5},{13,1},{2,14},{6,10},... | collective-permute-start | bytes 786440 | tf_op jit(solution)/shard_map/ppermute | solution.py:522
  28.5 22.7 %collective-permute-start.12 = (bf16[544,128]{1,0:T(8,128)(2,1)S(1)}, bf16[544,128]{1,0:T(8,128)(2,1)S(1)}, u32[]{:S(2)}, u32[]{:S(2)}) collective-permute-start(bf16[544,128]{1,0:T(8,128)(2,1)S(1)} %get-tuple-element.76), channel_id=1, source_target_pairs={{0,4},{4,0},{8,12},{12,8},{1,5},{5,1},{9,13},{13,9},{2,6},{6,2},{1... | collective-permute-start | bytes 417800 | tf_op jit(solution)/shard_map/ppermute | solution.py:522
  30.4 34.1 %collective-permute-start.10 = (bf16[512,128]{1,0:T(8,128)(2,1)S(1)}, bf16[512,128]{1,0:T(8,128)(2,1)S(1)}, u32[]{:S(2)}, u32[]{:S(2)}) collective-permute-start(bf16[512,128]{1,0:T(8,128)(2,1)S(1)} %get-tuple-element.74), channel_id=1, source_target_pairs={{0,8},{4,12},{8,0},{12,4},{1,9},{5,13},{9,1},{13,5},{2,10},{6,14},... | collective-permute-start | bytes 393224 | tf_op jit(solution)/shard_map/ppermute | solution.py:522
  42.9 21.8 %collective-permute-start.11 = (bf16[512,128]{1,0:T(8,128)(2,1)S(1)}, bf16[512,128]{1,0:T(8,128)(2,1)S(1)}, u32[]{:S(2)}, u32[]{:S(2)}) collective-permute-start(bf16[512,128]{1,0:T(8,128)(2,1)S(1)} %get-tuple-element.75), channel_id=1, source_target_pairs={{0,12},{4,8},{8,4},{12,0},{1,13},{5,9},{9,5},{13,1},{2,14},{6,10},... | collective-permute-start | bytes 393224 | tf_op jit(solution)/shard_map/ppermute | solution.py:522
  44.9 20.9 %collective-permute-start.9 = (bf16[512,128]{1,0:T(8,128)(2,1)S(1)}, bf16[512,128]{1,0:T(8,128)(2,1)S(1)}, u32[]{:S(2)}, u32[]{:S(2)}) collective-permute-start(bf16[512,128]{1,0:T(8,128)(2,1)S(1)} %get-tuple-element.73), channel_id=1, source_target_pairs={{0,4},{4,0},{8,12},{12,8},{1,5},{5,1},{9,13},{13,9},{2,6},{6,2},{1... | collective-permute-start | bytes 393224 | tf_op jit(solution)/shard_map/ppermute | solution.py:522
  51.2 14.5 %copy-start = (s32[256]{0:T(256)S(1)}, s32[256]{0:T(256)}, u32[]{:S(2)}) copy-start(s32[256]{0:T(256)} %param.11) | copy-start | bytes 3076
  56.7 19.1 %collective-permute-start.14 = (bf16[512,128]{1,0:T(8,128)(2,1)S(1)}, bf16[512,128]{1,0:T(8,128)(2,1)S(1)}, u32[]{:S(2)}, u32[]{:S(2)}) collective-permute-start(bf16[512,128]{1,0:T(8,128)(2,1)S(1)} %get-tuple-element.88), channel_id=1, source_target_pairs={{0,8},{4,12},{8,0},{12,4},{1,9},{5,13},{9,1},{13,5},{2,10},{6,14},... | collective-permute-start | bytes 393224 | tf_op jit(solution)/shard_map/ppermute | solution.py:522
  64.3 11.5 %collective-permute-start.15 = (bf16[512,128]{1,0:T(8,128)(2,1)S(1)}, bf16[512,128]{1,0:T(8,128)(2,1)S(1)}, u32[]{:S(2)}, u32[]{:S(2)}) collective-permute-start(bf16[512,128]{1,0:T(8,128)(2,1)S(1)} %get-tuple-element.89), channel_id=1, source_target_pairs={{0,12},{4,8},{8,4},{12,0},{1,13},{5,9},{9,5},{13,1},{2,14},{6,10},... | collective-permute-start | bytes 393224 | tf_op jit(solution)/shard_map/ppermute | solution.py:522
  64.5 10.3 %collective-permute-start.26 = (bf16[512,128]{1,0:T(8,128)(2,1)S(1)}, bf16[512,128]{1,0:T(8,128)(2,1)S(1)}, u32[]{:S(2)}, u32[]{:S(2)}) collective-permute-start(bf16[512,128]{1,0:T(8,128)(2,1)S(1)} %get-tuple-element.100), channel_id=1, source_target_pairs={{0,4},{4,0},{8,12},{12,8},{1,5},{5,1},{9,13},{13,9},{2,6},{6,2},{1... | collective-permute-start | bytes 393224 | tf_op jit(solution)/shard_map/ppermute | solution.py:522
  64.7 14.9 %collective-permute-start.27 = (bf16[512,128]{1,0:T(8,128)(2,1)S(1)}, bf16[512,128]{1,0:T(8,128)(2,1)S(1)}, u32[]{:S(2)}, u32[]{:S(2)}) collective-permute-start(bf16[512,128]{1,0:T(8,128)(2,1)S(1)} %get-tuple-element.99.refs_8_), channel_id=1, source_target_pairs={{0,1},{1,0},{2,3},{3,2},{4,5},{5,4},{6,7},{7,6},{8,9},{9,8},{10,11... | collective-permute-start | bytes 393224 | tf_op jit(solution)/shard_map/ppermute | solution.py:528
  74.7 5.8 %collective-permute-start.28 = (bf16[512,128]{1,0:T(8,128)(2,1)S(1)}, bf16[512,128]{1,0:T(8,128)(2,1)S(1)}, u32[]{:S(2)}, u32[]{:S(2)}) collective-permute-start(bf16[512,128]{1,0:T(8,128)(2,1)S(1)} %collective-permute-done.26.refs_9_), channel_id=1, source_target_pairs={{0,1},{1,0},{2,3},{3,2},{4,5},{5,4},{6,7},{7,6},{8,9},{9,8},{10,11... | collective-permute-start | bytes 393224 | tf_op jit(solution)/shard_map/ppermute | solution.py:528
  75.8 13.0 %collective-permute-start.21 = (bf16[1024,128]{1,0:T(8,128)(2,1)S(1)}, bf16[1024,128]{1,0:T(8,128)(2,1)S(1)}, u32[]{:S(2)}, u32[]{:S(2)}) collective-permute-start(bf16[1024,128]{1,0:T(8,128)(2,1)S(1)} %get-tuple-element.98), channel_id=1, source_target_pairs={{0,4},{4,0},{8,12},{12,8},{1,5},{5,1},{9,13},{13,9},{2,6},{6,2},{1... | collective-permute-start | bytes 786440 | tf_op jit(solution)/shard_map/ppermute | solution.py:522
  76.9 12.8 %collective-permute-start.16 = (bf16[1024,128]{1,0:T(8,128)(2,1)S(1)}, bf16[1024,128]{1,0:T(8,128)(2,1)S(1)}, u32[]{:S(2)}, u32[]{:S(2)}) collective-permute-start(bf16[1024,128]{1,0:T(8,128)(2,1)S(1)} %get-tuple-element.90), channel_id=1, source_target_pairs={{0,8},{4,12},{8,0},{12,4},{1,9},{5,13},{9,1},{13,5},{2,10},{6,14},... | collective-permute-start | bytes 786440 | tf_op jit(solution)/shard_map/ppermute | solution.py:522
  78.5 20.7 %collective-permute-start.17 = (bf16[1024,128]{1,0:T(8,128)(2,1)S(1)}, bf16[1024,128]{1,0:T(8,128)(2,1)S(1)}, u32[]{:S(2)}, u32[]{:S(2)}) collective-permute-start(bf16[1024,128]{1,0:T(8,128)(2,1)S(1)} %get-tuple-element.91), channel_id=1, source_target_pairs={{0,12},{4,8},{8,4},{12,0},{1,13},{5,9},{9,5},{13,1},{2,14},{6,10},... | collective-permute-start | bytes 786440 | tf_op jit(solution)/shard_map/ppermute | solution.py:522
  79.6 19.6 %collective-permute-start.13 = (bf16[4,288,128]{2,1,0:T(8,128)(2,1)S(1)}, bf16[4,288,128]{2,1,0:T(8,128)(2,1)S(1)}, u32[]{:S(2)}, u32[]{:S(2)}) collective-permute-start(bf16[4,288,128]{2,1,0:T(8,128)(2,1)S(1)} %get-tuple-element.79), channel_id=1, source_target_pairs={{0,1},{1,0},{2,3},{3,2},{4,5},{5,4},{6,7},{7,6},{8,9},{9,8},{10,11... | collective-permute-start | bytes 884744 | tf_op jit(solution)/shard_map/ppermute | solution.py:528
  80.5 1.4 %collective-permute-start.29 = (bf16[512,128]{1,0:T(8,128)(2,1)S(1)}, bf16[512,128]{1,0:T(8,128)(2,1)S(1)}, u32[]{:S(2)}, u32[]{:S(2)}) collective-permute-start(bf16[512,128]{1,0:T(8,128)(2,1)S(1)} %collective-permute-done.14.refs_10_), channel_id=1, source_target_pairs={{0,1},{1,0},{2,3},{3,2},{4,5},{5,4},{6,7},{7,6},{8,9},{9,8},{10,11... | collective-permute-start | bytes 393224 | tf_op jit(solution)/shard_map/ppermute | solution.py:528
  81.9 23.1 %collective-permute-start.22 = (bf16[1024,128]{1,0:T(8,128)(2,1)S(1)}, bf16[1024,128]{1,0:T(8,128)(2,1)S(1)}, u32[]{:S(2)}, u32[]{:S(2)}) collective-permute-start(bf16[1024,128]{1,0:T(8,128)(2,1)S(1)} %get-tuple-element.97.refs_0_), channel_id=1, source_target_pairs={{0,1},{1,0},{2,3},{3,2},{4,5},{5,4},{6,7},{7,6},{8,9},{9,8},{10,11... | collective-permute-start | bytes 786440 | tf_op jit(solution)/shard_map/ppermute | solution.py:528
  88.8 17.8 %collective-permute-start.23 = (bf16[1024,128]{1,0:T(8,128)(2,1)S(1)}, bf16[1024,128]{1,0:T(8,128)(2,1)S(1)}, u32[]{:S(2)}, u32[]{:S(2)}) collective-permute-start(bf16[1024,128]{1,0:T(8,128)(2,1)S(1)} %collective-permute-done.21.refs_1_), channel_id=1, source_target_pairs={{0,1},{1,0},{2,3},{3,2},{4,5},{5,4},{6,7},{7,6},{8,9},{9,8},{10,11... | collective-permute-start | bytes 786440 | tf_op jit(solution)/shard_map/ppermute | solution.py:528
  89.6 18.2 %collective-permute-start.24 = (bf16[1024,128]{1,0:T(8,128)(2,1)S(1)}, bf16[1024,128]{1,0:T(8,128)(2,1)S(1)}, u32[]{:S(2)}, u32[]{:S(2)}) collective-permute-start(bf16[1024,128]{1,0:T(8,128)(2,1)S(1)} %collective-permute-done.16.refs_2_), channel_id=1, source_target_pairs={{0,1},{1,0},{2,3},{3,2},{4,5},{5,4},{6,7},{7,6},{8,9},{9,8},{10,11... | collective-permute-start | bytes 786440 | tf_op jit(solution)/shard_map/ppermute | solution.py:528
  99.2 8.6 %collective-permute-start.25 = (bf16[1024,128]{1,0:T(8,128)(2,1)S(1)}, bf16[1024,128]{1,0:T(8,128)(2,1)S(1)}, u32[]{:S(2)}, u32[]{:S(2)}) collective-permute-start(bf16[1024,128]{1,0:T(8,128)(2,1)S(1)} %collective-permute-done.17.refs_3_), channel_id=1, source_target_pairs={{0,1},{1,0},{2,3},{3,2},{4,5},{5,4},{6,7},{7,6},{8,9},{9,8},{10,11... | collective-permute-start | bytes 786440 | tf_op jit(solution)/shard_map/ppermute | solution.py:528
  99.2 1.7 %collective-permute-start.30 = (bf16[512,128]{1,0:T(8,128)(2,1)S(1)}, bf16[512,128]{1,0:T(8,128)(2,1)S(1)}, u32[]{:S(2)}, u32[]{:S(2)}) collective-permute-start(bf16[512,128]{1,0:T(8,128)(2,1)S(1)} %collective-permute-done.15.refs_11_), channel_id=1, source_target_pairs={{0,1},{1,0},{2,3},{3,2},{4,5},{5,4},{6,7},{7,6},{8,9},{9,8},{10,11... | collective-permute-start | bytes 393224 | tf_op jit(solution)/shard_map/ppermute | solution.py:528
  100.9 17.2 %collective-permute-start.18 = (bf16[576,128]{1,0:T(8,128)(2,1)S(1)}, bf16[576,128]{1,0:T(8,128)(2,1)S(1)}, u32[]{:S(2)}, u32[]{:S(2)}) collective-permute-start(bf16[576,128]{1,0:T(8,128)(2,1)S(1)} %get-tuple-element.93), channel_id=1, source_target_pairs={{0,4},{4,0},{8,12},{12,8},{1,5},{5,1},{9,13},{13,9},{2,6},{6,2},{1... | collective-permute-start | bytes 442376 | tf_op jit(solution)/shard_map/ppermute | solution.py:522
  105.0 13.1 %collective-permute-start.19 = (bf16[576,128]{1,0:T(8,128)(2,1)S(1)}, bf16[576,128]{1,0:T(8,128)(2,1)S(1)}, u32[]{:S(2)}, u32[]{:S(2)}) collective-permute-start(bf16[576,128]{1,0:T(8,128)(2,1)S(1)} %get-tuple-element.94), channel_id=1, source_target_pairs={{0,8},{4,12},{8,0},{12,4},{1,9},{5,13},{9,1},{13,5},{2,10},{6,14},... | collective-permute-start | bytes 442376 | tf_op jit(solution)/shard_map/ppermute | solution.py:522
  106.5 11.6 %collective-permute-start.20 = (bf16[576,128]{1,0:T(8,128)(2,1)S(1)}, bf16[576,128]{1,0:T(8,128)(2,1)S(1)}, u32[]{:S(2)}, u32[]{:S(2)}) collective-permute-start(bf16[576,128]{1,0:T(8,128)(2,1)S(1)} %get-tuple-element.95), channel_id=1, source_target_pairs={{0,12},{4,8},{8,4},{12,0},{1,13},{5,9},{9,5},{13,1},{2,14},{6,10},... | collective-permute-start | bytes 442376 | tf_op jit(solution)/shard_map/ppermute | solution.py:522
  110.7 15.1 %collective-permute-start.31 = (bf16[256,1024]{1,0:T(8,128)(2,1)S(1)}, bf16[256,1024]{1,0:T(8,128)(2,1)S(1)}, u32[]{:S(2)}, u32[]{:S(2)}) collective-permute-start(bf16[256,1024]{1,0:T(8,128)(2,1)S(1)} %shard_map.104), channel_id=1, source_target_pairs={{0,1},{1,3},{3,2},{2,0},{4,5},{5,7},{7,6},{6,4},{8,9},{9,11},{11,1... | collective-permute-start | bytes 1572872 | tf_op jit(solution)/shard_map/ppermute | solution.py:649
  114.8 10.9 %collective-permute-start.32 = (bf16[256,1024]{1,0:T(8,128)(2,1)S(1)}, bf16[256,1024]{1,0:T(8,128)(2,1)S(1)}, u32[]{:S(2)}, u32[]{:S(2)}) collective-permute-start(bf16[256,1024]{1,0:T(8,128)(2,1)S(1)} %shard_map.105.kept_ref), channel_id=1, source_target_pairs={{1,2},{2,1},{5,6},{6,5},{9,10},{10,9},{13,14},{14,13},{17,18},{18,... | collective-permute-start | bytes 1572872 | tf_op jit(solution)/shard_map/ppermute | solution.py:651

commit v10 on v8

--- a/solution.py
+++ b/solution.py
@@ -197,20 +197,35 @@
     return -(-(rows // head_dim) // 16) * 16
 
 
-def pack_kernel(place_ref, grads_ref, assign_ref, mine_ref, theirs_ref):
+def pack_kernel(place_ref, grads_ref, assign_ref, mine_ref, theirs_ref, ids_ref, sems):
     chips, padded, head_dim = mine_ref.shape
     rows = grads_ref.shape[0]
     spare = padded - rows - rows // head_dim
+    copies = [pltpu.make_async_copy(assign_ref, ids_ref, sems.at[2 * chips])]
     for turn, out_ref in enumerate((mine_ref, theirs_ref)):
         for chip in range(chips):
             head = (place_ref[1] ^ turn) * chips + chip
             at = pl.multiple_of(head * head_dim, head_dim)
-            out_ref[chip, :rows, :] = grads_ref[:, pl.ds(at, head_dim)]
-            ids = assign_ref[pl.ds(head, 1), :].astype(jnp.float32)
+            copies.append(
+                pltpu.make_async_copy(
+                    grads_ref.at[:, pl.ds(at, head_dim)],
+                    out_ref.at[chip, pl.ds(0, rows)],
+                    sems.at[turn * chips + chip],
+                )
+            )
+    for copy in copies:
+        copy.start()
+    copies[0].wait()
+    for turn, out_ref in enumerate((mine_ref, theirs_ref)):
+        for chip in range(chips):
+            head = (place_ref[1] ^ turn) * chips + chip
+            ids = ids_ref[pl.ds(head, 1), :].astype(jnp.float32)
             lines = [
                 ids[:, start : start + head_dim] for start in range(0, rows, head_dim)
             ] + [jnp.zeros((spare, head_dim), jnp.float32)]
             out_ref[chip, rows:, :] = jnp.concatenate(lines, axis=0).astype(jnp.bfloat16)
+    for copy in copies[1:]:
+        copy.wait()
 
 
 def merge_kernel(place_ref, mine_ref, theirs_ref, *out_refs):
@@ -510,13 +525,21 @@
     def to_sibling(piece):
         return lax.ppermute(piece, "sub", swap)
 
+    def stay(array):
+        return pltpu.with_memory_space_constraint(array, pltpu.HBM)
+
     hidden_other = to_sibling(hidden)
     block = low(chips, rows + id_lines(rows, head_dim), head_dim)
-    grads_mine, grads_theirs = call(pack_kernel, (block, block), place, d_attended, assign)
+    grads_mine, grads_theirs = call(
+        pack_kernel,
+        (block, block),
+        place,
+        stay(d_attended),
+        stay(assign),
+        scratch=[pltpu.VMEM(assign.shape, jnp.int32), pltpu.SemaphoreType.DMA((count + 1,))],
+        hbm=2,
+    )
     grads_other = to_sibling(grads_theirs)
-
-    def stay(array):
-        return pltpu.with_memory_space_constraint(array, pltpu.HBM)
 
     def project(turn, weights, *arrived):
         number = len(weights)
@@ -612,24 +635,23 @@
             w_key,
             w_value,
             scratch=[pltpu.VMEM((rows, 3 * width), jnp.bfloat16)],
-            takes=3,
-        )
-
+        )
+
+    *outputs, _, _ = lax.optimization_barrier((*outputs, back[2], back[3]))
+    returned = exchange(outputs)
     square = ("head", "sub")
     crossing = input_part(3, place)
     first = lax.ppermute(crossing, square, [(0, 1), (1, 3), (3, 2), (2, 0)])
     kept = input_part(2, lax.optimization_barrier((place, crossing))[0])
     second = lax.ppermute(kept, square, [(1, 2), (2, 1)])
-    *outputs, _, _ = lax.optimization_barrier((*outputs, back[2], back[3]))
-    returned = exchange(outputs)
-    *returned, _ = lax.optimization_barrier((*returned, first))
     attended, centroid_sums = call(
         partial(attended_kernel, chips),
         (low(rows, width), jax.ShapeDtypeStruct((count, owned, head_dim), jnp.float32)),
         place,
         *returned,
-    )
-    first, _ = lax.optimization_barrier((first, attended))
+        takes=8,
+    )
+    first, second, _ = lax.optimization_barrier((first, second, attended))
     d_hidden = call(sum_kernel, low(rows, half), place, first, second, kept)
     return (attended, d_hidden, centroid_sums)
 

time: 127 us -> 125 us (0.984)
  waiting for transfers between devices: 37.5 us -> 26.9 us
  starting transfers between devices: 49 us -> 57.8 us
  local copies, waits for them, and re-layouts: 1.76 us -> 0.01 us
    ppermute x18, waiting for transfers between devices: 33.8 us -> 17.7 us  [exchange(): lax.ppermute(parts[offset], 'seq', [(at, at ^ offset) for at in range(chi...]
    ppermute x13, starting transfers between devices: 8.52 us -> 16.4 us  [to_sibling(): return lax.ppermute(piece, 'sub', swap)]
    ppermute x1, waiting for transfers between devices: 0.01 us -> 6.1 us  [by_head(): second = lax.ppermute(kept, square, [(1, 2), (2, 1)])]
    unnamed x12 -> x8, local copies, waits for them, and re-layouts: 1.76 us -> 0.01 us
  transfers between devices with their start and end apart: 33 -> 33, of which waited for: 8 -> 7; matrix products, arithmetic and copies ran while one was open for 0% -> 0% of each run, Pallas kernels for 26% -> 27%
where the time goes in v10:
time: 125 us; the launch traced here: 124 us
  starting transfers between devices  57.8 us (46%)
  Pallas kernels  38.7 us (31%)
  waiting for transfers between devices  26.9 us (22%)
    pallas_call x13, Pallas kernels, call(): pl.pallas_call(kernel, out_shape=outs, in_specs=[smem] + [vmem] * (len(op...  38.7 us
    ppermute x18, starting transfers between devices, exchange(): lax.ppermute(parts[offset], 'seq', [(at, at ^ offset) for at in range(chi...  36.9 us
    ppermute x18, waiting for transfers between devices, exchange(): lax.ppermute(parts[offset], 'seq', [(at, at ^ offset) for at in range(chi...  17.7 us
    ppermute x13, starting transfers between devices, to_sibling(): return lax.ppermute(piece, 'sub', swap)  16.4 us
    ppermute x1, waiting for transfers between devices, by_head(): second = lax.ppermute(kept, square, [(1, 2), (2, 1)])  6.1 us
    ppermute x1, starting transfers between devices, by_head(): second = lax.ppermute(kept, square, [(1, 2), (2, 1)])  3.25 us
    ppermute x13, waiting for transfers between devices, to_sibling(): return lax.ppermute(piece, 'sub', swap)  3.15 us
  transfers between devices with their start and end apart: 33, of which 7 were waited for; matrix products, arithmetic and copies ran while one was open for 0% of the time, Pallas kernels for 27%

profile of v10, /device:TPU:1, one launch (start us, length us, event | category | flops | bytes accessed | tf_op | source)
XLA Modules:
  0.0 124.3 jit_solution(1314886893497344822)
XLA Ops:
  0.6 0.1 collective-permute-start
  0.8 0.1 pad_add_fusion.place_ref
  0.8 1.7 %shard_map.94 = (bf16[4,272,128]{2,1,0:T(8,128)(2,1)S(1)}, bf16[4,272,128]{2,1,0:T(8,128)(2,1)S(1)}) custom-call(s32[4]{0:T(128)S(1)} %pad_add_fusion.place_ref, bf16[256,1024]{1,0:T(8,128)(2,1)} %grads_ref.1, s32[8,256]{1,0:T(8,128)} %assign_ref.1), custom_call_target="tpu_custom_call" | custom-call | flops 1150000000 | bytes 1048576 | tf_op jit(solution)/shard_map/pallas_call | solution.py:500
  2.5 0.5 collective-permute-start.1
  3.1 1.2 collective-permute-done.1.theirs_ref
  4.2 0.6 shard_map.95
  4.8 3.4 %shard_map.96 = bf16[2,512,512]{2,1,0:T(8,128)(2,1)S(1)} custom-call(s32[4]{0:T(128)S(1)} %pad_add_fusion.place_ref, bf16[256,2048]{1,0:T(8,128)(2,1)} %refs_1_.3, bf16[256,2048]{1,0:T(8,128)(2,1)S(1)} %collective-permute-done.refs_1_.refs_2_, bf16[1024,1024]{1,0:T(8,128)(2,1)} %refs_16_.3, bf16[1024,1024]{1,0:T(8,128)(2,1)} %refs_17_.3), custom_call_target="tpu_custom_call" | custom-call | flops 115000000 | bytes 1048576 | tf_op jit(solution)/shard_map/pallas_call | solution.py:500
  8.3 0.4 collective-permute-start.2
  8.7 3.4 %collective-permute-start.7 = (bf16[544,128]{1,0:T(8,128)(2,1)S(1)}, bf16[544,128]{1,0:T(8,128)(2,1)S(1)}, u32[]{:S(2)}, u32[]{:S(2)}) collective-permute-start(bf16[544,128]{1,0:T(8,128)(2,1)S(1)} %get-tuple-element.61), channel_id=1, source_target_pairs={{0,8},{4,12},{8,0},{12,4},{1,9},{5,13},{9,1},{13,5},{2,10},{6,14},... | collective-permute-start | bytes 417800 | tf_op jit(solution)/shard_map/ppermute | solution.py:520
  12.1 1.1 collective-permute-start.8
  13.2 2.7 %shard_map.98 = bf16[1,512,512]{2,1,0:T(8,128)(2,1)S(1)} custom-call(s32[4]{0:T(128)S(1)} %pad_add_fusion.place_ref, bf16[256,2048]{1,0:T(8,128)(2,1)} %refs_1_.3, bf16[256,2048]{1,0:T(8,128)(2,1)S(1)} %collective-permute-done.refs_1_.refs_2_, bf16[1024,1024]{1,0:T(8,128)(2,1)} %refs_18_.3), custom_call_target="tpu_custom_call" | custom-call | flops 115000000 | bytes 1048576 | tf_op jit(solution)/shard_map/pallas_call | solution.py:500
  15.9 1.0 collective-permute-start.6
  16.9 0.0 collective-permute-done.2.refs_0_
  16.9 3.6 %shard_map.97 = (bf16[1024,128]{1,0:T(8,128)(2,1)S(1)}, bf16[1024,128]{1,0:T(8,128)(2,1)S(1)}, bf16[1024,128]{1,0:T(8,128)(2,1)S(1)}, bf16[1024,128]{1,0:T(8,128)(2,1)S(1)}) custom-call(s32[4]{0:T(128)S(1)} %pad_add_fusion.place_ref, bf16[2,512,512]{2,1,0:T(8,128)(2,1)S(1)} %collective-permute-done.2.refs_0_, bf16[256,2048]{1,0:T(8,128)(2,1)} %refs_1_.3, ...), custom_call_target="tpu_custom_call" | custom-call | flops 9200000000 | bytes 1048576 | tf_op jit(solution)/shard_map/pallas_call | solution.py:500
  20.5 0.1 collective-permute-start.3
  20.6 2.5 %collective-permute-start.4 = (bf16[1024,128]{1,0:T(8,128)(2,1)S(1)}, bf16[1024,128]{1,0:T(8,128)(2,1)S(1)}, u32[]{:S(2)}, u32[]{:S(2)}) collective-permute-start(bf16[1024,128]{1,0:T(8,128)(2,1)S(1)} %get-tuple-element.59), channel_id=1, source_target_pairs={{0,8},{4,12},{8,0},{12,4},{1,9},{5,13},{9,1},{13,5},{2,10},{6,14},... | collective-permute-start | bytes 786440 | tf_op jit(solution)/shard_map/ppermute | solution.py:520
  23.0 2.5 %collective-permute-start.5 = (bf16[1024,128]{1,0:T(8,128)(2,1)S(1)}, bf16[1024,128]{1,0:T(8,128)(2,1)S(1)}, u32[]{:S(2)}, u32[]{:S(2)}) collective-permute-start(bf16[1024,128]{1,0:T(8,128)(2,1)S(1)} %get-tuple-element.60), channel_id=1, source_target_pairs={{0,12},{4,8},{8,4},{12,0},{1,13},{5,9},{9,5},{13,1},{2,14},{6,10},... | collective-permute-start | bytes 786440 | tf_op jit(solution)/shard_map/ppermute | solution.py:520
  25.5 0.2 collective-permute-start.12
  25.7 0.0 collective-permute-done.6.refs_0_
  25.7 2.8 %shard_map.99 = (bf16[512,128]{1,0:T(8,128)(2,1)S(1)}, bf16[512,128]{1,0:T(8,128)(2,1)S(1)}, bf16[512,128]{1,0:T(8,128)(2,1)S(1)}, bf16[512,128]{1,0:T(8,128)(2,1)S(1)}) custom-call(s32[4]{0:T(128)S(1)} %pad_add_fusion.place_ref, bf16[1,512,512]{2,1,0:T(8,128)(2,1)S(1)} %collective-permute-done.6.refs_0_, bf16[256,2048]{1,0:T(8,128)(2,1)} %refs_1_.3, ...), custom_call_target="tpu_custom_call" | custom-call | flops 115000000 | bytes 1048576 | tf_op jit(solution)/shard_map/pallas_call | solution.py:500
  28.6 2.0 %collective-permute-start.10 = (bf16[512,128]{1,0:T(8,128)(2,1)S(1)}, bf16[512,128]{1,0:T(8,128)(2,1)S(1)}, u32[]{:S(2)}, u32[]{:S(2)}) collective-permute-start(bf16[512,128]{1,0:T(8,128)(2,1)S(1)} %get-tuple-element.70), channel_id=1, source_target_pairs={{0,8},{4,12},{8,0},{12,4},{1,9},{5,13},{9,1},{13,5},{2,10},{6,14},... | collective-permute-start | bytes 393224 | tf_op jit(solution)/shard_map/ppermute | solution.py:520
  30.5 2.7 %collective-permute-done.3.refs_1_ = bf16[1024,128]{1,0:T(8,128)(2,1)S(1)} collective-permute-done((bf16[1024,128]{1,0:T(8,128)(2,1)S(1)}, bf16[1024,128]{1,0:T(8,128)(2,1)S(1)}, u32[]{:S(2)}, u32[]{:S(2)}) %collective-permute-start.3) | collective-permute-done | bytes 262176 | tf_op jit(solution)/shard_map/ppermute | solution.py:520
  33.2 0.0 collective-permute-start.11
  33.2 8.6 %collective-permute-done.4.refs_2_ = bf16[1024,128]{1,0:T(8,128)(2,1)S(1)} collective-permute-done((bf16[1024,128]{1,0:T(8,128)(2,1)S(1)}, bf16[1024,128]{1,0:T(8,128)(2,1)S(1)}, u32[]{:S(2)}, u32[]{:S(2)}) %collective-permute-start.4) | collective-permute-done | bytes 262176 | tf_op jit(solution)/shard_map/ppermute | solution.py:520
  41.8 6.3 %collective-permute-start.9 = (bf16[512,128]{1,0:T(8,128)(2,1)S(1)}, bf16[512,128]{1,0:T(8,128)(2,1)S(1)}, u32[]{:S(2)}, u32[]{:S(2)}) collective-permute-start(bf16[512,128]{1,0:T(8,128)(2,1)S(1)} %get-tuple-element.69), channel_id=1, source_target_pairs={{0,4},{4,0},{8,12},{12,8},{1,5},{5,1},{9,13},{13,9},{2,6},{6,2},{1... | collective-permute-start | bytes 393224 | tf_op jit(solution)/shard_map/ppermute | solution.py:520
  48.1 0.0 collective-permute-done.12.refs_5_.refs_9_
  48.1 5.5 %shard_map.100 = (bf16[512,128]{1,0:T(8,128)(2,1)S(1)}, bf16[512,128]{1,0:T(8,128)(2,1)S(1)}, bf16[512,128]{1,0:T(8,128)(2,1)S(1)}, bf16[512,128]{1,0:T(8,128)(2,1)S(1)}, f32[8,256]{1,0:T(8,128)S(1)}) custom-call(s32[4]{0:T(128)S(1)} %pad_add_fusion.place_ref, bf16[1024,128]{1,0:T(8,128)(2,1)S(1)} %get-tuple-element.65.refs_0_, ...), custom_call_target="tpu_custom_call" | custom-call | flops 8049999872 | bytes 1048576 | tf_op jit(solution)/shard_map/pallas_call | solution.py:500
  53.6 7.7 %collective-permute-start.14 = (bf16[512,128]{1,0:T(8,128)(2,1)S(1)}, bf16[512,128]{1,0:T(8,128)(2,1)S(1)}, u32[]{:S(2)}, u32[]{:S(2)}) collective-permute-start(bf16[512,128]{1,0:T(8,128)(2,1)S(1)} %get-tuple-element.84), channel_id=1, source_target_pairs={{0,8},{4,12},{8,0},{12,4},{1,9},{5,13},{9,1},{13,5},{2,10},{6,14},... | collective-permute-start | bytes 393224 | tf_op jit(solution)/shard_map/ppermute | solution.py:520
  61.3 0.2 collective-permute-start.15
  61.5 0.0 collective-permute-done.10.refs_6_
  61.5 0.2 collective-permute-start.26
  61.7 0.0 collective-permute-done.11.refs_7_
  61.7 1.3 %collective-permute-start.27 = (bf16[512,128]{1,0:T(8,128)(2,1)S(1)}, bf16[512,128]{1,0:T(8,128)(2,1)S(1)}, u32[]{:S(2)}, u32[]{:S(2)}) collective-permute-start(bf16[512,128]{1,0:T(8,128)(2,1)S(1)} %get-tuple-element.95.refs_8_), channel_id=1, source_target_pairs={{0,1},{1,0},{2,3},{3,2},{4,5},{5,4},{6,7},{7,6},{8,9},{9,8},{10,11... | collective-permute-start | bytes 393224 | tf_op jit(solution)/shard_map/ppermute | solution.py:526
  62.9 0.0 collective-permute-done.9.refs_5_
  63.0 9.0 %shard_map.101 = (bf16[1024,128]{1,0:T(8,128)(2,1)S(1)}, bf16[1024,128]{1,0:T(8,128)(2,1)S(1)}, bf16[1024,128]{1,0:T(8,128)(2,1)S(1)}, bf16[1024,128]{1,0:T(8,12...) custom-call(s32[4]{0:T(128)S(1)} %pad_add_fusion.place_ref, ...), custom_call_target="tpu_custom_call" | custom-call | flops 11500000256 | bytes 1048576 | tf_op jit(solution)/shard_map/pallas_call | solution.py:500
  72.0 0.0 collective-permute-done.26.refs_9_
  72.0 0.8 collective-permute-start.28
  72.8 0.0 collective-permute-done.14.refs_10_
  72.8 0.0 collective-permute-done.15.refs_11_
  72.8 1.1 collective-permute-start.21
  73.9 1.7 %collective-permute-start.16 = (bf16[1024,128]{1,0:T(8,128)(2,1)S(1)}, bf16[1024,128]{1,0:T(8,128)(2,1)S(1)}, u32[]{:S(2)}, u32[]{:S(2)}) collective-permute-start(bf16[1024,128]{1,0:T(8,128)(2,1)S(1)} %get-tuple-element.86), channel_id=1, source_target_pairs={{0,8},{4,12},{8,0},{12,4},{1,9},{5,13},{9,1},{13,5},{2,10},{6,14},... | collective-permute-start | bytes 786440 | tf_op jit(solution)/shard_map/ppermute | solution.py:520
  75.5 1.1 collective-permute-start.17
  76.6 1.0 collective-permute-start.13
  77.6 0.1 collective-permute-start.29
  77.7 1.3 %collective-permute-done.29.refs_14_ = bf16[512,128]{1,0:T(8,128)(2,1)S(1)} collective-permute-done((bf16[512,128]{1,0:T(8,128)(2,1)S(1)}, bf16[512,128]{1,0:T(8,128)(2,1)S(1)}, u32[]{:S(2)}, u32[]{:S(2)}) %collective-permute-start.29) | collective-permute-done | bytes 131104 | tf_op jit(solution)/shard_map/ppermute | solution.py:526
  79.0 0.4 collective-permute-start.22
  79.4 6.4 %collective-permute-done.21.refs_1_ = bf16[1024,128]{1,0:T(8,128)(2,1)S(1)} collective-permute-done((bf16[1024,128]{1,0:T(8,128)(2,1)S(1)}, bf16[1024,128]{1,0:T(8,128)(2,1)S(1)}, u32[]{:S(2)}, u32[]{:S(2)}) %collective-permute-start.21) | collective-permute-done | bytes 262176 | tf_op jit(solution)/shard_map/ppermute | solution.py:520
  85.8 0.9 collective-permute-start.23
  86.7 9.5 %collective-permute-start.24 = (bf16[1024,128]{1,0:T(8,128)(2,1)S(1)}, bf16[1024,128]{1,0:T(8,128)(2,1)S(1)}, u32[]{:S(2)}, u32[]{:S(2)}) collective-permute-start(bf16[1024,128]{1,0:T(8,128)(2,1)S(1)} %collective-permute-done.16.refs_2_), channel_id=1, source_target_pairs={{0,1},{1,0},{2,3},{3,2},{4,5},{5,4},{6,7},{7,6},{8,9},{9,8},{10,11... | collective-permute-start | bytes 786440 | tf_op jit(solution)/shard_map/ppermute | solution.py:526
  96.2 0.0 collective-permute-done.17.refs_3_
  96.2 0.0 collective-permute-start.25
  96.2 0.5 collective-permute-start.30
  96.7 0.6 shard_map.102
  97.3 0.6 collective-permute-done.30.refs_15_
  97.9 4.1 %collective-permute-start.18 = (bf16[576,128]{1,0:T(8,128)(2,1)S(1)}, bf16[576,128]{1,0:T(8,128)(2,1)S(1)}, u32[]{:S(2)}, u32[]{:S(2)}) collective-permute-start(bf16[576,128]{1,0:T(8,128)(2,1)S(1)} %get-tuple-element.89), channel_id=1, source_target_pairs={{0,4},{4,0},{8,12},{12,8},{1,5},{5,1},{9,13},{13,9},{2,6},{6,2},{1... | collective-permute-start | bytes 442376 | tf_op jit(solution)/shard_map/ppermute | solution.py:520
  102.0 1.6 %collective-permute-start.19 = (bf16[576,128]{1,0:T(8,128)(2,1)S(1)}, bf16[576,128]{1,0:T(8,128)(2,1)S(1)}, u32[]{:S(2)}, u32[]{:S(2)}) collective-permute-start(bf16[576,128]{1,0:T(8,128)(2,1)S(1)} %get-tuple-element.90), channel_id=1, source_target_pairs={{0,8},{4,12},{8,0},{12,4},{1,9},{5,13},{9,1},{13,5},{2,10},{6,14},... | collective-permute-start | bytes 442376 | tf_op jit(solution)/shard_map/ppermute | solution.py:520
  103.6 1.2 %collective-permute-start.20 = (bf16[576,128]{1,0:T(8,128)(2,1)S(1)}, bf16[576,128]{1,0:T(8,128)(2,1)S(1)}, u32[]{:S(2)}, u32[]{:S(2)}) collective-permute-start(bf16[576,128]{1,0:T(8,128)(2,1)S(1)} %get-tuple-element.91), channel_id=1, source_target_pairs={{0,12},{4,8},{8,4},{12,0},{1,13},{5,9},{9,5},{13,1},{2,14},{6,10},... | collective-permute-start | bytes 442376 | tf_op jit(solution)/shard_map/ppermute | solution.py:520
  104.9 2.9 %shard_map.104 = bf16[256,1024]{1,0:T(8,128)(2,1)S(1)} custom-call(s32[4]{0:T(128)S(1)} %pad_add_fusion.place_ref, bf16[1024,128]{1,0:T(8,128)(2,1)S(1)} %get-tuple-element.93.refs_0_, bf16[1024,128]{1,0:T(8,128)(2,1)S(1)} %collective-permute-done.21.refs_1_, bf16[1024,128]{1,0:T(8,128)(2,1)S(1)} %collective-permute-done.16.refs_2_, ...), custom_call_target="tpu_custom_call" | custom-call | flops 1150000000 | bytes 1048576 | tf_op jit(solution)/shard_map/pallas_call | solution.py:500
  107.8 1.2 collective-permute-start.31
  109.0 2.9 %shard_map.105.kept_ref = bf16[256,1024]{1,0:T(8,128)(2,1)S(1)} custom-call(s32[4]{0:T(128)S(1)} %pad_add_fusion.place_ref, bf16[1024,128]{1,0:T(8,128)(2,1)S(1)} %get-tuple-element.93.refs_0_, bf16[1024,128]{1,0:T(8,128)(2,1)S(1)} %collective-permute-done.21.refs_1_, bf16[1024,128]{1,0:T(8,128)(2,1)S(1)} %collective-permute-done.16.refs_2_, ...), custom_call_target="tpu_custom_call" | custom-call | flops 1150000000 | bytes 1048576 | tf_op jit(solution)/shard_map/pallas_call | solution.py:500
  111.9 3.3 %collective-permute-start.32 = (bf16[256,1024]{1,0:T(8,128)(2,1)S(1)}, bf16[256,1024]{1,0:T(8,128)(2,1)S(1)}, u32[]{:S(2)}, u32[]{:S(2)}) collective-permute-start(bf16[256,1024]{1,0:T(8,128)(2,1)S(1)} %shard_map.105.kept_ref), channel_id=1, source_target_pairs={{1,2},{2,1},{5,6},{6,5},{9,10},{10,9},{13,14},{14,13},{17,18},{18,... | collective-permute-start | bytes 1572872 | tf_op jit(solution)/shard_map/ppermute | solution.py:646
  115.2 1.5 %shard_map.103 = (bf16[256,1024]{1,0:T(8,128)(2,1)}, f32[8,32,128]{2,1,0:T(8,128)}) custom-call(s32[4]{0:T(128)S(1)} %pad_add_fusion.place_ref, bf16[576,128]{1,0:T(8,128)(2,1)S(1)} %get-tuple-element.88.refs_0_, bf16[576,128]{1,0:T(8,128)(2,1)S(1)} %collective-permute-done.18.refs_1_, bf16[576,128]{1,0:T(8,128)(2,1)S(1)} %collective-permute-done.19.refs_2_, ...), custom_call_target="tpu_custom_call" | custom-call | flops 9200000000 | bytes 1048576 | tf_op jit(solution)/shard_map/pallas_call | solution.py:500
  116.8 6.1 %collective-permute-done.32.second_ref = bf16[256,1024]{1,0:T(8,128)(2,1)S(1)} collective-permute-done((bf16[256,1024]{1,0:T(8,128)(2,1)S(1)}, bf16[256,1024]{1,0:T(8,128)(2,1)S(1)}, u32[]{:S(2)}, u32[]{:S(2)}) %collective-permute-start.32) | collective-permute-done | bytes 524320 | tf_op jit(solution)/shard_map/ppermute | solution.py:646
  122.9 1.5 %shard_map.106 = bf16[256,1024]{1,0:T(8,128)(2,1)} custom-call(s32[4]{0:T(128)S(1)} %pad_add_fusion.place_ref, bf16[256,1024]{1,0:T(8,128)(2,1)S(1)} %collective-permute-done.31.first_ref, bf16[256,1024]{1,0:T(8,128)(2,1)S(1)} %collective-permute-done.32.second_ref, bf16[256,1024]{1,0:T(8,128)(2,1)S(1)} %shard_map.105.kept_ref), custom_call_target="tpu_custom_call" | custom-call | flops 1150000000 | bytes 1048576 | tf_op jit(solution)/shard_map/pallas_call | solution.py:500
  (24 shorter events, 0.1 us)
Async XLA Ops:
  0.6 4.2 %collective-permute-start = (bf16[256,2048]{1,0:T(8,128)(2,1)}, bf16[256,2048]{1,0:T(8,128)(2,1)S(1)}, u32[]{:S(2)}, u32[]{:S(2)}) collective-permute-start(bf16[256,2048]{1,0:T(8,128)(2,1)} %refs_1_.3), channel_id=1, source_target_pairs={{0,1},{1,0},{2,3},{3,2},{4,5},{5,4},{6,7},{7,6},{8,9},{9,8},{10,11... | collective-permute-start | bytes 3145736 | tf_op jit(solution)/shard_map/ppermute | solution.py:526
  2.5 1.7 %collective-permute-start.1 = (bf16[4,272,128]{2,1,0:T(8,128)(2,1)S(1)}, bf16[4,272,128]{2,1,0:T(8,128)(2,1)S(1)}, u32[]{:S(2)}, u32[]{:S(2)}) collective-permute-start(bf16[4,272,128]{2,1,0:T(8,128)(2,1)S(1)} %get-tuple-element.53), channel_id=1, source_target_pairs={{0,1},{1,0},{2,3},{3,2},{4,5},{5,4},{6,7},{7,6},{8,9},{9,8},{10,11... | collective-permute-start | bytes 835592 | tf_op jit(solution)/shard_map/ppermute | solution.py:526
  8.3 8.6 %collective-permute-start.2 = (bf16[2,512,512]{2,1,0:T(8,128)(2,1)S(1)}, bf16[2,512,512]{2,1,0:T(8,128)(2,1)S(1)}, u32[]{:S(2)}, u32[]{:S(2)}) collective-permute-start(bf16[2,512,512]{2,1,0:T(8,128)(2,1)S(1)} %shard_map.96), channel_id=1, source_target_pairs={{0,1},{1,0},{2,3},{3,2},{4,5},{5,4},{6,7},{7,6},{8,9},{9,8},{10,11... | collective-permute-start | bytes 3145736 | tf_op jit(solution)/shard_map/ppermute | solution.py:526
  8.7 14.3 %collective-permute-start.7 = (bf16[544,128]{1,0:T(8,128)(2,1)S(1)}, bf16[544,128]{1,0:T(8,128)(2,1)S(1)}, u32[]{:S(2)}, u32[]{:S(2)}) collective-permute-start(bf16[544,128]{1,0:T(8,128)(2,1)S(1)} %get-tuple-element.61), channel_id=1, source_target_pairs={{0,8},{4,12},{8,0},{12,4},{1,9},{5,13},{9,1},{13,5},{2,10},{6,14},... | collective-permute-start | bytes 417800 | tf_op jit(solution)/shard_map/ppermute | solution.py:520
  12.1 13.4 %collective-permute-start.8 = (bf16[544,128]{1,0:T(8,128)(2,1)S(1)}, bf16[544,128]{1,0:T(8,128)(2,1)S(1)}, u32[]{:S(2)}, u32[]{:S(2)}) collective-permute-start(bf16[544,128]{1,0:T(8,128)(2,1)S(1)} %get-tuple-element.62), channel_id=1, source_target_pairs={{0,12},{4,8},{8,4},{12,0},{1,13},{5,9},{9,5},{13,1},{2,14},{6,10},... | collective-permute-start | bytes 417800 | tf_op jit(solution)/shard_map/ppermute | solution.py:520
  15.9 9.8 %collective-permute-start.6 = (bf16[1,512,512]{2,1,0:T(8,128)(2,1)S(1)}, bf16[1,512,512]{2,1,0:T(8,128)(2,1)S(1)}, u32[]{:S(2)}, u32[]{:S(2)}) collective-permute-start(bf16[1,512,512]{2,1,0:T(8,128)(2,1)S(1)} %shard_map.98), channel_id=1, source_target_pairs={{0,1},{1,0},{2,3},{3,2},{4,5},{5,4},{6,7},{7,6},{8,9},{9,8},{10,11... | collective-permute-start | bytes 1572872 | tf_op jit(solution)/shard_map/ppermute | solution.py:526
  20.5 12.7 %collective-permute-start.3 = (bf16[1024,128]{1,0:T(8,128)(2,1)S(1)}, bf16[1024,128]{1,0:T(8,128)(2,1)S(1)}, u32[]{:S(2)}, u32[]{:S(2)}) collective-permute-start(bf16[1024,128]{1,0:T(8,128)(2,1)S(1)} %get-tuple-element.58), channel_id=1, source_target_pairs={{0,4},{4,0},{8,12},{12,8},{1,5},{5,1},{9,13},{13,9},{2,6},{6,2},{1... | collective-permute-start | bytes 786440 | tf_op jit(solution)/shard_map/ppermute | solution.py:520
  20.6 21.2 %collective-permute-start.4 = (bf16[1024,128]{1,0:T(8,128)(2,1)S(1)}, bf16[1024,128]{1,0:T(8,128)(2,1)S(1)}, u32[]{:S(2)}, u32[]{:S(2)}) collective-permute-start(bf16[1024,128]{1,0:T(8,128)(2,1)S(1)} %get-tuple-element.59), channel_id=1, source_target_pairs={{0,8},{4,12},{8,0},{12,4},{1,9},{5,13},{9,1},{13,5},{2,10},{6,14},... | collective-permute-start | bytes 786440 | tf_op jit(solution)/shard_map/ppermute | solution.py:520
  23.0 25.0 %collective-permute-start.5 = (bf16[1024,128]{1,0:T(8,128)(2,1)S(1)}, bf16[1024,128]{1,0:T(8,128)(2,1)S(1)}, u32[]{:S(2)}, u32[]{:S(2)}) collective-permute-start(bf16[1024,128]{1,0:T(8,128)(2,1)S(1)} %get-tuple-element.60), channel_id=1, source_target_pairs={{0,12},{4,8},{8,4},{12,0},{1,13},{5,9},{9,5},{13,1},{2,14},{6,10},... | collective-permute-start | bytes 786440 | tf_op jit(solution)/shard_map/ppermute | solution.py:520
  25.5 22.5 %collective-permute-start.12 = (bf16[544,128]{1,0:T(8,128)(2,1)S(1)}, bf16[544,128]{1,0:T(8,128)(2,1)S(1)}, u32[]{:S(2)}, u32[]{:S(2)}) collective-permute-start(bf16[544,128]{1,0:T(8,128)(2,1)S(1)} %get-tuple-element.72), channel_id=1, source_target_pairs={{0,4},{4,0},{8,12},{12,8},{1,5},{5,1},{9,13},{13,9},{2,6},{6,2},{1... | collective-permute-start | bytes 417800 | tf_op jit(solution)/shard_map/ppermute | solution.py:520
  28.6 32.9 %collective-permute-start.10 = (bf16[512,128]{1,0:T(8,128)(2,1)S(1)}, bf16[512,128]{1,0:T(8,128)(2,1)S(1)}, u32[]{:S(2)}, u32[]{:S(2)}) collective-permute-start(bf16[512,128]{1,0:T(8,128)(2,1)S(1)} %get-tuple-element.70), channel_id=1, source_target_pairs={{0,8},{4,12},{8,0},{12,4},{1,9},{5,13},{9,1},{13,5},{2,10},{6,14},... | collective-permute-start | bytes 393224 | tf_op jit(solution)/shard_map/ppermute | solution.py:520
  33.2 28.5 %collective-permute-start.11 = (bf16[512,128]{1,0:T(8,128)(2,1)S(1)}, bf16[512,128]{1,0:T(8,128)(2,1)S(1)}, u32[]{:S(2)}, u32[]{:S(2)}) collective-permute-start(bf16[512,128]{1,0:T(8,128)(2,1)S(1)} %get-tuple-element.71), channel_id=1, source_target_pairs={{0,12},{4,8},{8,4},{12,0},{1,13},{5,9},{9,5},{13,1},{2,14},{6,10},... | collective-permute-start | bytes 393224 | tf_op jit(solution)/shard_map/ppermute | solution.py:520
  41.8 21.2 %collective-permute-start.9 = (bf16[512,128]{1,0:T(8,128)(2,1)S(1)}, bf16[512,128]{1,0:T(8,128)(2,1)S(1)}, u32[]{:S(2)}, u32[]{:S(2)}) collective-permute-start(bf16[512,128]{1,0:T(8,128)(2,1)S(1)} %get-tuple-element.69), channel_id=1, source_target_pairs={{0,4},{4,0},{8,12},{12,8},{1,5},{5,1},{9,13},{13,9},{2,6},{6,2},{1... | collective-permute-start | bytes 393224 | tf_op jit(solution)/shard_map/ppermute | solution.py:520
  48.1 14.9 %copy-start.3 = (s32[256]{0:T(256)S(1)}, s32[256]{0:T(256)}, u32[]{:S(2)}) copy-start(s32[256]{0:T(256)} %param.11) | copy-start | bytes 3076
  53.6 19.2 %collective-permute-start.14 = (bf16[512,128]{1,0:T(8,128)(2,1)S(1)}, bf16[512,128]{1,0:T(8,128)(2,1)S(1)}, u32[]{:S(2)}, u32[]{:S(2)}) collective-permute-start(bf16[512,128]{1,0:T(8,128)(2,1)S(1)} %get-tuple-element.84), channel_id=1, source_target_pairs={{0,8},{4,12},{8,0},{12,4},{1,9},{5,13},{9,1},{13,5},{2,10},{6,14},... | collective-permute-start | bytes 393224 | tf_op jit(solution)/shard_map/ppermute | solution.py:520
  61.3 11.5 %collective-permute-start.15 = (bf16[512,128]{1,0:T(8,128)(2,1)S(1)}, bf16[512,128]{1,0:T(8,128)(2,1)S(1)}, u32[]{:S(2)}, u32[]{:S(2)}) collective-permute-start(bf16[512,128]{1,0:T(8,128)(2,1)S(1)} %get-tuple-element.85), channel_id=1, source_target_pairs={{0,12},{4,8},{8,4},{12,0},{1,13},{5,9},{9,5},{13,1},{2,14},{6,10},... | collective-permute-start | bytes 393224 | tf_op jit(solution)/shard_map/ppermute | solution.py:520
  61.5 10.5 %collective-permute-start.26 = (bf16[512,128]{1,0:T(8,128)(2,1)S(1)}, bf16[512,128]{1,0:T(8,128)(2,1)S(1)}, u32[]{:S(2)}, u32[]{:S(2)}) collective-permute-start(bf16[512,128]{1,0:T(8,128)(2,1)S(1)} %get-tuple-element.96), channel_id=1, source_target_pairs={{0,4},{4,0},{8,12},{12,8},{1,5},{5,1},{9,13},{13,9},{2,6},{6,2},{1... | collective-permute-start | bytes 393224 | tf_op jit(solution)/shard_map/ppermute | solution.py:520
  61.7 15.0 %collective-permute-start.27 = (bf16[512,128]{1,0:T(8,128)(2,1)S(1)}, bf16[512,128]{1,0:T(8,128)(2,1)S(1)}, u32[]{:S(2)}, u32[]{:S(2)}) collective-permute-start(bf16[512,128]{1,0:T(8,128)(2,1)S(1)} %get-tuple-element.95.refs_8_), channel_id=1, source_target_pairs={{0,1},{1,0},{2,3},{3,2},{4,5},{5,4},{6,7},{7,6},{8,9},{9,8},{10,11... | collective-permute-start | bytes 393224 | tf_op jit(solution)/shard_map/ppermute | solution.py:526
  63.0 41.9 %copy-start.2 = (bf16[1024,1024]{1,0:T(8,128)(2,1)S(1)}, bf16[1024,1024]{1,0:T(8,128)(2,1)}, u32[]{:S(2)}) copy-start(bf16[1024,1024]{1,0:T(8,128)(2,1)} %refs_17_.3) | copy-start | bytes 6291460
  72.0 5.6 %collective-permute-start.28 = (bf16[512,128]{1,0:T(8,128)(2,1)S(1)}, bf16[512,128]{1,0:T(8,128)(2,1)S(1)}, u32[]{:S(2)}, u32[]{:S(2)}) collective-permute-start(bf16[512,128]{1,0:T(8,128)(2,1)S(1)} %collective-permute-done.26.refs_9_), channel_id=1, source_target_pairs={{0,1},{1,0},{2,3},{3,2},{4,5},{5,4},{6,7},{7,6},{8,9},{9,8},{10,11... | collective-permute-start | bytes 393224 | tf_op jit(solution)/shard_map/ppermute | solution.py:526
  72.8 13.0 %collective-permute-start.21 = (bf16[1024,128]{1,0:T(8,128)(2,1)S(1)}, bf16[1024,128]{1,0:T(8,128)(2,1)S(1)}, u32[]{:S(2)}, u32[]{:S(2)}) collective-permute-start(bf16[1024,128]{1,0:T(8,128)(2,1)S(1)} %get-tuple-element.94), channel_id=1, source_target_pairs={{0,4},{4,0},{8,12},{12,8},{1,5},{5,1},{9,13},{13,9},{2,6},{6,2},{1... | collective-permute-start | bytes 786440 | tf_op jit(solution)/shard_map/ppermute | solution.py:520
  73.9 12.8 %collective-permute-start.16 = (bf16[1024,128]{1,0:T(8,128)(2,1)S(1)}, bf16[1024,128]{1,0:T(8,128)(2,1)S(1)}, u32[]{:S(2)}, u32[]{:S(2)}) collective-permute-start(bf16[1024,128]{1,0:T(8,128)(2,1)S(1)} %get-tuple-element.86), channel_id=1, source_target_pairs={{0,8},{4,12},{8,0},{12,4},{1,9},{5,13},{9,1},{13,5},{2,10},{6,14},... | collective-permute-start | bytes 786440 | tf_op jit(solution)/shard_map/ppermute | solution.py:520
  75.5 20.6 %collective-permute-start.17 = (bf16[1024,128]{1,0:T(8,128)(2,1)S(1)}, bf16[1024,128]{1,0:T(8,128)(2,1)S(1)}, u32[]{:S(2)}, u32[]{:S(2)}) collective-permute-start(bf16[1024,128]{1,0:T(8,128)(2,1)S(1)} %get-tuple-element.87), channel_id=1, source_target_pairs={{0,12},{4,8},{8,4},{12,0},{1,13},{5,9},{9,5},{13,1},{2,14},{6,10},... | collective-permute-start | bytes 786440 | tf_op jit(solution)/shard_map/ppermute | solution.py:520
  76.6 19.5 %collective-permute-start.13 = (bf16[4,288,128]{2,1,0:T(8,128)(2,1)S(1)}, bf16[4,288,128]{2,1,0:T(8,128)(2,1)S(1)}, u32[]{:S(2)}, u32[]{:S(2)}) collective-permute-start(bf16[4,288,128]{2,1,0:T(8,128)(2,1)S(1)} %get-tuple-element.75), channel_id=1, source_target_pairs={{0,1},{1,0},{2,3},{3,2},{4,5},{5,4},{6,7},{7,6},{8,9},{9,8},{10,11... | collective-permute-start | bytes 884744 | tf_op jit(solution)/shard_map/ppermute | solution.py:526
  77.6 1.4 %collective-permute-start.29 = (bf16[512,128]{1,0:T(8,128)(2,1)S(1)}, bf16[512,128]{1,0:T(8,128)(2,1)S(1)}, u32[]{:S(2)}, u32[]{:S(2)}) collective-permute-start(bf16[512,128]{1,0:T(8,128)(2,1)S(1)} %collective-permute-done.14.refs_10_), channel_id=1, source_target_pairs={{0,1},{1,0},{2,3},{3,2},{4,5},{5,4},{6,7},{7,6},{8,9},{9,8},{10,11... | collective-permute-start | bytes 393224 | tf_op jit(solution)/shard_map/ppermute | solution.py:526
  79.0 23.0 %collective-permute-start.22 = (bf16[1024,128]{1,0:T(8,128)(2,1)S(1)}, bf16[1024,128]{1,0:T(8,128)(2,1)S(1)}, u32[]{:S(2)}, u32[]{:S(2)}) collective-permute-start(bf16[1024,128]{1,0:T(8,128)(2,1)S(1)} %get-tuple-element.93.refs_0_), channel_id=1, source_target_pairs={{0,1},{1,0},{2,3},{3,2},{4,5},{5,4},{6,7},{7,6},{8,9},{9,8},{10,11... | collective-permute-start | bytes 786440 | tf_op jit(solution)/shard_map/ppermute | solution.py:526
  85.8 17.8 %collective-permute-start.23 = (bf16[1024,128]{1,0:T(8,128)(2,1)S(1)}, bf16[1024,128]{1,0:T(8,128)(2,1)S(1)}, u32[]{:S(2)}, u32[]{:S(2)}) collective-permute-start(bf16[1024,128]{1,0:T(8,128)(2,1)S(1)} %collective-permute-done.21.refs_1_), channel_id=1, source_target_pairs={{0,1},{1,0},{2,3},{3,2},{4,5},{5,4},{6,7},{7,6},{8,9},{9,8},{10,11... | collective-permute-start | bytes 786440 | tf_op jit(solution)/shard_map/ppermute | solution.py:526
  86.7 18.2 %collective-permute-start.24 = (bf16[1024,128]{1,0:T(8,128)(2,1)S(1)}, bf16[1024,128]{1,0:T(8,128)(2,1)S(1)}, u32[]{:S(2)}, u32[]{:S(2)}) collective-permute-start(bf16[1024,128]{1,0:T(8,128)(2,1)S(1)} %collective-permute-done.16.refs_2_), channel_id=1, source_target_pairs={{0,1},{1,0},{2,3},{3,2},{4,5},{5,4},{6,7},{7,6},{8,9},{9,8},{10,11... | collective-permute-start | bytes 786440 | tf_op jit(solution)/shard_map/ppermute | solution.py:526
  96.2 8.7 %collective-permute-start.25 = (bf16[1024,128]{1,0:T(8,128)(2,1)S(1)}, bf16[1024,128]{1,0:T(8,128)(2,1)S(1)}, u32[]{:S(2)}, u32[]{:S(2)}) collective-permute-start(bf16[1024,128]{1,0:T(8,128)(2,1)S(1)} %collective-permute-done.17.refs_3_), channel_id=1, source_target_pairs={{0,1},{1,0},{2,3},{3,2},{4,5},{5,4},{6,7},{7,6},{8,9},{9,8},{10,11... | collective-permute-start | bytes 786440 | tf_op jit(solution)/shard_map/ppermute | solution.py:526
  96.2 1.7 %collective-permute-start.30 = (bf16[512,128]{1,0:T(8,128)(2,1)S(1)}, bf16[512,128]{1,0:T(8,128)(2,1)S(1)}, u32[]{:S(2)}, u32[]{:S(2)}) collective-permute-start(bf16[512,128]{1,0:T(8,128)(2,1)S(1)} %collective-permute-done.15.refs_11_), channel_id=1, source_target_pairs={{0,1},{1,0},{2,3},{3,2},{4,5},{5,4},{6,7},{7,6},{8,9},{9,8},{10,11... | collective-permute-start | bytes 393224 | tf_op jit(solution)/shard_map/ppermute | solution.py:526
  96.7 8.2 %copy-start = (bf16[1024,1024]{1,0:T(8,128)(2,1)S(1)}, bf16[1024,1024]{1,0:T(8,128)(2,1)}, u32[]{:S(2)}) copy-start(bf16[1024,1024]{1,0:T(8,128)(2,1)} %refs_18_.3) | copy-start | bytes 6291460
  96.7 8.2 %copy-start.1 = (bf16[1024,1024]{1,0:T(8,128)(2,1)S(1)}, bf16[1024,1024]{1,0:T(8,128)(2,1)}, u32[]{:S(2)}) copy-start(bf16[1024,1024]{1,0:T(8,128)(2,1)} %refs_16_.3) | copy-start | bytes 6291460
  97.9 17.3 %collective-permute-start.18 = (bf16[576,128]{1,0:T(8,128)(2,1)S(1)}, bf16[576,128]{1,0:T(8,128)(2,1)S(1)}, u32[]{:S(2)}, u32[]{:S(2)}) collective-permute-start(bf16[576,128]{1,0:T(8,128)(2,1)S(1)} %get-tuple-element.89), channel_id=1, source_target_pairs={{0,4},{4,0},{8,12},{12,8},{1,5},{5,1},{9,13},{13,9},{2,6},{6,2},{1... | collective-permute-start | bytes 442376 | tf_op jit(solution)/shard_map/ppermute | solution.py:520
  102.0 13.2 %collective-permute-start.19 = (bf16[576,128]{1,0:T(8,128)(2,1)S(1)}, bf16[576,128]{1,0:T(8,128)(2,1)S(1)}, u32[]{:S(2)}, u32[]{:S(2)}) collective-permute-start(bf16[576,128]{1,0:T(8,128)(2,1)S(1)} %get-tuple-element.90), channel_id=1, source_target_pairs={{0,8},{4,12},{8,0},{12,4},{1,9},{5,13},{9,1},{13,5},{2,10},{6,14},... | collective-permute-start | bytes 442376 | tf_op jit(solution)/shard_map/ppermute | solution.py:520
  103.6 11.6 %collective-permute-start.20 = (bf16[576,128]{1,0:T(8,128)(2,1)S(1)}, bf16[576,128]{1,0:T(8,128)(2,1)S(1)}, u32[]{:S(2)}, u32[]{:S(2)}) collective-permute-start(bf16[576,128]{1,0:T(8,128)(2,1)S(1)} %get-tuple-element.91), channel_id=1, source_target_pairs={{0,12},{4,8},{8,4},{12,0},{1,13},{5,9},{9,5},{13,1},{2,14},{6,10},... | collective-permute-start | bytes 442376 | tf_op jit(solution)/shard_map/ppermute | solution.py:520
  107.8 15.1 %collective-permute-start.31 = (bf16[256,1024]{1,0:T(8,128)(2,1)S(1)}, bf16[256,1024]{1,0:T(8,128)(2,1)S(1)}, u32[]{:S(2)}, u32[]{:S(2)}) collective-permute-start(bf16[256,1024]{1,0:T(8,128)(2,1)S(1)} %shard_map.104), channel_id=1, source_target_pairs={{0,1},{1,3},{3,2},{2,0},{4,5},{5,7},{7,6},{6,4},{8,9},{9,11},{11,1... | collective-permute-start | bytes 1572872 | tf_op jit(solution)/shard_map/ppermute | solution.py:644
  111.9 10.9 %collective-permute-start.32 = (bf16[256,1024]{1,0:T(8,128)(2,1)S(1)}, bf16[256,1024]{1,0:T(8,128)(2,1)S(1)}, u32[]{:S(2)}, u32[]{:S(2)}) collective-permute-start(bf16[256,1024]{1,0:T(8,128)(2,1)S(1)} %shard_map.105.kept_ref), channel_id=1, source_target_pairs={{1,2},{2,1},{5,6},{6,5},{9,10},{10,9},{13,14},{14,13},{17,18},{18,... | collective-permute-start | bytes 1572872 | tf_op jit(solution)/shard_map/ppermute | solution.py:646

commit v11 on v10

--- a/solution.py
+++ b/solution.py
@@ -311,6 +311,14 @@
             id_cols[at, :] = jnp.broadcast_to(ids, (head_dim, rows)).T
 
 
+def order_rows(place, parts, rows, ordered):
+    height = parts[0].shape[0] // 2
+    for offset, part in enumerate(parts):
+        for core in range(2):
+            at = pl.ds(pl.multiple_of(((place ^ offset) * 2 + core) * rows, rows), rows)
+            ordered[at, :] = part[core * height : core * height + rows, :]
+
+
 def block_scores(factor, block, rows, queries, keys_in, id_rows, id_cols):
     head_dim = queries.shape[1]
     seen = (block + 1) * rows
@@ -333,73 +341,34 @@
 
 
 def value_grad_kernel(factor, chips, rows, place_ref, *refs):
-    packed, grads = refs[:chips], refs[chips : 2 * chips]
-    out_refs, lse_ref = refs[2 * chips : 3 * chips], refs[3 * chips]
-    queries, keys_in, grad_rows, id_rows, id_cols, total_ref = refs[3 * chips + 1 :]
+    packed, grads, rank_ref = refs[:chips], refs[chips : 2 * chips], refs[2 * chips]
+    refs = refs[2 * chips + 1 :]
+    out_refs, probs_ref, sums_ref = refs[:chips], refs[chips], refs[chips + 1]
+    queries, keys_in, grad_rows, id_rows, id_cols, total_ref = refs[chips + 2 :]
+    head_dim = queries.shape[1]
+    clusters = rank_ref.shape[1]
     tall = 2 * rows
     place = place_ref[0]
     in_order(place, packed, 0, queries)
     in_order(place, packed, tall, keys_in)
     order_grads(place, grads, rows, grad_rows, id_rows, id_cols)
     total_ref[...] = jnp.zeros_like(total_ref)
+    stored = 0
     for block in range(2 * chips):
         seen = (block + 1) * rows
         scores = block_scores(factor, block, rows, queries, keys_in, id_rows, id_cols)
         top = jnp.max(scores, axis=0, keepdims=True)
         expd = jnp.exp2(scores - top)
         total = jnp.sum(expd, axis=0, keepdims=True)
-        lse_ref[block : block + 1, :] = top + jnp.log2(total)
+        probs_low = (expd * (1.0 / total)).astype(jnp.bfloat16)
+        probs_ref[stored : stored + seen, :] = probs_low
+        stored += seen
         total_ref[:seen, :] += jnp.dot(
-            (expd * (1.0 / total)).astype(jnp.bfloat16),
-            grad_rows[block * rows : seen, :],
-            preferred_element_type=jnp.float32,
+            probs_low, grad_rows[block * rows : seen, :], preferred_element_type=jnp.float32
         )
     for offset, out_ref in enumerate(out_refs):
         at = pl.multiple_of((place ^ offset) * tall, tall)
         out_ref[...] = total_ref[pl.ds(at, tall), :].astype(jnp.bfloat16)
-
-
-def query_grad_kernel(factor, scale, chips, rows, place_ref, *refs):
-    packed, valued, grads = refs[:chips], refs[chips : 2 * chips], refs[2 * chips : 3 * chips]
-    lse_ref, rank_ref = refs[3 * chips : 3 * chips + 2]
-    refs = refs[3 * chips + 2 :]
-    grad_refs, out_refs, refs = refs[:chips], refs[chips : chips + 2], refs[chips + 2 :]
-    queries, keys_in, values, grad_rows, id_rows, id_cols, total_ref, dq_ref, attended_ref = refs
-    head_dim = queries.shape[1]
-    clusters = rank_ref.shape[1]
-    tall = 2 * rows
-    place = place_ref[0]
-    in_order(place, packed, 0, queries)
-    in_order(place, packed, tall, keys_in)
-    in_order(place, valued, 0, values)
-    order_grads(place, grads, rows, grad_rows, id_rows, id_cols)
-    total_ref[...] = jnp.zeros_like(total_ref)
-    for block in range(2 * chips):
-        seen = (block + 1) * rows
-        mine = slice(block * rows, seen)
-        scores = block_scores(factor, block, rows, queries, keys_in, id_rows, id_cols)
-        probs = jnp.exp2(scores - lse_ref[block : block + 1, :])
-        seen_values = values[:seen, :]
-        grad_probs = lax.dot_general(
-            seen_values, grad_rows[mine, :], contract_last, preferred_element_type=jnp.float32
-        )
-        flipped = lax.dot_general(
-            seen_values,
-            probs.astype(jnp.bfloat16),
-            contract_first,
-            preferred_element_type=jnp.float32,
-        )
-        attended_ref[mine, :] = flipped.T.astype(jnp.bfloat16)
-        weighted = probs * grad_probs
-        delta = jnp.sum(weighted, axis=0, keepdims=True)
-        grad_low = (weighted - probs * delta).astype(jnp.bfloat16)
-        total_ref[:seen, :] += jnp.dot(
-            grad_low, queries[mine, :], preferred_element_type=jnp.float32
-        )
-        flipped = lax.dot_general(
-            keys_in[:seen, :], grad_low, contract_first, preferred_element_type=jnp.float32
-        )
-        dq_ref[mine, :] = (flipped.T * scale).astype(jnp.bfloat16)
     sums = jnp.zeros((clusters, head_dim), jnp.float32)
     cluster_at = lax.broadcasted_iota(jnp.int32, (clusters, rows), 0).astype(jnp.float32)
     for block in range(2 * chips):
@@ -415,32 +384,81 @@
     rank_at = lax.broadcasted_iota(jnp.int32, (clusters, clusters), 0)
     ordered = jnp.where(rank_at == rank_ref[...], 1.0, 0.0).astype(jnp.bfloat16)
     ranked = jnp.dot(ordered, sums.astype(jnp.bfloat16), preferred_element_type=jnp.float32)
-    attended_ref[2 * chips * rows :, :] = ranked.astype(jnp.bfloat16)
-    owned = clusters // (2 * chips)
+    sums_ref[...] = ranked.astype(jnp.bfloat16)
+
+
+def query_grad_kernel(scale, chips, rows, place_ref, *refs):
+    packed, valued, grads = refs[:chips], refs[chips : 2 * chips], refs[2 * chips : 3 * chips]
+    probs_ref, sums_ref = refs[3 * chips : 3 * chips + 2]
+    refs = refs[3 * chips + 2 :]
+    grad_refs, out_refs, refs = refs[:chips], refs[chips : chips + 2], refs[chips + 2 :]
+    queries, keys_in, values, grad_rows, total_ref, dq_ref, attended_ref = refs
+    tall = 2 * rows
+    place = place_ref[0]
+    in_order(place, packed, 0, queries)
+    in_order(place, packed, tall, keys_in)
+    in_order(place, valued, 0, values)
+    order_rows(place, grads, rows, grad_rows)
+    total_ref[...] = jnp.zeros_like(total_ref)
+    stored = 0
+    for block in range(2 * chips):
+        seen = (block + 1) * rows
+        mine = slice(block * rows, seen)
+        probs_low = probs_ref[stored : stored + seen, :]
+        stored += seen
+        seen_values = values[:seen, :]
+        grad_probs = lax.dot_general(
+            seen_values, grad_rows[mine, :], contract_last, preferred_element_type=jnp.float32
+        )
+        flipped = lax.dot_general(
+            seen_values, probs_low, contract_first, preferred_element_type=jnp.float32
+        )
+        attended_ref[mine, :] = flipped.T.astype(jnp.bfloat16)
+        probs = probs_low.astype(jnp.float32)
+        weighted = probs * grad_probs
+        delta = jnp.sum(weighted, axis=0, keepdims=True)
+        grad_low = (weighted - probs * delta).astype(jnp.bfloat16)
+        total_ref[:seen, :] += jnp.dot(
+            grad_low, queries[mine, :], preferred_element_type=jnp.float32
+        )
+        flipped = lax.dot_general(
+            keys_in[:seen, :], grad_low, contract_first, preferred_element_type=jnp.float32
+        )
+        dq_ref[mine, :] = (flipped.T * scale).astype(jnp.bfloat16)
     for offset in range(chips):
         at = pl.ds(pl.multiple_of((place ^ offset) * tall, tall), tall)
         grad_refs[offset][:tall, :] = dq_ref[at, :]
         grad_refs[offset][tall:, :] = (total_ref[at, :] * scale).astype(jnp.bfloat16)
+    owned = sums_ref.shape[0] // (2 * chips)
     for turn, out_ref in enumerate(out_refs):
         for chip in range(chips):
             shard = chip * 2 + (place_ref[1] ^ turn)
             at = pl.ds(pl.multiple_of(shard * rows, rows), rows)
             out_ref[chip, :rows, :] = attended_ref[at, :]
-            at = pl.ds(pl.multiple_of(2 * chips * rows + shard * owned, owned), owned)
-            out_ref[chip, rows:, :] = attended_ref[at, :]
+            at = pl.ds(pl.multiple_of(shard * owned, owned), owned)
+            out_ref[chip, rows:, :] = sums_ref[at, :]
+
+
+def join_kernel(*refs):
+    parts, out_ref = refs[1:-1], refs[-1]
+    for offset, part in enumerate(parts):
+        out_ref[offset] = part[...]
 
 
 def input_kernel(chips, which, place_ref, *refs):
-    weights, (out_ref, gathered_ref) = refs[4 * chips : -2], refs[-2:]
+    valued_other_ref, refs = refs[3 * chips], refs[: 3 * chips] + refs[3 * chips + 1 :]
+    weights, (out_ref, gathered_ref) = refs[3 * chips : -2], refs[-2:]
     rows, width = out_ref.shape[0], weights[0].shape[1]
     head_dim = width // (2 * chips)
     for turn in range(2):
         parts = refs[turn * chips : (turn + 1) * chips]
-        valued = refs[(2 + turn) * chips : (3 + turn) * chips]
+        valued = refs[2 * chips : 3 * chips]
         for offset in range(chips):
             head = (place_ref[1] ^ turn) * chips + (place_ref[0] ^ offset)
             for index in range(3):
                 source = parts[offset] if index < 2 else valued[offset]
+                if index == 2 and turn == 1:
+                    source = valued_other_ref.at[offset]
                 at = pl.multiple_of((2 * (index % 2) + place_ref[which]) * rows, rows)
                 start = pl.multiple_of(index * width + head * head_dim, head_dim)
                 gathered_ref[:, pl.ds(start, head_dim)] = source[pl.ds(at, rows), :]
@@ -584,32 +602,33 @@
         return pltpu.VMEM((tokens, head_dim), kind)
 
     id_scratch = [pltpu.VMEM((count, 8, rows), jnp.float32), held(jnp.float32)]
-    *value_grads, lse = call(
+    *value_grads, probs, sums = call(
         partial(value_grad_kernel, factor, chips, rows),
-        (*buffers(2 * rows), jax.ShapeDtypeStruct((count, rows), jnp.float32)),
+        (
+            *buffers(2 * rows),
+            pltpu.VMEM((count * (count + 1) // 2 * rows, rows), jnp.bfloat16),
+            low(clusters, head_dim),
+        ),
         place,
         *packed,
         *grads,
+        cluster_rank.reshape(1, clusters),
         scratch=[held(jnp.bfloat16)] * 3 + id_scratch + [held(jnp.float32)],
         takes=7,
     )
     value_back = exchange(value_grads)
     results = call(
-        partial(query_grad_kernel, factor, scale, chips, rows),
+        partial(query_grad_kernel, scale, chips, rows),
         (*buffers(4 * rows), *(low(chips, rows + owned, head_dim),) * 2),
         place,
         *packed,
         *valued,
         *grads,
-        lse,
-        cluster_rank.reshape(1, clusters),
+        probs,
+        sums,
         scratch=[held(jnp.bfloat16)] * 4
-        + id_scratch
-        + [
-            held(jnp.float32),
-            held(jnp.bfloat16),
-            pltpu.VMEM((tokens + clusters, head_dim), jnp.bfloat16),
-        ],
+        + [held(jnp.float32)]
+        + [held(jnp.bfloat16)] * 2,
         takes=10,
     )
     *ready, _, _ = lax.optimization_barrier((*results[:chips], value_back[2], value_back[3]))
@@ -619,8 +638,11 @@
     outputs = call(
         merge_kernel, buffers(2 * (rows + owned)), place, attended_mine, to_sibling(attended_theirs)
     )
+    back = (lax.optimization_barrier((back[0], outputs[0]))[0], *back[1:])
     back_other = tuple(to_sibling(part) for part in back)
-    value_other = tuple(to_sibling(part) for part in value_back)
+    value_other = to_sibling(
+        call(join_kernel, low(chips, 2 * rows, head_dim), place, *value_back)
+    )
 
     def input_part(which, place):
         return call(
@@ -630,7 +652,7 @@
             *back,
             *back_other,
             *value_back,
-            *value_other,
+            value_other,
             w_query,
             w_key,
             w_value,

time: 125 us -> 121 us (0.968)
  starting transfers between devices: 57.8 us -> 50.1 us
  waiting for transfers between devices: 26.9 us -> 31.8 us
    ppermute x13 -> x10, starting transfers between devices: 16.4 us -> 7.95 us  [to_sibling(): return lax.ppermute(piece, 'sub', swap)]
    ppermute x18, waiting for transfers between devices: 17.7 us -> 24.5 us  [exchange(): lax.ppermute(parts[offset], 'seq', [(at, at ^ offset) for at in range(chi...]
    ppermute x13 -> x10, waiting for transfers between devices: 3.15 us -> 1.21 us  [to_sibling(): return lax.ppermute(piece, 'sub', swap)]
    pallas_call x13 -> x14, Pallas kernels: 38.7 us -> 38.3 us  [call(): pl.pallas_call(kernel, out_shape=outs, in_specs=[smem] + [vmem] * (len(op...]
  transfers between devices with their start and end apart: 33 -> 30, of which waited for: 7 -> 6; matrix products, arithmetic and copies ran while one was open for 0% -> 0% of each run, Pallas kernels for 27% -> 28%
where the time goes in v11:
time: 121 us
  starting transfers between devices  50.1 us (41%)
  Pallas kernels  38.3 us (32%)
  waiting for transfers between devices  31.8 us (26%)
    pallas_call x14, Pallas kernels, call(): pl.pallas_call(kernel, out_shape=outs, in_specs=[smem] + [vmem] * (len(op...  38.3 us
    ppermute x18, starting transfers between devices, exchange(): lax.ppermute(parts[offset], 'seq', [(at, at ^ offset) for at in range(chi...  37.6 us
    ppermute x18, waiting for transfers between devices, exchange(): lax.ppermute(parts[offset], 'seq', [(at, at ^ offset) for at in range(chi...  24.5 us
    ppermute x10, starting transfers between devices, to_sibling(): return lax.ppermute(piece, 'sub', swap)  7.95 us
    ppermute x1, waiting for transfers between devices, by_head(): second = lax.ppermute(kept, square, [(1, 2), (2, 1)])  6.1 us
    ppermute x1, starting transfers between devices, by_head(): second = lax.ppermute(kept, square, [(1, 2), (2, 1)])  3.33 us
  transfers between devices with their start and end apart: 30, of which 6 were waited for; matrix products, arithmetic and copies ran while one was open for 0% of the time, Pallas kernels for 28%

profile of v11, /device:TPU:1, one launch (start us, length us, event | category | flops | bytes accessed | tf_op | source)
XLA Modules:
  0.0 121.1 jit_solution(5443864712088543268)
XLA Ops:
  0.6 0.1 collective-permute-start
  0.8 0.1 pad_add_fusion.place_ref.refs_0_
  0.8 1.7 %shard_map.94 = (bf16[4,272,128]{2,1,0:T(8,128)(2,1)S(1)}, bf16[4,272,128]{2,1,0:T(8,128)(2,1)S(1)}) custom-call(s32[4]{0:T(128)S(1)} %pad_add_fusion.place_ref.refs_0_, bf16[256,1024]{1,0:T(8,128)(2,1)} %grads_ref.1, s32[8,256]{1,0:T(8,128)} %assign_ref.1), custom_call_target="tpu_custom_call" | custom-call | flops 1150000000 | bytes 1048576 | tf_op jit(solution)/shard_map/pallas_call | solution.py:518
  2.5 0.5 collective-permute-start.1
  3.1 1.2 collective-permute-done.1.theirs_ref
  4.2 0.6 shard_map.95
  4.8 0.0 collective-permute-done.refs_1_.refs_2_
  4.8 3.4 %shard_map.96 = bf16[2,512,512]{2,1,0:T(8,128)(2,1)S(1)} custom-call(s32[4]{0:T(128)S(1)} %pad_add_fusion.place_ref.refs_0_, bf16[256,2048]{1,0:T(8,128)(2,1)} %refs_1_.3, bf16[256,2048]{1,0:T(8,128)(2,1)S(1)} %collective-permute-done.refs_1_.refs_2_, bf16[1024,1024]{1,0:T(8,128)(2,1)} %refs_13_.3, bf16[1024,1024]{1,0:T(8,128)(2,1)} %refs_14_.3), custom_call_target="tpu_custom_call" | custom-call | flops 115000000 | bytes 1048576 | tf_op jit(solution)/shard_map/pallas_call | solution.py:518
  8.3 0.4 collective-permute-start.2
  8.7 3.4 %collective-permute-start.7 = (bf16[544,128]{1,0:T(8,128)(2,1)S(1)}, bf16[544,128]{1,0:T(8,128)(2,1)S(1)}, u32[]{:S(2)}, u32[]{:S(2)}) collective-permute-start(bf16[544,128]{1,0:T(8,128)(2,1)S(1)} %get-tuple-element.63), channel_id=1, source_target_pairs={{0,8},{4,12},{8,0},{12,4},{1,9},{5,13},{9,1},{13,5},{2,10},{6,14},... | collective-permute-start | bytes 417800 | tf_op jit(solution)/shard_map/ppermute | solution.py:538
  12.1 1.1 collective-permute-start.8
  13.2 2.7 %shard_map.98 = bf16[1,512,512]{2,1,0:T(8,128)(2,1)S(1)} custom-call(s32[4]{0:T(128)S(1)} %pad_add_fusion.place_ref.refs_0_, bf16[256,2048]{1,0:T(8,128)(2,1)} %refs_1_.3, bf16[256,2048]{1,0:T(8,128)(2,1)S(1)} %collective-permute-done.refs_1_.refs_2_, bf16[1024,1024]{1,0:T(8,128)(2,1)} %refs_15_.3), custom_call_target="tpu_custom_call" | custom-call | flops 115000000 | bytes 1048576 | tf_op jit(solution)/shard_map/pallas_call | solution.py:518
  15.9 1.0 collective-permute-start.6
  16.9 0.0 collective-permute-done.2.refs_0_
  16.9 3.6 %shard_map.97 = (bf16[1024,128]{1,0:T(8,128)(2,1)S(1)}, bf16[1024,128]{1,0:T(8,128)(2,1)S(1)}, bf16[1024,128]{1,0:T(8,128)(2,1)S(1)}, bf16[1024,128]{1,0:T(8,128)(2,1)S(1)}) custom-call(s32[4]{0:T(128)S(1)} %pad_add_fusion.place_ref.refs_0_, bf16[2,512,512]{2,1,0:T(8,128)(2,1)S(1)} %collective-permute-done.2.refs_0_, bf16[256,2048]{1,0:T(8,128)(2,1)} %refs_1_.3, ...), custom_call_target="tpu_custom_call" | custom-call | flops 9200000000 | bytes 1048576 | tf_op jit(solution)/shard_map/pallas_call | solution.py:518
  20.5 0.1 collective-permute-start.3
  20.6 2.5 %collective-permute-start.4 = (bf16[1024,128]{1,0:T(8,128)(2,1)S(1)}, bf16[1024,128]{1,0:T(8,128)(2,1)S(1)}, u32[]{:S(2)}, u32[]{:S(2)}) collective-permute-start(bf16[1024,128]{1,0:T(8,128)(2,1)S(1)} %get-tuple-element.61), channel_id=1, source_target_pairs={{0,8},{4,12},{8,0},{12,4},{1,9},{5,13},{9,1},{13,5},{2,10},{6,14},... | collective-permute-start | bytes 786440 | tf_op jit(solution)/shard_map/ppermute | solution.py:538
  23.0 0.0 collective-permute-done.7.refs_6_.refs_10_
  23.0 2.5 %collective-permute-start.5 = (bf16[1024,128]{1,0:T(8,128)(2,1)S(1)}, bf16[1024,128]{1,0:T(8,128)(2,1)S(1)}, u32[]{:S(2)}, u32[]{:S(2)}) collective-permute-start(bf16[1024,128]{1,0:T(8,128)(2,1)S(1)} %get-tuple-element.62), channel_id=1, source_target_pairs={{0,12},{4,8},{8,4},{12,0},{1,13},{5,9},{9,5},{13,1},{2,14},{6,10},... | collective-permute-start | bytes 786440 | tf_op jit(solution)/shard_map/ppermute | solution.py:538
  25.5 0.0 collective-permute-done.8.refs_7_.refs_11_
  25.5 0.2 collective-permute-start.12
  25.7 0.0 collective-permute-done.6.refs_0_
  25.7 2.8 %shard_map.99 = (bf16[512,128]{1,0:T(8,128)(2,1)S(1)}, bf16[512,128]{1,0:T(8,128)(2,1)S(1)}, bf16[512,128]{1,0:T(8,128)(2,1)S(1)}, bf16[512,128]{1,0:T(8,128)(2,1)S(1)}) custom-call(s32[4]{0:T(128)S(1)} %pad_add_fusion.place_ref.refs_0_, bf16[1,512,512]{2,1,0:T(8,128)(2,1)S(1)} %collective-permute-done.6.refs_0_, bf16[256,2048]{1,0:T(8,128)(2,1)} %refs_1_.3, ...), custom_call_target="tpu_custom_call" | custom-call | flops 115000000 | bytes 1048576 | tf_op jit(solution)/shard_map/pallas_call | solution.py:518
  28.6 1.4 %collective-permute-start.9 = (bf16[512,128]{1,0:T(8,128)(2,1)S(1)}, bf16[512,128]{1,0:T(8,128)(2,1)S(1)}, u32[]{:S(2)}, u32[]{:S(2)}) collective-permute-start(bf16[512,128]{1,0:T(8,128)(2,1)S(1)} %get-tuple-element.71), channel_id=1, source_target_pairs={{0,4},{4,0},{8,12},{12,8},{1,5},{5,1},{9,13},{13,9},{2,6},{6,2},{1... | collective-permute-start | bytes 393224 | tf_op jit(solution)/shard_map/ppermute | solution.py:538
  29.9 3.3 %collective-permute-done.3.refs_1_ = bf16[1024,128]{1,0:T(8,128)(2,1)S(1)} collective-permute-done((bf16[1024,128]{1,0:T(8,128)(2,1)S(1)}, bf16[1024,128]{1,0:T(8,128)(2,1)S(1)}, u32[]{:S(2)}, u32[]{:S(2)}) %collective-permute-start.3) | collective-permute-done | bytes 262176 | tf_op jit(solution)/shard_map/ppermute | solution.py:538
  33.2 0.0 collective-permute-start.10
  33.2 8.6 %collective-permute-done.4.refs_2_ = bf16[1024,128]{1,0:T(8,128)(2,1)S(1)} collective-permute-done((bf16[1024,128]{1,0:T(8,128)(2,1)S(1)}, bf16[1024,128]{1,0:T(8,128)(2,1)S(1)}, u32[]{:S(2)}, u32[]{:S(2)}) %collective-permute-start.4) | collective-permute-done | bytes 262176 | tf_op jit(solution)/shard_map/ppermute | solution.py:538
  41.8 3.7 %collective-permute-start.11 = (bf16[512,128]{1,0:T(8,128)(2,1)S(1)}, bf16[512,128]{1,0:T(8,128)(2,1)S(1)}, u32[]{:S(2)}, u32[]{:S(2)}) collective-permute-start(bf16[512,128]{1,0:T(8,128)(2,1)S(1)} %get-tuple-element.73), channel_id=1, source_target_pairs={{0,12},{4,8},{8,4},{12,0},{1,13},{5,9},{9,5},{13,1},{2,14},{6,10},... | collective-permute-start | bytes 393224 | tf_op jit(solution)/shard_map/ppermute | solution.py:538
  45.5 0.0 collective-permute-done.5.refs_3_
  45.5 0.0 collective-permute-done.12.refs_5_.refs_9_
  45.5 6.5 %shard_map.100 = (bf16[512,128]{1,0:T(8,128)(2,1)S(1)}, bf16[512,128]{1,0:T(8,128)(2,1)S(1)}, bf16[512,128]{1,0:T(8,128)(2,1)S(1)}, bf16[512,128]{1,0:T(8,128)(2...) custom-call(s32[4]{0:T(128)S(1)} %pad_add_fusion.place_ref.refs_0_, ...), custom_call_target="tpu_custom_call" | custom-call | flops 8049999872 | bytes 1048576 | tf_op jit(solution)/shard_map/pallas_call | solution.py:518
  51.9 10.4 %collective-permute-start.14 = (bf16[512,128]{1,0:T(8,128)(2,1)S(1)}, bf16[512,128]{1,0:T(8,128)(2,1)S(1)}, u32[]{:S(2)}, u32[]{:S(2)}) collective-permute-start(bf16[512,128]{1,0:T(8,128)(2,1)S(1)} %get-tuple-element.87), channel_id=1, source_target_pairs={{0,8},{4,12},{8,0},{12,4},{1,9},{5,13},{9,1},{13,5},{2,10},{6,14},... | collective-permute-start | bytes 393224 | tf_op jit(solution)/shard_map/ppermute | solution.py:538
  62.3 0.2 collective-permute-start.15
  62.5 0.0 collective-permute-done.9.refs_5_
  62.5 0.2 collective-permute-start.26
  62.7 0.0 collective-permute-done.10.refs_6_
  62.7 0.0 collective-permute-done.11.refs_7_
  62.7 7.0 %shard_map.101 = (bf16[1024,128]{1,0:T(8,128)(2,1)S(1)}, bf16[1024,128]{1,0:T(8,128)(2,1)S(1)}, bf16[1024,128]{1,0:T(8,128)(2,1)S(1)}, bf16[1024,128]{1,0:T(8,12...) custom-call(s32[4]{0:T(128)S(1)} %pad_add_fusion.place_ref.refs_0_, ...), custom_call_target="tpu_custom_call" | custom-call | flops 11500000256 | bytes 1048576 | tf_op jit(solution)/shard_map/pallas_call | solution.py:518
  69.7 1.3 %collective-permute-start.13 = (bf16[4,288,128]{2,1,0:T(8,128)(2,1)S(1)}, bf16[4,288,128]{2,1,0:T(8,128)(2,1)S(1)}, u32[]{:S(2)}, u32[]{:S(2)}) collective-permute-start(bf16[4,288,128]{2,1,0:T(8,128)(2,1)S(1)} %get-tuple-element.78), channel_id=1, source_target_pairs={{0,1},{1,0},{2,3},{3,2},{4,5},{5,4},{6,7},{7,6},{8,9},{9,8},{10,11... | collective-permute-start | bytes 884744 | tf_op jit(solution)/shard_map/ppermute | solution.py:544
  71.0 0.8 collective-permute-done.14.refs_3_.refs_10_
  71.8 2.6 %collective-permute-start.16 = (bf16[1024,128]{1,0:T(8,128)(2,1)S(1)}, bf16[1024,128]{1,0:T(8,128)(2,1)S(1)}, u32[]{:S(2)}, u32[]{:S(2)}) collective-permute-start(bf16[1024,128]{1,0:T(8,128)(2,1)S(1)} %get-tuple-element.89), channel_id=1, source_target_pairs={{0,8},{4,12},{8,0},{12,4},{1,9},{5,13},{9,1},{13,5},{2,10},{6,14},... | collective-permute-start | bytes 786440 | tf_op jit(solution)/shard_map/ppermute | solution.py:538
  74.4 2.6 %collective-permute-start.17 = (bf16[1024,128]{1,0:T(8,128)(2,1)S(1)}, bf16[1024,128]{1,0:T(8,128)(2,1)S(1)}, u32[]{:S(2)}, u32[]{:S(2)}) collective-permute-start(bf16[1024,128]{1,0:T(8,128)(2,1)S(1)} %get-tuple-element.90), channel_id=1, source_target_pairs={{0,12},{4,8},{8,4},{12,0},{1,13},{5,9},{9,5},{13,1},{2,14},{6,10},... | collective-permute-start | bytes 786440 | tf_op jit(solution)/shard_map/ppermute | solution.py:538
  76.9 0.0 collective-permute-start.21
  76.9 0.0 collective-permute-done.26.refs_2_.refs_9_
  77.0 0.6 shard_map.104
  77.5 1.3 %collective-permute-start.27 = (bf16[4,512,128]{2,1,0:T(8,128)(2,1)S(1)}, bf16[4,512,128]{2,1,0:T(8,128)(2,1)S(1)}, u32[]{:S(2)}, u32[]{:S(2)}) collective-permute-start(bf16[4,512,128]{2,1,0:T(8,128)(2,1)S(1)} %shard_map.104), channel_id=1, source_target_pairs={{0,1},{1,0},{2,3},{3,2},{4,5},{5,4},{6,7},{7,6},{8,9},{9,8},{10,11... | collective-permute-start | bytes 1572872 | tf_op jit(solution)/shard_map/ppermute | solution.py:544
  78.8 0.6 shard_map.102
  79.4 0.1 collective-permute-start.22
  79.5 11.8 %collective-permute-done.16.refs_2_ = bf16[1024,128]{1,0:T(8,128)(2,1)S(1)} collective-permute-done((bf16[1024,128]{1,0:T(8,128)(2,1)S(1)}, bf16[1024,128]{1,0:T(8,128)(2,1)S(1)}, u32[]{:S(2)}, u32[]{:S(2)}) %collective-permute-start.16) | collective-permute-done | bytes 262176 | tf_op jit(solution)/shard_map/ppermute | solution.py:538
  91.4 2.7 %collective-permute-start.24 = (bf16[1024,128]{1,0:T(8,128)(2,1)S(1)}, bf16[1024,128]{1,0:T(8,128)(2,1)S(1)}, u32[]{:S(2)}, u32[]{:S(2)}) collective-permute-start(bf16[1024,128]{1,0:T(8,128)(2,1)S(1)} %collective-permute-done.16.refs_2_), channel_id=1, source_target_pairs={{0,1},{1,0},{2,3},{3,2},{4,5},{5,4},{6,7},{7,6},{8,9},{9,8},{10,11... | collective-permute-start | bytes 786440 | tf_op jit(solution)/shard_map/ppermute | solution.py:544
  94.1 0.0 collective-permute-start.25
  94.1 0.5 collective-permute-start.23
  94.6 4.3 %collective-permute-start.18 = (bf16[576,128]{1,0:T(8,128)(2,1)S(1)}, bf16[576,128]{1,0:T(8,128)(2,1)S(1)}, u32[]{:S(2)}, u32[]{:S(2)}) collective-permute-start(bf16[576,128]{1,0:T(8,128)(2,1)S(1)} %get-tuple-element.92), channel_id=1, source_target_pairs={{0,4},{4,0},{8,12},{12,8},{1,5},{5,1},{9,13},{13,9},{2,6},{6,2},{1... | collective-permute-start | bytes 442376 | tf_op jit(solution)/shard_map/ppermute | solution.py:538
  98.9 1.5 %collective-permute-start.19 = (bf16[576,128]{1,0:T(8,128)(2,1)S(1)}, bf16[576,128]{1,0:T(8,128)(2,1)S(1)}, u32[]{:S(2)}, u32[]{:S(2)}) collective-permute-start(bf16[576,128]{1,0:T(8,128)(2,1)S(1)} %get-tuple-element.93), channel_id=1, source_target_pairs={{0,8},{4,12},{8,0},{12,4},{1,9},{5,13},{9,1},{13,5},{2,10},{6,14},... | collective-permute-start | bytes 442376 | tf_op jit(solution)/shard_map/ppermute | solution.py:538
  100.4 1.2 collective-permute-start.20
  101.5 0.0 collective-permute-done.23.refs_5_
  101.6 2.9 %shard_map.105 = bf16[256,1024]{1,0:T(8,128)(2,1)S(1)} custom-call(s32[4]{0:T(128)S(1)} %pad_add_fusion.place_ref.refs_0_, bf16[1024,128]{1,0:T(8,128)(2,1)S(1)} %get-tuple-element.97.refs_0_, bf16[1024,128]{1,0:T(8,128)(2,1)S(1)} %collective-permute-done.21.refs_1_, bf16[1024,128]{1,0:T(8,128)(2,1)S(1)} %collective-permute-done.16.refs_2_, ...), custom_call_target="tpu_custom_call" | custom-call | flops 1150000000 | bytes 1048576 | tf_op jit(solution)/shard_map/pallas_call | solution.py:518
  104.5 1.2 %collective-permute-start.28 = (bf16[256,1024]{1,0:T(8,128)(2,1)S(1)}, bf16[256,1024]{1,0:T(8,128)(2,1)S(1)}, u32[]{:S(2)}, u32[]{:S(2)}) collective-permute-start(bf16[256,1024]{1,0:T(8,128)(2,1)S(1)} %shard_map.105), channel_id=1, source_target_pairs={{0,1},{1,3},{3,2},{2,0},{4,5},{5,7},{7,6},{6,4},{8,9},{9,11},{11,1... | collective-permute-start | bytes 1572872 | tf_op jit(solution)/shard_map/ppermute | solution.py:666
  105.7 2.9 %shard_map.106.kept_ref = bf16[256,1024]{1,0:T(8,128)(2,1)S(1)} custom-call(s32[4]{0:T(128)S(1)} %pad_add_fusion.place_ref.refs_0_, bf16[1024,128]{1,0:T(8,128)(2,1)S(1)} %get-tuple-element.97.refs_0_, bf16[1024,128]{1,0:T(8,128)(2,1)S(1)} %collective-permute-done.21.refs_1_, bf16[1024,128]{1,0:T(8,128)(2,1)S(1)} %collective-permute-done.16.refs_2_, ...), custom_call_target="tpu_custom_call" | custom-call | flops 1150000000 | bytes 1048576 | tf_op jit(solution)/shard_map/pallas_call | solution.py:518
  108.6 3.3 %collective-permute-start.29 = (bf16[256,1024]{1,0:T(8,128)(2,1)S(1)}, bf16[256,1024]{1,0:T(8,128)(2,1)S(1)}, u32[]{:S(2)}, u32[]{:S(2)}) collective-permute-start(bf16[256,1024]{1,0:T(8,128)(2,1)S(1)} %shard_map.106.kept_ref), channel_id=1, source_target_pairs={{1,2},{2,1},{5,6},{6,5},{9,10},{10,9},{13,14},{14,13},{17,18},{18,... | collective-permute-start | bytes 1572872 | tf_op jit(solution)/shard_map/ppermute | solution.py:668
  112.0 0.0 collective-permute-done.18.refs_1_
  112.0 1.5 %shard_map.103 = (bf16[256,1024]{1,0:T(8,128)(2,1)}, f32[8,32,128]{2,1,0:T(8,128)}) custom-call(s32[4]{0:T(128)S(1)} %pad_add_fusion.place_ref.refs_0_, bf16[576,128]{1,0:T(8,128)(2,1)S(1)} %get-tuple-element.91.refs_0_, bf16[576,128]{1,0:T(8,128)(2,1)S(1)} %collective-permute-done.18.refs_1_, bf16[576,128]{1,0:T(8,128)(2,1)S(1)} %collective-permute-done.19.refs_2_, ...), custom_call_target="tpu_custom_call" | custom-call | flops 9200000000 | bytes 1048576 | tf_op jit(solution)/shard_map/pallas_call | solution.py:518
  113.5 6.1 %collective-permute-done.29.second_ref = bf16[256,1024]{1,0:T(8,128)(2,1)S(1)} collective-permute-done((bf16[256,1024]{1,0:T(8,128)(2,1)S(1)}, bf16[256,1024]{1,0:T(8,128)(2,1)S(1)}, u32[]{:S(2)}, u32[]{:S(2)}) %collective-permute-start.29) | collective-permute-done | bytes 524320 | tf_op jit(solution)/shard_map/ppermute | solution.py:668
  119.6 1.5 %shard_map.107 = bf16[256,1024]{1,0:T(8,128)(2,1)} custom-call(s32[4]{0:T(128)S(1)} %pad_add_fusion.place_ref.refs_0_, bf16[256,1024]{1,0:T(8,128)(2,1)S(1)} %collective-permute-done.28.first_ref, bf16[256,1024]{1,0:T(8,128)(2,1)S(1)} %collective-permute-done.29.second_ref, bf16[256,1024]{1,0:T(8,128)(2,1)S(1)} %shard_map.106.kept_ref), custom_call_target="tpu_custom_call" | custom-call | flops 1150000000 | bytes 1048576 | tf_op jit(solution)/shard_map/pallas_call | solution.py:518
  (19 shorter events, 0.0 us)
Async XLA Ops:
  0.6 4.2 %collective-permute-start = (bf16[256,2048]{1,0:T(8,128)(2,1)}, bf16[256,2048]{1,0:T(8,128)(2,1)S(1)}, u32[]{:S(2)}, u32[]{:S(2)}) collective-permute-start(bf16[256,2048]{1,0:T(8,128)(2,1)} %refs_1_.3), channel_id=1, source_target_pairs={{0,1},{1,0},{2,3},{3,2},{4,5},{5,4},{6,7},{7,6},{8,9},{9,8},{10,11... | collective-permute-start | bytes 3145736 | tf_op jit(solution)/shard_map/ppermute | solution.py:544
  2.5 1.7 %collective-permute-start.1 = (bf16[4,272,128]{2,1,0:T(8,128)(2,1)S(1)}, bf16[4,272,128]{2,1,0:T(8,128)(2,1)S(1)}, u32[]{:S(2)}, u32[]{:S(2)}) collective-permute-start(bf16[4,272,128]{2,1,0:T(8,128)(2,1)S(1)} %get-tuple-element.55), channel_id=1, source_target_pairs={{0,1},{1,0},{2,3},{3,2},{4,5},{5,4},{6,7},{7,6},{8,9},{9,8},{10,11... | collective-permute-start | bytes 835592 | tf_op jit(solution)/shard_map/ppermute | solution.py:544
  8.3 8.6 %collective-permute-start.2 = (bf16[2,512,512]{2,1,0:T(8,128)(2,1)S(1)}, bf16[2,512,512]{2,1,0:T(8,128)(2,1)S(1)}, u32[]{:S(2)}, u32[]{:S(2)}) collective-permute-start(bf16[2,512,512]{2,1,0:T(8,128)(2,1)S(1)} %shard_map.96), channel_id=1, source_target_pairs={{0,1},{1,0},{2,3},{3,2},{4,5},{5,4},{6,7},{7,6},{8,9},{9,8},{10,11... | collective-permute-start | bytes 3145736 | tf_op jit(solution)/shard_map/ppermute | solution.py:544
  8.7 14.3 %collective-permute-start.7 = (bf16[544,128]{1,0:T(8,128)(2,1)S(1)}, bf16[544,128]{1,0:T(8,128)(2,1)S(1)}, u32[]{:S(2)}, u32[]{:S(2)}) collective-permute-start(bf16[544,128]{1,0:T(8,128)(2,1)S(1)} %get-tuple-element.63), channel_id=1, source_target_pairs={{0,8},{4,12},{8,0},{12,4},{1,9},{5,13},{9,1},{13,5},{2,10},{6,14},... | collective-permute-start | bytes 417800 | tf_op jit(solution)/shard_map/ppermute | solution.py:538
  12.1 13.4 %collective-permute-start.8 = (bf16[544,128]{1,0:T(8,128)(2,1)S(1)}, bf16[544,128]{1,0:T(8,128)(2,1)S(1)}, u32[]{:S(2)}, u32[]{:S(2)}) collective-permute-start(bf16[544,128]{1,0:T(8,128)(2,1)S(1)} %get-tuple-element.64), channel_id=1, source_target_pairs={{0,12},{4,8},{8,4},{12,0},{1,13},{5,9},{9,5},{13,1},{2,14},{6,10},... | collective-permute-start | bytes 417800 | tf_op jit(solution)/shard_map/ppermute | solution.py:538
  15.9 9.8 %collective-permute-start.6 = (bf16[1,512,512]{2,1,0:T(8,128)(2,1)S(1)}, bf16[1,512,512]{2,1,0:T(8,128)(2,1)S(1)}, u32[]{:S(2)}, u32[]{:S(2)}) collective-permute-start(bf16[1,512,512]{2,1,0:T(8,128)(2,1)S(1)} %shard_map.98), channel_id=1, source_target_pairs={{0,1},{1,0},{2,3},{3,2},{4,5},{5,4},{6,7},{7,6},{8,9},{9,8},{10,11... | collective-permute-start | bytes 1572872 | tf_op jit(solution)/shard_map/ppermute | solution.py:544
  20.5 12.7 %collective-permute-start.3 = (bf16[1024,128]{1,0:T(8,128)(2,1)S(1)}, bf16[1024,128]{1,0:T(8,128)(2,1)S(1)}, u32[]{:S(2)}, u32[]{:S(2)}) collective-permute-start(bf16[1024,128]{1,0:T(8,128)(2,1)S(1)} %get-tuple-element.60), channel_id=1, source_target_pairs={{0,4},{4,0},{8,12},{12,8},{1,5},{5,1},{9,13},{13,9},{2,6},{6,2},{1... | collective-permute-start | bytes 786440 | tf_op jit(solution)/shard_map/ppermute | solution.py:538
  20.6 21.2 %collective-permute-start.4 = (bf16[1024,128]{1,0:T(8,128)(2,1)S(1)}, bf16[1024,128]{1,0:T(8,128)(2,1)S(1)}, u32[]{:S(2)}, u32[]{:S(2)}) collective-permute-start(bf16[1024,128]{1,0:T(8,128)(2,1)S(1)} %get-tuple-element.61), channel_id=1, source_target_pairs={{0,8},{4,12},{8,0},{12,4},{1,9},{5,13},{9,1},{13,5},{2,10},{6,14},... | collective-permute-start | bytes 786440 | tf_op jit(solution)/shard_map/ppermute | solution.py:538
  23.0 22.4 %collective-permute-start.5 = (bf16[1024,128]{1,0:T(8,128)(2,1)S(1)}, bf16[1024,128]{1,0:T(8,128)(2,1)S(1)}, u32[]{:S(2)}, u32[]{:S(2)}) collective-permute-start(bf16[1024,128]{1,0:T(8,128)(2,1)S(1)} %get-tuple-element.62), channel_id=1, source_target_pairs={{0,12},{4,8},{8,4},{12,0},{1,13},{5,9},{9,5},{13,1},{2,14},{6,10},... | collective-permute-start | bytes 786440 | tf_op jit(solution)/shard_map/ppermute | solution.py:538
  25.5 19.9 %collective-permute-start.12 = (bf16[544,128]{1,0:T(8,128)(2,1)S(1)}, bf16[544,128]{1,0:T(8,128)(2,1)S(1)}, u32[]{:S(2)}, u32[]{:S(2)}) collective-permute-start(bf16[544,128]{1,0:T(8,128)(2,1)S(1)} %get-tuple-element.74), channel_id=1, source_target_pairs={{0,4},{4,0},{8,12},{12,8},{1,5},{5,1},{9,13},{13,9},{2,6},{6,2},{1... | collective-permute-start | bytes 417800 | tf_op jit(solution)/shard_map/ppermute | solution.py:538
  25.7 19.8 %copy-start.3 = (s32[256]{0:T(256)S(1)}, s32[256]{0:T(256)}, u32[]{:S(2)}) copy-start(s32[256]{0:T(256)} %param.11) | copy-start | bytes 3076
  28.6 33.9 %collective-permute-start.9 = (bf16[512,128]{1,0:T(8,128)(2,1)S(1)}, bf16[512,128]{1,0:T(8,128)(2,1)S(1)}, u32[]{:S(2)}, u32[]{:S(2)}) collective-permute-start(bf16[512,128]{1,0:T(8,128)(2,1)S(1)} %get-tuple-element.71), channel_id=1, source_target_pairs={{0,4},{4,0},{8,12},{12,8},{1,5},{5,1},{9,13},{13,9},{2,6},{6,2},{1... | collective-permute-start | bytes 393224 | tf_op jit(solution)/shard_map/ppermute | solution.py:538
  33.2 29.5 %collective-permute-start.10 = (bf16[512,128]{1,0:T(8,128)(2,1)S(1)}, bf16[512,128]{1,0:T(8,128)(2,1)S(1)}, u32[]{:S(2)}, u32[]{:S(2)}) collective-permute-start(bf16[512,128]{1,0:T(8,128)(2,1)S(1)} %get-tuple-element.72), channel_id=1, source_target_pairs={{0,8},{4,12},{8,0},{12,4},{1,9},{5,13},{9,1},{13,5},{2,10},{6,14},... | collective-permute-start | bytes 393224 | tf_op jit(solution)/shard_map/ppermute | solution.py:538
  41.8 20.9 %collective-permute-start.11 = (bf16[512,128]{1,0:T(8,128)(2,1)S(1)}, bf16[512,128]{1,0:T(8,128)(2,1)S(1)}, u32[]{:S(2)}, u32[]{:S(2)}) collective-permute-start(bf16[512,128]{1,0:T(8,128)(2,1)S(1)} %get-tuple-element.73), channel_id=1, source_target_pairs={{0,12},{4,8},{8,4},{12,0},{1,13},{5,9},{9,5},{13,1},{2,14},{6,10},... | collective-permute-start | bytes 393224 | tf_op jit(solution)/shard_map/ppermute | solution.py:538
  51.9 19.8 %collective-permute-start.14 = (bf16[512,128]{1,0:T(8,128)(2,1)S(1)}, bf16[512,128]{1,0:T(8,128)(2,1)S(1)}, u32[]{:S(2)}, u32[]{:S(2)}) collective-permute-start(bf16[512,128]{1,0:T(8,128)(2,1)S(1)} %get-tuple-element.87), channel_id=1, source_target_pairs={{0,8},{4,12},{8,0},{12,4},{1,9},{5,13},{9,1},{13,5},{2,10},{6,14},... | collective-permute-start | bytes 393224 | tf_op jit(solution)/shard_map/ppermute | solution.py:538
  62.3 9.5 %collective-permute-start.15 = (bf16[512,128]{1,0:T(8,128)(2,1)S(1)}, bf16[512,128]{1,0:T(8,128)(2,1)S(1)}, u32[]{:S(2)}, u32[]{:S(2)}) collective-permute-start(bf16[512,128]{1,0:T(8,128)(2,1)S(1)} %get-tuple-element.88), channel_id=1, source_target_pairs={{0,12},{4,8},{8,4},{12,0},{1,13},{5,9},{9,5},{13,1},{2,14},{6,10},... | collective-permute-start | bytes 393224 | tf_op jit(solution)/shard_map/ppermute | solution.py:538
  62.5 14.5 %collective-permute-start.26 = (bf16[512,128]{1,0:T(8,128)(2,1)S(1)}, bf16[512,128]{1,0:T(8,128)(2,1)S(1)}, u32[]{:S(2)}, u32[]{:S(2)}) collective-permute-start(bf16[512,128]{1,0:T(8,128)(2,1)S(1)} %get-tuple-element.100), channel_id=1, source_target_pairs={{0,4},{4,0},{8,12},{12,8},{1,5},{5,1},{9,13},{13,9},{2,6},{6,2},{1... | collective-permute-start | bytes 393224 | tf_op jit(solution)/shard_map/ppermute | solution.py:538
  69.7 9.1 %collective-permute-start.13 = (bf16[4,288,128]{2,1,0:T(8,128)(2,1)S(1)}, bf16[4,288,128]{2,1,0:T(8,128)(2,1)S(1)}, u32[]{:S(2)}, u32[]{:S(2)}) collective-permute-start(bf16[4,288,128]{2,1,0:T(8,128)(2,1)S(1)} %get-tuple-element.78), channel_id=1, source_target_pairs={{0,1},{1,0},{2,3},{3,2},{4,5},{5,4},{6,7},{7,6},{8,9},{9,8},{10,11... | collective-permute-start | bytes 884744 | tf_op jit(solution)/shard_map/ppermute | solution.py:544
  71.8 19.6 %collective-permute-start.16 = (bf16[1024,128]{1,0:T(8,128)(2,1)S(1)}, bf16[1024,128]{1,0:T(8,128)(2,1)S(1)}, u32[]{:S(2)}, u32[]{:S(2)}) collective-permute-start(bf16[1024,128]{1,0:T(8,128)(2,1)S(1)} %get-tuple-element.89), channel_id=1, source_target_pairs={{0,8},{4,12},{8,0},{12,4},{1,9},{5,13},{9,1},{13,5},{2,10},{6,14},... | collective-permute-start | bytes 786440 | tf_op jit(solution)/shard_map/ppermute | solution.py:538
  74.4 19.7 %collective-permute-start.17 = (bf16[1024,128]{1,0:T(8,128)(2,1)S(1)}, bf16[1024,128]{1,0:T(8,128)(2,1)S(1)}, u32[]{:S(2)}, u32[]{:S(2)}) collective-permute-start(bf16[1024,128]{1,0:T(8,128)(2,1)S(1)} %get-tuple-element.90), channel_id=1, source_target_pairs={{0,12},{4,8},{8,4},{12,0},{1,13},{5,9},{9,5},{13,1},{2,14},{6,10},... | collective-permute-start | bytes 786440 | tf_op jit(solution)/shard_map/ppermute | solution.py:538
  76.9 17.1 %collective-permute-start.21 = (bf16[1024,128]{1,0:T(8,128)(2,1)S(1)}, bf16[1024,128]{1,0:T(8,128)(2,1)S(1)}, u32[]{:S(2)}, u32[]{:S(2)}) collective-permute-start(bf16[1024,128]{1,0:T(8,128)(2,1)S(1)} %get-tuple-element.98), channel_id=1, source_target_pairs={{0,4},{4,0},{8,12},{12,8},{1,5},{5,1},{9,13},{13,9},{2,6},{6,2},{1... | collective-permute-start | bytes 786440 | tf_op jit(solution)/shard_map/ppermute | solution.py:538
  77.0 24.6 %copy-start.2 = (bf16[1024,1024]{1,0:T(8,128)(2,1)S(1)}, bf16[1024,1024]{1,0:T(8,128)(2,1)}, u32[]{:S(2)}) copy-start(bf16[1024,1024]{1,0:T(8,128)(2,1)} %refs_14_.3) | copy-start | bytes 6291460
  77.5 24.0 %collective-permute-start.27 = (bf16[4,512,128]{2,1,0:T(8,128)(2,1)S(1)}, bf16[4,512,128]{2,1,0:T(8,128)(2,1)S(1)}, u32[]{:S(2)}, u32[]{:S(2)}) collective-permute-start(bf16[4,512,128]{2,1,0:T(8,128)(2,1)S(1)} %shard_map.104), channel_id=1, source_target_pairs={{0,1},{1,0},{2,3},{3,2},{4,5},{5,4},{6,7},{7,6},{8,9},{9,8},{10,11... | collective-permute-start | bytes 1572872 | tf_op jit(solution)/shard_map/ppermute | solution.py:544
  78.8 22.7 %copy-start = (bf16[1024,1024]{1,0:T(8,128)(2,1)S(1)}, bf16[1024,1024]{1,0:T(8,128)(2,1)}, u32[]{:S(2)}) copy-start(bf16[1024,1024]{1,0:T(8,128)(2,1)} %refs_15_.3) | copy-start | bytes 6291460
  78.8 22.7 %copy-start.1 = (bf16[1024,1024]{1,0:T(8,128)(2,1)S(1)}, bf16[1024,1024]{1,0:T(8,128)(2,1)}, u32[]{:S(2)}) copy-start(bf16[1024,1024]{1,0:T(8,128)(2,1)} %refs_13_.3) | copy-start | bytes 6291460
  79.4 15.2 %collective-permute-start.22 = (bf16[1024,128]{1,0:T(8,128)(2,1)S(1)}, bf16[1024,128]{1,0:T(8,128)(2,1)S(1)}, u32[]{:S(2)}, u32[]{:S(2)}) collective-permute-start(bf16[1024,128]{1,0:T(8,128)(2,1)S(1)} %get-tuple-element.97.refs_0_), channel_id=1, source_target_pairs={{0,1},{1,0},{2,3},{3,2},{4,5},{5,4},{6,7},{7,6},{8,9},{9,8},{10,11... | collective-permute-start | bytes 786440 | tf_op jit(solution)/shard_map/ppermute | solution.py:544
  91.4 7.5 %collective-permute-start.24 = (bf16[1024,128]{1,0:T(8,128)(2,1)S(1)}, bf16[1024,128]{1,0:T(8,128)(2,1)S(1)}, u32[]{:S(2)}, u32[]{:S(2)}) collective-permute-start(bf16[1024,128]{1,0:T(8,128)(2,1)S(1)} %collective-permute-done.16.refs_2_), channel_id=1, source_target_pairs={{0,1},{1,0},{2,3},{3,2},{4,5},{5,4},{6,7},{7,6},{8,9},{9,8},{10,11... | collective-permute-start | bytes 786440 | tf_op jit(solution)/shard_map/ppermute | solution.py:544
  94.1 6.3 %collective-permute-start.25 = (bf16[1024,128]{1,0:T(8,128)(2,1)S(1)}, bf16[1024,128]{1,0:T(8,128)(2,1)S(1)}, u32[]{:S(2)}, u32[]{:S(2)}) collective-permute-start(bf16[1024,128]{1,0:T(8,128)(2,1)S(1)} %collective-permute-done.17.refs_3_), channel_id=1, source_target_pairs={{0,1},{1,0},{2,3},{3,2},{4,5},{5,4},{6,7},{7,6},{8,9},{9,8},{10,11... | collective-permute-start | bytes 786440 | tf_op jit(solution)/shard_map/ppermute | solution.py:544
  94.1 7.5 %collective-permute-start.23 = (bf16[1024,128]{1,0:T(8,128)(2,1)S(1)}, bf16[1024,128]{1,0:T(8,128)(2,1)S(1)}, u32[]{:S(2)}, u32[]{:S(2)}) collective-permute-start(bf16[1024,128]{1,0:T(8,128)(2,1)S(1)} %collective-permute-done.21.refs_1_), channel_id=1, source_target_pairs={{0,1},{1,0},{2,3},{3,2},{4,5},{5,4},{6,7},{7,6},{8,9},{9,8},{10,11... | collective-permute-start | bytes 786440 | tf_op jit(solution)/shard_map/ppermute | solution.py:544
  94.6 17.4 %collective-permute-start.18 = (bf16[576,128]{1,0:T(8,128)(2,1)S(1)}, bf16[576,128]{1,0:T(8,128)(2,1)S(1)}, u32[]{:S(2)}, u32[]{:S(2)}) collective-permute-start(bf16[576,128]{1,0:T(8,128)(2,1)S(1)} %get-tuple-element.92), channel_id=1, source_target_pairs={{0,4},{4,0},{8,12},{12,8},{1,5},{5,1},{9,13},{13,9},{2,6},{6,2},{1... | collective-permute-start | bytes 442376 | tf_op jit(solution)/shard_map/ppermute | solution.py:538
  98.9 13.1 %collective-permute-start.19 = (bf16[576,128]{1,0:T(8,128)(2,1)S(1)}, bf16[576,128]{1,0:T(8,128)(2,1)S(1)}, u32[]{:S(2)}, u32[]{:S(2)}) collective-permute-start(bf16[576,128]{1,0:T(8,128)(2,1)S(1)} %get-tuple-element.93), channel_id=1, source_target_pairs={{0,8},{4,12},{8,0},{12,4},{1,9},{5,13},{9,1},{13,5},{2,10},{6,14},... | collective-permute-start | bytes 442376 | tf_op jit(solution)/shard_map/ppermute | solution.py:538
  100.4 11.6 %collective-permute-start.20 = (bf16[576,128]{1,0:T(8,128)(2,1)S(1)}, bf16[576,128]{1,0:T(8,128)(2,1)S(1)}, u32[]{:S(2)}, u32[]{:S(2)}) collective-permute-start(bf16[576,128]{1,0:T(8,128)(2,1)S(1)} %get-tuple-element.94), channel_id=1, source_target_pairs={{0,12},{4,8},{8,4},{12,0},{1,13},{5,9},{9,5},{13,1},{2,14},{6,10},... | collective-permute-start | bytes 442376 | tf_op jit(solution)/shard_map/ppermute | solution.py:538
  104.5 15.1 %collective-permute-start.28 = (bf16[256,1024]{1,0:T(8,128)(2,1)S(1)}, bf16[256,1024]{1,0:T(8,128)(2,1)S(1)}, u32[]{:S(2)}, u32[]{:S(2)}) collective-permute-start(bf16[256,1024]{1,0:T(8,128)(2,1)S(1)} %shard_map.105), channel_id=1, source_target_pairs={{0,1},{1,3},{3,2},{2,0},{4,5},{5,7},{7,6},{6,4},{8,9},{9,11},{11,1... | collective-permute-start | bytes 1572872 | tf_op jit(solution)/shard_map/ppermute | solution.py:666
  108.6 11.0 %collective-permute-start.29 = (bf16[256,1024]{1,0:T(8,128)(2,1)S(1)}, bf16[256,1024]{1,0:T(8,128)(2,1)S(1)}, u32[]{:S(2)}, u32[]{:S(2)}) collective-permute-start(bf16[256,1024]{1,0:T(8,128)(2,1)S(1)} %shard_map.106.kept_ref), channel_id=1, source_target_pairs={{1,2},{2,1},{5,6},{6,5},{9,10},{10,9},{13,14},{14,13},{17,18},{18,... | collective-permute-start | bytes 1572872 | tf_op jit(solution)/shard_map/ppermute | solution.py:668

commit v12 on v11

--- a/solution.py
+++ b/solution.py
@@ -631,7 +631,7 @@
         + [held(jnp.bfloat16)] * 2,
         takes=10,
     )
-    *ready, _, _ = lax.optimization_barrier((*results[:chips], value_back[2], value_back[3]))
+    *ready, _ = lax.optimization_barrier((*results[:chips], value_back[2]))
     back = exchange(ready)
 
     attended_mine, attended_theirs = results[chips:]

time: 121 us -> 121 us (level)
  starting transfers between devices: 50.1 us -> 47.4 us
  waiting for transfers between devices: 31.8 us -> 33.8 us
    ppermute x18, waiting for transfers between devices: 24.5 us -> 26.5 us  [exchange(): lax.ppermute(parts[offset], 'seq', [(at, at ^ offset) for at in range(chi...]
    ppermute x18, starting transfers between devices: 37.6 us -> 35.9 us  [exchange(): lax.ppermute(parts[offset], 'seq', [(at, at ^ offset) for at in range(chi...]
  transfers between devices with their start and end apart: 30 -> 30, of which waited for: 6 -> 5; matrix products, arithmetic and copies ran while one was open for 0% -> 0% of each run, Pallas kernels for 28% -> 28%
where the time goes in v12:
time: 121 us; the launch traced here: 120 us
  starting transfers between devices  47.4 us (39%)
  Pallas kernels  38.2 us (32%)
  waiting for transfers between devices  33.8 us (28%)
    pallas_call x14, Pallas kernels, call(): pl.pallas_call(kernel, out_shape=outs, in_specs=[smem] + [vmem] * (len(op...  38.2 us
    ppermute x18, starting transfers between devices, exchange(): lax.ppermute(parts[offset], 'seq', [(at, at ^ offset) for at in range(chi...  35.9 us
    ppermute x18, waiting for transfers between devices, exchange(): lax.ppermute(parts[offset], 'seq', [(at, at ^ offset) for at in range(chi...  26.5 us
    ppermute x10, starting transfers between devices, to_sibling(): return lax.ppermute(piece, 'sub', swap)  7 us
    ppermute x1, waiting for transfers between devices, by_head(): second = lax.ppermute(kept, square, [(1, 2), (2, 1)])  6.1 us
    ppermute x1, starting transfers between devices, by_head(): second = lax.ppermute(kept, square, [(1, 2), (2, 1)])  3.27 us
  transfers between devices with their start and end apart: 30, of which 5 were waited for; matrix products, arithmetic and copies ran while one was open for 0% of the time, Pallas kernels for 28%

profile of v12, /device:TPU:1, one launch (start us, length us, event | category | flops | bytes accessed | tf_op | source)
XLA Modules:
  0.0 120.3 jit_solution(10522807471614912262)
XLA Ops:
  0.6 0.1 collective-permute-start
  0.8 0.1 pad_add_fusion.place_ref.refs_0_
  0.8 1.7 %shard_map.94 = (bf16[4,272,128]{2,1,0:T(8,128)(2,1)S(1)}, bf16[4,272,128]{2,1,0:T(8,128)(2,1)S(1)}) custom-call(s32[4]{0:T(128)S(1)} %pad_add_fusion.place_ref.refs_0_, bf16[256,1024]{1,0:T(8,128)(2,1)} %grads_ref.1, s32[8,256]{1,0:T(8,128)} %assign_ref.1), custom_call_target="tpu_custom_call" | custom-call | flops 1150000000 | bytes 1048576 | tf_op jit(solution)/shard_map/pallas_call | solution.py:518
  2.5 0.5 collective-permute-start.1
  3.1 1.2 collective-permute-done.1.theirs_ref
  4.2 0.6 shard_map.95
  4.8 0.0 collective-permute-done.refs_1_.refs_2_
  4.8 3.4 %shard_map.96 = bf16[2,512,512]{2,1,0:T(8,128)(2,1)S(1)} custom-call(s32[4]{0:T(128)S(1)} %pad_add_fusion.place_ref.refs_0_, bf16[256,2048]{1,0:T(8,128)(2,1)} %refs_1_.3, bf16[256,2048]{1,0:T(8,128)(2,1)S(1)} %collective-permute-done.refs_1_.refs_2_, bf16[1024,1024]{1,0:T(8,128)(2,1)} %refs_13_.3, bf16[1024,1024]{1,0:T(8,128)(2,1)} %refs_14_.3), custom_call_target="tpu_custom_call" | custom-call | flops 115000000 | bytes 1048576 | tf_op jit(solution)/shard_map/pallas_call | solution.py:518
  8.3 0.4 collective-permute-start.2
  8.7 3.4 %collective-permute-start.7 = (bf16[544,128]{1,0:T(8,128)(2,1)S(1)}, bf16[544,128]{1,0:T(8,128)(2,1)S(1)}, u32[]{:S(2)}, u32[]{:S(2)}) collective-permute-start(bf16[544,128]{1,0:T(8,128)(2,1)S(1)} %get-tuple-element.63), channel_id=1, source_target_pairs={{0,8},{4,12},{8,0},{12,4},{1,9},{5,13},{9,1},{13,5},{2,10},{6,14},... | collective-permute-start | bytes 417800 | tf_op jit(solution)/shard_map/ppermute | solution.py:538
  12.1 1.1 collective-permute-start.8
  13.2 2.7 %shard_map.98 = bf16[1,512,512]{2,1,0:T(8,128)(2,1)S(1)} custom-call(s32[4]{0:T(128)S(1)} %pad_add_fusion.place_ref.refs_0_, bf16[256,2048]{1,0:T(8,128)(2,1)} %refs_1_.3, bf16[256,2048]{1,0:T(8,128)(2,1)S(1)} %collective-permute-done.refs_1_.refs_2_, bf16[1024,1024]{1,0:T(8,128)(2,1)} %refs_15_.3), custom_call_target="tpu_custom_call" | custom-call | flops 115000000 | bytes 1048576 | tf_op jit(solution)/shard_map/pallas_call | solution.py:518
  15.9 1.0 collective-permute-start.6
  16.9 0.0 collective-permute-done.2.refs_0_
  16.9 3.6 %shard_map.97 = (bf16[1024,128]{1,0:T(8,128)(2,1)S(1)}, bf16[1024,128]{1,0:T(8,128)(2,1)S(1)}, bf16[1024,128]{1,0:T(8,128)(2,1)S(1)}, bf16[1024,128]{1,0:T(8,128)(2,1)S(1)}) custom-call(s32[4]{0:T(128)S(1)} %pad_add_fusion.place_ref.refs_0_, bf16[2,512,512]{2,1,0:T(8,128)(2,1)S(1)} %collective-permute-done.2.refs_0_, bf16[256,2048]{1,0:T(8,128)(2,1)} %refs_1_.3, ...), custom_call_target="tpu_custom_call" | custom-call | flops 9200000000 | bytes 1048576 | tf_op jit(solution)/shard_map/pallas_call | solution.py:518
  20.5 0.1 collective-permute-start.3
  20.6 2.5 %collective-permute-start.4 = (bf16[1024,128]{1,0:T(8,128)(2,1)S(1)}, bf16[1024,128]{1,0:T(8,128)(2,1)S(1)}, u32[]{:S(2)}, u32[]{:S(2)}) collective-permute-start(bf16[1024,128]{1,0:T(8,128)(2,1)S(1)} %get-tuple-element.61), channel_id=1, source_target_pairs={{0,8},{4,12},{8,0},{12,4},{1,9},{5,13},{9,1},{13,5},{2,10},{6,14},... | collective-permute-start | bytes 786440 | tf_op jit(solution)/shard_map/ppermute | solution.py:538
  23.0 0.0 collective-permute-done.7.refs_6_.refs_10_
  23.0 2.5 %collective-permute-start.5 = (bf16[1024,128]{1,0:T(8,128)(2,1)S(1)}, bf16[1024,128]{1,0:T(8,128)(2,1)S(1)}, u32[]{:S(2)}, u32[]{:S(2)}) collective-permute-start(bf16[1024,128]{1,0:T(8,128)(2,1)S(1)} %get-tuple-element.62), channel_id=1, source_target_pairs={{0,12},{4,8},{8,4},{12,0},{1,13},{5,9},{9,5},{13,1},{2,14},{6,10},... | collective-permute-start | bytes 786440 | tf_op jit(solution)/shard_map/ppermute | solution.py:538
  25.5 0.0 collective-permute-done.8.refs_7_.refs_11_
  25.5 0.2 collective-permute-start.12
  25.7 0.0 collective-permute-done.6.refs_0_
  25.7 2.8 %shard_map.99 = (bf16[512,128]{1,0:T(8,128)(2,1)S(1)}, bf16[512,128]{1,0:T(8,128)(2,1)S(1)}, bf16[512,128]{1,0:T(8,128)(2,1)S(1)}, bf16[512,128]{1,0:T(8,128)(2,1)S(1)}) custom-call(s32[4]{0:T(128)S(1)} %pad_add_fusion.place_ref.refs_0_, bf16[1,512,512]{2,1,0:T(8,128)(2,1)S(1)} %collective-permute-done.6.refs_0_, bf16[256,2048]{1,0:T(8,128)(2,1)} %refs_1_.3, ...), custom_call_target="tpu_custom_call" | custom-call | flops 115000000 | bytes 1048576 | tf_op jit(solution)/shard_map/pallas_call | solution.py:518
  28.6 1.4 %collective-permute-start.9 = (bf16[512,128]{1,0:T(8,128)(2,1)S(1)}, bf16[512,128]{1,0:T(8,128)(2,1)S(1)}, u32[]{:S(2)}, u32[]{:S(2)}) collective-permute-start(bf16[512,128]{1,0:T(8,128)(2,1)S(1)} %get-tuple-element.71), channel_id=1, source_target_pairs={{0,4},{4,0},{8,12},{12,8},{1,5},{5,1},{9,13},{13,9},{2,6},{6,2},{1... | collective-permute-start | bytes 393224 | tf_op jit(solution)/shard_map/ppermute | solution.py:538
  29.9 3.3 %collective-permute-done.3.refs_1_ = bf16[1024,128]{1,0:T(8,128)(2,1)S(1)} collective-permute-done((bf16[1024,128]{1,0:T(8,128)(2,1)S(1)}, bf16[1024,128]{1,0:T(8,128)(2,1)S(1)}, u32[]{:S(2)}, u32[]{:S(2)}) %collective-permute-start.3) | collective-permute-done | bytes 262176 | tf_op jit(solution)/shard_map/ppermute | solution.py:538
  33.2 0.0 collective-permute-start.10
  33.2 8.6 %collective-permute-done.4.refs_2_ = bf16[1024,128]{1,0:T(8,128)(2,1)S(1)} collective-permute-done((bf16[1024,128]{1,0:T(8,128)(2,1)S(1)}, bf16[1024,128]{1,0:T(8,128)(2,1)S(1)}, u32[]{:S(2)}, u32[]{:S(2)}) %collective-permute-start.4) | collective-permute-done | bytes 262176 | tf_op jit(solution)/shard_map/ppermute | solution.py:538
  41.8 3.7 %collective-permute-start.11 = (bf16[512,128]{1,0:T(8,128)(2,1)S(1)}, bf16[512,128]{1,0:T(8,128)(2,1)S(1)}, u32[]{:S(2)}, u32[]{:S(2)}) collective-permute-start(bf16[512,128]{1,0:T(8,128)(2,1)S(1)} %get-tuple-element.73), channel_id=1, source_target_pairs={{0,12},{4,8},{8,4},{12,0},{1,13},{5,9},{9,5},{13,1},{2,14},{6,10},... | collective-permute-start | bytes 393224 | tf_op jit(solution)/shard_map/ppermute | solution.py:538
  45.5 0.0 collective-permute-done.5.refs_3_
  45.5 0.0 collective-permute-done.12.refs_5_.refs_9_
  45.5 6.5 %shard_map.100 = (bf16[512,128]{1,0:T(8,128)(2,1)S(1)}, bf16[512,128]{1,0:T(8,128)(2,1)S(1)}, bf16[512,128]{1,0:T(8,128)(2,1)S(1)}, bf16[512,128]{1,0:T(8,128)(2...) custom-call(s32[4]{0:T(128)S(1)} %pad_add_fusion.place_ref.refs_0_, ...), custom_call_target="tpu_custom_call" | custom-call | flops 8049999872 | bytes 1048576 | tf_op jit(solution)/shard_map/pallas_call | solution.py:518
  51.9 10.4 %collective-permute-start.14 = (bf16[512,128]{1,0:T(8,128)(2,1)S(1)}, bf16[512,128]{1,0:T(8,128)(2,1)S(1)}, u32[]{:S(2)}, u32[]{:S(2)}) collective-permute-start(bf16[512,128]{1,0:T(8,128)(2,1)S(1)} %get-tuple-element.87), channel_id=1, source_target_pairs={{0,8},{4,12},{8,0},{12,4},{1,9},{5,13},{9,1},{13,5},{2,10},{6,14},... | collective-permute-start | bytes 393224 | tf_op jit(solution)/shard_map/ppermute | solution.py:538
  62.3 0.0 collective-permute-start.25
  62.3 0.0 collective-permute-done.9.refs_5_
  62.3 1.3 %collective-permute-start.26 = (bf16[512,128]{1,0:T(8,128)(2,1)S(1)}, bf16[512,128]{1,0:T(8,128)(2,1)S(1)}, u32[]{:S(2)}, u32[]{:S(2)}) collective-permute-start(bf16[512,128]{1,0:T(8,128)(2,1)S(1)} %get-tuple-element.100), channel_id=1, source_target_pairs={{0,12},{4,8},{8,4},{12,0},{1,13},{5,9},{9,5},{13,1},{2,14},{6,10},... | collective-permute-start | bytes 393224 | tf_op jit(solution)/shard_map/ppermute | solution.py:538
  63.6 7.0 %shard_map.101 = (bf16[1024,128]{1,0:T(8,128)(2,1)S(1)}, bf16[1024,128]{1,0:T(8,128)(2,1)S(1)}, bf16[1024,128]{1,0:T(8,128)(2,1)S(1)}, bf16[1024,128]{1,0:T(8,12...) custom-call(s32[4]{0:T(128)S(1)} %pad_add_fusion.place_ref.refs_0_, ...), custom_call_target="tpu_custom_call" | custom-call | flops 11500000256 | bytes 1048576 | tf_op jit(solution)/shard_map/pallas_call | solution.py:518
  70.6 1.2 collective-permute-start.13
  71.8 0.0 collective-permute-done.14.refs_3_.refs_10_
  71.8 1.7 %collective-permute-start.15 = (bf16[1024,128]{1,0:T(8,128)(2,1)S(1)}, bf16[1024,128]{1,0:T(8,128)(2,1)S(1)}, u32[]{:S(2)}, u32[]{:S(2)}) collective-permute-start(bf16[1024,128]{1,0:T(8,128)(2,1)S(1)} %get-tuple-element.88), channel_id=1, source_target_pairs={{0,8},{4,12},{8,0},{12,4},{1,9},{5,13},{9,1},{13,5},{2,10},{6,14},... | collective-permute-start | bytes 786440 | tf_op jit(solution)/shard_map/ppermute | solution.py:538
  73.5 0.6 collective-permute-start.16
  74.1 0.3 collective-permute-start.20
  74.5 0.6 shard_map.104
  75.0 1.8 %collective-permute-start.27 = (bf16[4,512,128]{2,1,0:T(8,128)(2,1)S(1)}, bf16[4,512,128]{2,1,0:T(8,128)(2,1)S(1)}, u32[]{:S(2)}, u32[]{:S(2)}) collective-permute-start(bf16[4,512,128]{2,1,0:T(8,128)(2,1)S(1)} %shard_map.104), channel_id=1, source_target_pairs={{0,1},{1,0},{2,3},{3,2},{4,5},{5,4},{6,7},{7,6},{8,9},{9,8},{10,11... | collective-permute-start | bytes 1572872 | tf_op jit(solution)/shard_map/ppermute | solution.py:544
  76.9 0.0 collective-permute-done.13.theirs_ref
  76.9 0.6 shard_map.102
  77.5 0.1 collective-permute-start.21
  77.6 14.6 %collective-permute-done.15.refs_2_ = bf16[1024,128]{1,0:T(8,128)(2,1)S(1)} collective-permute-done((bf16[1024,128]{1,0:T(8,128)(2,1)S(1)}, bf16[1024,128]{1,0:T(8,128)(2,1)S(1)}, u32[]{:S(2)}, u32[]{:S(2)}) %collective-permute-start.15) | collective-permute-done | bytes 262176 | tf_op jit(solution)/shard_map/ppermute | solution.py:538
  92.2 0.6 collective-permute-start.23
  92.8 0.0 collective-permute-start.24
  92.8 0.0 collective-permute-done.20.refs_1_
  92.8 1.2 %collective-permute-start.22 = (bf16[1024,128]{1,0:T(8,128)(2,1)S(1)}, bf16[1024,128]{1,0:T(8,128)(2,1)S(1)}, u32[]{:S(2)}, u32[]{:S(2)}) collective-permute-start(bf16[1024,128]{1,0:T(8,128)(2,1)S(1)} %collective-permute-done.20.refs_1_), channel_id=1, source_target_pairs={{0,1},{1,0},{2,3},{3,2},{4,5},{5,4},{6,7},{7,6},{8,9},{9,8},{10,11... | collective-permute-start | bytes 786440 | tf_op jit(solution)/shard_map/ppermute | solution.py:544
  94.0 0.0 collective-permute-done.21.refs_4_
  94.0 4.6 %collective-permute-start.17 = (bf16[576,128]{1,0:T(8,128)(2,1)S(1)}, bf16[576,128]{1,0:T(8,128)(2,1)S(1)}, u32[]{:S(2)}, u32[]{:S(2)}) collective-permute-start(bf16[576,128]{1,0:T(8,128)(2,1)S(1)} %get-tuple-element.91), channel_id=1, source_target_pairs={{0,4},{4,0},{8,12},{12,8},{1,5},{5,1},{9,13},{13,9},{2,6},{6,2},{1... | collective-permute-start | bytes 442376 | tf_op jit(solution)/shard_map/ppermute | solution.py:538
  98.6 1.0 collective-permute-start.18
  99.6 1.2 %collective-permute-start.19 = (bf16[576,128]{1,0:T(8,128)(2,1)S(1)}, bf16[576,128]{1,0:T(8,128)(2,1)S(1)}, u32[]{:S(2)}, u32[]{:S(2)}) collective-permute-start(bf16[576,128]{1,0:T(8,128)(2,1)S(1)} %get-tuple-element.93), channel_id=1, source_target_pairs={{0,12},{4,8},{8,4},{12,0},{1,13},{5,9},{9,5},{13,1},{2,14},{6,10},... | collective-permute-start | bytes 442376 | tf_op jit(solution)/shard_map/ppermute | solution.py:538
  100.8 0.0 collective-permute-done.27.refs_12_
  100.8 2.9 %shard_map.105 = bf16[256,1024]{1,0:T(8,128)(2,1)S(1)} custom-call(s32[4]{0:T(128)S(1)} %pad_add_fusion.place_ref.refs_0_, bf16[1024,128]{1,0:T(8,128)(2,1)S(1)} %get-tuple-element.96.refs_0_, bf16[1024,128]{1,0:T(8,128)(2,1)S(1)} %collective-permute-done.20.refs_1_, bf16[1024,128]{1,0:T(8,128)(2,1)S(1)} %collective-permute-done.15.refs_2_, ...), custom_call_target="tpu_custom_call" | custom-call | flops 1150000000 | bytes 1048576 | tf_op jit(solution)/shard_map/pallas_call | solution.py:518
  103.8 1.3 %collective-permute-start.28 = (bf16[256,1024]{1,0:T(8,128)(2,1)S(1)}, bf16[256,1024]{1,0:T(8,128)(2,1)S(1)}, u32[]{:S(2)}, u32[]{:S(2)}) collective-permute-start(bf16[256,1024]{1,0:T(8,128)(2,1)S(1)} %shard_map.105), channel_id=1, source_target_pairs={{0,1},{1,3},{3,2},{2,0},{4,5},{5,7},{7,6},{6,4},{8,9},{9,11},{11,1... | collective-permute-start | bytes 1572872 | tf_op jit(solution)/shard_map/ppermute | solution.py:666
  105.0 2.9 %shard_map.106.kept_ref = bf16[256,1024]{1,0:T(8,128)(2,1)S(1)} custom-call(s32[4]{0:T(128)S(1)} %pad_add_fusion.place_ref.refs_0_, bf16[1024,128]{1,0:T(8,128)(2,1)S(1)} %get-tuple-element.96.refs_0_, bf16[1024,128]{1,0:T(8,128)(2,1)S(1)} %collective-permute-done.20.refs_1_, bf16[1024,128]{1,0:T(8,128)(2,1)S(1)} %collective-permute-done.15.refs_2_, ...), custom_call_target="tpu_custom_call" | custom-call | flops 1150000000 | bytes 1048576 | tf_op jit(solution)/shard_map/pallas_call | solution.py:518
  107.9 3.3 %collective-permute-start.29 = (bf16[256,1024]{1,0:T(8,128)(2,1)S(1)}, bf16[256,1024]{1,0:T(8,128)(2,1)S(1)}, u32[]{:S(2)}, u32[]{:S(2)}) collective-permute-start(bf16[256,1024]{1,0:T(8,128)(2,1)S(1)} %shard_map.106.kept_ref), channel_id=1, source_target_pairs={{1,2},{2,1},{5,6},{6,5},{9,10},{10,9},{13,14},{14,13},{17,18},{18,... | collective-permute-start | bytes 1572872 | tf_op jit(solution)/shard_map/ppermute | solution.py:668
  111.2 0.0 collective-permute-done.17.refs_1_
  111.2 1.5 %shard_map.103 = (bf16[256,1024]{1,0:T(8,128)(2,1)}, f32[8,32,128]{2,1,0:T(8,128)}) custom-call(s32[4]{0:T(128)S(1)} %pad_add_fusion.place_ref.refs_0_, bf16[576,128]{1,0:T(8,128)(2,1)S(1)} %get-tuple-element.90.refs_0_, bf16[576,128]{1,0:T(8,128)(2,1)S(1)} %collective-permute-done.17.refs_1_, bf16[576,128]{1,0:T(8,128)(2,1)S(1)} %collective-permute-done.18.refs_2_, ...), custom_call_target="tpu_custom_call" | custom-call | flops 9200000000 | bytes 1048576 | tf_op jit(solution)/shard_map/pallas_call | solution.py:518
  112.8 6.1 %collective-permute-done.29.second_ref = bf16[256,1024]{1,0:T(8,128)(2,1)S(1)} collective-permute-done((bf16[256,1024]{1,0:T(8,128)(2,1)S(1)}, bf16[256,1024]{1,0:T(8,128)(2,1)S(1)}, u32[]{:S(2)}, u32[]{:S(2)}) %collective-permute-start.29) | collective-permute-done | bytes 524320 | tf_op jit(solution)/shard_map/ppermute | solution.py:668
  118.9 1.5 %shard_map.107 = bf16[256,1024]{1,0:T(8,128)(2,1)} custom-call(s32[4]{0:T(128)S(1)} %pad_add_fusion.place_ref.refs_0_, bf16[256,1024]{1,0:T(8,128)(2,1)S(1)} %collective-permute-done.28.first_ref, bf16[256,1024]{1,0:T(8,128)(2,1)S(1)} %collective-permute-done.29.second_ref, bf16[256,1024]{1,0:T(8,128)(2,1)S(1)} %shard_map.106.kept_ref), custom_call_target="tpu_custom_call" | custom-call | flops 1150000000 | bytes 1048576 | tf_op jit(solution)/shard_map/pallas_call | solution.py:518
  (19 shorter events, 0.0 us)
Async XLA Ops:
  0.6 4.2 %collective-permute-start = (bf16[256,2048]{1,0:T(8,128)(2,1)}, bf16[256,2048]{1,0:T(8,128)(2,1)S(1)}, u32[]{:S(2)}, u32[]{:S(2)}) collective-permute-start(bf16[256,2048]{1,0:T(8,128)(2,1)} %refs_1_.3), channel_id=1, source_target_pairs={{0,1},{1,0},{2,3},{3,2},{4,5},{5,4},{6,7},{7,6},{8,9},{9,8},{10,11... | collective-permute-start | bytes 3145736 | tf_op jit(solution)/shard_map/ppermute | solution.py:544
  2.5 1.7 %collective-permute-start.1 = (bf16[4,272,128]{2,1,0:T(8,128)(2,1)S(1)}, bf16[4,272,128]{2,1,0:T(8,128)(2,1)S(1)}, u32[]{:S(2)}, u32[]{:S(2)}) collective-permute-start(bf16[4,272,128]{2,1,0:T(8,128)(2,1)S(1)} %get-tuple-element.55), channel_id=1, source_target_pairs={{0,1},{1,0},{2,3},{3,2},{4,5},{5,4},{6,7},{7,6},{8,9},{9,8},{10,11... | collective-permute-start | bytes 835592 | tf_op jit(solution)/shard_map/ppermute | solution.py:544
  8.3 8.6 %collective-permute-start.2 = (bf16[2,512,512]{2,1,0:T(8,128)(2,1)S(1)}, bf16[2,512,512]{2,1,0:T(8,128)(2,1)S(1)}, u32[]{:S(2)}, u32[]{:S(2)}) collective-permute-start(bf16[2,512,512]{2,1,0:T(8,128)(2,1)S(1)} %shard_map.96), channel_id=1, source_target_pairs={{0,1},{1,0},{2,3},{3,2},{4,5},{5,4},{6,7},{7,6},{8,9},{9,8},{10,11... | collective-permute-start | bytes 3145736 | tf_op jit(solution)/shard_map/ppermute | solution.py:544
  8.7 14.3 %collective-permute-start.7 = (bf16[544,128]{1,0:T(8,128)(2,1)S(1)}, bf16[544,128]{1,0:T(8,128)(2,1)S(1)}, u32[]{:S(2)}, u32[]{:S(2)}) collective-permute-start(bf16[544,128]{1,0:T(8,128)(2,1)S(1)} %get-tuple-element.63), channel_id=1, source_target_pairs={{0,8},{4,12},{8,0},{12,4},{1,9},{5,13},{9,1},{13,5},{2,10},{6,14},... | collective-permute-start | bytes 417800 | tf_op jit(solution)/shard_map/ppermute | solution.py:538
  12.1 13.4 %collective-permute-start.8 = (bf16[544,128]{1,0:T(8,128)(2,1)S(1)}, bf16[544,128]{1,0:T(8,128)(2,1)S(1)}, u32[]{:S(2)}, u32[]{:S(2)}) collective-permute-start(bf16[544,128]{1,0:T(8,128)(2,1)S(1)} %get-tuple-element.64), channel_id=1, source_target_pairs={{0,12},{4,8},{8,4},{12,0},{1,13},{5,9},{9,5},{13,1},{2,14},{6,10},... | collective-permute-start | bytes 417800 | tf_op jit(solution)/shard_map/ppermute | solution.py:538
  15.9 9.8 %collective-permute-start.6 = (bf16[1,512,512]{2,1,0:T(8,128)(2,1)S(1)}, bf16[1,512,512]{2,1,0:T(8,128)(2,1)S(1)}, u32[]{:S(2)}, u32[]{:S(2)}) collective-permute-start(bf16[1,512,512]{2,1,0:T(8,128)(2,1)S(1)} %shard_map.98), channel_id=1, source_target_pairs={{0,1},{1,0},{2,3},{3,2},{4,5},{5,4},{6,7},{7,6},{8,9},{9,8},{10,11... | collective-permute-start | bytes 1572872 | tf_op jit(solution)/shard_map/ppermute | solution.py:544
  20.5 12.7 %collective-permute-start.3 = (bf16[1024,128]{1,0:T(8,128)(2,1)S(1)}, bf16[1024,128]{1,0:T(8,128)(2,1)S(1)}, u32[]{:S(2)}, u32[]{:S(2)}) collective-permute-start(bf16[1024,128]{1,0:T(8,128)(2,1)S(1)} %get-tuple-element.60), channel_id=1, source_target_pairs={{0,4},{4,0},{8,12},{12,8},{1,5},{5,1},{9,13},{13,9},{2,6},{6,2},{1... | collective-permute-start | bytes 786440 | tf_op jit(solution)/shard_map/ppermute | solution.py:538
  20.6 21.2 %collective-permute-start.4 = (bf16[1024,128]{1,0:T(8,128)(2,1)S(1)}, bf16[1024,128]{1,0:T(8,128)(2,1)S(1)}, u32[]{:S(2)}, u32[]{:S(2)}) collective-permute-start(bf16[1024,128]{1,0:T(8,128)(2,1)S(1)} %get-tuple-element.61), channel_id=1, source_target_pairs={{0,8},{4,12},{8,0},{12,4},{1,9},{5,13},{9,1},{13,5},{2,10},{6,14},... | collective-permute-start | bytes 786440 | tf_op jit(solution)/shard_map/ppermute | solution.py:538
  23.0 22.4 %collective-permute-start.5 = (bf16[1024,128]{1,0:T(8,128)(2,1)S(1)}, bf16[1024,128]{1,0:T(8,128)(2,1)S(1)}, u32[]{:S(2)}, u32[]{:S(2)}) collective-permute-start(bf16[1024,128]{1,0:T(8,128)(2,1)S(1)} %get-tuple-element.62), channel_id=1, source_target_pairs={{0,12},{4,8},{8,4},{12,0},{1,13},{5,9},{9,5},{13,1},{2,14},{6,10},... | collective-permute-start | bytes 786440 | tf_op jit(solution)/shard_map/ppermute | solution.py:538
  25.5 19.9 %collective-permute-start.12 = (bf16[544,128]{1,0:T(8,128)(2,1)S(1)}, bf16[544,128]{1,0:T(8,128)(2,1)S(1)}, u32[]{:S(2)}, u32[]{:S(2)}) collective-permute-start(bf16[544,128]{1,0:T(8,128)(2,1)S(1)} %get-tuple-element.74), channel_id=1, source_target_pairs={{0,4},{4,0},{8,12},{12,8},{1,5},{5,1},{9,13},{13,9},{2,6},{6,2},{1... | collective-permute-start | bytes 417800 | tf_op jit(solution)/shard_map/ppermute | solution.py:538
  25.7 19.8 %copy-start.3 = (s32[256]{0:T(256)S(1)}, s32[256]{0:T(256)}, u32[]{:S(2)}) copy-start(s32[256]{0:T(256)} %param.11) | copy-start | bytes 3076
  28.6 33.8 %collective-permute-start.9 = (bf16[512,128]{1,0:T(8,128)(2,1)S(1)}, bf16[512,128]{1,0:T(8,128)(2,1)S(1)}, u32[]{:S(2)}, u32[]{:S(2)}) collective-permute-start(bf16[512,128]{1,0:T(8,128)(2,1)S(1)} %get-tuple-element.71), channel_id=1, source_target_pairs={{0,4},{4,0},{8,12},{12,8},{1,5},{5,1},{9,13},{13,9},{2,6},{6,2},{1... | collective-permute-start | bytes 393224 | tf_op jit(solution)/shard_map/ppermute | solution.py:538
  33.2 30.4 %collective-permute-start.10 = (bf16[512,128]{1,0:T(8,128)(2,1)S(1)}, bf16[512,128]{1,0:T(8,128)(2,1)S(1)}, u32[]{:S(2)}, u32[]{:S(2)}) collective-permute-start(bf16[512,128]{1,0:T(8,128)(2,1)S(1)} %get-tuple-element.72), channel_id=1, source_target_pairs={{0,8},{4,12},{8,0},{12,4},{1,9},{5,13},{9,1},{13,5},{2,10},{6,14},... | collective-permute-start | bytes 393224 | tf_op jit(solution)/shard_map/ppermute | solution.py:538
  41.8 21.8 %collective-permute-start.11 = (bf16[512,128]{1,0:T(8,128)(2,1)S(1)}, bf16[512,128]{1,0:T(8,128)(2,1)S(1)}, u32[]{:S(2)}, u32[]{:S(2)}) collective-permute-start(bf16[512,128]{1,0:T(8,128)(2,1)S(1)} %get-tuple-element.73), channel_id=1, source_target_pairs={{0,12},{4,8},{8,4},{12,0},{1,13},{5,9},{9,5},{13,1},{2,14},{6,10},... | collective-permute-start | bytes 393224 | tf_op jit(solution)/shard_map/ppermute | solution.py:538
  51.9 19.9 %collective-permute-start.14 = (bf16[512,128]{1,0:T(8,128)(2,1)S(1)}, bf16[512,128]{1,0:T(8,128)(2,1)S(1)}, u32[]{:S(2)}, u32[]{:S(2)}) collective-permute-start(bf16[512,128]{1,0:T(8,128)(2,1)S(1)} %get-tuple-element.87), channel_id=1, source_target_pairs={{0,8},{4,12},{8,0},{12,4},{1,9},{5,13},{9,1},{13,5},{2,10},{6,14},... | collective-permute-start | bytes 393224 | tf_op jit(solution)/shard_map/ppermute | solution.py:538
  62.3 11.8 %collective-permute-start.25 = (bf16[512,128]{1,0:T(8,128)(2,1)S(1)}, bf16[512,128]{1,0:T(8,128)(2,1)S(1)}, u32[]{:S(2)}, u32[]{:S(2)}) collective-permute-start(bf16[512,128]{1,0:T(8,128)(2,1)S(1)} %get-tuple-element.99), channel_id=1, source_target_pairs={{0,4},{4,0},{8,12},{12,8},{1,5},{5,1},{9,13},{13,9},{2,6},{6,2},{1... | collective-permute-start | bytes 393224 | tf_op jit(solution)/shard_map/ppermute | solution.py:538
  62.3 12.1 %collective-permute-start.26 = (bf16[512,128]{1,0:T(8,128)(2,1)S(1)}, bf16[512,128]{1,0:T(8,128)(2,1)S(1)}, u32[]{:S(2)}, u32[]{:S(2)}) collective-permute-start(bf16[512,128]{1,0:T(8,128)(2,1)S(1)} %get-tuple-element.100), channel_id=1, source_target_pairs={{0,12},{4,8},{8,4},{12,0},{1,13},{5,9},{9,5},{13,1},{2,14},{6,10},... | collective-permute-start | bytes 393224 | tf_op jit(solution)/shard_map/ppermute | solution.py:538
  70.6 6.2 %collective-permute-start.13 = (bf16[4,288,128]{2,1,0:T(8,128)(2,1)S(1)}, bf16[4,288,128]{2,1,0:T(8,128)(2,1)S(1)}, u32[]{:S(2)}, u32[]{:S(2)}) collective-permute-start(bf16[4,288,128]{2,1,0:T(8,128)(2,1)S(1)} %get-tuple-element.78), channel_id=1, source_target_pairs={{0,1},{1,0},{2,3},{3,2},{4,5},{5,4},{6,7},{7,6},{8,9},{9,8},{10,11... | collective-permute-start | bytes 884744 | tf_op jit(solution)/shard_map/ppermute | solution.py:544
  71.8 20.4 %collective-permute-start.15 = (bf16[1024,128]{1,0:T(8,128)(2,1)S(1)}, bf16[1024,128]{1,0:T(8,128)(2,1)S(1)}, u32[]{:S(2)}, u32[]{:S(2)}) collective-permute-start(bf16[1024,128]{1,0:T(8,128)(2,1)S(1)} %get-tuple-element.88), channel_id=1, source_target_pairs={{0,8},{4,12},{8,0},{12,4},{1,9},{5,13},{9,1},{13,5},{2,10},{6,14},... | collective-permute-start | bytes 786440 | tf_op jit(solution)/shard_map/ppermute | solution.py:538
  73.5 19.3 %collective-permute-start.16 = (bf16[1024,128]{1,0:T(8,128)(2,1)S(1)}, bf16[1024,128]{1,0:T(8,128)(2,1)S(1)}, u32[]{:S(2)}, u32[]{:S(2)}) collective-permute-start(bf16[1024,128]{1,0:T(8,128)(2,1)S(1)} %get-tuple-element.89), channel_id=1, source_target_pairs={{0,12},{4,8},{8,4},{12,0},{1,13},{5,9},{9,5},{13,1},{2,14},{6,10},... | collective-permute-start | bytes 786440 | tf_op jit(solution)/shard_map/ppermute | solution.py:538
  74.1 18.6 %collective-permute-start.20 = (bf16[1024,128]{1,0:T(8,128)(2,1)S(1)}, bf16[1024,128]{1,0:T(8,128)(2,1)S(1)}, u32[]{:S(2)}, u32[]{:S(2)}) collective-permute-start(bf16[1024,128]{1,0:T(8,128)(2,1)S(1)} %get-tuple-element.97), channel_id=1, source_target_pairs={{0,4},{4,0},{8,12},{12,8},{1,5},{5,1},{9,13},{13,9},{2,6},{6,2},{1... | collective-permute-start | bytes 786440 | tf_op jit(solution)/shard_map/ppermute | solution.py:538
  74.5 26.4 %copy-start.2 = (bf16[1024,1024]{1,0:T(8,128)(2,1)S(1)}, bf16[1024,1024]{1,0:T(8,128)(2,1)}, u32[]{:S(2)}) copy-start(bf16[1024,1024]{1,0:T(8,128)(2,1)} %refs_14_.3) | copy-start | bytes 6291460
  75.0 25.8 %collective-permute-start.27 = (bf16[4,512,128]{2,1,0:T(8,128)(2,1)S(1)}, bf16[4,512,128]{2,1,0:T(8,128)(2,1)S(1)}, u32[]{:S(2)}, u32[]{:S(2)}) collective-permute-start(bf16[4,512,128]{2,1,0:T(8,128)(2,1)S(1)} %shard_map.104), channel_id=1, source_target_pairs={{0,1},{1,0},{2,3},{3,2},{4,5},{5,4},{6,7},{7,6},{8,9},{9,8},{10,11... | collective-permute-start | bytes 1572872 | tf_op jit(solution)/shard_map/ppermute | solution.py:544
  76.9 24.0 %copy-start = (bf16[1024,1024]{1,0:T(8,128)(2,1)S(1)}, bf16[1024,1024]{1,0:T(8,128)(2,1)}, u32[]{:S(2)}) copy-start(bf16[1024,1024]{1,0:T(8,128)(2,1)} %refs_15_.3) | copy-start | bytes 6291460
  76.9 24.0 %copy-start.1 = (bf16[1024,1024]{1,0:T(8,128)(2,1)S(1)}, bf16[1024,1024]{1,0:T(8,128)(2,1)}, u32[]{:S(2)}) copy-start(bf16[1024,1024]{1,0:T(8,128)(2,1)} %refs_13_.3) | copy-start | bytes 6291460
  77.5 16.5 %collective-permute-start.21 = (bf16[1024,128]{1,0:T(8,128)(2,1)S(1)}, bf16[1024,128]{1,0:T(8,128)(2,1)S(1)}, u32[]{:S(2)}, u32[]{:S(2)}) collective-permute-start(bf16[1024,128]{1,0:T(8,128)(2,1)S(1)} %get-tuple-element.96.refs_0_), channel_id=1, source_target_pairs={{0,1},{1,0},{2,3},{3,2},{4,5},{5,4},{6,7},{7,6},{8,9},{9,8},{10,11... | collective-permute-start | bytes 786440 | tf_op jit(solution)/shard_map/ppermute | solution.py:544
  92.2 6.5 %collective-permute-start.23 = (bf16[1024,128]{1,0:T(8,128)(2,1)S(1)}, bf16[1024,128]{1,0:T(8,128)(2,1)S(1)}, u32[]{:S(2)}, u32[]{:S(2)}) collective-permute-start(bf16[1024,128]{1,0:T(8,128)(2,1)S(1)} %collective-permute-done.15.refs_2_), channel_id=1, source_target_pairs={{0,1},{1,0},{2,3},{3,2},{4,5},{5,4},{6,7},{7,6},{8,9},{9,8},{10,11... | collective-permute-start | bytes 786440 | tf_op jit(solution)/shard_map/ppermute | solution.py:544
  92.8 6.9 %collective-permute-start.24 = (bf16[1024,128]{1,0:T(8,128)(2,1)S(1)}, bf16[1024,128]{1,0:T(8,128)(2,1)S(1)}, u32[]{:S(2)}, u32[]{:S(2)}) collective-permute-start(bf16[1024,128]{1,0:T(8,128)(2,1)S(1)} %collective-permute-done.16.refs_3_), channel_id=1, source_target_pairs={{0,1},{1,0},{2,3},{3,2},{4,5},{5,4},{6,7},{7,6},{8,9},{9,8},{10,11... | collective-permute-start | bytes 786440 | tf_op jit(solution)/shard_map/ppermute | solution.py:544
  92.8 8.1 %collective-permute-start.22 = (bf16[1024,128]{1,0:T(8,128)(2,1)S(1)}, bf16[1024,128]{1,0:T(8,128)(2,1)S(1)}, u32[]{:S(2)}, u32[]{:S(2)}) collective-permute-start(bf16[1024,128]{1,0:T(8,128)(2,1)S(1)} %collective-permute-done.20.refs_1_), channel_id=1, source_target_pairs={{0,1},{1,0},{2,3},{3,2},{4,5},{5,4},{6,7},{7,6},{8,9},{9,8},{10,11... | collective-permute-start | bytes 786440 | tf_op jit(solution)/shard_map/ppermute | solution.py:544
  94.0 17.2 %collective-permute-start.17 = (bf16[576,128]{1,0:T(8,128)(2,1)S(1)}, bf16[576,128]{1,0:T(8,128)(2,1)S(1)}, u32[]{:S(2)}, u32[]{:S(2)}) collective-permute-start(bf16[576,128]{1,0:T(8,128)(2,1)S(1)} %get-tuple-element.91), channel_id=1, source_target_pairs={{0,4},{4,0},{8,12},{12,8},{1,5},{5,1},{9,13},{13,9},{2,6},{6,2},{1... | collective-permute-start | bytes 442376 | tf_op jit(solution)/shard_map/ppermute | solution.py:538
  98.6 12.6 %collective-permute-start.18 = (bf16[576,128]{1,0:T(8,128)(2,1)S(1)}, bf16[576,128]{1,0:T(8,128)(2,1)S(1)}, u32[]{:S(2)}, u32[]{:S(2)}) collective-permute-start(bf16[576,128]{1,0:T(8,128)(2,1)S(1)} %get-tuple-element.92), channel_id=1, source_target_pairs={{0,8},{4,12},{8,0},{12,4},{1,9},{5,13},{9,1},{13,5},{2,10},{6,14},... | collective-permute-start | bytes 442376 | tf_op jit(solution)/shard_map/ppermute | solution.py:538
  99.6 11.6 %collective-permute-start.19 = (bf16[576,128]{1,0:T(8,128)(2,1)S(1)}, bf16[576,128]{1,0:T(8,128)(2,1)S(1)}, u32[]{:S(2)}, u32[]{:S(2)}) collective-permute-start(bf16[576,128]{1,0:T(8,128)(2,1)S(1)} %get-tuple-element.93), channel_id=1, source_target_pairs={{0,12},{4,8},{8,4},{12,0},{1,13},{5,9},{9,5},{13,1},{2,14},{6,10},... | collective-permute-start | bytes 442376 | tf_op jit(solution)/shard_map/ppermute | solution.py:538
  103.8 15.1 %collective-permute-start.28 = (bf16[256,1024]{1,0:T(8,128)(2,1)S(1)}, bf16[256,1024]{1,0:T(8,128)(2,1)S(1)}, u32[]{:S(2)}, u32[]{:S(2)}) collective-permute-start(bf16[256,1024]{1,0:T(8,128)(2,1)S(1)} %shard_map.105), channel_id=1, source_target_pairs={{0,1},{1,3},{3,2},{2,0},{4,5},{5,7},{7,6},{6,4},{8,9},{9,11},{11,1... | collective-permute-start | bytes 1572872 | tf_op jit(solution)/shard_map/ppermute | solution.py:666
  107.9 10.9 %collective-permute-start.29 = (bf16[256,1024]{1,0:T(8,128)(2,1)S(1)}, bf16[256,1024]{1,0:T(8,128)(2,1)S(1)}, u32[]{:S(2)}, u32[]{:S(2)}) collective-permute-start(bf16[256,1024]{1,0:T(8,128)(2,1)S(1)} %shard_map.106.kept_ref), channel_id=1, source_target_pairs={{1,2},{2,1},{5,6},{6,5},{9,10},{10,9},{13,14},{14,13},{17,18},{18,... | collective-permute-start | bytes 1572872 | tf_op jit(solution)/shard_map/ppermute | solution.py:668

commit v13 on v12

--- a/solution.py
+++ b/solution.py
@@ -287,6 +287,32 @@
             out_ref[index * tall : (index + 1) * tall, :] = low_ref[:, pl.ds(at, head_dim)]
 
 
+def fetch_kernel(turn, place_ref, *refs):
+    weights, (held_ref, sems) = refs[:-2], refs[-2:]
+    for copy in fetch_columns(place_ref[1] ^ turn, weights, held_ref, sems):
+        copy.wait()
+
+
+def opening_kernel(place_ref, held_ref, mine_ref, theirs_ref, *refs):
+    tokens, refs = refs[:2], refs[2:]
+    out_refs, (part_ref, joined_ref, sems) = refs[:-3], refs[-3:]
+    side = place_ref[1]
+    tall, depth = joined_ref.shape
+    rows = tall // 2
+    near = pl.ds(pl.multiple_of(side * depth, depth), depth)
+    joins = []
+    for core, source in enumerate(tokens):
+        at = pl.ds(pl.multiple_of((side ^ core) * rows, rows), rows)
+        joins.append(pltpu.make_async_copy(source.at[:, near], joined_ref.at[at], sems.at[core]))
+        joins[core].start()
+    merge_kernel(place_ref, mine_ref, theirs_ref, *out_refs)
+    for copy in joins:
+        copy.wait()
+    for index in range(held_ref.shape[0]):
+        total = jnp.dot(joined_ref[...], held_ref[index], preferred_element_type=jnp.float32)
+        part_ref[index] = total.astype(jnp.bfloat16)
+
+
 def in_order(place, parts, start, ordered):
     for offset, part in enumerate(parts):
         tall = ordered.shape[0] // len(parts)
@@ -475,17 +501,28 @@
 
 
 def attended_kernel(chips, place_ref, *refs):
-    parts, (attended_ref, sums_ref) = refs[:chips], refs[chips:]
+    parts, (attended_ref, sums_ref, sems) = refs[:chips], refs[chips:]
     rows = attended_ref.shape[0]
     head_dim = sums_ref.shape[2]
     height = parts[0].shape[0] // 2
-    for core in range(2):
-        start = core * height
-        for offset, part in enumerate(parts):
-            head = core * chips + (place_ref[0] ^ offset)
-            at = pl.multiple_of(head * head_dim, head_dim)
-            attended_ref[:, pl.ds(at, head_dim)] = part[start : start + rows, :]
-            sums_ref[head] = part[start + rows : start + height, :].astype(jnp.float32)
+    heads = [
+        (part, core * height, core * chips + (place_ref[0] ^ offset))
+        for core in range(2)
+        for offset, part in enumerate(parts)
+    ]
+    copies = []
+    for index, (part, start, head) in enumerate(heads):
+        at = pl.ds(pl.multiple_of(head * head_dim, head_dim), head_dim)
+        copies.append(
+            pltpu.make_async_copy(
+                part.at[pl.ds(start, rows)], attended_ref.at[:, at], sems.at[index]
+            )
+        )
+        copies[index].start()
+    for part, start, head in heads:
+        sums_ref[head] = part[start + rows : start + height, :].astype(jnp.float32)
+    for copy in copies:
+        copy.wait()
 
 
 def sum_kernel(place_ref, first_ref, second_ref, kept_ref, hidden_ref):
@@ -514,12 +551,12 @@
     chip, side, column = (lax.axis_index(name) for name in ("seq", "sub", "head"))
     place = jnp.stack([chip, side, column, 1 - column])
 
-    def call(kernel, outs, *operands, scratch=(), hbm=0, limits=params, takes=1):
+    def call(kernel, outs, *operands, scratch=(), hbm=0, limits=params, outside=None, takes=1):
         return pl.pallas_call(
             kernel,
             out_shape=outs,
             in_specs=[smem] + [vmem] * (len(operands) - 1 - hbm) + [anywhere] * hbm,
-            out_specs=jax.tree.map(lambda _: vmem, outs),
+            out_specs=outside or jax.tree.map(lambda _: vmem, outs),
             scratch_shapes=list(scratch),
             compiler_params=limits,
             cost_estimate=pl.CostEstimate(
@@ -559,7 +596,7 @@
     )
     grads_other = to_sibling(grads_theirs)
 
-    def project(turn, weights, *arrived):
+    def project(turn, weights, tokens_other, *arrived):
         number = len(weights)
         outs = buffers(2 * number * rows) if turn == 0 else low(number, 2 * rows, width // 2)
 
@@ -569,7 +606,7 @@
             place,
             *arrived,
             stay(hidden),
-            hidden_other,
+            tokens_other,
             *(stay(weight) for weight in weights),
             scratch=[
                 pltpu.VMEM((2 * rows, half), jnp.bfloat16),
@@ -583,18 +620,36 @@
             takes=(8 if number == 2 else 0.1) if turn == 0 else 0.1,
         )
 
-    merged = call(merge_kernel, buffers(2 * block.shape[1]), place, grads_mine, grads_other)
+    early, late = (w_query, w_key), (w_value,)
+    fetched = call(
+        partial(fetch_kernel, 1),
+        pltpu.VMEM((2, half, width // 2), jnp.bfloat16),
+        place,
+        *(stay(weight) for weight in early),
+        scratch=[pltpu.SemaphoreType.DMA((2, 4))],
+        hbm=2,
+    )
+    *merged, early_part = call(
+        opening_kernel,
+        (*buffers(2 * block.shape[1]), low(2, 2 * rows, width // 2)),
+        place,
+        fetched,
+        grads_mine,
+        grads_other,
+        stay(hidden),
+        hidden_other,
+        scratch=[pltpu.VMEM((2 * rows, half), jnp.bfloat16), pltpu.SemaphoreType.DMA((2,))],
+        hbm=2,
+        takes=0.1,
+    )
     grads = exchange(merged)
-    hidden_other, _ = lax.optimization_barrier((hidden_other, merged[0]))
-    early, late = (w_query, w_key), (w_value,)
-    early_arrived = to_sibling(project(1, early))
-    late_arrived = to_sibling(project(1, late))
-    grads = exchange(call(merge_kernel, buffers(2 * block.shape[1]), place, grads_mine, grads_other))
-    early_arrived, _ = lax.optimization_barrier((early_arrived, grads[0]))
-    early_projected = project(0, early, early_arrived)
+    early_arrived = to_sibling(early_part)
+    early_projected = project(0, early, hidden_other, early_arrived)
     packed = exchange(early_projected)
-    late_arrived, _, _ = lax.optimization_barrier((late_arrived, early_projected[0], (grads[2], grads[3])))
-    late_projected = project(0, late, late_arrived)
+    late_tokens, *_ = lax.optimization_barrier((hidden_other, early_arrived))
+    late_arrived = to_sibling(project(1, late, late_tokens))
+    late_arrived, *_ = lax.optimization_barrier((late_arrived, grads[2], grads[3]))
+    late_projected = project(0, late, late_tokens, late_arrived)
     valued = exchange(late_projected)
     packed = lax.optimization_barrier((*packed, late_projected[0]))[:chips]
 
@@ -671,6 +726,8 @@
         (low(rows, width), jax.ShapeDtypeStruct((count, owned, head_dim), jnp.float32)),
         place,
         *returned,
+        scratch=[pltpu.SemaphoreType.DMA((count,))],
+        outside=(anywhere, vmem),
         takes=8,
     )
     first, second, _ = lax.optimization_barrier((first, second, attended))

time: 121 us -> 121 us (level)
  Pallas kernels: 38.2 us -> 39.8 us
    pallas_call x14, Pallas kernels: 38.2 us -> 39.8 us  [call(): pl.pallas_call(kernel, out_shape=outs, in_specs=[smem] + [vmem] * (len(op...]
  transfers between devices with their start and end apart: 30 -> 30, of which waited for: 5 -> 4; matrix products, arithmetic and copies ran while one was open for 0% -> 0% of each run, Pallas kernels for 28% -> 29%
where the time goes in v13:
time: 121 us
  starting transfers between devices  47.5 us (39%)
  Pallas kernels  39.8 us (33%)
  waiting for transfers between devices  32.9 us (27%)
    pallas_call x14, Pallas kernels, call(): pl.pallas_call(kernel, out_shape=outs, in_specs=[smem] + [vmem] * (len(op...  39.8 us
    ppermute x18, starting transfers between devices, exchange(): lax.ppermute(parts[offset], 'seq', [(at, at ^ offset) for at in range(chi...  36.8 us
    ppermute x18, waiting for transfers between devices, exchange(): lax.ppermute(parts[offset], 'seq', [(at, at ^ offset) for at in range(chi...  27.3 us
    ppermute x10, starting transfers between devices, to_sibling(): return lax.ppermute(piece, 'sub', swap)  6.34 us
    ppermute x1, waiting for transfers between devices, by_head(): second = lax.ppermute(kept, square, [(1, 2), (2, 1)])  5.57 us
    ppermute x1, starting transfers between devices, by_head(): second = lax.ppermute(kept, square, [(1, 2), (2, 1)])  3.16 us
  transfers between devices with their start and end apart: 30, of which 4 were waited for; matrix products, arithmetic and copies ran while one was open for 0% of the time, Pallas kernels for 29%

profile of v13, /device:TPU:1, one launch (start us, length us, event | category | flops | bytes accessed | tf_op | source)
XLA Modules:
  0.0 121.1 jit_solution(12236650216609130012)
XLA Ops:
  0.6 0.1 collective-permute-start.1
  0.8 0.1 pad_add_fusion.place_ref.refs_0_
  0.8 1.7 %shard_map.95 = (bf16[4,272,128]{2,1,0:T(8,128)(2,1)S(1)}, bf16[4,272,128]{2,1,0:T(8,128)(2,1)S(1)}) custom-call(s32[4]{0:T(128)S(1)} %pad_add_fusion.place_ref.refs_0_, bf16[256,1024]{1,0:T(8,128)(2,1)} %grads_ref.1, s32[8,256]{1,0:T(8,128)} %assign_ref.1), custom_call_target="tpu_custom_call" | custom-call | flops 1150000000 | bytes 1048576 | tf_op jit(solution)/shard_map/pallas_call | solution.py:555
  2.5 0.5 collective-permute-start
  3.1 2.1 %shard_map.94.held_ref = bf16[2,1024,512]{2,1,0:T(8,128)(2,1)S(1)} custom-call(s32[4]{0:T(128)S(1)} %pad_add_fusion.place_ref.refs_0_, bf16[1024,1024]{1,0:T(8,128)(2,1)} %refs_13_.3, bf16[1024,1024]{1,0:T(8,128)(2,1)} %refs_14_.3), custom_call_target="tpu_custom_call" | custom-call | flops 1150000000 | bytes 1048576 | tf_op jit(solution)/shard_map/pallas_call | solution.py:555
  5.2 0.0 collective-permute-done.theirs_ref
  5.2 0.0 collective-permute-done.1.refs_1_.refs_2_
  5.2 2.9 %shard_map.96 = (bf16[544,128]{1,0:T(8,128)(2,1)S(1)}, bf16[544,128]{1,0:T(8,128)(2,1)S(1)}, bf16[544,128]{1,0:T(8,128)(2,1)S(1)}, bf16[544,128]{1,0:T(8,128)(2,1)S(1)}, bf16[2,512,512]{2,1,0:T(8,128)(2,1)S(1)}) custom-call(s32[4]{0:T(128)S(1)} %pad_add_fusion.place_ref.refs_0_, bf16[2,1024,512]{2,1,0:T(8,128)(2,1)S(1)} %shard_map.94.held_ref, ...), custom_call_target="tpu_custom_call" | custom-call | flops 115000000 | bytes 1048576 | tf_op jit(solution)/shard_map/pallas_call | solution.py:555
  8.1 0.1 collective-permute-start.2
  8.2 3.8 %collective-permute-start.7 = (bf16[544,128]{1,0:T(8,128)(2,1)S(1)}, bf16[544,128]{1,0:T(8,128)(2,1)S(1)}, u32[]{:S(2)}, u32[]{:S(2)}) collective-permute-start(bf16[544,128]{1,0:T(8,128)(2,1)S(1)} %get-tuple-element.62), channel_id=1, source_target_pairs={{0,8},{4,12},{8,0},{12,4},{1,9},{5,13},{9,1},{13,5},{2,10},{6,14},... | collective-permute-start | bytes 417800 | tf_op jit(solution)/shard_map/ppermute | solution.py:575
  12.0 1.1 collective-permute-start.8
  13.1 0.0 collective-permute-done.2.refs_0_
  13.1 2.7 %shard_map.98 = bf16[1,512,512]{2,1,0:T(8,128)(2,1)S(1)} custom-call(s32[4]{0:T(128)S(1)} %pad_add_fusion.place_ref.refs_0_, bf16[256,2048]{1,0:T(8,128)(2,1)} %refs_1_.5, bf16[256,2048]{1,0:T(8,128)(2,1)S(1)} %collective-permute-done.1.refs_1_.refs_2_, bf16[1024,1024]{1,0:T(8,128)(2,1)} %refs_15_.3), custom_call_target="tpu_custom_call" | custom-call | flops 115000000 | bytes 1048576 | tf_op jit(solution)/shard_map/pallas_call | solution.py:555
  15.7 0.7 collective-permute-start.6
  16.4 3.6 %shard_map.97 = (bf16[1024,128]{1,0:T(8,128)(2,1)S(1)}, bf16[1024,128]{1,0:T(8,128)(2,1)S(1)}, bf16[1024,128]{1,0:T(8,128)(2,1)S(1)}, bf16[1024,128]{1,0:T(8,128)(2,1)S(1)}) custom-call(s32[4]{0:T(128)S(1)} %pad_add_fusion.place_ref.refs_0_, bf16[2,512,512]{2,1,0:T(8,128)(2,1)S(1)} %collective-permute-done.2.refs_0_, bf16[256,2048]{1,0:T(8,128)(2,1)} %refs_1_.5, ...), custom_call_target="tpu_custom_call" | custom-call | flops 9200000000 | bytes 1048576 | tf_op jit(solution)/shard_map/pallas_call | solution.py:555
  20.0 0.1 collective-permute-start.3
  20.1 2.5 %collective-permute-start.4 = (bf16[1024,128]{1,0:T(8,128)(2,1)S(1)}, bf16[1024,128]{1,0:T(8,128)(2,1)S(1)}, u32[]{:S(2)}, u32[]{:S(2)}) collective-permute-start(bf16[1024,128]{1,0:T(8,128)(2,1)S(1)} %get-tuple-element.59), channel_id=1, source_target_pairs={{0,8},{4,12},{8,0},{12,4},{1,9},{5,13},{9,1},{13,5},{2,10},{6,14},... | collective-permute-start | bytes 786440 | tf_op jit(solution)/shard_map/ppermute | solution.py:575
  22.6 2.8 %collective-permute-start.5 = (bf16[1024,128]{1,0:T(8,128)(2,1)S(1)}, bf16[1024,128]{1,0:T(8,128)(2,1)S(1)}, u32[]{:S(2)}, u32[]{:S(2)}) collective-permute-start(bf16[1024,128]{1,0:T(8,128)(2,1)S(1)} %get-tuple-element.60), channel_id=1, source_target_pairs={{0,12},{4,8},{8,4},{12,0},{1,13},{5,9},{9,5},{13,1},{2,14},{6,10},... | collective-permute-start | bytes 786440 | tf_op jit(solution)/shard_map/ppermute | solution.py:575
  25.4 0.0 collective-permute-done.8.refs_7_.refs_11_
  25.4 0.2 collective-permute-start.12
  25.6 2.8 %shard_map.99 = (bf16[512,128]{1,0:T(8,128)(2,1)S(1)}, bf16[512,128]{1,0:T(8,128)(2,1)S(1)}, bf16[512,128]{1,0:T(8,128)(2,1)S(1)}, bf16[512,128]{1,0:T(8,128)(2,1)S(1)}) custom-call(s32[4]{0:T(128)S(1)} %pad_add_fusion.place_ref.refs_0_, bf16[1,512,512]{2,1,0:T(8,128)(2,1)S(1)} %collective-permute-done.6.refs_0_, bf16[256,2048]{1,0:T(8,128)(2,1)} %refs_1_.5, ...), custom_call_target="tpu_custom_call" | custom-call | flops 115000000 | bytes 1048576 | tf_op jit(solution)/shard_map/pallas_call | solution.py:555
  28.4 1.4 %collective-permute-start.9 = (bf16[512,128]{1,0:T(8,128)(2,1)S(1)}, bf16[512,128]{1,0:T(8,128)(2,1)S(1)}, u32[]{:S(2)}, u32[]{:S(2)}) collective-permute-start(bf16[512,128]{1,0:T(8,128)(2,1)S(1)} %get-tuple-element.70), channel_id=1, source_target_pairs={{0,4},{4,0},{8,12},{12,8},{1,5},{5,1},{9,13},{13,9},{2,6},{6,2},{1... | collective-permute-start | bytes 393224 | tf_op jit(solution)/shard_map/ppermute | solution.py:575
  29.8 2.6 %collective-permute-done.3.refs_1_ = bf16[1024,128]{1,0:T(8,128)(2,1)S(1)} collective-permute-done((bf16[1024,128]{1,0:T(8,128)(2,1)S(1)}, bf16[1024,128]{1,0:T(8,128)(2,1)S(1)}, u32[]{:S(2)}, u32[]{:S(2)}) %collective-permute-start.3) | collective-permute-done | bytes 262176 | tf_op jit(solution)/shard_map/ppermute | solution.py:575
  32.4 0.0 collective-permute-start.10
  32.4 9.4 %collective-permute-done.4.refs_2_ = bf16[1024,128]{1,0:T(8,128)(2,1)S(1)} collective-permute-done((bf16[1024,128]{1,0:T(8,128)(2,1)S(1)}, bf16[1024,128]{1,0:T(8,128)(2,1)S(1)}, u32[]{:S(2)}, u32[]{:S(2)}) %collective-permute-start.4) | collective-permute-done | bytes 262176 | tf_op jit(solution)/shard_map/ppermute | solution.py:575
  41.8 3.5 %collective-permute-start.11 = (bf16[512,128]{1,0:T(8,128)(2,1)S(1)}, bf16[512,128]{1,0:T(8,128)(2,1)S(1)}, u32[]{:S(2)}, u32[]{:S(2)}) collective-permute-start(bf16[512,128]{1,0:T(8,128)(2,1)S(1)} %get-tuple-element.72), channel_id=1, source_target_pairs={{0,12},{4,8},{8,4},{12,0},{1,13},{5,9},{9,5},{13,1},{2,14},{6,10},... | collective-permute-start | bytes 393224 | tf_op jit(solution)/shard_map/ppermute | solution.py:575
  45.3 0.0 collective-permute-done.12.refs_5_.refs_9_
  45.3 6.5 %shard_map.100 = (bf16[512,128]{1,0:T(8,128)(2,1)S(1)}, bf16[512,128]{1,0:T(8,128)(2,1)S(1)}, bf16[512,128]{1,0:T(8,128)(2,1)S(1)}, bf16[512,128]{1,0:T(8,128)(2...) custom-call(s32[4]{0:T(128)S(1)} %pad_add_fusion.place_ref.refs_0_, ...), custom_call_target="tpu_custom_call" | custom-call | flops 8049999872 | bytes 1048576 | tf_op jit(solution)/shard_map/pallas_call | solution.py:555
  51.8 10.4 %collective-permute-start.14 = (bf16[512,128]{1,0:T(8,128)(2,1)S(1)}, bf16[512,128]{1,0:T(8,128)(2,1)S(1)}, u32[]{:S(2)}, u32[]{:S(2)}) collective-permute-start(bf16[512,128]{1,0:T(8,128)(2,1)S(1)} %get-tuple-element.87), channel_id=1, source_target_pairs={{0,8},{4,12},{8,0},{12,4},{1,9},{5,13},{9,1},{13,5},{2,10},{6,14},... | collective-permute-start | bytes 393224 | tf_op jit(solution)/shard_map/ppermute | solution.py:575
  62.2 0.0 collective-permute-start.25
  62.2 0.0 collective-permute-done.9.refs_5_
  62.2 1.3 %collective-permute-start.26 = (bf16[512,128]{1,0:T(8,128)(2,1)S(1)}, bf16[512,128]{1,0:T(8,128)(2,1)S(1)}, u32[]{:S(2)}, u32[]{:S(2)}) collective-permute-start(bf16[512,128]{1,0:T(8,128)(2,1)S(1)} %get-tuple-element.100), channel_id=1, source_target_pairs={{0,12},{4,8},{8,4},{12,0},{1,13},{5,9},{9,5},{13,1},{2,14},{6,10},... | collective-permute-start | bytes 393224 | tf_op jit(solution)/shard_map/ppermute | solution.py:575
  63.5 0.0 collective-permute-done.10.refs_6_
  63.5 0.0 collective-permute-done.11.refs_7_
  63.5 7.0 %shard_map.101 = (bf16[1024,128]{1,0:T(8,128)(2,1)S(1)}, bf16[1024,128]{1,0:T(8,128)(2,1)S(1)}, bf16[1024,128]{1,0:T(8,128)(2,1)S(1)}, bf16[1024,128]{1,0:T(8,12...) custom-call(s32[4]{0:T(128)S(1)} %pad_add_fusion.place_ref.refs_0_, ...), custom_call_target="tpu_custom_call" | custom-call | flops 11500000256 | bytes 1048576 | tf_op jit(solution)/shard_map/pallas_call | solution.py:555
  70.5 1.1 collective-permute-start.13
  71.6 0.0 collective-permute-done.14.refs_3_.refs_10_
  71.6 1.7 %collective-permute-start.15 = (bf16[1024,128]{1,0:T(8,128)(2,1)S(1)}, bf16[1024,128]{1,0:T(8,128)(2,1)S(1)}, u32[]{:S(2)}, u32[]{:S(2)}) collective-permute-start(bf16[1024,128]{1,0:T(8,128)(2,1)S(1)} %get-tuple-element.88), channel_id=1, source_target_pairs={{0,8},{4,12},{8,0},{12,4},{1,9},{5,13},{9,1},{13,5},{2,10},{6,14},... | collective-permute-start | bytes 786440 | tf_op jit(solution)/shard_map/ppermute | solution.py:575
  73.3 0.6 collective-permute-start.16
  73.9 0.3 collective-permute-start.20
  74.3 0.6 shard_map.104
  74.8 1.9 %collective-permute-start.27 = (bf16[4,512,128]{2,1,0:T(8,128)(2,1)S(1)}, bf16[4,512,128]{2,1,0:T(8,128)(2,1)S(1)}, u32[]{:S(2)}, u32[]{:S(2)}) collective-permute-start(bf16[4,512,128]{2,1,0:T(8,128)(2,1)S(1)} %shard_map.104), channel_id=1, source_target_pairs={{0,1},{1,0},{2,3},{3,2},{4,5},{5,4},{6,7},{7,6},{8,9},{9,8},{10,11... | collective-permute-start | bytes 1572872 | tf_op jit(solution)/shard_map/ppermute | solution.py:581
  76.7 15.2 %collective-permute-done.15.refs_2_ = bf16[1024,128]{1,0:T(8,128)(2,1)S(1)} collective-permute-done((bf16[1024,128]{1,0:T(8,128)(2,1)S(1)}, bf16[1024,128]{1,0:T(8,128)(2,1)S(1)}, u32[]{:S(2)}, u32[]{:S(2)}) %collective-permute-start.15) | collective-permute-done | bytes 262176 | tf_op jit(solution)/shard_map/ppermute | solution.py:575
  92.0 0.6 collective-permute-start.23
  92.6 0.0 collective-permute-start.24
  92.6 0.0 collective-permute-done.20.refs_1_
  92.6 1.2 %collective-permute-start.22 = (bf16[1024,128]{1,0:T(8,128)(2,1)S(1)}, bf16[1024,128]{1,0:T(8,128)(2,1)S(1)}, u32[]{:S(2)}, u32[]{:S(2)}) collective-permute-start(bf16[1024,128]{1,0:T(8,128)(2,1)S(1)} %collective-permute-done.20.refs_1_), channel_id=1, source_target_pairs={{0,1},{1,0},{2,3},{3,2},{4,5},{5,4},{6,7},{7,6},{8,9},{9,8},{10,11... | collective-permute-start | bytes 786440 | tf_op jit(solution)/shard_map/ppermute | solution.py:581
  93.8 0.0 collective-permute-done.13.theirs_ref
  93.8 0.6 shard_map.102
  94.4 0.1 collective-permute-start.21
  94.5 0.0 collective-permute-done.23.refs_6_
  94.5 5.1 %collective-permute-start.17 = (bf16[576,128]{1,0:T(8,128)(2,1)S(1)}, bf16[576,128]{1,0:T(8,128)(2,1)S(1)}, u32[]{:S(2)}, u32[]{:S(2)}) collective-permute-start(bf16[576,128]{1,0:T(8,128)(2,1)S(1)} %get-tuple-element.91), channel_id=1, source_target_pairs={{0,4},{4,0},{8,12},{12,8},{1,5},{5,1},{9,13},{13,9},{2,6},{6,2},{1... | collective-permute-start | bytes 442376 | tf_op jit(solution)/shard_map/ppermute | solution.py:575
  99.6 0.9 collective-permute-start.18
  100.5 1.2 collective-permute-start.19
  101.7 0.0 collective-permute-done.21.refs_4_
  101.7 2.9 %shard_map.105 = bf16[256,1024]{1,0:T(8,128)(2,1)S(1)} custom-call(s32[4]{0:T(128)S(1)} %pad_add_fusion.place_ref.refs_0_, bf16[1024,128]{1,0:T(8,128)(2,1)S(1)} %get-tuple-element.96.refs_0_, bf16[1024,128]{1,0:T(8,128)(2,1)S(1)} %collective-permute-done.20.refs_1_, bf16[1024,128]{1,0:T(8,128)(2,1)S(1)} %collective-permute-done.15.refs_2_, ...), custom_call_target="tpu_custom_call" | custom-call | flops 1150000000 | bytes 1048576 | tf_op jit(solution)/shard_map/pallas_call | solution.py:555
  104.7 1.2 %collective-permute-start.28 = (bf16[256,1024]{1,0:T(8,128)(2,1)S(1)}, bf16[256,1024]{1,0:T(8,128)(2,1)S(1)}, u32[]{:S(2)}, u32[]{:S(2)}) collective-permute-start(bf16[256,1024]{1,0:T(8,128)(2,1)S(1)} %shard_map.105), channel_id=1, source_target_pairs={{0,1},{1,3},{3,2},{2,0},{4,5},{5,7},{7,6},{6,4},{8,9},{9,11},{11,1... | collective-permute-start | bytes 1572872 | tf_op jit(solution)/shard_map/ppermute | solution.py:721
  105.9 2.9 %shard_map.106.kept_ref = bf16[256,1024]{1,0:T(8,128)(2,1)S(1)} custom-call(s32[4]{0:T(128)S(1)} %pad_add_fusion.place_ref.refs_0_, bf16[1024,128]{1,0:T(8,128)(2,1)S(1)} %get-tuple-element.96.refs_0_, bf16[1024,128]{1,0:T(8,128)(2,1)S(1)} %collective-permute-done.20.refs_1_, bf16[1024,128]{1,0:T(8,128)(2,1)S(1)} %collective-permute-done.15.refs_2_, ...), custom_call_target="tpu_custom_call" | custom-call | flops 1150000000 | bytes 1048576 | tf_op jit(solution)/shard_map/pallas_call | solution.py:555
  108.8 3.2 %collective-permute-start.29 = (bf16[256,1024]{1,0:T(8,128)(2,1)S(1)}, bf16[256,1024]{1,0:T(8,128)(2,1)S(1)}, u32[]{:S(2)}, u32[]{:S(2)}) collective-permute-start(bf16[256,1024]{1,0:T(8,128)(2,1)S(1)} %shard_map.106.kept_ref), channel_id=1, source_target_pairs={{1,2},{2,1},{5,6},{6,5},{9,10},{10,9},{13,14},{14,13},{17,18},{18,... | collective-permute-start | bytes 1572872 | tf_op jit(solution)/shard_map/ppermute | solution.py:723
  112.0 0.0 collective-permute-done.17.refs_1_
  112.0 0.0 collective-permute-done.19.refs_3_
  112.0 2.0 %shard_map.103 = (bf16[256,1024]{1,0:T(8,128)(2,1)}, f32[8,32,128]{2,1,0:T(8,128)}) custom-call(s32[4]{0:T(128)S(1)} %pad_add_fusion.place_ref.refs_0_, bf16[576,128]{1,0:T(8,128)(2,1)S(1)} %get-tuple-element.90.refs_0_, bf16[576,128]{1,0:T(8,128)(2,1)S(1)} %collective-permute-done.17.refs_1_, bf16[576,128]{1,0:T(8,128)(2,1)S(1)} %collective-permute-done.18.refs_2_, ...), custom_call_target="tpu_custom_call" | custom-call | flops 9200000000 | bytes 1048576 | tf_op jit(solution)/shard_map/pallas_call | solution.py:555
  114.0 5.6 %collective-permute-done.29.second_ref = bf16[256,1024]{1,0:T(8,128)(2,1)S(1)} collective-permute-done((bf16[256,1024]{1,0:T(8,128)(2,1)S(1)}, bf16[256,1024]{1,0:T(8,128)(2,1)S(1)}, u32[]{:S(2)}, u32[]{:S(2)}) %collective-permute-start.29) | collective-permute-done | bytes 524320 | tf_op jit(solution)/shard_map/ppermute | solution.py:723
  119.6 1.5 %shard_map.107 = bf16[256,1024]{1,0:T(8,128)(2,1)} custom-call(s32[4]{0:T(128)S(1)} %pad_add_fusion.place_ref.refs_0_, bf16[256,1024]{1,0:T(8,128)(2,1)S(1)} %collective-permute-done.28.first_ref, bf16[256,1024]{1,0:T(8,128)(2,1)S(1)} %collective-permute-done.29.second_ref, bf16[256,1024]{1,0:T(8,128)(2,1)S(1)} %shard_map.106.kept_ref), custom_call_target="tpu_custom_call" | custom-call | flops 1150000000 | bytes 1048576 | tf_op jit(solution)/shard_map/pallas_call | solution.py:555
  (19 shorter events, 0.0 us)
Async XLA Ops:
  0.6 4.6 %collective-permute-start.1 = (bf16[256,2048]{1,0:T(8,128)(2,1)}, bf16[256,2048]{1,0:T(8,128)(2,1)S(1)}, u32[]{:S(2)}, u32[]{:S(2)}) collective-permute-start(bf16[256,2048]{1,0:T(8,128)(2,1)} %refs_1_.5), channel_id=1, source_target_pairs={{0,1},{1,0},{2,3},{3,2},{4,5},{5,4},{6,7},{7,6},{8,9},{9,8},{10,11... | collective-permute-start | bytes 3145736 | tf_op jit(solution)/shard_map/ppermute | solution.py:581
  2.5 2.6 %collective-permute-start = (bf16[4,272,128]{2,1,0:T(8,128)(2,1)S(1)}, bf16[4,272,128]{2,1,0:T(8,128)(2,1)S(1)}, u32[]{:S(2)}, u32[]{:S(2)}) collective-permute-start(bf16[4,272,128]{2,1,0:T(8,128)(2,1)S(1)} %get-tuple-element.55), channel_id=1, source_target_pairs={{0,1},{1,0},{2,3},{3,2},{4,5},{5,4},{6,7},{7,6},{8,9},{9,8},{10,11... | collective-permute-start | bytes 835592 | tf_op jit(solution)/shard_map/ppermute | solution.py:581
  8.1 5.0 %collective-permute-start.2 = (bf16[2,512,512]{2,1,0:T(8,128)(2,1)S(1)}, bf16[2,512,512]{2,1,0:T(8,128)(2,1)S(1)}, u32[]{:S(2)}, u32[]{:S(2)}) collective-permute-start(bf16[2,512,512]{2,1,0:T(8,128)(2,1)S(1)} %get-tuple-element.56), channel_id=1, source_target_pairs={{0,1},{1,0},{2,3},{3,2},{4,5},{5,4},{6,7},{7,6},{8,9},{9,8},{10,11... | collective-permute-start | bytes 3145736 | tf_op jit(solution)/shard_map/ppermute | solution.py:581
  8.2 14.4 %collective-permute-start.7 = (bf16[544,128]{1,0:T(8,128)(2,1)S(1)}, bf16[544,128]{1,0:T(8,128)(2,1)S(1)}, u32[]{:S(2)}, u32[]{:S(2)}) collective-permute-start(bf16[544,128]{1,0:T(8,128)(2,1)S(1)} %get-tuple-element.62), channel_id=1, source_target_pairs={{0,8},{4,12},{8,0},{12,4},{1,9},{5,13},{9,1},{13,5},{2,10},{6,14},... | collective-permute-start | bytes 417800 | tf_op jit(solution)/shard_map/ppermute | solution.py:575
  12.0 13.4 %collective-permute-start.8 = (bf16[544,128]{1,0:T(8,128)(2,1)S(1)}, bf16[544,128]{1,0:T(8,128)(2,1)S(1)}, u32[]{:S(2)}, u32[]{:S(2)}) collective-permute-start(bf16[544,128]{1,0:T(8,128)(2,1)S(1)} %get-tuple-element.63), channel_id=1, source_target_pairs={{0,12},{4,8},{8,4},{12,0},{1,13},{5,9},{9,5},{13,1},{2,14},{6,10},... | collective-permute-start | bytes 417800 | tf_op jit(solution)/shard_map/ppermute | solution.py:575
  15.7 9.8 %collective-permute-start.6 = (bf16[1,512,512]{2,1,0:T(8,128)(2,1)S(1)}, bf16[1,512,512]{2,1,0:T(8,128)(2,1)S(1)}, u32[]{:S(2)}, u32[]{:S(2)}) collective-permute-start(bf16[1,512,512]{2,1,0:T(8,128)(2,1)S(1)} %shard_map.98), channel_id=1, source_target_pairs={{0,1},{1,0},{2,3},{3,2},{4,5},{5,4},{6,7},{7,6},{8,9},{9,8},{10,11... | collective-permute-start | bytes 1572872 | tf_op jit(solution)/shard_map/ppermute | solution.py:581
  20.0 12.4 %collective-permute-start.3 = (bf16[1024,128]{1,0:T(8,128)(2,1)S(1)}, bf16[1024,128]{1,0:T(8,128)(2,1)S(1)}, u32[]{:S(2)}, u32[]{:S(2)}) collective-permute-start(bf16[1024,128]{1,0:T(8,128)(2,1)S(1)} %get-tuple-element.58), channel_id=1, source_target_pairs={{0,4},{4,0},{8,12},{12,8},{1,5},{5,1},{9,13},{13,9},{2,6},{6,2},{1... | collective-permute-start | bytes 786440 | tf_op jit(solution)/shard_map/ppermute | solution.py:575
  20.1 21.7 %collective-permute-start.4 = (bf16[1024,128]{1,0:T(8,128)(2,1)S(1)}, bf16[1024,128]{1,0:T(8,128)(2,1)S(1)}, u32[]{:S(2)}, u32[]{:S(2)}) collective-permute-start(bf16[1024,128]{1,0:T(8,128)(2,1)S(1)} %get-tuple-element.59), channel_id=1, source_target_pairs={{0,8},{4,12},{8,0},{12,4},{1,9},{5,13},{9,1},{13,5},{2,10},{6,14},... | collective-permute-start | bytes 786440 | tf_op jit(solution)/shard_map/ppermute | solution.py:575
  22.6 22.8 %collective-permute-start.5 = (bf16[1024,128]{1,0:T(8,128)(2,1)S(1)}, bf16[1024,128]{1,0:T(8,128)(2,1)S(1)}, u32[]{:S(2)}, u32[]{:S(2)}) collective-permute-start(bf16[1024,128]{1,0:T(8,128)(2,1)S(1)} %get-tuple-element.60), channel_id=1, source_target_pairs={{0,12},{4,8},{8,4},{12,0},{1,13},{5,9},{9,5},{13,1},{2,14},{6,10},... | collective-permute-start | bytes 786440 | tf_op jit(solution)/shard_map/ppermute | solution.py:575
  25.4 19.9 %copy-start.3 = (s32[256]{0:T(256)S(1)}, s32[256]{0:T(256)}, u32[]{:S(2)}) copy-start(s32[256]{0:T(256)} %param.11) | copy-start | bytes 3076
  25.4 19.9 %collective-permute-start.12 = (bf16[544,128]{1,0:T(8,128)(2,1)S(1)}, bf16[544,128]{1,0:T(8,128)(2,1)S(1)}, u32[]{:S(2)}, u32[]{:S(2)}) collective-permute-start(bf16[544,128]{1,0:T(8,128)(2,1)S(1)} %get-tuple-element.74), channel_id=1, source_target_pairs={{0,4},{4,0},{8,12},{12,8},{1,5},{5,1},{9,13},{13,9},{2,6},{6,2},{1... | collective-permute-start | bytes 417800 | tf_op jit(solution)/shard_map/ppermute | solution.py:575
  28.4 33.8 %collective-permute-start.9 = (bf16[512,128]{1,0:T(8,128)(2,1)S(1)}, bf16[512,128]{1,0:T(8,128)(2,1)S(1)}, u32[]{:S(2)}, u32[]{:S(2)}) collective-permute-start(bf16[512,128]{1,0:T(8,128)(2,1)S(1)} %get-tuple-element.70), channel_id=1, source_target_pairs={{0,4},{4,0},{8,12},{12,8},{1,5},{5,1},{9,13},{13,9},{2,6},{6,2},{1... | collective-permute-start | bytes 393224 | tf_op jit(solution)/shard_map/ppermute | solution.py:575
  32.4 31.0 %collective-permute-start.10 = (bf16[512,128]{1,0:T(8,128)(2,1)S(1)}, bf16[512,128]{1,0:T(8,128)(2,1)S(1)}, u32[]{:S(2)}, u32[]{:S(2)}) collective-permute-start(bf16[512,128]{1,0:T(8,128)(2,1)S(1)} %get-tuple-element.71), channel_id=1, source_target_pairs={{0,8},{4,12},{8,0},{12,4},{1,9},{5,13},{9,1},{13,5},{2,10},{6,14},... | collective-permute-start | bytes 393224 | tf_op jit(solution)/shard_map/ppermute | solution.py:575
  41.8 21.6 %collective-permute-start.11 = (bf16[512,128]{1,0:T(8,128)(2,1)S(1)}, bf16[512,128]{1,0:T(8,128)(2,1)S(1)}, u32[]{:S(2)}, u32[]{:S(2)}) collective-permute-start(bf16[512,128]{1,0:T(8,128)(2,1)S(1)} %get-tuple-element.72), channel_id=1, source_target_pairs={{0,12},{4,8},{8,4},{12,0},{1,13},{5,9},{9,5},{13,1},{2,14},{6,10},... | collective-permute-start | bytes 393224 | tf_op jit(solution)/shard_map/ppermute | solution.py:575
  51.8 19.8 %collective-permute-start.14 = (bf16[512,128]{1,0:T(8,128)(2,1)S(1)}, bf16[512,128]{1,0:T(8,128)(2,1)S(1)}, u32[]{:S(2)}, u32[]{:S(2)}) collective-permute-start(bf16[512,128]{1,0:T(8,128)(2,1)S(1)} %get-tuple-element.87), channel_id=1, source_target_pairs={{0,8},{4,12},{8,0},{12,4},{1,9},{5,13},{9,1},{13,5},{2,10},{6,14},... | collective-permute-start | bytes 393224 | tf_op jit(solution)/shard_map/ppermute | solution.py:575
  62.2 11.7 %collective-permute-start.25 = (bf16[512,128]{1,0:T(8,128)(2,1)S(1)}, bf16[512,128]{1,0:T(8,128)(2,1)S(1)}, u32[]{:S(2)}, u32[]{:S(2)}) collective-permute-start(bf16[512,128]{1,0:T(8,128)(2,1)S(1)} %get-tuple-element.99), channel_id=1, source_target_pairs={{0,4},{4,0},{8,12},{12,8},{1,5},{5,1},{9,13},{13,9},{2,6},{6,2},{1... | collective-permute-start | bytes 393224 | tf_op jit(solution)/shard_map/ppermute | solution.py:575
  62.2 12.1 %collective-permute-start.26 = (bf16[512,128]{1,0:T(8,128)(2,1)S(1)}, bf16[512,128]{1,0:T(8,128)(2,1)S(1)}, u32[]{:S(2)}, u32[]{:S(2)}) collective-permute-start(bf16[512,128]{1,0:T(8,128)(2,1)S(1)} %get-tuple-element.100), channel_id=1, source_target_pairs={{0,12},{4,8},{8,4},{12,0},{1,13},{5,9},{9,5},{13,1},{2,14},{6,10},... | collective-permute-start | bytes 393224 | tf_op jit(solution)/shard_map/ppermute | solution.py:575
  70.5 23.3 %collective-permute-start.13 = (bf16[4,288,128]{2,1,0:T(8,128)(2,1)S(1)}, bf16[4,288,128]{2,1,0:T(8,128)(2,1)S(1)}, u32[]{:S(2)}, u32[]{:S(2)}) collective-permute-start(bf16[4,288,128]{2,1,0:T(8,128)(2,1)S(1)} %get-tuple-element.78), channel_id=1, source_target_pairs={{0,1},{1,0},{2,3},{3,2},{4,5},{5,4},{6,7},{7,6},{8,9},{9,8},{10,11... | collective-permute-start | bytes 884744 | tf_op jit(solution)/shard_map/ppermute | solution.py:581
  71.6 20.4 %collective-permute-start.15 = (bf16[1024,128]{1,0:T(8,128)(2,1)S(1)}, bf16[1024,128]{1,0:T(8,128)(2,1)S(1)}, u32[]{:S(2)}, u32[]{:S(2)}) collective-permute-start(bf16[1024,128]{1,0:T(8,128)(2,1)S(1)} %get-tuple-element.88), channel_id=1, source_target_pairs={{0,8},{4,12},{8,0},{12,4},{1,9},{5,13},{9,1},{13,5},{2,10},{6,14},... | collective-permute-start | bytes 786440 | tf_op jit(solution)/shard_map/ppermute | solution.py:575
  73.3 19.3 %collective-permute-start.16 = (bf16[1024,128]{1,0:T(8,128)(2,1)S(1)}, bf16[1024,128]{1,0:T(8,128)(2,1)S(1)}, u32[]{:S(2)}, u32[]{:S(2)}) collective-permute-start(bf16[1024,128]{1,0:T(8,128)(2,1)S(1)} %get-tuple-element.89), channel_id=1, source_target_pairs={{0,12},{4,8},{8,4},{12,0},{1,13},{5,9},{9,5},{13,1},{2,14},{6,10},... | collective-permute-start | bytes 786440 | tf_op jit(solution)/shard_map/ppermute | solution.py:575
  73.9 18.6 %collective-permute-start.20 = (bf16[1024,128]{1,0:T(8,128)(2,1)S(1)}, bf16[1024,128]{1,0:T(8,128)(2,1)S(1)}, u32[]{:S(2)}, u32[]{:S(2)}) collective-permute-start(bf16[1024,128]{1,0:T(8,128)(2,1)S(1)} %get-tuple-element.97), channel_id=1, source_target_pairs={{0,4},{4,0},{8,12},{12,8},{1,5},{5,1},{9,13},{13,9},{2,6},{6,2},{1... | collective-permute-start | bytes 786440 | tf_op jit(solution)/shard_map/ppermute | solution.py:575
  74.3 27.5 %copy-start.2 = (bf16[1024,1024]{1,0:T(8,128)(2,1)S(1)}, bf16[1024,1024]{1,0:T(8,128)(2,1)}, u32[]{:S(2)}) copy-start(bf16[1024,1024]{1,0:T(8,128)(2,1)} %refs_14_.3) | copy-start | bytes 6291460
  74.8 26.9 %collective-permute-start.27 = (bf16[4,512,128]{2,1,0:T(8,128)(2,1)S(1)}, bf16[4,512,128]{2,1,0:T(8,128)(2,1)S(1)}, u32[]{:S(2)}, u32[]{:S(2)}) collective-permute-start(bf16[4,512,128]{2,1,0:T(8,128)(2,1)S(1)} %shard_map.104), channel_id=1, source_target_pairs={{0,1},{1,0},{2,3},{3,2},{4,5},{5,4},{6,7},{7,6},{8,9},{9,8},{10,11... | collective-permute-start | bytes 1572872 | tf_op jit(solution)/shard_map/ppermute | solution.py:581
  92.0 2.5 %collective-permute-start.23 = (bf16[1024,128]{1,0:T(8,128)(2,1)S(1)}, bf16[1024,128]{1,0:T(8,128)(2,1)S(1)}, u32[]{:S(2)}, u32[]{:S(2)}) collective-permute-start(bf16[1024,128]{1,0:T(8,128)(2,1)S(1)} %collective-permute-done.15.refs_2_), channel_id=1, source_target_pairs={{0,1},{1,0},{2,3},{3,2},{4,5},{5,4},{6,7},{7,6},{8,9},{9,8},{10,11... | collective-permute-start | bytes 786440 | tf_op jit(solution)/shard_map/ppermute | solution.py:581
  92.6 7.0 %collective-permute-start.24 = (bf16[1024,128]{1,0:T(8,128)(2,1)S(1)}, bf16[1024,128]{1,0:T(8,128)(2,1)S(1)}, u32[]{:S(2)}, u32[]{:S(2)}) collective-permute-start(bf16[1024,128]{1,0:T(8,128)(2,1)S(1)} %collective-permute-done.16.refs_3_), channel_id=1, source_target_pairs={{0,1},{1,0},{2,3},{3,2},{4,5},{5,4},{6,7},{7,6},{8,9},{9,8},{10,11... | collective-permute-start | bytes 786440 | tf_op jit(solution)/shard_map/ppermute | solution.py:581
  92.6 7.9 %collective-permute-start.22 = (bf16[1024,128]{1,0:T(8,128)(2,1)S(1)}, bf16[1024,128]{1,0:T(8,128)(2,1)S(1)}, u32[]{:S(2)}, u32[]{:S(2)}) collective-permute-start(bf16[1024,128]{1,0:T(8,128)(2,1)S(1)} %collective-permute-done.20.refs_1_), channel_id=1, source_target_pairs={{0,1},{1,0},{2,3},{3,2},{4,5},{5,4},{6,7},{7,6},{8,9},{9,8},{10,11... | collective-permute-start | bytes 786440 | tf_op jit(solution)/shard_map/ppermute | solution.py:581
  93.8 7.9 %copy-start = (bf16[1024,1024]{1,0:T(8,128)(2,1)S(1)}, bf16[1024,1024]{1,0:T(8,128)(2,1)}, u32[]{:S(2)}) copy-start(bf16[1024,1024]{1,0:T(8,128)(2,1)} %refs_15_.3) | copy-start | bytes 6291460
  93.8 7.9 %copy-start.1 = (bf16[1024,1024]{1,0:T(8,128)(2,1)S(1)}, bf16[1024,1024]{1,0:T(8,128)(2,1)}, u32[]{:S(2)}) copy-start(bf16[1024,1024]{1,0:T(8,128)(2,1)} %refs_13_.3) | copy-start | bytes 6291460
  94.4 7.3 %collective-permute-start.21 = (bf16[1024,128]{1,0:T(8,128)(2,1)S(1)}, bf16[1024,128]{1,0:T(8,128)(2,1)S(1)}, u32[]{:S(2)}, u32[]{:S(2)}) collective-permute-start(bf16[1024,128]{1,0:T(8,128)(2,1)S(1)} %get-tuple-element.96.refs_0_), channel_id=1, source_target_pairs={{0,1},{1,0},{2,3},{3,2},{4,5},{5,4},{6,7},{7,6},{8,9},{9,8},{10,11... | collective-permute-start | bytes 786440 | tf_op jit(solution)/shard_map/ppermute | solution.py:581
  94.5 17.5 %collective-permute-start.17 = (bf16[576,128]{1,0:T(8,128)(2,1)S(1)}, bf16[576,128]{1,0:T(8,128)(2,1)S(1)}, u32[]{:S(2)}, u32[]{:S(2)}) collective-permute-start(bf16[576,128]{1,0:T(8,128)(2,1)S(1)} %get-tuple-element.91), channel_id=1, source_target_pairs={{0,4},{4,0},{8,12},{12,8},{1,5},{5,1},{9,13},{13,9},{2,6},{6,2},{1... | collective-permute-start | bytes 442376 | tf_op jit(solution)/shard_map/ppermute | solution.py:575
  99.6 12.4 %collective-permute-start.18 = (bf16[576,128]{1,0:T(8,128)(2,1)S(1)}, bf16[576,128]{1,0:T(8,128)(2,1)S(1)}, u32[]{:S(2)}, u32[]{:S(2)}) collective-permute-start(bf16[576,128]{1,0:T(8,128)(2,1)S(1)} %get-tuple-element.92), channel_id=1, source_target_pairs={{0,8},{4,12},{8,0},{12,4},{1,9},{5,13},{9,1},{13,5},{2,10},{6,14},... | collective-permute-start | bytes 442376 | tf_op jit(solution)/shard_map/ppermute | solution.py:575
  100.5 11.5 %collective-permute-start.19 = (bf16[576,128]{1,0:T(8,128)(2,1)S(1)}, bf16[576,128]{1,0:T(8,128)(2,1)S(1)}, u32[]{:S(2)}, u32[]{:S(2)}) collective-permute-start(bf16[576,128]{1,0:T(8,128)(2,1)S(1)} %get-tuple-element.93), channel_id=1, source_target_pairs={{0,12},{4,8},{8,4},{12,0},{1,13},{5,9},{9,5},{13,1},{2,14},{6,10},... | collective-permute-start | bytes 442376 | tf_op jit(solution)/shard_map/ppermute | solution.py:575
  104.7 15.0 %collective-permute-start.28 = (bf16[256,1024]{1,0:T(8,128)(2,1)S(1)}, bf16[256,1024]{1,0:T(8,128)(2,1)S(1)}, u32[]{:S(2)}, u32[]{:S(2)}) collective-permute-start(bf16[256,1024]{1,0:T(8,128)(2,1)S(1)} %shard_map.105), channel_id=1, source_target_pairs={{0,1},{1,3},{3,2},{2,0},{4,5},{5,7},{7,6},{6,4},{8,9},{9,11},{11,1... | collective-permute-start | bytes 1572872 | tf_op jit(solution)/shard_map/ppermute | solution.py:721
  108.8 10.8 %collective-permute-start.29 = (bf16[256,1024]{1,0:T(8,128)(2,1)S(1)}, bf16[256,1024]{1,0:T(8,128)(2,1)S(1)}, u32[]{:S(2)}, u32[]{:S(2)}) collective-permute-start(bf16[256,1024]{1,0:T(8,128)(2,1)S(1)} %shard_map.106.kept_ref), channel_id=1, source_target_pairs={{1,2},{2,1},{5,6},{6,5},{9,10},{10,9},{13,14},{14,13},{17,18},{18,... | collective-permute-start | bytes 1572872 | tf_op jit(solution)/shard_map/ppermute | solution.py:723

commit v14 on v13

--- a/solution.py
+++ b/solution.py
@@ -501,28 +501,17 @@
 
 
 def attended_kernel(chips, place_ref, *refs):
-    parts, (attended_ref, sums_ref, sems) = refs[:chips], refs[chips:]
+    parts, (attended_ref, sums_ref) = refs[:chips], refs[chips:]
     rows = attended_ref.shape[0]
     head_dim = sums_ref.shape[2]
     height = parts[0].shape[0] // 2
-    heads = [
-        (part, core * height, core * chips + (place_ref[0] ^ offset))
-        for core in range(2)
-        for offset, part in enumerate(parts)
-    ]
-    copies = []
-    for index, (part, start, head) in enumerate(heads):
-        at = pl.ds(pl.multiple_of(head * head_dim, head_dim), head_dim)
-        copies.append(
-            pltpu.make_async_copy(
-                part.at[pl.ds(start, rows)], attended_ref.at[:, at], sems.at[index]
-            )
-        )
-        copies[index].start()
-    for part, start, head in heads:
-        sums_ref[head] = part[start + rows : start + height, :].astype(jnp.float32)
-    for copy in copies:
-        copy.wait()
+    for core in range(2):
+        start = core * height
+        for offset, part in enumerate(parts):
+            head = core * chips + (place_ref[0] ^ offset)
+            at = pl.multiple_of(head * head_dim, head_dim)
+            attended_ref[:, pl.ds(at, head_dim)] = part[start : start + rows, :]
+            sums_ref[head] = part[start + rows : start + height, :].astype(jnp.float32)
 
 
 def sum_kernel(place_ref, first_ref, second_ref, kept_ref, hidden_ref):
@@ -551,12 +540,12 @@
     chip, side, column = (lax.axis_index(name) for name in ("seq", "sub", "head"))
     place = jnp.stack([chip, side, column, 1 - column])
 
-    def call(kernel, outs, *operands, scratch=(), hbm=0, limits=params, outside=None, takes=1):
+    def call(kernel, outs, *operands, scratch=(), hbm=0, limits=params, takes=1):
         return pl.pallas_call(
             kernel,
             out_shape=outs,
             in_specs=[smem] + [vmem] * (len(operands) - 1 - hbm) + [anywhere] * hbm,
-            out_specs=outside or jax.tree.map(lambda _: vmem, outs),
+            out_specs=jax.tree.map(lambda _: vmem, outs),
             scratch_shapes=list(scratch),
             compiler_params=limits,
             cost_estimate=pl.CostEstimate(
@@ -693,8 +682,10 @@
     outputs = call(
         merge_kernel, buffers(2 * (rows + owned)), place, attended_mine, to_sibling(attended_theirs)
     )
-    back = (lax.optimization_barrier((back[0], outputs[0]))[0], *back[1:])
-    back_other = tuple(to_sibling(part) for part in back)
+    early_back, _ = lax.optimization_barrier((back[2], outputs[0]))
+    back_other = tuple(
+        to_sibling(early_back if offset == 2 else part) for offset, part in enumerate(back)
+    )
     value_other = to_sibling(
         call(join_kernel, low(chips, 2 * rows, head_dim), place, *value_back)
     )
@@ -726,8 +717,6 @@
         (low(rows, width), jax.ShapeDtypeStruct((count, owned, head_dim), jnp.float32)),
         place,
         *returned,
-        scratch=[pltpu.SemaphoreType.DMA((count,))],
-        outside=(anywhere, vmem),
         takes=8,
     )
     first, second, _ = lax.optimization_barrier((first, second, attended))

time: 121 us -> 121 us (level)
    ppermute x18, starting transfers between devices: 36.8 us -> 34 us  [exchange(): lax.ppermute(parts[offset], 'seq', [(at, at ^ offset) for at in range(chi...]
    ppermute x10, starting transfers between devices: 6.34 us -> 8.75 us  [to_sibling(): return lax.ppermute(piece, 'sub', swap)]
  transfers between devices with their start and end apart: 30 -> 30, of which waited for: 4 -> 6; matrix products, arithmetic and copies ran while one was open for 0% -> 0% of each run, Pallas kernels for 29% -> 29%
where the time goes in v14:
time: 121 us
  starting transfers between devices  47.1 us (39%)
  Pallas kernels  39.3 us (32%)
  waiting for transfers between devices  33.3 us (28%)
    pallas_call x14, Pallas kernels, call(): pl.pallas_call(kernel, out_shape=outs, in_specs=[smem] + [vmem] * (len(op...  39.3 us
    ppermute x18, starting transfers between devices, exchange(): lax.ppermute(parts[offset], 'seq', [(at, at ^ offset) for at in range(chi...  34 us
    ppermute x18, waiting for transfers between devices, exchange(): lax.ppermute(parts[offset], 'seq', [(at, at ^ offset) for at in range(chi...  27.1 us
    ppermute x10, starting transfers between devices, to_sibling(): return lax.ppermute(piece, 'sub', swap)  8.75 us
    ppermute x1, waiting for transfers between devices, by_head(): second = lax.ppermute(kept, square, [(1, 2), (2, 1)])  6.1 us
    ppermute x1, starting transfers between devices, by_head(): second = lax.ppermute(kept, square, [(1, 2), (2, 1)])  3.17 us
  transfers between devices with their start and end apart: 30, of which 6 were waited for; matrix products, arithmetic and copies ran while one was open for 0% of the time, Pallas kernels for 29%

profile of v14, /device:TPU:1, one launch (start us, length us, event | category | flops | bytes accessed | tf_op | source)
XLA Modules:
  0.0 120.6 jit_solution(708820343348549823)
XLA Ops:
  0.6 0.1 collective-permute-start.1
  0.8 0.1 pad_add_fusion.place_ref.refs_0_
  0.8 1.7 %shard_map.95 = (bf16[4,272,128]{2,1,0:T(8,128)(2,1)S(1)}, bf16[4,272,128]{2,1,0:T(8,128)(2,1)S(1)}) custom-call(s32[4]{0:T(128)S(1)} %pad_add_fusion.place_ref.refs_0_, bf16[256,1024]{1,0:T(8,128)(2,1)} %grads_ref.1, s32[8,256]{1,0:T(8,128)} %assign_ref.1), custom_call_target="tpu_custom_call" | custom-call | flops 1150000000 | bytes 1048576 | tf_op jit(solution)/shard_map/pallas_call | solution.py:544
  2.5 0.5 collective-permute-start
  3.1 2.1 %shard_map.94.held_ref = bf16[2,1024,512]{2,1,0:T(8,128)(2,1)S(1)} custom-call(s32[4]{0:T(128)S(1)} %pad_add_fusion.place_ref.refs_0_, bf16[1024,1024]{1,0:T(8,128)(2,1)} %refs_13_.3, bf16[1024,1024]{1,0:T(8,128)(2,1)} %refs_14_.3), custom_call_target="tpu_custom_call" | custom-call | flops 1150000000 | bytes 1048576 | tf_op jit(solution)/shard_map/pallas_call | solution.py:544
  5.2 0.0 collective-permute-done.theirs_ref
  5.2 0.0 collective-permute-done.1.refs_1_.refs_2_
  5.2 2.9 %shard_map.96 = (bf16[544,128]{1,0:T(8,128)(2,1)S(1)}, bf16[544,128]{1,0:T(8,128)(2,1)S(1)}, bf16[544,128]{1,0:T(8,128)(2,1)S(1)}, bf16[544,128]{1,0:T(8,128)(2,1)S(1)}, bf16[2,512,512]{2,1,0:T(8,128)(2,1)S(1)}) custom-call(s32[4]{0:T(128)S(1)} %pad_add_fusion.place_ref.refs_0_, bf16[2,1024,512]{2,1,0:T(8,128)(2,1)S(1)} %shard_map.94.held_ref, ...), custom_call_target="tpu_custom_call" | custom-call | flops 115000000 | bytes 1048576 | tf_op jit(solution)/shard_map/pallas_call | solution.py:544
  8.1 0.1 collective-permute-start.2
  8.2 3.8 %collective-permute-start.7 = (bf16[544,128]{1,0:T(8,128)(2,1)S(1)}, bf16[544,128]{1,0:T(8,128)(2,1)S(1)}, u32[]{:S(2)}, u32[]{:S(2)}) collective-permute-start(bf16[544,128]{1,0:T(8,128)(2,1)S(1)} %get-tuple-element.62), channel_id=1, source_target_pairs={{0,8},{4,12},{8,0},{12,4},{1,9},{5,13},{9,1},{13,5},{2,10},{6,14},... | collective-permute-start | bytes 417800 | tf_op jit(solution)/shard_map/ppermute | solution.py:564
  12.0 1.1 collective-permute-start.8
  13.1 0.0 collective-permute-done.2.refs_0_
  13.1 2.7 %shard_map.98 = bf16[1,512,512]{2,1,0:T(8,128)(2,1)S(1)} custom-call(s32[4]{0:T(128)S(1)} %pad_add_fusion.place_ref.refs_0_, bf16[256,2048]{1,0:T(8,128)(2,1)} %refs_1_.5, bf16[256,2048]{1,0:T(8,128)(2,1)S(1)} %collective-permute-done.1.refs_1_.refs_2_, bf16[1024,1024]{1,0:T(8,128)(2,1)} %refs_15_.3), custom_call_target="tpu_custom_call" | custom-call | flops 115000000 | bytes 1048576 | tf_op jit(solution)/shard_map/pallas_call | solution.py:544
  15.7 0.7 collective-permute-start.6
  16.4 3.6 %shard_map.97 = (bf16[1024,128]{1,0:T(8,128)(2,1)S(1)}, bf16[1024,128]{1,0:T(8,128)(2,1)S(1)}, bf16[1024,128]{1,0:T(8,128)(2,1)S(1)}, bf16[1024,128]{1,0:T(8,128)(2,1)S(1)}) custom-call(s32[4]{0:T(128)S(1)} %pad_add_fusion.place_ref.refs_0_, bf16[2,512,512]{2,1,0:T(8,128)(2,1)S(1)} %collective-permute-done.2.refs_0_, bf16[256,2048]{1,0:T(8,128)(2,1)} %refs_1_.5, ...), custom_call_target="tpu_custom_call" | custom-call | flops 9200000000 | bytes 1048576 | tf_op jit(solution)/shard_map/pallas_call | solution.py:544
  20.0 0.1 collective-permute-start.3
  20.1 2.5 %collective-permute-start.4 = (bf16[1024,128]{1,0:T(8,128)(2,1)S(1)}, bf16[1024,128]{1,0:T(8,128)(2,1)S(1)}, u32[]{:S(2)}, u32[]{:S(2)}) collective-permute-start(bf16[1024,128]{1,0:T(8,128)(2,1)S(1)} %get-tuple-element.59), channel_id=1, source_target_pairs={{0,8},{4,12},{8,0},{12,4},{1,9},{5,13},{9,1},{13,5},{2,10},{6,14},... | collective-permute-start | bytes 786440 | tf_op jit(solution)/shard_map/ppermute | solution.py:564
  22.6 0.0 collective-permute-done.7.refs_6_.refs_10_
  22.6 2.8 %collective-permute-start.5 = (bf16[1024,128]{1,0:T(8,128)(2,1)S(1)}, bf16[1024,128]{1,0:T(8,128)(2,1)S(1)}, u32[]{:S(2)}, u32[]{:S(2)}) collective-permute-start(bf16[1024,128]{1,0:T(8,128)(2,1)S(1)} %get-tuple-element.60), channel_id=1, source_target_pairs={{0,12},{4,8},{8,4},{12,0},{1,13},{5,9},{9,5},{13,1},{2,14},{6,10},... | collective-permute-start | bytes 786440 | tf_op jit(solution)/shard_map/ppermute | solution.py:564
  25.4 0.0 collective-permute-done.8.refs_7_.refs_11_
  25.4 0.2 collective-permute-start.12
  25.6 0.0 collective-permute-done.6.refs_0_
  25.6 2.8 %shard_map.99 = (bf16[512,128]{1,0:T(8,128)(2,1)S(1)}, bf16[512,128]{1,0:T(8,128)(2,1)S(1)}, bf16[512,128]{1,0:T(8,128)(2,1)S(1)}, bf16[512,128]{1,0:T(8,128)(2,1)S(1)}) custom-call(s32[4]{0:T(128)S(1)} %pad_add_fusion.place_ref.refs_0_, bf16[1,512,512]{2,1,0:T(8,128)(2,1)S(1)} %collective-permute-done.6.refs_0_, bf16[256,2048]{1,0:T(8,128)(2,1)} %refs_1_.5, ...), custom_call_target="tpu_custom_call" | custom-call | flops 115000000 | bytes 1048576 | tf_op jit(solution)/shard_map/pallas_call | solution.py:544
  28.4 1.4 %collective-permute-start.9 = (bf16[512,128]{1,0:T(8,128)(2,1)S(1)}, bf16[512,128]{1,0:T(8,128)(2,1)S(1)}, u32[]{:S(2)}, u32[]{:S(2)}) collective-permute-start(bf16[512,128]{1,0:T(8,128)(2,1)S(1)} %get-tuple-element.70), channel_id=1, source_target_pairs={{0,4},{4,0},{8,12},{12,8},{1,5},{5,1},{9,13},{13,9},{2,6},{6,2},{1... | collective-permute-start | bytes 393224 | tf_op jit(solution)/shard_map/ppermute | solution.py:564
  29.8 2.6 %collective-permute-done.3.refs_1_ = bf16[1024,128]{1,0:T(8,128)(2,1)S(1)} collective-permute-done((bf16[1024,128]{1,0:T(8,128)(2,1)S(1)}, bf16[1024,128]{1,0:T(8,128)(2,1)S(1)}, u32[]{:S(2)}, u32[]{:S(2)}) %collective-permute-start.3) | collective-permute-done | bytes 262176 | tf_op jit(solution)/shard_map/ppermute | solution.py:564
  32.4 0.0 collective-permute-start.10
  32.4 9.4 %collective-permute-done.4.refs_2_ = bf16[1024,128]{1,0:T(8,128)(2,1)S(1)} collective-permute-done((bf16[1024,128]{1,0:T(8,128)(2,1)S(1)}, bf16[1024,128]{1,0:T(8,128)(2,1)S(1)}, u32[]{:S(2)}, u32[]{:S(2)}) %collective-permute-start.4) | collective-permute-done | bytes 262176 | tf_op jit(solution)/shard_map/ppermute | solution.py:564
  41.8 3.5 %collective-permute-start.11 = (bf16[512,128]{1,0:T(8,128)(2,1)S(1)}, bf16[512,128]{1,0:T(8,128)(2,1)S(1)}, u32[]{:S(2)}, u32[]{:S(2)}) collective-permute-start(bf16[512,128]{1,0:T(8,128)(2,1)S(1)} %get-tuple-element.72), channel_id=1, source_target_pairs={{0,12},{4,8},{8,4},{12,0},{1,13},{5,9},{9,5},{13,1},{2,14},{6,10},... | collective-permute-start | bytes 393224 | tf_op jit(solution)/shard_map/ppermute | solution.py:564
  45.3 6.5 %shard_map.100 = (bf16[512,128]{1,0:T(8,128)(2,1)S(1)}, bf16[512,128]{1,0:T(8,128)(2,1)S(1)}, bf16[512,128]{1,0:T(8,128)(2,1)S(1)}, bf16[512,128]{1,0:T(8,128)(2...) custom-call(s32[4]{0:T(128)S(1)} %pad_add_fusion.place_ref.refs_0_, ...), custom_call_target="tpu_custom_call" | custom-call | flops 8049999872 | bytes 1048576 | tf_op jit(solution)/shard_map/pallas_call | solution.py:544
  51.8 10.4 %collective-permute-start.14 = (bf16[512,128]{1,0:T(8,128)(2,1)S(1)}, bf16[512,128]{1,0:T(8,128)(2,1)S(1)}, u32[]{:S(2)}, u32[]{:S(2)}) collective-permute-start(bf16[512,128]{1,0:T(8,128)(2,1)S(1)} %get-tuple-element.87), channel_id=1, source_target_pairs={{0,8},{4,12},{8,0},{12,4},{1,9},{5,13},{9,1},{13,5},{2,10},{6,14},... | collective-permute-start | bytes 393224 | tf_op jit(solution)/shard_map/ppermute | solution.py:564
  62.2 0.0 collective-permute-done.9.refs_5_
  62.2 1.3 %collective-permute-start.26 = (bf16[512,128]{1,0:T(8,128)(2,1)S(1)}, bf16[512,128]{1,0:T(8,128)(2,1)S(1)}, u32[]{:S(2)}, u32[]{:S(2)}) collective-permute-start(bf16[512,128]{1,0:T(8,128)(2,1)S(1)} %get-tuple-element.100), channel_id=1, source_target_pairs={{0,12},{4,8},{8,4},{12,0},{1,13},{5,9},{9,5},{13,1},{2,14},{6,10},... | collective-permute-start | bytes 393224 | tf_op jit(solution)/shard_map/ppermute | solution.py:564
  63.5 7.0 %shard_map.101 = (bf16[1024,128]{1,0:T(8,128)(2,1)S(1)}, bf16[1024,128]{1,0:T(8,128)(2,1)S(1)}, bf16[1024,128]{1,0:T(8,128)(2,1)S(1)}, bf16[1024,128]{1,0:T(8,12...) custom-call(s32[4]{0:T(128)S(1)} %pad_add_fusion.place_ref.refs_0_, ...), custom_call_target="tpu_custom_call" | custom-call | flops 11500000256 | bytes 1048576 | tf_op jit(solution)/shard_map/pallas_call | solution.py:544
  70.5 1.1 collective-permute-start.13
  71.6 0.0 collective-permute-done.14.refs_3_.refs_10_
  71.6 2.0 %collective-permute-start.16 = (bf16[1024,128]{1,0:T(8,128)(2,1)S(1)}, bf16[1024,128]{1,0:T(8,128)(2,1)S(1)}, u32[]{:S(2)}, u32[]{:S(2)}) collective-permute-start(bf16[1024,128]{1,0:T(8,128)(2,1)S(1)} %get-tuple-element.89), channel_id=1, source_target_pairs={{0,12},{4,8},{8,4},{12,0},{1,13},{5,9},{9,5},{13,1},{2,14},{6,10},... | collective-permute-start | bytes 786440 | tf_op jit(solution)/shard_map/ppermute | solution.py:564
  73.6 0.0 collective-permute-start.20
  73.6 0.0 collective-permute-done.25.refs_2_.refs_9_
  73.6 1.5 %collective-permute-start.15 = (bf16[1024,128]{1,0:T(8,128)(2,1)S(1)}, bf16[1024,128]{1,0:T(8,128)(2,1)S(1)}, u32[]{:S(2)}, u32[]{:S(2)}) collective-permute-start(bf16[1024,128]{1,0:T(8,128)(2,1)S(1)} %get-tuple-element.88), channel_id=1, source_target_pairs={{0,8},{4,12},{8,0},{12,4},{1,9},{5,13},{9,1},{13,5},{2,10},{6,14},... | collective-permute-start | bytes 786440 | tf_op jit(solution)/shard_map/ppermute | solution.py:564
  75.2 0.0 collective-permute-done.26.refs_4_.refs_11_
  75.2 0.6 shard_map.104
  75.8 1.9 %collective-permute-start.27 = (bf16[4,512,128]{2,1,0:T(8,128)(2,1)S(1)}, bf16[4,512,128]{2,1,0:T(8,128)(2,1)S(1)}, u32[]{:S(2)}, u32[]{:S(2)}) collective-permute-start(bf16[4,512,128]{2,1,0:T(8,128)(2,1)S(1)} %shard_map.104), channel_id=1, source_target_pairs={{0,1},{1,0},{2,3},{3,2},{4,5},{5,4},{6,7},{7,6},{8,9},{9,8},{10,11... | collective-permute-start | bytes 1572872 | tf_op jit(solution)/shard_map/ppermute | solution.py:570
  77.6 2.8 %collective-permute-done.16.refs_3_ = bf16[1024,128]{1,0:T(8,128)(2,1)S(1)} collective-permute-done((bf16[1024,128]{1,0:T(8,128)(2,1)S(1)}, bf16[1024,128]{1,0:T(8,128)(2,1)S(1)}, u32[]{:S(2)}, u32[]{:S(2)}) %collective-permute-start.16) | collective-permute-done | bytes 262176 | tf_op jit(solution)/shard_map/ppermute | solution.py:564
  80.4 3.3 %collective-permute-start.21 = (bf16[1024,128]{1,0:T(8,128)(2,1)S(1)}, bf16[1024,128]{1,0:T(8,128)(2,1)S(1)}, u32[]{:S(2)}, u32[]{:S(2)}) collective-permute-start(bf16[1024,128]{1,0:T(8,128)(2,1)S(1)} %get-tuple-element.95.refs_0_), channel_id=1, source_target_pairs={{0,1},{1,0},{2,3},{3,2},{4,5},{5,4},{6,7},{7,6},{8,9},{9,8},{10,11... | collective-permute-start | bytes 786440 | tf_op jit(solution)/shard_map/ppermute | solution.py:570
  83.7 5.2 %collective-permute-done.20.refs_1_ = bf16[1024,128]{1,0:T(8,128)(2,1)S(1)} collective-permute-done((bf16[1024,128]{1,0:T(8,128)(2,1)S(1)}, bf16[1024,128]{1,0:T(8,128)(2,1)S(1)}, u32[]{:S(2)}, u32[]{:S(2)}) %collective-permute-start.20) | collective-permute-done | bytes 262176 | tf_op jit(solution)/shard_map/ppermute | solution.py:564
  88.9 0.5 collective-permute-start.24
  89.4 0.0 collective-permute-done.13.theirs_ref
  89.4 0.0 collective-permute-start.22
  89.4 0.6 shard_map.102
  90.0 7.1 %collective-permute-done.15.refs_2_ = bf16[1024,128]{1,0:T(8,128)(2,1)S(1)} collective-permute-done((bf16[1024,128]{1,0:T(8,128)(2,1)S(1)}, bf16[1024,128]{1,0:T(8,128)(2,1)S(1)}, u32[]{:S(2)}, u32[]{:S(2)}) %collective-permute-start.15) | collective-permute-done | bytes 262176 | tf_op jit(solution)/shard_map/ppermute | solution.py:564
  97.1 0.5 collective-permute-start.23
  97.6 0.0 collective-permute-done.21.refs_4_
  97.6 0.0 collective-permute-start.17
  97.6 2.5 %collective-permute-start.18 = (bf16[576,128]{1,0:T(8,128)(2,1)S(1)}, bf16[576,128]{1,0:T(8,128)(2,1)S(1)}, u32[]{:S(2)}, u32[]{:S(2)}) collective-permute-start(bf16[576,128]{1,0:T(8,128)(2,1)S(1)} %get-tuple-element.92), channel_id=1, source_target_pairs={{0,8},{4,12},{8,0},{12,4},{1,9},{5,13},{9,1},{13,5},{2,10},{6,14},... | collective-permute-start | bytes 442376 | tf_op jit(solution)/shard_map/ppermute | solution.py:564
  100.1 1.1 collective-permute-start.19
  101.2 2.9 %shard_map.105 = bf16[256,1024]{1,0:T(8,128)(2,1)S(1)} custom-call(s32[4]{0:T(128)S(1)} %pad_add_fusion.place_ref.refs_0_, bf16[1024,128]{1,0:T(8,128)(2,1)S(1)} %get-tuple-element.95.refs_0_, bf16[1024,128]{1,0:T(8,128)(2,1)S(1)} %collective-permute-done.20.refs_1_, bf16[1024,128]{1,0:T(8,128)(2,1)S(1)} %collective-permute-done.15.refs_2_, ...), custom_call_target="tpu_custom_call" | custom-call | flops 1150000000 | bytes 1048576 | tf_op jit(solution)/shard_map/pallas_call | solution.py:544
  104.1 1.2 %collective-permute-start.28 = (bf16[256,1024]{1,0:T(8,128)(2,1)S(1)}, bf16[256,1024]{1,0:T(8,128)(2,1)S(1)}, u32[]{:S(2)}, u32[]{:S(2)}) collective-permute-start(bf16[256,1024]{1,0:T(8,128)(2,1)S(1)} %shard_map.105), channel_id=1, source_target_pairs={{0,1},{1,3},{3,2},{2,0},{4,5},{5,7},{7,6},{6,4},{8,9},{9,11},{11,1... | collective-permute-start | bytes 1572872 | tf_op jit(solution)/shard_map/ppermute | solution.py:712
  105.3 2.9 %shard_map.106.kept_ref = bf16[256,1024]{1,0:T(8,128)(2,1)S(1)} custom-call(s32[4]{0:T(128)S(1)} %pad_add_fusion.place_ref.refs_0_, bf16[1024,128]{1,0:T(8,128)(2,1)S(1)} %get-tuple-element.95.refs_0_, bf16[1024,128]{1,0:T(8,128)(2,1)S(1)} %collective-permute-done.20.refs_1_, bf16[1024,128]{1,0:T(8,128)(2,1)S(1)} %collective-permute-done.15.refs_2_, ...), custom_call_target="tpu_custom_call" | custom-call | flops 1150000000 | bytes 1048576 | tf_op jit(solution)/shard_map/pallas_call | solution.py:544
  108.2 3.2 %collective-permute-start.29 = (bf16[256,1024]{1,0:T(8,128)(2,1)S(1)}, bf16[256,1024]{1,0:T(8,128)(2,1)S(1)}, u32[]{:S(2)}, u32[]{:S(2)}) collective-permute-start(bf16[256,1024]{1,0:T(8,128)(2,1)S(1)} %shard_map.106.kept_ref), channel_id=1, source_target_pairs={{1,2},{2,1},{5,6},{6,5},{9,10},{10,9},{13,14},{14,13},{17,18},{18,... | collective-permute-start | bytes 1572872 | tf_op jit(solution)/shard_map/ppermute | solution.py:714
  111.4 0.0 collective-permute-done.18.refs_2_
  111.4 0.0 collective-permute-done.19.refs_3_
  111.4 1.5 %shard_map.103 = (bf16[256,1024]{1,0:T(8,128)(2,1)}, f32[8,32,128]{2,1,0:T(8,128)}) custom-call(s32[4]{0:T(128)S(1)} %pad_add_fusion.place_ref.refs_0_, bf16[576,128]{1,0:T(8,128)(2,1)S(1)} %get-tuple-element.90.refs_0_, bf16[576,128]{1,0:T(8,128)(2,1)S(1)} %collective-permute-done.17.refs_1_, bf16[576,128]{1,0:T(8,128)(2,1)S(1)} %collective-permute-done.18.refs_2_, ...), custom_call_target="tpu_custom_call" | custom-call | flops 9200000000 | bytes 1048576 | tf_op jit(solution)/shard_map/pallas_call | solution.py:544
  113.0 6.1 %collective-permute-done.29.second_ref = bf16[256,1024]{1,0:T(8,128)(2,1)S(1)} collective-permute-done((bf16[256,1024]{1,0:T(8,128)(2,1)S(1)}, bf16[256,1024]{1,0:T(8,128)(2,1)S(1)}, u32[]{:S(2)}, u32[]{:S(2)}) %collective-permute-start.29) | collective-permute-done | bytes 524320 | tf_op jit(solution)/shard_map/ppermute | solution.py:714
  119.1 1.5 %shard_map.107 = bf16[256,1024]{1,0:T(8,128)(2,1)} custom-call(s32[4]{0:T(128)S(1)} %pad_add_fusion.place_ref.refs_0_, bf16[256,1024]{1,0:T(8,128)(2,1)S(1)} %collective-permute-done.28.first_ref, bf16[256,1024]{1,0:T(8,128)(2,1)S(1)} %collective-permute-done.29.second_ref, bf16[256,1024]{1,0:T(8,128)(2,1)S(1)} %shard_map.106.kept_ref), custom_call_target="tpu_custom_call" | custom-call | flops 1150000000 | bytes 1048576 | tf_op jit(solution)/shard_map/pallas_call | solution.py:544
  (19 shorter events, 0.0 us)
Async XLA Ops:
  0.6 4.6 %collective-permute-start.1 = (bf16[256,2048]{1,0:T(8,128)(2,1)}, bf16[256,2048]{1,0:T(8,128)(2,1)S(1)}, u32[]{:S(2)}, u32[]{:S(2)}) collective-permute-start(bf16[256,2048]{1,0:T(8,128)(2,1)} %refs_1_.5), channel_id=1, source_target_pairs={{0,1},{1,0},{2,3},{3,2},{4,5},{5,4},{6,7},{7,6},{8,9},{9,8},{10,11... | collective-permute-start | bytes 3145736 | tf_op jit(solution)/shard_map/ppermute | solution.py:570
  2.5 2.6 %collective-permute-start = (bf16[4,272,128]{2,1,0:T(8,128)(2,1)S(1)}, bf16[4,272,128]{2,1,0:T(8,128)(2,1)S(1)}, u32[]{:S(2)}, u32[]{:S(2)}) collective-permute-start(bf16[4,272,128]{2,1,0:T(8,128)(2,1)S(1)} %get-tuple-element.55), channel_id=1, source_target_pairs={{0,1},{1,0},{2,3},{3,2},{4,5},{5,4},{6,7},{7,6},{8,9},{9,8},{10,11... | collective-permute-start | bytes 835592 | tf_op jit(solution)/shard_map/ppermute | solution.py:570
  8.1 5.0 %collective-permute-start.2 = (bf16[2,512,512]{2,1,0:T(8,128)(2,1)S(1)}, bf16[2,512,512]{2,1,0:T(8,128)(2,1)S(1)}, u32[]{:S(2)}, u32[]{:S(2)}) collective-permute-start(bf16[2,512,512]{2,1,0:T(8,128)(2,1)S(1)} %get-tuple-element.56), channel_id=1, source_target_pairs={{0,1},{1,0},{2,3},{3,2},{4,5},{5,4},{6,7},{7,6},{8,9},{9,8},{10,11... | collective-permute-start | bytes 3145736 | tf_op jit(solution)/shard_map/ppermute | solution.py:570
  8.2 14.4 %collective-permute-start.7 = (bf16[544,128]{1,0:T(8,128)(2,1)S(1)}, bf16[544,128]{1,0:T(8,128)(2,1)S(1)}, u32[]{:S(2)}, u32[]{:S(2)}) collective-permute-start(bf16[544,128]{1,0:T(8,128)(2,1)S(1)} %get-tuple-element.62), channel_id=1, source_target_pairs={{0,8},{4,12},{8,0},{12,4},{1,9},{5,13},{9,1},{13,5},{2,10},{6,14},... | collective-permute-start | bytes 417800 | tf_op jit(solution)/shard_map/ppermute | solution.py:564
  12.0 13.4 %collective-permute-start.8 = (bf16[544,128]{1,0:T(8,128)(2,1)S(1)}, bf16[544,128]{1,0:T(8,128)(2,1)S(1)}, u32[]{:S(2)}, u32[]{:S(2)}) collective-permute-start(bf16[544,128]{1,0:T(8,128)(2,1)S(1)} %get-tuple-element.63), channel_id=1, source_target_pairs={{0,12},{4,8},{8,4},{12,0},{1,13},{5,9},{9,5},{13,1},{2,14},{6,10},... | collective-permute-start | bytes 417800 | tf_op jit(solution)/shard_map/ppermute | solution.py:564
  15.7 9.8 %collective-permute-start.6 = (bf16[1,512,512]{2,1,0:T(8,128)(2,1)S(1)}, bf16[1,512,512]{2,1,0:T(8,128)(2,1)S(1)}, u32[]{:S(2)}, u32[]{:S(2)}) collective-permute-start(bf16[1,512,512]{2,1,0:T(8,128)(2,1)S(1)} %shard_map.98), channel_id=1, source_target_pairs={{0,1},{1,0},{2,3},{3,2},{4,5},{5,4},{6,7},{7,6},{8,9},{9,8},{10,11... | collective-permute-start | bytes 1572872 | tf_op jit(solution)/shard_map/ppermute | solution.py:570
  20.0 12.4 %collective-permute-start.3 = (bf16[1024,128]{1,0:T(8,128)(2,1)S(1)}, bf16[1024,128]{1,0:T(8,128)(2,1)S(1)}, u32[]{:S(2)}, u32[]{:S(2)}) collective-permute-start(bf16[1024,128]{1,0:T(8,128)(2,1)S(1)} %get-tuple-element.58), channel_id=1, source_target_pairs={{0,4},{4,0},{8,12},{12,8},{1,5},{5,1},{9,13},{13,9},{2,6},{6,2},{1... | collective-permute-start | bytes 786440 | tf_op jit(solution)/shard_map/ppermute | solution.py:564
  20.1 21.7 %collective-permute-start.4 = (bf16[1024,128]{1,0:T(8,128)(2,1)S(1)}, bf16[1024,128]{1,0:T(8,128)(2,1)S(1)}, u32[]{:S(2)}, u32[]{:S(2)}) collective-permute-start(bf16[1024,128]{1,0:T(8,128)(2,1)S(1)} %get-tuple-element.59), channel_id=1, source_target_pairs={{0,8},{4,12},{8,0},{12,4},{1,9},{5,13},{9,1},{13,5},{2,10},{6,14},... | collective-permute-start | bytes 786440 | tf_op jit(solution)/shard_map/ppermute | solution.py:564
  22.6 22.8 %collective-permute-start.5 = (bf16[1024,128]{1,0:T(8,128)(2,1)S(1)}, bf16[1024,128]{1,0:T(8,128)(2,1)S(1)}, u32[]{:S(2)}, u32[]{:S(2)}) collective-permute-start(bf16[1024,128]{1,0:T(8,128)(2,1)S(1)} %get-tuple-element.60), channel_id=1, source_target_pairs={{0,12},{4,8},{8,4},{12,0},{1,13},{5,9},{9,5},{13,1},{2,14},{6,10},... | collective-permute-start | bytes 786440 | tf_op jit(solution)/shard_map/ppermute | solution.py:564
  25.4 19.9 %copy-start.3 = (s32[256]{0:T(256)S(1)}, s32[256]{0:T(256)}, u32[]{:S(2)}) copy-start(s32[256]{0:T(256)} %param.11) | copy-start | bytes 3076
  25.4 19.9 %collective-permute-start.12 = (bf16[544,128]{1,0:T(8,128)(2,1)S(1)}, bf16[544,128]{1,0:T(8,128)(2,1)S(1)}, u32[]{:S(2)}, u32[]{:S(2)}) collective-permute-start(bf16[544,128]{1,0:T(8,128)(2,1)S(1)} %get-tuple-element.74), channel_id=1, source_target_pairs={{0,4},{4,0},{8,12},{12,8},{1,5},{5,1},{9,13},{13,9},{2,6},{6,2},{1... | collective-permute-start | bytes 417800 | tf_op jit(solution)/shard_map/ppermute | solution.py:564
  28.4 33.8 %collective-permute-start.9 = (bf16[512,128]{1,0:T(8,128)(2,1)S(1)}, bf16[512,128]{1,0:T(8,128)(2,1)S(1)}, u32[]{:S(2)}, u32[]{:S(2)}) collective-permute-start(bf16[512,128]{1,0:T(8,128)(2,1)S(1)} %get-tuple-element.70), channel_id=1, source_target_pairs={{0,4},{4,0},{8,12},{12,8},{1,5},{5,1},{9,13},{13,9},{2,6},{6,2},{1... | collective-permute-start | bytes 393224 | tf_op jit(solution)/shard_map/ppermute | solution.py:564
  32.4 31.0 %collective-permute-start.10 = (bf16[512,128]{1,0:T(8,128)(2,1)S(1)}, bf16[512,128]{1,0:T(8,128)(2,1)S(1)}, u32[]{:S(2)}, u32[]{:S(2)}) collective-permute-start(bf16[512,128]{1,0:T(8,128)(2,1)S(1)} %get-tuple-element.71), channel_id=1, source_target_pairs={{0,8},{4,12},{8,0},{12,4},{1,9},{5,13},{9,1},{13,5},{2,10},{6,14},... | collective-permute-start | bytes 393224 | tf_op jit(solution)/shard_map/ppermute | solution.py:564
  41.8 21.6 %collective-permute-start.11 = (bf16[512,128]{1,0:T(8,128)(2,1)S(1)}, bf16[512,128]{1,0:T(8,128)(2,1)S(1)}, u32[]{:S(2)}, u32[]{:S(2)}) collective-permute-start(bf16[512,128]{1,0:T(8,128)(2,1)S(1)} %get-tuple-element.72), channel_id=1, source_target_pairs={{0,12},{4,8},{8,4},{12,0},{1,13},{5,9},{9,5},{13,1},{2,14},{6,10},... | collective-permute-start | bytes 393224 | tf_op jit(solution)/shard_map/ppermute | solution.py:564
  51.8 19.8 %collective-permute-start.14 = (bf16[512,128]{1,0:T(8,128)(2,1)S(1)}, bf16[512,128]{1,0:T(8,128)(2,1)S(1)}, u32[]{:S(2)}, u32[]{:S(2)}) collective-permute-start(bf16[512,128]{1,0:T(8,128)(2,1)S(1)} %get-tuple-element.87), channel_id=1, source_target_pairs={{0,8},{4,12},{8,0},{12,4},{1,9},{5,13},{9,1},{13,5},{2,10},{6,14},... | collective-permute-start | bytes 393224 | tf_op jit(solution)/shard_map/ppermute | solution.py:564
  62.2 11.4 %collective-permute-start.25 = (bf16[512,128]{1,0:T(8,128)(2,1)S(1)}, bf16[512,128]{1,0:T(8,128)(2,1)S(1)}, u32[]{:S(2)}, u32[]{:S(2)}) collective-permute-start(bf16[512,128]{1,0:T(8,128)(2,1)S(1)} %get-tuple-element.99), channel_id=1, source_target_pairs={{0,4},{4,0},{8,12},{12,8},{1,5},{5,1},{9,13},{13,9},{2,6},{6,2},{1... | collective-permute-start | bytes 393224 | tf_op jit(solution)/shard_map/ppermute | solution.py:564
  62.2 13.0 %collective-permute-start.26 = (bf16[512,128]{1,0:T(8,128)(2,1)S(1)}, bf16[512,128]{1,0:T(8,128)(2,1)S(1)}, u32[]{:S(2)}, u32[]{:S(2)}) collective-permute-start(bf16[512,128]{1,0:T(8,128)(2,1)S(1)} %get-tuple-element.100), channel_id=1, source_target_pairs={{0,12},{4,8},{8,4},{12,0},{1,13},{5,9},{9,5},{13,1},{2,14},{6,10},... | collective-permute-start | bytes 393224 | tf_op jit(solution)/shard_map/ppermute | solution.py:564
  70.5 18.9 %collective-permute-start.13 = (bf16[4,288,128]{2,1,0:T(8,128)(2,1)S(1)}, bf16[4,288,128]{2,1,0:T(8,128)(2,1)S(1)}, u32[]{:S(2)}, u32[]{:S(2)}) collective-permute-start(bf16[4,288,128]{2,1,0:T(8,128)(2,1)S(1)} %get-tuple-element.78), channel_id=1, source_target_pairs={{0,1},{1,0},{2,3},{3,2},{4,5},{5,4},{6,7},{7,6},{8,9},{9,8},{10,11... | collective-permute-start | bytes 884744 | tf_op jit(solution)/shard_map/ppermute | solution.py:570
  71.6 8.8 %collective-permute-start.16 = (bf16[1024,128]{1,0:T(8,128)(2,1)S(1)}, bf16[1024,128]{1,0:T(8,128)(2,1)S(1)}, u32[]{:S(2)}, u32[]{:S(2)}) collective-permute-start(bf16[1024,128]{1,0:T(8,128)(2,1)S(1)} %get-tuple-element.89), channel_id=1, source_target_pairs={{0,12},{4,8},{8,4},{12,0},{1,13},{5,9},{9,5},{13,1},{2,14},{6,10},... | collective-permute-start | bytes 786440 | tf_op jit(solution)/shard_map/ppermute | solution.py:564
  73.6 15.2 %collective-permute-start.20 = (bf16[1024,128]{1,0:T(8,128)(2,1)S(1)}, bf16[1024,128]{1,0:T(8,128)(2,1)S(1)}, u32[]{:S(2)}, u32[]{:S(2)}) collective-permute-start(bf16[1024,128]{1,0:T(8,128)(2,1)S(1)} %get-tuple-element.96), channel_id=1, source_target_pairs={{0,4},{4,0},{8,12},{12,8},{1,5},{5,1},{9,13},{13,9},{2,6},{6,2},{1... | collective-permute-start | bytes 786440 | tf_op jit(solution)/shard_map/ppermute | solution.py:564
  73.6 23.4 %collective-permute-start.15 = (bf16[1024,128]{1,0:T(8,128)(2,1)S(1)}, bf16[1024,128]{1,0:T(8,128)(2,1)S(1)}, u32[]{:S(2)}, u32[]{:S(2)}) collective-permute-start(bf16[1024,128]{1,0:T(8,128)(2,1)S(1)} %get-tuple-element.88), channel_id=1, source_target_pairs={{0,8},{4,12},{8,0},{12,4},{1,9},{5,13},{9,1},{13,5},{2,10},{6,14},... | collective-permute-start | bytes 786440 | tf_op jit(solution)/shard_map/ppermute | solution.py:564
  75.2 26.0 %copy-start.2 = (bf16[1024,1024]{1,0:T(8,128)(2,1)S(1)}, bf16[1024,1024]{1,0:T(8,128)(2,1)}, u32[]{:S(2)}) copy-start(bf16[1024,1024]{1,0:T(8,128)(2,1)} %refs_14_.3) | copy-start | bytes 6291460
  75.8 25.4 %collective-permute-start.27 = (bf16[4,512,128]{2,1,0:T(8,128)(2,1)S(1)}, bf16[4,512,128]{2,1,0:T(8,128)(2,1)S(1)}, u32[]{:S(2)}, u32[]{:S(2)}) collective-permute-start(bf16[4,512,128]{2,1,0:T(8,128)(2,1)S(1)} %shard_map.104), channel_id=1, source_target_pairs={{0,1},{1,0},{2,3},{3,2},{4,5},{5,4},{6,7},{7,6},{8,9},{9,8},{10,11... | collective-permute-start | bytes 1572872 | tf_op jit(solution)/shard_map/ppermute | solution.py:570
  80.4 17.2 %collective-permute-start.21 = (bf16[1024,128]{1,0:T(8,128)(2,1)S(1)}, bf16[1024,128]{1,0:T(8,128)(2,1)S(1)}, u32[]{:S(2)}, u32[]{:S(2)}) collective-permute-start(bf16[1024,128]{1,0:T(8,128)(2,1)S(1)} %get-tuple-element.95.refs_0_), channel_id=1, source_target_pairs={{0,1},{1,0},{2,3},{3,2},{4,5},{5,4},{6,7},{7,6},{8,9},{9,8},{10,11... | collective-permute-start | bytes 786440 | tf_op jit(solution)/shard_map/ppermute | solution.py:570
  88.9 8.7 %collective-permute-start.24 = (bf16[1024,128]{1,0:T(8,128)(2,1)S(1)}, bf16[1024,128]{1,0:T(8,128)(2,1)S(1)}, u32[]{:S(2)}, u32[]{:S(2)}) collective-permute-start(bf16[1024,128]{1,0:T(8,128)(2,1)S(1)} %collective-permute-done.16.refs_3_), channel_id=1, source_target_pairs={{0,1},{1,0},{2,3},{3,2},{4,5},{5,4},{6,7},{7,6},{8,9},{9,8},{10,11... | collective-permute-start | bytes 786440 | tf_op jit(solution)/shard_map/ppermute | solution.py:570
  89.4 10.7 %collective-permute-start.22 = (bf16[1024,128]{1,0:T(8,128)(2,1)S(1)}, bf16[1024,128]{1,0:T(8,128)(2,1)S(1)}, u32[]{:S(2)}, u32[]{:S(2)}) collective-permute-start(bf16[1024,128]{1,0:T(8,128)(2,1)S(1)} %collective-permute-done.20.refs_1_), channel_id=1, source_target_pairs={{0,1},{1,0},{2,3},{3,2},{4,5},{5,4},{6,7},{7,6},{8,9},{9,8},{10,11... | collective-permute-start | bytes 786440 | tf_op jit(solution)/shard_map/ppermute | solution.py:570
  89.4 11.8 %copy-start = (bf16[1024,1024]{1,0:T(8,128)(2,1)S(1)}, bf16[1024,1024]{1,0:T(8,128)(2,1)}, u32[]{:S(2)}) copy-start(bf16[1024,1024]{1,0:T(8,128)(2,1)} %refs_15_.3) | copy-start | bytes 6291460
  89.4 11.8 %copy-start.1 = (bf16[1024,1024]{1,0:T(8,128)(2,1)S(1)}, bf16[1024,1024]{1,0:T(8,128)(2,1)}, u32[]{:S(2)}) copy-start(bf16[1024,1024]{1,0:T(8,128)(2,1)} %refs_13_.3) | copy-start | bytes 6291460
  97.1 4.1 %collective-permute-start.23 = (bf16[1024,128]{1,0:T(8,128)(2,1)S(1)}, bf16[1024,128]{1,0:T(8,128)(2,1)S(1)}, u32[]{:S(2)}, u32[]{:S(2)}) collective-permute-start(bf16[1024,128]{1,0:T(8,128)(2,1)S(1)} %collective-permute-done.15.refs_2_), channel_id=1, source_target_pairs={{0,1},{1,0},{2,3},{3,2},{4,5},{5,4},{6,7},{7,6},{8,9},{9,8},{10,11... | collective-permute-start | bytes 786440 | tf_op jit(solution)/shard_map/ppermute | solution.py:570
  97.6 13.8 %collective-permute-start.17 = (bf16[576,128]{1,0:T(8,128)(2,1)S(1)}, bf16[576,128]{1,0:T(8,128)(2,1)S(1)}, u32[]{:S(2)}, u32[]{:S(2)}) collective-permute-start(bf16[576,128]{1,0:T(8,128)(2,1)S(1)} %get-tuple-element.91), channel_id=1, source_target_pairs={{0,4},{4,0},{8,12},{12,8},{1,5},{5,1},{9,13},{13,9},{2,6},{6,2},{1... | collective-permute-start | bytes 442376 | tf_op jit(solution)/shard_map/ppermute | solution.py:564
  97.6 13.8 %collective-permute-start.18 = (bf16[576,128]{1,0:T(8,128)(2,1)S(1)}, bf16[576,128]{1,0:T(8,128)(2,1)S(1)}, u32[]{:S(2)}, u32[]{:S(2)}) collective-permute-start(bf16[576,128]{1,0:T(8,128)(2,1)S(1)} %get-tuple-element.92), channel_id=1, source_target_pairs={{0,8},{4,12},{8,0},{12,4},{1,9},{5,13},{9,1},{13,5},{2,10},{6,14},... | collective-permute-start | bytes 442376 | tf_op jit(solution)/shard_map/ppermute | solution.py:564
  100.1 11.4 %collective-permute-start.19 = (bf16[576,128]{1,0:T(8,128)(2,1)S(1)}, bf16[576,128]{1,0:T(8,128)(2,1)S(1)}, u32[]{:S(2)}, u32[]{:S(2)}) collective-permute-start(bf16[576,128]{1,0:T(8,128)(2,1)S(1)} %get-tuple-element.93), channel_id=1, source_target_pairs={{0,12},{4,8},{8,4},{12,0},{1,13},{5,9},{9,5},{13,1},{2,14},{6,10},... | collective-permute-start | bytes 442376 | tf_op jit(solution)/shard_map/ppermute | solution.py:564
  104.1 15.0 %collective-permute-start.28 = (bf16[256,1024]{1,0:T(8,128)(2,1)S(1)}, bf16[256,1024]{1,0:T(8,128)(2,1)S(1)}, u32[]{:S(2)}, u32[]{:S(2)}) collective-permute-start(bf16[256,1024]{1,0:T(8,128)(2,1)S(1)} %shard_map.105), channel_id=1, source_target_pairs={{0,1},{1,3},{3,2},{2,0},{4,5},{5,7},{7,6},{6,4},{8,9},{9,11},{11,1... | collective-permute-start | bytes 1572872 | tf_op jit(solution)/shard_map/ppermute | solution.py:712
  108.2 10.8 %collective-permute-start.29 = (bf16[256,1024]{1,0:T(8,128)(2,1)S(1)}, bf16[256,1024]{1,0:T(8,128)(2,1)S(1)}, u32[]{:S(2)}, u32[]{:S(2)}) collective-permute-start(bf16[256,1024]{1,0:T(8,128)(2,1)S(1)} %shard_map.106.kept_ref), channel_id=1, source_target_pairs={{1,2},{2,1},{5,6},{6,5},{9,10},{10,9},{13,14},{14,13},{17,18},{18,... | collective-permute-start | bytes 1572872 | tf_op jit(solution)/shard_map/ppermute | solution.py:714

commit v15 on v14

--- a/solution.py
+++ b/solution.py
@@ -287,30 +287,32 @@
             out_ref[index * tall : (index + 1) * tall, :] = low_ref[:, pl.ds(at, head_dim)]
 
 
-def fetch_kernel(turn, place_ref, *refs):
-    weights, (held_ref, sems) = refs[:-2], refs[-2:]
-    for copy in fetch_columns(place_ref[1] ^ turn, weights, held_ref, sems):
-        copy.wait()
-
-
-def opening_kernel(place_ref, held_ref, mine_ref, theirs_ref, *refs):
-    tokens, refs = refs[:2], refs[2:]
-    out_refs, (part_ref, joined_ref, sems) = refs[:-3], refs[-3:]
+def fetch_kernel(place_ref, mine_ref, theirs_ref, weight_ref, joined_ref, held_ref, sems, token_sems):
     side = place_ref[1]
     tall, depth = joined_ref.shape
     rows = tall // 2
     near = pl.ds(pl.multiple_of(side * depth, depth), depth)
     joins = []
-    for core, source in enumerate(tokens):
+    for core, source in enumerate((mine_ref, theirs_ref)):
         at = pl.ds(pl.multiple_of((side ^ core) * rows, rows), rows)
-        joins.append(pltpu.make_async_copy(source.at[:, near], joined_ref.at[at], sems.at[core]))
+        joins.append(
+            pltpu.make_async_copy(source.at[:, near], joined_ref.at[at], token_sems.at[core])
+        )
         joins[core].start()
+    for copy in (*fetch_columns(1 - side, (weight_ref,), held_ref, sems), *joins):
+        copy.wait()
+
+
+def opening_kernel(place_ref, joined_ref, held_ref, mine_ref, theirs_ref, weight_ref, *refs):
+    out_refs, (part_ref, second_ref, sems) = refs[:-3], refs[-3:]
+    copies = fetch_columns(1 - place_ref[1], (weight_ref,), second_ref, sems)
     merge_kernel(place_ref, mine_ref, theirs_ref, *out_refs)
-    for copy in joins:
+    total = jnp.dot(joined_ref[...], held_ref[0], preferred_element_type=jnp.float32)
+    part_ref[0] = total.astype(jnp.bfloat16)
+    for copy in copies:
         copy.wait()
-    for index in range(held_ref.shape[0]):
-        total = jnp.dot(joined_ref[...], held_ref[index], preferred_element_type=jnp.float32)
-        part_ref[index] = total.astype(jnp.bfloat16)
+    total = jnp.dot(joined_ref[...], second_ref[0], preferred_element_type=jnp.float32)
+    part_ref[1] = total.astype(jnp.bfloat16)
 
 
 def in_order(place, parts, start, ordered):
@@ -610,25 +612,28 @@
         )
 
     early, late = (w_query, w_key), (w_value,)
-    fetched = call(
-        partial(fetch_kernel, 1),
-        pltpu.VMEM((2, half, width // 2), jnp.bfloat16),
+    half_columns = (1, half, width // 2)
+    joined, fetched = call(
+        fetch_kernel,
+        (pltpu.VMEM((2 * rows, half), jnp.bfloat16), pltpu.VMEM(half_columns, jnp.bfloat16)),
         place,
-        *(stay(weight) for weight in early),
-        scratch=[pltpu.SemaphoreType.DMA((2, 4))],
-        hbm=2,
+        stay(hidden),
+        hidden_other,
+        stay(w_query),
+        scratch=[pltpu.SemaphoreType.DMA((1, 4)), pltpu.SemaphoreType.DMA((2,))],
+        hbm=3,
     )
     *merged, early_part = call(
         opening_kernel,
         (*buffers(2 * block.shape[1]), low(2, 2 * rows, width // 2)),
         place,
+        joined,
         fetched,
         grads_mine,
         grads_other,
-        stay(hidden),
-        hidden_other,
-        scratch=[pltpu.VMEM((2 * rows, half), jnp.bfloat16), pltpu.SemaphoreType.DMA((2,))],
-        hbm=2,
+        stay(w_key),
+        scratch=[pltpu.VMEM(half_columns, jnp.bfloat16), pltpu.SemaphoreType.DMA((1, 4))],
+        hbm=1,
         takes=0.1,
     )
     grads = exchange(merged)

time: 121 us -> 121 us (level)
  transfers between devices with their start and end apart: 30 -> 30, of which waited for: 6 -> 7; matrix products, arithmetic and copies ran while one was open for 0% -> 0% of each run, Pallas kernels for 29% -> 29%
where the time goes in v15:
time: 121 us
  starting transfers between devices  47.1 us (39%)
  Pallas kernels  39.1 us (32%)
  waiting for transfers between devices  33.8 us (28%)
    pallas_call x14, Pallas kernels, call(): pl.pallas_call(kernel, out_shape=outs, in_specs=[smem] + [vmem] * (len(op...  39.1 us
    ppermute x18, starting transfers between devices, exchange(): lax.ppermute(parts[offset], 'seq', [(at, at ^ offset) for at in range(chi...  33.8 us
    ppermute x18, waiting for transfers between devices, exchange(): lax.ppermute(parts[offset], 'seq', [(at, at ^ offset) for at in range(chi...  27.2 us
    ppermute x10, starting transfers between devices, to_sibling(): return lax.ppermute(piece, 'sub', swap)  8.84 us
    ppermute x1, waiting for transfers between devices, by_head(): second = lax.ppermute(kept, square, [(1, 2), (2, 1)])  6.1 us
    ppermute x1, starting transfers between devices, by_head(): second = lax.ppermute(kept, square, [(1, 2), (2, 1)])  3.17 us
  transfers between devices with their start and end apart: 30, of which 7 were waited for; matrix products, arithmetic and copies ran while one was open for 0% of the time, Pallas kernels for 29%

profile of v15, /device:TPU:1, one launch (start us, length us, event | category | flops | bytes accessed | tf_op | source)
XLA Modules:
  0.0 120.9 jit_solution(2052723131913722948)
XLA Ops:
  0.6 0.1 collective-permute-start
  0.8 0.1 pad_add_fusion.place_ref.refs_0_
  0.8 1.7 %shard_map.95 = (bf16[4,272,128]{2,1,0:T(8,128)(2,1)S(1)}, bf16[4,272,128]{2,1,0:T(8,128)(2,1)S(1)}) custom-call(s32[4]{0:T(128)S(1)} %pad_add_fusion.place_ref.refs_0_, bf16[256,1024]{1,0:T(8,128)(2,1)} %grads_ref.1, s32[8,256]{1,0:T(8,128)} %assign_ref.1), custom_call_target="tpu_custom_call" | custom-call | flops 1150000000 | bytes 1048576 | tf_op jit(solution)/shard_map/pallas_call | solution.py:546
  2.5 0.5 collective-permute-start.1
  3.1 0.5 collective-permute-done.theirs_ref.refs_2_.refs_1_
  3.6 2.0 %shard_map.94 = (bf16[512,1024]{1,0:T(8,128)(2,1)S(1)}, bf16[1,1024,512]{2,1,0:T(8,128)(2,1)S(1)}) custom-call(s32[4]{0:T(128)S(1)} %pad_add_fusion.place_ref.refs_0_, bf16[256,2048]{1,0:T(8,128)(2,1)} %refs_1_.3, bf16[256,2048]{1,0:T(8,128)(2,1)S(1)} %collective-permute-done.theirs_ref.refs_2_.refs_1_, bf16[1024,1024]{1,0:T(8,128)(2,1)} %refs_13_.3), custom_call_target="tpu_custom_call" | custom-call | flops 1150000000 | bytes 1048576 | tf_op jit(solution)/shard_map/pallas_call | solution.py:546
  5.5 0.0 collective-permute-done.1.theirs_ref
  5.5 2.9 %shard_map.96 = (bf16[544,128]{1,0:T(8,128)(2,1)S(1)}, bf16[544,128]{1,0:T(8,128)(2,1)S(1)}, bf16[544,128]{1,0:T(8,128)(2,1)S(1)}, bf16[544,128]{1,0:T(8,128)(2,1)S(1)}, bf16[2,512,512]{2,1,0:T(8,128)(2,1)S(1)}) custom-call(s32[4]{0:T(128)S(1)} %pad_add_fusion.place_ref.refs_0_, bf16[512,1024]{1,0:T(8,128)(2,1)S(1)} %get-tuple-element.56.joined_ref, ...), custom_call_target="tpu_custom_call" | custom-call | flops 115000000 | bytes 1048576 | tf_op jit(solution)/shard_map/pallas_call | solution.py:546
  8.4 0.2 collective-permute-start.2
  8.6 3.7 %collective-permute-start.7 = (bf16[544,128]{1,0:T(8,128)(2,1)S(1)}, bf16[544,128]{1,0:T(8,128)(2,1)S(1)}, u32[]{:S(2)}, u32[]{:S(2)}) collective-permute-start(bf16[544,128]{1,0:T(8,128)(2,1)S(1)} %get-tuple-element.66), channel_id=1, source_target_pairs={{0,8},{4,12},{8,0},{12,4},{1,9},{5,13},{9,1},{13,5},{2,10},{6,14},... | collective-permute-start | bytes 417800 | tf_op jit(solution)/shard_map/ppermute | solution.py:566
  12.3 1.1 collective-permute-start.8
  13.4 0.0 collective-permute-done.2.refs_0_
  13.4 2.7 %shard_map.98 = bf16[1,512,512]{2,1,0:T(8,128)(2,1)S(1)} custom-call(s32[4]{0:T(128)S(1)} %pad_add_fusion.place_ref.refs_0_, bf16[256,2048]{1,0:T(8,128)(2,1)} %refs_1_.3, bf16[256,2048]{1,0:T(8,128)(2,1)S(1)} %collective-permute-done.theirs_ref.refs_2_.refs_1_, bf16[1024,1024]{1,0:T(8,128)(2,1)} %refs_15_.3), custom_call_target="tpu_custom_call" | custom-call | flops 115000000 | bytes 1048576 | tf_op jit(solution)/shard_map/pallas_call | solution.py:546
  16.0 0.8 collective-permute-start.6
  16.8 3.6 %shard_map.97 = (bf16[1024,128]{1,0:T(8,128)(2,1)S(1)}, bf16[1024,128]{1,0:T(8,128)(2,1)S(1)}, bf16[1024,128]{1,0:T(8,128)(2,1)S(1)}, bf16[1024,128]{1,0:T(8,128)(2,1)S(1)}) custom-call(s32[4]{0:T(128)S(1)} %pad_add_fusion.place_ref.refs_0_, bf16[2,512,512]{2,1,0:T(8,128)(2,1)S(1)} %collective-permute-done.2.refs_0_, bf16[256,2048]{1,0:T(8,128)(2,1)} %refs_1_.3, ...), custom_call_target="tpu_custom_call" | custom-call | flops 9200000000 | bytes 1048576 | tf_op jit(solution)/shard_map/pallas_call | solution.py:546
  20.4 0.1 collective-permute-start.3
  20.5 2.5 %collective-permute-start.4 = (bf16[1024,128]{1,0:T(8,128)(2,1)S(1)}, bf16[1024,128]{1,0:T(8,128)(2,1)S(1)}, u32[]{:S(2)}, u32[]{:S(2)}) collective-permute-start(bf16[1024,128]{1,0:T(8,128)(2,1)S(1)} %get-tuple-element.63), channel_id=1, source_target_pairs={{0,8},{4,12},{8,0},{12,4},{1,9},{5,13},{9,1},{13,5},{2,10},{6,14},... | collective-permute-start | bytes 786440 | tf_op jit(solution)/shard_map/ppermute | solution.py:566
  23.0 0.0 collective-permute-done.7.refs_6_.refs_10_
  23.0 2.7 %collective-permute-start.5 = (bf16[1024,128]{1,0:T(8,128)(2,1)S(1)}, bf16[1024,128]{1,0:T(8,128)(2,1)S(1)}, u32[]{:S(2)}, u32[]{:S(2)}) collective-permute-start(bf16[1024,128]{1,0:T(8,128)(2,1)S(1)} %get-tuple-element.64), channel_id=1, source_target_pairs={{0,12},{4,8},{8,4},{12,0},{1,13},{5,9},{9,5},{13,1},{2,14},{6,10},... | collective-permute-start | bytes 786440 | tf_op jit(solution)/shard_map/ppermute | solution.py:566
  25.7 0.0 collective-permute-done.8.refs_7_.refs_11_
  25.7 0.2 collective-permute-start.12
  25.9 2.8 %shard_map.99 = (bf16[512,128]{1,0:T(8,128)(2,1)S(1)}, bf16[512,128]{1,0:T(8,128)(2,1)S(1)}, bf16[512,128]{1,0:T(8,128)(2,1)S(1)}, bf16[512,128]{1,0:T(8,128)(2,1)S(1)}) custom-call(s32[4]{0:T(128)S(1)} %pad_add_fusion.place_ref.refs_0_, bf16[1,512,512]{2,1,0:T(8,128)(2,1)S(1)} %collective-permute-done.6.refs_0_, bf16[256,2048]{1,0:T(8,128)(2,1)} %refs_1_.3, ...), custom_call_target="tpu_custom_call" | custom-call | flops 115000000 | bytes 1048576 | tf_op jit(solution)/shard_map/pallas_call | solution.py:546
  28.7 1.4 %collective-permute-start.9 = (bf16[512,128]{1,0:T(8,128)(2,1)S(1)}, bf16[512,128]{1,0:T(8,128)(2,1)S(1)}, u32[]{:S(2)}, u32[]{:S(2)}) collective-permute-start(bf16[512,128]{1,0:T(8,128)(2,1)S(1)} %get-tuple-element.74), channel_id=1, source_target_pairs={{0,4},{4,0},{8,12},{12,8},{1,5},{5,1},{9,13},{13,9},{2,6},{6,2},{1... | collective-permute-start | bytes 393224 | tf_op jit(solution)/shard_map/ppermute | solution.py:566
  30.1 2.8 %collective-permute-done.3.refs_1_ = bf16[1024,128]{1,0:T(8,128)(2,1)S(1)} collective-permute-done((bf16[1024,128]{1,0:T(8,128)(2,1)S(1)}, bf16[1024,128]{1,0:T(8,128)(2,1)S(1)}, u32[]{:S(2)}, u32[]{:S(2)}) %collective-permute-start.3) | collective-permute-done | bytes 262176 | tf_op jit(solution)/shard_map/ppermute | solution.py:566
  32.9 9.2 %collective-permute-done.4.refs_2_ = bf16[1024,128]{1,0:T(8,128)(2,1)S(1)} collective-permute-done((bf16[1024,128]{1,0:T(8,128)(2,1)S(1)}, bf16[1024,128]{1,0:T(8,128)(2,1)S(1)}, u32[]{:S(2)}, u32[]{:S(2)}) %collective-permute-start.4) | collective-permute-done | bytes 262176 | tf_op jit(solution)/shard_map/ppermute | solution.py:566
  42.1 3.5 %collective-permute-start.11 = (bf16[512,128]{1,0:T(8,128)(2,1)S(1)}, bf16[512,128]{1,0:T(8,128)(2,1)S(1)}, u32[]{:S(2)}, u32[]{:S(2)}) collective-permute-start(bf16[512,128]{1,0:T(8,128)(2,1)S(1)} %get-tuple-element.76), channel_id=1, source_target_pairs={{0,12},{4,8},{8,4},{12,0},{1,13},{5,9},{9,5},{13,1},{2,14},{6,10},... | collective-permute-start | bytes 393224 | tf_op jit(solution)/shard_map/ppermute | solution.py:566
  45.6 6.5 %shard_map.100 = (bf16[512,128]{1,0:T(8,128)(2,1)S(1)}, bf16[512,128]{1,0:T(8,128)(2,1)S(1)}, bf16[512,128]{1,0:T(8,128)(2,1)S(1)}, bf16[512,128]{1,0:T(8,128)(2...) custom-call(s32[4]{0:T(128)S(1)} %pad_add_fusion.place_ref.refs_0_, ...), custom_call_target="tpu_custom_call" | custom-call | flops 8049999872 | bytes 1048576 | tf_op jit(solution)/shard_map/pallas_call | solution.py:546
  52.1 10.4 %collective-permute-start.14 = (bf16[512,128]{1,0:T(8,128)(2,1)S(1)}, bf16[512,128]{1,0:T(8,128)(2,1)S(1)}, u32[]{:S(2)}, u32[]{:S(2)}) collective-permute-start(bf16[512,128]{1,0:T(8,128)(2,1)S(1)} %get-tuple-element.91), channel_id=1, source_target_pairs={{0,8},{4,12},{8,0},{12,4},{1,9},{5,13},{9,1},{13,5},{2,10},{6,14},... | collective-permute-start | bytes 393224 | tf_op jit(solution)/shard_map/ppermute | solution.py:566
  62.5 1.3 %collective-permute-start.26 = (bf16[512,128]{1,0:T(8,128)(2,1)S(1)}, bf16[512,128]{1,0:T(8,128)(2,1)S(1)}, u32[]{:S(2)}, u32[]{:S(2)}) collective-permute-start(bf16[512,128]{1,0:T(8,128)(2,1)S(1)} %get-tuple-element.104), channel_id=1, source_target_pairs={{0,12},{4,8},{8,4},{12,0},{1,13},{5,9},{9,5},{13,1},{2,14},{6,10},... | collective-permute-start | bytes 393224 | tf_op jit(solution)/shard_map/ppermute | solution.py:566
  63.8 0.0 collective-permute-done.10.refs_6_
  63.8 7.0 %shard_map.101 = (bf16[1024,128]{1,0:T(8,128)(2,1)S(1)}, bf16[1024,128]{1,0:T(8,128)(2,1)S(1)}, bf16[1024,128]{1,0:T(8,128)(2,1)S(1)}, bf16[1024,128]{1,0:T(8,12...) custom-call(s32[4]{0:T(128)S(1)} %pad_add_fusion.place_ref.refs_0_, ...), custom_call_target="tpu_custom_call" | custom-call | flops 11500000256 | bytes 1048576 | tf_op jit(solution)/shard_map/pallas_call | solution.py:546
  70.8 1.1 collective-permute-start.13
  71.9 0.0 collective-permute-done.14.refs_3_.refs_10_
  71.9 2.0 %collective-permute-start.16 = (bf16[1024,128]{1,0:T(8,128)(2,1)S(1)}, bf16[1024,128]{1,0:T(8,128)(2,1)S(1)}, u32[]{:S(2)}, u32[]{:S(2)}) collective-permute-start(bf16[1024,128]{1,0:T(8,128)(2,1)S(1)} %get-tuple-element.93), channel_id=1, source_target_pairs={{0,12},{4,8},{8,4},{12,0},{1,13},{5,9},{9,5},{13,1},{2,14},{6,10},... | collective-permute-start | bytes 786440 | tf_op jit(solution)/shard_map/ppermute | solution.py:566
  74.0 1.5 %collective-permute-start.15 = (bf16[1024,128]{1,0:T(8,128)(2,1)S(1)}, bf16[1024,128]{1,0:T(8,128)(2,1)S(1)}, u32[]{:S(2)}, u32[]{:S(2)}) collective-permute-start(bf16[1024,128]{1,0:T(8,128)(2,1)S(1)} %get-tuple-element.92), channel_id=1, source_target_pairs={{0,8},{4,12},{8,0},{12,4},{1,9},{5,13},{9,1},{13,5},{2,10},{6,14},... | collective-permute-start | bytes 786440 | tf_op jit(solution)/shard_map/ppermute | solution.py:566
  75.5 0.0 collective-permute-done.26.refs_4_.refs_11_
  75.5 0.6 shard_map.104
  76.1 1.8 %collective-permute-start.27 = (bf16[4,512,128]{2,1,0:T(8,128)(2,1)S(1)}, bf16[4,512,128]{2,1,0:T(8,128)(2,1)S(1)}, u32[]{:S(2)}, u32[]{:S(2)}) collective-permute-start(bf16[4,512,128]{2,1,0:T(8,128)(2,1)S(1)} %shard_map.104), channel_id=1, source_target_pairs={{0,1},{1,0},{2,3},{3,2},{4,5},{5,4},{6,7},{7,6},{8,9},{9,8},{10,11... | collective-permute-start | bytes 1572872 | tf_op jit(solution)/shard_map/ppermute | solution.py:572
  77.9 2.8 %collective-permute-done.16.refs_3_ = bf16[1024,128]{1,0:T(8,128)(2,1)S(1)} collective-permute-done((bf16[1024,128]{1,0:T(8,128)(2,1)S(1)}, bf16[1024,128]{1,0:T(8,128)(2,1)S(1)}, u32[]{:S(2)}, u32[]{:S(2)}) %collective-permute-start.16) | collective-permute-done | bytes 262176 | tf_op jit(solution)/shard_map/ppermute | solution.py:566
  80.7 3.2 %collective-permute-start.21 = (bf16[1024,128]{1,0:T(8,128)(2,1)S(1)}, bf16[1024,128]{1,0:T(8,128)(2,1)S(1)}, u32[]{:S(2)}, u32[]{:S(2)}) collective-permute-start(bf16[1024,128]{1,0:T(8,128)(2,1)S(1)} %get-tuple-element.99.refs_0_), channel_id=1, source_target_pairs={{0,1},{1,0},{2,3},{3,2},{4,5},{5,4},{6,7},{7,6},{8,9},{9,8},{10,11... | collective-permute-start | bytes 786440 | tf_op jit(solution)/shard_map/ppermute | solution.py:572
  84.0 5.3 %collective-permute-done.20.refs_1_ = bf16[1024,128]{1,0:T(8,128)(2,1)S(1)} collective-permute-done((bf16[1024,128]{1,0:T(8,128)(2,1)S(1)}, bf16[1024,128]{1,0:T(8,128)(2,1)S(1)}, u32[]{:S(2)}, u32[]{:S(2)}) %collective-permute-start.20) | collective-permute-done | bytes 262176 | tf_op jit(solution)/shard_map/ppermute | solution.py:566
  89.2 0.5 collective-permute-start.24
  89.7 0.0 collective-permute-done.13.theirs_ref
  89.7 0.0 collective-permute-start.22
  89.7 0.6 shard_map.102
  90.3 7.1 %collective-permute-done.15.refs_2_ = bf16[1024,128]{1,0:T(8,128)(2,1)S(1)} collective-permute-done((bf16[1024,128]{1,0:T(8,128)(2,1)S(1)}, bf16[1024,128]{1,0:T(8,128)(2,1)S(1)}, u32[]{:S(2)}, u32[]{:S(2)}) %collective-permute-start.15) | collective-permute-done | bytes 262176 | tf_op jit(solution)/shard_map/ppermute | solution.py:566
  97.4 0.5 collective-permute-start.23
  97.9 0.0 collective-permute-done.21.refs_4_
  97.9 0.0 collective-permute-start.17
  97.9 0.0 collective-permute-done.24.refs_7_
  97.9 2.5 %collective-permute-start.18 = (bf16[576,128]{1,0:T(8,128)(2,1)S(1)}, bf16[576,128]{1,0:T(8,128)(2,1)S(1)}, u32[]{:S(2)}, u32[]{:S(2)}) collective-permute-start(bf16[576,128]{1,0:T(8,128)(2,1)S(1)} %get-tuple-element.96), channel_id=1, source_target_pairs={{0,8},{4,12},{8,0},{12,4},{1,9},{5,13},{9,1},{13,5},{2,10},{6,14},... | collective-permute-start | bytes 442376 | tf_op jit(solution)/shard_map/ppermute | solution.py:566
  100.4 0.0 collective-permute-done.22.refs_5_
  100.4 1.1 collective-permute-start.19
  101.5 0.0 collective-permute-done.27.refs_12_
  101.5 0.0 collective-permute-done.23.refs_6_
  101.5 2.9 %shard_map.105 = bf16[256,1024]{1,0:T(8,128)(2,1)S(1)} custom-call(s32[4]{0:T(128)S(1)} %pad_add_fusion.place_ref.refs_0_, bf16[1024,128]{1,0:T(8,128)(2,1)S(1)} %get-tuple-element.99.refs_0_, bf16[1024,128]{1,0:T(8,128)(2,1)S(1)} %collective-permute-done.20.refs_1_, bf16[1024,128]{1,0:T(8,128)(2,1)S(1)} %collective-permute-done.15.refs_2_, ...), custom_call_target="tpu_custom_call" | custom-call | flops 1150000000 | bytes 1048576 | tf_op jit(solution)/shard_map/pallas_call | solution.py:546
  104.4 1.2 %collective-permute-start.28 = (bf16[256,1024]{1,0:T(8,128)(2,1)S(1)}, bf16[256,1024]{1,0:T(8,128)(2,1)S(1)}, u32[]{:S(2)}, u32[]{:S(2)}) collective-permute-start(bf16[256,1024]{1,0:T(8,128)(2,1)S(1)} %shard_map.105), channel_id=1, source_target_pairs={{0,1},{1,3},{3,2},{2,0},{4,5},{5,7},{7,6},{6,4},{8,9},{9,11},{11,1... | collective-permute-start | bytes 1572872 | tf_op jit(solution)/shard_map/ppermute | solution.py:717
  105.6 2.9 %shard_map.106.kept_ref = bf16[256,1024]{1,0:T(8,128)(2,1)S(1)} custom-call(s32[4]{0:T(128)S(1)} %pad_add_fusion.place_ref.refs_0_, bf16[1024,128]{1,0:T(8,128)(2,1)S(1)} %get-tuple-element.99.refs_0_, bf16[1024,128]{1,0:T(8,128)(2,1)S(1)} %collective-permute-done.20.refs_1_, bf16[1024,128]{1,0:T(8,128)(2,1)S(1)} %collective-permute-done.15.refs_2_, ...), custom_call_target="tpu_custom_call" | custom-call | flops 1150000000 | bytes 1048576 | tf_op jit(solution)/shard_map/pallas_call | solution.py:546
  108.5 3.2 %collective-permute-start.29 = (bf16[256,1024]{1,0:T(8,128)(2,1)S(1)}, bf16[256,1024]{1,0:T(8,128)(2,1)S(1)}, u32[]{:S(2)}, u32[]{:S(2)}) collective-permute-start(bf16[256,1024]{1,0:T(8,128)(2,1)S(1)} %shard_map.106.kept_ref), channel_id=1, source_target_pairs={{1,2},{2,1},{5,6},{6,5},{9,10},{10,9},{13,14},{14,13},{17,18},{18,... | collective-permute-start | bytes 1572872 | tf_op jit(solution)/shard_map/ppermute | solution.py:719
  111.7 0.0 collective-permute-done.18.refs_2_
  111.7 0.0 collective-permute-done.19.refs_3_
  111.7 1.5 %shard_map.103 = (bf16[256,1024]{1,0:T(8,128)(2,1)}, f32[8,32,128]{2,1,0:T(8,128)}) custom-call(s32[4]{0:T(128)S(1)} %pad_add_fusion.place_ref.refs_0_, bf16[576,128]{1,0:T(8,128)(2,1)S(1)} %get-tuple-element.94.refs_0_, bf16[576,128]{1,0:T(8,128)(2,1)S(1)} %collective-permute-done.17.refs_1_, bf16[576,128]{1,0:T(8,128)(2,1)S(1)} %collective-permute-done.18.refs_2_, ...), custom_call_target="tpu_custom_call" | custom-call | flops 9200000000 | bytes 1048576 | tf_op jit(solution)/shard_map/pallas_call | solution.py:546
  113.3 6.1 %collective-permute-done.29.second_ref = bf16[256,1024]{1,0:T(8,128)(2,1)S(1)} collective-permute-done((bf16[256,1024]{1,0:T(8,128)(2,1)S(1)}, bf16[256,1024]{1,0:T(8,128)(2,1)S(1)}, u32[]{:S(2)}, u32[]{:S(2)}) %collective-permute-start.29) | collective-permute-done | bytes 524320 | tf_op jit(solution)/shard_map/ppermute | solution.py:719
  119.4 1.5 %shard_map.107 = bf16[256,1024]{1,0:T(8,128)(2,1)} custom-call(s32[4]{0:T(128)S(1)} %pad_add_fusion.place_ref.refs_0_, bf16[256,1024]{1,0:T(8,128)(2,1)S(1)} %collective-permute-done.28.first_ref, bf16[256,1024]{1,0:T(8,128)(2,1)S(1)} %collective-permute-done.29.second_ref, bf16[256,1024]{1,0:T(8,128)(2,1)S(1)} %shard_map.106.kept_ref), custom_call_target="tpu_custom_call" | custom-call | flops 1150000000 | bytes 1048576 | tf_op jit(solution)/shard_map/pallas_call | solution.py:546
  (19 shorter events, 0.0 us)
Async XLA Ops:
  0.6 2.9 %collective-permute-start = (bf16[256,2048]{1,0:T(8,128)(2,1)}, bf16[256,2048]{1,0:T(8,128)(2,1)S(1)}, u32[]{:S(2)}, u32[]{:S(2)}) collective-permute-start(bf16[256,2048]{1,0:T(8,128)(2,1)} %refs_1_.3), channel_id=1, source_target_pairs={{0,1},{1,0},{2,3},{3,2},{4,5},{5,4},{6,7},{7,6},{8,9},{9,8},{10,11... | collective-permute-start | bytes 3145736 | tf_op jit(solution)/shard_map/ppermute | solution.py:572
  2.5 3.0 %collective-permute-start.1 = (bf16[4,272,128]{2,1,0:T(8,128)(2,1)S(1)}, bf16[4,272,128]{2,1,0:T(8,128)(2,1)S(1)}, u32[]{:S(2)}, u32[]{:S(2)}) collective-permute-start(bf16[4,272,128]{2,1,0:T(8,128)(2,1)S(1)} %get-tuple-element.59), channel_id=1, source_target_pairs={{0,1},{1,0},{2,3},{3,2},{4,5},{5,4},{6,7},{7,6},{8,9},{9,8},{10,11... | collective-permute-start | bytes 835592 | tf_op jit(solution)/shard_map/ppermute | solution.py:572
  8.4 5.0 %collective-permute-start.2 = (bf16[2,512,512]{2,1,0:T(8,128)(2,1)S(1)}, bf16[2,512,512]{2,1,0:T(8,128)(2,1)S(1)}, u32[]{:S(2)}, u32[]{:S(2)}) collective-permute-start(bf16[2,512,512]{2,1,0:T(8,128)(2,1)S(1)} %get-tuple-element.60), channel_id=1, source_target_pairs={{0,1},{1,0},{2,3},{3,2},{4,5},{5,4},{6,7},{7,6},{8,9},{9,8},{10,11... | collective-permute-start | bytes 3145736 | tf_op jit(solution)/shard_map/ppermute | solution.py:572
  8.6 14.3 %collective-permute-start.7 = (bf16[544,128]{1,0:T(8,128)(2,1)S(1)}, bf16[544,128]{1,0:T(8,128)(2,1)S(1)}, u32[]{:S(2)}, u32[]{:S(2)}) collective-permute-start(bf16[544,128]{1,0:T(8,128)(2,1)S(1)} %get-tuple-element.66), channel_id=1, source_target_pairs={{0,8},{4,12},{8,0},{12,4},{1,9},{5,13},{9,1},{13,5},{2,10},{6,14},... | collective-permute-start | bytes 417800 | tf_op jit(solution)/shard_map/ppermute | solution.py:566
  12.3 13.4 %collective-permute-start.8 = (bf16[544,128]{1,0:T(8,128)(2,1)S(1)}, bf16[544,128]{1,0:T(8,128)(2,1)S(1)}, u32[]{:S(2)}, u32[]{:S(2)}) collective-permute-start(bf16[544,128]{1,0:T(8,128)(2,1)S(1)} %get-tuple-element.67), channel_id=1, source_target_pairs={{0,12},{4,8},{8,4},{12,0},{1,13},{5,9},{9,5},{13,1},{2,14},{6,10},... | collective-permute-start | bytes 417800 | tf_op jit(solution)/shard_map/ppermute | solution.py:566
  16.0 9.8 %collective-permute-start.6 = (bf16[1,512,512]{2,1,0:T(8,128)(2,1)S(1)}, bf16[1,512,512]{2,1,0:T(8,128)(2,1)S(1)}, u32[]{:S(2)}, u32[]{:S(2)}) collective-permute-start(bf16[1,512,512]{2,1,0:T(8,128)(2,1)S(1)} %shard_map.98), channel_id=1, source_target_pairs={{0,1},{1,0},{2,3},{3,2},{4,5},{5,4},{6,7},{7,6},{8,9},{9,8},{10,11... | collective-permute-start | bytes 1572872 | tf_op jit(solution)/shard_map/ppermute | solution.py:572
  20.4 12.5 %collective-permute-start.3 = (bf16[1024,128]{1,0:T(8,128)(2,1)S(1)}, bf16[1024,128]{1,0:T(8,128)(2,1)S(1)}, u32[]{:S(2)}, u32[]{:S(2)}) collective-permute-start(bf16[1024,128]{1,0:T(8,128)(2,1)S(1)} %get-tuple-element.62), channel_id=1, source_target_pairs={{0,4},{4,0},{8,12},{12,8},{1,5},{5,1},{9,13},{13,9},{2,6},{6,2},{1... | collective-permute-start | bytes 786440 | tf_op jit(solution)/shard_map/ppermute | solution.py:566
  20.5 21.6 %collective-permute-start.4 = (bf16[1024,128]{1,0:T(8,128)(2,1)S(1)}, bf16[1024,128]{1,0:T(8,128)(2,1)S(1)}, u32[]{:S(2)}, u32[]{:S(2)}) collective-permute-start(bf16[1024,128]{1,0:T(8,128)(2,1)S(1)} %get-tuple-element.63), channel_id=1, source_target_pairs={{0,8},{4,12},{8,0},{12,4},{1,9},{5,13},{9,1},{13,5},{2,10},{6,14},... | collective-permute-start | bytes 786440 | tf_op jit(solution)/shard_map/ppermute | solution.py:566
  23.0 22.7 %collective-permute-start.5 = (bf16[1024,128]{1,0:T(8,128)(2,1)S(1)}, bf16[1024,128]{1,0:T(8,128)(2,1)S(1)}, u32[]{:S(2)}, u32[]{:S(2)}) collective-permute-start(bf16[1024,128]{1,0:T(8,128)(2,1)S(1)} %get-tuple-element.64), channel_id=1, source_target_pairs={{0,12},{4,8},{8,4},{12,0},{1,13},{5,9},{9,5},{13,1},{2,14},{6,10},... | collective-permute-start | bytes 786440 | tf_op jit(solution)/shard_map/ppermute | solution.py:566
  25.7 19.9 %copy-start.3 = (s32[256]{0:T(256)S(1)}, s32[256]{0:T(256)}, u32[]{:S(2)}) copy-start(s32[256]{0:T(256)} %param.11) | copy-start | bytes 3076
  25.7 19.9 %collective-permute-start.12 = (bf16[544,128]{1,0:T(8,128)(2,1)S(1)}, bf16[544,128]{1,0:T(8,128)(2,1)S(1)}, u32[]{:S(2)}, u32[]{:S(2)}) collective-permute-start(bf16[544,128]{1,0:T(8,128)(2,1)S(1)} %get-tuple-element.78), channel_id=1, source_target_pairs={{0,4},{4,0},{8,12},{12,8},{1,5},{5,1},{9,13},{13,9},{2,6},{6,2},{1... | collective-permute-start | bytes 417800 | tf_op jit(solution)/shard_map/ppermute | solution.py:566
  28.7 33.8 %collective-permute-start.9 = (bf16[512,128]{1,0:T(8,128)(2,1)S(1)}, bf16[512,128]{1,0:T(8,128)(2,1)S(1)}, u32[]{:S(2)}, u32[]{:S(2)}) collective-permute-start(bf16[512,128]{1,0:T(8,128)(2,1)S(1)} %get-tuple-element.74), channel_id=1, source_target_pairs={{0,4},{4,0},{8,12},{12,8},{1,5},{5,1},{9,13},{13,9},{2,6},{6,2},{1... | collective-permute-start | bytes 393224 | tf_op jit(solution)/shard_map/ppermute | solution.py:566
  32.9 30.9 %collective-permute-start.10 = (bf16[512,128]{1,0:T(8,128)(2,1)S(1)}, bf16[512,128]{1,0:T(8,128)(2,1)S(1)}, u32[]{:S(2)}, u32[]{:S(2)}) collective-permute-start(bf16[512,128]{1,0:T(8,128)(2,1)S(1)} %get-tuple-element.75), channel_id=1, source_target_pairs={{0,8},{4,12},{8,0},{12,4},{1,9},{5,13},{9,1},{13,5},{2,10},{6,14},... | collective-permute-start | bytes 393224 | tf_op jit(solution)/shard_map/ppermute | solution.py:566
  42.1 21.7 %collective-permute-start.11 = (bf16[512,128]{1,0:T(8,128)(2,1)S(1)}, bf16[512,128]{1,0:T(8,128)(2,1)S(1)}, u32[]{:S(2)}, u32[]{:S(2)}) collective-permute-start(bf16[512,128]{1,0:T(8,128)(2,1)S(1)} %get-tuple-element.76), channel_id=1, source_target_pairs={{0,12},{4,8},{8,4},{12,0},{1,13},{5,9},{9,5},{13,1},{2,14},{6,10},... | collective-permute-start | bytes 393224 | tf_op jit(solution)/shard_map/ppermute | solution.py:566
  52.1 19.8 %collective-permute-start.14 = (bf16[512,128]{1,0:T(8,128)(2,1)S(1)}, bf16[512,128]{1,0:T(8,128)(2,1)S(1)}, u32[]{:S(2)}, u32[]{:S(2)}) collective-permute-start(bf16[512,128]{1,0:T(8,128)(2,1)S(1)} %get-tuple-element.91), channel_id=1, source_target_pairs={{0,8},{4,12},{8,0},{12,4},{1,9},{5,13},{9,1},{13,5},{2,10},{6,14},... | collective-permute-start | bytes 393224 | tf_op jit(solution)/shard_map/ppermute | solution.py:566
  62.5 11.5 %collective-permute-start.25 = (bf16[512,128]{1,0:T(8,128)(2,1)S(1)}, bf16[512,128]{1,0:T(8,128)(2,1)S(1)}, u32[]{:S(2)}, u32[]{:S(2)}) collective-permute-start(bf16[512,128]{1,0:T(8,128)(2,1)S(1)} %get-tuple-element.103), channel_id=1, source_target_pairs={{0,4},{4,0},{8,12},{12,8},{1,5},{5,1},{9,13},{13,9},{2,6},{6,2},{1... | collective-permute-start | bytes 393224 | tf_op jit(solution)/shard_map/ppermute | solution.py:566
  62.5 13.0 %collective-permute-start.26 = (bf16[512,128]{1,0:T(8,128)(2,1)S(1)}, bf16[512,128]{1,0:T(8,128)(2,1)S(1)}, u32[]{:S(2)}, u32[]{:S(2)}) collective-permute-start(bf16[512,128]{1,0:T(8,128)(2,1)S(1)} %get-tuple-element.104), channel_id=1, source_target_pairs={{0,12},{4,8},{8,4},{12,0},{1,13},{5,9},{9,5},{13,1},{2,14},{6,10},... | collective-permute-start | bytes 393224 | tf_op jit(solution)/shard_map/ppermute | solution.py:566
  70.8 18.9 %collective-permute-start.13 = (bf16[4,288,128]{2,1,0:T(8,128)(2,1)S(1)}, bf16[4,288,128]{2,1,0:T(8,128)(2,1)S(1)}, u32[]{:S(2)}, u32[]{:S(2)}) collective-permute-start(bf16[4,288,128]{2,1,0:T(8,128)(2,1)S(1)} %get-tuple-element.82), channel_id=1, source_target_pairs={{0,1},{1,0},{2,3},{3,2},{4,5},{5,4},{6,7},{7,6},{8,9},{9,8},{10,11... | collective-permute-start | bytes 884744 | tf_op jit(solution)/shard_map/ppermute | solution.py:572
  71.9 8.8 %collective-permute-start.16 = (bf16[1024,128]{1,0:T(8,128)(2,1)S(1)}, bf16[1024,128]{1,0:T(8,128)(2,1)S(1)}, u32[]{:S(2)}, u32[]{:S(2)}) collective-permute-start(bf16[1024,128]{1,0:T(8,128)(2,1)S(1)} %get-tuple-element.93), channel_id=1, source_target_pairs={{0,12},{4,8},{8,4},{12,0},{1,13},{5,9},{9,5},{13,1},{2,14},{6,10},... | collective-permute-start | bytes 786440 | tf_op jit(solution)/shard_map/ppermute | solution.py:566
  74.0 15.3 %collective-permute-start.20 = (bf16[1024,128]{1,0:T(8,128)(2,1)S(1)}, bf16[1024,128]{1,0:T(8,128)(2,1)S(1)}, u32[]{:S(2)}, u32[]{:S(2)}) collective-permute-start(bf16[1024,128]{1,0:T(8,128)(2,1)S(1)} %get-tuple-element.100), channel_id=1, source_target_pairs={{0,4},{4,0},{8,12},{12,8},{1,5},{5,1},{9,13},{13,9},{2,6},{6,2},{1... | collective-permute-start | bytes 786440 | tf_op jit(solution)/shard_map/ppermute | solution.py:566
  74.0 23.4 %collective-permute-start.15 = (bf16[1024,128]{1,0:T(8,128)(2,1)S(1)}, bf16[1024,128]{1,0:T(8,128)(2,1)S(1)}, u32[]{:S(2)}, u32[]{:S(2)}) collective-permute-start(bf16[1024,128]{1,0:T(8,128)(2,1)S(1)} %get-tuple-element.92), channel_id=1, source_target_pairs={{0,8},{4,12},{8,0},{12,4},{1,9},{5,13},{9,1},{13,5},{2,10},{6,14},... | collective-permute-start | bytes 786440 | tf_op jit(solution)/shard_map/ppermute | solution.py:566
  75.5 26.0 %copy-start.2 = (bf16[1024,1024]{1,0:T(8,128)(2,1)S(1)}, bf16[1024,1024]{1,0:T(8,128)(2,1)}, u32[]{:S(2)}) copy-start(bf16[1024,1024]{1,0:T(8,128)(2,1)} %refs_13_.3) | copy-start | bytes 6291460
  76.1 25.4 %collective-permute-start.27 = (bf16[4,512,128]{2,1,0:T(8,128)(2,1)S(1)}, bf16[4,512,128]{2,1,0:T(8,128)(2,1)S(1)}, u32[]{:S(2)}, u32[]{:S(2)}) collective-permute-start(bf16[4,512,128]{2,1,0:T(8,128)(2,1)S(1)} %shard_map.104), channel_id=1, source_target_pairs={{0,1},{1,0},{2,3},{3,2},{4,5},{5,4},{6,7},{7,6},{8,9},{9,8},{10,11... | collective-permute-start | bytes 1572872 | tf_op jit(solution)/shard_map/ppermute | solution.py:572
  80.7 17.2 %collective-permute-start.21 = (bf16[1024,128]{1,0:T(8,128)(2,1)S(1)}, bf16[1024,128]{1,0:T(8,128)(2,1)S(1)}, u32[]{:S(2)}, u32[]{:S(2)}) collective-permute-start(bf16[1024,128]{1,0:T(8,128)(2,1)S(1)} %get-tuple-element.99.refs_0_), channel_id=1, source_target_pairs={{0,1},{1,0},{2,3},{3,2},{4,5},{5,4},{6,7},{7,6},{8,9},{9,8},{10,11... | collective-permute-start | bytes 786440 | tf_op jit(solution)/shard_map/ppermute | solution.py:572
  89.2 8.7 %collective-permute-start.24 = (bf16[1024,128]{1,0:T(8,128)(2,1)S(1)}, bf16[1024,128]{1,0:T(8,128)(2,1)S(1)}, u32[]{:S(2)}, u32[]{:S(2)}) collective-permute-start(bf16[1024,128]{1,0:T(8,128)(2,1)S(1)} %collective-permute-done.16.refs_3_), channel_id=1, source_target_pairs={{0,1},{1,0},{2,3},{3,2},{4,5},{5,4},{6,7},{7,6},{8,9},{9,8},{10,11... | collective-permute-start | bytes 786440 | tf_op jit(solution)/shard_map/ppermute | solution.py:572
  89.7 10.7 %collective-permute-start.22 = (bf16[1024,128]{1,0:T(8,128)(2,1)S(1)}, bf16[1024,128]{1,0:T(8,128)(2,1)S(1)}, u32[]{:S(2)}, u32[]{:S(2)}) collective-permute-start(bf16[1024,128]{1,0:T(8,128)(2,1)S(1)} %collective-permute-done.20.refs_1_), channel_id=1, source_target_pairs={{0,1},{1,0},{2,3},{3,2},{4,5},{5,4},{6,7},{7,6},{8,9},{9,8},{10,11... | collective-permute-start | bytes 786440 | tf_op jit(solution)/shard_map/ppermute | solution.py:572
  89.7 11.7 %copy-start = (bf16[1024,1024]{1,0:T(8,128)(2,1)S(1)}, bf16[1024,1024]{1,0:T(8,128)(2,1)}, u32[]{:S(2)}) copy-start(bf16[1024,1024]{1,0:T(8,128)(2,1)} %refs_15_.3) | copy-start | bytes 6291460
  89.7 11.7 %copy-start.1 = (bf16[1024,1024]{1,0:T(8,128)(2,1)S(1)}, bf16[1024,1024]{1,0:T(8,128)(2,1)}, u32[]{:S(2)}) copy-start(bf16[1024,1024]{1,0:T(8,128)(2,1)} %refs_14_.3) | copy-start | bytes 6291460
  97.4 4.1 %collective-permute-start.23 = (bf16[1024,128]{1,0:T(8,128)(2,1)S(1)}, bf16[1024,128]{1,0:T(8,128)(2,1)S(1)}, u32[]{:S(2)}, u32[]{:S(2)}) collective-permute-start(bf16[1024,128]{1,0:T(8,128)(2,1)S(1)} %collective-permute-done.15.refs_2_), channel_id=1, source_target_pairs={{0,1},{1,0},{2,3},{3,2},{4,5},{5,4},{6,7},{7,6},{8,9},{9,8},{10,11... | collective-permute-start | bytes 786440 | tf_op jit(solution)/shard_map/ppermute | solution.py:572
  97.9 13.8 %collective-permute-start.17 = (bf16[576,128]{1,0:T(8,128)(2,1)S(1)}, bf16[576,128]{1,0:T(8,128)(2,1)S(1)}, u32[]{:S(2)}, u32[]{:S(2)}) collective-permute-start(bf16[576,128]{1,0:T(8,128)(2,1)S(1)} %get-tuple-element.95), channel_id=1, source_target_pairs={{0,4},{4,0},{8,12},{12,8},{1,5},{5,1},{9,13},{13,9},{2,6},{6,2},{1... | collective-permute-start | bytes 442376 | tf_op jit(solution)/shard_map/ppermute | solution.py:566
  97.9 13.8 %collective-permute-start.18 = (bf16[576,128]{1,0:T(8,128)(2,1)S(1)}, bf16[576,128]{1,0:T(8,128)(2,1)S(1)}, u32[]{:S(2)}, u32[]{:S(2)}) collective-permute-start(bf16[576,128]{1,0:T(8,128)(2,1)S(1)} %get-tuple-element.96), channel_id=1, source_target_pairs={{0,8},{4,12},{8,0},{12,4},{1,9},{5,13},{9,1},{13,5},{2,10},{6,14},... | collective-permute-start | bytes 442376 | tf_op jit(solution)/shard_map/ppermute | solution.py:566
  100.4 11.3 %collective-permute-start.19 = (bf16[576,128]{1,0:T(8,128)(2,1)S(1)}, bf16[576,128]{1,0:T(8,128)(2,1)S(1)}, u32[]{:S(2)}, u32[]{:S(2)}) collective-permute-start(bf16[576,128]{1,0:T(8,128)(2,1)S(1)} %get-tuple-element.97), channel_id=1, source_target_pairs={{0,12},{4,8},{8,4},{12,0},{1,13},{5,9},{9,5},{13,1},{2,14},{6,10},... | collective-permute-start | bytes 442376 | tf_op jit(solution)/shard_map/ppermute | solution.py:566
  104.4 15.0 %collective-permute-start.28 = (bf16[256,1024]{1,0:T(8,128)(2,1)S(1)}, bf16[256,1024]{1,0:T(8,128)(2,1)S(1)}, u32[]{:S(2)}, u32[]{:S(2)}) collective-permute-start(bf16[256,1024]{1,0:T(8,128)(2,1)S(1)} %shard_map.105), channel_id=1, source_target_pairs={{0,1},{1,3},{3,2},{2,0},{4,5},{5,7},{7,6},{6,4},{8,9},{9,11},{11,1... | collective-permute-start | bytes 1572872 | tf_op jit(solution)/shard_map/ppermute | solution.py:717
  108.5 10.8 %collective-permute-start.29 = (bf16[256,1024]{1,0:T(8,128)(2,1)S(1)}, bf16[256,1024]{1,0:T(8,128)(2,1)S(1)}, u32[]{:S(2)}, u32[]{:S(2)}) collective-permute-start(bf16[256,1024]{1,0:T(8,128)(2,1)S(1)} %shard_map.106.kept_ref), channel_id=1, source_target_pairs={{1,2},{2,1},{5,6},{6,5},{9,10},{10,9},{13,14},{14,13},{17,18},{18,... | collective-permute-start | bytes 1572872 | tf_op jit(solution)/shard_map/ppermute | solution.py:719

commit v16 on v14

--- a/solution.py
+++ b/solution.py
@@ -682,13 +682,12 @@
     outputs = call(
         merge_kernel, buffers(2 * (rows + owned)), place, attended_mine, to_sibling(attended_theirs)
     )
-    early_back, _ = lax.optimization_barrier((back[2], outputs[0]))
-    back_other = tuple(
-        to_sibling(early_back if offset == 2 else part) for offset, part in enumerate(back)
-    )
     value_other = to_sibling(
         call(join_kernel, low(chips, 2 * rows, head_dim), place, *value_back)
     )
+    zero, one, three = (to_sibling(back[offset]) for offset in (0, 1, 3))
+    last, *_ = lax.optimization_barrier((back[2], outputs[0], zero, one, three, value_other))
+    back_other = (zero, one, to_sibling(last), three)
 
     def input_part(which, place):
         return call(
@@ -705,7 +704,7 @@
             scratch=[pltpu.VMEM((rows, 3 * width), jnp.bfloat16)],
         )
 
-    *outputs, _, _ = lax.optimization_barrier((*outputs, back[2], back[3]))
+    *outputs, _ = lax.optimization_barrier((*outputs, back[3]))
     returned = exchange(outputs)
     square = ("head", "sub")
     crossing = input_part(3, place)
@@ -717,7 +716,7 @@
         (low(rows, width), jax.ShapeDtypeStruct((count, owned, head_dim), jnp.float32)),
         place,
         *returned,
-        takes=8,
+        takes=20,
     )
     first, second, _ = lax.optimization_barrier((first, second, attended))
     d_hidden = call(sum_kernel, low(rows, half), place, first, second, kept)

time: 121 us -> 121 us (level)
  starting transfers between devices: 47.1 us -> 49.3 us
  waiting for transfers between devices: 33.3 us -> 31.2 us
    ppermute x18, waiting for transfers between devices: 27.1 us -> 25.1 us  [exchange(): lax.ppermute(parts[offset], 'seq', [(at, at ^ offset) for at in range(chi...]
where the time goes in v16:
time: 121 us
  starting transfers between devices  49.3 us (41%)
  Pallas kernels  39.3 us (32%)
  waiting for transfers between devices  31.2 us (26%)
    pallas_call x14, Pallas kernels, call(): pl.pallas_call(kernel, out_shape=outs, in_specs=[smem] + [vmem] * (len(op...  39.3 us
    ppermute x18, starting transfers between devices, exchange(): lax.ppermute(parts[offset], 'seq', [(at, at ^ offset) for at in range(chi...  35.1 us
    ppermute x18, waiting for transfers between devices, exchange(): lax.ppermute(parts[offset], 'seq', [(at, at ^ offset) for at in range(chi...  25.1 us
    ppermute x10, starting transfers between devices, to_sibling(): return lax.ppermute(piece, 'sub', swap)  9.69 us
    ppermute x1, waiting for transfers between devices, by_head(): second = lax.ppermute(kept, square, [(1, 2), (2, 1)])  6.1 us
    ppermute x1, starting transfers between devices, by_head(): second = lax.ppermute(kept, square, [(1, 2), (2, 1)])  3.24 us
  transfers between devices with their start and end apart: 30, of which 6 were waited for; matrix products, arithmetic and copies ran while one was open for 0% of the time, Pallas kernels for 29%

profile of v16, /device:TPU:1, one launch (start us, length us, event | category | flops | bytes accessed | tf_op | source)
XLA Modules:
  0.0 120.7 jit_solution(10675904481618143147)
XLA Ops:
  0.6 0.1 collective-permute-start.1
  0.8 0.1 pad_add_fusion.place_ref.refs_0_
  0.8 1.7 %shard_map.95 = (bf16[4,272,128]{2,1,0:T(8,128)(2,1)S(1)}, bf16[4,272,128]{2,1,0:T(8,128)(2,1)S(1)}) custom-call(s32[4]{0:T(128)S(1)} %pad_add_fusion.place_ref.refs_0_, bf16[256,1024]{1,0:T(8,128)(2,1)} %grads_ref.1, s32[8,256]{1,0:T(8,128)} %assign_ref.1), custom_call_target="tpu_custom_call" | custom-call | flops 1150000000 | bytes 1048576 | tf_op jit(solution)/shard_map/pallas_call | solution.py:544
  2.5 0.5 collective-permute-start
  3.1 2.1 %shard_map.94.held_ref = bf16[2,1024,512]{2,1,0:T(8,128)(2,1)S(1)} custom-call(s32[4]{0:T(128)S(1)} %pad_add_fusion.place_ref.refs_0_, bf16[1024,1024]{1,0:T(8,128)(2,1)} %refs_13_.3, bf16[1024,1024]{1,0:T(8,128)(2,1)} %refs_14_.3), custom_call_target="tpu_custom_call" | custom-call | flops 1150000000 | bytes 1048576 | tf_op jit(solution)/shard_map/pallas_call | solution.py:544
  5.2 0.0 collective-permute-done.theirs_ref
  5.2 0.0 collective-permute-done.1.refs_1_.refs_2_
  5.2 2.9 %shard_map.96 = (bf16[544,128]{1,0:T(8,128)(2,1)S(1)}, bf16[544,128]{1,0:T(8,128)(2,1)S(1)}, bf16[544,128]{1,0:T(8,128)(2,1)S(1)}, bf16[544,128]{1,0:T(8,128)(2,1)S(1)}, bf16[2,512,512]{2,1,0:T(8,128)(2,1)S(1)}) custom-call(s32[4]{0:T(128)S(1)} %pad_add_fusion.place_ref.refs_0_, bf16[2,1024,512]{2,1,0:T(8,128)(2,1)S(1)} %shard_map.94.held_ref, ...), custom_call_target="tpu_custom_call" | custom-call | flops 115000000 | bytes 1048576 | tf_op jit(solution)/shard_map/pallas_call | solution.py:544
  8.1 0.1 collective-permute-start.2
  8.2 3.8 %collective-permute-start.7 = (bf16[544,128]{1,0:T(8,128)(2,1)S(1)}, bf16[544,128]{1,0:T(8,128)(2,1)S(1)}, u32[]{:S(2)}, u32[]{:S(2)}) collective-permute-start(bf16[544,128]{1,0:T(8,128)(2,1)S(1)} %get-tuple-element.62), channel_id=1, source_target_pairs={{0,8},{4,12},{8,0},{12,4},{1,9},{5,13},{9,1},{13,5},{2,10},{6,14},... | collective-permute-start | bytes 417800 | tf_op jit(solution)/shard_map/ppermute | solution.py:564
  12.0 1.1 collective-permute-start.8
  13.1 2.7 %shard_map.98 = bf16[1,512,512]{2,1,0:T(8,128)(2,1)S(1)} custom-call(s32[4]{0:T(128)S(1)} %pad_add_fusion.place_ref.refs_0_, bf16[256,2048]{1,0:T(8,128)(2,1)} %refs_1_.5, bf16[256,2048]{1,0:T(8,128)(2,1)S(1)} %collective-permute-done.1.refs_1_.refs_2_, bf16[1024,1024]{1,0:T(8,128)(2,1)} %refs_15_.3), custom_call_target="tpu_custom_call" | custom-call | flops 115000000 | bytes 1048576 | tf_op jit(solution)/shard_map/pallas_call | solution.py:544
  15.7 0.7 collective-permute-start.6
  16.4 3.6 %shard_map.97 = (bf16[1024,128]{1,0:T(8,128)(2,1)S(1)}, bf16[1024,128]{1,0:T(8,128)(2,1)S(1)}, bf16[1024,128]{1,0:T(8,128)(2,1)S(1)}, bf16[1024,128]{1,0:T(8,128)(2,1)S(1)}) custom-call(s32[4]{0:T(128)S(1)} %pad_add_fusion.place_ref.refs_0_, bf16[2,512,512]{2,1,0:T(8,128)(2,1)S(1)} %collective-permute-done.2.refs_0_, bf16[256,2048]{1,0:T(8,128)(2,1)} %refs_1_.5, ...), custom_call_target="tpu_custom_call" | custom-call | flops 9200000000 | bytes 1048576 | tf_op jit(solution)/shard_map/pallas_call | solution.py:544
  20.0 0.1 collective-permute-start.3
  20.1 2.5 %collective-permute-start.4 = (bf16[1024,128]{1,0:T(8,128)(2,1)S(1)}, bf16[1024,128]{1,0:T(8,128)(2,1)S(1)}, u32[]{:S(2)}, u32[]{:S(2)}) collective-permute-start(bf16[1024,128]{1,0:T(8,128)(2,1)S(1)} %get-tuple-element.59), channel_id=1, source_target_pairs={{0,8},{4,12},{8,0},{12,4},{1,9},{5,13},{9,1},{13,5},{2,10},{6,14},... | collective-permute-start | bytes 786440 | tf_op jit(solution)/shard_map/ppermute | solution.py:564
  22.6 2.8 %collective-permute-start.5 = (bf16[1024,128]{1,0:T(8,128)(2,1)S(1)}, bf16[1024,128]{1,0:T(8,128)(2,1)S(1)}, u32[]{:S(2)}, u32[]{:S(2)}) collective-permute-start(bf16[1024,128]{1,0:T(8,128)(2,1)S(1)} %get-tuple-element.60), channel_id=1, source_target_pairs={{0,12},{4,8},{8,4},{12,0},{1,13},{5,9},{9,5},{13,1},{2,14},{6,10},... | collective-permute-start | bytes 786440 | tf_op jit(solution)/shard_map/ppermute | solution.py:564
  25.4 0.0 collective-permute-done.8.refs_7_.refs_11_
  25.4 0.2 collective-permute-start.12
  25.6 2.8 %shard_map.99 = (bf16[512,128]{1,0:T(8,128)(2,1)S(1)}, bf16[512,128]{1,0:T(8,128)(2,1)S(1)}, bf16[512,128]{1,0:T(8,128)(2,1)S(1)}, bf16[512,128]{1,0:T(8,128)(2,1)S(1)}) custom-call(s32[4]{0:T(128)S(1)} %pad_add_fusion.place_ref.refs_0_, bf16[1,512,512]{2,1,0:T(8,128)(2,1)S(1)} %collective-permute-done.6.refs_0_, bf16[256,2048]{1,0:T(8,128)(2,1)} %refs_1_.5, ...), custom_call_target="tpu_custom_call" | custom-call | flops 115000000 | bytes 1048576 | tf_op jit(solution)/shard_map/pallas_call | solution.py:544
  28.4 1.4 %collective-permute-start.9 = (bf16[512,128]{1,0:T(8,128)(2,1)S(1)}, bf16[512,128]{1,0:T(8,128)(2,1)S(1)}, u32[]{:S(2)}, u32[]{:S(2)}) collective-permute-start(bf16[512,128]{1,0:T(8,128)(2,1)S(1)} %get-tuple-element.70), channel_id=1, source_target_pairs={{0,4},{4,0},{8,12},{12,8},{1,5},{5,1},{9,13},{13,9},{2,6},{6,2},{1... | collective-permute-start | bytes 393224 | tf_op jit(solution)/shard_map/ppermute | solution.py:564
  29.8 2.6 %collective-permute-done.3.refs_1_ = bf16[1024,128]{1,0:T(8,128)(2,1)S(1)} collective-permute-done((bf16[1024,128]{1,0:T(8,128)(2,1)S(1)}, bf16[1024,128]{1,0:T(8,128)(2,1)S(1)}, u32[]{:S(2)}, u32[]{:S(2)}) %collective-permute-start.3) | collective-permute-done | bytes 262176 | tf_op jit(solution)/shard_map/ppermute | solution.py:564
  32.4 0.0 collective-permute-start.10
  32.4 9.4 %collective-permute-done.4.refs_2_ = bf16[1024,128]{1,0:T(8,128)(2,1)S(1)} collective-permute-done((bf16[1024,128]{1,0:T(8,128)(2,1)S(1)}, bf16[1024,128]{1,0:T(8,128)(2,1)S(1)}, u32[]{:S(2)}, u32[]{:S(2)}) %collective-permute-start.4) | collective-permute-done | bytes 262176 | tf_op jit(solution)/shard_map/ppermute | solution.py:564
  41.8 3.5 %collective-permute-start.11 = (bf16[512,128]{1,0:T(8,128)(2,1)S(1)}, bf16[512,128]{1,0:T(8,128)(2,1)S(1)}, u32[]{:S(2)}, u32[]{:S(2)}) collective-permute-start(bf16[512,128]{1,0:T(8,128)(2,1)S(1)} %get-tuple-element.72), channel_id=1, source_target_pairs={{0,12},{4,8},{8,4},{12,0},{1,13},{5,9},{9,5},{13,1},{2,14},{6,10},... | collective-permute-start | bytes 393224 | tf_op jit(solution)/shard_map/ppermute | solution.py:564
  45.3 0.0 collective-permute-done.5.refs_3_
  45.3 0.0 collective-permute-done.12.refs_5_.refs_9_
  45.3 6.5 %shard_map.100 = (bf16[512,128]{1,0:T(8,128)(2,1)S(1)}, bf16[512,128]{1,0:T(8,128)(2,1)S(1)}, bf16[512,128]{1,0:T(8,128)(2,1)S(1)}, bf16[512,128]{1,0:T(8,128)(2...) custom-call(s32[4]{0:T(128)S(1)} %pad_add_fusion.place_ref.refs_0_, ...), custom_call_target="tpu_custom_call" | custom-call | flops 8049999872 | bytes 1048576 | tf_op jit(solution)/shard_map/pallas_call | solution.py:544
  51.8 10.4 %collective-permute-start.14 = (bf16[512,128]{1,0:T(8,128)(2,1)S(1)}, bf16[512,128]{1,0:T(8,128)(2,1)S(1)}, u32[]{:S(2)}, u32[]{:S(2)}) collective-permute-start(bf16[512,128]{1,0:T(8,128)(2,1)S(1)} %get-tuple-element.87), channel_id=1, source_target_pairs={{0,8},{4,12},{8,0},{12,4},{1,9},{5,13},{9,1},{13,5},{2,10},{6,14},... | collective-permute-start | bytes 393224 | tf_op jit(solution)/shard_map/ppermute | solution.py:564
  62.2 0.0 collective-permute-start.24
  62.2 0.0 collective-permute-done.9.refs_5_
  62.2 1.3 %collective-permute-start.25 = (bf16[512,128]{1,0:T(8,128)(2,1)S(1)}, bf16[512,128]{1,0:T(8,128)(2,1)S(1)}, u32[]{:S(2)}, u32[]{:S(2)}) collective-permute-start(bf16[512,128]{1,0:T(8,128)(2,1)S(1)} %get-tuple-element.99), channel_id=1, source_target_pairs={{0,12},{4,8},{8,4},{12,0},{1,13},{5,9},{9,5},{13,1},{2,14},{6,10},... | collective-permute-start | bytes 393224 | tf_op jit(solution)/shard_map/ppermute | solution.py:564
  63.5 0.0 collective-permute-done.10.refs_6_
  63.5 0.0 collective-permute-done.11.refs_7_
  63.5 7.0 %shard_map.101 = (bf16[1024,128]{1,0:T(8,128)(2,1)S(1)}, bf16[1024,128]{1,0:T(8,128)(2,1)S(1)}, bf16[1024,128]{1,0:T(8,128)(2,1)S(1)}, bf16[1024,128]{1,0:T(8,12...) custom-call(s32[4]{0:T(128)S(1)} %pad_add_fusion.place_ref.refs_0_, ...), custom_call_target="tpu_custom_call" | custom-call | flops 11500000256 | bytes 1048576 | tf_op jit(solution)/shard_map/pallas_call | solution.py:544
  70.5 0.0 collective-permute-done.14.refs_3_.refs_10_
  70.5 2.1 %collective-permute-start.15 = (bf16[1024,128]{1,0:T(8,128)(2,1)S(1)}, bf16[1024,128]{1,0:T(8,128)(2,1)S(1)}, u32[]{:S(2)}, u32[]{:S(2)}) collective-permute-start(bf16[1024,128]{1,0:T(8,128)(2,1)S(1)} %get-tuple-element.88), channel_id=1, source_target_pairs={{0,12},{4,8},{8,4},{12,0},{1,13},{5,9},{9,5},{13,1},{2,14},{6,10},... | collective-permute-start | bytes 786440 | tf_op jit(solution)/shard_map/ppermute | solution.py:564
  72.6 0.0 collective-permute-start.19
  72.6 1.5 %collective-permute-start.13 = (bf16[4,288,128]{2,1,0:T(8,128)(2,1)S(1)}, bf16[4,288,128]{2,1,0:T(8,128)(2,1)S(1)}, u32[]{:S(2)}, u32[]{:S(2)}) collective-permute-start(bf16[4,288,128]{2,1,0:T(8,128)(2,1)S(1)} %get-tuple-element.78), channel_id=1, source_target_pairs={{0,1},{1,0},{2,3},{3,2},{4,5},{5,4},{6,7},{7,6},{8,9},{9,8},{10,11... | collective-permute-start | bytes 884744 | tf_op jit(solution)/shard_map/ppermute | solution.py:570
  74.1 0.0 collective-permute-done.24.refs_2_.refs_9_
  74.1 0.6 shard_map.104
  74.7 0.1 collective-permute-start.26
  74.8 2.6 %collective-permute-start.20 = (bf16[1024,128]{1,0:T(8,128)(2,1)S(1)}, bf16[1024,128]{1,0:T(8,128)(2,1)S(1)}, u32[]{:S(2)}, u32[]{:S(2)}) collective-permute-start(bf16[1024,128]{1,0:T(8,128)(2,1)S(1)} %get-tuple-element.96), channel_id=1, source_target_pairs={{0,8},{4,12},{8,0},{12,4},{1,9},{5,13},{9,1},{13,5},{2,10},{6,14},... | collective-permute-start | bytes 786440 | tf_op jit(solution)/shard_map/ppermute | solution.py:564
  77.4 0.9 collective-permute-done.15.refs_3_
  78.3 5.4 %collective-permute-start.21 = (bf16[1024,128]{1,0:T(8,128)(2,1)S(1)}, bf16[1024,128]{1,0:T(8,128)(2,1)S(1)}, u32[]{:S(2)}, u32[]{:S(2)}) collective-permute-start(bf16[1024,128]{1,0:T(8,128)(2,1)S(1)} %get-tuple-element.94.refs_0_), channel_id=1, source_target_pairs={{0,1},{1,0},{2,3},{3,2},{4,5},{5,4},{6,7},{7,6},{8,9},{9,8},{10,11... | collective-permute-start | bytes 786440 | tf_op jit(solution)/shard_map/ppermute | solution.py:570
  83.7 2.6 %collective-permute-done.19.refs_1_ = bf16[1024,128]{1,0:T(8,128)(2,1)S(1)} collective-permute-done((bf16[1024,128]{1,0:T(8,128)(2,1)S(1)}, bf16[1024,128]{1,0:T(8,128)(2,1)S(1)}, u32[]{:S(2)}, u32[]{:S(2)}) %collective-permute-start.19) | collective-permute-done | bytes 262176 | tf_op jit(solution)/shard_map/ppermute | solution.py:564
  86.3 0.5 collective-permute-start.23
  86.8 0.0 collective-permute-start.22
  86.8 0.6 shard_map.102
  87.4 9.5 %collective-permute-done.20.refs_2_ = bf16[1024,128]{1,0:T(8,128)(2,1)S(1)} collective-permute-done((bf16[1024,128]{1,0:T(8,128)(2,1)S(1)}, bf16[1024,128]{1,0:T(8,128)(2,1)S(1)}, u32[]{:S(2)}, u32[]{:S(2)}) %collective-permute-start.20) | collective-permute-done | bytes 262176 | tf_op jit(solution)/shard_map/ppermute | solution.py:564
  96.9 0.0 collective-permute-done.26.refs_12_
  97.0 0.7 collective-permute-start.27
  97.7 1.1 collective-permute-start.17
  98.8 2.4 %collective-permute-start.18 = (bf16[576,128]{1,0:T(8,128)(2,1)S(1)}, bf16[576,128]{1,0:T(8,128)(2,1)S(1)}, u32[]{:S(2)}, u32[]{:S(2)}) collective-permute-start(bf16[576,128]{1,0:T(8,128)(2,1)S(1)} %get-tuple-element.92), channel_id=1, source_target_pairs={{0,12},{4,8},{8,4},{12,0},{1,13},{5,9},{9,5},{13,1},{2,14},{6,10},... | collective-permute-start | bytes 442376 | tf_op jit(solution)/shard_map/ppermute | solution.py:564
  101.2 0.0 collective-permute-done.27.refs_6_
  101.3 2.9 %shard_map.105 = bf16[256,1024]{1,0:T(8,128)(2,1)S(1)} custom-call(s32[4]{0:T(128)S(1)} %pad_add_fusion.place_ref.refs_0_, bf16[1024,128]{1,0:T(8,128)(2,1)S(1)} %get-tuple-element.94.refs_0_, bf16[1024,128]{1,0:T(8,128)(2,1)S(1)} %collective-permute-done.19.refs_1_, bf16[1024,128]{1,0:T(8,128)(2,1)S(1)} %collective-permute-done.20.refs_2_, ...), custom_call_target="tpu_custom_call" | custom-call | flops 1150000000 | bytes 1048576 | tf_op jit(solution)/shard_map/pallas_call | solution.py:544
  104.2 1.2 %collective-permute-start.28 = (bf16[256,1024]{1,0:T(8,128)(2,1)S(1)}, bf16[256,1024]{1,0:T(8,128)(2,1)S(1)}, u32[]{:S(2)}, u32[]{:S(2)}) collective-permute-start(bf16[256,1024]{1,0:T(8,128)(2,1)S(1)} %shard_map.105), channel_id=1, source_target_pairs={{0,1},{1,3},{3,2},{2,0},{4,5},{5,7},{7,6},{6,4},{8,9},{9,11},{11,1... | collective-permute-start | bytes 1572872 | tf_op jit(solution)/shard_map/ppermute | solution.py:711
  105.4 2.9 %shard_map.106.kept_ref = bf16[256,1024]{1,0:T(8,128)(2,1)S(1)} custom-call(s32[4]{0:T(128)S(1)} %pad_add_fusion.place_ref.refs_0_, bf16[1024,128]{1,0:T(8,128)(2,1)S(1)} %get-tuple-element.94.refs_0_, bf16[1024,128]{1,0:T(8,128)(2,1)S(1)} %collective-permute-done.19.refs_1_, bf16[1024,128]{1,0:T(8,128)(2,1)S(1)} %collective-permute-done.20.refs_2_, ...), custom_call_target="tpu_custom_call" | custom-call | flops 1150000000 | bytes 1048576 | tf_op jit(solution)/shard_map/pallas_call | solution.py:544
  108.3 3.2 %collective-permute-start.29 = (bf16[256,1024]{1,0:T(8,128)(2,1)S(1)}, bf16[256,1024]{1,0:T(8,128)(2,1)S(1)}, u32[]{:S(2)}, u32[]{:S(2)}) collective-permute-start(bf16[256,1024]{1,0:T(8,128)(2,1)S(1)} %shard_map.106.kept_ref), channel_id=1, source_target_pairs={{1,2},{2,1},{5,6},{6,5},{9,10},{10,9},{13,14},{14,13},{17,18},{18,... | collective-permute-start | bytes 1572872 | tf_op jit(solution)/shard_map/ppermute | solution.py:713
  111.5 0.0 collective-permute-done.16.refs_1_
  111.6 0.0 collective-permute-done.18.refs_3_
  111.6 1.5 %shard_map.103 = (bf16[256,1024]{1,0:T(8,128)(2,1)}, f32[8,32,128]{2,1,0:T(8,128)}) custom-call(s32[4]{0:T(128)S(1)} %pad_add_fusion.place_ref.refs_0_, bf16[576,128]{1,0:T(8,128)(2,1)S(1)} %get-tuple-element.89.refs_0_, bf16[576,128]{1,0:T(8,128)(2,1)S(1)} %collective-permute-done.16.refs_1_, bf16[576,128]{1,0:T(8,128)(2,1)S(1)} %collective-permute-done.17.refs_2_, ...), custom_call_target="tpu_custom_call" | custom-call | flops 23000000512 | bytes 1048576 | tf_op jit(solution)/shard_map/pallas_call | solution.py:544
  113.1 6.1 %collective-permute-done.29.second_ref = bf16[256,1024]{1,0:T(8,128)(2,1)S(1)} collective-permute-done((bf16[256,1024]{1,0:T(8,128)(2,1)S(1)}, bf16[256,1024]{1,0:T(8,128)(2,1)S(1)}, u32[]{:S(2)}, u32[]{:S(2)}) %collective-permute-start.29) | collective-permute-done | bytes 524320 | tf_op jit(solution)/shard_map/ppermute | solution.py:713
  119.2 1.5 %shard_map.107 = bf16[256,1024]{1,0:T(8,128)(2,1)} custom-call(s32[4]{0:T(128)S(1)} %pad_add_fusion.place_ref.refs_0_, bf16[256,1024]{1,0:T(8,128)(2,1)S(1)} %collective-permute-done.28.first_ref, bf16[256,1024]{1,0:T(8,128)(2,1)S(1)} %collective-permute-done.29.second_ref, bf16[256,1024]{1,0:T(8,128)(2,1)S(1)} %shard_map.106.kept_ref), custom_call_target="tpu_custom_call" | custom-call | flops 1150000000 | bytes 1048576 | tf_op jit(solution)/shard_map/pallas_call | solution.py:544
  (19 shorter events, 0.0 us)
Async XLA Ops:
  0.6 4.6 %collective-permute-start.1 = (bf16[256,2048]{1,0:T(8,128)(2,1)}, bf16[256,2048]{1,0:T(8,128)(2,1)S(1)}, u32[]{:S(2)}, u32[]{:S(2)}) collective-permute-start(bf16[256,2048]{1,0:T(8,128)(2,1)} %refs_1_.5), channel_id=1, source_target_pairs={{0,1},{1,0},{2,3},{3,2},{4,5},{5,4},{6,7},{7,6},{8,9},{9,8},{10,11... | collective-permute-start | bytes 3145736 | tf_op jit(solution)/shard_map/ppermute | solution.py:570
  2.5 2.6 %collective-permute-start = (bf16[4,272,128]{2,1,0:T(8,128)(2,1)S(1)}, bf16[4,272,128]{2,1,0:T(8,128)(2,1)S(1)}, u32[]{:S(2)}, u32[]{:S(2)}) collective-permute-start(bf16[4,272,128]{2,1,0:T(8,128)(2,1)S(1)} %get-tuple-element.55), channel_id=1, source_target_pairs={{0,1},{1,0},{2,3},{3,2},{4,5},{5,4},{6,7},{7,6},{8,9},{9,8},{10,11... | collective-permute-start | bytes 835592 | tf_op jit(solution)/shard_map/ppermute | solution.py:570
  8.1 5.0 %collective-permute-start.2 = (bf16[2,512,512]{2,1,0:T(8,128)(2,1)S(1)}, bf16[2,512,512]{2,1,0:T(8,128)(2,1)S(1)}, u32[]{:S(2)}, u32[]{:S(2)}) collective-permute-start(bf16[2,512,512]{2,1,0:T(8,128)(2,1)S(1)} %get-tuple-element.56), channel_id=1, source_target_pairs={{0,1},{1,0},{2,3},{3,2},{4,5},{5,4},{6,7},{7,6},{8,9},{9,8},{10,11... | collective-permute-start | bytes 3145736 | tf_op jit(solution)/shard_map/ppermute | solution.py:570
  8.2 14.4 %collective-permute-start.7 = (bf16[544,128]{1,0:T(8,128)(2,1)S(1)}, bf16[544,128]{1,0:T(8,128)(2,1)S(1)}, u32[]{:S(2)}, u32[]{:S(2)}) collective-permute-start(bf16[544,128]{1,0:T(8,128)(2,1)S(1)} %get-tuple-element.62), channel_id=1, source_target_pairs={{0,8},{4,12},{8,0},{12,4},{1,9},{5,13},{9,1},{13,5},{2,10},{6,14},... | collective-permute-start | bytes 417800 | tf_op jit(solution)/shard_map/ppermute | solution.py:564
  12.0 13.4 %collective-permute-start.8 = (bf16[544,128]{1,0:T(8,128)(2,1)S(1)}, bf16[544,128]{1,0:T(8,128)(2,1)S(1)}, u32[]{:S(2)}, u32[]{:S(2)}) collective-permute-start(bf16[544,128]{1,0:T(8,128)(2,1)S(1)} %get-tuple-element.63), channel_id=1, source_target_pairs={{0,12},{4,8},{8,4},{12,0},{1,13},{5,9},{9,5},{13,1},{2,14},{6,10},... | collective-permute-start | bytes 417800 | tf_op jit(solution)/shard_map/ppermute | solution.py:564
  15.7 9.8 %collective-permute-start.6 = (bf16[1,512,512]{2,1,0:T(8,128)(2,1)S(1)}, bf16[1,512,512]{2,1,0:T(8,128)(2,1)S(1)}, u32[]{:S(2)}, u32[]{:S(2)}) collective-permute-start(bf16[1,512,512]{2,1,0:T(8,128)(2,1)S(1)} %shard_map.98), channel_id=1, source_target_pairs={{0,1},{1,0},{2,3},{3,2},{4,5},{5,4},{6,7},{7,6},{8,9},{9,8},{10,11... | collective-permute-start | bytes 1572872 | tf_op jit(solution)/shard_map/ppermute | solution.py:570
  20.0 12.4 %collective-permute-start.3 = (bf16[1024,128]{1,0:T(8,128)(2,1)S(1)}, bf16[1024,128]{1,0:T(8,128)(2,1)S(1)}, u32[]{:S(2)}, u32[]{:S(2)}) collective-permute-start(bf16[1024,128]{1,0:T(8,128)(2,1)S(1)} %get-tuple-element.58), channel_id=1, source_target_pairs={{0,4},{4,0},{8,12},{12,8},{1,5},{5,1},{9,13},{13,9},{2,6},{6,2},{1... | collective-permute-start | bytes 786440 | tf_op jit(solution)/shard_map/ppermute | solution.py:564
  20.1 21.7 %collective-permute-start.4 = (bf16[1024,128]{1,0:T(8,128)(2,1)S(1)}, bf16[1024,128]{1,0:T(8,128)(2,1)S(1)}, u32[]{:S(2)}, u32[]{:S(2)}) collective-permute-start(bf16[1024,128]{1,0:T(8,128)(2,1)S(1)} %get-tuple-element.59), channel_id=1, source_target_pairs={{0,8},{4,12},{8,0},{12,4},{1,9},{5,13},{9,1},{13,5},{2,10},{6,14},... | collective-permute-start | bytes 786440 | tf_op jit(solution)/shard_map/ppermute | solution.py:564
  22.6 22.8 %collective-permute-start.5 = (bf16[1024,128]{1,0:T(8,128)(2,1)S(1)}, bf16[1024,128]{1,0:T(8,128)(2,1)S(1)}, u32[]{:S(2)}, u32[]{:S(2)}) collective-permute-start(bf16[1024,128]{1,0:T(8,128)(2,1)S(1)} %get-tuple-element.60), channel_id=1, source_target_pairs={{0,12},{4,8},{8,4},{12,0},{1,13},{5,9},{9,5},{13,1},{2,14},{6,10},... | collective-permute-start | bytes 786440 | tf_op jit(solution)/shard_map/ppermute | solution.py:564
  25.4 19.9 %copy-start.3 = (s32[256]{0:T(256)S(1)}, s32[256]{0:T(256)}, u32[]{:S(2)}) copy-start(s32[256]{0:T(256)} %param.11) | copy-start | bytes 3076
  25.4 19.9 %collective-permute-start.12 = (bf16[544,128]{1,0:T(8,128)(2,1)S(1)}, bf16[544,128]{1,0:T(8,128)(2,1)S(1)}, u32[]{:S(2)}, u32[]{:S(2)}) collective-permute-start(bf16[544,128]{1,0:T(8,128)(2,1)S(1)} %get-tuple-element.74), channel_id=1, source_target_pairs={{0,4},{4,0},{8,12},{12,8},{1,5},{5,1},{9,13},{13,9},{2,6},{6,2},{1... | collective-permute-start | bytes 417800 | tf_op jit(solution)/shard_map/ppermute | solution.py:564
  28.4 33.8 %collective-permute-start.9 = (bf16[512,128]{1,0:T(8,128)(2,1)S(1)}, bf16[512,128]{1,0:T(8,128)(2,1)S(1)}, u32[]{:S(2)}, u32[]{:S(2)}) collective-permute-start(bf16[512,128]{1,0:T(8,128)(2,1)S(1)} %get-tuple-element.70), channel_id=1, source_target_pairs={{0,4},{4,0},{8,12},{12,8},{1,5},{5,1},{9,13},{13,9},{2,6},{6,2},{1... | collective-permute-start | bytes 393224 | tf_op jit(solution)/shard_map/ppermute | solution.py:564
  32.4 31.0 %collective-permute-start.10 = (bf16[512,128]{1,0:T(8,128)(2,1)S(1)}, bf16[512,128]{1,0:T(8,128)(2,1)S(1)}, u32[]{:S(2)}, u32[]{:S(2)}) collective-permute-start(bf16[512,128]{1,0:T(8,128)(2,1)S(1)} %get-tuple-element.71), channel_id=1, source_target_pairs={{0,8},{4,12},{8,0},{12,4},{1,9},{5,13},{9,1},{13,5},{2,10},{6,14},... | collective-permute-start | bytes 393224 | tf_op jit(solution)/shard_map/ppermute | solution.py:564
  41.8 21.6 %collective-permute-start.11 = (bf16[512,128]{1,0:T(8,128)(2,1)S(1)}, bf16[512,128]{1,0:T(8,128)(2,1)S(1)}, u32[]{:S(2)}, u32[]{:S(2)}) collective-permute-start(bf16[512,128]{1,0:T(8,128)(2,1)S(1)} %get-tuple-element.72), channel_id=1, source_target_pairs={{0,12},{4,8},{8,4},{12,0},{1,13},{5,9},{9,5},{13,1},{2,14},{6,10},... | collective-permute-start | bytes 393224 | tf_op jit(solution)/shard_map/ppermute | solution.py:564
  51.8 18.7 %collective-permute-start.14 = (bf16[512,128]{1,0:T(8,128)(2,1)S(1)}, bf16[512,128]{1,0:T(8,128)(2,1)S(1)}, u32[]{:S(2)}, u32[]{:S(2)}) collective-permute-start(bf16[512,128]{1,0:T(8,128)(2,1)S(1)} %get-tuple-element.87), channel_id=1, source_target_pairs={{0,8},{4,12},{8,0},{12,4},{1,9},{5,13},{9,1},{13,5},{2,10},{6,14},... | collective-permute-start | bytes 393224 | tf_op jit(solution)/shard_map/ppermute | solution.py:564
  62.2 11.9 %collective-permute-start.24 = (bf16[512,128]{1,0:T(8,128)(2,1)S(1)}, bf16[512,128]{1,0:T(8,128)(2,1)S(1)}, u32[]{:S(2)}, u32[]{:S(2)}) collective-permute-start(bf16[512,128]{1,0:T(8,128)(2,1)S(1)} %get-tuple-element.98), channel_id=1, source_target_pairs={{0,4},{4,0},{8,12},{12,8},{1,5},{5,1},{9,13},{13,9},{2,6},{6,2},{1... | collective-permute-start | bytes 393224 | tf_op jit(solution)/shard_map/ppermute | solution.py:564
  62.2 11.9 %collective-permute-start.25 = (bf16[512,128]{1,0:T(8,128)(2,1)S(1)}, bf16[512,128]{1,0:T(8,128)(2,1)S(1)}, u32[]{:S(2)}, u32[]{:S(2)}) collective-permute-start(bf16[512,128]{1,0:T(8,128)(2,1)S(1)} %get-tuple-element.99), channel_id=1, source_target_pairs={{0,12},{4,8},{8,4},{12,0},{1,13},{5,9},{9,5},{13,1},{2,14},{6,10},... | collective-permute-start | bytes 393224 | tf_op jit(solution)/shard_map/ppermute | solution.py:564
  70.5 7.8 %collective-permute-start.15 = (bf16[1024,128]{1,0:T(8,128)(2,1)S(1)}, bf16[1024,128]{1,0:T(8,128)(2,1)S(1)}, u32[]{:S(2)}, u32[]{:S(2)}) collective-permute-start(bf16[1024,128]{1,0:T(8,128)(2,1)S(1)} %get-tuple-element.88), channel_id=1, source_target_pairs={{0,12},{4,8},{8,4},{12,0},{1,13},{5,9},{9,5},{13,1},{2,14},{6,10},... | collective-permute-start | bytes 786440 | tf_op jit(solution)/shard_map/ppermute | solution.py:564
  72.6 13.7 %collective-permute-start.19 = (bf16[1024,128]{1,0:T(8,128)(2,1)S(1)}, bf16[1024,128]{1,0:T(8,128)(2,1)S(1)}, u32[]{:S(2)}, u32[]{:S(2)}) collective-permute-start(bf16[1024,128]{1,0:T(8,128)(2,1)S(1)} %get-tuple-element.95), channel_id=1, source_target_pairs={{0,4},{4,0},{8,12},{12,8},{1,5},{5,1},{9,13},{13,9},{2,6},{6,2},{1... | collective-permute-start | bytes 786440 | tf_op jit(solution)/shard_map/ppermute | solution.py:564
  72.6 14.2 %collective-permute-start.13 = (bf16[4,288,128]{2,1,0:T(8,128)(2,1)S(1)}, bf16[4,288,128]{2,1,0:T(8,128)(2,1)S(1)}, u32[]{:S(2)}, u32[]{:S(2)}) collective-permute-start(bf16[4,288,128]{2,1,0:T(8,128)(2,1)S(1)} %get-tuple-element.78), channel_id=1, source_target_pairs={{0,1},{1,0},{2,3},{3,2},{4,5},{5,4},{6,7},{7,6},{8,9},{9,8},{10,11... | collective-permute-start | bytes 884744 | tf_op jit(solution)/shard_map/ppermute | solution.py:570
  74.1 27.1 %copy-start.2 = (bf16[1024,1024]{1,0:T(8,128)(2,1)S(1)}, bf16[1024,1024]{1,0:T(8,128)(2,1)}, u32[]{:S(2)}) copy-start(bf16[1024,1024]{1,0:T(8,128)(2,1)} %refs_14_.3) | copy-start | bytes 6291460
  74.7 22.2 %collective-permute-start.26 = (bf16[4,512,128]{2,1,0:T(8,128)(2,1)S(1)}, bf16[4,512,128]{2,1,0:T(8,128)(2,1)S(1)}, u32[]{:S(2)}, u32[]{:S(2)}) collective-permute-start(bf16[4,512,128]{2,1,0:T(8,128)(2,1)S(1)} %shard_map.104), channel_id=1, source_target_pairs={{0,1},{1,0},{2,3},{3,2},{4,5},{5,4},{6,7},{7,6},{8,9},{9,8},{10,11... | collective-permute-start | bytes 1572872 | tf_op jit(solution)/shard_map/ppermute | solution.py:570
  74.8 22.1 %collective-permute-start.20 = (bf16[1024,128]{1,0:T(8,128)(2,1)S(1)}, bf16[1024,128]{1,0:T(8,128)(2,1)S(1)}, u32[]{:S(2)}, u32[]{:S(2)}) collective-permute-start(bf16[1024,128]{1,0:T(8,128)(2,1)S(1)} %get-tuple-element.96), channel_id=1, source_target_pairs={{0,8},{4,12},{8,0},{12,4},{1,9},{5,13},{9,1},{13,5},{2,10},{6,14},... | collective-permute-start | bytes 786440 | tf_op jit(solution)/shard_map/ppermute | solution.py:564
  78.3 18.7 %collective-permute-start.21 = (bf16[1024,128]{1,0:T(8,128)(2,1)S(1)}, bf16[1024,128]{1,0:T(8,128)(2,1)S(1)}, u32[]{:S(2)}, u32[]{:S(2)}) collective-permute-start(bf16[1024,128]{1,0:T(8,128)(2,1)S(1)} %get-tuple-element.94.refs_0_), channel_id=1, source_target_pairs={{0,1},{1,0},{2,3},{3,2},{4,5},{5,4},{6,7},{7,6},{8,9},{9,8},{10,11... | collective-permute-start | bytes 786440 | tf_op jit(solution)/shard_map/ppermute | solution.py:570
  86.3 10.6 %collective-permute-start.23 = (bf16[1024,128]{1,0:T(8,128)(2,1)S(1)}, bf16[1024,128]{1,0:T(8,128)(2,1)S(1)}, u32[]{:S(2)}, u32[]{:S(2)}) collective-permute-start(bf16[1024,128]{1,0:T(8,128)(2,1)S(1)} %collective-permute-done.15.refs_3_), channel_id=1, source_target_pairs={{0,1},{1,0},{2,3},{3,2},{4,5},{5,4},{6,7},{7,6},{8,9},{9,8},{10,11... | collective-permute-start | bytes 786440 | tf_op jit(solution)/shard_map/ppermute | solution.py:570
  86.8 10.1 %collective-permute-start.22 = (bf16[1024,128]{1,0:T(8,128)(2,1)S(1)}, bf16[1024,128]{1,0:T(8,128)(2,1)S(1)}, u32[]{:S(2)}, u32[]{:S(2)}) collective-permute-start(bf16[1024,128]{1,0:T(8,128)(2,1)S(1)} %collective-permute-done.19.refs_1_), channel_id=1, source_target_pairs={{0,1},{1,0},{2,3},{3,2},{4,5},{5,4},{6,7},{7,6},{8,9},{9,8},{10,11... | collective-permute-start | bytes 786440 | tf_op jit(solution)/shard_map/ppermute | solution.py:570
  86.8 14.4 %copy-start = (bf16[1024,1024]{1,0:T(8,128)(2,1)S(1)}, bf16[1024,1024]{1,0:T(8,128)(2,1)}, u32[]{:S(2)}) copy-start(bf16[1024,1024]{1,0:T(8,128)(2,1)} %refs_15_.3) | copy-start | bytes 6291460
  86.8 14.4 %copy-start.1 = (bf16[1024,1024]{1,0:T(8,128)(2,1)S(1)}, bf16[1024,1024]{1,0:T(8,128)(2,1)}, u32[]{:S(2)}) copy-start(bf16[1024,1024]{1,0:T(8,128)(2,1)} %refs_13_.3) | copy-start | bytes 6291460
  97.0 4.3 %collective-permute-start.27 = (bf16[1024,128]{1,0:T(8,128)(2,1)S(1)}, bf16[1024,128]{1,0:T(8,128)(2,1)S(1)}, u32[]{:S(2)}, u32[]{:S(2)}) collective-permute-start(bf16[1024,128]{1,0:T(8,128)(2,1)S(1)} %collective-permute-done.20.refs_2_), channel_id=1, source_target_pairs={{0,1},{1,0},{2,3},{3,2},{4,5},{5,4},{6,7},{7,6},{8,9},{9,8},{10,11... | collective-permute-start | bytes 786440 | tf_op jit(solution)/shard_map/ppermute | solution.py:570
  97.7 13.9 %collective-permute-start.16 = (bf16[576,128]{1,0:T(8,128)(2,1)S(1)}, bf16[576,128]{1,0:T(8,128)(2,1)S(1)}, u32[]{:S(2)}, u32[]{:S(2)}) collective-permute-start(bf16[576,128]{1,0:T(8,128)(2,1)S(1)} %get-tuple-element.90), channel_id=1, source_target_pairs={{0,4},{4,0},{8,12},{12,8},{1,5},{5,1},{9,13},{13,9},{2,6},{6,2},{1... | collective-permute-start | bytes 442376 | tf_op jit(solution)/shard_map/ppermute | solution.py:564
  97.7 13.9 %collective-permute-start.17 = (bf16[576,128]{1,0:T(8,128)(2,1)S(1)}, bf16[576,128]{1,0:T(8,128)(2,1)S(1)}, u32[]{:S(2)}, u32[]{:S(2)}) collective-permute-start(bf16[576,128]{1,0:T(8,128)(2,1)S(1)} %get-tuple-element.91), channel_id=1, source_target_pairs={{0,8},{4,12},{8,0},{12,4},{1,9},{5,13},{9,1},{13,5},{2,10},{6,14},... | collective-permute-start | bytes 442376 | tf_op jit(solution)/shard_map/ppermute | solution.py:564
  98.8 12.7 %collective-permute-start.18 = (bf16[576,128]{1,0:T(8,128)(2,1)S(1)}, bf16[576,128]{1,0:T(8,128)(2,1)S(1)}, u32[]{:S(2)}, u32[]{:S(2)}) collective-permute-start(bf16[576,128]{1,0:T(8,128)(2,1)S(1)} %get-tuple-element.92), channel_id=1, source_target_pairs={{0,12},{4,8},{8,4},{12,0},{1,13},{5,9},{9,5},{13,1},{2,14},{6,10},... | collective-permute-start | bytes 442376 | tf_op jit(solution)/shard_map/ppermute | solution.py:564
  104.2 15.0 %collective-permute-start.28 = (bf16[256,1024]{1,0:T(8,128)(2,1)S(1)}, bf16[256,1024]{1,0:T(8,128)(2,1)S(1)}, u32[]{:S(2)}, u32[]{:S(2)}) collective-permute-start(bf16[256,1024]{1,0:T(8,128)(2,1)S(1)} %shard_map.105), channel_id=1, source_target_pairs={{0,1},{1,3},{3,2},{2,0},{4,5},{5,7},{7,6},{6,4},{8,9},{9,11},{11,1... | collective-permute-start | bytes 1572872 | tf_op jit(solution)/shard_map/ppermute | solution.py:711
  108.3 10.9 %collective-permute-start.29 = (bf16[256,1024]{1,0:T(8,128)(2,1)S(1)}, bf16[256,1024]{1,0:T(8,128)(2,1)S(1)}, u32[]{:S(2)}, u32[]{:S(2)}) collective-permute-start(bf16[256,1024]{1,0:T(8,128)(2,1)S(1)} %shard_map.106.kept_ref), channel_id=1, source_target_pairs={{1,2},{2,1},{5,6},{6,5},{9,10},{10,9},{13,14},{14,13},{17,18},{18,... | collective-permute-start | bytes 1572872 | tf_op jit(solution)/shard_map/ppermute | solution.py:713

commit v17 on v14

--- a/solution.py
+++ b/solution.py
@@ -220,10 +220,13 @@
         for chip in range(chips):
             head = (place_ref[1] ^ turn) * chips + chip
             ids = ids_ref[pl.ds(head, 1), :].astype(jnp.float32)
-            lines = [
-                ids[:, start : start + head_dim] for start in range(0, rows, head_dim)
-            ] + [jnp.zeros((spare, head_dim), jnp.float32)]
-            out_ref[chip, rows:, :] = jnp.concatenate(lines, axis=0).astype(jnp.bfloat16)
+            lines = [ids[:, start : start + head_dim] for start in range(0, rows, head_dim)]
+            gap = [jnp.zeros((len(lines), head_dim), jnp.float32)]
+            rest = [jnp.zeros((spare - len(lines), head_dim), jnp.float32)]
+            first = jnp.concatenate(lines + gap + rest, axis=0)
+            second = jnp.concatenate(gap + lines + rest, axis=0)
+            tile = jnp.where(place_ref[1] == 0, first, second)
+            out_ref[chip, rows:, :] = tile.astype(jnp.bfloat16)
     for copy in copies[1:]:
         copy.wait()
 
@@ -234,6 +237,16 @@
         at = pl.ds(pl.multiple_of((place_ref[1] ^ turn) * height, height), height)
         for offset, out_ref in enumerate(out_refs):
             out_ref[at, :] = held_ref[place_ref[0] ^ offset]
+
+
+def merge_grads(place_ref, mine_ref, theirs_ref, out_refs):
+    rows = out_refs[0].shape[0] - mine_ref.shape[1]
+    for offset, out_ref in enumerate(out_refs):
+        chip = place_ref[0] ^ offset
+        for turn, held_ref in enumerate((mine_ref, theirs_ref)):
+            at = pl.ds(pl.multiple_of((place_ref[1] ^ turn) * rows, rows), rows)
+            out_ref[at, :] = held_ref[chip, :rows, :]
+        out_ref[2 * rows :, :] = mine_ref[chip, rows:, :] + theirs_ref[chip, rows:, :]
 
 
 def fetch_columns(half, weights, held_ref, sems):
@@ -305,7 +318,7 @@
         at = pl.ds(pl.multiple_of((side ^ core) * rows, rows), rows)
         joins.append(pltpu.make_async_copy(source.at[:, near], joined_ref.at[at], sems.at[core]))
         joins[core].start()
-    merge_kernel(place_ref, mine_ref, theirs_ref, *out_refs)
+    merge_grads(place_ref, mine_ref, theirs_ref, out_refs)
     for copy in joins:
         copy.wait()
     for index in range(held_ref.shape[0]):
@@ -322,27 +335,25 @@
 
 def order_grads(place, parts, rows, grad_rows, id_rows, id_cols):
     head_dim = grad_rows.shape[1]
-    height = parts[0].shape[0] // 2
+    count = rows // head_dim
     for offset, part in enumerate(parts):
+        lines = part[2 * rows :, :].astype(jnp.float32)
         for core in range(2):
             block = (place ^ offset) * 2 + core
             at = pl.ds(pl.multiple_of(block * rows, rows), rows)
-            start = core * height
-            grad_rows[at, :] = part[start : start + rows, :]
-            lines = part[start + rows : start + rows + 16, :].astype(jnp.float32)
+            grad_rows[at, :] = part[core * rows : (core + 1) * rows, :]
+            first = core * count
             ids = jnp.concatenate(
-                [lines[line : line + 1, :] for line in range(rows // head_dim)], axis=1
+                [lines[line : line + 1, :] for line in range(first, first + count)], axis=1
             )
             id_rows[block] = jnp.broadcast_to(ids, id_rows.shape[1:])
             id_cols[at, :] = jnp.broadcast_to(ids, (head_dim, rows)).T
 
 
 def order_rows(place, parts, rows, ordered):
-    height = parts[0].shape[0] // 2
     for offset, part in enumerate(parts):
-        for core in range(2):
-            at = pl.ds(pl.multiple_of(((place ^ offset) * 2 + core) * rows, rows), rows)
-            ordered[at, :] = part[core * height : core * height + rows, :]
+        at = pl.ds(pl.multiple_of((place ^ offset) * 2 * rows, 2 * rows), 2 * rows)
+        ordered[at, :] = part[: 2 * rows, :]
 
 
 def block_scores(factor, block, rows, queries, keys_in, id_rows, id_cols):
@@ -573,7 +584,7 @@
         return pltpu.with_memory_space_constraint(array, pltpu.HBM)
 
     hidden_other = to_sibling(hidden)
-    block = low(chips, rows + id_lines(rows, head_dim), head_dim)
+    block = low(chips, rows + id_lines(2 * rows, head_dim), head_dim)
     grads_mine, grads_theirs = call(
         pack_kernel,
         (block, block),
@@ -620,7 +631,7 @@
     )
     *merged, early_part = call(
         opening_kernel,
-        (*buffers(2 * block.shape[1]), low(2, 2 * rows, width // 2)),
+        (*buffers(rows + block.shape[1]), low(2, 2 * rows, width // 2)),
         place,
         fetched,
         grads_mine,

time: 121 us -> 121 us (level)
  no operation moved by 1% of the time
where the time goes in v17:
time: 121 us; the launch traced here: 120 us
  starting transfers between devices  46.8 us (39%)
  Pallas kernels  39.3 us (32%)
  waiting for transfers between devices  33.2 us (27%)
    pallas_call x14, Pallas kernels, call(): pl.pallas_call(kernel, out_shape=outs, in_specs=[smem] + [vmem] * (len(op...  39.3 us
    ppermute x18, starting transfers between devices, exchange(): lax.ppermute(parts[offset], 'seq', [(at, at ^ offset) for at in range(chi...  33.7 us
    ppermute x18, waiting for transfers between devices, exchange(): lax.ppermute(parts[offset], 'seq', [(at, at ^ offset) for at in range(chi...  27.1 us
    ppermute x10, starting transfers between devices, to_sibling(): return lax.ppermute(piece, 'sub', swap)  8.72 us
    ppermute x1, waiting for transfers between devices, by_head(): second = lax.ppermute(kept, square, [(1, 2), (2, 1)])  6.1 us
    ppermute x1, starting transfers between devices, by_head(): second = lax.ppermute(kept, square, [(1, 2), (2, 1)])  3.18 us
  transfers between devices with their start and end apart: 30, of which 6 were waited for; matrix products, arithmetic and copies ran while one was open for 0% of the time, Pallas kernels for 29%

profile of v17, /device:TPU:1, one launch (start us, length us, event | category | flops | bytes accessed | tf_op | source)
XLA Modules:
  0.0 120.2 jit_solution(17556990322101292181)
XLA Ops:
  0.6 0.1 collective-permute-start.1
  0.8 0.1 pad_add_fusion.place_ref.refs_0_
  0.8 1.7 %shard_map.95 = (bf16[4,272,128]{2,1,0:T(8,128)(2,1)S(1)}, bf16[4,272,128]{2,1,0:T(8,128)(2,1)S(1)}) custom-call(s32[4]{0:T(128)S(1)} %pad_add_fusion.place_ref.refs_0_, bf16[256,1024]{1,0:T(8,128)(2,1)} %grads_ref.1, s32[8,256]{1,0:T(8,128)} %assign_ref.1), custom_call_target="tpu_custom_call" | custom-call | flops 1150000000 | bytes 1048576 | tf_op jit(solution)/shard_map/pallas_call | solution.py:555
  2.5 0.5 collective-permute-start
  3.1 2.1 %shard_map.94.held_ref = bf16[2,1024,512]{2,1,0:T(8,128)(2,1)S(1)} custom-call(s32[4]{0:T(128)S(1)} %pad_add_fusion.place_ref.refs_0_, bf16[1024,1024]{1,0:T(8,128)(2,1)} %refs_13_.3, bf16[1024,1024]{1,0:T(8,128)(2,1)} %refs_14_.3), custom_call_target="tpu_custom_call" | custom-call | flops 1150000000 | bytes 1048576 | tf_op jit(solution)/shard_map/pallas_call | solution.py:555
  5.2 0.0 collective-permute-done.theirs_ref
  5.2 2.9 %shard_map.96 = (bf16[528,128]{1,0:T(8,128)(2,1)S(1)}, bf16[528,128]{1,0:T(8,128)(2,1)S(1)}, bf16[528,128]{1,0:T(8,128)(2,1)S(1)}, bf16[528,128]{1,0:T(8,128)(2,1)S(1)}, bf16[2,512,512]{2,1,0:T(8,128)(2,1)S(1)}) custom-call(s32[4]{0:T(128)S(1)} %pad_add_fusion.place_ref.refs_0_, bf16[2,1024,512]{2,1,0:T(8,128)(2,1)S(1)} %shard_map.94.held_ref, ...), custom_call_target="tpu_custom_call" | custom-call | flops 115000000 | bytes 1048576 | tf_op jit(solution)/shard_map/pallas_call | solution.py:555
  8.1 0.1 collective-permute-start.2
  8.2 3.8 %collective-permute-start.7 = (bf16[528,128]{1,0:T(8,128)(2,1)S(1)}, bf16[528,128]{1,0:T(8,128)(2,1)S(1)}, u32[]{:S(2)}, u32[]{:S(2)}) collective-permute-start(bf16[528,128]{1,0:T(8,128)(2,1)S(1)} %get-tuple-element.62), channel_id=1, source_target_pairs={{0,8},{4,12},{8,0},{12,4},{1,9},{5,13},{9,1},{13,5},{2,10},{6,14},... | collective-permute-start | bytes 405512 | tf_op jit(solution)/shard_map/ppermute | solution.py:575
  12.0 1.1 collective-permute-start.8
  13.1 0.0 collective-permute-done.2.refs_0_
  13.1 2.7 %shard_map.98 = bf16[1,512,512]{2,1,0:T(8,128)(2,1)S(1)} custom-call(s32[4]{0:T(128)S(1)} %pad_add_fusion.place_ref.refs_0_, bf16[256,2048]{1,0:T(8,128)(2,1)} %refs_1_.5, bf16[256,2048]{1,0:T(8,128)(2,1)S(1)} %collective-permute-done.1.refs_1_.refs_2_, bf16[1024,1024]{1,0:T(8,128)(2,1)} %refs_15_.3), custom_call_target="tpu_custom_call" | custom-call | flops 115000000 | bytes 1048576 | tf_op jit(solution)/shard_map/pallas_call | solution.py:555
  15.7 0.7 collective-permute-start.6
  16.4 3.6 %shard_map.97 = (bf16[1024,128]{1,0:T(8,128)(2,1)S(1)}, bf16[1024,128]{1,0:T(8,128)(2,1)S(1)}, bf16[1024,128]{1,0:T(8,128)(2,1)S(1)}, bf16[1024,128]{1,0:T(8,128)(2,1)S(1)}) custom-call(s32[4]{0:T(128)S(1)} %pad_add_fusion.place_ref.refs_0_, bf16[2,512,512]{2,1,0:T(8,128)(2,1)S(1)} %collective-permute-done.2.refs_0_, bf16[256,2048]{1,0:T(8,128)(2,1)} %refs_1_.5, ...), custom_call_target="tpu_custom_call" | custom-call | flops 9200000000 | bytes 1048576 | tf_op jit(solution)/shard_map/pallas_call | solution.py:555
  20.0 0.1 collective-permute-start.3
  20.1 2.5 %collective-permute-start.4 = (bf16[1024,128]{1,0:T(8,128)(2,1)S(1)}, bf16[1024,128]{1,0:T(8,128)(2,1)S(1)}, u32[]{:S(2)}, u32[]{:S(2)}) collective-permute-start(bf16[1024,128]{1,0:T(8,128)(2,1)S(1)} %get-tuple-element.59), channel_id=1, source_target_pairs={{0,8},{4,12},{8,0},{12,4},{1,9},{5,13},{9,1},{13,5},{2,10},{6,14},... | collective-permute-start | bytes 786440 | tf_op jit(solution)/shard_map/ppermute | solution.py:575
  22.6 0.0 collective-permute-done.7.refs_6_.refs_10_
  22.6 2.6 %collective-permute-start.5 = (bf16[1024,128]{1,0:T(8,128)(2,1)S(1)}, bf16[1024,128]{1,0:T(8,128)(2,1)S(1)}, u32[]{:S(2)}, u32[]{:S(2)}) collective-permute-start(bf16[1024,128]{1,0:T(8,128)(2,1)S(1)} %get-tuple-element.60), channel_id=1, source_target_pairs={{0,12},{4,8},{8,4},{12,0},{1,13},{5,9},{9,5},{13,1},{2,14},{6,10},... | collective-permute-start | bytes 786440 | tf_op jit(solution)/shard_map/ppermute | solution.py:575
  25.1 0.0 collective-permute-done.8.refs_7_.refs_11_
  25.1 0.1 collective-permute-start.12
  25.2 0.0 collective-permute-done.6.refs_0_
  25.2 2.8 %shard_map.99 = (bf16[512,128]{1,0:T(8,128)(2,1)S(1)}, bf16[512,128]{1,0:T(8,128)(2,1)S(1)}, bf16[512,128]{1,0:T(8,128)(2,1)S(1)}, bf16[512,128]{1,0:T(8,128)(2,1)S(1)}) custom-call(s32[4]{0:T(128)S(1)} %pad_add_fusion.place_ref.refs_0_, bf16[1,512,512]{2,1,0:T(8,128)(2,1)S(1)} %collective-permute-done.6.refs_0_, bf16[256,2048]{1,0:T(8,128)(2,1)} %refs_1_.5, ...), custom_call_target="tpu_custom_call" | custom-call | flops 115000000 | bytes 1048576 | tf_op jit(solution)/shard_map/pallas_call | solution.py:555
  28.1 1.5 %collective-permute-start.9 = (bf16[512,128]{1,0:T(8,128)(2,1)S(1)}, bf16[512,128]{1,0:T(8,128)(2,1)S(1)}, u32[]{:S(2)}, u32[]{:S(2)}) collective-permute-start(bf16[512,128]{1,0:T(8,128)(2,1)S(1)} %get-tuple-element.70), channel_id=1, source_target_pairs={{0,4},{4,0},{8,12},{12,8},{1,5},{5,1},{9,13},{13,9},{2,6},{6,2},{1... | collective-permute-start | bytes 393224 | tf_op jit(solution)/shard_map/ppermute | solution.py:575
  29.5 3.2 %collective-permute-done.3.refs_1_ = bf16[1024,128]{1,0:T(8,128)(2,1)S(1)} collective-permute-done((bf16[1024,128]{1,0:T(8,128)(2,1)S(1)}, bf16[1024,128]{1,0:T(8,128)(2,1)S(1)}, u32[]{:S(2)}, u32[]{:S(2)}) %collective-permute-start.3) | collective-permute-done | bytes 262176 | tf_op jit(solution)/shard_map/ppermute | solution.py:575
  32.8 0.0 collective-permute-start.10
  32.8 8.7 %collective-permute-done.4.refs_2_ = bf16[1024,128]{1,0:T(8,128)(2,1)S(1)} collective-permute-done((bf16[1024,128]{1,0:T(8,128)(2,1)S(1)}, bf16[1024,128]{1,0:T(8,128)(2,1)S(1)}, u32[]{:S(2)}, u32[]{:S(2)}) %collective-permute-start.4) | collective-permute-done | bytes 262176 | tf_op jit(solution)/shard_map/ppermute | solution.py:575
  41.5 3.5 %collective-permute-start.11 = (bf16[512,128]{1,0:T(8,128)(2,1)S(1)}, bf16[512,128]{1,0:T(8,128)(2,1)S(1)}, u32[]{:S(2)}, u32[]{:S(2)}) collective-permute-start(bf16[512,128]{1,0:T(8,128)(2,1)S(1)} %get-tuple-element.72), channel_id=1, source_target_pairs={{0,12},{4,8},{8,4},{12,0},{1,13},{5,9},{9,5},{13,1},{2,14},{6,10},... | collective-permute-start | bytes 393224 | tf_op jit(solution)/shard_map/ppermute | solution.py:575
  45.0 0.0 collective-permute-done.5.refs_3_
  45.0 0.0 collective-permute-done.12.refs_5_.refs_9_
  45.0 6.5 %shard_map.100 = (bf16[512,128]{1,0:T(8,128)(2,1)S(1)}, bf16[512,128]{1,0:T(8,128)(2,1)S(1)}, bf16[512,128]{1,0:T(8,128)(2,1)S(1)}, bf16[512,128]{1,0:T(8,128)(2...) custom-call(s32[4]{0:T(128)S(1)} %pad_add_fusion.place_ref.refs_0_, ...), custom_call_target="tpu_custom_call" | custom-call | flops 8049999872 | bytes 1048576 | tf_op jit(solution)/shard_map/pallas_call | solution.py:555
  51.5 10.4 %collective-permute-start.14 = (bf16[512,128]{1,0:T(8,128)(2,1)S(1)}, bf16[512,128]{1,0:T(8,128)(2,1)S(1)}, u32[]{:S(2)}, u32[]{:S(2)}) collective-permute-start(bf16[512,128]{1,0:T(8,128)(2,1)S(1)} %get-tuple-element.87), channel_id=1, source_target_pairs={{0,8},{4,12},{8,0},{12,4},{1,9},{5,13},{9,1},{13,5},{2,10},{6,14},... | collective-permute-start | bytes 393224 | tf_op jit(solution)/shard_map/ppermute | solution.py:575
  61.9 0.0 collective-permute-start.25
  61.9 0.0 collective-permute-done.9.refs_5_
  61.9 1.3 %collective-permute-start.26 = (bf16[512,128]{1,0:T(8,128)(2,1)S(1)}, bf16[512,128]{1,0:T(8,128)(2,1)S(1)}, u32[]{:S(2)}, u32[]{:S(2)}) collective-permute-start(bf16[512,128]{1,0:T(8,128)(2,1)S(1)} %get-tuple-element.100), channel_id=1, source_target_pairs={{0,12},{4,8},{8,4},{12,0},{1,13},{5,9},{9,5},{13,1},{2,14},{6,10},... | collective-permute-start | bytes 393224 | tf_op jit(solution)/shard_map/ppermute | solution.py:575
  63.1 0.0 collective-permute-done.10.refs_6_
  63.1 0.0 collective-permute-done.11.refs_7_
  63.1 7.0 %shard_map.101 = (bf16[1024,128]{1,0:T(8,128)(2,1)S(1)}, bf16[1024,128]{1,0:T(8,128)(2,1)S(1)}, bf16[1024,128]{1,0:T(8,128)(2,1)S(1)}, bf16[1024,128]{1,0:T(8,12...) custom-call(s32[4]{0:T(128)S(1)} %pad_add_fusion.place_ref.refs_0_, ...), custom_call_target="tpu_custom_call" | custom-call | flops 11500000256 | bytes 1048576 | tf_op jit(solution)/shard_map/pallas_call | solution.py:555
  70.2 1.1 collective-permute-start.13
  71.3 0.0 collective-permute-done.14.refs_3_.refs_10_
  71.3 2.0 %collective-permute-start.16 = (bf16[1024,128]{1,0:T(8,128)(2,1)S(1)}, bf16[1024,128]{1,0:T(8,128)(2,1)S(1)}, u32[]{:S(2)}, u32[]{:S(2)}) collective-permute-start(bf16[1024,128]{1,0:T(8,128)(2,1)S(1)} %get-tuple-element.89), channel_id=1, source_target_pairs={{0,12},{4,8},{8,4},{12,0},{1,13},{5,9},{9,5},{13,1},{2,14},{6,10},... | collective-permute-start | bytes 786440 | tf_op jit(solution)/shard_map/ppermute | solution.py:575
  73.3 0.0 collective-permute-start.20
  73.3 1.5 %collective-permute-start.15 = (bf16[1024,128]{1,0:T(8,128)(2,1)S(1)}, bf16[1024,128]{1,0:T(8,128)(2,1)S(1)}, u32[]{:S(2)}, u32[]{:S(2)}) collective-permute-start(bf16[1024,128]{1,0:T(8,128)(2,1)S(1)} %get-tuple-element.88), channel_id=1, source_target_pairs={{0,8},{4,12},{8,0},{12,4},{1,9},{5,13},{9,1},{13,5},{2,10},{6,14},... | collective-permute-start | bytes 786440 | tf_op jit(solution)/shard_map/ppermute | solution.py:575
  74.8 0.0 collective-permute-done.26.refs_4_.refs_11_
  74.8 0.6 shard_map.104
  75.4 1.9 %collective-permute-start.27 = (bf16[4,512,128]{2,1,0:T(8,128)(2,1)S(1)}, bf16[4,512,128]{2,1,0:T(8,128)(2,1)S(1)}, u32[]{:S(2)}, u32[]{:S(2)}) collective-permute-start(bf16[4,512,128]{2,1,0:T(8,128)(2,1)S(1)} %shard_map.104), channel_id=1, source_target_pairs={{0,1},{1,0},{2,3},{3,2},{4,5},{5,4},{6,7},{7,6},{8,9},{9,8},{10,11... | collective-permute-start | bytes 1572872 | tf_op jit(solution)/shard_map/ppermute | solution.py:581
  77.3 2.8 %collective-permute-done.16.refs_3_ = bf16[1024,128]{1,0:T(8,128)(2,1)S(1)} collective-permute-done((bf16[1024,128]{1,0:T(8,128)(2,1)S(1)}, bf16[1024,128]{1,0:T(8,128)(2,1)S(1)}, u32[]{:S(2)}, u32[]{:S(2)}) %collective-permute-start.16) | collective-permute-done | bytes 262176 | tf_op jit(solution)/shard_map/ppermute | solution.py:575
  80.0 3.3 %collective-permute-start.21 = (bf16[1024,128]{1,0:T(8,128)(2,1)S(1)}, bf16[1024,128]{1,0:T(8,128)(2,1)S(1)}, u32[]{:S(2)}, u32[]{:S(2)}) collective-permute-start(bf16[1024,128]{1,0:T(8,128)(2,1)S(1)} %get-tuple-element.95.refs_0_), channel_id=1, source_target_pairs={{0,1},{1,0},{2,3},{3,2},{4,5},{5,4},{6,7},{7,6},{8,9},{9,8},{10,11... | collective-permute-start | bytes 786440 | tf_op jit(solution)/shard_map/ppermute | solution.py:581
  83.3 5.2 %collective-permute-done.20.refs_1_ = bf16[1024,128]{1,0:T(8,128)(2,1)S(1)} collective-permute-done((bf16[1024,128]{1,0:T(8,128)(2,1)S(1)}, bf16[1024,128]{1,0:T(8,128)(2,1)S(1)}, u32[]{:S(2)}, u32[]{:S(2)}) %collective-permute-start.20) | collective-permute-done | bytes 262176 | tf_op jit(solution)/shard_map/ppermute | solution.py:575
  88.5 0.5 collective-permute-start.24
  89.0 0.0 collective-permute-done.13.theirs_ref
  89.0 0.0 collective-permute-start.22
  89.0 0.6 shard_map.102
  89.6 7.1 %collective-permute-done.15.refs_2_ = bf16[1024,128]{1,0:T(8,128)(2,1)S(1)} collective-permute-done((bf16[1024,128]{1,0:T(8,128)(2,1)S(1)}, bf16[1024,128]{1,0:T(8,128)(2,1)S(1)}, u32[]{:S(2)}, u32[]{:S(2)}) %collective-permute-start.15) | collective-permute-done | bytes 262176 | tf_op jit(solution)/shard_map/ppermute | solution.py:575
  96.7 0.5 collective-permute-start.23
  97.3 2.5 %collective-permute-start.18 = (bf16[576,128]{1,0:T(8,128)(2,1)S(1)}, bf16[576,128]{1,0:T(8,128)(2,1)S(1)}, u32[]{:S(2)}, u32[]{:S(2)}) collective-permute-start(bf16[576,128]{1,0:T(8,128)(2,1)S(1)} %get-tuple-element.92), channel_id=1, source_target_pairs={{0,8},{4,12},{8,0},{12,4},{1,9},{5,13},{9,1},{13,5},{2,10},{6,14},... | collective-permute-start | bytes 442376 | tf_op jit(solution)/shard_map/ppermute | solution.py:575
  99.7 0.0 collective-permute-done.22.refs_5_
  99.7 1.1 collective-permute-start.19
  100.8 2.9 %shard_map.105 = bf16[256,1024]{1,0:T(8,128)(2,1)S(1)} custom-call(s32[4]{0:T(128)S(1)} %pad_add_fusion.place_ref.refs_0_, bf16[1024,128]{1,0:T(8,128)(2,1)S(1)} %get-tuple-element.95.refs_0_, bf16[1024,128]{1,0:T(8,128)(2,1)S(1)} %collective-permute-done.20.refs_1_, bf16[1024,128]{1,0:T(8,128)(2,1)S(1)} %collective-permute-done.15.refs_2_, ...), custom_call_target="tpu_custom_call" | custom-call | flops 1150000000 | bytes 1048576 | tf_op jit(solution)/shard_map/pallas_call | solution.py:555
  103.8 1.2 %collective-permute-start.28 = (bf16[256,1024]{1,0:T(8,128)(2,1)S(1)}, bf16[256,1024]{1,0:T(8,128)(2,1)S(1)}, u32[]{:S(2)}, u32[]{:S(2)}) collective-permute-start(bf16[256,1024]{1,0:T(8,128)(2,1)S(1)} %shard_map.105), channel_id=1, source_target_pairs={{0,1},{1,3},{3,2},{2,0},{4,5},{5,7},{7,6},{6,4},{8,9},{9,11},{11,1... | collective-permute-start | bytes 1572872 | tf_op jit(solution)/shard_map/ppermute | solution.py:723
  105.0 2.9 %shard_map.106.kept_ref = bf16[256,1024]{1,0:T(8,128)(2,1)S(1)} custom-call(s32[4]{0:T(128)S(1)} %pad_add_fusion.place_ref.refs_0_, bf16[1024,128]{1,0:T(8,128)(2,1)S(1)} %get-tuple-element.95.refs_0_, bf16[1024,128]{1,0:T(8,128)(2,1)S(1)} %collective-permute-done.20.refs_1_, bf16[1024,128]{1,0:T(8,128)(2,1)S(1)} %collective-permute-done.15.refs_2_, ...), custom_call_target="tpu_custom_call" | custom-call | flops 1150000000 | bytes 1048576 | tf_op jit(solution)/shard_map/pallas_call | solution.py:555
  107.9 3.2 %collective-permute-start.29 = (bf16[256,1024]{1,0:T(8,128)(2,1)S(1)}, bf16[256,1024]{1,0:T(8,128)(2,1)S(1)}, u32[]{:S(2)}, u32[]{:S(2)}) collective-permute-start(bf16[256,1024]{1,0:T(8,128)(2,1)S(1)} %shard_map.106.kept_ref), channel_id=1, source_target_pairs={{1,2},{2,1},{5,6},{6,5},{9,10},{10,9},{13,14},{14,13},{17,18},{18,... | collective-permute-start | bytes 1572872 | tf_op jit(solution)/shard_map/ppermute | solution.py:725
  111.1 1.5 %shard_map.103 = (bf16[256,1024]{1,0:T(8,128)(2,1)}, f32[8,32,128]{2,1,0:T(8,128)}) custom-call(s32[4]{0:T(128)S(1)} %pad_add_fusion.place_ref.refs_0_, bf16[576,128]{1,0:T(8,128)(2,1)S(1)} %get-tuple-element.90.refs_0_, bf16[576,128]{1,0:T(8,128)(2,1)S(1)} %collective-permute-done.17.refs_1_, bf16[576,128]{1,0:T(8,128)(2,1)S(1)} %collective-permute-done.18.refs_2_, ...), custom_call_target="tpu_custom_call" | custom-call | flops 9200000000 | bytes 1048576 | tf_op jit(solution)/shard_map/pallas_call | solution.py:555
  112.6 6.1 %collective-permute-done.29.second_ref = bf16[256,1024]{1,0:T(8,128)(2,1)S(1)} collective-permute-done((bf16[256,1024]{1,0:T(8,128)(2,1)S(1)}, bf16[256,1024]{1,0:T(8,128)(2,1)S(1)}, u32[]{:S(2)}, u32[]{:S(2)}) %collective-permute-start.29) | collective-permute-done | bytes 524320 | tf_op jit(solution)/shard_map/ppermute | solution.py:725
  118.7 1.5 %shard_map.107 = bf16[256,1024]{1,0:T(8,128)(2,1)} custom-call(s32[4]{0:T(128)S(1)} %pad_add_fusion.place_ref.refs_0_, bf16[256,1024]{1,0:T(8,128)(2,1)S(1)} %collective-permute-done.28.first_ref, bf16[256,1024]{1,0:T(8,128)(2,1)S(1)} %collective-permute-done.29.second_ref, bf16[256,1024]{1,0:T(8,128)(2,1)S(1)} %shard_map.106.kept_ref), custom_call_target="tpu_custom_call" | custom-call | flops 1150000000 | bytes 1048576 | tf_op jit(solution)/shard_map/pallas_call | solution.py:555
  (19 shorter events, 0.0 us)
Async XLA Ops:
  0.6 4.6 %collective-permute-start.1 = (bf16[256,2048]{1,0:T(8,128)(2,1)}, bf16[256,2048]{1,0:T(8,128)(2,1)S(1)}, u32[]{:S(2)}, u32[]{:S(2)}) collective-permute-start(bf16[256,2048]{1,0:T(8,128)(2,1)} %refs_1_.5), channel_id=1, source_target_pairs={{0,1},{1,0},{2,3},{3,2},{4,5},{5,4},{6,7},{7,6},{8,9},{9,8},{10,11... | collective-permute-start | bytes 3145736 | tf_op jit(solution)/shard_map/ppermute | solution.py:581
  2.5 2.6 %collective-permute-start = (bf16[4,272,128]{2,1,0:T(8,128)(2,1)S(1)}, bf16[4,272,128]{2,1,0:T(8,128)(2,1)S(1)}, u32[]{:S(2)}, u32[]{:S(2)}) collective-permute-start(bf16[4,272,128]{2,1,0:T(8,128)(2,1)S(1)} %get-tuple-element.55), channel_id=1, source_target_pairs={{0,1},{1,0},{2,3},{3,2},{4,5},{5,4},{6,7},{7,6},{8,9},{9,8},{10,11... | collective-permute-start | bytes 835592 | tf_op jit(solution)/shard_map/ppermute | solution.py:581
  8.1 5.0 %collective-permute-start.2 = (bf16[2,512,512]{2,1,0:T(8,128)(2,1)S(1)}, bf16[2,512,512]{2,1,0:T(8,128)(2,1)S(1)}, u32[]{:S(2)}, u32[]{:S(2)}) collective-permute-start(bf16[2,512,512]{2,1,0:T(8,128)(2,1)S(1)} %get-tuple-element.56), channel_id=1, source_target_pairs={{0,1},{1,0},{2,3},{3,2},{4,5},{5,4},{6,7},{7,6},{8,9},{9,8},{10,11... | collective-permute-start | bytes 3145736 | tf_op jit(solution)/shard_map/ppermute | solution.py:581
  8.2 14.4 %collective-permute-start.7 = (bf16[528,128]{1,0:T(8,128)(2,1)S(1)}, bf16[528,128]{1,0:T(8,128)(2,1)S(1)}, u32[]{:S(2)}, u32[]{:S(2)}) collective-permute-start(bf16[528,128]{1,0:T(8,128)(2,1)S(1)} %get-tuple-element.62), channel_id=1, source_target_pairs={{0,8},{4,12},{8,0},{12,4},{1,9},{5,13},{9,1},{13,5},{2,10},{6,14},... | collective-permute-start | bytes 405512 | tf_op jit(solution)/shard_map/ppermute | solution.py:575
  12.0 13.2 %collective-permute-start.8 = (bf16[528,128]{1,0:T(8,128)(2,1)S(1)}, bf16[528,128]{1,0:T(8,128)(2,1)S(1)}, u32[]{:S(2)}, u32[]{:S(2)}) collective-permute-start(bf16[528,128]{1,0:T(8,128)(2,1)S(1)} %get-tuple-element.63), channel_id=1, source_target_pairs={{0,12},{4,8},{8,4},{12,0},{1,13},{5,9},{9,5},{13,1},{2,14},{6,10},... | collective-permute-start | bytes 405512 | tf_op jit(solution)/shard_map/ppermute | solution.py:575
  15.7 9.5 %collective-permute-start.6 = (bf16[1,512,512]{2,1,0:T(8,128)(2,1)S(1)}, bf16[1,512,512]{2,1,0:T(8,128)(2,1)S(1)}, u32[]{:S(2)}, u32[]{:S(2)}) collective-permute-start(bf16[1,512,512]{2,1,0:T(8,128)(2,1)S(1)} %shard_map.98), channel_id=1, source_target_pairs={{0,1},{1,0},{2,3},{3,2},{4,5},{5,4},{6,7},{7,6},{8,9},{9,8},{10,11... | collective-permute-start | bytes 1572872 | tf_op jit(solution)/shard_map/ppermute | solution.py:581
  20.0 12.8 %collective-permute-start.3 = (bf16[1024,128]{1,0:T(8,128)(2,1)S(1)}, bf16[1024,128]{1,0:T(8,128)(2,1)S(1)}, u32[]{:S(2)}, u32[]{:S(2)}) collective-permute-start(bf16[1024,128]{1,0:T(8,128)(2,1)S(1)} %get-tuple-element.58), channel_id=1, source_target_pairs={{0,4},{4,0},{8,12},{12,8},{1,5},{5,1},{9,13},{13,9},{2,6},{6,2},{1... | collective-permute-start | bytes 786440 | tf_op jit(solution)/shard_map/ppermute | solution.py:575
  20.1 21.4 %collective-permute-start.4 = (bf16[1024,128]{1,0:T(8,128)(2,1)S(1)}, bf16[1024,128]{1,0:T(8,128)(2,1)S(1)}, u32[]{:S(2)}, u32[]{:S(2)}) collective-permute-start(bf16[1024,128]{1,0:T(8,128)(2,1)S(1)} %get-tuple-element.59), channel_id=1, source_target_pairs={{0,8},{4,12},{8,0},{12,4},{1,9},{5,13},{9,1},{13,5},{2,10},{6,14},... | collective-permute-start | bytes 786440 | tf_op jit(solution)/shard_map/ppermute | solution.py:575
  22.6 22.4 %collective-permute-start.5 = (bf16[1024,128]{1,0:T(8,128)(2,1)S(1)}, bf16[1024,128]{1,0:T(8,128)(2,1)S(1)}, u32[]{:S(2)}, u32[]{:S(2)}) collective-permute-start(bf16[1024,128]{1,0:T(8,128)(2,1)S(1)} %get-tuple-element.60), channel_id=1, source_target_pairs={{0,12},{4,8},{8,4},{12,0},{1,13},{5,9},{9,5},{13,1},{2,14},{6,10},... | collective-permute-start | bytes 786440 | tf_op jit(solution)/shard_map/ppermute | solution.py:575
  25.1 19.8 %copy-start.3 = (s32[256]{0:T(256)S(1)}, s32[256]{0:T(256)}, u32[]{:S(2)}) copy-start(s32[256]{0:T(256)} %param.11) | copy-start | bytes 3076
  25.1 19.8 %collective-permute-start.12 = (bf16[528,128]{1,0:T(8,128)(2,1)S(1)}, bf16[528,128]{1,0:T(8,128)(2,1)S(1)}, u32[]{:S(2)}, u32[]{:S(2)}) collective-permute-start(bf16[528,128]{1,0:T(8,128)(2,1)S(1)} %get-tuple-element.74), channel_id=1, source_target_pairs={{0,4},{4,0},{8,12},{12,8},{1,5},{5,1},{9,13},{13,9},{2,6},{6,2},{1... | collective-permute-start | bytes 405512 | tf_op jit(solution)/shard_map/ppermute | solution.py:575
  28.1 33.8 %collective-permute-start.9 = (bf16[512,128]{1,0:T(8,128)(2,1)S(1)}, bf16[512,128]{1,0:T(8,128)(2,1)S(1)}, u32[]{:S(2)}, u32[]{:S(2)}) collective-permute-start(bf16[512,128]{1,0:T(8,128)(2,1)S(1)} %get-tuple-element.70), channel_id=1, source_target_pairs={{0,4},{4,0},{8,12},{12,8},{1,5},{5,1},{9,13},{13,9},{2,6},{6,2},{1... | collective-permute-start | bytes 393224 | tf_op jit(solution)/shard_map/ppermute | solution.py:575
  32.8 30.3 %collective-permute-start.10 = (bf16[512,128]{1,0:T(8,128)(2,1)S(1)}, bf16[512,128]{1,0:T(8,128)(2,1)S(1)}, u32[]{:S(2)}, u32[]{:S(2)}) collective-permute-start(bf16[512,128]{1,0:T(8,128)(2,1)S(1)} %get-tuple-element.71), channel_id=1, source_target_pairs={{0,8},{4,12},{8,0},{12,4},{1,9},{5,13},{9,1},{13,5},{2,10},{6,14},... | collective-permute-start | bytes 393224 | tf_op jit(solution)/shard_map/ppermute | solution.py:575
  41.5 21.6 %collective-permute-start.11 = (bf16[512,128]{1,0:T(8,128)(2,1)S(1)}, bf16[512,128]{1,0:T(8,128)(2,1)S(1)}, u32[]{:S(2)}, u32[]{:S(2)}) collective-permute-start(bf16[512,128]{1,0:T(8,128)(2,1)S(1)} %get-tuple-element.72), channel_id=1, source_target_pairs={{0,12},{4,8},{8,4},{12,0},{1,13},{5,9},{9,5},{13,1},{2,14},{6,10},... | collective-permute-start | bytes 393224 | tf_op jit(solution)/shard_map/ppermute | solution.py:575
  51.5 19.8 %collective-permute-start.14 = (bf16[512,128]{1,0:T(8,128)(2,1)S(1)}, bf16[512,128]{1,0:T(8,128)(2,1)S(1)}, u32[]{:S(2)}, u32[]{:S(2)}) collective-permute-start(bf16[512,128]{1,0:T(8,128)(2,1)S(1)} %get-tuple-element.87), channel_id=1, source_target_pairs={{0,8},{4,12},{8,0},{12,4},{1,9},{5,13},{9,1},{13,5},{2,10},{6,14},... | collective-permute-start | bytes 393224 | tf_op jit(solution)/shard_map/ppermute | solution.py:575
  61.9 11.4 %collective-permute-start.25 = (bf16[512,128]{1,0:T(8,128)(2,1)S(1)}, bf16[512,128]{1,0:T(8,128)(2,1)S(1)}, u32[]{:S(2)}, u32[]{:S(2)}) collective-permute-start(bf16[512,128]{1,0:T(8,128)(2,1)S(1)} %get-tuple-element.99), channel_id=1, source_target_pairs={{0,4},{4,0},{8,12},{12,8},{1,5},{5,1},{9,13},{13,9},{2,6},{6,2},{1... | collective-permute-start | bytes 393224 | tf_op jit(solution)/shard_map/ppermute | solution.py:575
  61.9 13.0 %collective-permute-start.26 = (bf16[512,128]{1,0:T(8,128)(2,1)S(1)}, bf16[512,128]{1,0:T(8,128)(2,1)S(1)}, u32[]{:S(2)}, u32[]{:S(2)}) collective-permute-start(bf16[512,128]{1,0:T(8,128)(2,1)S(1)} %get-tuple-element.100), channel_id=1, source_target_pairs={{0,12},{4,8},{8,4},{12,0},{1,13},{5,9},{9,5},{13,1},{2,14},{6,10},... | collective-permute-start | bytes 393224 | tf_op jit(solution)/shard_map/ppermute | solution.py:575
  70.2 18.8 %collective-permute-start.13 = (bf16[4,288,128]{2,1,0:T(8,128)(2,1)S(1)}, bf16[4,288,128]{2,1,0:T(8,128)(2,1)S(1)}, u32[]{:S(2)}, u32[]{:S(2)}) collective-permute-start(bf16[4,288,128]{2,1,0:T(8,128)(2,1)S(1)} %get-tuple-element.78), channel_id=1, source_target_pairs={{0,1},{1,0},{2,3},{3,2},{4,5},{5,4},{6,7},{7,6},{8,9},{9,8},{10,11... | collective-permute-start | bytes 884744 | tf_op jit(solution)/shard_map/ppermute | solution.py:581
  71.3 8.8 %collective-permute-start.16 = (bf16[1024,128]{1,0:T(8,128)(2,1)S(1)}, bf16[1024,128]{1,0:T(8,128)(2,1)S(1)}, u32[]{:S(2)}, u32[]{:S(2)}) collective-permute-start(bf16[1024,128]{1,0:T(8,128)(2,1)S(1)} %get-tuple-element.89), channel_id=1, source_target_pairs={{0,12},{4,8},{8,4},{12,0},{1,13},{5,9},{9,5},{13,1},{2,14},{6,10},... | collective-permute-start | bytes 786440 | tf_op jit(solution)/shard_map/ppermute | solution.py:575
  73.3 15.2 %collective-permute-start.20 = (bf16[1024,128]{1,0:T(8,128)(2,1)S(1)}, bf16[1024,128]{1,0:T(8,128)(2,1)S(1)}, u32[]{:S(2)}, u32[]{:S(2)}) collective-permute-start(bf16[1024,128]{1,0:T(8,128)(2,1)S(1)} %get-tuple-element.96), channel_id=1, source_target_pairs={{0,4},{4,0},{8,12},{12,8},{1,5},{5,1},{9,13},{13,9},{2,6},{6,2},{1... | collective-permute-start | bytes 786440 | tf_op jit(solution)/shard_map/ppermute | solution.py:575
  73.3 23.4 %collective-permute-start.15 = (bf16[1024,128]{1,0:T(8,128)(2,1)S(1)}, bf16[1024,128]{1,0:T(8,128)(2,1)S(1)}, u32[]{:S(2)}, u32[]{:S(2)}) collective-permute-start(bf16[1024,128]{1,0:T(8,128)(2,1)S(1)} %get-tuple-element.88), channel_id=1, source_target_pairs={{0,8},{4,12},{8,0},{12,4},{1,9},{5,13},{9,1},{13,5},{2,10},{6,14},... | collective-permute-start | bytes 786440 | tf_op jit(solution)/shard_map/ppermute | solution.py:575
  74.8 26.0 %copy-start.2 = (bf16[1024,1024]{1,0:T(8,128)(2,1)S(1)}, bf16[1024,1024]{1,0:T(8,128)(2,1)}, u32[]{:S(2)}) copy-start(bf16[1024,1024]{1,0:T(8,128)(2,1)} %refs_14_.3) | copy-start | bytes 6291460
  75.4 25.4 %collective-permute-start.27 = (bf16[4,512,128]{2,1,0:T(8,128)(2,1)S(1)}, bf16[4,512,128]{2,1,0:T(8,128)(2,1)S(1)}, u32[]{:S(2)}, u32[]{:S(2)}) collective-permute-start(bf16[4,512,128]{2,1,0:T(8,128)(2,1)S(1)} %shard_map.104), channel_id=1, source_target_pairs={{0,1},{1,0},{2,3},{3,2},{4,5},{5,4},{6,7},{7,6},{8,9},{9,8},{10,11... | collective-permute-start | bytes 1572872 | tf_op jit(solution)/shard_map/ppermute | solution.py:581
  80.0 17.2 %collective-permute-start.21 = (bf16[1024,128]{1,0:T(8,128)(2,1)S(1)}, bf16[1024,128]{1,0:T(8,128)(2,1)S(1)}, u32[]{:S(2)}, u32[]{:S(2)}) collective-permute-start(bf16[1024,128]{1,0:T(8,128)(2,1)S(1)} %get-tuple-element.95.refs_0_), channel_id=1, source_target_pairs={{0,1},{1,0},{2,3},{3,2},{4,5},{5,4},{6,7},{7,6},{8,9},{9,8},{10,11... | collective-permute-start | bytes 786440 | tf_op jit(solution)/shard_map/ppermute | solution.py:581
  88.5 8.8 %collective-permute-start.24 = (bf16[1024,128]{1,0:T(8,128)(2,1)S(1)}, bf16[1024,128]{1,0:T(8,128)(2,1)S(1)}, u32[]{:S(2)}, u32[]{:S(2)}) collective-permute-start(bf16[1024,128]{1,0:T(8,128)(2,1)S(1)} %collective-permute-done.16.refs_3_), channel_id=1, source_target_pairs={{0,1},{1,0},{2,3},{3,2},{4,5},{5,4},{6,7},{7,6},{8,9},{9,8},{10,11... | collective-permute-start | bytes 786440 | tf_op jit(solution)/shard_map/ppermute | solution.py:581
  89.0 10.7 %collective-permute-start.22 = (bf16[1024,128]{1,0:T(8,128)(2,1)S(1)}, bf16[1024,128]{1,0:T(8,128)(2,1)S(1)}, u32[]{:S(2)}, u32[]{:S(2)}) collective-permute-start(bf16[1024,128]{1,0:T(8,128)(2,1)S(1)} %collective-permute-done.20.refs_1_), channel_id=1, source_target_pairs={{0,1},{1,0},{2,3},{3,2},{4,5},{5,4},{6,7},{7,6},{8,9},{9,8},{10,11... | collective-permute-start | bytes 786440 | tf_op jit(solution)/shard_map/ppermute | solution.py:581
  89.0 11.8 %copy-start = (bf16[1024,1024]{1,0:T(8,128)(2,1)S(1)}, bf16[1024,1024]{1,0:T(8,128)(2,1)}, u32[]{:S(2)}) copy-start(bf16[1024,1024]{1,0:T(8,128)(2,1)} %refs_15_.3) | copy-start | bytes 6291460
  89.0 11.8 %copy-start.1 = (bf16[1024,1024]{1,0:T(8,128)(2,1)S(1)}, bf16[1024,1024]{1,0:T(8,128)(2,1)}, u32[]{:S(2)}) copy-start(bf16[1024,1024]{1,0:T(8,128)(2,1)} %refs_13_.3) | copy-start | bytes 6291460
  96.7 4.1 %collective-permute-start.23 = (bf16[1024,128]{1,0:T(8,128)(2,1)S(1)}, bf16[1024,128]{1,0:T(8,128)(2,1)S(1)}, u32[]{:S(2)}, u32[]{:S(2)}) collective-permute-start(bf16[1024,128]{1,0:T(8,128)(2,1)S(1)} %collective-permute-done.15.refs_2_), channel_id=1, source_target_pairs={{0,1},{1,0},{2,3},{3,2},{4,5},{5,4},{6,7},{7,6},{8,9},{9,8},{10,11... | collective-permute-start | bytes 786440 | tf_op jit(solution)/shard_map/ppermute | solution.py:581
  97.2 13.8 %collective-permute-start.17 = (bf16[576,128]{1,0:T(8,128)(2,1)S(1)}, bf16[576,128]{1,0:T(8,128)(2,1)S(1)}, u32[]{:S(2)}, u32[]{:S(2)}) collective-permute-start(bf16[576,128]{1,0:T(8,128)(2,1)S(1)} %get-tuple-element.91), channel_id=1, source_target_pairs={{0,4},{4,0},{8,12},{12,8},{1,5},{5,1},{9,13},{13,9},{2,6},{6,2},{1... | collective-permute-start | bytes 442376 | tf_op jit(solution)/shard_map/ppermute | solution.py:575
  97.3 13.8 %collective-permute-start.18 = (bf16[576,128]{1,0:T(8,128)(2,1)S(1)}, bf16[576,128]{1,0:T(8,128)(2,1)S(1)}, u32[]{:S(2)}, u32[]{:S(2)}) collective-permute-start(bf16[576,128]{1,0:T(8,128)(2,1)S(1)} %get-tuple-element.92), channel_id=1, source_target_pairs={{0,8},{4,12},{8,0},{12,4},{1,9},{5,13},{9,1},{13,5},{2,10},{6,14},... | collective-permute-start | bytes 442376 | tf_op jit(solution)/shard_map/ppermute | solution.py:575
  99.7 11.4 %collective-permute-start.19 = (bf16[576,128]{1,0:T(8,128)(2,1)S(1)}, bf16[576,128]{1,0:T(8,128)(2,1)S(1)}, u32[]{:S(2)}, u32[]{:S(2)}) collective-permute-start(bf16[576,128]{1,0:T(8,128)(2,1)S(1)} %get-tuple-element.93), channel_id=1, source_target_pairs={{0,12},{4,8},{8,4},{12,0},{1,13},{5,9},{9,5},{13,1},{2,14},{6,10},... | collective-permute-start | bytes 442376 | tf_op jit(solution)/shard_map/ppermute | solution.py:575
  103.8 15.0 %collective-permute-start.28 = (bf16[256,1024]{1,0:T(8,128)(2,1)S(1)}, bf16[256,1024]{1,0:T(8,128)(2,1)S(1)}, u32[]{:S(2)}, u32[]{:S(2)}) collective-permute-start(bf16[256,1024]{1,0:T(8,128)(2,1)S(1)} %shard_map.105), channel_id=1, source_target_pairs={{0,1},{1,3},{3,2},{2,0},{4,5},{5,7},{7,6},{6,4},{8,9},{9,11},{11,1... | collective-permute-start | bytes 1572872 | tf_op jit(solution)/shard_map/ppermute | solution.py:723
  107.9 10.8 %collective-permute-start.29 = (bf16[256,1024]{1,0:T(8,128)(2,1)S(1)}, bf16[256,1024]{1,0:T(8,128)(2,1)S(1)}, u32[]{:S(2)}, u32[]{:S(2)}) collective-permute-start(bf16[256,1024]{1,0:T(8,128)(2,1)S(1)} %shard_map.106.kept_ref), channel_id=1, source_target_pairs={{1,2},{2,1},{5,6},{6,5},{9,10},{10,9},{13,14},{14,13},{17,18},{18,... | collective-permute-start | bytes 1572872 | tf_op jit(solution)/shard_map/ppermute | solution.py:725

commit v18 on v17

--- a/solution.py
+++ b/solution.py
@@ -197,36 +197,38 @@
     return -(-(rows // head_dim) // 16) * 16
 
 
-def pack_kernel(place_ref, grads_ref, assign_ref, mine_ref, theirs_ref, ids_ref, sems):
-    chips, padded, head_dim = mine_ref.shape
+def id_tile(side, ids, spare):
+    head_dim = 128 if ids.shape[1] % 128 == 0 else ids.shape[1]
+    lines = [ids[:, at : at + head_dim] for at in range(0, ids.shape[1], head_dim)]
+    gap = [jnp.zeros((len(lines), head_dim), jnp.float32)]
+    rest = [jnp.zeros((spare - len(lines), head_dim), jnp.float32)]
+    first = jnp.concatenate(lines + gap + rest, axis=0)
+    second = jnp.concatenate(gap + lines + rest, axis=0)
+    return jnp.where(side == 0, first, second).astype(jnp.bfloat16)
+
+
+def pack_kernel(place_ref, grads_ref, assign_ref, theirs_ref, ids_ref, sems):
+    chips, padded, head_dim = theirs_ref.shape
     rows = grads_ref.shape[0]
     spare = padded - rows - rows // head_dim
-    copies = [pltpu.make_async_copy(assign_ref, ids_ref, sems.at[2 * chips])]
-    for turn, out_ref in enumerate((mine_ref, theirs_ref)):
-        for chip in range(chips):
-            head = (place_ref[1] ^ turn) * chips + chip
-            at = pl.multiple_of(head * head_dim, head_dim)
-            copies.append(
-                pltpu.make_async_copy(
-                    grads_ref.at[:, pl.ds(at, head_dim)],
-                    out_ref.at[chip, pl.ds(0, rows)],
-                    sems.at[turn * chips + chip],
-                )
+    copies = [pltpu.make_async_copy(assign_ref, ids_ref, sems.at[chips])]
+    for chip in range(chips):
+        head = (1 - place_ref[1]) * chips + chip
+        at = pl.multiple_of(head * head_dim, head_dim)
+        copies.append(
+            pltpu.make_async_copy(
+                grads_ref.at[:, pl.ds(at, head_dim)],
+                theirs_ref.at[chip, pl.ds(0, rows)],
+                sems.at[chip],
             )
+        )
     for copy in copies:
         copy.start()
     copies[0].wait()
-    for turn, out_ref in enumerate((mine_ref, theirs_ref)):
-        for chip in range(chips):
-            head = (place_ref[1] ^ turn) * chips + chip
-            ids = ids_ref[pl.ds(head, 1), :].astype(jnp.float32)
-            lines = [ids[:, start : start + head_dim] for start in range(0, rows, head_dim)]
-            gap = [jnp.zeros((len(lines), head_dim), jnp.float32)]
-            rest = [jnp.zeros((spare - len(lines), head_dim), jnp.float32)]
-            first = jnp.concatenate(lines + gap + rest, axis=0)
-            second = jnp.concatenate(gap + lines + rest, axis=0)
-            tile = jnp.where(place_ref[1] == 0, first, second)
-            out_ref[chip, rows:, :] = tile.astype(jnp.bfloat16)
+    for chip in range(chips):
+        head = (1 - place_ref[1]) * chips + chip
+        ids = ids_ref[pl.ds(head, 1), :].astype(jnp.float32)
+        theirs_ref[chip, rows:, :] = id_tile(place_ref[1], ids, spare)
     for copy in copies[1:]:
         copy.wait()
 
@@ -237,16 +239,6 @@
         at = pl.ds(pl.multiple_of((place_ref[1] ^ turn) * height, height), height)
         for offset, out_ref in enumerate(out_refs):
             out_ref[at, :] = held_ref[place_ref[0] ^ offset]
-
-
-def merge_grads(place_ref, mine_ref, theirs_ref, out_refs):
-    rows = out_refs[0].shape[0] - mine_ref.shape[1]
-    for offset, out_ref in enumerate(out_refs):
-        chip = place_ref[0] ^ offset
-        for turn, held_ref in enumerate((mine_ref, theirs_ref)):
-            at = pl.ds(pl.multiple_of((place_ref[1] ^ turn) * rows, rows), rows)
-            out_ref[at, :] = held_ref[chip, :rows, :]
-        out_ref[2 * rows :, :] = mine_ref[chip, rows:, :] + theirs_ref[chip, rows:, :]
 
 
 def fetch_columns(half, weights, held_ref, sems):
@@ -306,24 +298,47 @@
         copy.wait()
 
 
-def opening_kernel(place_ref, held_ref, mine_ref, theirs_ref, *refs):
-    tokens, refs = refs[:2], refs[2:]
-    out_refs, (part_ref, joined_ref, sems) = refs[:-3], refs[-3:]
+def opening_kernel(place_ref, held_ref, theirs_ref, *refs):
+    tokens, (grads_ref, assign_ref), refs = refs[:2], refs[2:4], refs[4:]
+    out_refs, (part_ref, joined_ref, ids_ref, sems, grad_sems) = refs[:-5], refs[-5:]
     side = place_ref[1]
+    chips = len(out_refs)
     tall, depth = joined_ref.shape
     rows = tall // 2
+    head_dim = out_refs[0].shape[1]
     near = pl.ds(pl.multiple_of(side * depth, depth), depth)
     joins = []
     for core, source in enumerate(tokens):
         at = pl.ds(pl.multiple_of((side ^ core) * rows, rows), rows)
         joins.append(pltpu.make_async_copy(source.at[:, near], joined_ref.at[at], sems.at[core]))
         joins[core].start()
-    merge_grads(place_ref, mine_ref, theirs_ref, out_refs)
+    copies = [pltpu.make_async_copy(assign_ref, ids_ref, grad_sems.at[chips])]
+    mine = pl.ds(pl.multiple_of(side * rows, rows), rows)
+    other = pl.ds(pl.multiple_of((1 - side) * rows, rows), rows)
+    for offset, out_ref in enumerate(out_refs):
+        head = side * chips + (place_ref[0] ^ offset)
+        at = pl.multiple_of(head * head_dim, head_dim)
+        copies.append(
+            pltpu.make_async_copy(
+                grads_ref.at[:, pl.ds(at, head_dim)], out_ref.at[mine], grad_sems.at[offset]
+            )
+        )
+    for copy in copies:
+        copy.start()
+    copies[0].wait()
+    for offset, out_ref in enumerate(out_refs):
+        chip = place_ref[0] ^ offset
+        ids = ids_ref[pl.ds(side * chips + chip, 1), :].astype(jnp.float32)
+        spare = theirs_ref.shape[1] - rows - rows // head_dim
+        out_ref[other, :] = theirs_ref[chip, :rows, :]
+        out_ref[tall:, :] = theirs_ref[chip, rows:, :] + id_tile(side, ids, spare)
     for copy in joins:
         copy.wait()
     for index in range(held_ref.shape[0]):
         total = jnp.dot(joined_ref[...], held_ref[index], preferred_element_type=jnp.float32)
         part_ref[index] = total.astype(jnp.bfloat16)
+    for copy in copies[1:]:
+        copy.wait()
 
 
 def in_order(place, parts, start, ordered):
@@ -585,13 +600,13 @@
 
     hidden_other = to_sibling(hidden)
     block = low(chips, rows + id_lines(2 * rows, head_dim), head_dim)
-    grads_mine, grads_theirs = call(
+    grads_theirs = call(
         pack_kernel,
-        (block, block),
+        block,
         place,
         stay(d_attended),
         stay(assign),
-        scratch=[pltpu.VMEM(assign.shape, jnp.int32), pltpu.SemaphoreType.DMA((count + 1,))],
+        scratch=[pltpu.VMEM(assign.shape, jnp.int32), pltpu.SemaphoreType.DMA((chips + 1,))],
         hbm=2,
     )
     grads_other = to_sibling(grads_theirs)
@@ -634,12 +649,18 @@
         (*buffers(rows + block.shape[1]), low(2, 2 * rows, width // 2)),
         place,
         fetched,
-        grads_mine,
         grads_other,
         stay(hidden),
         hidden_other,
-        scratch=[pltpu.VMEM((2 * rows, half), jnp.bfloat16), pltpu.SemaphoreType.DMA((2,))],
-        hbm=2,
+        stay(d_attended),
+        stay(assign),
+        scratch=[
+            pltpu.VMEM((2 * rows, half), jnp.bfloat16),
+            pltpu.VMEM(assign.shape, jnp.int32),
+            pltpu.SemaphoreType.DMA((2,)),
+            pltpu.SemaphoreType.DMA((chips + 1,)),
+        ],
+        hbm=4,
         takes=0.1,
     )
     grads = exchange(merged)

time: 121 us -> 120 us (level)
  no operation moved by 1% of the time
where the time goes in v18:
time: 120 us
  starting transfers between devices  46.8 us (39%)
  Pallas kernels  39.1 us (33%)
  waiting for transfers between devices  33.2 us (28%)
    pallas_call x14, Pallas kernels, call(): pl.pallas_call(kernel, out_shape=outs, in_specs=[smem] + [vmem] * (len(op...  39.1 us
    ppermute x18, starting transfers between devices, exchange(): lax.ppermute(parts[offset], 'seq', [(at, at ^ offset) for at in range(chi...  33.7 us
    ppermute x18, waiting for transfers between devices, exchange(): lax.ppermute(parts[offset], 'seq', [(at, at ^ offset) for at in range(chi...  27.1 us
    ppermute x10, starting transfers between devices, to_sibling(): return lax.ppermute(piece, 'sub', swap)  8.72 us
    ppermute x1, waiting for transfers between devices, by_head(): second = lax.ppermute(kept, square, [(1, 2), (2, 1)])  6.1 us
    ppermute x1, starting transfers between devices, by_head(): second = lax.ppermute(kept, square, [(1, 2), (2, 1)])  3.17 us
  transfers between devices with their start and end apart: 30, of which 6 were waited for; matrix products, arithmetic and copies ran while one was open for 0% of the time, Pallas kernels for 29%

profile of v18, /device:TPU:1, one launch (start us, length us, event | category | flops | bytes accessed | tf_op | source)
XLA Modules:
  0.0 120.1 jit_solution(13675077875996123067)
XLA Ops:
  0.6 0.1 collective-permute-start.1
  0.8 0.1 pad_add_fusion.place_ref.refs_0_
  0.8 1.5 %shard_map.95 = bf16[4,272,128]{2,1,0:T(8,128)(2,1)S(1)} custom-call(s32[4]{0:T(128)S(1)} %pad_add_fusion.place_ref.refs_0_, bf16[256,1024]{1,0:T(8,128)(2,1)} %refs_2_.2, s32[8,256]{1,0:T(8,128)} %refs_3_.3), custom_call_target="tpu_custom_call" | custom-call | flops 1150000000 | bytes 1048576 | tf_op jit(solution)/shard_map/pallas_call | solution.py:570
  2.4 0.5 collective-permute-start
  2.9 2.1 %shard_map.94.held_ref = bf16[2,1024,512]{2,1,0:T(8,128)(2,1)S(1)} custom-call(s32[4]{0:T(128)S(1)} %pad_add_fusion.place_ref.refs_0_, bf16[1024,1024]{1,0:T(8,128)(2,1)} %refs_13_.3, bf16[1024,1024]{1,0:T(8,128)(2,1)} %refs_14_.3), custom_call_target="tpu_custom_call" | custom-call | flops 1150000000 | bytes 1048576 | tf_op jit(solution)/shard_map/pallas_call | solution.py:570
  5.0 0.0 collective-permute-done.theirs_ref
  5.0 0.0 collective-permute-done.1.refs_1_.refs_2_
  5.0 2.9 %shard_map.96 = (bf16[528,128]{1,0:T(8,128)(2,1)S(1)}, bf16[528,128]{1,0:T(8,128)(2,1)S(1)}, bf16[528,128]{1,0:T(8,128)(2,1)S(1)}, bf16[528,128]{1,0:T(8,128)(2,1)S(1)}, bf16[2,512,512]{2,1,0:T(8,128)(2,1)S(1)}) custom-call(s32[4]{0:T(128)S(1)} %pad_add_fusion.place_ref.refs_0_, bf16[2,1024,512]{2,1,0:T(8,128)(2,1)S(1)} %shard_map.94.held_ref, ...), custom_call_target="tpu_custom_call" | custom-call | flops 115000000 | bytes 1048576 | tf_op jit(solution)/shard_map/pallas_call | solution.py:570
  8.0 0.1 collective-permute-start.2
  8.1 3.8 %collective-permute-start.7 = (bf16[528,128]{1,0:T(8,128)(2,1)S(1)}, bf16[528,128]{1,0:T(8,128)(2,1)S(1)}, u32[]{:S(2)}, u32[]{:S(2)}) collective-permute-start(bf16[528,128]{1,0:T(8,128)(2,1)S(1)} %get-tuple-element.58), channel_id=1, source_target_pairs={{0,8},{4,12},{8,0},{12,4},{1,9},{5,13},{9,1},{13,5},{2,10},{6,14},... | collective-permute-start | bytes 405512 | tf_op jit(solution)/shard_map/ppermute | solution.py:590
  11.9 1.1 collective-permute-start.8
  12.9 0.0 collective-permute-done.2.refs_0_
  12.9 2.7 %shard_map.98 = bf16[1,512,512]{2,1,0:T(8,128)(2,1)S(1)} custom-call(s32[4]{0:T(128)S(1)} %pad_add_fusion.place_ref.refs_0_, bf16[256,2048]{1,0:T(8,128)(2,1)} %refs_1_.5, bf16[256,2048]{1,0:T(8,128)(2,1)S(1)} %collective-permute-done.1.refs_1_.refs_2_, bf16[1024,1024]{1,0:T(8,128)(2,1)} %refs_15_.3), custom_call_target="tpu_custom_call" | custom-call | flops 115000000 | bytes 1048576 | tf_op jit(solution)/shard_map/pallas_call | solution.py:570
  15.6 0.7 collective-permute-start.6
  16.3 3.6 %shard_map.97 = (bf16[1024,128]{1,0:T(8,128)(2,1)S(1)}, bf16[1024,128]{1,0:T(8,128)(2,1)S(1)}, bf16[1024,128]{1,0:T(8,128)(2,1)S(1)}, bf16[1024,128]{1,0:T(8,128)(2,1)S(1)}) custom-call(s32[4]{0:T(128)S(1)} %pad_add_fusion.place_ref.refs_0_, bf16[2,512,512]{2,1,0:T(8,128)(2,1)S(1)} %collective-permute-done.2.refs_0_, bf16[256,2048]{1,0:T(8,128)(2,1)} %refs_1_.5, ...), custom_call_target="tpu_custom_call" | custom-call | flops 9200000000 | bytes 1048576 | tf_op jit(solution)/shard_map/pallas_call | solution.py:570
  19.9 0.1 collective-permute-start.3
  20.0 2.5 %collective-permute-start.4 = (bf16[1024,128]{1,0:T(8,128)(2,1)S(1)}, bf16[1024,128]{1,0:T(8,128)(2,1)S(1)}, u32[]{:S(2)}, u32[]{:S(2)}) collective-permute-start(bf16[1024,128]{1,0:T(8,128)(2,1)S(1)} %get-tuple-element.55), channel_id=1, source_target_pairs={{0,8},{4,12},{8,0},{12,4},{1,9},{5,13},{9,1},{13,5},{2,10},{6,14},... | collective-permute-start | bytes 786440 | tf_op jit(solution)/shard_map/ppermute | solution.py:590
  22.4 0.0 collective-permute-done.7.refs_6_.refs_10_
  22.4 2.6 %collective-permute-start.5 = (bf16[1024,128]{1,0:T(8,128)(2,1)S(1)}, bf16[1024,128]{1,0:T(8,128)(2,1)S(1)}, u32[]{:S(2)}, u32[]{:S(2)}) collective-permute-start(bf16[1024,128]{1,0:T(8,128)(2,1)S(1)} %get-tuple-element.56), channel_id=1, source_target_pairs={{0,12},{4,8},{8,4},{12,0},{1,13},{5,9},{9,5},{13,1},{2,14},{6,10},... | collective-permute-start | bytes 786440 | tf_op jit(solution)/shard_map/ppermute | solution.py:590
  25.0 0.0 collective-permute-done.8.refs_7_.refs_11_
  25.0 0.1 collective-permute-start.12
  25.1 0.0 collective-permute-done.6.refs_0_
  25.1 2.8 %shard_map.99 = (bf16[512,128]{1,0:T(8,128)(2,1)S(1)}, bf16[512,128]{1,0:T(8,128)(2,1)S(1)}, bf16[512,128]{1,0:T(8,128)(2,1)S(1)}, bf16[512,128]{1,0:T(8,128)(2,1)S(1)}) custom-call(s32[4]{0:T(128)S(1)} %pad_add_fusion.place_ref.refs_0_, bf16[1,512,512]{2,1,0:T(8,128)(2,1)S(1)} %collective-permute-done.6.refs_0_, bf16[256,2048]{1,0:T(8,128)(2,1)} %refs_1_.5, ...), custom_call_target="tpu_custom_call" | custom-call | flops 115000000 | bytes 1048576 | tf_op jit(solution)/shard_map/pallas_call | solution.py:570
  28.0 1.5 %collective-permute-start.9 = (bf16[512,128]{1,0:T(8,128)(2,1)S(1)}, bf16[512,128]{1,0:T(8,128)(2,1)S(1)}, u32[]{:S(2)}, u32[]{:S(2)}) collective-permute-start(bf16[512,128]{1,0:T(8,128)(2,1)S(1)} %get-tuple-element.66), channel_id=1, source_target_pairs={{0,4},{4,0},{8,12},{12,8},{1,5},{5,1},{9,13},{13,9},{2,6},{6,2},{1... | collective-permute-start | bytes 393224 | tf_op jit(solution)/shard_map/ppermute | solution.py:590
  29.4 3.3 %collective-permute-done.3.refs_1_ = bf16[1024,128]{1,0:T(8,128)(2,1)S(1)} collective-permute-done((bf16[1024,128]{1,0:T(8,128)(2,1)S(1)}, bf16[1024,128]{1,0:T(8,128)(2,1)S(1)}, u32[]{:S(2)}, u32[]{:S(2)}) %collective-permute-start.3) | collective-permute-done | bytes 262176 | tf_op jit(solution)/shard_map/ppermute | solution.py:590
  32.7 0.0 collective-permute-start.10
  32.7 8.7 %collective-permute-done.4.refs_2_ = bf16[1024,128]{1,0:T(8,128)(2,1)S(1)} collective-permute-done((bf16[1024,128]{1,0:T(8,128)(2,1)S(1)}, bf16[1024,128]{1,0:T(8,128)(2,1)S(1)}, u32[]{:S(2)}, u32[]{:S(2)}) %collective-permute-start.4) | collective-permute-done | bytes 262176 | tf_op jit(solution)/shard_map/ppermute | solution.py:590
  41.4 3.5 %collective-permute-start.11 = (bf16[512,128]{1,0:T(8,128)(2,1)S(1)}, bf16[512,128]{1,0:T(8,128)(2,1)S(1)}, u32[]{:S(2)}, u32[]{:S(2)}) collective-permute-start(bf16[512,128]{1,0:T(8,128)(2,1)S(1)} %get-tuple-element.68), channel_id=1, source_target_pairs={{0,12},{4,8},{8,4},{12,0},{1,13},{5,9},{9,5},{13,1},{2,14},{6,10},... | collective-permute-start | bytes 393224 | tf_op jit(solution)/shard_map/ppermute | solution.py:590
  44.9 0.0 collective-permute-done.12.refs_5_.refs_9_
  44.9 6.5 %shard_map.100 = (bf16[512,128]{1,0:T(8,128)(2,1)S(1)}, bf16[512,128]{1,0:T(8,128)(2,1)S(1)}, bf16[512,128]{1,0:T(8,128)(2,1)S(1)}, bf16[512,128]{1,0:T(8,128)(2...) custom-call(s32[4]{0:T(128)S(1)} %pad_add_fusion.place_ref.refs_0_, ...), custom_call_target="tpu_custom_call" | custom-call | flops 8049999872 | bytes 1048576 | tf_op jit(solution)/shard_map/pallas_call | solution.py:570
  51.3 10.4 %collective-permute-start.14 = (bf16[512,128]{1,0:T(8,128)(2,1)S(1)}, bf16[512,128]{1,0:T(8,128)(2,1)S(1)}, u32[]{:S(2)}, u32[]{:S(2)}) collective-permute-start(bf16[512,128]{1,0:T(8,128)(2,1)S(1)} %get-tuple-element.83), channel_id=1, source_target_pairs={{0,8},{4,12},{8,0},{12,4},{1,9},{5,13},{9,1},{13,5},{2,10},{6,14},... | collective-permute-start | bytes 393224 | tf_op jit(solution)/shard_map/ppermute | solution.py:590
  61.7 0.0 collective-permute-done.9.refs_5_
  61.7 1.3 %collective-permute-start.26 = (bf16[512,128]{1,0:T(8,128)(2,1)S(1)}, bf16[512,128]{1,0:T(8,128)(2,1)S(1)}, u32[]{:S(2)}, u32[]{:S(2)}) collective-permute-start(bf16[512,128]{1,0:T(8,128)(2,1)S(1)} %get-tuple-element.96), channel_id=1, source_target_pairs={{0,12},{4,8},{8,4},{12,0},{1,13},{5,9},{9,5},{13,1},{2,14},{6,10},... | collective-permute-start | bytes 393224 | tf_op jit(solution)/shard_map/ppermute | solution.py:590
  63.0 7.0 %shard_map.101 = (bf16[1024,128]{1,0:T(8,128)(2,1)S(1)}, bf16[1024,128]{1,0:T(8,128)(2,1)S(1)}, bf16[1024,128]{1,0:T(8,128)(2,1)S(1)}, bf16[1024,128]{1,0:T(8,12...) custom-call(s32[4]{0:T(128)S(1)} %pad_add_fusion.place_ref.refs_0_, ...), custom_call_target="tpu_custom_call" | custom-call | flops 11500000256 | bytes 1048576 | tf_op jit(solution)/shard_map/pallas_call | solution.py:570
  70.0 1.1 collective-permute-start.13
  71.1 2.0 %collective-permute-start.16 = (bf16[1024,128]{1,0:T(8,128)(2,1)S(1)}, bf16[1024,128]{1,0:T(8,128)(2,1)S(1)}, u32[]{:S(2)}, u32[]{:S(2)}) collective-permute-start(bf16[1024,128]{1,0:T(8,128)(2,1)S(1)} %get-tuple-element.85), channel_id=1, source_target_pairs={{0,12},{4,8},{8,4},{12,0},{1,13},{5,9},{9,5},{13,1},{2,14},{6,10},... | collective-permute-start | bytes 786440 | tf_op jit(solution)/shard_map/ppermute | solution.py:590
  73.2 0.0 collective-permute-start.20
  73.2 0.0 collective-permute-done.25.refs_2_.refs_9_
  73.2 1.5 %collective-permute-start.15 = (bf16[1024,128]{1,0:T(8,128)(2,1)S(1)}, bf16[1024,128]{1,0:T(8,128)(2,1)S(1)}, u32[]{:S(2)}, u32[]{:S(2)}) collective-permute-start(bf16[1024,128]{1,0:T(8,128)(2,1)S(1)} %get-tuple-element.84), channel_id=1, source_target_pairs={{0,8},{4,12},{8,0},{12,4},{1,9},{5,13},{9,1},{13,5},{2,10},{6,14},... | collective-permute-start | bytes 786440 | tf_op jit(solution)/shard_map/ppermute | solution.py:590
  74.7 0.0 collective-permute-done.26.refs_4_.refs_11_
  74.7 0.6 shard_map.104
  75.3 1.9 %collective-permute-start.27 = (bf16[4,512,128]{2,1,0:T(8,128)(2,1)S(1)}, bf16[4,512,128]{2,1,0:T(8,128)(2,1)S(1)}, u32[]{:S(2)}, u32[]{:S(2)}) collective-permute-start(bf16[4,512,128]{2,1,0:T(8,128)(2,1)S(1)} %shard_map.104), channel_id=1, source_target_pairs={{0,1},{1,0},{2,3},{3,2},{4,5},{5,4},{6,7},{7,6},{8,9},{9,8},{10,11... | collective-permute-start | bytes 1572872 | tf_op jit(solution)/shard_map/ppermute | solution.py:596
  77.2 2.8 %collective-permute-done.16.refs_3_ = bf16[1024,128]{1,0:T(8,128)(2,1)S(1)} collective-permute-done((bf16[1024,128]{1,0:T(8,128)(2,1)S(1)}, bf16[1024,128]{1,0:T(8,128)(2,1)S(1)}, u32[]{:S(2)}, u32[]{:S(2)}) %collective-permute-start.16) | collective-permute-done | bytes 262176 | tf_op jit(solution)/shard_map/ppermute | solution.py:590
  79.9 3.3 %collective-permute-start.21 = (bf16[1024,128]{1,0:T(8,128)(2,1)S(1)}, bf16[1024,128]{1,0:T(8,128)(2,1)S(1)}, u32[]{:S(2)}, u32[]{:S(2)}) collective-permute-start(bf16[1024,128]{1,0:T(8,128)(2,1)S(1)} %get-tuple-element.91.refs_0_), channel_id=1, source_target_pairs={{0,1},{1,0},{2,3},{3,2},{4,5},{5,4},{6,7},{7,6},{8,9},{9,8},{10,11... | collective-permute-start | bytes 786440 | tf_op jit(solution)/shard_map/ppermute | solution.py:596
  83.2 5.2 %collective-permute-done.20.refs_1_ = bf16[1024,128]{1,0:T(8,128)(2,1)S(1)} collective-permute-done((bf16[1024,128]{1,0:T(8,128)(2,1)S(1)}, bf16[1024,128]{1,0:T(8,128)(2,1)S(1)}, u32[]{:S(2)}, u32[]{:S(2)}) %collective-permute-start.20) | collective-permute-done | bytes 262176 | tf_op jit(solution)/shard_map/ppermute | solution.py:590
  88.4 0.5 collective-permute-start.24
  88.9 0.0 collective-permute-start.22
  88.9 0.6 shard_map.102
  89.5 7.1 %collective-permute-done.15.refs_2_ = bf16[1024,128]{1,0:T(8,128)(2,1)S(1)} collective-permute-done((bf16[1024,128]{1,0:T(8,128)(2,1)S(1)}, bf16[1024,128]{1,0:T(8,128)(2,1)S(1)}, u32[]{:S(2)}, u32[]{:S(2)}) %collective-permute-start.15) | collective-permute-done | bytes 262176 | tf_op jit(solution)/shard_map/ppermute | solution.py:590
  96.6 0.5 collective-permute-start.23
  97.1 0.0 collective-permute-done.21.refs_4_
  97.1 0.0 collective-permute-start.17
  97.1 2.5 %collective-permute-start.18 = (bf16[576,128]{1,0:T(8,128)(2,1)S(1)}, bf16[576,128]{1,0:T(8,128)(2,1)S(1)}, u32[]{:S(2)}, u32[]{:S(2)}) collective-permute-start(bf16[576,128]{1,0:T(8,128)(2,1)S(1)} %get-tuple-element.88), channel_id=1, source_target_pairs={{0,8},{4,12},{8,0},{12,4},{1,9},{5,13},{9,1},{13,5},{2,10},{6,14},... | collective-permute-start | bytes 442376 | tf_op jit(solution)/shard_map/ppermute | solution.py:590
  99.6 1.1 collective-permute-start.19
  100.7 2.9 %shard_map.105 = bf16[256,1024]{1,0:T(8,128)(2,1)S(1)} custom-call(s32[4]{0:T(128)S(1)} %pad_add_fusion.place_ref.refs_0_, bf16[1024,128]{1,0:T(8,128)(2,1)S(1)} %get-tuple-element.91.refs_0_, bf16[1024,128]{1,0:T(8,128)(2,1)S(1)} %collective-permute-done.20.refs_1_, bf16[1024,128]{1,0:T(8,128)(2,1)S(1)} %collective-permute-done.15.refs_2_, ...), custom_call_target="tpu_custom_call" | custom-call | flops 1150000000 | bytes 1048576 | tf_op jit(solution)/shard_map/pallas_call | solution.py:570
  103.6 1.2 %collective-permute-start.28 = (bf16[256,1024]{1,0:T(8,128)(2,1)S(1)}, bf16[256,1024]{1,0:T(8,128)(2,1)S(1)}, u32[]{:S(2)}, u32[]{:S(2)}) collective-permute-start(bf16[256,1024]{1,0:T(8,128)(2,1)S(1)} %shard_map.105), channel_id=1, source_target_pairs={{0,1},{1,3},{3,2},{2,0},{4,5},{5,7},{7,6},{6,4},{8,9},{9,11},{11,1... | collective-permute-start | bytes 1572872 | tf_op jit(solution)/shard_map/ppermute | solution.py:744
  104.9 2.9 %shard_map.106.kept_ref = bf16[256,1024]{1,0:T(8,128)(2,1)S(1)} custom-call(s32[4]{0:T(128)S(1)} %pad_add_fusion.place_ref.refs_0_, bf16[1024,128]{1,0:T(8,128)(2,1)S(1)} %get-tuple-element.91.refs_0_, bf16[1024,128]{1,0:T(8,128)(2,1)S(1)} %collective-permute-done.20.refs_1_, bf16[1024,128]{1,0:T(8,128)(2,1)S(1)} %collective-permute-done.15.refs_2_, ...), custom_call_target="tpu_custom_call" | custom-call | flops 1150000000 | bytes 1048576 | tf_op jit(solution)/shard_map/pallas_call | solution.py:570
  107.8 3.2 %collective-permute-start.29 = (bf16[256,1024]{1,0:T(8,128)(2,1)S(1)}, bf16[256,1024]{1,0:T(8,128)(2,1)S(1)}, u32[]{:S(2)}, u32[]{:S(2)}) collective-permute-start(bf16[256,1024]{1,0:T(8,128)(2,1)S(1)} %shard_map.106.kept_ref), channel_id=1, source_target_pairs={{1,2},{2,1},{5,6},{6,5},{9,10},{10,9},{13,14},{14,13},{17,18},{18,... | collective-permute-start | bytes 1572872 | tf_op jit(solution)/shard_map/ppermute | solution.py:746
  110.9 0.0 collective-permute-done.17.refs_1_
  111.0 0.0 collective-permute-done.19.refs_3_
  111.0 1.5 %shard_map.103 = (bf16[256,1024]{1,0:T(8,128)(2,1)}, f32[8,32,128]{2,1,0:T(8,128)}) custom-call(s32[4]{0:T(128)S(1)} %pad_add_fusion.place_ref.refs_0_, bf16[576,128]{1,0:T(8,128)(2,1)S(1)} %get-tuple-element.86.refs_0_, bf16[576,128]{1,0:T(8,128)(2,1)S(1)} %collective-permute-done.17.refs_1_, bf16[576,128]{1,0:T(8,128)(2,1)S(1)} %collective-permute-done.18.refs_2_, ...), custom_call_target="tpu_custom_call" | custom-call | flops 9200000000 | bytes 1048576 | tf_op jit(solution)/shard_map/pallas_call | solution.py:570
  112.5 6.1 %collective-permute-done.29.second_ref = bf16[256,1024]{1,0:T(8,128)(2,1)S(1)} collective-permute-done((bf16[256,1024]{1,0:T(8,128)(2,1)S(1)}, bf16[256,1024]{1,0:T(8,128)(2,1)S(1)}, u32[]{:S(2)}, u32[]{:S(2)}) %collective-permute-start.29) | collective-permute-done | bytes 524320 | tf_op jit(solution)/shard_map/ppermute | solution.py:746
  118.6 0.0 collective-permute-done.28.first_ref
  118.6 1.5 %shard_map.107 = bf16[256,1024]{1,0:T(8,128)(2,1)} custom-call(s32[4]{0:T(128)S(1)} %pad_add_fusion.place_ref.refs_0_, bf16[256,1024]{1,0:T(8,128)(2,1)S(1)} %collective-permute-done.28.first_ref, bf16[256,1024]{1,0:T(8,128)(2,1)S(1)} %collective-permute-done.29.second_ref, bf16[256,1024]{1,0:T(8,128)(2,1)S(1)} %shard_map.106.kept_ref), custom_call_target="tpu_custom_call" | custom-call | flops 1150000000 | bytes 1048576 | tf_op jit(solution)/shard_map/pallas_call | solution.py:570
  (19 shorter events, 0.0 us)
Async XLA Ops:
  0.6 4.4 %collective-permute-start.1 = (bf16[256,2048]{1,0:T(8,128)(2,1)}, bf16[256,2048]{1,0:T(8,128)(2,1)S(1)}, u32[]{:S(2)}, u32[]{:S(2)}) collective-permute-start(bf16[256,2048]{1,0:T(8,128)(2,1)} %refs_1_.5), channel_id=1, source_target_pairs={{0,1},{1,0},{2,3},{3,2},{4,5},{5,4},{6,7},{7,6},{8,9},{9,8},{10,11... | collective-permute-start | bytes 3145736 | tf_op jit(solution)/shard_map/ppermute | solution.py:596
  2.4 2.6 %collective-permute-start = (bf16[4,272,128]{2,1,0:T(8,128)(2,1)S(1)}, bf16[4,272,128]{2,1,0:T(8,128)(2,1)S(1)}, u32[]{:S(2)}, u32[]{:S(2)}) collective-permute-start(bf16[4,272,128]{2,1,0:T(8,128)(2,1)S(1)} %shard_map.95), channel_id=1, source_target_pairs={{0,1},{1,0},{2,3},{3,2},{4,5},{5,4},{6,7},{7,6},{8,9},{9,8},{10,11... | collective-permute-start | bytes 835592 | tf_op jit(solution)/shard_map/ppermute | solution.py:596
  8.0 5.0 %collective-permute-start.2 = (bf16[2,512,512]{2,1,0:T(8,128)(2,1)S(1)}, bf16[2,512,512]{2,1,0:T(8,128)(2,1)S(1)}, u32[]{:S(2)}, u32[]{:S(2)}) collective-permute-start(bf16[2,512,512]{2,1,0:T(8,128)(2,1)S(1)} %get-tuple-element.52), channel_id=1, source_target_pairs={{0,1},{1,0},{2,3},{3,2},{4,5},{5,4},{6,7},{7,6},{8,9},{9,8},{10,11... | collective-permute-start | bytes 3145736 | tf_op jit(solution)/shard_map/ppermute | solution.py:596
  8.1 14.3 %collective-permute-start.7 = (bf16[528,128]{1,0:T(8,128)(2,1)S(1)}, bf16[528,128]{1,0:T(8,128)(2,1)S(1)}, u32[]{:S(2)}, u32[]{:S(2)}) collective-permute-start(bf16[528,128]{1,0:T(8,128)(2,1)S(1)} %get-tuple-element.58), channel_id=1, source_target_pairs={{0,8},{4,12},{8,0},{12,4},{1,9},{5,13},{9,1},{13,5},{2,10},{6,14},... | collective-permute-start | bytes 405512 | tf_op jit(solution)/shard_map/ppermute | solution.py:590
  11.9 13.2 %collective-permute-start.8 = (bf16[528,128]{1,0:T(8,128)(2,1)S(1)}, bf16[528,128]{1,0:T(8,128)(2,1)S(1)}, u32[]{:S(2)}, u32[]{:S(2)}) collective-permute-start(bf16[528,128]{1,0:T(8,128)(2,1)S(1)} %get-tuple-element.59), channel_id=1, source_target_pairs={{0,12},{4,8},{8,4},{12,0},{1,13},{5,9},{9,5},{13,1},{2,14},{6,10},... | collective-permute-start | bytes 405512 | tf_op jit(solution)/shard_map/ppermute | solution.py:590
  15.6 9.5 %collective-permute-start.6 = (bf16[1,512,512]{2,1,0:T(8,128)(2,1)S(1)}, bf16[1,512,512]{2,1,0:T(8,128)(2,1)S(1)}, u32[]{:S(2)}, u32[]{:S(2)}) collective-permute-start(bf16[1,512,512]{2,1,0:T(8,128)(2,1)S(1)} %shard_map.98), channel_id=1, source_target_pairs={{0,1},{1,0},{2,3},{3,2},{4,5},{5,4},{6,7},{7,6},{8,9},{9,8},{10,11... | collective-permute-start | bytes 1572872 | tf_op jit(solution)/shard_map/ppermute | solution.py:596
  19.9 12.8 %collective-permute-start.3 = (bf16[1024,128]{1,0:T(8,128)(2,1)S(1)}, bf16[1024,128]{1,0:T(8,128)(2,1)S(1)}, u32[]{:S(2)}, u32[]{:S(2)}) collective-permute-start(bf16[1024,128]{1,0:T(8,128)(2,1)S(1)} %get-tuple-element.54), channel_id=1, source_target_pairs={{0,4},{4,0},{8,12},{12,8},{1,5},{5,1},{9,13},{13,9},{2,6},{6,2},{1... | collective-permute-start | bytes 786440 | tf_op jit(solution)/shard_map/ppermute | solution.py:590
  20.0 21.4 %collective-permute-start.4 = (bf16[1024,128]{1,0:T(8,128)(2,1)S(1)}, bf16[1024,128]{1,0:T(8,128)(2,1)S(1)}, u32[]{:S(2)}, u32[]{:S(2)}) collective-permute-start(bf16[1024,128]{1,0:T(8,128)(2,1)S(1)} %get-tuple-element.55), channel_id=1, source_target_pairs={{0,8},{4,12},{8,0},{12,4},{1,9},{5,13},{9,1},{13,5},{2,10},{6,14},... | collective-permute-start | bytes 786440 | tf_op jit(solution)/shard_map/ppermute | solution.py:590
  22.4 22.4 %collective-permute-start.5 = (bf16[1024,128]{1,0:T(8,128)(2,1)S(1)}, bf16[1024,128]{1,0:T(8,128)(2,1)S(1)}, u32[]{:S(2)}, u32[]{:S(2)}) collective-permute-start(bf16[1024,128]{1,0:T(8,128)(2,1)S(1)} %get-tuple-element.56), channel_id=1, source_target_pairs={{0,12},{4,8},{8,4},{12,0},{1,13},{5,9},{9,5},{13,1},{2,14},{6,10},... | collective-permute-start | bytes 786440 | tf_op jit(solution)/shard_map/ppermute | solution.py:590
  25.0 19.8 %copy-start.3 = (s32[256]{0:T(256)S(1)}, s32[256]{0:T(256)}, u32[]{:S(2)}) copy-start(s32[256]{0:T(256)} %param.11) | copy-start | bytes 3076
  25.0 19.8 %collective-permute-start.12 = (bf16[528,128]{1,0:T(8,128)(2,1)S(1)}, bf16[528,128]{1,0:T(8,128)(2,1)S(1)}, u32[]{:S(2)}, u32[]{:S(2)}) collective-permute-start(bf16[528,128]{1,0:T(8,128)(2,1)S(1)} %get-tuple-element.70), channel_id=1, source_target_pairs={{0,4},{4,0},{8,12},{12,8},{1,5},{5,1},{9,13},{13,9},{2,6},{6,2},{1... | collective-permute-start | bytes 405512 | tf_op jit(solution)/shard_map/ppermute | solution.py:590
  28.0 33.8 %collective-permute-start.9 = (bf16[512,128]{1,0:T(8,128)(2,1)S(1)}, bf16[512,128]{1,0:T(8,128)(2,1)S(1)}, u32[]{:S(2)}, u32[]{:S(2)}) collective-permute-start(bf16[512,128]{1,0:T(8,128)(2,1)S(1)} %get-tuple-element.66), channel_id=1, source_target_pairs={{0,4},{4,0},{8,12},{12,8},{1,5},{5,1},{9,13},{13,9},{2,6},{6,2},{1... | collective-permute-start | bytes 393224 | tf_op jit(solution)/shard_map/ppermute | solution.py:590
  32.7 30.3 %collective-permute-start.10 = (bf16[512,128]{1,0:T(8,128)(2,1)S(1)}, bf16[512,128]{1,0:T(8,128)(2,1)S(1)}, u32[]{:S(2)}, u32[]{:S(2)}) collective-permute-start(bf16[512,128]{1,0:T(8,128)(2,1)S(1)} %get-tuple-element.67), channel_id=1, source_target_pairs={{0,8},{4,12},{8,0},{12,4},{1,9},{5,13},{9,1},{13,5},{2,10},{6,14},... | collective-permute-start | bytes 393224 | tf_op jit(solution)/shard_map/ppermute | solution.py:590
  41.4 21.6 %collective-permute-start.11 = (bf16[512,128]{1,0:T(8,128)(2,1)S(1)}, bf16[512,128]{1,0:T(8,128)(2,1)S(1)}, u32[]{:S(2)}, u32[]{:S(2)}) collective-permute-start(bf16[512,128]{1,0:T(8,128)(2,1)S(1)} %get-tuple-element.68), channel_id=1, source_target_pairs={{0,12},{4,8},{8,4},{12,0},{1,13},{5,9},{9,5},{13,1},{2,14},{6,10},... | collective-permute-start | bytes 393224 | tf_op jit(solution)/shard_map/ppermute | solution.py:590
  51.3 19.8 %collective-permute-start.14 = (bf16[512,128]{1,0:T(8,128)(2,1)S(1)}, bf16[512,128]{1,0:T(8,128)(2,1)S(1)}, u32[]{:S(2)}, u32[]{:S(2)}) collective-permute-start(bf16[512,128]{1,0:T(8,128)(2,1)S(1)} %get-tuple-element.83), channel_id=1, source_target_pairs={{0,8},{4,12},{8,0},{12,4},{1,9},{5,13},{9,1},{13,5},{2,10},{6,14},... | collective-permute-start | bytes 393224 | tf_op jit(solution)/shard_map/ppermute | solution.py:590
  61.7 11.4 %collective-permute-start.25 = (bf16[512,128]{1,0:T(8,128)(2,1)S(1)}, bf16[512,128]{1,0:T(8,128)(2,1)S(1)}, u32[]{:S(2)}, u32[]{:S(2)}) collective-permute-start(bf16[512,128]{1,0:T(8,128)(2,1)S(1)} %get-tuple-element.95), channel_id=1, source_target_pairs={{0,4},{4,0},{8,12},{12,8},{1,5},{5,1},{9,13},{13,9},{2,6},{6,2},{1... | collective-permute-start | bytes 393224 | tf_op jit(solution)/shard_map/ppermute | solution.py:590
  61.7 13.0 %collective-permute-start.26 = (bf16[512,128]{1,0:T(8,128)(2,1)S(1)}, bf16[512,128]{1,0:T(8,128)(2,1)S(1)}, u32[]{:S(2)}, u32[]{:S(2)}) collective-permute-start(bf16[512,128]{1,0:T(8,128)(2,1)S(1)} %get-tuple-element.96), channel_id=1, source_target_pairs={{0,12},{4,8},{8,4},{12,0},{1,13},{5,9},{9,5},{13,1},{2,14},{6,10},... | collective-permute-start | bytes 393224 | tf_op jit(solution)/shard_map/ppermute | solution.py:590
  70.0 18.8 %collective-permute-start.13 = (bf16[4,288,128]{2,1,0:T(8,128)(2,1)S(1)}, bf16[4,288,128]{2,1,0:T(8,128)(2,1)S(1)}, u32[]{:S(2)}, u32[]{:S(2)}) collective-permute-start(bf16[4,288,128]{2,1,0:T(8,128)(2,1)S(1)} %get-tuple-element.74), channel_id=1, source_target_pairs={{0,1},{1,0},{2,3},{3,2},{4,5},{5,4},{6,7},{7,6},{8,9},{9,8},{10,11... | collective-permute-start | bytes 884744 | tf_op jit(solution)/shard_map/ppermute | solution.py:596
  71.1 8.8 %collective-permute-start.16 = (bf16[1024,128]{1,0:T(8,128)(2,1)S(1)}, bf16[1024,128]{1,0:T(8,128)(2,1)S(1)}, u32[]{:S(2)}, u32[]{:S(2)}) collective-permute-start(bf16[1024,128]{1,0:T(8,128)(2,1)S(1)} %get-tuple-element.85), channel_id=1, source_target_pairs={{0,12},{4,8},{8,4},{12,0},{1,13},{5,9},{9,5},{13,1},{2,14},{6,10},... | collective-permute-start | bytes 786440 | tf_op jit(solution)/shard_map/ppermute | solution.py:590
  73.2 15.2 %collective-permute-start.20 = (bf16[1024,128]{1,0:T(8,128)(2,1)S(1)}, bf16[1024,128]{1,0:T(8,128)(2,1)S(1)}, u32[]{:S(2)}, u32[]{:S(2)}) collective-permute-start(bf16[1024,128]{1,0:T(8,128)(2,1)S(1)} %get-tuple-element.92), channel_id=1, source_target_pairs={{0,4},{4,0},{8,12},{12,8},{1,5},{5,1},{9,13},{13,9},{2,6},{6,2},{1... | collective-permute-start | bytes 786440 | tf_op jit(solution)/shard_map/ppermute | solution.py:590
  73.2 23.4 %collective-permute-start.15 = (bf16[1024,128]{1,0:T(8,128)(2,1)S(1)}, bf16[1024,128]{1,0:T(8,128)(2,1)S(1)}, u32[]{:S(2)}, u32[]{:S(2)}) collective-permute-start(bf16[1024,128]{1,0:T(8,128)(2,1)S(1)} %get-tuple-element.84), channel_id=1, source_target_pairs={{0,8},{4,12},{8,0},{12,4},{1,9},{5,13},{9,1},{13,5},{2,10},{6,14},... | collective-permute-start | bytes 786440 | tf_op jit(solution)/shard_map/ppermute | solution.py:590
  74.7 26.0 %copy-start.2 = (bf16[1024,1024]{1,0:T(8,128)(2,1)S(1)}, bf16[1024,1024]{1,0:T(8,128)(2,1)}, u32[]{:S(2)}) copy-start(bf16[1024,1024]{1,0:T(8,128)(2,1)} %refs_14_.3) | copy-start | bytes 6291460
  75.3 25.4 %collective-permute-start.27 = (bf16[4,512,128]{2,1,0:T(8,128)(2,1)S(1)}, bf16[4,512,128]{2,1,0:T(8,128)(2,1)S(1)}, u32[]{:S(2)}, u32[]{:S(2)}) collective-permute-start(bf16[4,512,128]{2,1,0:T(8,128)(2,1)S(1)} %shard_map.104), channel_id=1, source_target_pairs={{0,1},{1,0},{2,3},{3,2},{4,5},{5,4},{6,7},{7,6},{8,9},{9,8},{10,11... | collective-permute-start | bytes 1572872 | tf_op jit(solution)/shard_map/ppermute | solution.py:596
  79.9 17.2 %collective-permute-start.21 = (bf16[1024,128]{1,0:T(8,128)(2,1)S(1)}, bf16[1024,128]{1,0:T(8,128)(2,1)S(1)}, u32[]{:S(2)}, u32[]{:S(2)}) collective-permute-start(bf16[1024,128]{1,0:T(8,128)(2,1)S(1)} %get-tuple-element.91.refs_0_), channel_id=1, source_target_pairs={{0,1},{1,0},{2,3},{3,2},{4,5},{5,4},{6,7},{7,6},{8,9},{9,8},{10,11... | collective-permute-start | bytes 786440 | tf_op jit(solution)/shard_map/ppermute | solution.py:596
  88.4 8.8 %collective-permute-start.24 = (bf16[1024,128]{1,0:T(8,128)(2,1)S(1)}, bf16[1024,128]{1,0:T(8,128)(2,1)S(1)}, u32[]{:S(2)}, u32[]{:S(2)}) collective-permute-start(bf16[1024,128]{1,0:T(8,128)(2,1)S(1)} %collective-permute-done.16.refs_3_), channel_id=1, source_target_pairs={{0,1},{1,0},{2,3},{3,2},{4,5},{5,4},{6,7},{7,6},{8,9},{9,8},{10,11... | collective-permute-start | bytes 786440 | tf_op jit(solution)/shard_map/ppermute | solution.py:596
  88.9 10.7 %collective-permute-start.22 = (bf16[1024,128]{1,0:T(8,128)(2,1)S(1)}, bf16[1024,128]{1,0:T(8,128)(2,1)S(1)}, u32[]{:S(2)}, u32[]{:S(2)}) collective-permute-start(bf16[1024,128]{1,0:T(8,128)(2,1)S(1)} %collective-permute-done.20.refs_1_), channel_id=1, source_target_pairs={{0,1},{1,0},{2,3},{3,2},{4,5},{5,4},{6,7},{7,6},{8,9},{9,8},{10,11... | collective-permute-start | bytes 786440 | tf_op jit(solution)/shard_map/ppermute | solution.py:596
  88.9 11.8 %copy-start = (bf16[1024,1024]{1,0:T(8,128)(2,1)S(1)}, bf16[1024,1024]{1,0:T(8,128)(2,1)}, u32[]{:S(2)}) copy-start(bf16[1024,1024]{1,0:T(8,128)(2,1)} %refs_15_.3) | copy-start | bytes 6291460
  88.9 11.8 %copy-start.1 = (bf16[1024,1024]{1,0:T(8,128)(2,1)S(1)}, bf16[1024,1024]{1,0:T(8,128)(2,1)}, u32[]{:S(2)}) copy-start(bf16[1024,1024]{1,0:T(8,128)(2,1)} %refs_13_.3) | copy-start | bytes 6291460
  96.6 4.1 %collective-permute-start.23 = (bf16[1024,128]{1,0:T(8,128)(2,1)S(1)}, bf16[1024,128]{1,0:T(8,128)(2,1)S(1)}, u32[]{:S(2)}, u32[]{:S(2)}) collective-permute-start(bf16[1024,128]{1,0:T(8,128)(2,1)S(1)} %collective-permute-done.15.refs_2_), channel_id=1, source_target_pairs={{0,1},{1,0},{2,3},{3,2},{4,5},{5,4},{6,7},{7,6},{8,9},{9,8},{10,11... | collective-permute-start | bytes 786440 | tf_op jit(solution)/shard_map/ppermute | solution.py:596
  97.1 13.8 %collective-permute-start.17 = (bf16[576,128]{1,0:T(8,128)(2,1)S(1)}, bf16[576,128]{1,0:T(8,128)(2,1)S(1)}, u32[]{:S(2)}, u32[]{:S(2)}) collective-permute-start(bf16[576,128]{1,0:T(8,128)(2,1)S(1)} %get-tuple-element.87), channel_id=1, source_target_pairs={{0,4},{4,0},{8,12},{12,8},{1,5},{5,1},{9,13},{13,9},{2,6},{6,2},{1... | collective-permute-start | bytes 442376 | tf_op jit(solution)/shard_map/ppermute | solution.py:590
  97.1 13.8 %collective-permute-start.18 = (bf16[576,128]{1,0:T(8,128)(2,1)S(1)}, bf16[576,128]{1,0:T(8,128)(2,1)S(1)}, u32[]{:S(2)}, u32[]{:S(2)}) collective-permute-start(bf16[576,128]{1,0:T(8,128)(2,1)S(1)} %get-tuple-element.88), channel_id=1, source_target_pairs={{0,8},{4,12},{8,0},{12,4},{1,9},{5,13},{9,1},{13,5},{2,10},{6,14},... | collective-permute-start | bytes 442376 | tf_op jit(solution)/shard_map/ppermute | solution.py:590
  99.6 11.4 %collective-permute-start.19 = (bf16[576,128]{1,0:T(8,128)(2,1)S(1)}, bf16[576,128]{1,0:T(8,128)(2,1)S(1)}, u32[]{:S(2)}, u32[]{:S(2)}) collective-permute-start(bf16[576,128]{1,0:T(8,128)(2,1)S(1)} %get-tuple-element.89), channel_id=1, source_target_pairs={{0,12},{4,8},{8,4},{12,0},{1,13},{5,9},{9,5},{13,1},{2,14},{6,10},... | collective-permute-start | bytes 442376 | tf_op jit(solution)/shard_map/ppermute | solution.py:590
  103.6 15.0 %collective-permute-start.28 = (bf16[256,1024]{1,0:T(8,128)(2,1)S(1)}, bf16[256,1024]{1,0:T(8,128)(2,1)S(1)}, u32[]{:S(2)}, u32[]{:S(2)}) collective-permute-start(bf16[256,1024]{1,0:T(8,128)(2,1)S(1)} %shard_map.105), channel_id=1, source_target_pairs={{0,1},{1,3},{3,2},{2,0},{4,5},{5,7},{7,6},{6,4},{8,9},{9,11},{11,1... | collective-permute-start | bytes 1572872 | tf_op jit(solution)/shard_map/ppermute | solution.py:744
  107.8 10.8 %collective-permute-start.29 = (bf16[256,1024]{1,0:T(8,128)(2,1)S(1)}, bf16[256,1024]{1,0:T(8,128)(2,1)S(1)}, u32[]{:S(2)}, u32[]{:S(2)}) collective-permute-start(bf16[256,1024]{1,0:T(8,128)(2,1)S(1)} %shard_map.106.kept_ref), channel_id=1, source_target_pairs={{1,2},{2,1},{5,6},{6,5},{9,10},{10,9},{13,14},{14,13},{17,18},{18,... | collective-permute-start | bytes 1572872 | tf_op jit(solution)/shard_map/ppermute | solution.py:746

commit v19 on v18

--- a/solution.py
+++ b/solution.py
@@ -627,7 +627,7 @@
                 pltpu.VMEM((2 * rows, half), jnp.bfloat16),
                 pltpu.VMEM((number, half, width // 2), jnp.bfloat16),
                 pltpu.VMEM((2 * rows, width // 2), jnp.bfloat16),
-                pltpu.SemaphoreType.DMA((number, 4)),
+                pltpu.SemaphoreType.DMA((number, 8)),
                 pltpu.SemaphoreType.DMA((2,)),
             ],
             hbm=2 + number,
@@ -641,7 +641,7 @@
         pltpu.VMEM((2, half, width // 2), jnp.bfloat16),
         place,
         *(stay(weight) for weight in early),
-        scratch=[pltpu.SemaphoreType.DMA((2, 4))],
+        scratch=[pltpu.SemaphoreType.DMA((2, 8))],
         hbm=2,
     )
     *merged, early_part = call(

time: 120 us -> 121 us (level)
  no operation moved by 1% of the time
where the time goes in v19:
time: 121 us; the launch traced here: 120 us
  starting transfers between devices  46.7 us (39%)
  Pallas kernels  39.4 us (33%)
  waiting for transfers between devices  33.2 us (27%)
    pallas_call x14, Pallas kernels, call(): pl.pallas_call(kernel, out_shape=outs, in_specs=[smem] + [vmem] * (len(op...  39.4 us
    ppermute x18, starting transfers between devices, exchange(): lax.ppermute(parts[offset], 'seq', [(at, at ^ offset) for at in range(chi...  33.6 us
    ppermute x18, waiting for transfers between devices, exchange(): lax.ppermute(parts[offset], 'seq', [(at, at ^ offset) for at in range(chi...  27 us
    ppermute x10, starting transfers between devices, to_sibling(): return lax.ppermute(piece, 'sub', swap)  8.7 us
    ppermute x1, waiting for transfers between devices, by_head(): second = lax.ppermute(kept, square, [(1, 2), (2, 1)])  6.1 us
    ppermute x1, starting transfers between devices, by_head(): second = lax.ppermute(kept, square, [(1, 2), (2, 1)])  3.18 us
  transfers between devices with their start and end apart: 30, of which 6 were waited for; matrix products, arithmetic and copies ran while one was open for 0% of the time, Pallas kernels for 29%

profile of v19, /device:TPU:1, one launch (start us, length us, event | category | flops | bytes accessed | tf_op | source)
XLA Modules:
  0.0 120.3 jit_solution(2015804903376113951)
XLA Ops:
  0.6 0.1 collective-permute-start.1
  0.8 0.1 pad_add_fusion.place_ref.refs_0_
  0.8 1.5 %shard_map.95 = bf16[4,272,128]{2,1,0:T(8,128)(2,1)S(1)} custom-call(s32[4]{0:T(128)S(1)} %pad_add_fusion.place_ref.refs_0_, bf16[256,1024]{1,0:T(8,128)(2,1)} %refs_2_.2, s32[8,256]{1,0:T(8,128)} %refs_3_.3), custom_call_target="tpu_custom_call" | custom-call | flops 1150000000 | bytes 1048576 | tf_op jit(solution)/shard_map/pallas_call | solution.py:570
  2.4 0.5 collective-permute-start
  2.9 2.3 %shard_map.94.held_ref = bf16[2,1024,512]{2,1,0:T(8,128)(2,1)S(1)} custom-call(s32[4]{0:T(128)S(1)} %pad_add_fusion.place_ref.refs_0_, bf16[1024,1024]{1,0:T(8,128)(2,1)} %refs_13_.3, bf16[1024,1024]{1,0:T(8,128)(2,1)} %refs_14_.3), custom_call_target="tpu_custom_call" | custom-call | flops 1150000000 | bytes 1048576 | tf_op jit(solution)/shard_map/pallas_call | solution.py:570
  5.2 0.0 collective-permute-done.theirs_ref
  5.2 0.0 collective-permute-done.1.refs_1_.refs_2_
  5.2 2.9 %shard_map.96 = (bf16[528,128]{1,0:T(8,128)(2,1)S(1)}, bf16[528,128]{1,0:T(8,128)(2,1)S(1)}, bf16[528,128]{1,0:T(8,128)(2,1)S(1)}, bf16[528,128]{1,0:T(8,128)(2,1)S(1)}, bf16[2,512,512]{2,1,0:T(8,128)(2,1)S(1)}) custom-call(s32[4]{0:T(128)S(1)} %pad_add_fusion.place_ref.refs_0_, bf16[2,1024,512]{2,1,0:T(8,128)(2,1)S(1)} %shard_map.94.held_ref, ...), custom_call_target="tpu_custom_call" | custom-call | flops 115000000 | bytes 1048576 | tf_op jit(solution)/shard_map/pallas_call | solution.py:570
  8.1 0.1 collective-permute-start.2
  8.3 3.8 %collective-permute-start.7 = (bf16[528,128]{1,0:T(8,128)(2,1)S(1)}, bf16[528,128]{1,0:T(8,128)(2,1)S(1)}, u32[]{:S(2)}, u32[]{:S(2)}) collective-permute-start(bf16[528,128]{1,0:T(8,128)(2,1)S(1)} %get-tuple-element.58), channel_id=1, source_target_pairs={{0,8},{4,12},{8,0},{12,4},{1,9},{5,13},{9,1},{13,5},{2,10},{6,14},... | collective-permute-start | bytes 405512 | tf_op jit(solution)/shard_map/ppermute | solution.py:590
  12.0 1.1 collective-permute-start.8
  13.1 0.0 collective-permute-done.2.refs_0_
  13.1 2.7 %shard_map.98 = bf16[1,512,512]{2,1,0:T(8,128)(2,1)S(1)} custom-call(s32[4]{0:T(128)S(1)} %pad_add_fusion.place_ref.refs_0_, bf16[256,2048]{1,0:T(8,128)(2,1)} %refs_1_.5, bf16[256,2048]{1,0:T(8,128)(2,1)S(1)} %collective-permute-done.1.refs_1_.refs_2_, bf16[1024,1024]{1,0:T(8,128)(2,1)} %refs_15_.3), custom_call_target="tpu_custom_call" | custom-call | flops 115000000 | bytes 1048576 | tf_op jit(solution)/shard_map/pallas_call | solution.py:570
  15.8 0.7 collective-permute-start.6
  16.5 3.7 %shard_map.97 = (bf16[1024,128]{1,0:T(8,128)(2,1)S(1)}, bf16[1024,128]{1,0:T(8,128)(2,1)S(1)}, bf16[1024,128]{1,0:T(8,128)(2,1)S(1)}, bf16[1024,128]{1,0:T(8,128)(2,1)S(1)}) custom-call(s32[4]{0:T(128)S(1)} %pad_add_fusion.place_ref.refs_0_, bf16[2,512,512]{2,1,0:T(8,128)(2,1)S(1)} %collective-permute-done.2.refs_0_, bf16[256,2048]{1,0:T(8,128)(2,1)} %refs_1_.5, ...), custom_call_target="tpu_custom_call" | custom-call | flops 9200000000 | bytes 1048576 | tf_op jit(solution)/shard_map/pallas_call | solution.py:570
  20.2 0.1 collective-permute-start.3
  20.2 2.5 %collective-permute-start.4 = (bf16[1024,128]{1,0:T(8,128)(2,1)S(1)}, bf16[1024,128]{1,0:T(8,128)(2,1)S(1)}, u32[]{:S(2)}, u32[]{:S(2)}) collective-permute-start(bf16[1024,128]{1,0:T(8,128)(2,1)S(1)} %get-tuple-element.55), channel_id=1, source_target_pairs={{0,8},{4,12},{8,0},{12,4},{1,9},{5,13},{9,1},{13,5},{2,10},{6,14},... | collective-permute-start | bytes 786440 | tf_op jit(solution)/shard_map/ppermute | solution.py:590
  22.7 0.0 collective-permute-done.7.refs_6_.refs_10_
  22.7 2.5 %collective-permute-start.5 = (bf16[1024,128]{1,0:T(8,128)(2,1)S(1)}, bf16[1024,128]{1,0:T(8,128)(2,1)S(1)}, u32[]{:S(2)}, u32[]{:S(2)}) collective-permute-start(bf16[1024,128]{1,0:T(8,128)(2,1)S(1)} %get-tuple-element.56), channel_id=1, source_target_pairs={{0,12},{4,8},{8,4},{12,0},{1,13},{5,9},{9,5},{13,1},{2,14},{6,10},... | collective-permute-start | bytes 786440 | tf_op jit(solution)/shard_map/ppermute | solution.py:590
  25.2 0.0 collective-permute-done.8.refs_7_.refs_11_
  25.2 0.1 collective-permute-start.12
  25.3 0.0 collective-permute-done.6.refs_0_
  25.3 2.9 %shard_map.99 = (bf16[512,128]{1,0:T(8,128)(2,1)S(1)}, bf16[512,128]{1,0:T(8,128)(2,1)S(1)}, bf16[512,128]{1,0:T(8,128)(2,1)S(1)}, bf16[512,128]{1,0:T(8,128)(2,1)S(1)}) custom-call(s32[4]{0:T(128)S(1)} %pad_add_fusion.place_ref.refs_0_, bf16[1,512,512]{2,1,0:T(8,128)(2,1)S(1)} %collective-permute-done.6.refs_0_, bf16[256,2048]{1,0:T(8,128)(2,1)} %refs_1_.5, ...), custom_call_target="tpu_custom_call" | custom-call | flops 115000000 | bytes 1048576 | tf_op jit(solution)/shard_map/pallas_call | solution.py:570
  28.2 1.5 %collective-permute-start.9 = (bf16[512,128]{1,0:T(8,128)(2,1)S(1)}, bf16[512,128]{1,0:T(8,128)(2,1)S(1)}, u32[]{:S(2)}, u32[]{:S(2)}) collective-permute-start(bf16[512,128]{1,0:T(8,128)(2,1)S(1)} %get-tuple-element.66), channel_id=1, source_target_pairs={{0,4},{4,0},{8,12},{12,8},{1,5},{5,1},{9,13},{13,9},{2,6},{6,2},{1... | collective-permute-start | bytes 393224 | tf_op jit(solution)/shard_map/ppermute | solution.py:590
  29.6 3.4 %collective-permute-done.3.refs_1_ = bf16[1024,128]{1,0:T(8,128)(2,1)S(1)} collective-permute-done((bf16[1024,128]{1,0:T(8,128)(2,1)S(1)}, bf16[1024,128]{1,0:T(8,128)(2,1)S(1)}, u32[]{:S(2)}, u32[]{:S(2)}) %collective-permute-start.3) | collective-permute-done | bytes 262176 | tf_op jit(solution)/shard_map/ppermute | solution.py:590
  33.0 8.5 %collective-permute-done.4.refs_2_ = bf16[1024,128]{1,0:T(8,128)(2,1)S(1)} collective-permute-done((bf16[1024,128]{1,0:T(8,128)(2,1)S(1)}, bf16[1024,128]{1,0:T(8,128)(2,1)S(1)}, u32[]{:S(2)}, u32[]{:S(2)}) %collective-permute-start.4) | collective-permute-done | bytes 262176 | tf_op jit(solution)/shard_map/ppermute | solution.py:590
  41.5 3.5 %collective-permute-start.11 = (bf16[512,128]{1,0:T(8,128)(2,1)S(1)}, bf16[512,128]{1,0:T(8,128)(2,1)S(1)}, u32[]{:S(2)}, u32[]{:S(2)}) collective-permute-start(bf16[512,128]{1,0:T(8,128)(2,1)S(1)} %get-tuple-element.68), channel_id=1, source_target_pairs={{0,12},{4,8},{8,4},{12,0},{1,13},{5,9},{9,5},{13,1},{2,14},{6,10},... | collective-permute-start | bytes 393224 | tf_op jit(solution)/shard_map/ppermute | solution.py:590
  45.0 6.5 %shard_map.100 = (bf16[512,128]{1,0:T(8,128)(2,1)S(1)}, bf16[512,128]{1,0:T(8,128)(2,1)S(1)}, bf16[512,128]{1,0:T(8,128)(2,1)S(1)}, bf16[512,128]{1,0:T(8,128)(2...) custom-call(s32[4]{0:T(128)S(1)} %pad_add_fusion.place_ref.refs_0_, ...), custom_call_target="tpu_custom_call" | custom-call | flops 8049999872 | bytes 1048576 | tf_op jit(solution)/shard_map/pallas_call | solution.py:570
  51.5 10.4 %collective-permute-start.14 = (bf16[512,128]{1,0:T(8,128)(2,1)S(1)}, bf16[512,128]{1,0:T(8,128)(2,1)S(1)}, u32[]{:S(2)}, u32[]{:S(2)}) collective-permute-start(bf16[512,128]{1,0:T(8,128)(2,1)S(1)} %get-tuple-element.83), channel_id=1, source_target_pairs={{0,8},{4,12},{8,0},{12,4},{1,9},{5,13},{9,1},{13,5},{2,10},{6,14},... | collective-permute-start | bytes 393224 | tf_op jit(solution)/shard_map/ppermute | solution.py:590
  61.9 0.0 collective-permute-done.9.refs_5_
  61.9 1.3 %collective-permute-start.26 = (bf16[512,128]{1,0:T(8,128)(2,1)S(1)}, bf16[512,128]{1,0:T(8,128)(2,1)S(1)}, u32[]{:S(2)}, u32[]{:S(2)}) collective-permute-start(bf16[512,128]{1,0:T(8,128)(2,1)S(1)} %get-tuple-element.96), channel_id=1, source_target_pairs={{0,12},{4,8},{8,4},{12,0},{1,13},{5,9},{9,5},{13,1},{2,14},{6,10},... | collective-permute-start | bytes 393224 | tf_op jit(solution)/shard_map/ppermute | solution.py:590
  63.2 7.0 %shard_map.101 = (bf16[1024,128]{1,0:T(8,128)(2,1)S(1)}, bf16[1024,128]{1,0:T(8,128)(2,1)S(1)}, bf16[1024,128]{1,0:T(8,128)(2,1)S(1)}, bf16[1024,128]{1,0:T(8,12...) custom-call(s32[4]{0:T(128)S(1)} %pad_add_fusion.place_ref.refs_0_, ...), custom_call_target="tpu_custom_call" | custom-call | flops 11500000256 | bytes 1048576 | tf_op jit(solution)/shard_map/pallas_call | solution.py:570
  70.2 1.1 collective-permute-start.13
  71.3 0.0 collective-permute-done.14.refs_3_.refs_10_
  71.3 2.0 %collective-permute-start.16 = (bf16[1024,128]{1,0:T(8,128)(2,1)S(1)}, bf16[1024,128]{1,0:T(8,128)(2,1)S(1)}, u32[]{:S(2)}, u32[]{:S(2)}) collective-permute-start(bf16[1024,128]{1,0:T(8,128)(2,1)S(1)} %get-tuple-element.85), channel_id=1, source_target_pairs={{0,12},{4,8},{8,4},{12,0},{1,13},{5,9},{9,5},{13,1},{2,14},{6,10},... | collective-permute-start | bytes 786440 | tf_op jit(solution)/shard_map/ppermute | solution.py:590
  73.3 0.0 collective-permute-start.20
  73.3 0.0 collective-permute-done.25.refs_2_.refs_9_
  73.3 1.5 %collective-permute-start.15 = (bf16[1024,128]{1,0:T(8,128)(2,1)S(1)}, bf16[1024,128]{1,0:T(8,128)(2,1)S(1)}, u32[]{:S(2)}, u32[]{:S(2)}) collective-permute-start(bf16[1024,128]{1,0:T(8,128)(2,1)S(1)} %get-tuple-element.84), channel_id=1, source_target_pairs={{0,8},{4,12},{8,0},{12,4},{1,9},{5,13},{9,1},{13,5},{2,10},{6,14},... | collective-permute-start | bytes 786440 | tf_op jit(solution)/shard_map/ppermute | solution.py:590
  74.9 0.0 collective-permute-done.26.refs_4_.refs_11_
  74.9 0.6 shard_map.104
  75.5 1.9 %collective-permute-start.27 = (bf16[4,512,128]{2,1,0:T(8,128)(2,1)S(1)}, bf16[4,512,128]{2,1,0:T(8,128)(2,1)S(1)}, u32[]{:S(2)}, u32[]{:S(2)}) collective-permute-start(bf16[4,512,128]{2,1,0:T(8,128)(2,1)S(1)} %shard_map.104), channel_id=1, source_target_pairs={{0,1},{1,0},{2,3},{3,2},{4,5},{5,4},{6,7},{7,6},{8,9},{9,8},{10,11... | collective-permute-start | bytes 1572872 | tf_op jit(solution)/shard_map/ppermute | solution.py:596
  77.3 2.8 %collective-permute-done.16.refs_3_ = bf16[1024,128]{1,0:T(8,128)(2,1)S(1)} collective-permute-done((bf16[1024,128]{1,0:T(8,128)(2,1)S(1)}, bf16[1024,128]{1,0:T(8,128)(2,1)S(1)}, u32[]{:S(2)}, u32[]{:S(2)}) %collective-permute-start.16) | collective-permute-done | bytes 262176 | tf_op jit(solution)/shard_map/ppermute | solution.py:590
  80.1 3.2 %collective-permute-start.21 = (bf16[1024,128]{1,0:T(8,128)(2,1)S(1)}, bf16[1024,128]{1,0:T(8,128)(2,1)S(1)}, u32[]{:S(2)}, u32[]{:S(2)}) collective-permute-start(bf16[1024,128]{1,0:T(8,128)(2,1)S(1)} %get-tuple-element.91.refs_0_), channel_id=1, source_target_pairs={{0,1},{1,0},{2,3},{3,2},{4,5},{5,4},{6,7},{7,6},{8,9},{9,8},{10,11... | collective-permute-start | bytes 786440 | tf_op jit(solution)/shard_map/ppermute | solution.py:596
  83.4 5.2 %collective-permute-done.20.refs_1_ = bf16[1024,128]{1,0:T(8,128)(2,1)S(1)} collective-permute-done((bf16[1024,128]{1,0:T(8,128)(2,1)S(1)}, bf16[1024,128]{1,0:T(8,128)(2,1)S(1)}, u32[]{:S(2)}, u32[]{:S(2)}) %collective-permute-start.20) | collective-permute-done | bytes 262176 | tf_op jit(solution)/shard_map/ppermute | solution.py:590
  88.6 0.5 collective-permute-start.24
  89.1 0.0 collective-permute-done.13.theirs_ref
  89.1 0.0 collective-permute-start.22
  89.1 0.6 shard_map.102
  89.7 7.1 %collective-permute-done.15.refs_2_ = bf16[1024,128]{1,0:T(8,128)(2,1)S(1)} collective-permute-done((bf16[1024,128]{1,0:T(8,128)(2,1)S(1)}, bf16[1024,128]{1,0:T(8,128)(2,1)S(1)}, u32[]{:S(2)}, u32[]{:S(2)}) %collective-permute-start.15) | collective-permute-done | bytes 262176 | tf_op jit(solution)/shard_map/ppermute | solution.py:590
  96.8 0.5 collective-permute-start.23
  97.3 0.0 collective-permute-done.21.refs_4_
  97.3 0.0 collective-permute-start.17
  97.3 2.5 %collective-permute-start.18 = (bf16[576,128]{1,0:T(8,128)(2,1)S(1)}, bf16[576,128]{1,0:T(8,128)(2,1)S(1)}, u32[]{:S(2)}, u32[]{:S(2)}) collective-permute-start(bf16[576,128]{1,0:T(8,128)(2,1)S(1)} %get-tuple-element.88), channel_id=1, source_target_pairs={{0,8},{4,12},{8,0},{12,4},{1,9},{5,13},{9,1},{13,5},{2,10},{6,14},... | collective-permute-start | bytes 442376 | tf_op jit(solution)/shard_map/ppermute | solution.py:590
  99.8 1.1 collective-permute-start.19
  100.9 2.9 %shard_map.105 = bf16[256,1024]{1,0:T(8,128)(2,1)S(1)} custom-call(s32[4]{0:T(128)S(1)} %pad_add_fusion.place_ref.refs_0_, bf16[1024,128]{1,0:T(8,128)(2,1)S(1)} %get-tuple-element.91.refs_0_, bf16[1024,128]{1,0:T(8,128)(2,1)S(1)} %collective-permute-done.20.refs_1_, bf16[1024,128]{1,0:T(8,128)(2,1)S(1)} %collective-permute-done.15.refs_2_, ...), custom_call_target="tpu_custom_call" | custom-call | flops 1150000000 | bytes 1048576 | tf_op jit(solution)/shard_map/pallas_call | solution.py:570
  103.8 1.2 %collective-permute-start.28 = (bf16[256,1024]{1,0:T(8,128)(2,1)S(1)}, bf16[256,1024]{1,0:T(8,128)(2,1)S(1)}, u32[]{:S(2)}, u32[]{:S(2)}) collective-permute-start(bf16[256,1024]{1,0:T(8,128)(2,1)S(1)} %shard_map.105), channel_id=1, source_target_pairs={{0,1},{1,3},{3,2},{2,0},{4,5},{5,7},{7,6},{6,4},{8,9},{9,11},{11,1... | collective-permute-start | bytes 1572872 | tf_op jit(solution)/shard_map/ppermute | solution.py:744
  105.0 2.9 %shard_map.106.kept_ref = bf16[256,1024]{1,0:T(8,128)(2,1)S(1)} custom-call(s32[4]{0:T(128)S(1)} %pad_add_fusion.place_ref.refs_0_, bf16[1024,128]{1,0:T(8,128)(2,1)S(1)} %get-tuple-element.91.refs_0_, bf16[1024,128]{1,0:T(8,128)(2,1)S(1)} %collective-permute-done.20.refs_1_, bf16[1024,128]{1,0:T(8,128)(2,1)S(1)} %collective-permute-done.15.refs_2_, ...), custom_call_target="tpu_custom_call" | custom-call | flops 1150000000 | bytes 1048576 | tf_op jit(solution)/shard_map/pallas_call | solution.py:570
  107.9 3.2 %collective-permute-start.29 = (bf16[256,1024]{1,0:T(8,128)(2,1)S(1)}, bf16[256,1024]{1,0:T(8,128)(2,1)S(1)}, u32[]{:S(2)}, u32[]{:S(2)}) collective-permute-start(bf16[256,1024]{1,0:T(8,128)(2,1)S(1)} %shard_map.106.kept_ref), channel_id=1, source_target_pairs={{1,2},{2,1},{5,6},{6,5},{9,10},{10,9},{13,14},{14,13},{17,18},{18,... | collective-permute-start | bytes 1572872 | tf_op jit(solution)/shard_map/ppermute | solution.py:746
  111.1 0.0 collective-permute-done.17.refs_1_
  111.1 0.0 collective-permute-done.19.refs_3_
  111.1 1.5 %shard_map.103 = (bf16[256,1024]{1,0:T(8,128)(2,1)}, f32[8,32,128]{2,1,0:T(8,128)}) custom-call(s32[4]{0:T(128)S(1)} %pad_add_fusion.place_ref.refs_0_, bf16[576,128]{1,0:T(8,128)(2,1)S(1)} %get-tuple-element.86.refs_0_, bf16[576,128]{1,0:T(8,128)(2,1)S(1)} %collective-permute-done.17.refs_1_, bf16[576,128]{1,0:T(8,128)(2,1)S(1)} %collective-permute-done.18.refs_2_, ...), custom_call_target="tpu_custom_call" | custom-call | flops 9200000000 | bytes 1048576 | tf_op jit(solution)/shard_map/pallas_call | solution.py:570
  112.7 6.1 %collective-permute-done.29.second_ref = bf16[256,1024]{1,0:T(8,128)(2,1)S(1)} collective-permute-done((bf16[256,1024]{1,0:T(8,128)(2,1)S(1)}, bf16[256,1024]{1,0:T(8,128)(2,1)S(1)}, u32[]{:S(2)}, u32[]{:S(2)}) %collective-permute-start.29) | collective-permute-done | bytes 524320 | tf_op jit(solution)/shard_map/ppermute | solution.py:746
  118.8 0.0 collective-permute-done.28.first_ref
  118.8 1.5 %shard_map.107 = bf16[256,1024]{1,0:T(8,128)(2,1)} custom-call(s32[4]{0:T(128)S(1)} %pad_add_fusion.place_ref.refs_0_, bf16[256,1024]{1,0:T(8,128)(2,1)S(1)} %collective-permute-done.28.first_ref, bf16[256,1024]{1,0:T(8,128)(2,1)S(1)} %collective-permute-done.29.second_ref, bf16[256,1024]{1,0:T(8,128)(2,1)S(1)} %shard_map.106.kept_ref), custom_call_target="tpu_custom_call" | custom-call | flops 1150000000 | bytes 1048576 | tf_op jit(solution)/shard_map/pallas_call | solution.py:570
  (19 shorter events, 0.0 us)
Async XLA Ops:
  0.6 4.6 %collective-permute-start.1 = (bf16[256,2048]{1,0:T(8,128)(2,1)}, bf16[256,2048]{1,0:T(8,128)(2,1)S(1)}, u32[]{:S(2)}, u32[]{:S(2)}) collective-permute-start(bf16[256,2048]{1,0:T(8,128)(2,1)} %refs_1_.5), channel_id=1, source_target_pairs={{0,1},{1,0},{2,3},{3,2},{4,5},{5,4},{6,7},{7,6},{8,9},{9,8},{10,11... | collective-permute-start | bytes 3145736 | tf_op jit(solution)/shard_map/ppermute | solution.py:596
  2.4 2.8 %collective-permute-start = (bf16[4,272,128]{2,1,0:T(8,128)(2,1)S(1)}, bf16[4,272,128]{2,1,0:T(8,128)(2,1)S(1)}, u32[]{:S(2)}, u32[]{:S(2)}) collective-permute-start(bf16[4,272,128]{2,1,0:T(8,128)(2,1)S(1)} %shard_map.95), channel_id=1, source_target_pairs={{0,1},{1,0},{2,3},{3,2},{4,5},{5,4},{6,7},{7,6},{8,9},{9,8},{10,11... | collective-permute-start | bytes 835592 | tf_op jit(solution)/shard_map/ppermute | solution.py:596
  8.1 5.0 %collective-permute-start.2 = (bf16[2,512,512]{2,1,0:T(8,128)(2,1)S(1)}, bf16[2,512,512]{2,1,0:T(8,128)(2,1)S(1)}, u32[]{:S(2)}, u32[]{:S(2)}) collective-permute-start(bf16[2,512,512]{2,1,0:T(8,128)(2,1)S(1)} %get-tuple-element.52), channel_id=1, source_target_pairs={{0,1},{1,0},{2,3},{3,2},{4,5},{5,4},{6,7},{7,6},{8,9},{9,8},{10,11... | collective-permute-start | bytes 3145736 | tf_op jit(solution)/shard_map/ppermute | solution.py:596
  8.3 14.4 %collective-permute-start.7 = (bf16[528,128]{1,0:T(8,128)(2,1)S(1)}, bf16[528,128]{1,0:T(8,128)(2,1)S(1)}, u32[]{:S(2)}, u32[]{:S(2)}) collective-permute-start(bf16[528,128]{1,0:T(8,128)(2,1)S(1)} %get-tuple-element.58), channel_id=1, source_target_pairs={{0,8},{4,12},{8,0},{12,4},{1,9},{5,13},{9,1},{13,5},{2,10},{6,14},... | collective-permute-start | bytes 405512 | tf_op jit(solution)/shard_map/ppermute | solution.py:590
  12.0 13.2 %collective-permute-start.8 = (bf16[528,128]{1,0:T(8,128)(2,1)S(1)}, bf16[528,128]{1,0:T(8,128)(2,1)S(1)}, u32[]{:S(2)}, u32[]{:S(2)}) collective-permute-start(bf16[528,128]{1,0:T(8,128)(2,1)S(1)} %get-tuple-element.59), channel_id=1, source_target_pairs={{0,12},{4,8},{8,4},{12,0},{1,13},{5,9},{9,5},{13,1},{2,14},{6,10},... | collective-permute-start | bytes 405512 | tf_op jit(solution)/shard_map/ppermute | solution.py:590
  15.8 9.5 %collective-permute-start.6 = (bf16[1,512,512]{2,1,0:T(8,128)(2,1)S(1)}, bf16[1,512,512]{2,1,0:T(8,128)(2,1)S(1)}, u32[]{:S(2)}, u32[]{:S(2)}) collective-permute-start(bf16[1,512,512]{2,1,0:T(8,128)(2,1)S(1)} %shard_map.98), channel_id=1, source_target_pairs={{0,1},{1,0},{2,3},{3,2},{4,5},{5,4},{6,7},{7,6},{8,9},{9,8},{10,11... | collective-permute-start | bytes 1572872 | tf_op jit(solution)/shard_map/ppermute | solution.py:596
  20.2 12.9 %collective-permute-start.3 = (bf16[1024,128]{1,0:T(8,128)(2,1)S(1)}, bf16[1024,128]{1,0:T(8,128)(2,1)S(1)}, u32[]{:S(2)}, u32[]{:S(2)}) collective-permute-start(bf16[1024,128]{1,0:T(8,128)(2,1)S(1)} %get-tuple-element.54), channel_id=1, source_target_pairs={{0,4},{4,0},{8,12},{12,8},{1,5},{5,1},{9,13},{13,9},{2,6},{6,2},{1... | collective-permute-start | bytes 786440 | tf_op jit(solution)/shard_map/ppermute | solution.py:590
  20.2 21.3 %collective-permute-start.4 = (bf16[1024,128]{1,0:T(8,128)(2,1)S(1)}, bf16[1024,128]{1,0:T(8,128)(2,1)S(1)}, u32[]{:S(2)}, u32[]{:S(2)}) collective-permute-start(bf16[1024,128]{1,0:T(8,128)(2,1)S(1)} %get-tuple-element.55), channel_id=1, source_target_pairs={{0,8},{4,12},{8,0},{12,4},{1,9},{5,13},{9,1},{13,5},{2,10},{6,14},... | collective-permute-start | bytes 786440 | tf_op jit(solution)/shard_map/ppermute | solution.py:590
  22.7 22.3 %collective-permute-start.5 = (bf16[1024,128]{1,0:T(8,128)(2,1)S(1)}, bf16[1024,128]{1,0:T(8,128)(2,1)S(1)}, u32[]{:S(2)}, u32[]{:S(2)}) collective-permute-start(bf16[1024,128]{1,0:T(8,128)(2,1)S(1)} %get-tuple-element.56), channel_id=1, source_target_pairs={{0,12},{4,8},{8,4},{12,0},{1,13},{5,9},{9,5},{13,1},{2,14},{6,10},... | collective-permute-start | bytes 786440 | tf_op jit(solution)/shard_map/ppermute | solution.py:590
  25.2 19.8 %copy-start.3 = (s32[256]{0:T(256)S(1)}, s32[256]{0:T(256)}, u32[]{:S(2)}) copy-start(s32[256]{0:T(256)} %param.11) | copy-start | bytes 3076
  25.2 19.8 %collective-permute-start.12 = (bf16[528,128]{1,0:T(8,128)(2,1)S(1)}, bf16[528,128]{1,0:T(8,128)(2,1)S(1)}, u32[]{:S(2)}, u32[]{:S(2)}) collective-permute-start(bf16[528,128]{1,0:T(8,128)(2,1)S(1)} %get-tuple-element.70), channel_id=1, source_target_pairs={{0,4},{4,0},{8,12},{12,8},{1,5},{5,1},{9,13},{13,9},{2,6},{6,2},{1... | collective-permute-start | bytes 405512 | tf_op jit(solution)/shard_map/ppermute | solution.py:590
  28.2 33.8 %collective-permute-start.9 = (bf16[512,128]{1,0:T(8,128)(2,1)S(1)}, bf16[512,128]{1,0:T(8,128)(2,1)S(1)}, u32[]{:S(2)}, u32[]{:S(2)}) collective-permute-start(bf16[512,128]{1,0:T(8,128)(2,1)S(1)} %get-tuple-element.66), channel_id=1, source_target_pairs={{0,4},{4,0},{8,12},{12,8},{1,5},{5,1},{9,13},{13,9},{2,6},{6,2},{1... | collective-permute-start | bytes 393224 | tf_op jit(solution)/shard_map/ppermute | solution.py:590
  33.0 30.1 %collective-permute-start.10 = (bf16[512,128]{1,0:T(8,128)(2,1)S(1)}, bf16[512,128]{1,0:T(8,128)(2,1)S(1)}, u32[]{:S(2)}, u32[]{:S(2)}) collective-permute-start(bf16[512,128]{1,0:T(8,128)(2,1)S(1)} %get-tuple-element.67), channel_id=1, source_target_pairs={{0,8},{4,12},{8,0},{12,4},{1,9},{5,13},{9,1},{13,5},{2,10},{6,14},... | collective-permute-start | bytes 393224 | tf_op jit(solution)/shard_map/ppermute | solution.py:590
  41.5 21.6 %collective-permute-start.11 = (bf16[512,128]{1,0:T(8,128)(2,1)S(1)}, bf16[512,128]{1,0:T(8,128)(2,1)S(1)}, u32[]{:S(2)}, u32[]{:S(2)}) collective-permute-start(bf16[512,128]{1,0:T(8,128)(2,1)S(1)} %get-tuple-element.68), channel_id=1, source_target_pairs={{0,12},{4,8},{8,4},{12,0},{1,13},{5,9},{9,5},{13,1},{2,14},{6,10},... | collective-permute-start | bytes 393224 | tf_op jit(solution)/shard_map/ppermute | solution.py:590
  51.5 19.8 %collective-permute-start.14 = (bf16[512,128]{1,0:T(8,128)(2,1)S(1)}, bf16[512,128]{1,0:T(8,128)(2,1)S(1)}, u32[]{:S(2)}, u32[]{:S(2)}) collective-permute-start(bf16[512,128]{1,0:T(8,128)(2,1)S(1)} %get-tuple-element.83), channel_id=1, source_target_pairs={{0,8},{4,12},{8,0},{12,4},{1,9},{5,13},{9,1},{13,5},{2,10},{6,14},... | collective-permute-start | bytes 393224 | tf_op jit(solution)/shard_map/ppermute | solution.py:590
  61.9 11.4 %collective-permute-start.25 = (bf16[512,128]{1,0:T(8,128)(2,1)S(1)}, bf16[512,128]{1,0:T(8,128)(2,1)S(1)}, u32[]{:S(2)}, u32[]{:S(2)}) collective-permute-start(bf16[512,128]{1,0:T(8,128)(2,1)S(1)} %get-tuple-element.95), channel_id=1, source_target_pairs={{0,4},{4,0},{8,12},{12,8},{1,5},{5,1},{9,13},{13,9},{2,6},{6,2},{1... | collective-permute-start | bytes 393224 | tf_op jit(solution)/shard_map/ppermute | solution.py:590
  61.9 13.0 %collective-permute-start.26 = (bf16[512,128]{1,0:T(8,128)(2,1)S(1)}, bf16[512,128]{1,0:T(8,128)(2,1)S(1)}, u32[]{:S(2)}, u32[]{:S(2)}) collective-permute-start(bf16[512,128]{1,0:T(8,128)(2,1)S(1)} %get-tuple-element.96), channel_id=1, source_target_pairs={{0,12},{4,8},{8,4},{12,0},{1,13},{5,9},{9,5},{13,1},{2,14},{6,10},... | collective-permute-start | bytes 393224 | tf_op jit(solution)/shard_map/ppermute | solution.py:590
  70.2 18.9 %collective-permute-start.13 = (bf16[4,288,128]{2,1,0:T(8,128)(2,1)S(1)}, bf16[4,288,128]{2,1,0:T(8,128)(2,1)S(1)}, u32[]{:S(2)}, u32[]{:S(2)}) collective-permute-start(bf16[4,288,128]{2,1,0:T(8,128)(2,1)S(1)} %get-tuple-element.74), channel_id=1, source_target_pairs={{0,1},{1,0},{2,3},{3,2},{4,5},{5,4},{6,7},{7,6},{8,9},{9,8},{10,11... | collective-permute-start | bytes 884744 | tf_op jit(solution)/shard_map/ppermute | solution.py:596
  71.3 8.8 %collective-permute-start.16 = (bf16[1024,128]{1,0:T(8,128)(2,1)S(1)}, bf16[1024,128]{1,0:T(8,128)(2,1)S(1)}, u32[]{:S(2)}, u32[]{:S(2)}) collective-permute-start(bf16[1024,128]{1,0:T(8,128)(2,1)S(1)} %get-tuple-element.85), channel_id=1, source_target_pairs={{0,12},{4,8},{8,4},{12,0},{1,13},{5,9},{9,5},{13,1},{2,14},{6,10},... | collective-permute-start | bytes 786440 | tf_op jit(solution)/shard_map/ppermute | solution.py:590
  73.3 15.2 %collective-permute-start.20 = (bf16[1024,128]{1,0:T(8,128)(2,1)S(1)}, bf16[1024,128]{1,0:T(8,128)(2,1)S(1)}, u32[]{:S(2)}, u32[]{:S(2)}) collective-permute-start(bf16[1024,128]{1,0:T(8,128)(2,1)S(1)} %get-tuple-element.92), channel_id=1, source_target_pairs={{0,4},{4,0},{8,12},{12,8},{1,5},{5,1},{9,13},{13,9},{2,6},{6,2},{1... | collective-permute-start | bytes 786440 | tf_op jit(solution)/shard_map/ppermute | solution.py:590
  73.3 23.4 %collective-permute-start.15 = (bf16[1024,128]{1,0:T(8,128)(2,1)S(1)}, bf16[1024,128]{1,0:T(8,128)(2,1)S(1)}, u32[]{:S(2)}, u32[]{:S(2)}) collective-permute-start(bf16[1024,128]{1,0:T(8,128)(2,1)S(1)} %get-tuple-element.84), channel_id=1, source_target_pairs={{0,8},{4,12},{8,0},{12,4},{1,9},{5,13},{9,1},{13,5},{2,10},{6,14},... | collective-permute-start | bytes 786440 | tf_op jit(solution)/shard_map/ppermute | solution.py:590
  74.9 26.0 %copy-start.2 = (bf16[1024,1024]{1,0:T(8,128)(2,1)S(1)}, bf16[1024,1024]{1,0:T(8,128)(2,1)}, u32[]{:S(2)}) copy-start(bf16[1024,1024]{1,0:T(8,128)(2,1)} %refs_14_.3) | copy-start | bytes 6291460
  75.5 25.4 %collective-permute-start.27 = (bf16[4,512,128]{2,1,0:T(8,128)(2,1)S(1)}, bf16[4,512,128]{2,1,0:T(8,128)(2,1)S(1)}, u32[]{:S(2)}, u32[]{:S(2)}) collective-permute-start(bf16[4,512,128]{2,1,0:T(8,128)(2,1)S(1)} %shard_map.104), channel_id=1, source_target_pairs={{0,1},{1,0},{2,3},{3,2},{4,5},{5,4},{6,7},{7,6},{8,9},{9,8},{10,11... | collective-permute-start | bytes 1572872 | tf_op jit(solution)/shard_map/ppermute | solution.py:596
  80.1 17.2 %collective-permute-start.21 = (bf16[1024,128]{1,0:T(8,128)(2,1)S(1)}, bf16[1024,128]{1,0:T(8,128)(2,1)S(1)}, u32[]{:S(2)}, u32[]{:S(2)}) collective-permute-start(bf16[1024,128]{1,0:T(8,128)(2,1)S(1)} %get-tuple-element.91.refs_0_), channel_id=1, source_target_pairs={{0,1},{1,0},{2,3},{3,2},{4,5},{5,4},{6,7},{7,6},{8,9},{9,8},{10,11... | collective-permute-start | bytes 786440 | tf_op jit(solution)/shard_map/ppermute | solution.py:596
  88.6 8.7 %collective-permute-start.24 = (bf16[1024,128]{1,0:T(8,128)(2,1)S(1)}, bf16[1024,128]{1,0:T(8,128)(2,1)S(1)}, u32[]{:S(2)}, u32[]{:S(2)}) collective-permute-start(bf16[1024,128]{1,0:T(8,128)(2,1)S(1)} %collective-permute-done.16.refs_3_), channel_id=1, source_target_pairs={{0,1},{1,0},{2,3},{3,2},{4,5},{5,4},{6,7},{7,6},{8,9},{9,8},{10,11... | collective-permute-start | bytes 786440 | tf_op jit(solution)/shard_map/ppermute | solution.py:596
  89.1 10.7 %collective-permute-start.22 = (bf16[1024,128]{1,0:T(8,128)(2,1)S(1)}, bf16[1024,128]{1,0:T(8,128)(2,1)S(1)}, u32[]{:S(2)}, u32[]{:S(2)}) collective-permute-start(bf16[1024,128]{1,0:T(8,128)(2,1)S(1)} %collective-permute-done.20.refs_1_), channel_id=1, source_target_pairs={{0,1},{1,0},{2,3},{3,2},{4,5},{5,4},{6,7},{7,6},{8,9},{9,8},{10,11... | collective-permute-start | bytes 786440 | tf_op jit(solution)/shard_map/ppermute | solution.py:596
  89.1 11.8 %copy-start = (bf16[1024,1024]{1,0:T(8,128)(2,1)S(1)}, bf16[1024,1024]{1,0:T(8,128)(2,1)}, u32[]{:S(2)}) copy-start(bf16[1024,1024]{1,0:T(8,128)(2,1)} %refs_15_.3) | copy-start | bytes 6291460
  89.1 11.8 %copy-start.1 = (bf16[1024,1024]{1,0:T(8,128)(2,1)S(1)}, bf16[1024,1024]{1,0:T(8,128)(2,1)}, u32[]{:S(2)}) copy-start(bf16[1024,1024]{1,0:T(8,128)(2,1)} %refs_13_.3) | copy-start | bytes 6291460
  96.8 4.1 %collective-permute-start.23 = (bf16[1024,128]{1,0:T(8,128)(2,1)S(1)}, bf16[1024,128]{1,0:T(8,128)(2,1)S(1)}, u32[]{:S(2)}, u32[]{:S(2)}) collective-permute-start(bf16[1024,128]{1,0:T(8,128)(2,1)S(1)} %collective-permute-done.15.refs_2_), channel_id=1, source_target_pairs={{0,1},{1,0},{2,3},{3,2},{4,5},{5,4},{6,7},{7,6},{8,9},{9,8},{10,11... | collective-permute-start | bytes 786440 | tf_op jit(solution)/shard_map/ppermute | solution.py:596
  97.3 13.8 %collective-permute-start.17 = (bf16[576,128]{1,0:T(8,128)(2,1)S(1)}, bf16[576,128]{1,0:T(8,128)(2,1)S(1)}, u32[]{:S(2)}, u32[]{:S(2)}) collective-permute-start(bf16[576,128]{1,0:T(8,128)(2,1)S(1)} %get-tuple-element.87), channel_id=1, source_target_pairs={{0,4},{4,0},{8,12},{12,8},{1,5},{5,1},{9,13},{13,9},{2,6},{6,2},{1... | collective-permute-start | bytes 442376 | tf_op jit(solution)/shard_map/ppermute | solution.py:590
  97.3 13.8 %collective-permute-start.18 = (bf16[576,128]{1,0:T(8,128)(2,1)S(1)}, bf16[576,128]{1,0:T(8,128)(2,1)S(1)}, u32[]{:S(2)}, u32[]{:S(2)}) collective-permute-start(bf16[576,128]{1,0:T(8,128)(2,1)S(1)} %get-tuple-element.88), channel_id=1, source_target_pairs={{0,8},{4,12},{8,0},{12,4},{1,9},{5,13},{9,1},{13,5},{2,10},{6,14},... | collective-permute-start | bytes 442376 | tf_op jit(solution)/shard_map/ppermute | solution.py:590
  99.8 11.4 %collective-permute-start.19 = (bf16[576,128]{1,0:T(8,128)(2,1)S(1)}, bf16[576,128]{1,0:T(8,128)(2,1)S(1)}, u32[]{:S(2)}, u32[]{:S(2)}) collective-permute-start(bf16[576,128]{1,0:T(8,128)(2,1)S(1)} %get-tuple-element.89), channel_id=1, source_target_pairs={{0,12},{4,8},{8,4},{12,0},{1,13},{5,9},{9,5},{13,1},{2,14},{6,10},... | collective-permute-start | bytes 442376 | tf_op jit(solution)/shard_map/ppermute | solution.py:590
  103.8 15.0 %collective-permute-start.28 = (bf16[256,1024]{1,0:T(8,128)(2,1)S(1)}, bf16[256,1024]{1,0:T(8,128)(2,1)S(1)}, u32[]{:S(2)}, u32[]{:S(2)}) collective-permute-start(bf16[256,1024]{1,0:T(8,128)(2,1)S(1)} %shard_map.105), channel_id=1, source_target_pairs={{0,1},{1,3},{3,2},{2,0},{4,5},{5,7},{7,6},{6,4},{8,9},{9,11},{11,1... | collective-permute-start | bytes 1572872 | tf_op jit(solution)/shard_map/ppermute | solution.py:744
  107.9 10.8 %collective-permute-start.29 = (bf16[256,1024]{1,0:T(8,128)(2,1)S(1)}, bf16[256,1024]{1,0:T(8,128)(2,1)S(1)}, u32[]{:S(2)}, u32[]{:S(2)}) collective-permute-start(bf16[256,1024]{1,0:T(8,128)(2,1)S(1)} %shard_map.106.kept_ref), channel_id=1, source_target_pairs={{1,2},{2,1},{5,6},{6,5},{9,10},{10,9},{13,14},{14,13},{17,18},{18,... | collective-permute-start | bytes 1572872 | tf_op jit(solution)/shard_map/ppermute | solution.py:746
